TPU v7x, 32 devices: a whole 2x2x4 slice. The times are simulated.
32 devices in a mesh: groups: 2 (over y), pool: 4 (over z), heads: 2 (over x), sub: 2 (over core).
Axes of the slice: x: 2, y: 2, z: 4, core: 2. Of those that a mesh axis runs over, the one named last changes fastest.
Arguments:
- queries: bfloat16 [16, 128, 8192], P(('groups', 'pool'), None, ('heads', 'sub')), parts along dimension 0, may hold values from -6 to 6
- latent_store: bfloat16 [32768, 512], P(('groups', 'pool')), parts along dimension 0, may hold values from -6 to 6
- kv_up: bfloat16 [512, 8, 2, 128], P(None, ('heads', 'sub')), may hold values from -0.25 to 0.25
- q_gain: float32 [128], replicated, may hold values from 0.1 to 1.9
- k_gain: float32 [128], replicated, may hold values from 0.1 to 1.9
- out_weight: bfloat16 [8192, 8192], P(('heads', 'sub'), 'pool'), may hold values from -0.5 to 0.5
- place_holder: int32 [16, 8], P('groups'), parts along dimension 0, may hold values from 0 to 3, as said below
- place_block: int32 [16, 8], P('groups'), parts along dimension 0, may hold values from 0 to 31, as said below
- image_count: int32 [16], P('groups'), parts along dimension 0, may hold values from 1 to 1024, 5120 in all
- serving_request: int32 [16], P('groups'), parts along dimension 0, may hold values from 0 to 7, as said below
Outputs:
- update: bfloat16 [2048, 8192], P(('groups', 'pool', 'heads', 'sub')), parts along dimension 0
There are 2 independent parts, one for each index of `groups`. A program takes and returns all parts, laid end to end along the dimension named above; an argument that names none is the same for every part. Nothing has to cross between parts.
Inputs may be any that keep to these rules, and one draw needn't show every extreme that they name: `place_holder`: the 16 blocks of the requests of the 2 slots at one pool index lie on one holder at most 8 times, and some holder takes exactly 8 of them; one holder of each part stores exactly 32 blocks. `place_block`: no two blocks on one holder share a block slot. `serving_request`: each request is served in exactly one slot; slot k stands at pool index k // 2. The first image_count[r] image token slots of request r are live; the others are left out of its softmax.
All inputs are finite; a program needn't handle non-finite values.
Results may differ from a plain program's by a relative error of at most 0.0072.
Values may be sent and summed in bfloat16 or wider, within the bound.
No kernel may reach another device: no remote copies, remote signals or barrier semaphores. Data moves between devices by JAX's collectives and lax.ppermute only.
A program may use at most 128 MiB of HBM per device.

v0:
```python
import math

import jax
import jax.numpy as jnp
from jax import lax
from jax.sharding import PartitionSpec as P

BLK = 128


def rms_scale(values, gain):
    return values * lax.rsqrt(jnp.mean(values * values, axis=-1, keepdims=True) + 1e-05) * gain


def pair_rank(holders):
    count = holders.shape[1]
    same = holders[:, :, None] == holders[:, None, :]
    earlier = jnp.arange(count)[None, :] < jnp.arange(count)[:, None]
    return jnp.sum((same & earlier[None]).astype(jnp.int32), axis=2)


def project_kv(latent_rows, kv_local, k_gain):
    row_count = latent_rows.shape[0]
    projected = jnp.dot(
        latent_rows, kv_local.reshape(kv_local.shape[0], -1), preferred_element_type=jnp.float32
    )
    projected = projected.reshape(row_count, kv_local.shape[1], 2, kv_local.shape[3])
    keys = rms_scale(projected[:, :, 0], k_gain).astype(jnp.bfloat16)
    values = projected[:, :, 1].astype(jnp.bfloat16)
    return (keys, values)


def per_device(
    queries,
    latent_store,
    kv_up,
    q_gain,
    k_gain,
    out_weight,
    place_holder,
    place_block,
    image_count,
    serving_request,
):
    pool_size = lax.axis_size("pool")
    pool_index = lax.axis_index("pool")
    requests_here = queries.shape[0]
    text_rows = queries.shape[1]
    blocks_each = place_holder.shape[1]
    items = requests_here * blocks_each
    rank_width = latent_store.shape[1]
    block_rows = BLK
    store_blocks = latent_store.shape[0] // block_rows
    capacity = 2 * ((items + pool_size - 1) // pool_size)
    heads_here = kv_up.shape[1]
    head_width = kv_up.shape[3]
    total_requests = serving_request.shape[0]
    request_ids = jnp.arange(total_requests, dtype=jnp.int32)
    selector = (serving_request[:, None] == request_ids[None, :]).astype(jnp.int32)
    holder_slot = jnp.dot(selector, place_holder)
    block_slot = jnp.dot(selector, place_block)
    count_slot = jnp.dot(selector, image_count)
    holders = holder_slot.reshape(pool_size, items)
    blocks = block_slot.reshape(pool_size, items)
    ranks = pair_rank(holders)
    slot_ids = jnp.arange(capacity, dtype=jnp.int32)
    matched = (holders[:, None, :] == pool_index) & (ranks[:, None, :] == slot_ids[None, :, None])
    send_block = jnp.sum(jnp.where(matched, blocks[:, None, :], 0), axis=2)
    send_live = jnp.any(matched, axis=2)
    store = latent_store.reshape(store_blocks, block_rows, rank_width)
    outgoing = jnp.take(store, send_block.reshape(-1), axis=0)
    outgoing = jnp.where(
        send_live.reshape(-1)[:, None, None], outgoing, jnp.zeros((), jnp.bfloat16)
    )
    my_holders = lax.dynamic_index_in_dim(holders, pool_index, 0, keepdims=False)
    my_ranks = lax.dynamic_index_in_dim(ranks, pool_index, 0, keepdims=False)
    arrival = my_holders * capacity + my_ranks
    incoming = lax.all_to_all(
        outgoing.reshape(pool_size, capacity * block_rows, rank_width),
        "pool",
        split_axis=0,
        concat_axis=0,
        tiled=True,
    )
    chosen = jnp.take(
        incoming.reshape(pool_size * capacity, block_rows, rank_width), arrival, axis=0
    )
    keys, values = project_kv(chosen.reshape(items * block_rows, rank_width), kv_up, k_gain)
    image_slots = blocks_each * block_rows
    keys = keys.reshape(requests_here, image_slots, heads_here, head_width)
    values = values.reshape(requests_here, image_slots, heads_here, head_width)
    per_group = queries.shape[2] // (heads_here * head_width)
    shaped = queries.reshape(requests_here, text_rows, heads_here, per_group, head_width).astype(
        jnp.float32
    )
    normed = rms_scale(shaped, q_gain).astype(jnp.bfloat16)
    softmax_scale = 1.0 / math.sqrt(head_width)
    scores = (
        jnp.einsum("rtgqd,rsgd->rgqts", normed, keys, preferred_element_type=jnp.float32)
        * softmax_scale
    )
    count_here = lax.dynamic_slice_in_dim(count_slot, pool_index * requests_here, requests_here)
    positions = jnp.arange(image_slots, dtype=jnp.int32)
    live = positions[None, :] < count_here[:, None]
    expo = jnp.where(live[:, None, None, None, :], jnp.exp(scores), jnp.zeros((), jnp.float32))
    probs = (expo / jnp.sum(expo, axis=-1, keepdims=True)).astype(jnp.bfloat16)
    attended = jnp.einsum("rgqts,rsgd->rtgqd", probs, values, preferred_element_type=jnp.float32)
    attended = attended.astype(jnp.bfloat16).reshape(requests_here * text_rows, -1)
    partial_rows = jnp.dot(
        attended,
        lax.all_gather(out_weight, "pool", axis=1, tiled=True),
        preferred_element_type=jnp.float32,
    )
    summed = lax.psum_scatter(partial_rows, ("heads", "sub"), scatter_dimension=0, tiled=True)
    return summed.astype(jnp.bfloat16)


def solution(mesh):
    in_specs = (
        P(("groups", "pool"), None, ("heads", "sub")),
        P(("groups", "pool"), None),
        P(None, ("heads", "sub"), None, None),
        P(),
        P(),
        P(("heads", "sub"), "pool"),
        P("groups", None),
        P("groups", None),
        P("groups"),
        P("groups"),
    )
    out_specs = P(("groups", "pool", "heads", "sub"), None)
    return jax.shard_map(
        per_device, mesh=mesh, in_specs=in_specs, out_specs=out_specs, check_vma=False
    )
```

profile of v0, /device:TPU:0, one launch (start us, length us, event | category | flops | bytes accessed | tf_op | source)
XLA Modules:
  0.0 756.9 jit_solution(6324475005068507298)
XLA Ops:
  6.5 0.7 all-gather.2.cloned.1.call-update
  7.8 0.2 convert_reduce_fusion
  8.3 5.0 gather_fusion
  13.6 5.3 fusion.3
  18.9 6.7 all-to-all-start
  25.7 0.2 reshape.221
  25.9 0.2 copy.34
  26.1 1.6 copy.50
  27.7 0.9 multiply_reduce_fusion
  29.3 1.5 multiply_convert_fusion
  30.8 201.0 %all-to-all-done = bf16[4,1024,512]{2,1,0:T(8,128)(2,1)} async-done(((bf16[4,1024,512]{2,1,0:T(8,128)(2,1)}), bf16[4,1024,512]{2,1,0:T(8,128)(2,1)}, u32[]{:S(2)}, u32[]{:S(2)}) %all-to-all-start) | async-done | bytes 4194336 | tf_op jit(solution)/shard_map/all_to_all | solution.py:78
  231.7 2.9 gather_fusion.1
  234.7 0.3 broadcast_select_fusion
  234.9 1.3 fusion.31
  236.4 0.6 multiply_reduce_fusion.1
  237.0 0.4 copy-done.2
  237.5 4.1 bitcast_reduce_fusion
  241.5 4.1 fusion.9
  245.6 1.0 copy.41
  246.6 0.5 reshape.222
  247.1 412.3 %all-gather.2.cloned.1.call-done = bf16[2048,8192]{1,0:T(8,128)(2,1)} async-done(((bf16[2048,2048]{1,0:T(8,128)(2,1)}), bf16[2048,8192]{1,0:T(8,128)(2,1)}) %all-gather.2.cloned.1.call-update) | async-done | bytes 33554448 | tf_op jit(solution)/shard_map/all_gather | solution.py:111
  659.4 17.0 %fusion.32 = f32[256,8192]{1,0:T(8,128)} fusion(bf16[256,2048]{1,0:T(8,128)(2,1)S(1)} %reshape.222, bf16[2048,8192]{1,0:T(8,128)(2,1)} %all-gather.2.cloned.1.call-done), kind=kOutput, calls=%fused_computation.61 | convolution fusion | flops 8589934592 | bytes 42991616 | tf_op jit(solution)/shard_map/dot_general | solution.py:109
  676.4 71.0 %reduce-scatter.2.cloned.1.call-done = f32[64,8192]{1,0:T(8,128)} async-done(((f32[256,8192]{1,0:T(8,128)}), f32[64,8192]{1,0:T(8,128)}) %reduce-scatter.2.cloned.1.call-update) | async-done | bytes 2097168 | tf_op jit(solution)/shard_map/reduce_scatter | solution.py:114
  747.4 2.7 convert_element_type.43
  (46 shorter events, 2.0 us)
Async XLA Ops:
  6.5 0.7 copy-start
  6.5 0.7 copy-start.6
  6.5 1.0 copy-start.5
  6.5 652.8 %all-gather.2.cloned.1.call-start = ((), (), s32[]{:S(2)}) async-start(), calls=%async_computation.2 | async-start | bytes 41943040 | tf_op jit(solution)/shard_map/all_gather | solution.py:111
  18.9 6.8 copy-start.3
  18.9 212.8 %all-to-all-start = ((bf16[4,1024,512]{2,1,0:T(8,128)(2,1)}), bf16[4,1024,512]{2,1,0:T(8,128)(2,1)}, u32[]{:S(2)}, u32[]{:S(2)}) async-start(bf16[4,1024,512]{2,1,0:T(8,128)(2,1)} %fusion.3), calls=%async_computation | async-start | bytes 8388608 | tf_op jit(solution)/shard_map/all_to_all | solution.py:78
  25.6 3.3 copy-start.7
  25.6 3.7 copy-start.4
  25.6 721.8 %reduce-scatter.2.cloned.1.call-start = ((), (), s32[]{:S(2)}) async-start(), calls=%async_computation.3 | async-start | bytes 10485760 | tf_op jit(solution)/shard_map/reduce_scatter | solution.py:114
  236.2 1.2 copy-start.2
  236.2 1.2 copy-start.8
  676.4 73.7 %copy-start.1 = (s32[8,8]{1,0:T(8,128)S(1)}, s32[8,8]{1,0:T(8,128)}, u32[]{:S(2)}) copy-start(s32[8,8]{1,0:T(8,128)} %param.16) | copy-start | bytes 772
Sparse Core Ops, SparseCore 0:
  8.9 650.3 all-gather.1
  676.5 70.8 reduce-scatter.1
where the time goes:
time: 757 us
  waiting for transfers between devices  685 us (90%)
  matrix products  27 us (4%)
  between operations  13.6 us (2%)
  local copies, waits for them, and re-layouts  12.7 us (2%)
  other arithmetic  11.9 us (2%)
    all_gather x1, waiting for transfers between devices, per_device(): lax.all_gather(out_weight, 'pool', axis=1, tiled=True)  412 us
    all_to_all x1, waiting for transfers between devices, per_device(): lax.all_to_all(outgoing.reshape(pool_size, capacity * block_rows, rank_wi...  201 us
    reduce_scatter x1, waiting for transfers between devices, per_device(): lax.psum_scatter(partial_rows, ('heads', 'sub'), scatter_dimension=0, til...  71 us
    dot_general x1, matrix products, per_device(): jnp.dot(attended, lax.all_gather(out_weight, 'pool', axis=1, tiled=True),...  17 us
  transfers between devices with their start and end apart: 3, of which 3 were waited for; matrix products, arithmetic and copies ran while one was open for 4% of the time, Pallas kernels for 0%

commit v1 on v0

v1 whole, which is shorter than its diff:
```python
import math

import jax
import jax.numpy as jnp
from jax import lax
from jax.sharding import PartitionSpec as P

BLK = 128
CHUNKS = 2


def rms_scale(values, gain):
    return values * lax.rsqrt(jnp.mean(values * values, axis=-1, keepdims=True) + 1e-05) * gain


def pair_rank(holders):
    count = holders.shape[1]
    same = holders[:, :, None] == holders[:, None, :]
    earlier = jnp.arange(count)[None, :] < jnp.arange(count)[:, None]
    return jnp.sum((same & earlier[None]).astype(jnp.int32), axis=2)


def shift(values, axis, step):
    size = lax.axis_size(axis)
    return lax.ppermute(values, axis, [(i, (i + step) % size) for i in range(size)])


def exchange_sum(pieces, axis):
    size = lax.axis_size(axis)
    index = lax.axis_index(axis)
    total = lax.dynamic_index_in_dim(pieces, index, 0, keepdims=False)
    for step in range(1, size):
        away = lax.dynamic_index_in_dim(pieces, (index + step) % size, 0, keepdims=False)
        total = total + shift(away.astype(jnp.bfloat16), axis, step).astype(jnp.float32)
    return total


def fetch_latents(latent_store, place_holder, place_block, serving_request, items):
    pool_size = lax.axis_size("pool")
    pool_index = lax.axis_index("pool")
    share_count = lax.axis_size(("heads", "sub"))
    share = lax.axis_index(("heads", "sub"))
    capacity = 2 * ((items + pool_size - 1) // pool_size)
    total_requests = serving_request.shape[0]
    request_ids = jnp.arange(total_requests, dtype=jnp.int32)
    selector = (serving_request[:, None] == request_ids[None, :]).astype(jnp.int32)
    holders = jnp.dot(selector, place_holder).reshape(pool_size, items)
    blocks = jnp.dot(selector, place_block).reshape(pool_size, items)
    ranks = pair_rank(holders)
    slot_ids = jnp.arange(capacity, dtype=jnp.int32)
    matched = (holders[:, None, :] == pool_index) & (ranks[:, None, :] == slot_ids[None, :, None])
    send_block = jnp.sum(jnp.where(matched, blocks[:, None, :], 0), axis=2)
    rows = BLK // share_count
    rank_width = latent_store.shape[1]
    store = latent_store.reshape(-1, rows, rank_width)
    outgoing = jnp.take(store, send_block.reshape(-1) * share_count + share, axis=0)
    incoming = lax.all_to_all(
        outgoing.reshape(pool_size, capacity * rows, rank_width),
        "pool",
        split_axis=0,
        concat_axis=0,
        tiled=True,
    )
    my_holders = lax.dynamic_index_in_dim(holders, pool_index, 0, keepdims=False)
    my_ranks = lax.dynamic_index_in_dim(ranks, pool_index, 0, keepdims=False)
    chosen = jnp.take(
        incoming.reshape(pool_size * capacity, rows, rank_width),
        my_holders * capacity + my_ranks,
        axis=0,
    )
    return selector, chosen


def per_device(
    queries,
    latent_store,
    kv_up,
    q_gain,
    k_gain,
    out_weight,
    place_holder,
    place_block,
    image_count,
    serving_request,
):
    pool_size = lax.axis_size("pool")
    pool_index = lax.axis_index("pool")
    heads_size = lax.axis_size("heads")
    sub_size = lax.axis_size("sub")
    share_count = heads_size * sub_size
    requests_here, text_rows, query_width = queries.shape
    blocks_each = place_holder.shape[1]
    items = requests_here * blocks_each
    heads_here, head_width = kv_up.shape[1], kv_up.shape[3]
    per_group = query_width // (heads_here * head_width)
    selector, chosen = fetch_latents(
        latent_store, place_holder, place_block, serving_request, items
    )
    rank_width = chosen.shape[2]
    share_rows = chosen.shape[1]
    image_slots = blocks_each * BLK
    latents = lax.all_gather(
        chosen.reshape(requests_here, blocks_each * share_rows, rank_width),
        ("heads", "sub"),
        axis=1,
        tiled=True,
    )
    projected = jnp.einsum("rsk,kgcd->rsgcd", latents, kv_up, preferred_element_type=jnp.float32)
    keys = rms_scale(projected[:, :, :, 0], k_gain).astype(jnp.bfloat16)
    values = projected[:, :, :, 1].astype(jnp.bfloat16)
    slots = jnp.arange(image_slots, dtype=jnp.int32)
    share_of, within = slots // (blocks_each * share_rows), slots % (blocks_each * share_rows)
    positions = (within // share_rows) * BLK + share_of * share_rows + within % share_rows
    count_here = lax.dynamic_slice_in_dim(
        jnp.dot(selector, image_count), pool_index * requests_here, requests_here
    )
    live = positions[None, :] < count_here[:, None]
    softmax_scale = 1.0 / math.sqrt(head_width)
    segment = requests_here * text_rows // share_count
    part_rows = segment // CHUNKS
    shaped = queries.reshape(
        requests_here,
        share_count // requests_here,
        CHUNKS,
        part_rows,
        heads_here,
        per_group,
        head_width,
    )
    outputs = []
    for chunk in range(CHUNKS):
        part = shaped[:, :, chunk].reshape(requests_here, -1, heads_here, per_group, head_width)
        normed = rms_scale(part.astype(jnp.float32), q_gain).astype(jnp.bfloat16)
        scores = (
            jnp.einsum("rtgqd,rsgd->rgqts", normed, keys, preferred_element_type=jnp.float32)
            * softmax_scale
        )
        expo = jnp.where(live[:, None, None, None, :], jnp.exp(scores), jnp.zeros((), jnp.float32))
        probs = (expo / jnp.sum(expo, axis=-1, keepdims=True)).astype(jnp.bfloat16)
        attended = jnp.einsum(
            "rgqts,rsgd->rtgqd", probs, values, preferred_element_type=jnp.float32
        )
        attended = attended.astype(jnp.bfloat16).reshape(share_count * part_rows, query_width)
        rows = lax.all_gather(attended, "pool", axis=0, tiled=True)
        partial = jnp.dot(rows, out_weight, preferred_element_type=jnp.float32)
        columns = partial.shape[1]
        partial = partial.reshape(pool_size, heads_size, sub_size, part_rows, columns)
        by_sub = exchange_sum(jnp.moveaxis(partial, 2, 0), "sub")
        by_heads = exchange_sum(jnp.moveaxis(by_sub, 1, 0), "heads")
        mine = by_heads.astype(jnp.bfloat16)
        arrived = lax.all_to_all(mine, "pool", split_axis=0, concat_axis=0, tiled=True)
        outputs.append(jnp.moveaxis(arrived, 0, 1).reshape(part_rows, pool_size * columns))
    return jnp.concatenate(outputs, axis=0)


def solution(mesh):
    in_specs = (
        P(("groups", "pool"), None, ("heads", "sub")),
        P(("groups", "pool"), None),
        P(None, ("heads", "sub"), None, None),
        P(),
        P(),
        P(("heads", "sub"), "pool"),
        P("groups", None),
        P("groups", None),
        P("groups"),
        P("groups"),
    )
    out_specs = P(("groups", "pool", "heads", "sub"), None)
    return jax.shard_map(
        per_device, mesh=mesh, in_specs=in_specs, out_specs=out_specs, check_vma=False
    )
```

time: 757 us -> 245 us (0.32)
  waiting for transfers between devices: 685 us -> 154 us
  starting transfers between devices: 6.74 us -> 15.8 us
    all_gather x1 -> x3, waiting for transfers between devices: 412 us -> 92 us  [the longest x2 75.2 us: per_device(): rows = lax.all_gather(attended, 'pool', axis=0, tiled=True)]
    all_to_all x1 -> x3, waiting for transfers between devices: 201 us -> 44.9 us  [the longest x1 24.2 us: fetch_latents(): lax.all_to_all(outgoing.reshape(pool_size, capacity * rows, rank_width),...]
    reduce_scatter x1 -> x0, waiting for transfers between devices: 71 us -> none  [per_device(): lax.psum_scatter(partial_rows, ('heads', 'sub'), scatter_dimension=0, til...]
    ppermute x0 -> x4, waiting for transfers between devices: none -> 16.7 us  [shift(): lax.ppermute(values, axis, [(i, (i + step) % size) for i in range(size)])]
    dot_general x5 -> x6, matrix products: 18.9 us -> 19.9 us  [the longest x2 15.1 us: per_device(): partial = jnp.dot(rows, out_weight, preferred_element_type=jnp.float32)]
  transfers between devices with their start and end apart: 3 -> 10, of which waited for: 3 -> 8; matrix products, arithmetic and copies ran while one was open for 4% -> 14% of each run, Pallas kernels for 0% -> 0%
where the time goes in v1:
time: 245 us; the launch traced here: 244 us
  waiting for transfers between devices  154 us (63%)
  matrix products  33 us (13%)
  local copies, waits for them, and re-layouts  16.4 us (7%)
  starting transfers between devices  15.8 us (6%)
  between operations  13.5 us (6%)
  other arithmetic  12.1 us (5%)
    all_gather x2, waiting for transfers between devices, per_device(): rows = lax.all_gather(attended, 'pool', axis=0, tiled=True)  75.2 us
    all_to_all x1, waiting for transfers between devices, fetch_latents(): lax.all_to_all(outgoing.reshape(pool_size, capacity * rows, rank_width),...  24.2 us
    all_to_all x2, waiting for transfers between devices, per_device(): lax.all_to_all(mine, 'pool', split_axis=0, concat_axis=0, tiled=True)  20.7 us
    all_gather x1, waiting for transfers between devices, per_device(): lax.all_gather(chosen.reshape(requests_here, blocks_each * share_rows, ra...  16.8 us
    ppermute x4, waiting for transfers between devices, shift(): lax.ppermute(values, axis, [(i, (i + step) % size) for i in range(size)])  16.7 us
    dot_general x2, matrix products, per_device(): partial = jnp.dot(rows, out_weight, preferred_element_type=jnp.float32)  15.1 us
    dot_general x2, matrix products, per_device(): jnp.einsum('rgqts,rsgd->rtgqd', probs, values, preferred_element_type=jnp...  7.84 us
    unnamed x28, local copies, waits for them, and re-layouts  7.45 us
  transfers between devices with their start and end apart: 10, of which 8 were waited for; matrix products, arithmetic and copies ran while one was open for 14% of the time, Pallas kernels for 0%

profile of v1, /device:TPU:0, one launch (start us, length us, event | category | flops | bytes accessed | tf_op | source)
XLA Modules:
  0.0 244.5 jit_solution(1710615136481472042)
XLA Ops:
  9.8 2.9 %gather_fusion = bf16[32,32,512]{2,1,0:T(8,128)(2,1)S(1)} fusion(bf16[128,32,512]{2,1,0:T(8,128)(2,1)} %bitcast.145, s32[1024]{0:T(1024)S(1)} %pad_clamp_fusion.1), kind=kCustom, calls=%fused_computation | custom fusion | bytes 2097280 | tf_op jit(solution)/shard_map/jit(_take)/gather | solution.py:56
  13.8 6.3 %all-to-all-start = ((bf16[4,256,512]{2,1,0:T(8,128)(2,1)}), bf16[4,256,512]{2,1,0:T(8,128)(2,1)S(1)}, u32[]{:S(2)}, u32[]{:S(2)}) async-start(bf16[4,256,512]{2,1,0:T(8,128)(2,1)} %bitcast_select_fusion), calls=%async_computation | async-start | bytes 2097152 | tf_op jit(solution)/shard_map/all_to_all | solution.py:57
  21.7 24.2 %all-to-all-done = bf16[4,256,512]{2,1,0:T(8,128)(2,1)S(1)} async-done(((bf16[4,256,512]{2,1,0:T(8,128)(2,1)}), bf16[4,256,512]{2,1,0:T(8,128)(2,1)S(1)}, u32[]{:S(2)}, u32[]{:S(2)}) %all-to-all-start) | async-done | bytes 1048608 | tf_op jit(solution)/shard_map/all_to_all | solution.py:57
  48.2 1.5 copy.72
  52.5 16.8 %all-gather.4.cloned.1.call-done = bf16[2,1024,512]{2,1,0:T(8,128)(2,1)} async-done(((bf16[2,256,512]{2,1,0:T(8,128)(2,1)}), bf16[2,1024,512]{2,1,0:T(8,128)(2,1)}) %all-gather.4.cloned.1.call-update) | async-done | bytes 2097168 | tf_op jit(solution)/shard_map/all_gather | solution.py:102
  69.3 2.9 %fusion.6 = f32[2,1024,2,2,128]{1,4,3,2,0:T(8,128)S(1)} fusion(bf16[2,1024,512]{2,1,0:T(8,128)(2,1)} %all-gather.4.cloned.1.call-done, bf16[512,2,2,128]{0,3,2,1:T(8,128)(2,1)S(1)} %copy.44), kind=kOutput, calls=%fused_computation.14 | convolution fusion | flops 1073741824 | bytes 6815744 | tf_op jit(solution)/shard_map/rsk,kgcd->rsgcd/dot_general | solution.py:108
  74.5 3.9 %bitcast_reduce_fusion.1 = (f32[2,2,8,64]{3,2,1,0:T(8,128)S(1)}, f32[2,2,8,64]{3,2,1,0:T(8,128)S(1)}, f32[2,2,1024,64,8]{2,3,4,1,0:T(8,128)S(1)}) fusion(pred[2,1024]{1,0:T(4,128)(4,1)S(1)} %broadcast_compare_fusion, f32[2,2,1024,64,8]{2,3,4,1,0:T(8,128)S(1)} %fusion.34, f32[2,64,2,8,128]{4,3,2,1,0:T(8,128)S(1)} %bitcast.141, f32[128]{0:T(128)S(1)} %copy-done.9, ...), kind=kOutput, calls=%fused_computation.6 | convolution fusion | flops 551809024 | bytes 19977216 | tf_op jit(solution)/shard_map/rtgqd,rsgd->rgqts/dot_general | solution.py:135
  78.4 2.0 fusion.14
  82.1 5.8 %fusion.17 = bf16[2,64,2,8,128]{4,1,3,2,0:T(8,128)(2,1)S(1)} fusion(f32[2,2,1024,64,8]{2,3,4,1,0:T(8,128)} %copy-done.3, f32[2,2,8,64]{3,2,1,0:T(8,128)S(1)} %get-tuple-element.8, pred[2,1024]{1,0:T(4,128)(4,1)S(1)} %broadcast_compare_fusion, f32[2,1024,2,2,128]{1,4,3,2,0:T(8,128)} %copy-done.2), kind=kOutput, calls=%fused_computation.25 | convolution fusion | flops 545521664 | bytes 9971712 | tf_op jit(solution)/shard_map/rgqts,rsgd->rtgqd/dot_general | solution.py:140
  89.3 38.6 %all-gather.6.cloned.1.call-done = bf16[512,2048]{1,0:T(8,128)(2,1)} async-done(((bf16[128,2048]{1,0:T(8,128)(2,1)}), bf16[512,2048]{1,0:T(8,128)(2,1)}) %all-gather.6.cloned.1.call-update) | async-done | bytes 2097168 | tf_op jit(solution)/shard_map/all_gather | solution.py:144
  127.9 7.6 %fusion.80 = f32[512,2048]{1,0:T(8,128)S(1)} fusion(bf16[512,2048]{1,0:T(8,128)(2,1)} %all-gather.6.cloned.1.call-done, bf16[2048,2048]{1,0:T(8,128)(2,1)} %param.15), kind=kOutput, calls=%fused_computation.123 | convolution fusion | flops 4294967296 | bytes 14680064 | tf_op jit(solution)/shard_map/dot_general | solution.py:145
  135.5 1.9 copy-done.6
  137.6 36.5 %all-gather.8.cloned.1.call-done = bf16[512,2048]{1,0:T(8,128)(2,1)} async-done(((bf16[128,2048]{1,0:T(8,128)(2,1)}), bf16[512,2048]{1,0:T(8,128)(2,1)}) %all-gather.8.cloned.1.call-update) | async-done | bytes 2097168 | tf_op jit(solution)/shard_map/all_gather | solution.py:144
  174.2 7.6 %fusion.81 = f32[512,2048]{1,0:T(8,128)S(1)} fusion(bf16[512,2048]{1,0:T(8,128)(2,1)} %all-gather.8.cloned.1.call-done, bf16[2048,2048]{1,0:T(8,128)(2,1)} %param.15), kind=kOutput, calls=%fused_computation.124 | convolution fusion | flops 4294967296 | bytes 14680064 | tf_op jit(solution)/shard_map/dot_general | solution.py:145
  181.8 2.0 copy-done.4
  184.0 2.0 bitcast_add_fusion.1
  186.1 1.5 collective-permute-start.1
  187.7 1.5 bitcast_add_fusion
  190.6 10.3 %collective-permute-done.1 = bf16[4,32,2048]{2,1,0:T(8,128)(2,1)S(1)} collective-permute-done((bf16[4,32,2048]{2,1,0:T(8,128)(2,1)S(1)}, bf16[4,32,2048]{2,1,0:T(8,128)(2,1)S(1)}, u32[]{:S(2)}, u32[]{:S(2)}) %collective-permute-start.1) | collective-permute-done | bytes 524320 | tf_op jit(solution)/shard_map/ppermute | solution.py:25
  201.8 3.5 %all-to-all-start.1 = ((bf16[4,32,2048]{2,1,0:T(8,128)(2,1)}), bf16[4,32,2048]{2,1,0:T(8,128)(2,1)S(1)}, u32[]{:S(2)}, u32[]{:S(2)}) async-start(bf16[4,32,2048]{2,1,0:T(8,128)(2,1)} %fusion.25), calls=%async_computation.1 | async-start | bytes 1048576 | tf_op jit(solution)/shard_map/all_to_all | solution.py:151
  205.3 6.4 %collective-permute-done.3 = bf16[4,32,2048]{2,1,0:T(8,128)(2,1)S(1)} collective-permute-done((bf16[4,32,2048]{2,1,0:T(8,128)(2,1)}, bf16[4,32,2048]{2,1,0:T(8,128)(2,1)S(1)}, u32[]{:S(2)}, u32[]{:S(2)}) %collective-permute-start.3) | collective-permute-done | bytes 524320 | tf_op jit(solution)/shard_map/ppermute | solution.py:25
  212.6 6.8 %all-to-all-done.1 = bf16[4,32,2048]{2,1,0:T(8,128)(2,1)S(1)} async-done(((bf16[4,32,2048]{2,1,0:T(8,128)(2,1)}), bf16[4,32,2048]{2,1,0:T(8,128)(2,1)S(1)}, u32[]{:S(2)}, u32[]{:S(2)}) %all-to-all-start.1) | async-done | bytes 524320 | tf_op jit(solution)/shard_map/all_to_all | solution.py:151
  219.4 3.5 %all-to-all-start.2 = ((bf16[4,32,2048]{2,1,0:T(8,128)(2,1)}), bf16[4,32,2048]{2,1,0:T(8,128)(2,1)S(1)}, u32[]{:S(2)}, u32[]{:S(2)}) async-start(bf16[4,32,2048]{2,1,0:T(8,128)(2,1)} %fusion.24), calls=%async_computation.2 | async-start | bytes 1048576 | tf_op jit(solution)/shard_map/all_to_all | solution.py:151
  222.9 13.9 %all-to-all-done.2 = bf16[4,32,2048]{2,1,0:T(8,128)(2,1)S(1)} async-done(((bf16[4,32,2048]{2,1,0:T(8,128)(2,1)}), bf16[4,32,2048]{2,1,0:T(8,128)(2,1)S(1)}, u32[]{:S(2)}, u32[]{:S(2)}) %all-to-all-start.2) | async-done | bytes 524320 | tf_op jit(solution)/shard_map/all_to_all | solution.py:151
  (86 shorter events, 21.1 us)
Async XLA Ops:
  6.5 0.7 copy-start
  9.8 37.7 %copy-start.8 = (bf16[512,2,2,128]{3,2,1,0:T(2,128)(2,1)S(1)}, bf16[512,2,2,128]{3,2,1,0:T(2,128)(2,1)}, u32[]{:S(2)}) copy-start(bf16[512,2,2,128]{3,2,1,0:T(2,128)(2,1)} %param.12) | copy-start | bytes 1572868
  13.8 32.0 %all-to-all-start = ((bf16[4,256,512]{2,1,0:T(8,128)(2,1)}), bf16[4,256,512]{2,1,0:T(8,128)(2,1)S(1)}, u32[]{:S(2)}, u32[]{:S(2)}) async-start(bf16[4,256,512]{2,1,0:T(8,128)(2,1)} %bitcast_select_fusion), calls=%async_computation | async-start | bytes 2097152 | tf_op jit(solution)/shard_map/all_to_all | solution.py:57
  20.1 30.7 %copy-start.11 = (s32[8]{0:T(128)S(1)}, s32[8]{0:T(128)}, u32[]{:S(2)}) copy-start(s32[8]{0:T(128)} %param.19) | copy-start | bytes 100
  20.2 30.7 %copy-start.12 = (s32[8]{0:T(128)S(1)}, s32[8]{0:T(128)}, u32[]{:S(2)}) copy-start(s32[8]{0:T(128)} %param.18) | copy-start | bytes 100
  20.2 49.1 %all-gather.4.cloned.1.call-start = ((), (), s32[]{:S(2)}) async-start(), calls=%async_computation.3 | async-start | bytes 2621440 | tf_op jit(solution)/shard_map/all_gather | solution.py:102
  47.4 80.5 %all-gather.6.cloned.1.call-start = ((), (), s32[]{:S(2)}) async-start(), calls=%async_computation.4 | async-start | bytes 2621440 | tf_op jit(solution)/shard_map/all_gather | solution.py:144
  52.4 20.0 %copy-start.9 = (f32[128]{0:T(128)S(1)}, f32[128]{0:T(128)}, u32[]{:S(2)}) copy-start(f32[128]{0:T(128)} %param.13) | copy-start | bytes 1540
  52.4 20.0 %copy-start.10 = (f32[128]{0:T(128)S(1)}, f32[128]{0:T(128)}, u32[]{:S(2)}) copy-start(f32[128]{0:T(128)} %param.14) | copy-start | bytes 1540
  72.2 6.2 %copy-start.2 = (f32[2,1024,2,2,128]{1,4,3,2,0:T(8,128)}, f32[2,1024,2,2,128]{1,4,3,2,0:T(8,128)S(1)}, u32[]{:S(2)}) copy-start(f32[2,1024,2,2,128]{1,4,3,2,0:T(8,128)S(1)} %fusion.6) | copy-start | bytes 12582916
  72.4 2.0 copy-start.7
  73.8 4.5 %copy-start.3 = (f32[2,2,1024,64,8]{2,3,4,1,0:T(8,128)}, f32[2,2,1024,64,8]{2,3,4,1,0:T(8,128)S(1)}, u32[]{:S(2)}) copy-start(f32[2,2,1024,64,8]{2,3,4,1,0:T(8,128)S(1)} %fusion.34) | copy-start | bytes 25165828
  81.8 92.4 %all-gather.8.cloned.1.call-start = ((), (), s32[]{:S(2)}) async-start(), calls=%async_computation.5 | async-start | bytes 2621440 | tf_op jit(solution)/shard_map/all_gather | solution.py:144
  135.5 1.9 copy-start.6
  137.6 46.4 %collective-permute-start = (bf16[4,2,32,2048]{3,2,1,0:T(8,128)(2,1)S(1)}, bf16[4,2,32,2048]{3,2,1,0:T(8,128)(2,1)S(1)}, u32[]{:S(2)}, u32[]{:S(2)}) collective-permute-start(bf16[4,2,32,2048]{3,2,1,0:T(8,128)(2,1)S(1)} %fusion.21), channel_id=1, source_target_pairs={{0,1},{1,0},{2,3},{3,2},{4,5},{5,4},{6,7},{7,6},{8,9},{9,8},{10,11... | collective-permute-start | bytes 3145736 | tf_op jit(solution)/shard_map/ppermute | solution.py:25
  181.8 2.0 copy-start.4
  183.9 3.8 %collective-permute-start.2 = (bf16[4,2,32,2048]{3,2,1,0:T(8,128)(2,1)S(1)}, bf16[4,2,32,2048]{3,2,1,0:T(8,128)(2,1)}, u32[]{:S(2)}, u32[]{:S(2)}) collective-permute-start(bf16[4,2,32,2048]{3,2,1,0:T(8,128)(2,1)S(1)} %fusion.22), channel_id=1, source_target_pairs={{0,1},{1,0},{2,3},{3,2},{4,5},{5,4},{6,7},{7,6},{8,9},{9,8},{10,11... | collective-permute-start | bytes 3145736 | tf_op jit(solution)/shard_map/ppermute | solution.py:25
  184.0 3.7 %copy-start.5 = (f32[512,2048]{1,0:T(8,128)S(1)}, f32[512,2048]{1,0:T(8,128)}, u32[]{:S(2)}) copy-start(f32[512,2048]{1,0:T(8,128)} %copy-done.4) | copy-start | bytes 12582916
  186.1 14.8 %collective-permute-start.1 = (bf16[4,32,2048]{2,1,0:T(8,128)(2,1)S(1)}, bf16[4,32,2048]{2,1,0:T(8,128)(2,1)S(1)}, u32[]{:S(2)}, u32[]{:S(2)}) collective-permute-start(bf16[4,32,2048]{2,1,0:T(8,128)(2,1)S(1)} %fusion.30), channel_id=1, source_target_pairs={{0,2},{2,0},{1,3},{3,1},{4,6},{6,4},{5,7},{7,5},{8,10},{10,8},{9,1... | collective-permute-start | bytes 1572872 | tf_op jit(solution)/shard_map/ppermute | solution.py:25
  190.0 21.7 %collective-permute-start.3 = (bf16[4,32,2048]{2,1,0:T(8,128)(2,1)}, bf16[4,32,2048]{2,1,0:T(8,128)(2,1)S(1)}, u32[]{:S(2)}, u32[]{:S(2)}) collective-permute-start(bf16[4,32,2048]{2,1,0:T(8,128)(2,1)} %fusion.31), channel_id=1, source_target_pairs={{0,2},{2,0},{1,3},{3,1},{4,6},{6,4},{5,7},{7,5},{8,10},{10,8},{9,1... | collective-permute-start | bytes 1572872 | tf_op jit(solution)/shard_map/ppermute | solution.py:25
  200.9 37.0 %copy-start.1 = (s32[8,8]{1,0:T(8,128)S(1)}, s32[8,8]{1,0:T(8,128)}, u32[]{:S(2)}) copy-start(s32[8,8]{1,0:T(8,128)} %param.16) | copy-start | bytes 772
  201.8 17.6 %all-to-all-start.1 = ((bf16[4,32,2048]{2,1,0:T(8,128)(2,1)}), bf16[4,32,2048]{2,1,0:T(8,128)(2,1)S(1)}, u32[]{:S(2)}, u32[]{:S(2)}) async-start(bf16[4,32,2048]{2,1,0:T(8,128)(2,1)} %fusion.25), calls=%async_computation.1 | async-start | bytes 1048576 | tf_op jit(solution)/shard_map/all_to_all | solution.py:151
  219.4 17.4 %all-to-all-start.2 = ((bf16[4,32,2048]{2,1,0:T(8,128)(2,1)}), bf16[4,32,2048]{2,1,0:T(8,128)(2,1)S(1)}, u32[]{:S(2)}, u32[]{:S(2)}) async-start(bf16[4,32,2048]{2,1,0:T(8,128)(2,1)} %fusion.24), calls=%async_computation.2 | async-start | bytes 1048576 | tf_op jit(solution)/shard_map/all_to_all | solution.py:151
Sparse Core Ops, SparseCore 0:
  47.5 21.6 all-gather.3
  81.9 45.9 all-gather.5
  129.5 44.6 all-gather.7

commit v2 on v1

--- a/solution.py
+++ b/solution.py
@@ -20,19 +20,28 @@
     return jnp.sum((same & earlier[None]).astype(jnp.int32), axis=2)
 
 
-def shift(values, axis, step):
-    size = lax.axis_size(axis)
-    return lax.ppermute(values, axis, [(i, (i + step) % size) for i in range(size)])
+def swap(values, axis, flip):
+    return lax.ppermute(values, axis, [(i, i ^ flip) for i in range(lax.axis_size(axis))])
 
 
-def exchange_sum(pieces, axis):
-    size = lax.axis_size(axis)
-    index = lax.axis_index(axis)
-    total = lax.dynamic_index_in_dim(pieces, index, 0, keepdims=False)
-    for step in range(1, size):
-        away = lax.dynamic_index_in_dim(pieces, (index + step) % size, 0, keepdims=False)
-        total = total + shift(away.astype(jnp.bfloat16), axis, step).astype(jnp.float32)
-    return total
+def spread_over_pool(block):
+    index = lax.axis_index("pool")
+    at_end = (index == 0) | (index == 3)
+    across = swap(block, "pool", 3)
+    beside = swap(block, "pool", 1)
+    passed = jnp.where(at_end, block, across)
+    second = lax.ppermute(passed, "pool", [(0, 2), (3, 1), (1, 0), (2, 3)])
+    return [block, beside, second, across]
+
+
+def reduce_shares(partial):
+    axes = ("heads", "sub")
+    share = lax.axis_index(axes)
+    total = lax.dynamic_index_in_dim(partial, share, 0, keepdims=False)
+    for flip in range(1, lax.axis_size(axes)):
+        away = lax.dynamic_index_in_dim(partial, share ^ flip, 0, keepdims=False)
+        total = total + swap(away.astype(jnp.bfloat16), axes, flip).astype(jnp.float32)
+    return total.astype(jnp.bfloat16)
 
 
 def fetch_latents(latent_store, place_holder, place_block, serving_request, items):
@@ -51,24 +60,16 @@
     matched = (holders[:, None, :] == pool_index) & (ranks[:, None, :] == slot_ids[None, :, None])
     send_block = jnp.sum(jnp.where(matched, blocks[:, None, :], 0), axis=2)
     rows = BLK // share_count
-    rank_width = latent_store.shape[1]
-    store = latent_store.reshape(-1, rows, rank_width)
-    outgoing = jnp.take(store, send_block.reshape(-1) * share_count + share, axis=0)
-    incoming = lax.all_to_all(
-        outgoing.reshape(pool_size, capacity * rows, rank_width),
-        "pool",
-        split_axis=0,
-        concat_axis=0,
-        tiled=True,
-    )
+    store = latent_store.reshape(-1, rows, latent_store.shape[1])
+    pieces = []
+    for flip in range(pool_size):
+        wanted = lax.dynamic_index_in_dim(send_block, pool_index ^ flip, 0, keepdims=False)
+        piece = store.at[wanted * share_count + share].get(mode="promise_in_bounds")
+        pieces.append(piece if flip == 0 else swap(piece, "pool", flip))
     my_holders = lax.dynamic_index_in_dim(holders, pool_index, 0, keepdims=False)
     my_ranks = lax.dynamic_index_in_dim(ranks, pool_index, 0, keepdims=False)
-    chosen = jnp.take(
-        incoming.reshape(pool_size * capacity, rows, rank_width),
-        my_holders * capacity + my_ranks,
-        axis=0,
-    )
-    return selector, chosen
+    chosen = jnp.concatenate(pieces, axis=0).at[(my_holders ^ pool_index) * capacity + my_ranks]
+    return selector, chosen.get(mode="promise_in_bounds")
 
 
 def per_device(
@@ -88,6 +89,7 @@
     heads_size = lax.axis_size("heads")
     sub_size = lax.axis_size("sub")
     share_count = heads_size * sub_size
+    share = lax.axis_index(("heads", "sub"))
     requests_here, text_rows, query_width = queries.shape
     blocks_each = place_holder.shape[1]
     items = requests_here * blocks_each
@@ -99,25 +101,27 @@
     rank_width = chosen.shape[2]
     share_rows = chosen.shape[1]
     image_slots = blocks_each * BLK
-    latents = lax.all_gather(
-        chosen.reshape(requests_here, blocks_each * share_rows, rank_width),
-        ("heads", "sub"),
-        axis=1,
-        tiled=True,
-    )
+    chosen = chosen.reshape(requests_here, blocks_each * share_rows, rank_width)
+    over_heads = [chosen] + [swap(chosen, "heads", flip) for flip in range(1, heads_size)]
+    quarters = []
+    for part in over_heads:
+        quarters += [part] + [swap(part, "sub", flip) for flip in range(1, sub_size)]
+    latents = jnp.concatenate(quarters, axis=1)
     projected = jnp.einsum("rsk,kgcd->rsgcd", latents, kv_up, preferred_element_type=jnp.float32)
     keys = rms_scale(projected[:, :, :, 0], k_gain).astype(jnp.bfloat16)
     values = projected[:, :, :, 1].astype(jnp.bfloat16)
     slots = jnp.arange(image_slots, dtype=jnp.int32)
     share_of, within = slots // (blocks_each * share_rows), slots % (blocks_each * share_rows)
-    positions = (within // share_rows) * BLK + share_of * share_rows + within % share_rows
+    positions = (
+        (within // share_rows) * BLK + (share_of ^ share) * share_rows + within % share_rows
+    )
     count_here = lax.dynamic_slice_in_dim(
         jnp.dot(selector, image_count), pool_index * requests_here, requests_here
     )
     live = positions[None, :] < count_here[:, None]
     softmax_scale = 1.0 / math.sqrt(head_width)
-    segment = requests_here * text_rows // share_count
-    part_rows = segment // CHUNKS
+    part_rows = requests_here * text_rows // share_count // CHUNKS
+    columns = out_weight.shape[1]
     shaped = queries.reshape(
         requests_here,
         share_count // requests_here,
@@ -127,7 +131,7 @@
         per_group,
         head_width,
     )
-    outputs = []
+    output = jnp.zeros((CHUNKS * part_rows, pool_size * columns), jnp.bfloat16)
     for chunk in range(CHUNKS):
         part = shaped[:, :, chunk].reshape(requests_here, -1, heads_here, per_group, head_width)
         normed = rms_scale(part.astype(jnp.float32), q_gain).astype(jnp.bfloat16)
@@ -141,16 +145,23 @@
             "rgqts,rsgd->rtgqd", probs, values, preferred_element_type=jnp.float32
         )
         attended = attended.astype(jnp.bfloat16).reshape(share_count * part_rows, query_width)
-        rows = lax.all_gather(attended, "pool", axis=0, tiled=True)
-        partial = jnp.dot(rows, out_weight, preferred_element_type=jnp.float32)
-        columns = partial.shape[1]
-        partial = partial.reshape(pool_size, heads_size, sub_size, part_rows, columns)
-        by_sub = exchange_sum(jnp.moveaxis(partial, 2, 0), "sub")
-        by_heads = exchange_sum(jnp.moveaxis(by_sub, 1, 0), "heads")
-        mine = by_heads.astype(jnp.bfloat16)
-        arrived = lax.all_to_all(mine, "pool", split_axis=0, concat_axis=0, tiled=True)
-        outputs.append(jnp.moveaxis(arrived, 0, 1).reshape(part_rows, pool_size * columns))
-    return jnp.concatenate(outputs, axis=0)
+        if pool_size != 4:
+            rows = lax.all_gather(attended, "pool", axis=0, tiled=True)
+            partial = jnp.dot(rows, out_weight, preferred_element_type=jnp.float32)
+            partial = partial.reshape(pool_size, share_count, part_rows, columns)
+            mine = reduce_shares(jnp.moveaxis(partial, 1, 0))
+            back = lax.all_to_all(mine, "pool", split_axis=0, concat_axis=0, tiled=True)
+            back = jnp.moveaxis(back, 0, 1).reshape(part_rows, pool_size * columns)
+            output = lax.dynamic_update_slice(output, back, (chunk * part_rows, 0))
+            continue
+        for flip, rows in enumerate(spread_over_pool(attended)):
+            partial = jnp.dot(rows, out_weight, preferred_element_type=jnp.float32)
+            mine = reduce_shares(partial.reshape(share_count, part_rows, columns))
+            back = mine if flip == 0 else swap(mine, "pool", flip)
+            output = lax.dynamic_update_slice(
+                output, back, (chunk * part_rows, (pool_index ^ flip) * columns)
+            )
+    return output
 
 
 def solution(mesh):

time: 245 us -> 205 us (0.84)
  waiting for transfers between devices: 154 us -> 92.5 us
  starting transfers between devices: 15.8 us -> 43.8 us
  between operations: 13.5 us -> 0.72 us
  matrix products: 33 us -> 40.3 us
  other arithmetic: 12.1 us -> 5.06 us
  local copies, waits for them, and re-layouts: 16.4 us -> 21.8 us
    all_gather x3 -> x0, waiting for transfers between devices: 92 us -> none  [the longest x2 75.2 us: per_device(): rows = lax.all_gather(attended, 'pool', axis=0, tiled=True)]
    ppermute x4 -> x42, waiting for transfers between devices: 16.7 us -> 92.5 us  [the longest x40 92.5 us: swap(): lax.ppermute(values, axis, [(i, i ^ flip) for i in range(lax.axis_size(ax...]
    all_to_all x3 -> x0, waiting for transfers between devices: 44.9 us -> none  [the longest x1 24.2 us: fetch_latents(): lax.all_to_all(outgoing.reshape(pool_size, capacity * rows, rank_width),...]
    ppermute x4 -> x42, starting transfers between devices: 2.28 us -> 43.8 us  [the longest x40 42.6 us: swap(): lax.ppermute(values, axis, [(i, i ^ flip) for i in range(lax.axis_size(ax...]
    all_to_all x3 -> x0, starting transfers between devices: 13.3 us -> none  [the longest x2 6.94 us: per_device(): lax.all_to_all(mine, 'pool', split_axis=0, concat_axis=0, tiled=True)]
    gather x2 -> x5, local copies, waits for them, and re-layouts: 3.44 us -> 11.6 us  [the longest x4 11 us: fetch_latents(): piece = store.at[wanted * share_count + share].get(mode='promise_in_bounds')]
    dot_general x2 -> x8, matrix products: 15.1 us -> 21.7 us  [per_device(): partial = jnp.dot(rows, out_weight, preferred_element_type=jnp.float32)]
    add x4 -> x1, other arithmetic: 4.22 us -> 0.01 us  [per_device(): within // share_rows * BLK + (share_of ^ share) * share_rows]
  transfers between devices with their start and end apart: 10 -> 42, of which waited for: 8 -> 22; matrix products, arithmetic and copies ran while one was open for 14% -> 23% of each run, Pallas kernels for 0% -> 0%
where the time goes in v2:
time: 205 us; the launch traced here: 204 us
  waiting for transfers between devices  92.5 us (45%)
  starting transfers between devices  43.8 us (21%)
  matrix products  40.3 us (20%)
  local copies, waits for them, and re-layouts  21.8 us (11%)
  other arithmetic  5.06 us (2%)
    ppermute x40, waiting for transfers between devices, swap(): lax.ppermute(values, axis, [(i, i ^ flip) for i in range(lax.axis_size(ax...  92.5 us
    ppermute x40, starting transfers between devices, swap(): lax.ppermute(values, axis, [(i, i ^ flip) for i in range(lax.axis_size(ax...  42.6 us
    dot_general x8, matrix products, per_device(): partial = jnp.dot(rows, out_weight, preferred_element_type=jnp.float32)  21.7 us
    gather x4, local copies, waits for them, and re-layouts, fetch_latents(): piece = store.at[wanted * share_count + share].get(mode='promise_in_bounds')  11 us
    dot_general x2, matrix products, per_device(): jnp.einsum('rgqts,rsgd->rtgqd', probs, values, preferred_element_type=jnp...  8.02 us
    dot_general x2, matrix products, per_device(): jnp.einsum('rtgqd,rsgd->rgqts', normed, keys, preferred_element_type=jnp....  5.26 us
  transfers between devices with their start and end apart: 42, of which 22 were waited for; matrix products, arithmetic and copies ran while one was open for 23% of the time, Pallas kernels for 0%

profile of v2, /device:TPU:0, one launch (start us, length us, event | category | flops | bytes accessed | tf_op | source)
XLA Modules:
  0.0 204.1 jit_solution(18130721255551171794)
XLA Ops:
  3.0 2.8 %gather_fusion.1 = bf16[8,32,512]{2,1,0:T(8,128)(2,1)S(1)} fusion(bf16[128,32,512]{2,1,0:T(8,128)(2,1)} %bitcast.272, s32[1024]{0:T(1024)S(1)} %pad_clamp_fusion.3), kind=kCustom, calls=%fused_computation.1 | custom fusion | bytes 524320 | tf_op jit(solution)/shard_map/gather | solution.py:67
  5.8 3.1 %collective-permute-start = (bf16[8,32,512]{2,1,0:T(8,128)(2,1)S(1)}, bf16[8,32,512]{2,1,0:T(8,128)(2,1)S(1)}, u32[]{:S(2)}, u32[]{:S(2)}) collective-permute-start(bf16[8,32,512]{2,1,0:T(8,128)(2,1)S(1)} %gather_fusion.1), channel_id=1, source_target_pairs={{0,4},{4,0},{8,12},{12,8},{1,5},{5,1},{9,13},{13,9},{2,6},{6,2},{1... | collective-permute-start | bytes 786440 | tf_op jit(solution)/shard_map/ppermute | solution.py:24
  8.9 2.7 %gather_fusion.2 = bf16[8,32,512]{2,1,0:T(8,128)(2,1)S(1)} fusion(bf16[128,32,512]{2,1,0:T(8,128)(2,1)} %bitcast.273, s32[1024]{0:T(1024)S(1)} %pad_clamp_fusion.2), kind=kCustom, calls=%fused_computation.2 | custom fusion | bytes 524320 | tf_op jit(solution)/shard_map/gather | solution.py:67
  11.6 2.7 %collective-permute-start.1 = (bf16[8,32,512]{2,1,0:T(8,128)(2,1)S(1)}, bf16[8,32,512]{2,1,0:T(8,128)(2,1)S(1)}, u32[]{:S(2)}, u32[]{:S(2)}) collective-permute-start(bf16[8,32,512]{2,1,0:T(8,128)(2,1)S(1)} %gather_fusion.2), channel_id=1, source_target_pairs={{0,8},{4,12},{8,0},{12,4},{1,9},{5,13},{9,1},{13,5},{2,10},{6,14},... | collective-permute-start | bytes 786440 | tf_op jit(solution)/shard_map/ppermute | solution.py:24
  14.3 2.7 %gather_fusion.3 = bf16[8,32,512]{2,1,0:T(8,128)(2,1)S(1)} fusion(bf16[128,32,512]{2,1,0:T(8,128)(2,1)} %bitcast.274, s32[1024]{0:T(1024)S(1)} %pad_clamp_fusion.1), kind=kCustom, calls=%fused_computation.3 | custom fusion | bytes 524320 | tf_op jit(solution)/shard_map/gather | solution.py:67
  17.1 2.8 %gather_fusion = bf16[8,32,512]{2,1,0:T(8,128)(2,1)S(1)} fusion(bf16[128,32,512]{2,1,0:T(8,128)(2,1)} %bitcast.275, s32[1024]{0:T(1024)S(1)} %pad_clamp_fusion.4), kind=kCustom, calls=%fused_computation | custom fusion | bytes 524320 | tf_op jit(solution)/shard_map/gather | solution.py:67
  19.9 13.1 %collective-permute-done.1 = bf16[8,32,512]{2,1,0:T(8,128)(2,1)S(1)} collective-permute-done((bf16[8,32,512]{2,1,0:T(8,128)(2,1)S(1)}, bf16[8,32,512]{2,1,0:T(8,128)(2,1)S(1)}, u32[]{:S(2)}, u32[]{:S(2)}) %collective-permute-start.1) | collective-permute-done | bytes 262176 | tf_op jit(solution)/shard_map/ppermute | solution.py:24
  38.8 6.3 %collective-permute-done.4 = bf16[2,256,512]{2,1,0:T(8,128)(2,1)} collective-permute-done((bf16[2,256,512]{2,1,0:T(8,128)(2,1)S(1)}, bf16[2,256,512]{2,1,0:T(8,128)(2,1)}, u32[]{:S(2)}, u32[]{:S(2)}) %collective-permute-start.4) | collective-permute-done | bytes 524320 | tf_op jit(solution)/shard_map/ppermute | solution.py:24
  47.3 2.7 %fusion.10 = f32[2,1024,2,2,128]{1,4,3,2,0:T(8,128)S(1)} fusion(bf16[2,256,512]{2,1,0:T(8,128)(2,1)} %collective-permute-done.5, bf16[2,256,512]{2,1,0:T(8,128)(2,1)} %collective-permute-done.4, bf16[2,256,512]{2,1,0:T(8,128)(2,1)} %collective-permute-done.3, bf16[2,256,512]{2,1,0:T(8,128)(2,1)S(1)} %bitcast.269, bf16[512,2,2,128]{0,3,2,1:T(8,128)(2,1)S(1)} %copy.42), kind=kOutput, calls=%fused_computation.22 | convolution fusion | flops 1082130432 | bytes 6815744 | tf_op jit(solution)/shard_map/rsk,kgcd->rsgcd/dot_general | solution.py:110
  51.6 3.9 %bitcast_reduce_fusion = (f32[2,2,8,64]{3,2,1,0:T(8,128)S(1)}, f32[2,2,8,64]{3,2,1,0:T(8,128)S(1)}, f32[2,2,1024,64,8]{2,3,4,1,0:T(8,128)S(1)}) fusion(pred[2,1024]{1,0:T(4,128)(4,1)S(1)} %broadcast_compare_fusion, f32[2,2,1024,64,8]{2,3,4,1,0:T(8,128)S(1)} %fusion.35, f32[2,64,2,8,128]{4,3,2,1,0:T(8,128)S(1)} %bitcast.265, f32[2,64,2,8]{1,3,2,0:T(8,128)S(1)} %copy.49, ...), kind=kOutput, calls=%fused_computation.6 | convolution fusion | flops 551809024 | bytes 19977216 | tf_op jit(solution)/shard_map/rtgqd,rsgd->rgqts/dot_general | solution.py:139
  59.2 2.6 %collective-permute-start.32 = (bf16[128,2048]{1,0:T(8,128)(2,1)}, bf16[128,2048]{1,0:T(8,128)(2,1)S(1)}, u32[]{:S(2)}, u32[]{:S(2)}) collective-permute-start(bf16[128,2048]{1,0:T(8,128)(2,1)} %reshape.365), channel_id=1, source_target_pairs={{0,12},{4,8},{8,4},{12,0},{1,13},{5,9},{9,5},{13,1},{2,14},{6,10},... | collective-permute-start | bytes 1572872 | tf_op jit(solution)/shard_map/ppermute | solution.py:24
  61.8 5.3 %collective-permute-start.27 = (bf16[128,2048]{1,0:T(8,128)(2,1)}, bf16[128,2048]{1,0:T(8,128)(2,1)}, u32[]{:S(2)}, u32[]{:S(2)}) collective-permute-start(bf16[128,2048]{1,0:T(8,128)(2,1)} %reshape.365), channel_id=1, source_target_pairs={{0,4},{4,0},{8,12},{12,8},{1,5},{5,1},{9,13},{13,9},{2,6},{6,2},{1... | collective-permute-start | bytes 1572872 | tf_op jit(solution)/shard_map/ppermute | solution.py:24
  67.3 5.8 %fusion.23 = bf16[2,64,2,8,128]{4,1,3,2,0:T(8,128)(2,1)S(1)} fusion(f32[2,2,1024,64,8]{2,3,4,1,0:T(8,128)} %copy-done.2, f32[2,2,8,64]{3,2,1,0:T(8,128)S(1)} %get-tuple-element.8, pred[2,1024]{1,0:T(4,128)(4,1)S(1)} %broadcast_compare_fusion, f32[2,1024,2,2,128]{1,4,3,2,0:T(8,128)} %copy-done.3), kind=kOutput, calls=%fused_computation.33 | convolution fusion | flops 545521664 | bytes 9971712 | tf_op jit(solution)/shard_map/rgqts,rsgd->rtgqd/dot_general | solution.py:144
  74.5 4.7 %fusion.1 = f32[4,32,2048]{2,1,0:T(8,128)S(1)} fusion(bf16[4,32,2048]{2,1,0:T(8,128)(2,1)S(1)} %dot_general.65, bf16[2048,2048]{1,0:T(8,128)(2,1)} %param.15), kind=kOutput, calls=%fused_computation.8 | convolution fusion | flops 1073741824 | bytes 9961472 | tf_op jit(solution)/shard_map/dot_general | solution.py:158
  79.2 4.7 %fusion.3 = f32[4,32,2048]{2,1,0:T(8,128)S(1)} fusion(bf16[4,32,2048]{2,1,0:T(8,128)(2,1)S(1)} %copy-done.4, bf16[2048,2048]{1,0:T(8,128)(2,1)} %param.15), kind=kOutput, calls=%fused_computation.10 | convolution fusion | flops 1073741824 | bytes 9961472 | tf_op jit(solution)/shard_map/dot_general | solution.py:158
  88.8 2.5 %collective-permute-done.7 = bf16[32,2048]{1,0:T(8,128)(2,1)} collective-permute-done((bf16[32,2048]{1,0:T(8,128)(2,1)}, bf16[32,2048]{1,0:T(8,128)(2,1)}, u32[]{:S(2)}, u32[]{:S(2)}) %collective-permute-start.7) | collective-permute-done | bytes 131104 | tf_op jit(solution)/shard_map/ppermute | solution.py:24
  96.7 4.7 %fusion.146 = f32[128,2048]{1,0:T(8,128)S(1)} fusion(bf16[128,2048]{1,0:T(8,128)(2,1)S(1)} %collective-permute-done.32, bf16[2048,2048]{1,0:T(8,128)(2,1)} %param.15), kind=kOutput, calls=%fused_computation.231 | convolution fusion | flops 1073741824 | bytes 9961472 | tf_op jit(solution)/shard_map/dot_general | solution.py:158
  107.5 7.6 %collective-permute-done.9 = bf16[128,2048]{1,0:T(8,128)(2,1)S(1)} collective-permute-done((bf16[128,2048]{1,0:T(8,128)(2,1)}, bf16[128,2048]{1,0:T(8,128)(2,1)S(1)}, u32[]{:S(2)}, u32[]{:S(2)}) %collective-permute-start.9) | collective-permute-done | bytes 524320 | tf_op jit(solution)/shard_map/ppermute | solution.py:24
  138.3 23.1 %collective-permute-done.13 = bf16[32,2048]{1,0:T(8,128)(2,1)S(1)} collective-permute-done((bf16[32,2048]{1,0:T(8,128)(2,1)S(1)}, bf16[32,2048]{1,0:T(8,128)(2,1)S(1)}, u32[]{:S(2)}, u32[]{:S(2)}) %collective-permute-start.13) | collective-permute-done | bytes 131104 | tf_op jit(solution)/shard_map/ppermute | solution.py:24
  166.4 2.7 %collective-permute-done.17 = bf16[32,2048]{1,0:T(8,128)(2,1)S(1)} collective-permute-done((bf16[32,2048]{1,0:T(8,128)(2,1)S(1)}, bf16[32,2048]{1,0:T(8,128)(2,1)S(1)}, u32[]{:S(2)}, u32[]{:S(2)}) %collective-permute-start.17) | collective-permute-done | bytes 131104 | tf_op jit(solution)/shard_map/ppermute | solution.py:24
  177.8 10.2 %collective-permute-done.19 = bf16[32,2048]{1,0:T(8,128)(2,1)S(1)} collective-permute-done((bf16[32,2048]{1,0:T(8,128)(2,1)S(1)}, bf16[32,2048]{1,0:T(8,128)(2,1)S(1)}, u32[]{:S(2)}, u32[]{:S(2)}) %collective-permute-start.19) | collective-permute-done | bytes 131104 | tf_op jit(solution)/shard_map/ppermute | solution.py:24
  189.6 5.2 %collective-permute-done.23 = bf16[32,2048]{1,0:T(8,128)(2,1)S(1)} collective-permute-done((bf16[32,2048]{1,0:T(8,128)(2,1)S(1)}, bf16[32,2048]{1,0:T(8,128)(2,1)S(1)}, u32[]{:S(2)}, u32[]{:S(2)}) %collective-permute-start.23) | collective-permute-done | bytes 131104 | tf_op jit(solution)/shard_map/ppermute | solution.py:24
  197.0 3.1 %collective-permute-done.31 = bf16[32,2048]{1,0:T(8,128)(2,1)S(1)} collective-permute-done((bf16[32,2048]{1,0:T(8,128)(2,1)S(1)}, bf16[32,2048]{1,0:T(8,128)(2,1)S(1)}, u32[]{:S(2)}, u32[]{:S(2)}) %collective-permute-start.31) | collective-permute-done | bytes 131104 | tf_op jit(solution)/shard_map/ppermute | solution.py:24
  200.1 2.3 %collective-permute-done.37 = bf16[32,2048]{1,0:T(8,128)(2,1)S(1)} collective-permute-done((bf16[32,2048]{1,0:T(8,128)(2,1)S(1)}, bf16[32,2048]{1,0:T(8,128)(2,1)S(1)}, u32[]{:S(2)}, u32[]{:S(2)}) %collective-permute-start.37) | collective-permute-done | bytes 131104 | tf_op jit(solution)/shard_map/ppermute | solution.py:24
  (163 shorter events, 76.2 us)
Async XLA Ops:
  5.8 14.2 %collective-permute-start = (bf16[8,32,512]{2,1,0:T(8,128)(2,1)S(1)}, bf16[8,32,512]{2,1,0:T(8,128)(2,1)S(1)}, u32[]{:S(2)}, u32[]{:S(2)}) collective-permute-start(bf16[8,32,512]{2,1,0:T(8,128)(2,1)S(1)} %gather_fusion.1), channel_id=1, source_target_pairs={{0,4},{4,0},{8,12},{12,8},{1,5},{5,1},{9,13},{13,9},{2,6},{6,2},{1... | collective-permute-start | bytes 786440 | tf_op jit(solution)/shard_map/ppermute | solution.py:24
  11.6 21.4 %collective-permute-start.1 = (bf16[8,32,512]{2,1,0:T(8,128)(2,1)S(1)}, bf16[8,32,512]{2,1,0:T(8,128)(2,1)S(1)}, u32[]{:S(2)}, u32[]{:S(2)}) collective-permute-start(bf16[8,32,512]{2,1,0:T(8,128)(2,1)S(1)} %gather_fusion.2), channel_id=1, source_target_pairs={{0,8},{4,12},{8,0},{12,4},{1,9},{5,13},{9,1},{13,5},{2,10},{6,14},... | collective-permute-start | bytes 786440 | tf_op jit(solution)/shard_map/ppermute | solution.py:24
  17.0 16.0 %collective-permute-start.2 = (bf16[8,32,512]{2,1,0:T(8,128)(2,1)S(1)}, bf16[8,32,512]{2,1,0:T(8,128)(2,1)S(1)}, u32[]{:S(2)}, u32[]{:S(2)}) collective-permute-start(bf16[8,32,512]{2,1,0:T(8,128)(2,1)S(1)} %gather_fusion.3), channel_id=1, source_target_pairs={{0,12},{4,8},{8,4},{12,0},{1,13},{5,9},{9,5},{13,1},{2,14},{6,10},... | collective-permute-start | bytes 786440 | tf_op jit(solution)/shard_map/ppermute | solution.py:24
  33.8 11.3 %collective-permute-start.4 = (bf16[2,256,512]{2,1,0:T(8,128)(2,1)S(1)}, bf16[2,256,512]{2,1,0:T(8,128)(2,1)}, u32[]{:S(2)}, u32[]{:S(2)}) collective-permute-start(bf16[2,256,512]{2,1,0:T(8,128)(2,1)S(1)} %bitcast.267), channel_id=1, source_target_pairs={{0,2},{2,0},{1,3},{3,1},{4,6},{6,4},{5,7},{7,5},{8,10},{10,8},{9,1... | collective-permute-start | bytes 1572872 | tf_op jit(solution)/shard_map/ppermute | solution.py:24
  38.7 7.7 %collective-permute-start.3 = (bf16[2,256,512]{2,1,0:T(8,128)(2,1)S(1)}, bf16[2,256,512]{2,1,0:T(8,128)(2,1)}, u32[]{:S(2)}, u32[]{:S(2)}) collective-permute-start(bf16[2,256,512]{2,1,0:T(8,128)(2,1)S(1)} %bitcast.268), channel_id=1, source_target_pairs={{0,1},{1,0},{2,3},{3,2},{4,5},{5,4},{6,7},{7,6},{8,9},{9,8},{10,11... | collective-permute-start | bytes 1572872 | tf_op jit(solution)/shard_map/ppermute | solution.py:24
  59.2 35.9 %collective-permute-start.32 = (bf16[128,2048]{1,0:T(8,128)(2,1)}, bf16[128,2048]{1,0:T(8,128)(2,1)S(1)}, u32[]{:S(2)}, u32[]{:S(2)}) collective-permute-start(bf16[128,2048]{1,0:T(8,128)(2,1)} %reshape.365), channel_id=1, source_target_pairs={{0,12},{4,8},{8,4},{12,0},{1,13},{5,9},{9,5},{13,1},{2,14},{6,10},... | collective-permute-start | bytes 1572872 | tf_op jit(solution)/shard_map/ppermute | solution.py:24
  61.8 39.6 %collective-permute-start.27 = (bf16[128,2048]{1,0:T(8,128)(2,1)}, bf16[128,2048]{1,0:T(8,128)(2,1)}, u32[]{:S(2)}, u32[]{:S(2)}) collective-permute-start(bf16[128,2048]{1,0:T(8,128)(2,1)} %reshape.365), channel_id=1, source_target_pairs={{0,4},{4,0},{8,12},{12,8},{1,5},{5,1},{9,13},{13,9},{2,6},{6,2},{1... | collective-permute-start | bytes 1572872 | tf_op jit(solution)/shard_map/ppermute | solution.py:24
  84.7 6.6 %collective-permute-start.7 = (bf16[32,2048]{1,0:T(8,128)(2,1)}, bf16[32,2048]{1,0:T(8,128)(2,1)}, u32[]{:S(2)}, u32[]{:S(2)}) collective-permute-start(bf16[32,2048]{1,0:T(8,128)(2,1)} %get-tuple-element.32), channel_id=1, source_target_pairs={{0,2},{1,3},{2,0},{3,1},{4,6},{5,7},{6,4},{7,5},{8,10},{9,11},{10,... | collective-permute-start | bytes 393224 | tf_op jit(solution)/shard_map/ppermute | solution.py:24
  86.2 7.2 %collective-permute-start.8 = (bf16[32,2048]{1,0:T(8,128)(2,1)}, bf16[32,2048]{1,0:T(8,128)(2,1)}, u32[]{:S(2)}, u32[]{:S(2)}) collective-permute-start(bf16[32,2048]{1,0:T(8,128)(2,1)} %get-tuple-element.31), channel_id=1, source_target_pairs={{0,3},{1,2},{2,1},{3,0},{4,7},{5,6},{6,5},{7,4},{8,11},{9,10},{10,... | collective-permute-start | bytes 393224 | tf_op jit(solution)/shard_map/ppermute | solution.py:24
  87.6 17.5 %collective-permute-start.14 = (bf16[128,2048]{1,0:T(8,128)(2,1)}, bf16[128,2048]{1,0:T(8,128)(2,1)S(1)}, u32[]{:S(2)}, u32[]{:S(2)}) collective-permute-start(bf16[128,2048]{1,0:T(8,128)(2,1)} %reshape.361), channel_id=1, source_target_pairs={{0,12},{4,8},{8,4},{12,0},{1,13},{5,9},{9,5},{13,1},{2,14},{6,10},... | collective-permute-start | bytes 1572872 | tf_op jit(solution)/shard_map/ppermute | solution.py:24
  91.3 23.8 %collective-permute-start.9 = (bf16[128,2048]{1,0:T(8,128)(2,1)}, bf16[128,2048]{1,0:T(8,128)(2,1)S(1)}, u32[]{:S(2)}, u32[]{:S(2)}) collective-permute-start(bf16[128,2048]{1,0:T(8,128)(2,1)} %reshape.361), channel_id=1, source_target_pairs={{0,4},{4,0},{8,12},{12,8},{1,5},{5,1},{9,13},{13,9},{2,6},{6,2},{1... | collective-permute-start | bytes 1572872 | tf_op jit(solution)/shard_map/ppermute | solution.py:24
  93.4 101.4 %collective-permute-start.24 = (bf16[32,2048]{1,0:T(8,128)(2,1)S(1)}, bf16[32,2048]{1,0:T(8,128)(2,1)S(1)}, u32[]{:S(2)}, u32[]{:S(2)}) collective-permute-start(bf16[32,2048]{1,0:T(8,128)(2,1)S(1)} %get-tuple-element.18), channel_id=1, source_target_pairs={{0,1},{1,0},{2,3},{3,2},{4,5},{5,4},{6,7},{7,6},{8,9},{9,8},{10,11... | collective-permute-start | bytes 393224 | tf_op jit(solution)/shard_map/ppermute | solution.py:24
  95.1 101.8 %collective-permute-start.25 = (bf16[32,2048]{1,0:T(8,128)(2,1)S(1)}, bf16[32,2048]{1,0:T(8,128)(2,1)S(1)}, u32[]{:S(2)}, u32[]{:S(2)}) collective-permute-start(bf16[32,2048]{1,0:T(8,128)(2,1)S(1)} %get-tuple-element.20), channel_id=1, source_target_pairs={{0,2},{1,3},{2,0},{3,1},{4,6},{5,7},{6,4},{7,5},{8,10},{9,11},{10,... | collective-permute-start | bytes 393224 | tf_op jit(solution)/shard_map/ppermute | solution.py:24
  101.4 16.4 %collective-permute-start.38 = (bf16[32,2048]{1,0:T(8,128)(2,1)S(1)}, bf16[32,2048]{1,0:T(8,128)(2,1)S(1)}, u32[]{:S(2)}, u32[]{:S(2)}) collective-permute-start(bf16[32,2048]{1,0:T(8,128)(2,1)S(1)} %get-tuple-element.9), channel_id=1, source_target_pairs={{0,1},{1,0},{2,3},{3,2},{4,5},{5,4},{6,7},{7,6},{8,9},{9,8},{10,11... | collective-permute-start | bytes 393224 | tf_op jit(solution)/shard_map/ppermute | solution.py:24
  105.1 13.2 %collective-permute-start.39 = (bf16[32,2048]{1,0:T(8,128)(2,1)S(1)}, bf16[32,2048]{1,0:T(8,128)(2,1)S(1)}, u32[]{:S(2)}, u32[]{:S(2)}) collective-permute-start(bf16[32,2048]{1,0:T(8,128)(2,1)S(1)} %get-tuple-element.11), channel_id=1, source_target_pairs={{0,2},{1,3},{2,0},{3,1},{4,6},{5,7},{6,4},{7,5},{8,10},{9,11},{10,... | collective-permute-start | bytes 393224 | tf_op jit(solution)/shard_map/ppermute | solution.py:24
  133.5 30.1 %collective-permute-start.33 = (bf16[128,2048]{1,0:T(8,128)(2,1)S(1)}, bf16[128,2048]{1,0:T(8,128)(2,1)S(1)}, u32[]{:S(2)}, u32[]{:S(2)}) collective-permute-start(bf16[128,2048]{1,0:T(8,128)(2,1)S(1)} %broadcast_select_fusion), channel_id=1, source_target_pairs={{0,8},{12,4},{4,0},{8,12},{1,9},{13,5},{5,1},{9,13},{2,10},{14,6},... | collective-permute-start | bytes 1572872 | tf_op jit(solution)/shard_map/ppermute | solution.py:33
  135.2 26.2 %collective-permute-start.15 = (bf16[128,2048]{1,0:T(8,128)(2,1)S(1)}, bf16[128,2048]{1,0:T(8,128)(2,1)S(1)}, u32[]{:S(2)}, u32[]{:S(2)}) collective-permute-start(bf16[128,2048]{1,0:T(8,128)(2,1)S(1)} %broadcast_select_fusion.1), channel_id=1, source_target_pairs={{0,8},{12,4},{4,0},{8,12},{1,9},{13,5},{5,1},{9,13},{2,10},{14,6},... | collective-permute-start | bytes 1572872 | tf_op jit(solution)/shard_map/ppermute | solution.py:33
  137.5 23.9 %collective-permute-start.13 = (bf16[32,2048]{1,0:T(8,128)(2,1)S(1)}, bf16[32,2048]{1,0:T(8,128)(2,1)S(1)}, u32[]{:S(2)}, u32[]{:S(2)}) collective-permute-start(bf16[32,2048]{1,0:T(8,128)(2,1)S(1)} %fusion.66), channel_id=1, source_target_pairs={{0,4},{4,0},{8,12},{12,8},{1,5},{5,1},{9,13},{13,9},{2,6},{6,2},{1... | collective-permute-start | bytes 393224 | tf_op jit(solution)/shard_map/ppermute | solution.py:24
  163.7 7.4 %collective-permute-start.18 = (bf16[32,2048]{1,0:T(8,128)(2,1)S(1)}, bf16[32,2048]{1,0:T(8,128)(2,1)S(1)}, u32[]{:S(2)}, u32[]{:S(2)}) collective-permute-start(bf16[32,2048]{1,0:T(8,128)(2,1)S(1)} %get-tuple-element.25), channel_id=1, source_target_pairs={{0,3},{1,2},{2,1},{3,0},{4,7},{5,6},{6,5},{7,4},{8,11},{9,10},{10,... | collective-permute-start | bytes 393224 | tf_op jit(solution)/shard_map/ppermute | solution.py:24
  172.3 24.7 %collective-permute-start.26 = (bf16[32,2048]{1,0:T(8,128)(2,1)S(1)}, bf16[32,2048]{1,0:T(8,128)(2,1)S(1)}, u32[]{:S(2)}, u32[]{:S(2)}) collective-permute-start(bf16[32,2048]{1,0:T(8,128)(2,1)S(1)} %get-tuple-element.19), channel_id=1, source_target_pairs={{0,3},{1,2},{2,1},{3,0},{4,7},{5,6},{6,5},{7,4},{8,11},{9,10},{10,... | collective-permute-start | bytes 393224 | tf_op jit(solution)/shard_map/ppermute | solution.py:24
  174.5 28.0 %collective-permute-start.41 = (bf16[32,2048]{1,0:T(8,128)(2,1)S(1)}, bf16[32,2048]{1,0:T(8,128)(2,1)S(1)}, u32[]{:S(2)}, u32[]{:S(2)}) collective-permute-start(bf16[32,2048]{1,0:T(8,128)(2,1)S(1)} %fusion.48), channel_id=1, source_target_pairs={{0,12},{4,8},{8,4},{12,0},{1,13},{5,9},{9,5},{13,1},{2,14},{6,10},... | collective-permute-start | bytes 393224 | tf_op jit(solution)/shard_map/ppermute | solution.py:24
  176.5 11.5 %collective-permute-start.19 = (bf16[32,2048]{1,0:T(8,128)(2,1)S(1)}, bf16[32,2048]{1,0:T(8,128)(2,1)S(1)}, u32[]{:S(2)}, u32[]{:S(2)}) collective-permute-start(bf16[32,2048]{1,0:T(8,128)(2,1)S(1)} %fusion.63), channel_id=1, source_target_pairs={{0,8},{4,12},{8,0},{12,4},{1,9},{5,13},{9,1},{13,5},{2,10},{6,14},... | collective-permute-start | bytes 393224 | tf_op jit(solution)/shard_map/ppermute | solution.py:24
  188.0 6.8 %collective-permute-start.23 = (bf16[32,2048]{1,0:T(8,128)(2,1)S(1)}, bf16[32,2048]{1,0:T(8,128)(2,1)S(1)}, u32[]{:S(2)}, u32[]{:S(2)}) collective-permute-start(bf16[32,2048]{1,0:T(8,128)(2,1)S(1)} %fusion.60), channel_id=1, source_target_pairs={{0,12},{4,8},{8,4},{12,0},{1,13},{5,9},{9,5},{13,1},{2,14},{6,10},... | collective-permute-start | bytes 393224 | tf_op jit(solution)/shard_map/ppermute | solution.py:24
  194.8 7.7 %collective-permute-start.37 = (bf16[32,2048]{1,0:T(8,128)(2,1)S(1)}, bf16[32,2048]{1,0:T(8,128)(2,1)S(1)}, u32[]{:S(2)}, u32[]{:S(2)}) collective-permute-start(bf16[32,2048]{1,0:T(8,128)(2,1)S(1)} %fusion.51), channel_id=1, source_target_pairs={{0,8},{4,12},{8,0},{12,4},{1,9},{5,13},{9,1},{13,5},{2,10},{6,14},... | collective-permute-start | bytes 393224 | tf_op jit(solution)/shard_map/ppermute | solution.py:24
  (30 other events, 218.9 us)

commit v3 on v2

--- a/solution.py
+++ b/solution.py
@@ -24,24 +24,30 @@
     return lax.ppermute(values, axis, [(i, i ^ flip) for i in range(lax.axis_size(axis))])
 
 
-def spread_over_pool(block):
+def second_hop(block, across):
     index = lax.axis_index("pool")
     at_end = (index == 0) | (index == 3)
-    across = swap(block, "pool", 3)
-    beside = swap(block, "pool", 1)
     passed = jnp.where(at_end, block, across)
-    second = lax.ppermute(passed, "pool", [(0, 2), (3, 1), (1, 0), (2, 3)])
-    return [block, beside, second, across]
-
-
-def reduce_shares(partial):
-    axes = ("heads", "sub")
-    share = lax.axis_index(axes)
-    total = lax.dynamic_index_in_dim(partial, share, 0, keepdims=False)
-    for flip in range(1, lax.axis_size(axes)):
-        away = lax.dynamic_index_in_dim(partial, share ^ flip, 0, keepdims=False)
-        total = total + swap(away.astype(jnp.bfloat16), axes, flip).astype(jnp.float32)
-    return total.astype(jnp.bfloat16)
+    return lax.ppermute(passed, "pool", [(0, 2), (3, 1), (1, 0), (2, 3)])
+
+
+def exchange_sum(pieces, axis):
+    index = lax.axis_index(axis)
+    total = lax.dynamic_index_in_dim(pieces, index, 0, keepdims=False)
+    for flip in range(1, lax.axis_size(axis)):
+        away = lax.dynamic_index_in_dim(pieces, index ^ flip, 0, keepdims=False)
+        total = total + swap(away.astype(jnp.bfloat16), axis, flip).astype(jnp.float32)
+    return total
+
+
+def project_out(blocks, out_weight, part_rows):
+    heads_size, sub_size = lax.axis_size("heads"), lax.axis_size("sub")
+    rows = jnp.concatenate(blocks, axis=0)
+    partial = jnp.dot(rows, out_weight, preferred_element_type=jnp.float32)
+    partial = partial.reshape(len(blocks), heads_size, sub_size, part_rows, -1)
+    by_sub = exchange_sum(jnp.moveaxis(partial, 2, 0), "sub")
+    by_heads = exchange_sum(jnp.moveaxis(by_sub, 1, 0), "heads").astype(jnp.bfloat16)
+    return [by_heads[i] for i in range(len(blocks))]
 
 
 def fetch_latents(latent_store, place_holder, place_block, serving_request, items):
@@ -61,11 +67,11 @@
     send_block = jnp.sum(jnp.where(matched, blocks[:, None, :], 0), axis=2)
     rows = BLK // share_count
     store = latent_store.reshape(-1, rows, latent_store.shape[1])
-    pieces = []
-    for flip in range(pool_size):
-        wanted = lax.dynamic_index_in_dim(send_block, pool_index ^ flip, 0, keepdims=False)
-        piece = store.at[wanted * share_count + share].get(mode="promise_in_bounds")
-        pieces.append(piece if flip == 0 else swap(piece, "pool", flip))
+    partners = jnp.arange(pool_size, dtype=jnp.int32) ^ pool_index
+    wanted = send_block.at[partners].get(mode="promise_in_bounds").reshape(-1)
+    outgoing = store.at[wanted * share_count + share].get(mode="promise_in_bounds")
+    outgoing = outgoing.reshape(pool_size, capacity, rows, -1)
+    pieces = [outgoing[0]] + [swap(outgoing[flip], "pool", flip) for flip in range(1, pool_size)]
     my_holders = lax.dynamic_index_in_dim(holders, pool_index, 0, keepdims=False)
     my_ranks = lax.dynamic_index_in_dim(ranks, pool_index, 0, keepdims=False)
     chosen = jnp.concatenate(pieces, axis=0).at[(my_holders ^ pool_index) * capacity + my_ranks]
@@ -131,8 +137,8 @@
         per_group,
         head_width,
     )
-    output = jnp.zeros((CHUNKS * part_rows, pool_size * columns), jnp.bfloat16)
-    for chunk in range(CHUNKS):
+
+    def attend(chunk):
         part = shaped[:, :, chunk].reshape(requests_here, -1, heads_here, per_group, head_width)
         normed = rms_scale(part.astype(jnp.float32), q_gain).astype(jnp.bfloat16)
         scores = (
@@ -144,22 +150,50 @@
         attended = jnp.einsum(
             "rgqts,rsgd->rtgqd", probs, values, preferred_element_type=jnp.float32
         )
-        attended = attended.astype(jnp.bfloat16).reshape(share_count * part_rows, query_width)
-        if pool_size != 4:
-            rows = lax.all_gather(attended, "pool", axis=0, tiled=True)
-            partial = jnp.dot(rows, out_weight, preferred_element_type=jnp.float32)
-            partial = partial.reshape(pool_size, share_count, part_rows, columns)
-            mine = reduce_shares(jnp.moveaxis(partial, 1, 0))
+        return attended.astype(jnp.bfloat16).reshape(share_count * part_rows, query_width)
+
+    if pool_size != 4:
+        outputs = []
+        for chunk in range(CHUNKS):
+            rows = lax.all_gather(attend(chunk), "pool", axis=0)
+            blocks = [rows[i] for i in range(pool_size)]
+            mine = jnp.stack(project_out(blocks, out_weight, part_rows))
             back = lax.all_to_all(mine, "pool", split_axis=0, concat_axis=0, tiled=True)
-            back = jnp.moveaxis(back, 0, 1).reshape(part_rows, pool_size * columns)
-            output = lax.dynamic_update_slice(output, back, (chunk * part_rows, 0))
-            continue
-        for flip, rows in enumerate(spread_over_pool(attended)):
-            partial = jnp.dot(rows, out_weight, preferred_element_type=jnp.float32)
-            mine = reduce_shares(partial.reshape(share_count, part_rows, columns))
-            back = mine if flip == 0 else swap(mine, "pool", flip)
+            outputs.append(jnp.moveaxis(back, 0, 1).reshape(part_rows, pool_size * columns))
+        return jnp.concatenate(outputs, axis=0)
+
+    tie = lax.optimization_barrier
+    first = attend(0)
+    across0, beside0 = swap(first, "pool", 3), swap(first, "pool", 1)
+    last = attend(1)
+    (own0,) = project_out([first], out_weight, part_rows)
+    across0, beside0, last, own0, first = tie((across0, beside0, last, own0, first))
+    second0 = second_hop(first, across0)
+    across1, beside1 = swap(last, "pool", 3), swap(last, "pool", 1)
+    mine = project_out([across0, beside0, last], out_weight, part_rows)
+    second0, across1, beside1, last, mine = tie((second0, across1, beside1, last, mine))
+    out_across0, out_beside0, own1 = mine
+    second1 = second_hop(last, across1)
+    back_across0, back_beside0 = swap(out_across0, "pool", 3), swap(out_beside0, "pool", 1)
+    mine = project_out([across1, beside1, second0], out_weight, part_rows)
+    second1, back_across0, back_beside0, mine = tie((second1, back_across0, back_beside0, mine))
+    out_across1, out_beside1, out_second0 = mine
+    back_second0, back_across1 = swap(out_second0, "pool", 2), swap(out_across1, "pool", 3)
+    back_beside1 = swap(out_beside1, "pool", 1)
+    mine = project_out([second1], out_weight, part_rows)
+    back_second0, back_across1, back_beside1, mine = tie(
+        (back_second0, back_across1, back_beside1, mine)
+    )
+    back_second1 = swap(mine[0], "pool", 2)
+    output = jnp.zeros((CHUNKS * part_rows, pool_size * columns), jnp.bfloat16)
+    backs = [
+        [own0, back_beside0, back_second0, back_across0],
+        [own1, back_beside1, back_second1, back_across1],
+    ]
+    for chunk in range(CHUNKS):
+        for flip in (0, 1, 3, 2):
             output = lax.dynamic_update_slice(
-                output, back, (chunk * part_rows, (pool_index ^ flip) * columns)
+                output, backs[chunk][flip], (chunk * part_rows, (pool_index ^ flip) * columns)
             )
     return output
 

time: 205 us -> 201 us (0.980)
  waiting for transfers between devices: 92.5 us -> 103 us
  starting transfers between devices: 43.8 us -> 34.8 us
  local copies, waits for them, and re-layouts: 21.8 us -> 13.8 us
    ppermute x2, waiting for transfers between devices: 0.01 us -> 22.6 us  [second_hop(): return lax.ppermute(passed, 'pool', [(0, 2), (3, 1), (1, 0), (2, 3)])]
    ppermute x40 -> x24, waiting for transfers between devices: 92.5 us -> 80.6 us  [swap(): lax.ppermute(values, axis, [(i, i ^ flip) for i in range(lax.axis_size(ax...]
    ppermute x40 -> x24, starting transfers between devices: 42.6 us -> 31.3 us  [swap(): lax.ppermute(values, axis, [(i, i ^ flip) for i in range(lax.axis_size(ax...]
    gather x4 -> x2, local copies, waits for them, and re-layouts: 11 us -> 3.37 us  [the longest x1 2.8 us: fetch_latents(): store.at[wanted * share_count + share].get(mode='promise_in_bounds')]
    add x0 -> x5, other arithmetic: none -> 3.33 us  [the longest x4 3.33 us: exchange_sum(): total + swap(away.astype(jnp.bfloat16), axis, flip).astype(jnp.float32)]
    ppermute x2, starting transfers between devices: 1.21 us -> 3.58 us  [second_hop(): return lax.ppermute(passed, 'pool', [(0, 2), (3, 1), (1, 0), (2, 3)])]
    unnamed x26 -> x32, local copies, waits for them, and re-layouts: 3.87 us -> 5.83 us
    dot_general x12 -> x8, matrix products: 35 us -> 36.7 us  [the longest x4 21.2 us: project_out(): partial = jnp.dot(rows, out_weight, preferred_element_type=jnp.float32)]
  transfers between devices with their start and end apart: 42 -> 26, of which waited for: 22 -> 16; matrix products, arithmetic and copies ran while one was open for 23% -> 6% of each run, Pallas kernels for 0% -> 0%
where the time goes in v3:
time: 201 us; the launch traced here: 200 us
  waiting for transfers between devices  103 us (51%)
  matrix products  41.3 us (21%)
  starting transfers between devices  34.8 us (17%)
  local copies, waits for them, and re-layouts  13.8 us (7%)
  other arithmetic  6.8 us (3%)
    ppermute x24, waiting for transfers between devices, swap(): lax.ppermute(values, axis, [(i, i ^ flip) for i in range(lax.axis_size(ax...  80.6 us
    ppermute x24, starting transfers between devices, swap(): lax.ppermute(values, axis, [(i, i ^ flip) for i in range(lax.axis_size(ax...  31.3 us
    ppermute x2, waiting for transfers between devices, second_hop(): return lax.ppermute(passed, 'pool', [(0, 2), (3, 1), (1, 0), (2, 3)])  22.6 us
    dot_general x4, matrix products, project_out(): partial = jnp.dot(rows, out_weight, preferred_element_type=jnp.float32)  21.2 us
    dot_general x2, matrix products, attend(): jnp.einsum('rgqts,rsgd->rtgqd', probs, values, preferred_element_type=jnp...  7.8 us
    dot_general x2, matrix products, attend(): jnp.einsum('rtgqd,rsgd->rgqts', normed, keys, preferred_element_type=jnp....  7.63 us
    unnamed x32, local copies, waits for them, and re-layouts  5.83 us
  transfers between devices with their start and end apart: 26, of which 16 were waited for; matrix products, arithmetic and copies ran while one was open for 6% of the time, Pallas kernels for 0%

profile of v3, /device:TPU:0, one launch (start us, length us, event | category | flops | bytes accessed | tf_op | source)
XLA Modules:
  0.0 200.5 jit_solution(16056615626672503481)
XLA Ops:
  3.7 2.8 %gather_fusion.1 = bf16[32,32,512]{2,1,0:T(8,128)(2,1)S(1)} fusion(bf16[128,32,512]{2,1,0:T(8,128)(2,1)} %bitcast.186, s32[1024]{0:T(1024)S(1)} %pad_clamp_fusion.1), kind=kCustom, calls=%fused_computation.1 | custom fusion | bytes 2097280 | tf_op jit(solution)/shard_map/gather | solution.py:72
  7.3 3.0 %collective-permute-start = (bf16[8,32,512]{2,1,0:T(8,128)(2,1)}, bf16[8,32,512]{2,1,0:T(8,128)(2,1)S(1)}, u32[]{:S(2)}, u32[]{:S(2)}) collective-permute-start(bf16[8,32,512]{2,1,0:T(8,128)(2,1)} %get-tuple-element.57), channel_id=1, source_target_pairs={{0,4},{4,0},{8,12},{12,8},{1,5},{5,1},{9,13},{13,9},{2,6},{6,2},{1... | collective-permute-start | bytes 786440 | tf_op jit(solution)/shard_map/ppermute | solution.py:24
  10.3 2.6 %collective-permute-start.1 = (bf16[8,32,512]{2,1,0:T(8,128)(2,1)S(1)}, bf16[8,32,512]{2,1,0:T(8,128)(2,1)S(1)}, u32[]{:S(2)}, u32[]{:S(2)}) collective-permute-start(bf16[8,32,512]{2,1,0:T(8,128)(2,1)S(1)} %get-tuple-element.56), channel_id=1, source_target_pairs={{0,8},{4,12},{8,0},{12,4},{1,9},{5,13},{9,1},{13,5},{2,10},{6,14},... | collective-permute-start | bytes 786440 | tf_op jit(solution)/shard_map/ppermute | solution.py:24
  12.9 8.8 %collective-permute-done = bf16[8,32,512]{2,1,0:T(8,128)(2,1)S(1)} collective-permute-done((bf16[8,32,512]{2,1,0:T(8,128)(2,1)}, bf16[8,32,512]{2,1,0:T(8,128)(2,1)S(1)}, u32[]{:S(2)}, u32[]{:S(2)}) %collective-permute-start) | collective-permute-done | bytes 262176 | tf_op jit(solution)/shard_map/ppermute | solution.py:24
  21.8 9.9 %collective-permute-done.1 = bf16[8,32,512]{2,1,0:T(8,128)(2,1)S(1)} collective-permute-done((bf16[8,32,512]{2,1,0:T(8,128)(2,1)S(1)}, bf16[8,32,512]{2,1,0:T(8,128)(2,1)S(1)}, u32[]{:S(2)}, u32[]{:S(2)}) %collective-permute-start.1) | collective-permute-done | bytes 262176 | tf_op jit(solution)/shard_map/ppermute | solution.py:24
  37.2 8.5 %collective-permute-done.4 = bf16[2,256,512]{2,1,0:T(8,128)(2,1)} collective-permute-done((bf16[2,256,512]{2,1,0:T(8,128)(2,1)S(1)}, bf16[2,256,512]{2,1,0:T(8,128)(2,1)}, u32[]{:S(2)}, u32[]{:S(2)}) %collective-permute-start.4) | collective-permute-done | bytes 524320 | tf_op jit(solution)/shard_map/ppermute | solution.py:24
  48.0 2.7 %fusion.8 = f32[2,1024,2,2,128]{1,4,3,2,0:T(8,128)S(1)} fusion(bf16[2,256,512]{2,1,0:T(8,128)(2,1)} %collective-permute-done.5, bf16[2,256,512]{2,1,0:T(8,128)(2,1)} %collective-permute-done.4, bf16[2,256,512]{2,1,0:T(8,128)(2,1)} %collective-permute-done.3, bf16[2,256,512]{2,1,0:T(8,128)(2,1)S(1)} %bitcast.183, bf16[512,2,2,128]{0,3,2,1:T(8,128)(2,1)S(1)} %copy.55), kind=kOutput, calls=%fused_computation.18 | convolution fusion | flops 1082130432 | bytes 6815744 | tf_op jit(solution)/shard_map/rsk,kgcd->rsgcd/dot_general | solution.py:116
  52.3 6.3 %bitcast_reduce_fusion = (f32[2,2,8,64]{3,2,1,0:T(8,128)}, f32[2,2,8,64]{3,2,1,0:T(8,128)S(1)}, f32[2,2,1024,64,8]{2,3,4,1,0:T(8,128)}) fusion(pred[2,1024]{1,0:T(4,128)(4,1)S(1)} %broadcast_compare_fusion, f32[2,2,1024,64,8]{2,3,4,1,0:T(8,128)S(1)} %fusion.49, f32[2,64,2,8,128]{4,3,2,1,0:T(8,128)S(1)} %bitcast.179, f32[2,64,2,8]{1,3,2,0:T(8,128)S(1)} %copy.61, ...), kind=kOutput, calls=%fused_computation.6 | convolution fusion | flops 551809024 | bytes 19977216 | tf_op jit(solution)/shard_map/rtgqd,rsgd->rgqts/dot_general | solution.py:145
  61.2 4.7 %fusion = f32[2,2,32,2048]{3,2,1,0:T(8,128)S(1)} fusion(bf16[2,2,32,2048]{3,2,1,0:T(8,128)(2,1)S(1)} %reshape.372, bf16[2048,2048]{1,0:T(8,128)(2,1)} %param.15), kind=kOutput, calls=%fused_computation.3 | convolution fusion | flops 1073741824 | bytes 9961472 | tf_op jit(solution)/shard_map/dot_general | solution.py:46
  67.7 6.1 %collective-permute-start.7 = (bf16[128,2048]{1,0:T(8,128)(2,1)S(1)}, bf16[128,2048]{1,0:T(8,128)(2,1)}, u32[]{:S(2)}, u32[]{:S(2)}) collective-permute-start(bf16[128,2048]{1,0:T(8,128)(2,1)S(1)} %reshape.370), channel_id=1, source_target_pairs={{0,4},{4,0},{8,12},{12,8},{1,5},{5,1},{9,13},{13,9},{2,6},{6,2},{1... | collective-permute-start | bytes 1572872 | tf_op jit(solution)/shard_map/ppermute | solution.py:24
  75.5 5.8 %fusion.36 = bf16[2,64,2,8,128]{4,1,3,2,0:T(8,128)(2,1)S(1)} fusion(f32[2,2,1024,64,8]{2,3,4,1,0:T(8,128)} %get-tuple-element.65, f32[2,2,8,64]{3,2,1,0:T(8,128)} %get-tuple-element.51, pred[2,1024]{1,0:T(4,128)(4,1)S(1)} %broadcast_compare_fusion, f32[2,1024,2,2,128]{1,4,3,2,0:T(8,128)} %copy-done.2), kind=kOutput, calls=%fused_computation.46 | convolution fusion | flops 545521664 | bytes 9979904 | tf_op jit(solution)/shard_map/rgqts,rsgd->rtgqd/dot_general | solution.py:150
  83.0 10.8 %collective-permute-done.7 = bf16[128,2048]{1,0:T(8,128)(2,1)} collective-permute-done((bf16[128,2048]{1,0:T(8,128)(2,1)S(1)}, bf16[128,2048]{1,0:T(8,128)(2,1)}, u32[]{:S(2)}, u32[]{:S(2)}) %collective-permute-start.7) | collective-permute-done | bytes 524320 | tf_op jit(solution)/shard_map/ppermute | solution.py:24
  93.7 6.0 %fusion.15 = f32[384,2048]{1,0:T(8,128)S(1)} fusion(bf16[2048,2048]{1,0:T(8,128)(2,1)} %param.15, bf16[128,2048]{1,0:T(8,128)(2,1)S(1)} %reshape.371, bf16[128,2048]{1,0:T(8,128)(2,1)} %collective-permute-done.7, bf16[128,2048]{1,0:T(8,128)(2,1)S(1)} %collective-permute-done.6), kind=kOutput, calls=%fused_computation.27 | convolution fusion | flops 3225944064 | bytes 13107200 | tf_op jit(solution)/shard_map/dot_general | solution.py:46
  109.4 7.4 %collective-permute-done.14 = bf16[3,32,2048]{2,1,0:T(8,128)(2,1)S(1)} collective-permute-done((bf16[3,32,2048]{2,1,0:T(8,128)(2,1)S(1)}, bf16[3,32,2048]{2,1,0:T(8,128)(2,1)S(1)}, u32[]{:S(2)}, u32[]{:S(2)}) %collective-permute-start.14) | collective-permute-done | bytes 393248 | tf_op jit(solution)/shard_map/ppermute | solution.py:24
  116.9 22.6 %collective-permute-done.10 = bf16[128,2048]{1,0:T(8,128)(2,1)S(1)} collective-permute-done((bf16[128,2048]{1,0:T(8,128)(2,1)S(1)}, bf16[128,2048]{1,0:T(8,128)(2,1)S(1)}, u32[]{:S(2)}, u32[]{:S(2)}) %collective-permute-start.10) | collective-permute-done | bytes 524320 | tf_op jit(solution)/shard_map/ppermute | solution.py:31
  139.4 5.9 %fusion.21 = f32[384,2048]{1,0:T(8,128)S(1)} fusion(bf16[2048,2048]{1,0:T(8,128)(2,1)} %param.15, bf16[128,2048]{1,0:T(8,128)(2,1)S(1)} %collective-permute-done.10, bf16[128,2048]{1,0:T(8,128)(2,1)S(1)} %collective-permute-done.12, bf16[128,2048]{1,0:T(8,128)(2,1)S(1)} %collective-permute-done.11), kind=kOutput, calls=%fused_computation.33 | convolution fusion | flops 3225944064 | bytes 13107200 | tf_op jit(solution)/shard_map/dot_general | solution.py:46
  154.0 2.4 %collective-permute-start.16 = (bf16[32,2048]{1,0:T(8,128)(2,1)S(1)}, bf16[32,2048]{1,0:T(8,128)(2,1)S(1)}, u32[]{:S(2)}, u32[]{:S(2)}) collective-permute-start(bf16[32,2048]{1,0:T(8,128)(2,1)S(1)} %get-tuple-element.34), channel_id=1, source_target_pairs={{0,12},{4,8},{8,4},{12,0},{1,13},{5,9},{9,5},{13,1},{2,14},{6,10},... | collective-permute-start | bytes 393224 | tf_op jit(solution)/shard_map/ppermute | solution.py:24
  156.5 5.8 %collective-permute-done.19 = bf16[3,32,2048]{2,1,0:T(8,128)(2,1)S(1)} collective-permute-done((bf16[3,32,2048]{2,1,0:T(8,128)(2,1)S(1)}, bf16[3,32,2048]{2,1,0:T(8,128)(2,1)S(1)}, u32[]{:S(2)}, u32[]{:S(2)}) %collective-permute-start.19) | collective-permute-done | bytes 393248 | tf_op jit(solution)/shard_map/ppermute | solution.py:24
  162.4 9.6 %collective-permute-done.16 = bf16[32,2048]{1,0:T(8,128)(2,1)S(1)} collective-permute-done((bf16[32,2048]{1,0:T(8,128)(2,1)S(1)}, bf16[32,2048]{1,0:T(8,128)(2,1)S(1)}, u32[]{:S(2)}, u32[]{:S(2)}) %collective-permute-start.16) | collective-permute-done | bytes 131104 | tf_op jit(solution)/shard_map/ppermute | solution.py:24
  172.1 4.7 %fusion.108 = f32[128,2048]{1,0:T(8,128)S(1)} fusion(bf16[128,2048]{1,0:T(8,128)(2,1)S(1)} %collective-permute-done.15, bf16[2048,2048]{1,0:T(8,128)(2,1)} %param.15), kind=kOutput, calls=%fused_computation.180 | convolution fusion | flops 1073741824 | bytes 9961472 | tf_op jit(solution)/shard_map/dot_general | solution.py:46
  181.9 4.8 %collective-permute-done.24 = bf16[1,32,2048]{2,1,0:T(8,128)(2,1)S(1)} collective-permute-done((bf16[1,32,2048]{2,1,0:T(8,128)(2,1)S(1)}, bf16[1,32,2048]{2,1,0:T(8,128)(2,1)S(1)}, u32[]{:S(2)}, u32[]{:S(2)}) %collective-permute-start.24) | collective-permute-done | bytes 131104 | tf_op jit(solution)/shard_map/ppermute | solution.py:24
  186.7 3.2 %collective-permute-done.20 = bf16[32,2048]{1,0:T(8,128)(2,1)S(1)} collective-permute-done((bf16[32,2048]{1,0:T(8,128)(2,1)S(1)}, bf16[32,2048]{1,0:T(8,128)(2,1)S(1)}, u32[]{:S(2)}, u32[]{:S(2)}) %collective-permute-start.20) | collective-permute-done | bytes 131104 | tf_op jit(solution)/shard_map/ppermute | solution.py:24
  190.8 2.8 %collective-permute-start.25 = (bf16[32,2048]{1,0:T(8,128)(2,1)S(1)}, bf16[32,2048]{1,0:T(8,128)(2,1)S(1)}, u32[]{:S(2)}, u32[]{:S(2)}) collective-permute-start(bf16[32,2048]{1,0:T(8,128)(2,1)S(1)} %fusion.69), channel_id=1, source_target_pairs={{0,8},{4,12},{8,0},{12,4},{1,9},{5,13},{9,1},{13,5},{2,10},{6,14},... | collective-permute-start | bytes 393224 | tf_op jit(solution)/shard_map/ppermute | solution.py:24
  193.7 6.1 %collective-permute-done.25 = bf16[32,2048]{1,0:T(8,128)(2,1)S(1)} collective-permute-done((bf16[32,2048]{1,0:T(8,128)(2,1)S(1)}, bf16[32,2048]{1,0:T(8,128)(2,1)S(1)}, u32[]{:S(2)}, u32[]{:S(2)}) %collective-permute-start.25) | collective-permute-done | bytes 131104 | tf_op jit(solution)/shard_map/ppermute | solution.py:24
  (135 shorter events, 46.8 us)
Async XLA Ops:
  7.3 14.5 %collective-permute-start = (bf16[8,32,512]{2,1,0:T(8,128)(2,1)}, bf16[8,32,512]{2,1,0:T(8,128)(2,1)S(1)}, u32[]{:S(2)}, u32[]{:S(2)}) collective-permute-start(bf16[8,32,512]{2,1,0:T(8,128)(2,1)} %get-tuple-element.57), channel_id=1, source_target_pairs={{0,4},{4,0},{8,12},{12,8},{1,5},{5,1},{9,13},{13,9},{2,6},{6,2},{1... | collective-permute-start | bytes 786440 | tf_op jit(solution)/shard_map/ppermute | solution.py:24
  10.3 21.4 %collective-permute-start.1 = (bf16[8,32,512]{2,1,0:T(8,128)(2,1)S(1)}, bf16[8,32,512]{2,1,0:T(8,128)(2,1)S(1)}, u32[]{:S(2)}, u32[]{:S(2)}) collective-permute-start(bf16[8,32,512]{2,1,0:T(8,128)(2,1)S(1)} %get-tuple-element.56), channel_id=1, source_target_pairs={{0,8},{4,12},{8,0},{12,4},{1,9},{5,13},{9,1},{13,5},{2,10},{6,14},... | collective-permute-start | bytes 786440 | tf_op jit(solution)/shard_map/ppermute | solution.py:24
  12.9 18.8 %collective-permute-start.2 = (bf16[8,32,512]{2,1,0:T(8,128)(2,1)S(1)}, bf16[8,32,512]{2,1,0:T(8,128)(2,1)S(1)}, u32[]{:S(2)}, u32[]{:S(2)}) collective-permute-start(bf16[8,32,512]{2,1,0:T(8,128)(2,1)S(1)} %get-tuple-element.58), channel_id=1, source_target_pairs={{0,12},{4,8},{8,4},{12,0},{1,13},{5,9},{9,5},{13,1},{2,14},{6,10},... | collective-permute-start | bytes 786440 | tf_op jit(solution)/shard_map/ppermute | solution.py:24
  34.1 11.6 %collective-permute-start.4 = (bf16[2,256,512]{2,1,0:T(8,128)(2,1)S(1)}, bf16[2,256,512]{2,1,0:T(8,128)(2,1)}, u32[]{:S(2)}, u32[]{:S(2)}) collective-permute-start(bf16[2,256,512]{2,1,0:T(8,128)(2,1)S(1)} %bitcast.181), channel_id=1, source_target_pairs={{0,2},{2,0},{1,3},{3,1},{4,6},{6,4},{5,7},{7,5},{8,10},{10,8},{9,1... | collective-permute-start | bytes 1572872 | tf_op jit(solution)/shard_map/ppermute | solution.py:24
  37.2 10.1 %collective-permute-start.3 = (bf16[2,256,512]{2,1,0:T(8,128)(2,1)S(1)}, bf16[2,256,512]{2,1,0:T(8,128)(2,1)}, u32[]{:S(2)}, u32[]{:S(2)}) collective-permute-start(bf16[2,256,512]{2,1,0:T(8,128)(2,1)S(1)} %bitcast.182), channel_id=1, source_target_pairs={{0,1},{1,0},{2,3},{3,2},{4,5},{5,4},{6,7},{7,6},{8,9},{9,8},{10,11... | collective-permute-start | bytes 1572872 | tf_op jit(solution)/shard_map/ppermute | solution.py:24
  65.9 8.0 %collective-permute-start.8 = (bf16[1,2,32,2048]{3,2,1,0:T(8,128)(2,1)S(1)}, bf16[1,2,32,2048]{3,2,1,0:T(8,128)(2,1)S(1)}, u32[]{:S(2)}, u32[]{:S(2)}) collective-permute-start(bf16[1,2,32,2048]{3,2,1,0:T(8,128)(2,1)S(1)} %fusion.62), channel_id=1, source_target_pairs={{0,1},{1,0},{2,3},{3,2},{4,5},{5,4},{6,7},{7,6},{8,9},{9,8},{10,11... | collective-permute-start | bytes 786440 | tf_op jit(solution)/shard_map/ppermute | solution.py:24
  66.3 16.7 %collective-permute-start.6 = (bf16[128,2048]{1,0:T(8,128)(2,1)S(1)}, bf16[128,2048]{1,0:T(8,128)(2,1)S(1)}, u32[]{:S(2)}, u32[]{:S(2)}) collective-permute-start(bf16[128,2048]{1,0:T(8,128)(2,1)S(1)} %reshape.370), channel_id=1, source_target_pairs={{0,12},{4,8},{8,4},{12,0},{1,13},{5,9},{9,5},{13,1},{2,14},{6,10},... | collective-permute-start | bytes 1572872 | tf_op jit(solution)/shard_map/ppermute | solution.py:24
  67.7 26.0 %collective-permute-start.7 = (bf16[128,2048]{1,0:T(8,128)(2,1)S(1)}, bf16[128,2048]{1,0:T(8,128)(2,1)}, u32[]{:S(2)}, u32[]{:S(2)}) collective-permute-start(bf16[128,2048]{1,0:T(8,128)(2,1)S(1)} %reshape.370), channel_id=1, source_target_pairs={{0,4},{4,0},{8,12},{12,8},{1,5},{5,1},{9,13},{13,9},{2,6},{6,2},{1... | collective-permute-start | bytes 1572872 | tf_op jit(solution)/shard_map/ppermute | solution.py:24
  73.9 7.9 %collective-permute-start.9 = (bf16[1,32,2048]{2,1,0:T(8,128)(2,1)S(1)}, bf16[1,32,2048]{2,1,0:T(8,128)(2,1)S(1)}, u32[]{:S(2)}, u32[]{:S(2)}) collective-permute-start(bf16[1,32,2048]{2,1,0:T(8,128)(2,1)S(1)} %fusion.66), channel_id=1, source_target_pairs={{0,2},{2,0},{1,3},{3,1},{4,6},{6,4},{5,7},{7,5},{8,10},{10,8},{9,1... | collective-permute-start | bytes 393224 | tf_op jit(solution)/shard_map/ppermute | solution.py:24
  101.5 2.4 %collective-permute-start.13 = (bf16[3,2,32,2048]{3,2,0,1:T(8,128)(2,1)S(1)}, bf16[3,2,32,2048]{3,2,0,1:T(8,128)(2,1)S(1)}, u32[]{:S(2)}, u32[]{:S(2)}) collective-permute-start(bf16[3,2,32,2048]{3,2,0,1:T(8,128)(2,1)S(1)} %fusion.45), channel_id=1, source_target_pairs={{0,1},{1,0},{2,3},{3,2},{4,5},{5,4},{6,7},{7,6},{8,9},{9,8},{10,11... | collective-permute-start | bytes 2359304 | tf_op jit(solution)/shard_map/ppermute | solution.py:24
  101.6 37.8 %collective-permute-start.11 = (bf16[128,2048]{1,0:T(8,128)(2,1)S(1)}, bf16[128,2048]{1,0:T(8,128)(2,1)S(1)}, u32[]{:S(2)}, u32[]{:S(2)}) collective-permute-start(bf16[128,2048]{1,0:T(8,128)(2,1)S(1)} %reshape.371), channel_id=1, source_target_pairs={{0,12},{4,8},{8,4},{12,0},{1,13},{5,9},{9,5},{13,1},{2,14},{6,10},... | collective-permute-start | bytes 1572872 | tf_op jit(solution)/shard_map/ppermute | solution.py:24
  103.0 36.5 %collective-permute-start.12 = (bf16[128,2048]{1,0:T(8,128)(2,1)S(1)}, bf16[128,2048]{1,0:T(8,128)(2,1)S(1)}, u32[]{:S(2)}, u32[]{:S(2)}) collective-permute-start(bf16[128,2048]{1,0:T(8,128)(2,1)S(1)} %reshape.371), channel_id=1, source_target_pairs={{0,4},{4,0},{8,12},{12,8},{1,5},{5,1},{9,13},{13,9},{2,6},{6,2},{1... | collective-permute-start | bytes 1572872 | tf_op jit(solution)/shard_map/ppermute | solution.py:24
  105.5 11.2 %collective-permute-start.14 = (bf16[3,32,2048]{2,1,0:T(8,128)(2,1)S(1)}, bf16[3,32,2048]{2,1,0:T(8,128)(2,1)S(1)}, u32[]{:S(2)}, u32[]{:S(2)}) collective-permute-start(bf16[3,32,2048]{2,1,0:T(8,128)(2,1)S(1)} %fusion.60), channel_id=1, source_target_pairs={{0,2},{2,0},{1,3},{3,1},{4,6},{6,4},{5,7},{7,5},{8,10},{10,8},{9,1... | collective-permute-start | bytes 1179656 | tf_op jit(solution)/shard_map/ppermute | solution.py:24
  107.1 32.3 %collective-permute-start.10 = (bf16[128,2048]{1,0:T(8,128)(2,1)S(1)}, bf16[128,2048]{1,0:T(8,128)(2,1)S(1)}, u32[]{:S(2)}, u32[]{:S(2)}) collective-permute-start(bf16[128,2048]{1,0:T(8,128)(2,1)S(1)} %broadcast_select_fusion.1), channel_id=1, source_target_pairs={{0,8},{12,4},{4,0},{8,12},{1,9},{13,5},{5,1},{9,13},{2,10},{14,6},... | collective-permute-start | bytes 1572872 | tf_op jit(solution)/shard_map/ppermute | solution.py:31
  151.1 11.2 %collective-permute-start.19 = (bf16[3,32,2048]{2,1,0:T(8,128)(2,1)S(1)}, bf16[3,32,2048]{2,1,0:T(8,128)(2,1)S(1)}, u32[]{:S(2)}, u32[]{:S(2)}) collective-permute-start(bf16[3,32,2048]{2,1,0:T(8,128)(2,1)S(1)} %fusion.61), channel_id=1, source_target_pairs={{0,2},{2,0},{1,3},{3,1},{4,6},{6,4},{5,7},{7,5},{8,10},{10,8},{9,1... | collective-permute-start | bytes 1179656 | tf_op jit(solution)/shard_map/ppermute | solution.py:24
  152.7 19.4 %collective-permute-start.15 = (bf16[128,2048]{1,0:T(8,128)(2,1)S(1)}, bf16[128,2048]{1,0:T(8,128)(2,1)S(1)}, u32[]{:S(2)}, u32[]{:S(2)}) collective-permute-start(bf16[128,2048]{1,0:T(8,128)(2,1)S(1)} %broadcast_select_fusion), channel_id=1, source_target_pairs={{0,8},{12,4},{4,0},{8,12},{1,9},{13,5},{5,1},{9,13},{2,10},{14,6},... | collective-permute-start | bytes 1572872 | tf_op jit(solution)/shard_map/ppermute | solution.py:31
  154.0 18.0 %collective-permute-start.16 = (bf16[32,2048]{1,0:T(8,128)(2,1)S(1)}, bf16[32,2048]{1,0:T(8,128)(2,1)S(1)}, u32[]{:S(2)}, u32[]{:S(2)}) collective-permute-start(bf16[32,2048]{1,0:T(8,128)(2,1)S(1)} %get-tuple-element.34), channel_id=1, source_target_pairs={{0,12},{4,8},{8,4},{12,0},{1,13},{5,9},{9,5},{13,1},{2,14},{6,10},... | collective-permute-start | bytes 393224 | tf_op jit(solution)/shard_map/ppermute | solution.py:24
  156.5 15.6 %collective-permute-start.17 = (bf16[32,2048]{1,0:T(8,128)(2,1)S(1)}, bf16[32,2048]{1,0:T(8,128)(2,1)S(1)}, u32[]{:S(2)}, u32[]{:S(2)}) collective-permute-start(bf16[32,2048]{1,0:T(8,128)(2,1)S(1)} %get-tuple-element.35), channel_id=1, source_target_pairs={{0,4},{4,0},{8,12},{12,8},{1,5},{5,1},{9,13},{13,9},{2,6},{6,2},{1... | collective-permute-start | bytes 393224 | tf_op jit(solution)/shard_map/ppermute | solution.py:24
  176.8 4.4 %collective-permute-start.23 = (bf16[1,2,32,2048]{3,2,1,0:T(8,128)(2,1)S(1)}, bf16[1,2,32,2048]{3,2,1,0:T(8,128)(2,1)S(1)}, u32[]{:S(2)}, u32[]{:S(2)}) collective-permute-start(bf16[1,2,32,2048]{3,2,1,0:T(8,128)(2,1)S(1)} %fusion.63), channel_id=1, source_target_pairs={{0,1},{1,0},{2,3},{3,2},{4,5},{5,4},{6,7},{7,6},{8,9},{9,8},{10,11... | collective-permute-start | bytes 786440 | tf_op jit(solution)/shard_map/ppermute | solution.py:24
  177.0 12.9 %collective-permute-start.20 = (bf16[32,2048]{1,0:T(8,128)(2,1)S(1)}, bf16[32,2048]{1,0:T(8,128)(2,1)S(1)}, u32[]{:S(2)}, u32[]{:S(2)}) collective-permute-start(bf16[32,2048]{1,0:T(8,128)(2,1)S(1)} %get-tuple-element.40), channel_id=1, source_target_pairs={{0,8},{4,12},{8,0},{12,4},{1,9},{5,13},{9,1},{13,5},{2,10},{6,14},... | collective-permute-start | bytes 393224 | tf_op jit(solution)/shard_map/ppermute | solution.py:24
  179.3 10.6 %collective-permute-start.21 = (bf16[32,2048]{1,0:T(8,128)(2,1)S(1)}, bf16[32,2048]{1,0:T(8,128)(2,1)S(1)}, u32[]{:S(2)}, u32[]{:S(2)}) collective-permute-start(bf16[32,2048]{1,0:T(8,128)(2,1)S(1)} %get-tuple-element.41), channel_id=1, source_target_pairs={{0,12},{4,8},{8,4},{12,0},{1,13},{5,9},{9,5},{13,1},{2,14},{6,10},... | collective-permute-start | bytes 393224 | tf_op jit(solution)/shard_map/ppermute | solution.py:24
  181.2 9.7 %collective-permute-start.22 = (bf16[32,2048]{1,0:T(8,128)(2,1)S(1)}, bf16[32,2048]{1,0:T(8,128)(2,1)S(1)}, u32[]{:S(2)}, u32[]{:S(2)}) collective-permute-start(bf16[32,2048]{1,0:T(8,128)(2,1)S(1)} %get-tuple-element.42), channel_id=1, source_target_pairs={{0,4},{4,0},{8,12},{12,8},{1,5},{5,1},{9,13},{13,9},{2,6},{6,2},{1... | collective-permute-start | bytes 393224 | tf_op jit(solution)/shard_map/ppermute | solution.py:24
  181.3 5.4 %collective-permute-start.24 = (bf16[1,32,2048]{2,1,0:T(8,128)(2,1)S(1)}, bf16[1,32,2048]{2,1,0:T(8,128)(2,1)S(1)}, u32[]{:S(2)}, u32[]{:S(2)}) collective-permute-start(bf16[1,32,2048]{2,1,0:T(8,128)(2,1)S(1)} %fusion.67), channel_id=1, source_target_pairs={{0,2},{2,0},{1,3},{3,1},{4,6},{6,4},{5,7},{7,5},{8,10},{10,8},{9,1... | collective-permute-start | bytes 393224 | tf_op jit(solution)/shard_map/ppermute | solution.py:24
  190.8 8.9 %collective-permute-start.25 = (bf16[32,2048]{1,0:T(8,128)(2,1)S(1)}, bf16[32,2048]{1,0:T(8,128)(2,1)S(1)}, u32[]{:S(2)}, u32[]{:S(2)}) collective-permute-start(bf16[32,2048]{1,0:T(8,128)(2,1)S(1)} %fusion.69), channel_id=1, source_target_pairs={{0,8},{4,12},{8,0},{12,4},{1,9},{5,13},{9,1},{13,5},{2,10},{6,14},... | collective-permute-start | bytes 393224 | tf_op jit(solution)/shard_map/ppermute | solution.py:24
  (17 other events, 181.1 us)

commit v4 on v3

--- a/solution.py
+++ b/solution.py
@@ -33,21 +33,32 @@
 
 def exchange_sum(pieces, axis):
     index = lax.axis_index(axis)
-    total = lax.dynamic_index_in_dim(pieces, index, 0, keepdims=False)
+    total = lax.dynamic_index_in_dim(pieces, index, 0, keepdims=False).astype(jnp.float32)
     for flip in range(1, lax.axis_size(axis)):
         away = lax.dynamic_index_in_dim(pieces, index ^ flip, 0, keepdims=False)
         total = total + swap(away.astype(jnp.bfloat16), axis, flip).astype(jnp.float32)
     return total
 
 
-def project_out(blocks, out_weight, part_rows):
-    heads_size, sub_size = lax.axis_size("heads"), lax.axis_size("sub")
+def project_out(blocks, out_weight):
     rows = jnp.concatenate(blocks, axis=0)
     partial = jnp.dot(rows, out_weight, preferred_element_type=jnp.float32)
-    partial = partial.reshape(len(blocks), heads_size, sub_size, part_rows, -1)
-    by_sub = exchange_sum(jnp.moveaxis(partial, 2, 0), "sub")
-    by_heads = exchange_sum(jnp.moveaxis(by_sub, 1, 0), "heads").astype(jnp.bfloat16)
-    return [by_heads[i] for i in range(len(blocks))]
+    return partial.astype(jnp.bfloat16)
+
+
+def sum_direct(partial, count):
+    axes = ("heads", "sub")
+    pieces = partial.reshape(count, lax.axis_size(axes), -1, partial.shape[1])
+    total = exchange_sum(jnp.moveaxis(pieces, 1, 0), axes).astype(jnp.bfloat16)
+    return [total[i] for i in range(count)]
+
+
+def sum_in_turn(partial, count):
+    heads_size, sub_size = lax.axis_size("heads"), lax.axis_size("sub")
+    pieces = partial.reshape(count, heads_size, sub_size, -1, partial.shape[1])
+    by_sub = exchange_sum(jnp.moveaxis(pieces, 2, 0), "sub")
+    total = exchange_sum(jnp.moveaxis(by_sub, 1, 0), "heads").astype(jnp.bfloat16)
+    return [total[i] for i in range(count)]
 
 
 def fetch_latents(latent_store, place_holder, place_block, serving_request, items):
@@ -157,7 +168,7 @@
         for chunk in range(CHUNKS):
             rows = lax.all_gather(attend(chunk), "pool", axis=0)
             blocks = [rows[i] for i in range(pool_size)]
-            mine = jnp.stack(project_out(blocks, out_weight, part_rows))
+            mine = jnp.stack(sum_in_turn(project_out(blocks, out_weight), pool_size))
             back = lax.all_to_all(mine, "pool", split_axis=0, concat_axis=0, tiled=True)
             outputs.append(jnp.moveaxis(back, 0, 1).reshape(part_rows, pool_size * columns))
         return jnp.concatenate(outputs, axis=0)
@@ -166,23 +177,27 @@
     first = attend(0)
     across0, beside0 = swap(first, "pool", 3), swap(first, "pool", 1)
     last = attend(1)
-    (own0,) = project_out([first], out_weight, part_rows)
-    across0, beside0, last, own0, first = tie((across0, beside0, last, own0, first))
+    first, last, across0, beside0 = tie((first, last, across0, beside0))
     second0 = second_hop(first, across0)
+    partial = project_out([first, beside0, across0, last], out_weight)
+    second0, partial, last = tie((second0, partial, last))
     across1, beside1 = swap(last, "pool", 3), swap(last, "pool", 1)
-    mine = project_out([across0, beside0, last], out_weight, part_rows)
-    second0, across1, beside1, last, mine = tie((second0, across1, beside1, last, mine))
-    out_across0, out_beside0, own1 = mine
+    mine = sum_direct(partial, 4)
+    across1, beside1, mine, last = tie((across1, beside1, mine, last))
+    own0, out_beside0, out_across0, own1 = mine
     second1 = second_hop(last, across1)
+    partial = project_out([beside1, across1, second0], out_weight)
+    second1, partial = tie((second1, partial))
     back_across0, back_beside0 = swap(out_across0, "pool", 3), swap(out_beside0, "pool", 1)
-    mine = project_out([across1, beside1, second0], out_weight, part_rows)
-    second1, back_across0, back_beside0, mine = tie((second1, back_across0, back_beside0, mine))
-    out_across1, out_beside1, out_second0 = mine
-    back_second0, back_across1 = swap(out_second0, "pool", 2), swap(out_across1, "pool", 3)
+    mine = sum_in_turn(partial, 3)
+    partial = project_out([second1], out_weight)
+    back_across0, back_beside0, mine, partial = tie((back_across0, back_beside0, mine, partial))
+    out_beside1, out_across1, out_second0 = mine
+    back_across1, back_second0 = swap(out_across1, "pool", 3), swap(out_second0, "pool", 2)
     back_beside1 = swap(out_beside1, "pool", 1)
-    mine = project_out([second1], out_weight, part_rows)
-    back_second0, back_across1, back_beside1, mine = tie(
-        (back_second0, back_across1, back_beside1, mine)
+    mine = sum_in_turn(partial, 1)
+    back_across1, back_second0, back_beside1, mine = tie(
+        (back_across1, back_second0, back_beside1, mine)
     )
     back_second1 = swap(mine[0], "pool", 2)
     output = jnp.zeros((CHUNKS * part_rows, pool_size * columns), jnp.bfloat16)

time: 201 us -> 184 us (0.915)
  waiting for transfers between devices: 103 us -> 94.7 us
  starting transfers between devices: 34.8 us -> 31.6 us
  matrix products: 41.3 us -> 39.2 us
    ppermute x2, waiting for transfers between devices: 22.6 us -> 10.9 us  [second_hop(): return lax.ppermute(passed, 'pool', [(0, 2), (3, 1), (1, 0), (2, 3)])]
    ppermute x24 -> x23, waiting for transfers between devices: 80.6 us -> 83.8 us  [swap(): lax.ppermute(values, axis, [(i, i ^ flip) for i in range(lax.axis_size(ax...]
    add x4 -> x2, other arithmetic: 3.33 us -> 0.27 us  [exchange_sum(): total + swap(away.astype(jnp.bfloat16), axis, flip).astype(jnp.float32)]
    ppermute x2, starting transfers between devices: 3.58 us -> 1.18 us  [second_hop(): return lax.ppermute(passed, 'pool', [(0, 2), (3, 1), (1, 0), (2, 3)])]
    unnamed x32 -> x34, local copies, waits for them, and re-layouts: 5.83 us -> 3.84 us
    dot_general x4 -> x3, matrix products: 21.2 us -> 19.7 us  [project_out(): partial = jnp.dot(rows, out_weight, preferred_element_type=jnp.float32)]
    ppermute x24 -> x23, starting transfers between devices: 31.3 us -> 30.4 us  [swap(): lax.ppermute(values, axis, [(i, i ^ flip) for i in range(lax.axis_size(ax...]
  transfers between devices with their start and end apart: 26 -> 25, of which waited for: 16 -> 15; matrix products, arithmetic and copies ran while one was open for 6% -> 17% of each run, Pallas kernels for 0% -> 0%
where the time goes in v4:
time: 184 us
  waiting for transfers between devices  94.7 us (51%)
  matrix products  39.2 us (21%)
  starting transfers between devices  31.6 us (17%)
  local copies, waits for them, and re-layouts  12.6 us (7%)
  other arithmetic  5.33 us (3%)
    ppermute x23, waiting for transfers between devices, swap(): lax.ppermute(values, axis, [(i, i ^ flip) for i in range(lax.axis_size(ax...  83.8 us
    ppermute x23, starting transfers between devices, swap(): lax.ppermute(values, axis, [(i, i ^ flip) for i in range(lax.axis_size(ax...  30.4 us
    dot_general x3, matrix products, project_out(): partial = jnp.dot(rows, out_weight, preferred_element_type=jnp.float32)  19.7 us
    ppermute x2, waiting for transfers between devices, second_hop(): return lax.ppermute(passed, 'pool', [(0, 2), (3, 1), (1, 0), (2, 3)])  10.9 us
    dot_general x2, matrix products, attend(): jnp.einsum('rgqts,rsgd->rtgqd', probs, values, preferred_element_type=jnp...  7.82 us
    dot_general x2, matrix products, attend(): jnp.einsum('rtgqd,rsgd->rgqts', normed, keys, preferred_element_type=jnp....  7.03 us
    unnamed x34, local copies, waits for them, and re-layouts  3.84 us
  transfers between devices with their start and end apart: 25, of which 15 were waited for; matrix products, arithmetic and copies ran while one was open for 17% of the time, Pallas kernels for 0%

profile of v4, /device:TPU:0, one launch (start us, length us, event | category | flops | bytes accessed | tf_op | source)
XLA Modules:
  0.0 184.0 jit_solution(312022573310640003)
XLA Ops:
  3.7 2.8 %gather_fusion.1 = bf16[32,32,512]{2,1,0:T(8,128)(2,1)S(1)} fusion(bf16[128,32,512]{2,1,0:T(8,128)(2,1)} %bitcast.170, s32[1024]{0:T(1024)S(1)} %pad_clamp_fusion.1), kind=kCustom, calls=%fused_computation.1 | custom fusion | bytes 2097280 | tf_op jit(solution)/shard_map/gather | solution.py:83
  7.4 3.0 %collective-permute-start = (bf16[8,32,512]{2,1,0:T(8,128)(2,1)}, bf16[8,32,512]{2,1,0:T(8,128)(2,1)S(1)}, u32[]{:S(2)}, u32[]{:S(2)}) collective-permute-start(bf16[8,32,512]{2,1,0:T(8,128)(2,1)} %get-tuple-element.70), channel_id=1, source_target_pairs={{0,4},{4,0},{8,12},{12,8},{1,5},{5,1},{9,13},{13,9},{2,6},{6,2},{1... | collective-permute-start | bytes 786440 | tf_op jit(solution)/shard_map/ppermute | solution.py:24
  10.4 2.6 %collective-permute-start.1 = (bf16[8,32,512]{2,1,0:T(8,128)(2,1)}, bf16[8,32,512]{2,1,0:T(8,128)(2,1)S(1)}, u32[]{:S(2)}, u32[]{:S(2)}) collective-permute-start(bf16[8,32,512]{2,1,0:T(8,128)(2,1)} %get-tuple-element.69), channel_id=1, source_target_pairs={{0,8},{4,12},{8,0},{12,4},{1,9},{5,13},{9,1},{13,5},{2,10},{6,14},... | collective-permute-start | bytes 786440 | tf_op jit(solution)/shard_map/ppermute | solution.py:24
  13.0 8.7 %collective-permute-done = bf16[8,32,512]{2,1,0:T(8,128)(2,1)S(1)} collective-permute-done((bf16[8,32,512]{2,1,0:T(8,128)(2,1)}, bf16[8,32,512]{2,1,0:T(8,128)(2,1)S(1)}, u32[]{:S(2)}, u32[]{:S(2)}) %collective-permute-start) | collective-permute-done | bytes 262176 | tf_op jit(solution)/shard_map/ppermute | solution.py:24
  21.8 10.2 %collective-permute-done.1 = bf16[8,32,512]{2,1,0:T(8,128)(2,1)S(1)} collective-permute-done((bf16[8,32,512]{2,1,0:T(8,128)(2,1)}, bf16[8,32,512]{2,1,0:T(8,128)(2,1)S(1)}, u32[]{:S(2)}, u32[]{:S(2)}) %collective-permute-start.1) | collective-permute-done | bytes 262176 | tf_op jit(solution)/shard_map/ppermute | solution.py:24
  38.3 7.6 %collective-permute-done.4 = bf16[2,256,512]{2,1,0:T(8,128)(2,1)} collective-permute-done((bf16[2,256,512]{2,1,0:T(8,128)(2,1)S(1)}, bf16[2,256,512]{2,1,0:T(8,128)(2,1)}, u32[]{:S(2)}, u32[]{:S(2)}) %collective-permute-start.4) | collective-permute-done | bytes 524320 | tf_op jit(solution)/shard_map/ppermute | solution.py:24
  48.1 2.7 %fusion.6 = f32[2,1024,2,2,128]{1,4,3,2,0:T(8,128)S(1)} fusion(bf16[2,256,512]{2,1,0:T(8,128)(2,1)} %collective-permute-done.5, bf16[2,256,512]{2,1,0:T(8,128)(2,1)} %collective-permute-done.4, bf16[2,256,512]{2,1,0:T(8,128)(2,1)} %collective-permute-done.3, bf16[2,256,512]{2,1,0:T(8,128)(2,1)S(1)} %bitcast.167, bf16[512,2,2,128]{0,3,2,1:T(8,128)(2,1)S(1)} %copy.50), kind=kOutput, calls=%fused_computation.19 | convolution fusion | flops 1082130432 | bytes 6815744 | tf_op jit(solution)/shard_map/rsk,kgcd->rsgcd/dot_general | solution.py:127
  52.4 5.7 %bitcast_reduce_fusion = (f32[2,2,8,64]{3,2,1,0:T(8,128)S(1)}, f32[2,2,8,64]{3,2,1,0:T(8,128)S(1)}, f32[2,2,1024,64,8]{2,3,4,1,0:T(8,128)}) fusion(pred[2,1024]{1,0:T(4,128)(4,1)S(1)} %broadcast_compare_fusion, f32[2,2,1024,64,8]{2,3,4,1,0:T(8,128)S(1)} %fusion.47, f32[2,64,2,8,128]{4,3,2,1,0:T(8,128)S(1)} %bitcast.162, f32[2,64,2,8]{1,3,2,0:T(8,128)S(1)} %copy.56, ...), kind=kOutput, calls=%fused_computation.4 | convolution fusion | flops 551809024 | bytes 19977216 | tf_op jit(solution)/shard_map/rtgqd,rsgd->rgqts/dot_general | solution.py:156
  62.1 6.3 %collective-permute-start.7 = (bf16[128,2048]{1,0:T(8,128)(2,1)S(1)}, bf16[128,2048]{1,0:T(8,128)(2,1)S(1)}, u32[]{:S(2)}, u32[]{:S(2)}) collective-permute-start(bf16[128,2048]{1,0:T(8,128)(2,1)S(1)} %reshape.326), channel_id=1, source_target_pairs={{0,4},{4,0},{8,12},{12,8},{1,5},{5,1},{9,13},{13,9},{2,6},{6,2},{1... | collective-permute-start | bytes 1572872 | tf_op jit(solution)/shard_map/ppermute | solution.py:24
  68.4 5.8 %fusion.34 = bf16[2,64,2,8,128]{4,1,3,2,0:T(8,128)(2,1)S(1)} fusion(f32[2,2,1024,64,8]{2,3,4,1,0:T(8,128)} %get-tuple-element.79, f32[2,2,8,64]{3,2,1,0:T(8,128)S(1)} %get-tuple-element.59, pred[2,1024]{1,0:T(4,128)(4,1)S(1)} %broadcast_compare_fusion, f32[2,1024,2,2,128]{1,4,3,2,0:T(8,128)} %copy-done.2), kind=kOutput, calls=%fused_computation.44 | convolution fusion | flops 545521664 | bytes 9971712 | tf_op jit(solution)/shard_map/rgqts,rsgd->rtgqd/dot_general | solution.py:161
  74.8 2.6 %collective-permute-done.6 = bf16[128,2048]{1,0:T(8,128)(2,1)S(1)} collective-permute-done((bf16[128,2048]{1,0:T(8,128)(2,1)S(1)}, bf16[128,2048]{1,0:T(8,128)(2,1)S(1)}, u32[]{:S(2)}, u32[]{:S(2)}) %collective-permute-start.6) | collective-permute-done | bytes 524320 | tf_op jit(solution)/shard_map/ppermute | solution.py:24
  77.4 10.4 %collective-permute-done.7 = bf16[128,2048]{1,0:T(8,128)(2,1)S(1)} collective-permute-done((bf16[128,2048]{1,0:T(8,128)(2,1)S(1)}, bf16[128,2048]{1,0:T(8,128)(2,1)S(1)}, u32[]{:S(2)}, u32[]{:S(2)}) %collective-permute-start.7) | collective-permute-done | bytes 524320 | tf_op jit(solution)/shard_map/ppermute | solution.py:24
  89.2 8.3 %convolution_convert_fusion = bf16[512,2048]{1,0:T(8,128)(2,1)S(1)} fusion(bf16[2048,2048]{1,0:T(8,128)(2,1)} %param.15, bf16[128,2048]{1,0:T(8,128)(2,1)S(1)} %reshape.327, bf16[128,2048]{1,0:T(8,128)(2,1)} %copy-done.6, bf16[128,2048]{1,0:T(8,128)(2,1)} %copy-done.13, bf16[128,2048]{1,0:T(8,128)(2,1)S(1)} %reshape.326), kind=kOutput, calls=%fused_computation.13 | convolution fusion | flops 4304404480 | bytes 12582912 | tf_op jit(solution)/shard_map/dot_general | solution.py:45
  97.4 4.9 %collective-permute-done.8 = bf16[128,2048]{1,0:T(8,128)(2,1)S(1)} collective-permute-done((bf16[128,2048]{1,0:T(8,128)(2,1)S(1)}, bf16[128,2048]{1,0:T(8,128)(2,1)S(1)}, u32[]{:S(2)}, u32[]{:S(2)}) %collective-permute-start.8) | collective-permute-done | bytes 524320 | tf_op jit(solution)/shard_map/ppermute | solution.py:31
  108.4 10.1 %collective-permute-done.12 = bf16[4,32,2048]{2,1,0:T(8,128)(2,1)} collective-permute-done((bf16[4,32,2048]{2,1,0:T(8,128)(2,1)}, bf16[4,32,2048]{2,1,0:T(8,128)(2,1)}, u32[]{:S(2)}, u32[]{:S(2)}) %collective-permute-start.12) | collective-permute-done | bytes 524320 | tf_op jit(solution)/shard_map/ppermute | solution.py:24
  118.6 10.5 %collective-permute-done.13 = bf16[4,32,2048]{2,1,0:T(8,128)(2,1)} collective-permute-done((bf16[4,32,2048]{2,1,0:T(8,128)(2,1)S(1)}, bf16[4,32,2048]{2,1,0:T(8,128)(2,1)}, u32[]{:S(2)}, u32[]{:S(2)}) %collective-permute-start.13) | collective-permute-done | bytes 524320 | tf_op jit(solution)/shard_map/ppermute | solution.py:24
  132.5 6.8 %convolution_convert_fusion.1 = bf16[384,2048]{1,0:T(8,128)(2,1)S(1)} fusion(bf16[2048,2048]{1,0:T(8,128)(2,1)} %param.15, bf16[128,2048]{1,0:T(8,128)(2,1)S(1)} %copy-done.12, bf16[128,2048]{1,0:T(8,128)(2,1)S(1)} %collective-permute-done.9, bf16[128,2048]{1,0:T(8,128)(2,1)S(1)} %collective-permute-done.10), kind=kOutput, calls=%fused_computation.14 | convolution fusion | flops 3226730496 | bytes 11534336 | tf_op jit(solution)/shard_map/dot_general | solution.py:45
  139.3 5.9 %collective-permute-done.16 = bf16[128,2048]{1,0:T(8,128)(2,1)S(1)} collective-permute-done((bf16[128,2048]{1,0:T(8,128)(2,1)S(1)}, bf16[128,2048]{1,0:T(8,128)(2,1)S(1)}, u32[]{:S(2)}, u32[]{:S(2)}) %collective-permute-start.16) | collective-permute-done | bytes 524320 | tf_op jit(solution)/shard_map/ppermute | solution.py:31
  150.2 4.7 %convolution_convert_fusion.2 = bf16[128,2048]{1,0:T(8,128)(2,1)S(1)} fusion(bf16[128,2048]{1,0:T(8,128)(2,1)S(1)} %collective-permute-done.16, bf16[2048,2048]{1,0:T(8,128)(2,1)} %param.15), kind=kOutput, calls=%fused_computation.15 | convolution fusion | flops 1074003968 | bytes 9437184 | tf_op jit(solution)/shard_map/dot_general | solution.py:45
  154.9 4.7 %collective-permute-done.18 = bf16[3,32,2048]{2,1,0:T(8,128)(2,1)S(1)} collective-permute-done((bf16[3,32,2048]{2,1,0:T(8,128)(2,1)S(1)}, bf16[3,32,2048]{2,1,0:T(8,128)(2,1)S(1)}, u32[]{:S(2)}, u32[]{:S(2)}) %collective-permute-start.18) | collective-permute-done | bytes 393248 | tf_op jit(solution)/shard_map/ppermute | solution.py:24
  159.9 2.7 %collective-permute-start.19 = (bf16[32,2048]{1,0:T(8,128)(2,1)S(1)}, bf16[32,2048]{1,0:T(8,128)(2,1)S(1)}, u32[]{:S(2)}, u32[]{:S(2)}) collective-permute-start(bf16[32,2048]{1,0:T(8,128)(2,1)S(1)} %get-tuple-element.48), channel_id=1, source_target_pairs={{0,12},{4,8},{8,4},{12,0},{1,13},{5,9},{9,5},{13,1},{2,14},{6,10},... | collective-permute-start | bytes 393224 | tf_op jit(solution)/shard_map/ppermute | solution.py:24
  166.1 3.5 %collective-permute-done.23 = bf16[1,32,2048]{2,1,0:T(8,128)(2,1)S(1)} collective-permute-done((bf16[1,32,2048]{2,1,0:T(8,128)(2,1)S(1)}, bf16[1,32,2048]{2,1,0:T(8,128)(2,1)S(1)}, u32[]{:S(2)}, u32[]{:S(2)}) %collective-permute-start.23) | collective-permute-done | bytes 131104 | tf_op jit(solution)/shard_map/ppermute | solution.py:24
  169.7 6.3 %collective-permute-done.20 = bf16[32,2048]{1,0:T(8,128)(2,1)S(1)} collective-permute-done((bf16[32,2048]{1,0:T(8,128)(2,1)S(1)}, bf16[32,2048]{1,0:T(8,128)(2,1)S(1)}, u32[]{:S(2)}, u32[]{:S(2)}) %collective-permute-start.20) | collective-permute-done | bytes 131104 | tf_op jit(solution)/shard_map/ppermute | solution.py:24
  176.1 7.3 %collective-permute-done.24 = bf16[32,2048]{1,0:T(8,128)(2,1)S(1)} collective-permute-done((bf16[32,2048]{1,0:T(8,128)(2,1)S(1)}, bf16[32,2048]{1,0:T(8,128)(2,1)S(1)}, u32[]{:S(2)}, u32[]{:S(2)}) %collective-permute-start.24) | collective-permute-done | bytes 131104 | tf_op jit(solution)/shard_map/ppermute | solution.py:24
  (128 shorter events, 39.4 us)
Async XLA Ops:
  7.4 14.4 %collective-permute-start = (bf16[8,32,512]{2,1,0:T(8,128)(2,1)}, bf16[8,32,512]{2,1,0:T(8,128)(2,1)S(1)}, u32[]{:S(2)}, u32[]{:S(2)}) collective-permute-start(bf16[8,32,512]{2,1,0:T(8,128)(2,1)} %get-tuple-element.70), channel_id=1, source_target_pairs={{0,4},{4,0},{8,12},{12,8},{1,5},{5,1},{9,13},{13,9},{2,6},{6,2},{1... | collective-permute-start | bytes 786440 | tf_op jit(solution)/shard_map/ppermute | solution.py:24
  10.4 21.6 %collective-permute-start.1 = (bf16[8,32,512]{2,1,0:T(8,128)(2,1)}, bf16[8,32,512]{2,1,0:T(8,128)(2,1)S(1)}, u32[]{:S(2)}, u32[]{:S(2)}) collective-permute-start(bf16[8,32,512]{2,1,0:T(8,128)(2,1)} %get-tuple-element.69), channel_id=1, source_target_pairs={{0,8},{4,12},{8,0},{12,4},{1,9},{5,13},{9,1},{13,5},{2,10},{6,14},... | collective-permute-start | bytes 786440 | tf_op jit(solution)/shard_map/ppermute | solution.py:24
  13.0 19.0 %collective-permute-start.2 = (bf16[8,32,512]{2,1,0:T(8,128)(2,1)S(1)}, bf16[8,32,512]{2,1,0:T(8,128)(2,1)S(1)}, u32[]{:S(2)}, u32[]{:S(2)}) collective-permute-start(bf16[8,32,512]{2,1,0:T(8,128)(2,1)S(1)} %get-tuple-element.71), channel_id=1, source_target_pairs={{0,12},{4,8},{8,4},{12,0},{1,13},{5,9},{9,5},{13,1},{2,14},{6,10},... | collective-permute-start | bytes 786440 | tf_op jit(solution)/shard_map/ppermute | solution.py:24
  35.1 10.7 %collective-permute-start.4 = (bf16[2,256,512]{2,1,0:T(8,128)(2,1)S(1)}, bf16[2,256,512]{2,1,0:T(8,128)(2,1)}, u32[]{:S(2)}, u32[]{:S(2)}) collective-permute-start(bf16[2,256,512]{2,1,0:T(8,128)(2,1)S(1)} %bitcast.165), channel_id=1, source_target_pairs={{0,2},{2,0},{1,3},{3,1},{4,6},{6,4},{5,7},{7,5},{8,10},{10,8},{9,1... | collective-permute-start | bytes 1572872 | tf_op jit(solution)/shard_map/ppermute | solution.py:24
  38.2 9.0 %collective-permute-start.3 = (bf16[2,256,512]{2,1,0:T(8,128)(2,1)S(1)}, bf16[2,256,512]{2,1,0:T(8,128)(2,1)}, u32[]{:S(2)}, u32[]{:S(2)}) collective-permute-start(bf16[2,256,512]{2,1,0:T(8,128)(2,1)S(1)} %bitcast.166), channel_id=1, source_target_pairs={{0,1},{1,0},{2,3},{3,2},{4,5},{5,4},{6,7},{7,6},{8,9},{9,8},{10,11... | collective-permute-start | bytes 1572872 | tf_op jit(solution)/shard_map/ppermute | solution.py:24
  60.7 16.7 %collective-permute-start.6 = (bf16[128,2048]{1,0:T(8,128)(2,1)S(1)}, bf16[128,2048]{1,0:T(8,128)(2,1)S(1)}, u32[]{:S(2)}, u32[]{:S(2)}) collective-permute-start(bf16[128,2048]{1,0:T(8,128)(2,1)S(1)} %reshape.326), channel_id=1, source_target_pairs={{0,12},{4,8},{8,4},{12,0},{1,13},{5,9},{9,5},{13,1},{2,14},{6,10},... | collective-permute-start | bytes 1572872 | tf_op jit(solution)/shard_map/ppermute | solution.py:24
  62.1 25.6 %collective-permute-start.7 = (bf16[128,2048]{1,0:T(8,128)(2,1)S(1)}, bf16[128,2048]{1,0:T(8,128)(2,1)S(1)}, u32[]{:S(2)}, u32[]{:S(2)}) collective-permute-start(bf16[128,2048]{1,0:T(8,128)(2,1)S(1)} %reshape.326), channel_id=1, source_target_pairs={{0,4},{4,0},{8,12},{12,8},{1,5},{5,1},{9,13},{13,9},{2,6},{6,2},{1... | collective-permute-start | bytes 1572872 | tf_op jit(solution)/shard_map/ppermute | solution.py:24
  88.6 13.8 %collective-permute-start.8 = (bf16[128,2048]{1,0:T(8,128)(2,1)S(1)}, bf16[128,2048]{1,0:T(8,128)(2,1)S(1)}, u32[]{:S(2)}, u32[]{:S(2)}) collective-permute-start(bf16[128,2048]{1,0:T(8,128)(2,1)S(1)} %broadcast_select_fusion.1), channel_id=1, source_target_pairs={{0,8},{12,4},{4,0},{8,12},{1,9},{13,5},{5,1},{9,13},{2,10},{14,6},... | collective-permute-start | bytes 1572872 | tf_op jit(solution)/shard_map/ppermute | solution.py:31
  103.5 4.9 %collective-permute-start.11 = (bf16[4,32,2048]{2,1,0:T(8,128)(2,1)}, bf16[4,32,2048]{2,1,0:T(8,128)(2,1)}, u32[]{:S(2)}, u32[]{:S(2)}) collective-permute-start(bf16[4,32,2048]{2,1,0:T(8,128)(2,1)} %get-tuple-element.61), channel_id=1, source_target_pairs={{0,1},{1,0},{2,3},{3,2},{4,5},{5,4},{6,7},{7,6},{8,9},{9,8},{10,11... | collective-permute-start | bytes 1572872 | tf_op jit(solution)/shard_map/ppermute | solution.py:24
  103.5 15.0 %collective-permute-start.12 = (bf16[4,32,2048]{2,1,0:T(8,128)(2,1)}, bf16[4,32,2048]{2,1,0:T(8,128)(2,1)}, u32[]{:S(2)}, u32[]{:S(2)}) collective-permute-start(bf16[4,32,2048]{2,1,0:T(8,128)(2,1)} %get-tuple-element.63), channel_id=1, source_target_pairs={{0,2},{1,3},{2,0},{3,1},{4,6},{5,7},{6,4},{7,5},{8,10},{9,11},{10,... | collective-permute-start | bytes 1572872 | tf_op jit(solution)/shard_map/ppermute | solution.py:24
  105.1 23.9 %collective-permute-start.13 = (bf16[4,32,2048]{2,1,0:T(8,128)(2,1)S(1)}, bf16[4,32,2048]{2,1,0:T(8,128)(2,1)}, u32[]{:S(2)}, u32[]{:S(2)}) collective-permute-start(bf16[4,32,2048]{2,1,0:T(8,128)(2,1)S(1)} %get-tuple-element.62), channel_id=1, source_target_pairs={{0,3},{1,2},{2,1},{3,0},{4,7},{5,6},{6,5},{7,4},{8,11},{9,10},{10,... | collective-permute-start | bytes 1572872 | tf_op jit(solution)/shard_map/ppermute | solution.py:24
  105.4 25.4 %collective-permute-start.10 = (bf16[128,2048]{1,0:T(8,128)(2,1)S(1)}, bf16[128,2048]{1,0:T(8,128)(2,1)S(1)}, u32[]{:S(2)}, u32[]{:S(2)}) collective-permute-start(bf16[128,2048]{1,0:T(8,128)(2,1)S(1)} %reshape.327), channel_id=1, source_target_pairs={{0,4},{4,0},{8,12},{12,8},{1,5},{5,1},{9,13},{13,9},{2,6},{6,2},{1... | collective-permute-start | bytes 1572872 | tf_op jit(solution)/shard_map/ppermute | solution.py:24
  107.1 24.8 %collective-permute-start.9 = (bf16[128,2048]{1,0:T(8,128)(2,1)S(1)}, bf16[128,2048]{1,0:T(8,128)(2,1)S(1)}, u32[]{:S(2)}, u32[]{:S(2)}) collective-permute-start(bf16[128,2048]{1,0:T(8,128)(2,1)S(1)} %reshape.327), channel_id=1, source_target_pairs={{0,12},{4,8},{8,4},{12,0},{1,13},{5,9},{9,5},{13,1},{2,14},{6,10},... | collective-permute-start | bytes 1572872 | tf_op jit(solution)/shard_map/ppermute | solution.py:24
  131.9 13.3 %collective-permute-start.16 = (bf16[128,2048]{1,0:T(8,128)(2,1)S(1)}, bf16[128,2048]{1,0:T(8,128)(2,1)S(1)}, u32[]{:S(2)}, u32[]{:S(2)}) collective-permute-start(bf16[128,2048]{1,0:T(8,128)(2,1)S(1)} %broadcast_select_fusion), channel_id=1, source_target_pairs={{0,8},{12,4},{4,0},{8,12},{1,9},{13,5},{5,1},{9,13},{2,10},{14,6},... | collective-permute-start | bytes 1572872 | tf_op jit(solution)/shard_map/ppermute | solution.py:31
  145.4 3.0 %collective-permute-start.17 = (bf16[3,2,32,2048]{3,2,0,1:T(8,128)(2,1)S(1)}, bf16[3,2,32,2048]{3,2,0,1:T(8,128)(2,1)S(1)}, u32[]{:S(2)}, u32[]{:S(2)}) collective-permute-start(bf16[3,2,32,2048]{3,2,0,1:T(8,128)(2,1)S(1)} %bitcast.164), channel_id=1, source_target_pairs={{0,1},{1,0},{2,3},{3,2},{4,5},{5,4},{6,7},{7,6},{8,9},{9,8},{10,11... | collective-permute-start | bytes 2359304 | tf_op jit(solution)/shard_map/ppermute | solution.py:24
  145.5 14.2 %collective-permute-start.14 = (bf16[32,2048]{1,0:T(8,128)(2,1)S(1)}, bf16[32,2048]{1,0:T(8,128)(2,1)S(1)}, u32[]{:S(2)}, u32[]{:S(2)}) collective-permute-start(bf16[32,2048]{1,0:T(8,128)(2,1)S(1)} %get-tuple-element.38), channel_id=1, source_target_pairs={{0,12},{4,8},{8,4},{12,0},{1,13},{5,9},{9,5},{13,1},{2,14},{6,10},... | collective-permute-start | bytes 393224 | tf_op jit(solution)/shard_map/ppermute | solution.py:24
  148.0 11.7 %collective-permute-start.15 = (bf16[32,2048]{1,0:T(8,128)(2,1)S(1)}, bf16[32,2048]{1,0:T(8,128)(2,1)S(1)}, u32[]{:S(2)}, u32[]{:S(2)}) collective-permute-start(bf16[32,2048]{1,0:T(8,128)(2,1)S(1)} %get-tuple-element.39), channel_id=1, source_target_pairs={{0,4},{4,0},{8,12},{12,8},{1,5},{5,1},{9,13},{13,9},{2,6},{6,2},{1... | collective-permute-start | bytes 393224 | tf_op jit(solution)/shard_map/ppermute | solution.py:24
  148.6 11.0 %collective-permute-start.18 = (bf16[3,32,2048]{2,1,0:T(8,128)(2,1)S(1)}, bf16[3,32,2048]{2,1,0:T(8,128)(2,1)S(1)}, u32[]{:S(2)}, u32[]{:S(2)}) collective-permute-start(bf16[3,32,2048]{2,1,0:T(8,128)(2,1)S(1)} %fusion.58), channel_id=1, source_target_pairs={{0,2},{2,0},{1,3},{3,1},{4,6},{6,4},{5,7},{7,5},{8,10},{10,8},{9,1... | collective-permute-start | bytes 1179656 | tf_op jit(solution)/shard_map/ppermute | solution.py:24
  159.8 4.7 %collective-permute-start.22 = (bf16[1,2,32,2048]{3,2,1,0:T(8,128)(2,1)S(1)}, bf16[1,2,32,2048]{3,2,1,0:T(8,128)(2,1)S(1)}, u32[]{:S(2)}, u32[]{:S(2)}) collective-permute-start(bf16[1,2,32,2048]{3,2,1,0:T(8,128)(2,1)S(1)} %dynamic-slice_bitcast_fusion.3), channel_id=1, source_target_pairs={{0,1},{1,0},{2,3},{3,2},{4,5},{5,4},{6,7},{7,6},{8,9},{9,8},{10,11... | collective-permute-start | bytes 786440 | tf_op jit(solution)/shard_map/ppermute | solution.py:24
  159.9 9.7 %collective-permute-start.19 = (bf16[32,2048]{1,0:T(8,128)(2,1)S(1)}, bf16[32,2048]{1,0:T(8,128)(2,1)S(1)}, u32[]{:S(2)}, u32[]{:S(2)}) collective-permute-start(bf16[32,2048]{1,0:T(8,128)(2,1)S(1)} %get-tuple-element.48), channel_id=1, source_target_pairs={{0,12},{4,8},{8,4},{12,0},{1,13},{5,9},{9,5},{13,1},{2,14},{6,10},... | collective-permute-start | bytes 393224 | tf_op jit(solution)/shard_map/ppermute | solution.py:24
  162.7 13.3 %collective-permute-start.20 = (bf16[32,2048]{1,0:T(8,128)(2,1)S(1)}, bf16[32,2048]{1,0:T(8,128)(2,1)S(1)}, u32[]{:S(2)}, u32[]{:S(2)}) collective-permute-start(bf16[32,2048]{1,0:T(8,128)(2,1)S(1)} %get-tuple-element.49), channel_id=1, source_target_pairs={{0,8},{4,12},{8,0},{12,4},{1,9},{5,13},{9,1},{13,5},{2,10},{6,14},... | collective-permute-start | bytes 393224 | tf_op jit(solution)/shard_map/ppermute | solution.py:24
  163.7 12.3 %collective-permute-start.21 = (bf16[32,2048]{1,0:T(8,128)(2,1)S(1)}, bf16[32,2048]{1,0:T(8,128)(2,1)S(1)}, u32[]{:S(2)}, u32[]{:S(2)}) collective-permute-start(bf16[32,2048]{1,0:T(8,128)(2,1)S(1)} %get-tuple-element.50), channel_id=1, source_target_pairs={{0,4},{4,0},{8,12},{12,8},{1,5},{5,1},{9,13},{13,9},{2,6},{6,2},{1... | collective-permute-start | bytes 393224 | tf_op jit(solution)/shard_map/ppermute | solution.py:24
  164.5 5.1 %collective-permute-start.23 = (bf16[1,32,2048]{2,1,0:T(8,128)(2,1)S(1)}, bf16[1,32,2048]{2,1,0:T(8,128)(2,1)S(1)}, u32[]{:S(2)}, u32[]{:S(2)}) collective-permute-start(bf16[1,32,2048]{2,1,0:T(8,128)(2,1)S(1)} %fusion.60), channel_id=1, source_target_pairs={{0,2},{2,0},{1,3},{3,1},{4,6},{6,4},{5,7},{7,5},{8,10},{10,8},{9,1... | collective-permute-start | bytes 393224 | tf_op jit(solution)/shard_map/ppermute | solution.py:24
  176.0 7.4 %collective-permute-start.24 = (bf16[32,2048]{1,0:T(8,128)(2,1)S(1)}, bf16[32,2048]{1,0:T(8,128)(2,1)S(1)}, u32[]{:S(2)}, u32[]{:S(2)}) collective-permute-start(bf16[32,2048]{1,0:T(8,128)(2,1)S(1)} %fusion.61), channel_id=1, source_target_pairs={{0,8},{4,12},{8,0},{12,4},{1,9},{5,13},{9,1},{13,5},{2,10},{6,14},... | collective-permute-start | bytes 393224 | tf_op jit(solution)/shard_map/ppermute | solution.py:24
  (17 other events, 238.6 us)

commit v5 on v4

v5 whole, which is shorter than its diff:
```python
import functools
import math

import jax
import jax.numpy as jnp
from jax import lax
from jax.experimental import pallas as pl
from jax.experimental.pallas import tpu as pltpu
from jax.sharding import PartitionSpec as P

BLK = 128


def rms_scale(values, gain):
    return values * lax.rsqrt(jnp.mean(values * values, axis=-1, keepdims=True) + 1e-05) * gain


def pair_rank(holders):
    count = holders.shape[1]
    same = holders[:, :, None] == holders[:, None, :]
    earlier = jnp.arange(count)[None, :] < jnp.arange(count)[:, None]
    return jnp.sum((same & earlier[None]).astype(jnp.int32), axis=2)


def swap(values, axis, flip):
    return lax.ppermute(values, axis, [(i, i ^ flip) for i in range(lax.axis_size(axis))])


def second_hop(block, across):
    index = lax.axis_index("pool")
    at_end = (index == 0) | (index == 3)
    passed = jnp.where(at_end, block, across)
    return lax.ppermute(passed, "pool", [(0, 2), (3, 1), (1, 0), (2, 3)])


def exchange_sum(pieces, axis):
    index = lax.axis_index(axis)
    total = lax.dynamic_index_in_dim(pieces, index, 0, keepdims=False).astype(jnp.float32)
    for flip in range(1, lax.axis_size(axis)):
        away = lax.dynamic_index_in_dim(pieces, index ^ flip, 0, keepdims=False)
        total = total + swap(away.astype(jnp.bfloat16), axis, flip).astype(jnp.float32)
    return total


def project_out(blocks, out_weight):
    rows = jnp.concatenate(blocks, axis=0)
    partial = jnp.dot(rows, out_weight, preferred_element_type=jnp.float32)
    return partial.astype(jnp.bfloat16)


def sum_in_turn(partial, count):
    heads_size, sub_size = lax.axis_size("heads"), lax.axis_size("sub")
    pieces = partial.reshape(count, heads_size, sub_size, -1, partial.shape[1])
    by_sub = exchange_sum(jnp.moveaxis(pieces, 2, 0), "sub")
    total = exchange_sum(jnp.moveaxis(by_sub, 1, 0), "heads").astype(jnp.bfloat16)
    return [total[i] for i in range(count)]


def fetch_latents(latent_store, place_holder, place_block, serving_request, items):
    pool_size = lax.axis_size("pool")
    pool_index = lax.axis_index("pool")
    share_count = lax.axis_size(("heads", "sub"))
    share = lax.axis_index(("heads", "sub"))
    capacity = 2 * ((items + pool_size - 1) // pool_size)
    total_requests = serving_request.shape[0]
    request_ids = jnp.arange(total_requests, dtype=jnp.int32)
    selector = (serving_request[:, None] == request_ids[None, :]).astype(jnp.int32)
    holders = jnp.dot(selector, place_holder).reshape(pool_size, items)
    blocks = jnp.dot(selector, place_block).reshape(pool_size, items)
    ranks = pair_rank(holders)
    slot_ids = jnp.arange(capacity, dtype=jnp.int32)
    matched = (holders[:, None, :] == pool_index) & (ranks[:, None, :] == slot_ids[None, :, None])
    send_block = jnp.sum(jnp.where(matched, blocks[:, None, :], 0), axis=2)
    rows = BLK // share_count
    store = latent_store.reshape(-1, rows, latent_store.shape[1])
    partners = jnp.arange(pool_size, dtype=jnp.int32) ^ pool_index
    wanted = send_block.at[partners].get(mode="promise_in_bounds").reshape(-1)
    outgoing = store.at[wanted * share_count + share].get(mode="promise_in_bounds")
    outgoing = outgoing.reshape(pool_size, capacity, rows, -1)
    pieces = [outgoing[0]] + [swap(outgoing[flip], "pool", flip) for flip in range(1, pool_size)]
    my_holders = lax.dynamic_index_in_dim(holders, pool_index, 0, keepdims=False)
    my_ranks = lax.dynamic_index_in_dim(ranks, pool_index, 0, keepdims=False)
    chosen = jnp.concatenate(pieces, axis=0).at[(my_holders ^ pool_index) * capacity + my_ranks]
    return selector, chosen.get(mode="promise_in_bounds")


def attend_kernel(share_count, scalars, queries, *refs):
    parts, (kv_up, q_gain, k_gain, out, keys, values) = refs[:share_count], refs[share_count:]
    head_width = q_gain.shape[1]
    per_group = queries.shape[2] // head_width
    part_slots = parts[0].shape[1]
    share_rows = BLK // share_count
    count, share = scalars[0], scalars[1]
    for flip in range(share_count):
        rows = pl.ds(flip * part_slots, part_slots)
        projected = jnp.dot(parts[flip][0], kv_up[...], preferred_element_type=jnp.float32)
        key = rms_scale(projected[:, :head_width], k_gain[...])
        keys[rows, :] = key.astype(jnp.bfloat16)
        slot = lax.broadcasted_iota(jnp.int32, (part_slots, head_width), 0)
        position = (slot // share_rows) * BLK + (share ^ flip) * share_rows + slot % share_rows
        live = jnp.where(position < count, 1.0, 0.0)
        values[rows, :head_width] = (projected[:, head_width:] * live).astype(jnp.bfloat16)
        values[rows, head_width:] = live.astype(jnp.bfloat16)
    scale = math.log2(math.e) / math.sqrt(head_width)
    together = 2 if per_group % 2 == 0 else 1
    text = queries.shape[1]
    for first in range(0, per_group, together):
        normed = []
        for head in range(first, first + together):
            query = queries[0, :, head * head_width : (head + 1) * head_width]
            normed.append(rms_scale(query.astype(jnp.float32), q_gain[...]).astype(jnp.bfloat16))
        scores = lax.dot_general(
            jnp.concatenate(normed, axis=0),
            keys[...],
            (((1,), (1,)), ((), ())),
            preferred_element_type=jnp.float32,
        )
        expo = jnp.exp2(scores * scale).astype(jnp.bfloat16)
        total = jnp.dot(expo, values[...], preferred_element_type=jnp.float32)
        result = (total[:, :head_width] / total[:, head_width:]).astype(jnp.bfloat16)
        for i in range(together):
            head = first + i
            columns = slice(head * head_width, (head + 1) * head_width)
            out[:, columns] = result[i * text : (i + 1) * text]


def attend(request, queries, parts, kv_flat, q_gain, k_gain, scalars):
    _, text, width = queries.shape
    heads_here, rank_width, pair_width = kv_flat.shape
    head_width = q_gain.shape[1]
    part_slots = parts[0].shape[1]
    slots = len(parts) * part_slots
    here = lambda g: (request, 0, 0)
    return pl.pallas_call(
        functools.partial(attend_kernel, len(parts)),
        grid=(heads_here,),
        in_specs=[
            pl.BlockSpec(memory_space=pltpu.SMEM),
            pl.BlockSpec((1, text, width // heads_here), lambda g: (request, 0, g)),
        ]
        + [pl.BlockSpec((1, part_slots, rank_width), here) for _ in parts]
        + [
            pl.BlockSpec((None, rank_width, pair_width), lambda g: (g, 0, 0)),
            pl.BlockSpec((1, head_width), lambda g: (0, 0)),
            pl.BlockSpec((1, head_width), lambda g: (0, 0)),
        ],
        out_specs=pl.BlockSpec((text, width // heads_here), lambda g: (0, g)),
        out_shape=jax.ShapeDtypeStruct((text, width), jnp.bfloat16),
        scratch_shapes=[
            pltpu.VMEM((slots, head_width), jnp.bfloat16),
            pltpu.VMEM((slots, 2 * head_width), jnp.bfloat16),
        ],
        compiler_params=pltpu.CompilerParams(vmem_limit_bytes=32 * 1024 * 1024),
        cost_estimate=pl.CostEstimate(
            flops=4 * text * width * slots + 2 * slots * rank_width * heads_here * pair_width,
            bytes_accessed=4 * text * width + 2 * slots * rank_width,
            transcendentals=text * slots * (width // head_width),
        ),
    )(scalars, queries, *parts, kv_flat, q_gain, k_gain)


def per_device(
    queries,
    latent_store,
    kv_up,
    q_gain,
    k_gain,
    out_weight,
    place_holder,
    place_block,
    image_count,
    serving_request,
):
    pool_size = lax.axis_size("pool")
    pool_index = lax.axis_index("pool")
    heads_size = lax.axis_size("heads")
    sub_size = lax.axis_size("sub")
    share_count = heads_size * sub_size
    share = lax.axis_index(("heads", "sub"))
    requests_here, text_rows, _ = queries.shape
    blocks_each = place_holder.shape[1]
    items = requests_here * blocks_each
    selector, chosen = fetch_latents(
        latent_store, place_holder, place_block, serving_request, items
    )
    rank_width = chosen.shape[2]
    chosen = chosen.reshape(requests_here, -1, rank_width)
    over_heads = [chosen] + [swap(chosen, "heads", flip) for flip in range(1, heads_size)]
    parts = []
    for part in over_heads:
        parts += [part] + [swap(part, "sub", flip) for flip in range(1, sub_size)]
    kv_flat = jnp.moveaxis(kv_up.reshape(rank_width, kv_up.shape[1], -1), 1, 0)
    gains = q_gain.reshape(1, -1), k_gain.reshape(1, -1)
    count_here = lax.dynamic_slice_in_dim(
        jnp.dot(selector, image_count), pool_index * requests_here, requests_here
    )

    def attended(request):
        scalars = jnp.stack([count_here[request], share])
        return attend(request, queries, parts, kv_flat, *gains, scalars)

    columns = out_weight.shape[1]
    part_rows = requests_here * text_rows // share_count
    if pool_size != 4 or requests_here != 2:
        block = jnp.concatenate([attended(request) for request in range(requests_here)])
        rows = lax.all_gather(block, "pool", axis=0)
        blocks = [rows[i] for i in range(pool_size)]
        mine = jnp.stack(sum_in_turn(project_out(blocks, out_weight), pool_size))
        back = lax.all_to_all(mine, "pool", split_axis=0, concat_axis=0, tiled=True)
        return jnp.moveaxis(back, 0, 1).reshape(part_rows, pool_size * columns)

    tie = lax.optimization_barrier
    first = attended(0)
    across0, beside0 = swap(first, "pool", 3), swap(first, "pool", 1)
    last = attended(1)
    first, last, across0, beside0 = tie((first, last, across0, beside0))
    across1, beside1 = swap(last, "pool", 3), swap(last, "pool", 1)
    partial0 = project_out([first, last, beside0, across0], out_weight)
    first, last, across0, across1, beside1, partial0 = tie(
        (first, last, across0, across1, beside1, partial0)
    )
    second0 = second_hop(first, across0)
    partial1 = project_out([beside1, across1], out_weight)
    second0, partial0, partial1, last, across1 = tie((second0, partial0, partial1, last, across1))
    second1 = second_hop(last, across1)
    half = partial1.shape[0] // 2
    own, partial0 = partial0[: 2 * half], partial0[2 * half :]
    partial = [partial0[:half], partial1[:half], partial0[half:], partial1[half:]]
    out_beside, out_across = sum_in_turn(jnp.concatenate(partial), 2)
    second0, second1, out_beside, out_across, own = tie(
        (second0, second1, out_beside, out_across, own)
    )
    back_beside, back_across = swap(out_beside, "pool", 1), swap(out_across, "pool", 3)
    (out_second,) = sum_in_turn(project_out([second0, second1], out_weight), 1)
    back_beside, back_across, out_second, own = tie((back_beside, back_across, out_second, own))
    back_second = swap(out_second, "pool", 2)
    (own,) = sum_in_turn(own, 1)
    output = jnp.zeros((part_rows, pool_size * columns), jnp.bfloat16)
    backs = [own, back_beside, back_second, back_across]
    for flip in (0, 1, 3, 2):
        output = lax.dynamic_update_slice(output, backs[flip], (0, (pool_index ^ flip) * columns))
    return output


def solution(mesh):
    in_specs = (
        P(("groups", "pool"), None, ("heads", "sub")),
        P(("groups", "pool"), None),
        P(None, ("heads", "sub"), None, None),
        P(),
        P(),
        P(("heads", "sub"), "pool"),
        P("groups", None),
        P("groups", None),
        P("groups"),
        P("groups"),
    )
    out_specs = P(("groups", "pool", "heads", "sub"), None)
    return jax.shard_map(
        per_device, mesh=mesh, in_specs=in_specs, out_specs=out_specs, check_vma=False
    )
```

time: 184 us -> 192 us (1.043)
  matrix products: 39.2 us -> 18.3 us
  waiting for transfers between devices: 94.7 us -> 107 us
  Pallas kernels: 0 us -> 9.93 us
  local copies, waits for them, and re-layouts: 12.6 us -> 19.3 us
    dot_general x5 -> x0, matrix products: 17.5 us -> none  [the longest x2 7.82 us: attend(): jnp.einsum('rgqts,rsgd->rtgqd', probs, values, preferred_element_type=jnp...]
    ppermute x23 -> x19, waiting for transfers between devices: 83.8 us -> 96 us  [swap(): lax.ppermute(values, axis, [(i, i ^ flip) for i in range(lax.axis_size(ax...]
    pallas_call x0 -> x2, Pallas kernels: none -> 9.93 us  [attend(): pl.pallas_call(functools.partial(attend_kernel, len(parts)), grid=(heads_...]
    ppermute x23 -> x19, starting transfers between devices: 30.4 us -> 25 us  [swap(): lax.ppermute(values, axis, [(i, i ^ flip) for i in range(lax.axis_size(ax...]
    ppermute x2, starting transfers between devices: 1.18 us -> 5.97 us  [second_hop(): return lax.ppermute(passed, 'pool', [(0, 2), (3, 1), (1, 0), (2, 3)])]
    reshape x2, local copies, waits for them, and re-layouts: 0.45 us -> 4.35 us  [per_device(): kv_flat = jnp.moveaxis(kv_up.reshape(rank_width, kv_up.shape[1], -1), 1, 0)]
    dot_general x3, matrix products: 19.7 us -> 16.4 us  [project_out(): partial = jnp.dot(rows, out_weight, preferred_element_type=jnp.float32)]
    slice x0 -> x3, local copies, waits for them, and re-layouts: none -> 2.18 us  [the longest x1 1.35 us: per_device(): own, partial0 = (partial0[:2 * half], partial0[2 * half:])]
  transfers between devices with their start and end apart: 25 -> 21, of which waited for: 15 -> 18; matrix products, arithmetic and copies ran while one was open for 17% -> 10% of each run, Pallas kernels for 0% -> 3%
where the time goes in v5:
time: 192 us; the launch traced here: 191 us
  waiting for transfers between devices  107 us (56%)
  starting transfers between devices  31 us (16%)
  local copies, waits for them, and re-layouts  19.3 us (10%)
  matrix products  18.3 us (10%)
  Pallas kernels  9.93 us (5%)
  other arithmetic  4.74 us (2%)
    ppermute x19, waiting for transfers between devices, swap(): lax.ppermute(values, axis, [(i, i ^ flip) for i in range(lax.axis_size(ax...  96 us
    ppermute x19, starting transfers between devices, swap(): lax.ppermute(values, axis, [(i, i ^ flip) for i in range(lax.axis_size(ax...  25 us
    dot_general x3, matrix products, project_out(): partial = jnp.dot(rows, out_weight, preferred_element_type=jnp.float32)  16.4 us
    ppermute x2, waiting for transfers between devices, second_hop(): return lax.ppermute(passed, 'pool', [(0, 2), (3, 1), (1, 0), (2, 3)])  11.4 us
    pallas_call x2, Pallas kernels, attend(): pl.pallas_call(functools.partial(attend_kernel, len(parts)), grid=(heads_...  9.93 us
    ppermute x2, starting transfers between devices, second_hop(): return lax.ppermute(passed, 'pool', [(0, 2), (3, 1), (1, 0), (2, 3)])  5.97 us
    unnamed x38, local copies, waits for them, and re-layouts  5.28 us
    reshape x2, local copies, waits for them, and re-layouts, per_device(): kv_flat = jnp.moveaxis(kv_up.reshape(rank_width, kv_up.shape[1], -1), 1, 0)  4.35 us
  transfers between devices with their start and end apart: 21, of which 18 were waited for; matrix products, arithmetic and copies ran while one was open for 10% of the time, Pallas kernels for 3%

profile of v5, /device:TPU:0, one launch (start us, length us, event | category | flops | bytes accessed | tf_op | source)
XLA Modules:
  0.0 191.1 jit_solution(14035816822586889303)
XLA Ops:
  3.7 2.8 %gather_fusion.1 = bf16[32,32,512]{2,1,0:T(8,128)(2,1)S(1)} fusion(bf16[128,32,512]{2,1,0:T(8,128)(2,1)} %bitcast.101, s32[1024]{0:T(1024)S(1)} %pad_clamp_fusion.1), kind=kCustom, calls=%fused_computation.1 | custom fusion | bytes 2097280 | tf_op jit(solution)/shard_map/gather | solution.py:78
  6.6 3.1 %collective-permute-start = (bf16[8,32,512]{2,1,0:T(8,128)(2,1)S(1)}, bf16[8,32,512]{2,1,0:T(8,128)(2,1)S(1)}, u32[]{:S(2)}, u32[]{:S(2)}) collective-permute-start(bf16[8,32,512]{2,1,0:T(8,128)(2,1)S(1)} %get-tuple-element.61), channel_id=1, source_target_pairs={{0,4},{4,0},{8,12},{12,8},{1,5},{5,1},{9,13},{13,9},{2,6},{6,2},{1... | collective-permute-start | bytes 786440 | tf_op jit(solution)/shard_map/ppermute | solution.py:26
  12.3 8.5 %collective-permute-done = bf16[8,32,512]{2,1,0:T(8,128)(2,1)S(1)} collective-permute-done((bf16[8,32,512]{2,1,0:T(8,128)(2,1)S(1)}, bf16[8,32,512]{2,1,0:T(8,128)(2,1)S(1)}, u32[]{:S(2)}, u32[]{:S(2)}) %collective-permute-start) | collective-permute-done | bytes 262176 | tf_op jit(solution)/shard_map/ppermute | solution.py:26
  20.8 10.2 %collective-permute-done.1 = bf16[8,32,512]{2,1,0:T(8,128)(2,1)S(1)} collective-permute-done((bf16[8,32,512]{2,1,0:T(8,128)(2,1)S(1)}, bf16[8,32,512]{2,1,0:T(8,128)(2,1)S(1)}, u32[]{:S(2)}, u32[]{:S(2)}) %collective-permute-start.1) | collective-permute-done | bytes 262176 | tf_op jit(solution)/shard_map/ppermute | solution.py:26
  33.4 9.7 %collective-permute-done.4.refs_2_ = bf16[2,256,512]{2,1,0:T(8,128)(2,1)S(1)} collective-permute-done((bf16[2,256,512]{2,1,0:T(8,128)(2,1)S(1)}, bf16[2,256,512]{2,1,0:T(8,128)(2,1)S(1)}, u32[]{:S(2)}, u32[]{:S(2)}) %collective-permute-start.4) | collective-permute-done | bytes 524320 | tf_op jit(solution)/shard_map/ppermute | solution.py:26
  43.1 3.2 %reshape.256 = bf16[512,2,256]{2,1,0:T(2,128)(2,1)} reshape(bf16[512,2,2,128]{3,2,1,0:T(2,128)(2,1)} %param.12) | data formatting | bytes 1048576 | tf_op jit(solution)/shard_map/reshape | solution.py:192
  51.0 4.9 %shard_map.100 = bf16[128,2048]{1,0:T(8,128)(2,1)S(1)} custom-call(s32[2]{0:T(128)S(1)} %pad_add_fusion.scalars, bf16[2,128,2048]{2,1,0:T(8,128)(2,1)S(1)} %copy-done.1, bf16[2,256,512]{2,1,0:T(8,128)(2,1)S(1)} %bitcast.89, bf16[2,256,512]{2,1,0:T(8,128)(2,1)S(1)} %copy-done.5, bf16[2,256,512]{2,1,0:T(8,128)(2,1)S(1)} %collective-permute-done.4.refs_2_, ...), custom_call_target="tpu_custom_call" | custom-call | flops 1610612736 | bytes 2097152 | tf_op jit(solution)/shard_map/pallas_call | solution.py:134
  57.3 6.3 %collective-permute-start.7 = (bf16[128,2048]{1,0:T(8,128)(2,1)S(1)}, bf16[128,2048]{1,0:T(8,128)(2,1)}, u32[]{:S(2)}, u32[]{:S(2)}) collective-permute-start(bf16[128,2048]{1,0:T(8,128)(2,1)S(1)} %shard_map.100), channel_id=1, source_target_pairs={{0,4},{4,0},{8,12},{12,8},{1,5},{5,1},{9,13},{13,9},{2,6},{6,2},{1... | collective-permute-start | bytes 1572872 | tf_op jit(solution)/shard_map/ppermute | solution.py:26
  66.4 5.0 %shard_map.101 = bf16[128,2048]{1,0:T(8,128)(2,1)S(1)} custom-call(s32[2]{0:T(128)S(1)} %pad_add_fusion.1.scalars, bf16[2,128,2048]{2,1,0:T(8,128)(2,1)S(1)} %copy-done.1, bf16[2,256,512]{2,1,0:T(8,128)(2,1)S(1)} %bitcast.90, bf16[2,256,512]{2,1,0:T(8,128)(2,1)S(1)} %copy-done.6, bf16[2,256,512]{2,1,0:T(8,128)(2,1)S(1)} %copy-done.3, ...), custom_call_target="tpu_custom_call" | custom-call | flops 1610612736 | bytes 2097152 | tf_op jit(solution)/shard_map/pallas_call | solution.py:134
  72.6 10.6 %collective-permute-done.7 = bf16[128,2048]{1,0:T(8,128)(2,1)} collective-permute-done((bf16[128,2048]{1,0:T(8,128)(2,1)S(1)}, bf16[128,2048]{1,0:T(8,128)(2,1)}, u32[]{:S(2)}, u32[]{:S(2)}) %collective-permute-start.7) | collective-permute-done | bytes 524320 | tf_op jit(solution)/shard_map/ppermute | solution.py:26
  84.6 8.2 %convolution_convert_fusion = bf16[512,2048]{1,0:T(8,128)(2,1)S(1)} fusion(bf16[2048,2048]{1,0:T(8,128)(2,1)} %param.15, bf16[128,2048]{1,0:T(8,128)(2,1)} %collective-permute-done.6, bf16[128,2048]{1,0:T(8,128)(2,1)} %collective-permute-done.7, bf16[128,2048]{1,0:T(8,128)(2,1)S(1)} %shard_map.101, bf16[128,2048]{1,0:T(8,128)(2,1)S(1)} %shard_map.100), kind=kOutput, calls=%fused_computation.3 | convolution fusion | flops 4304404480 | bytes 12582912 | tf_op jit(solution)/shard_map/dot_general | solution.py:47
  92.8 7.0 %collective-permute-done.8 = bf16[128,2048]{1,0:T(8,128)(2,1)S(1)} collective-permute-done((bf16[128,2048]{1,0:T(8,128)(2,1)S(1)}, bf16[128,2048]{1,0:T(8,128)(2,1)S(1)}, u32[]{:S(2)}, u32[]{:S(2)}) %collective-permute-start.8) | collective-permute-done | bytes 524320 | tf_op jit(solution)/shard_map/ppermute | solution.py:26
  99.9 9.5 %collective-permute-done.9 = bf16[128,2048]{1,0:T(8,128)(2,1)S(1)} collective-permute-done((bf16[128,2048]{1,0:T(8,128)(2,1)S(1)}, bf16[128,2048]{1,0:T(8,128)(2,1)S(1)}, u32[]{:S(2)}, u32[]{:S(2)}) %collective-permute-start.9) | collective-permute-done | bytes 524320 | tf_op jit(solution)/shard_map/ppermute | solution.py:26
  109.5 2.6 %collective-permute-start.10 = (bf16[128,2048]{1,0:T(8,128)(2,1)S(1)}, bf16[128,2048]{1,0:T(8,128)(2,1)S(1)}, u32[]{:S(2)}, u32[]{:S(2)}) collective-permute-start(bf16[128,2048]{1,0:T(8,128)(2,1)S(1)} %broadcast_select_fusion.1), channel_id=1, source_target_pairs={{0,8},{12,4},{4,0},{8,12},{1,9},{13,5},{5,1},{9,13},{2,10},{14,6},... | collective-permute-start | bytes 1572872 | tf_op jit(solution)/shard_map/ppermute | solution.py:33
  114.5 8.2 %collective-permute-done.10 = bf16[128,2048]{1,0:T(8,128)(2,1)S(1)} collective-permute-done((bf16[128,2048]{1,0:T(8,128)(2,1)S(1)}, bf16[128,2048]{1,0:T(8,128)(2,1)S(1)}, u32[]{:S(2)}, u32[]{:S(2)}) %collective-permute-start.10) | collective-permute-done | bytes 524320 | tf_op jit(solution)/shard_map/ppermute | solution.py:33
  125.1 2.8 %collective-permute-done.12 = bf16[2,2,64,2048]{3,2,0,1:T(8,128)(2,1)} collective-permute-done((bf16[2,2,64,2048]{3,2,0,1:T(8,128)(2,1)S(1)}, bf16[2,2,64,2048]{3,2,0,1:T(8,128)(2,1)}, u32[]{:S(2)}, u32[]{:S(2)}) %collective-permute-start.12) | collective-permute-done | bytes 1048608 | tf_op jit(solution)/shard_map/ppermute | solution.py:26
  133.6 3.3 %collective-permute-start.11 = (bf16[128,2048]{1,0:T(8,128)(2,1)S(1)}, bf16[128,2048]{1,0:T(8,128)(2,1)S(1)}, u32[]{:S(2)}, u32[]{:S(2)}) collective-permute-start(bf16[128,2048]{1,0:T(8,128)(2,1)S(1)} %broadcast_select_fusion), channel_id=1, source_target_pairs={{0,8},{12,4},{4,0},{8,12},{1,9},{13,5},{5,1},{9,13},{2,10},{14,6},... | collective-permute-start | bytes 1572872 | tf_op jit(solution)/shard_map/ppermute | solution.py:33
  137.0 7.9 %collective-permute-done.13 = bf16[2,64,2048]{2,1,0:T(8,128)(2,1)S(1)} collective-permute-done((bf16[2,64,2048]{2,1,0:T(8,128)(2,1)}, bf16[2,64,2048]{2,1,0:T(8,128)(2,1)S(1)}, u32[]{:S(2)}, u32[]{:S(2)}) %collective-permute-start.13) | collective-permute-done | bytes 524320 | tf_op jit(solution)/shard_map/ppermute | solution.py:26
  145.0 3.1 %collective-permute-done.11 = bf16[128,2048]{1,0:T(8,128)(2,1)S(1)} collective-permute-done((bf16[128,2048]{1,0:T(8,128)(2,1)S(1)}, bf16[128,2048]{1,0:T(8,128)(2,1)S(1)}, u32[]{:S(2)}, u32[]{:S(2)}) %collective-permute-start.11) | collective-permute-done | bytes 524320 | tf_op jit(solution)/shard_map/ppermute | solution.py:33
  148.2 5.7 %convolution_convert_fusion.1 = bf16[256,2048]{1,0:T(8,128)(2,1)S(1)} fusion(bf16[2048,2048]{1,0:T(8,128)(2,1)} %param.15, bf16[128,2048]{1,0:T(8,128)(2,1)S(1)} %collective-permute-done.11, bf16[128,2048]{1,0:T(8,128)(2,1)S(1)} %copy-done.14), kind=kOutput, calls=%fused_computation.4 | convolution fusion | flops 2150105088 | bytes 10485760 | tf_op jit(solution)/shard_map/dot_general | solution.py:47
  161.6 2.9 %collective-permute-done.17 = bf16[1,64,2048]{2,1,0:T(8,128)(2,1)S(1)} collective-permute-done((bf16[1,64,2048]{2,1,0:T(8,128)(2,1)S(1)}, bf16[1,64,2048]{2,1,0:T(8,128)(2,1)S(1)}, u32[]{:S(2)}, u32[]{:S(2)}) %collective-permute-start.17) | collective-permute-done | bytes 262176 | tf_op jit(solution)/shard_map/ppermute | solution.py:26
  165.8 7.4 %collective-permute-done.15 = bf16[64,2048]{1,0:T(8,128)(2,1)S(1)} collective-permute-done((bf16[64,2048]{1,0:T(8,128)(2,1)S(1)}, bf16[64,2048]{1,0:T(8,128)(2,1)S(1)}, u32[]{:S(2)}, u32[]{:S(2)}) %collective-permute-start.15) | collective-permute-done | bytes 262176 | tf_op jit(solution)/shard_map/ppermute | solution.py:26
  177.0 6.9 %collective-permute-done.19 = bf16[1,64,2048]{2,1,0:T(8,128)(2,1)S(1)} collective-permute-done((bf16[1,64,2048]{2,1,0:T(8,128)(2,1)S(1)}, bf16[1,64,2048]{2,1,0:T(8,128)(2,1)S(1)}, u32[]{:S(2)}, u32[]{:S(2)}) %collective-permute-start.19) | collective-permute-done | bytes 262176 | tf_op jit(solution)/shard_map/ppermute | solution.py:26
  184.1 6.3 %collective-permute-done.20 = bf16[64,2048]{1,0:T(8,128)(2,1)S(1)} collective-permute-done((bf16[64,2048]{1,0:T(8,128)(2,1)S(1)}, bf16[64,2048]{1,0:T(8,128)(2,1)S(1)}, u32[]{:S(2)}, u32[]{:S(2)}) %collective-permute-start.20) | collective-permute-done | bytes 262176 | tf_op jit(solution)/shard_map/ppermute | solution.py:26
  (113 shorter events, 44.2 us)
Async XLA Ops:
  6.6 14.2 %collective-permute-start = (bf16[8,32,512]{2,1,0:T(8,128)(2,1)S(1)}, bf16[8,32,512]{2,1,0:T(8,128)(2,1)S(1)}, u32[]{:S(2)}, u32[]{:S(2)}) collective-permute-start(bf16[8,32,512]{2,1,0:T(8,128)(2,1)S(1)} %get-tuple-element.61), channel_id=1, source_target_pairs={{0,4},{4,0},{8,12},{12,8},{1,5},{5,1},{9,13},{13,9},{2,6},{6,2},{1... | collective-permute-start | bytes 786440 | tf_op jit(solution)/shard_map/ppermute | solution.py:26
  9.7 21.4 %collective-permute-start.1 = (bf16[8,32,512]{2,1,0:T(8,128)(2,1)S(1)}, bf16[8,32,512]{2,1,0:T(8,128)(2,1)S(1)}, u32[]{:S(2)}, u32[]{:S(2)}) collective-permute-start(bf16[8,32,512]{2,1,0:T(8,128)(2,1)S(1)} %get-tuple-element.60), channel_id=1, source_target_pairs={{0,8},{4,12},{8,0},{12,4},{1,9},{5,13},{9,1},{13,5},{2,10},{6,14},... | collective-permute-start | bytes 786440 | tf_op jit(solution)/shard_map/ppermute | solution.py:26
  12.2 18.8 %collective-permute-start.2 = (bf16[8,32,512]{2,1,0:T(8,128)(2,1)S(1)}, bf16[8,32,512]{2,1,0:T(8,128)(2,1)S(1)}, u32[]{:S(2)}, u32[]{:S(2)}) collective-permute-start(bf16[8,32,512]{2,1,0:T(8,128)(2,1)S(1)} %get-tuple-element.62), channel_id=1, source_target_pairs={{0,12},{4,8},{8,4},{12,0},{1,13},{5,9},{9,5},{13,1},{2,14},{6,10},... | collective-permute-start | bytes 786440 | tf_op jit(solution)/shard_map/ppermute | solution.py:26
  31.8 11.3 %collective-permute-start.4 = (bf16[2,256,512]{2,1,0:T(8,128)(2,1)S(1)}, bf16[2,256,512]{2,1,0:T(8,128)(2,1)S(1)}, u32[]{:S(2)}, u32[]{:S(2)}) collective-permute-start(bf16[2,256,512]{2,1,0:T(8,128)(2,1)S(1)} %bitcast.87), channel_id=1, source_target_pairs={{0,2},{2,0},{1,3},{3,1},{4,6},{6,4},{5,7},{7,5},{8,10},{10,8},{9,1... | collective-permute-start | bytes 1572872 | tf_op jit(solution)/shard_map/ppermute | solution.py:26
  33.4 15.7 %collective-permute-start.3 = (bf16[2,256,512]{2,1,0:T(8,128)(2,1)S(1)}, bf16[2,256,512]{2,1,0:T(8,128)(2,1)S(1)}, u32[]{:S(2)}, u32[]{:S(2)}) collective-permute-start(bf16[2,256,512]{2,1,0:T(8,128)(2,1)S(1)} %bitcast.88), channel_id=1, source_target_pairs={{0,1},{1,0},{2,3},{3,2},{4,5},{5,4},{6,7},{7,6},{8,9},{9,8},{10,11... | collective-permute-start | bytes 1572872 | tf_op jit(solution)/shard_map/ppermute | solution.py:26
  43.1 6.8 %collective-permute-start.5 = (bf16[2,256,512]{2,1,0:T(8,128)(2,1)S(1)}, bf16[2,256,512]{2,1,0:T(8,128)(2,1)}, u32[]{:S(2)}, u32[]{:S(2)}) collective-permute-start(bf16[2,256,512]{2,1,0:T(8,128)(2,1)S(1)} %collective-permute-done.4.refs_2_), channel_id=1, source_target_pairs={{0,1},{1,0},{2,3},{3,2},{4,5},{5,4},{6,7},{7,6},{8,9},{9,8},{10,11... | collective-permute-start | bytes 1572872 | tf_op jit(solution)/shard_map/ppermute | solution.py:26
  55.9 16.8 %collective-permute-start.6 = (bf16[128,2048]{1,0:T(8,128)(2,1)S(1)}, bf16[128,2048]{1,0:T(8,128)(2,1)}, u32[]{:S(2)}, u32[]{:S(2)}) collective-permute-start(bf16[128,2048]{1,0:T(8,128)(2,1)S(1)} %shard_map.100), channel_id=1, source_target_pairs={{0,12},{4,8},{8,4},{12,0},{1,13},{5,9},{9,5},{13,1},{2,14},{6,10},... | collective-permute-start | bytes 1572872 | tf_op jit(solution)/shard_map/ppermute | solution.py:26
  57.3 25.9 %collective-permute-start.7 = (bf16[128,2048]{1,0:T(8,128)(2,1)S(1)}, bf16[128,2048]{1,0:T(8,128)(2,1)}, u32[]{:S(2)}, u32[]{:S(2)}) collective-permute-start(bf16[128,2048]{1,0:T(8,128)(2,1)S(1)} %shard_map.100), channel_id=1, source_target_pairs={{0,4},{4,0},{8,12},{12,8},{1,5},{5,1},{9,13},{13,9},{2,6},{6,2},{1... | collective-permute-start | bytes 1572872 | tf_op jit(solution)/shard_map/ppermute | solution.py:26
  66.4 45.7 %slice-start = ((s8[8388608]{0:T(1024)(128)(4,1)}), s8[4194304]{0:T(1024)(128)(4,1)S(1)}, s32[]{:S(2)}) async-start(s8[8388608]{0:T(1024)(128)(4,1)} %bitcast.102), calls=%async_computation | async-start | bytes 8388608
  71.5 40.6 %slice-start.1 = ((s8[8388608]{0:T(1024)(128)(4,1)}), s8[4194304]{0:T(1024)(128)(4,1)S(1)}, s32[]{:S(2)}) async-start(s8[8388608]{0:T(1024)(128)(4,1)} %bitcast.102), calls=%async_computation.1 | async-start | bytes 8388608
  83.2 16.6 %collective-permute-start.8 = (bf16[128,2048]{1,0:T(8,128)(2,1)S(1)}, bf16[128,2048]{1,0:T(8,128)(2,1)S(1)}, u32[]{:S(2)}, u32[]{:S(2)}) collective-permute-start(bf16[128,2048]{1,0:T(8,128)(2,1)S(1)} %shard_map.101), channel_id=1, source_target_pairs={{0,12},{4,8},{8,4},{12,0},{1,13},{5,9},{9,5},{13,1},{2,14},{6,10},... | collective-permute-start | bytes 1572872 | tf_op jit(solution)/shard_map/ppermute | solution.py:26
  84.6 24.8 %collective-permute-start.9 = (bf16[128,2048]{1,0:T(8,128)(2,1)S(1)}, bf16[128,2048]{1,0:T(8,128)(2,1)S(1)}, u32[]{:S(2)}, u32[]{:S(2)}) collective-permute-start(bf16[128,2048]{1,0:T(8,128)(2,1)S(1)} %shard_map.101), channel_id=1, source_target_pairs={{0,4},{4,0},{8,12},{12,8},{1,5},{5,1},{9,13},{13,9},{2,6},{6,2},{1... | collective-permute-start | bytes 1572872 | tf_op jit(solution)/shard_map/ppermute | solution.py:26
  92.8 29.9 %copy-start.9 = (bf16[512,2048]{1,0:T(8,128)(2,1)}, bf16[512,2048]{1,0:T(8,128)(2,1)S(1)}, u32[]{:S(2)}) copy-start(bf16[512,2048]{1,0:T(8,128)(2,1)S(1)} %convolution_convert_fusion) | copy-start | bytes 6291460
  109.5 13.3 %collective-permute-start.10 = (bf16[128,2048]{1,0:T(8,128)(2,1)S(1)}, bf16[128,2048]{1,0:T(8,128)(2,1)S(1)}, u32[]{:S(2)}, u32[]{:S(2)}) collective-permute-start(bf16[128,2048]{1,0:T(8,128)(2,1)S(1)} %broadcast_select_fusion.1), channel_id=1, source_target_pairs={{0,8},{12,4},{4,0},{8,12},{1,9},{13,5},{5,1},{9,13},{2,10},{14,6},... | collective-permute-start | bytes 1572872 | tf_op jit(solution)/shard_map/ppermute | solution.py:33
  125.1 2.9 %collective-permute-start.12 = (bf16[2,2,64,2048]{3,2,0,1:T(8,128)(2,1)S(1)}, bf16[2,2,64,2048]{3,2,0,1:T(8,128)(2,1)}, u32[]{:S(2)}, u32[]{:S(2)}) collective-permute-start(bf16[2,2,64,2048]{3,2,0,1:T(8,128)(2,1)S(1)} %bitcast.100), channel_id=1, source_target_pairs={{0,1},{1,0},{2,3},{3,2},{4,5},{5,4},{6,7},{7,6},{8,9},{9,8},{10,11... | collective-permute-start | bytes 3145736 | tf_op jit(solution)/shard_map/ppermute | solution.py:26
  130.7 14.2 %collective-permute-start.13 = (bf16[2,64,2048]{2,1,0:T(8,128)(2,1)}, bf16[2,64,2048]{2,1,0:T(8,128)(2,1)S(1)}, u32[]{:S(2)}, u32[]{:S(2)}) collective-permute-start(bf16[2,64,2048]{2,1,0:T(8,128)(2,1)} %fusion.14), channel_id=1, source_target_pairs={{0,2},{2,0},{1,3},{3,1},{4,6},{6,4},{5,7},{7,5},{8,10},{10,8},{9,1... | collective-permute-start | bytes 1572872 | tf_op jit(solution)/shard_map/ppermute | solution.py:26
  133.6 14.5 %collective-permute-start.11 = (bf16[128,2048]{1,0:T(8,128)(2,1)S(1)}, bf16[128,2048]{1,0:T(8,128)(2,1)S(1)}, u32[]{:S(2)}, u32[]{:S(2)}) collective-permute-start(bf16[128,2048]{1,0:T(8,128)(2,1)S(1)} %broadcast_select_fusion), channel_id=1, source_target_pairs={{0,8},{12,4},{4,0},{8,12},{1,9},{13,5},{5,1},{9,13},{2,10},{14,6},... | collective-permute-start | bytes 1572872 | tf_op jit(solution)/shard_map/ppermute | solution.py:33
  154.0 2.0 %collective-permute-start.16 = (bf16[1,2,64,2048]{3,2,1,0:T(8,128)(2,1)S(1)}, bf16[1,2,64,2048]{3,2,1,0:T(8,128)(2,1)S(1)}, u32[]{:S(2)}, u32[]{:S(2)}) collective-permute-start(bf16[1,2,64,2048]{3,2,1,0:T(8,128)(2,1)S(1)} %dynamic-slice_bitcast_fusion.1), channel_id=1, source_target_pairs={{0,1},{1,0},{2,3},{3,2},{4,5},{5,4},{6,7},{7,6},{8,9},{9,8},{10,11... | collective-permute-start | bytes 1572872 | tf_op jit(solution)/shard_map/ppermute | solution.py:26
  156.1 8.4 %collective-permute-start.17 = (bf16[1,64,2048]{2,1,0:T(8,128)(2,1)S(1)}, bf16[1,64,2048]{2,1,0:T(8,128)(2,1)S(1)}, u32[]{:S(2)}, u32[]{:S(2)}) collective-permute-start(bf16[1,64,2048]{2,1,0:T(8,128)(2,1)S(1)} %fusion.17), channel_id=1, source_target_pairs={{0,2},{2,0},{1,3},{3,1},{4,6},{6,4},{5,7},{7,5},{8,10},{10,8},{9,1... | collective-permute-start | bytes 786440 | tf_op jit(solution)/shard_map/ppermute | solution.py:26
  156.7 9.1 %collective-permute-start.14 = (bf16[64,2048]{1,0:T(8,128)(2,1)S(1)}, bf16[64,2048]{1,0:T(8,128)(2,1)S(1)}, u32[]{:S(2)}, u32[]{:S(2)}) collective-permute-start(bf16[64,2048]{1,0:T(8,128)(2,1)S(1)} %get-tuple-element.44), channel_id=1, source_target_pairs={{0,4},{4,0},{8,12},{12,8},{1,5},{5,1},{9,13},{13,9},{2,6},{6,2},{1... | collective-permute-start | bytes 786440 | tf_op jit(solution)/shard_map/ppermute | solution.py:26
  159.1 14.1 %collective-permute-start.15 = (bf16[64,2048]{1,0:T(8,128)(2,1)S(1)}, bf16[64,2048]{1,0:T(8,128)(2,1)S(1)}, u32[]{:S(2)}, u32[]{:S(2)}) collective-permute-start(bf16[64,2048]{1,0:T(8,128)(2,1)S(1)} %get-tuple-element.45), channel_id=1, source_target_pairs={{0,12},{4,8},{8,4},{12,0},{1,13},{5,9},{9,5},{13,1},{2,14},{6,10},... | collective-permute-start | bytes 786440 | tf_op jit(solution)/shard_map/ppermute | solution.py:26
  173.3 2.0 %collective-permute-start.18 = (bf16[1,2,64,2048]{3,2,1,0:T(8,128)(2,1)S(1)}, bf16[1,2,64,2048]{3,2,1,0:T(8,128)(2,1)S(1)}, u32[]{:S(2)}, u32[]{:S(2)}) collective-permute-start(bf16[1,2,64,2048]{3,2,1,0:T(8,128)(2,1)S(1)} %dynamic-slice_bitcast_fusion), channel_id=1, source_target_pairs={{0,1},{1,0},{2,3},{3,2},{4,5},{5,4},{6,7},{7,6},{8,9},{9,8},{10,11... | collective-permute-start | bytes 1572872 | tf_op jit(solution)/shard_map/ppermute | solution.py:26
  175.4 8.4 %collective-permute-start.19 = (bf16[1,64,2048]{2,1,0:T(8,128)(2,1)S(1)}, bf16[1,64,2048]{2,1,0:T(8,128)(2,1)S(1)}, u32[]{:S(2)}, u32[]{:S(2)}) collective-permute-start(bf16[1,64,2048]{2,1,0:T(8,128)(2,1)S(1)} %fusion.18), channel_id=1, source_target_pairs={{0,2},{2,0},{1,3},{3,1},{4,6},{6,4},{5,7},{7,5},{8,10},{10,8},{9,1... | collective-permute-start | bytes 786440 | tf_op jit(solution)/shard_map/ppermute | solution.py:26
  177.0 13.4 %collective-permute-start.20 = (bf16[64,2048]{1,0:T(8,128)(2,1)S(1)}, bf16[64,2048]{1,0:T(8,128)(2,1)S(1)}, u32[]{:S(2)}, u32[]{:S(2)}) collective-permute-start(bf16[64,2048]{1,0:T(8,128)(2,1)S(1)} %fusion.19), channel_id=1, source_target_pairs={{0,8},{4,12},{8,0},{12,4},{1,9},{5,13},{9,1},{13,5},{2,10},{6,14},... | collective-permute-start | bytes 786440 | tf_op jit(solution)/shard_map/ppermute | solution.py:26
  (16 other events, 143.8 us)

commit v6 on v5

v6 whole, which is shorter than its diff:
```python
import functools
import math

import jax
import jax.numpy as jnp
from jax import lax
from jax.experimental import pallas as pl
from jax.experimental.pallas import tpu as pltpu
from jax.sharding import PartitionSpec as P

BLK = 128
CHUNKS = 2


def rms_scale(values, gain):
    return values * lax.rsqrt(jnp.mean(values * values, axis=-1, keepdims=True) + 1e-05) * gain


def pair_rank(holders):
    count = holders.shape[1]
    same = holders[:, :, None] == holders[:, None, :]
    earlier = jnp.arange(count)[None, :] < jnp.arange(count)[:, None]
    return jnp.sum((same & earlier[None]).astype(jnp.int32), axis=2)


def swap(values, axis, flip):
    return lax.ppermute(values, axis, [(i, i ^ flip) for i in range(lax.axis_size(axis))])


def second_hop(block, across):
    index = lax.axis_index("pool")
    at_end = (index == 0) | (index == 3)
    passed = jnp.where(at_end, block, across)
    return lax.ppermute(passed, "pool", [(0, 2), (3, 1), (1, 0), (2, 3)])


def exchange_sum(pieces, axis):
    index = lax.axis_index(axis)
    total = lax.dynamic_index_in_dim(pieces, index, 0, keepdims=False).astype(jnp.float32)
    for flip in range(1, lax.axis_size(axis)):
        away = lax.dynamic_index_in_dim(pieces, index ^ flip, 0, keepdims=False)
        total = total + swap(away.astype(jnp.bfloat16), axis, flip).astype(jnp.float32)
    return total


def project_out(blocks, out_weight):
    rows = jnp.concatenate(blocks, axis=0)
    partial = jnp.dot(rows, out_weight, preferred_element_type=jnp.float32)
    return partial.astype(jnp.bfloat16)


def sum_shares(partial, count):
    axes = ("heads", "sub")
    pieces = partial.reshape(count, lax.axis_size(axes), -1, partial.shape[1])
    total = exchange_sum(jnp.moveaxis(pieces, 1, 0), axes).astype(jnp.bfloat16)
    return [total[i] for i in range(count)]


def find_blocks(place_holder, place_block, serving_request, items):
    pool_size = lax.axis_size("pool")
    pool_index = lax.axis_index("pool")
    capacity = 2 * ((items + pool_size - 1) // pool_size)
    total_requests = serving_request.shape[0]
    request_ids = jnp.arange(total_requests, dtype=jnp.int32)
    selector = (serving_request[:, None] == request_ids[None, :]).astype(jnp.int32)
    holders = jnp.dot(selector, place_holder).reshape(pool_size, items)
    blocks = jnp.dot(selector, place_block).reshape(pool_size, items)
    ranks = pair_rank(holders)
    slot_ids = jnp.arange(capacity, dtype=jnp.int32)
    matched = (holders[:, None, :] == pool_index) & (ranks[:, None, :] == slot_ids[None, :, None])
    send_block = jnp.sum(jnp.where(matched, blocks[:, None, :], 0), axis=2)
    partners = jnp.arange(pool_size, dtype=jnp.int32) ^ pool_index
    wanted = send_block.at[partners].get(mode="promise_in_bounds")
    my_holders = lax.dynamic_index_in_dim(holders, pool_index, 0, keepdims=False)
    my_ranks = lax.dynamic_index_in_dim(ranks, pool_index, 0, keepdims=False)
    return selector, wanted, (my_holders ^ pool_index) * capacity + my_ranks


def fetch_pieces(latent_store, wanted):
    share_count = lax.axis_size(("heads", "sub"))
    share = lax.axis_index(("heads", "sub"))
    rows = BLK // share_count
    store = latent_store.reshape(-1, rows, latent_store.shape[1])
    outgoing = store.at[wanted.reshape(-1) * share_count + share].get(mode="promise_in_bounds")
    outgoing = outgoing.reshape(*wanted.shape, rows, -1)
    arriving = {flip: swap(outgoing[flip], "pool", flip) for flip in (*range(2, len(wanted)), 1)}
    return [outgoing[0]] + [arriving[flip] for flip in range(1, len(wanted))]


def attend_kernel(share_count, scalars, queries, *refs):
    parts, (kv_up, q_gain, k_gain, out, keys, values) = refs[:share_count], refs[share_count:]
    request = pl.program_id(0)
    head_width = q_gain.shape[1]
    text, width = out.shape
    per_group = width // head_width
    part_slots = parts[0].shape[1]
    share_rows = BLK // share_count
    count, share = scalars[1 + request], scalars[0]
    for flip in range(share_count):
        rows = pl.ds(flip * part_slots, part_slots)
        projected = jnp.dot(parts[flip][request], kv_up[...], preferred_element_type=jnp.float32)
        key = rms_scale(projected[:, :head_width], k_gain[...])
        keys[rows, :] = key.astype(jnp.bfloat16)
        slot = lax.broadcasted_iota(jnp.int32, (part_slots, head_width), 0)
        position = (slot // share_rows) * BLK + (share ^ flip) * share_rows + slot % share_rows
        live = jnp.where(position < count, 1.0, 0.0)
        values[rows, :head_width] = (projected[:, head_width:] * live).astype(jnp.bfloat16)
        values[rows, head_width:] = live.astype(jnp.bfloat16)
    scale = math.log2(math.e) / math.sqrt(head_width)
    together = min(per_group, max(1, 256 // text))
    for first in range(0, per_group, together):
        normed = []
        for head in range(first, first + together):
            query = queries[0, :, 0, :, head * head_width : (head + 1) * head_width]
            query = query.reshape(text, head_width).astype(jnp.float32)
            normed.append(rms_scale(query, q_gain[...]).astype(jnp.bfloat16))
        scores = lax.dot_general(
            jnp.concatenate(normed, axis=0),
            keys[...],
            (((1,), (1,)), ((), ())),
            preferred_element_type=jnp.float32,
        )
        expo = jnp.exp2(scores * scale).astype(jnp.bfloat16)
        total = jnp.dot(expo, values[...], preferred_element_type=jnp.float32)
        result = (total[:, :head_width] / total[:, head_width:]).astype(jnp.bfloat16)
        for i in range(together):
            head = first + i
            columns = slice(head * head_width, (head + 1) * head_width)
            out[:, columns] = result[i * text : (i + 1) * text]


def attend(chunk, queries, parts, kv_flat, q_gain, k_gain, scalars):
    requests, request_shares, _, part_rows, width = queries.shape
    heads_here, rank_width, pair_width = kv_flat.shape
    head_width = q_gain.shape[1]
    slots = len(parts) * parts[0].shape[1]
    text = request_shares * part_rows
    whole = pl.BlockSpec(memory_space=pltpu.VMEM)
    return pl.pallas_call(
        functools.partial(attend_kernel, len(parts)),
        grid=(requests, heads_here),
        in_specs=[
            pl.BlockSpec(memory_space=pltpu.SMEM),
            pl.BlockSpec(
                (1, request_shares, 1, part_rows, width // heads_here),
                lambda r, g: (r, 0, chunk, 0, g),
            ),
        ]
        + [whole for _ in parts]
        + [pl.BlockSpec((None, rank_width, pair_width), lambda r, g: (g, 0, 0)), whole, whole],
        out_specs=pl.BlockSpec((text, width // heads_here), lambda r, g: (r, g)),
        out_shape=jax.ShapeDtypeStruct((requests * text, width), jnp.bfloat16),
        scratch_shapes=[
            pltpu.VMEM((slots, head_width), jnp.bfloat16),
            pltpu.VMEM((slots, 2 * head_width), jnp.bfloat16),
        ],
        compiler_params=pltpu.CompilerParams(vmem_limit_bytes=32 * 1024 * 1024),
        cost_estimate=pl.CostEstimate(
            flops=requests
            * slots
            * (4 * text * width + 2 * rank_width * heads_here * pair_width),
            bytes_accessed=requests * (4 * text * width + 2 * slots * rank_width),
            transcendentals=requests * text * slots * (width // head_width),
        ),
    )(scalars, queries, *parts, kv_flat, q_gain, k_gain)


def per_device(
    queries,
    latent_store,
    kv_up,
    q_gain,
    k_gain,
    out_weight,
    place_holder,
    place_block,
    image_count,
    serving_request,
):
    pool_size = lax.axis_size("pool")
    pool_index = lax.axis_index("pool")
    heads_size = lax.axis_size("heads")
    sub_size = lax.axis_size("sub")
    share_count = heads_size * sub_size
    share = lax.axis_index(("heads", "sub"))
    requests_here, text_rows, _ = queries.shape
    blocks_each = place_holder.shape[1]
    items = requests_here * blocks_each
    rank_width = latent_store.shape[1]
    tie = lax.optimization_barrier
    selector, wanted, where = find_blocks(place_holder, place_block, serving_request, items)
    kv_flat = jnp.moveaxis(kv_up.reshape(rank_width, kv_up.shape[1], -1), 1, 0)
    gains = q_gain.reshape(1, -1), k_gain.reshape(1, -1)
    count_here = lax.dynamic_slice_in_dim(
        jnp.dot(selector, image_count), pool_index * requests_here, requests_here
    )
    scalars = jnp.concatenate([share.reshape(1), count_here])
    pieces = fetch_pieces(latent_store, wanted)
    pieces, kv_flat, scalars = tie((pieces, kv_flat, scalars))
    chosen = jnp.concatenate(pieces, axis=0).at[where].get(mode="promise_in_bounds")
    chosen = chosen.reshape(requests_here, -1, rank_width)
    over_heads = [chosen] + [swap(chosen, "heads", flip) for flip in range(1, heads_size)]
    parts = []
    for part in over_heads:
        parts += [part] + [swap(part, "sub", flip) for flip in range(1, sub_size)]
    part_rows = requests_here * text_rows // share_count
    shaped = queries.reshape(
        requests_here, share_count // requests_here, CHUNKS, part_rows // CHUNKS, -1
    )

    def attended(chunk):
        return attend(chunk, shaped, parts, kv_flat, *gains, scalars)

    columns = out_weight.shape[1]
    if pool_size != 4:
        outputs = []
        for chunk in range(CHUNKS):
            rows = lax.all_gather(attended(chunk), "pool", axis=0)
            blocks = [rows[i] for i in range(pool_size)]
            mine = jnp.stack(sum_shares(project_out(blocks, out_weight), pool_size))
            back = lax.all_to_all(mine, "pool", split_axis=0, concat_axis=0, tiled=True)
            outputs.append(jnp.moveaxis(back, 0, 1).reshape(-1, pool_size * columns))
        return jnp.concatenate(outputs, axis=0)

    first = attended(0)
    across0, beside0 = swap(first, "pool", 3), swap(first, "pool", 1)
    last = attended(1)
    first, last, across0, beside0 = tie((first, last, across0, beside0))
    across1, beside1 = swap(last, "pool", 3), swap(last, "pool", 1)
    partial = project_out([first, last, beside0, across0], out_weight)
    first, last, across0, across1, beside1, partial = tie(
        (first, last, across0, across1, beside1, partial)
    )
    half = partial.shape[0] // 2
    own, partial = partial[:half], partial[half:]
    second0 = second_hop(first, across0)
    out_beside0, out_across0 = sum_shares(partial, 2)
    partial = project_out([beside1, across1], out_weight)
    second0, out_beside0, out_across0, partial, own, last, across1 = tie(
        (second0, out_beside0, out_across0, partial, own, last, across1)
    )
    second1 = second_hop(last, across1)
    out_beside1, out_across1 = sum_shares(partial, 2)
    partial = project_out([second0], out_weight)
    second1, out_beside1, out_across1, partial, out_beside0, out_across0, own = tie(
        (second1, out_beside1, out_across1, partial, out_beside0, out_across0, own)
    )
    back_across = swap(jnp.concatenate([out_across0, out_across1]), "pool", 3)
    back_beside = swap(jnp.concatenate([out_beside0, out_beside1]), "pool", 1)
    partial = jnp.concatenate([partial, project_out([second1], out_weight)])
    out_second = jnp.concatenate(sum_shares(partial, 2))
    back_across, back_beside, out_second, own = tie((back_across, back_beside, out_second, own))
    back_second = swap(out_second, "pool", 2)
    own = jnp.concatenate(sum_shares(own, 2))
    output = jnp.zeros((part_rows, pool_size * columns), jnp.bfloat16)
    backs = [own, back_beside, back_second, back_across]
    for flip in (0, 1, 3, 2):
        output = lax.dynamic_update_slice(output, backs[flip], (0, (pool_index ^ flip) * columns))
    return output


def solution(mesh):
    in_specs = (
        P(("groups", "pool"), None, ("heads", "sub")),
        P(("groups", "pool"), None),
        P(None, ("heads", "sub"), None, None),
        P(),
        P(),
        P(("heads", "sub"), "pool"),
        P("groups", None),
        P("groups", None),
        P("groups"),
        P("groups"),
    )
    out_specs = P(("groups", "pool", "heads", "sub"), None)
    return jax.shard_map(
        per_device, mesh=mesh, in_specs=in_specs, out_specs=out_specs, check_vma=False
    )
```

time: 192 us -> 180 us (0.938)
  local copies, waits for them, and re-layouts: 19.3 us -> 10.8 us
  waiting for transfers between devices: 107 us -> 102 us
  starting transfers between devices: 31 us -> 35.4 us
  matrix products: 18.3 us -> 15.1 us
  Pallas kernels: 9.93 us -> 12.4 us
    ppermute x2, waiting for transfers between devices: 11.4 us -> 5.18 us  [second_hop(): return lax.ppermute(passed, 'pool', [(0, 2), (3, 1), (1, 0), (2, 3)])]
    ppermute x19 -> x25, starting transfers between devices: 25 us -> 29.4 us  [swap(): lax.ppermute(values, axis, [(i, i ^ flip) for i in range(lax.axis_size(ax...]
    reshape x2, local copies, waits for them, and re-layouts: 4.35 us -> 0.41 us  [per_device(): kv_flat = jnp.moveaxis(kv_up.reshape(rank_width, kv_up.shape[1], -1), 1, 0)]
    dot_general x3 -> x4, matrix products: 16.4 us -> 13.2 us  [project_out(): partial = jnp.dot(rows, out_weight, preferred_element_type=jnp.float32)]
    unnamed x38 -> x28, local copies, waits for them, and re-layouts: 5.28 us -> 2.79 us
    pallas_call x2, Pallas kernels: 9.93 us -> 12.4 us  [attend(): pl.pallas_call(functools.partial(attend_kernel, len(parts)), grid=(reques...]
    add x4 -> x1, other arithmetic: 2.16 us -> 0.01 us  [fetch_pieces(): wanted.reshape(-1) * share_count + share]
    ppermute x19 -> x25, waiting for transfers between devices: 96 us -> 96.8 us  [swap(): lax.ppermute(values, axis, [(i, i ^ flip) for i in range(lax.axis_size(ax...]
  transfers between devices with their start and end apart: 21 -> 27, of which waited for: 18 -> 20; matrix products, arithmetic and copies ran while one was open for 10% -> 8% of each run, Pallas kernels for 3% -> 3%
where the time goes in v6:
time: 180 us; the launch traced here: 179 us
  waiting for transfers between devices  102 us (57%)
  starting transfers between devices  35.4 us (20%)
  matrix products  15.1 us (8%)
  Pallas kernels  12.4 us (7%)
  local copies, waits for them, and re-layouts  10.8 us (6%)
  other arithmetic  3.38 us (2%)
    ppermute x25, waiting for transfers between devices, swap(): lax.ppermute(values, axis, [(i, i ^ flip) for i in range(lax.axis_size(ax...  96.8 us
    ppermute x25, starting transfers between devices, swap(): lax.ppermute(values, axis, [(i, i ^ flip) for i in range(lax.axis_size(ax...  29.4 us
    dot_general x4, matrix products, project_out(): partial = jnp.dot(rows, out_weight, preferred_element_type=jnp.float32)  13.2 us
    pallas_call x2, Pallas kernels, attend(): pl.pallas_call(functools.partial(attend_kernel, len(parts)), grid=(reques...  12.4 us
    ppermute x2, starting transfers between devices, second_hop(): return lax.ppermute(passed, 'pool', [(0, 2), (3, 1), (1, 0), (2, 3)])  5.96 us
    ppermute x2, waiting for transfers between devices, second_hop(): return lax.ppermute(passed, 'pool', [(0, 2), (3, 1), (1, 0), (2, 3)])  5.18 us
  transfers between devices with their start and end apart: 27, of which 20 were waited for; matrix products, arithmetic and copies ran while one was open for 8% of the time, Pallas kernels for 3%

profile of v6, /device:TPU:0, one launch (start us, length us, event | category | flops | bytes accessed | tf_op | source)
XLA Modules:
  0.0 179.5 jit_solution(363701978343634168)
XLA Ops:
  3.6 2.8 %gather_fusion.1 = bf16[32,32,512]{2,1,0:T(8,128)(2,1)S(1)} fusion(bf16[128,32,512]{2,1,0:T(8,128)(2,1)} %bitcast.116, s32[1024]{0:T(1024)S(1)} %pad_clamp_fusion.1), kind=kCustom, calls=%fused_computation.1 | custom fusion | bytes 2097280 | tf_op jit(solution)/shard_map/gather | solution.py:84
  7.3 3.0 %collective-permute-start = (bf16[8,32,512]{2,1,0:T(8,128)(2,1)}, bf16[8,32,512]{2,1,0:T(8,128)(2,1)S(1)}, u32[]{:S(2)}, u32[]{:S(2)}) collective-permute-start(bf16[8,32,512]{2,1,0:T(8,128)(2,1)} %get-tuple-element.89), channel_id=1, source_target_pairs={{0,4},{4,0},{8,12},{12,8},{1,5},{5,1},{9,13},{13,9},{2,6},{6,2},{1... | collective-permute-start | bytes 786440 | tf_op jit(solution)/shard_map/ppermute | solution.py:27
  10.3 2.6 %collective-permute-start.1 = (bf16[8,32,512]{2,1,0:T(8,128)(2,1)S(1)}, bf16[8,32,512]{2,1,0:T(8,128)(2,1)S(1)}, u32[]{:S(2)}, u32[]{:S(2)}) collective-permute-start(bf16[8,32,512]{2,1,0:T(8,128)(2,1)S(1)} %get-tuple-element.88), channel_id=1, source_target_pairs={{0,8},{4,12},{8,0},{12,4},{1,9},{5,13},{9,1},{13,5},{2,10},{6,14},... | collective-permute-start | bytes 786440 | tf_op jit(solution)/shard_map/ppermute | solution.py:27
  13.7 8.1 %collective-permute-done = bf16[8,32,512]{2,1,0:T(8,128)(2,1)S(1)} collective-permute-done((bf16[8,32,512]{2,1,0:T(8,128)(2,1)}, bf16[8,32,512]{2,1,0:T(8,128)(2,1)S(1)}, u32[]{:S(2)}, u32[]{:S(2)}) %collective-permute-start) | collective-permute-done | bytes 262176 | tf_op jit(solution)/shard_map/ppermute | solution.py:27
  21.8 9.9 %collective-permute-done.1 = bf16[8,32,512]{2,1,0:T(8,128)(2,1)S(1)} collective-permute-done((bf16[8,32,512]{2,1,0:T(8,128)(2,1)S(1)}, bf16[8,32,512]{2,1,0:T(8,128)(2,1)S(1)}, u32[]{:S(2)}, u32[]{:S(2)}) %collective-permute-start.1) | collective-permute-done | bytes 262176 | tf_op jit(solution)/shard_map/ppermute | solution.py:27
  37.1 10.0 %collective-permute-done.4.refs_2_ = bf16[2,256,512]{2,1,0:T(8,128)(2,1)S(1)} collective-permute-done((bf16[2,256,512]{2,1,0:T(8,128)(2,1)S(1)}, bf16[2,256,512]{2,1,0:T(8,128)(2,1)S(1)}, u32[]{:S(2)}, u32[]{:S(2)}) %collective-permute-start.4) | collective-permute-done | bytes 524320 | tf_op jit(solution)/shard_map/ppermute | solution.py:27
  49.1 6.2 %shard_map.100 = bf16[128,2048]{1,0:T(8,128)(2,1)S(1)} custom-call(s32[3]{0:T(128)S(1)} %pad_add_fusion.scalars, bf16[2,2,2,32,2048]{4,3,2,1,0:T(8,128)(2,1)S(1)} %bitcast.100, bf16[2,256,512]{2,1,0:T(8,128)(2,1)S(1)} %bitcast.98, bf16[2,256,512]{2,1,0:T(8,128)(2,1)S(1)} %collective-permute-done.3.refs_1_, ...), custom_call_target="tpu_custom_call" | custom-call | flops 2147483648 | bytes 3145728 | tf_op jit(solution)/shard_map/pallas_call | solution.py:139
  56.7 6.1 %collective-permute-start.7 = (bf16[128,2048]{1,0:T(8,128)(2,1)S(1)}, bf16[128,2048]{1,0:T(8,128)(2,1)}, u32[]{:S(2)}, u32[]{:S(2)}) collective-permute-start(bf16[128,2048]{1,0:T(8,128)(2,1)S(1)} %shard_map.100), channel_id=1, source_target_pairs={{0,4},{4,0},{8,12},{12,8},{1,5},{5,1},{9,13},{13,9},{2,6},{6,2},{1... | collective-permute-start | bytes 1572872 | tf_op jit(solution)/shard_map/ppermute | solution.py:27
  64.9 6.2 %shard_map.101 = bf16[128,2048]{1,0:T(8,128)(2,1)S(1)} custom-call(s32[3]{0:T(128)S(1)} %pad_add_fusion.scalars, bf16[2,2,2,32,2048]{4,3,2,1,0:T(8,128)(2,1)S(1)} %bitcast.101, bf16[2,256,512]{2,1,0:T(8,128)(2,1)S(1)} %bitcast.99, bf16[2,256,512]{2,1,0:T(8,128)(2,1)S(1)} %copy-done.3, bf16[2,256,512]{2,1,0:T(8,128)(2,1)S(1)} %collective-permute-done.4.refs_2_, ...), custom_call_target="tpu_custom_call" | custom-call | flops 2147483648 | bytes 3145728 | tf_op jit(solution)/shard_map/pallas_call | solution.py:139
  72.0 10.4 %collective-permute-done.7 = bf16[128,2048]{1,0:T(8,128)(2,1)} collective-permute-done((bf16[128,2048]{1,0:T(8,128)(2,1)S(1)}, bf16[128,2048]{1,0:T(8,128)(2,1)}, u32[]{:S(2)}, u32[]{:S(2)}) %collective-permute-start.7) | collective-permute-done | bytes 524320 | tf_op jit(solution)/shard_map/ppermute | solution.py:27
  83.8 8.2 %convolution_convert_fusion = bf16[512,2048]{1,0:T(8,128)(2,1)S(1)} fusion(bf16[2048,2048]{1,0:T(8,128)(2,1)} %param.15, bf16[128,2048]{1,0:T(8,128)(2,1)} %collective-permute-done.6, bf16[128,2048]{1,0:T(8,128)(2,1)} %collective-permute-done.7, bf16[128,2048]{1,0:T(8,128)(2,1)S(1)} %shard_map.101, bf16[128,2048]{1,0:T(8,128)(2,1)S(1)} %shard_map.100), kind=kOutput, calls=%fused_computation.3 | convolution fusion | flops 4304404480 | bytes 12582912 | tf_op jit(solution)/shard_map/dot_general | solution.py:48
  92.0 7.1 %collective-permute-done.8 = bf16[128,2048]{1,0:T(8,128)(2,1)S(1)} collective-permute-done((bf16[128,2048]{1,0:T(8,128)(2,1)S(1)}, bf16[128,2048]{1,0:T(8,128)(2,1)S(1)}, u32[]{:S(2)}, u32[]{:S(2)}) %collective-permute-start.8) | collective-permute-done | bytes 524320 | tf_op jit(solution)/shard_map/ppermute | solution.py:27
  99.1 9.5 %collective-permute-done.9 = bf16[128,2048]{1,0:T(8,128)(2,1)S(1)} collective-permute-done((bf16[128,2048]{1,0:T(8,128)(2,1)S(1)}, bf16[128,2048]{1,0:T(8,128)(2,1)S(1)}, u32[]{:S(2)}, u32[]{:S(2)}) %collective-permute-start.9) | collective-permute-done | bytes 524320 | tf_op jit(solution)/shard_map/ppermute | solution.py:27
  110.8 2.4 %collective-permute-start.10 = (bf16[128,2048]{1,0:T(8,128)(2,1)S(1)}, bf16[128,2048]{1,0:T(8,128)(2,1)S(1)}, u32[]{:S(2)}, u32[]{:S(2)}) collective-permute-start(bf16[128,2048]{1,0:T(8,128)(2,1)S(1)} %broadcast_select_fusion.1), channel_id=1, source_target_pairs={{0,8},{12,4},{4,0},{8,12},{1,9},{13,5},{5,1},{9,13},{2,10},{14,6},... | collective-permute-start | bytes 1572872 | tf_op jit(solution)/shard_map/ppermute | solution.py:34
  118.1 4.7 %collective-permute-done.13 = bf16[2,32,2048]{2,1,0:T(8,128)(2,1)S(1)} collective-permute-done((bf16[2,32,2048]{2,1,0:T(8,128)(2,1)S(1)}, bf16[2,32,2048]{2,1,0:T(8,128)(2,1)S(1)}, u32[]{:S(2)}, u32[]{:S(2)}) %collective-permute-start.13) | collective-permute-done | bytes 262176 | tf_op jit(solution)/shard_map/ppermute | solution.py:27
  127.1 3.5 %collective-permute-start.14 = (bf16[128,2048]{1,0:T(8,128)(2,1)S(1)}, bf16[128,2048]{1,0:T(8,128)(2,1)S(1)}, u32[]{:S(2)}, u32[]{:S(2)}) collective-permute-start(bf16[128,2048]{1,0:T(8,128)(2,1)S(1)} %broadcast_select_fusion), channel_id=1, source_target_pairs={{0,8},{12,4},{4,0},{8,12},{1,9},{13,5},{5,1},{9,13},{2,10},{14,6},... | collective-permute-start | bytes 1572872 | tf_op jit(solution)/shard_map/ppermute | solution.py:34
  134.4 4.7 %collective-permute-done.17 = bf16[2,32,2048]{2,1,0:T(8,128)(2,1)S(1)} collective-permute-done((bf16[2,32,2048]{2,1,0:T(8,128)(2,1)S(1)}, bf16[2,32,2048]{2,1,0:T(8,128)(2,1)S(1)}, u32[]{:S(2)}, u32[]{:S(2)}) %collective-permute-start.17) | collective-permute-done | bytes 262176 | tf_op jit(solution)/shard_map/ppermute | solution.py:27
  139.3 3.1 %collective-permute-done.14 = bf16[128,2048]{1,0:T(8,128)(2,1)S(1)} collective-permute-done((bf16[128,2048]{1,0:T(8,128)(2,1)S(1)}, bf16[128,2048]{1,0:T(8,128)(2,1)S(1)}, u32[]{:S(2)}, u32[]{:S(2)}) %collective-permute-start.14) | collective-permute-done | bytes 524320 | tf_op jit(solution)/shard_map/ppermute | solution.py:34
  145.8 2.5 %collective-permute-start.19 = (bf16[64,2048]{1,0:T(8,128)(2,1)S(1)}, bf16[64,2048]{1,0:T(8,128)(2,1)S(1)}, u32[]{:S(2)}, u32[]{:S(2)}) collective-permute-start(bf16[64,2048]{1,0:T(8,128)(2,1)S(1)} %pad_maximum_fusion.3), channel_id=1, source_target_pairs={{0,4},{4,0},{8,12},{12,8},{1,5},{5,1},{9,13},{13,9},{2,6},{6,2},{1... | collective-permute-start | bytes 786440 | tf_op jit(solution)/shard_map/ppermute | solution.py:27
  148.3 2.5 %collective-permute-start.18 = (bf16[64,2048]{1,0:T(8,128)(2,1)S(1)}, bf16[64,2048]{1,0:T(8,128)(2,1)S(1)}, u32[]{:S(2)}, u32[]{:S(2)}) collective-permute-start(bf16[64,2048]{1,0:T(8,128)(2,1)S(1)} %pad_maximum_fusion.2), channel_id=1, source_target_pairs={{0,12},{4,8},{8,4},{12,0},{1,13},{5,9},{9,5},{13,1},{2,14},{6,10},... | collective-permute-start | bytes 786440 | tf_op jit(solution)/shard_map/ppermute | solution.py:27
  153.1 4.7 %collective-permute-done.22 = bf16[2,32,2048]{2,1,0:T(8,128)(2,1)S(1)} collective-permute-done((bf16[2,32,2048]{2,1,0:T(8,128)(2,1)S(1)}, bf16[2,32,2048]{2,1,0:T(8,128)(2,1)S(1)}, u32[]{:S(2)}, u32[]{:S(2)}) %collective-permute-start.22) | collective-permute-done | bytes 262176 | tf_op jit(solution)/shard_map/ppermute | solution.py:27
  158.0 4.8 %collective-permute-done.18 = bf16[64,2048]{1,0:T(8,128)(2,1)S(1)} collective-permute-done((bf16[64,2048]{1,0:T(8,128)(2,1)S(1)}, bf16[64,2048]{1,0:T(8,128)(2,1)S(1)}, u32[]{:S(2)}, u32[]{:S(2)}) %collective-permute-start.18) | collective-permute-done | bytes 262176 | tf_op jit(solution)/shard_map/ppermute | solution.py:27
  165.5 6.6 %collective-permute-done.24 = bf16[2,32,2048]{2,1,0:T(8,128)(2,1)S(1)} collective-permute-done((bf16[2,32,2048]{2,1,0:T(8,128)(2,1)S(1)}, bf16[2,32,2048]{2,1,0:T(8,128)(2,1)S(1)}, u32[]{:S(2)}, u32[]{:S(2)}) %collective-permute-start.24) | collective-permute-done | bytes 262176 | tf_op jit(solution)/shard_map/ppermute | solution.py:27
  172.2 4.7 %collective-permute-done.25 = bf16[2,32,2048]{2,1,0:T(8,128)(2,1)S(1)} collective-permute-done((bf16[2,32,2048]{2,1,0:T(8,128)(2,1)S(1)}, bf16[2,32,2048]{2,1,0:T(8,128)(2,1)S(1)}, u32[]{:S(2)}, u32[]{:S(2)}) %collective-permute-start.25) | collective-permute-done | bytes 262176 | tf_op jit(solution)/shard_map/ppermute | solution.py:27
  (115 shorter events, 44.7 us)
Async XLA Ops:
  7.3 14.5 %collective-permute-start = (bf16[8,32,512]{2,1,0:T(8,128)(2,1)}, bf16[8,32,512]{2,1,0:T(8,128)(2,1)S(1)}, u32[]{:S(2)}, u32[]{:S(2)}) collective-permute-start(bf16[8,32,512]{2,1,0:T(8,128)(2,1)} %get-tuple-element.89), channel_id=1, source_target_pairs={{0,4},{4,0},{8,12},{12,8},{1,5},{5,1},{9,13},{13,9},{2,6},{6,2},{1... | collective-permute-start | bytes 786440 | tf_op jit(solution)/shard_map/ppermute | solution.py:27
  10.3 21.4 %collective-permute-start.1 = (bf16[8,32,512]{2,1,0:T(8,128)(2,1)S(1)}, bf16[8,32,512]{2,1,0:T(8,128)(2,1)S(1)}, u32[]{:S(2)}, u32[]{:S(2)}) collective-permute-start(bf16[8,32,512]{2,1,0:T(8,128)(2,1)S(1)} %get-tuple-element.88), channel_id=1, source_target_pairs={{0,8},{4,12},{8,0},{12,4},{1,9},{5,13},{9,1},{13,5},{2,10},{6,14},... | collective-permute-start | bytes 786440 | tf_op jit(solution)/shard_map/ppermute | solution.py:27
  12.9 18.8 %collective-permute-start.2 = (bf16[8,32,512]{2,1,0:T(8,128)(2,1)S(1)}, bf16[8,32,512]{2,1,0:T(8,128)(2,1)}, u32[]{:S(2)}, u32[]{:S(2)}) collective-permute-start(bf16[8,32,512]{2,1,0:T(8,128)(2,1)S(1)} %get-tuple-element.87), channel_id=1, source_target_pairs={{0,12},{4,8},{8,4},{12,0},{1,13},{5,9},{9,5},{13,1},{2,14},{6,10},... | collective-permute-start | bytes 786440 | tf_op jit(solution)/shard_map/ppermute | solution.py:27
  35.6 11.6 %collective-permute-start.4 = (bf16[2,256,512]{2,1,0:T(8,128)(2,1)S(1)}, bf16[2,256,512]{2,1,0:T(8,128)(2,1)S(1)}, u32[]{:S(2)}, u32[]{:S(2)}) collective-permute-start(bf16[2,256,512]{2,1,0:T(8,128)(2,1)S(1)} %bitcast.96), channel_id=1, source_target_pairs={{0,2},{2,0},{1,3},{3,1},{4,6},{6,4},{5,7},{7,5},{8,10},{10,8},{9,1... | collective-permute-start | bytes 1572872 | tf_op jit(solution)/shard_map/ppermute | solution.py:27
  37.1 10.0 %collective-permute-start.3 = (bf16[2,256,512]{2,1,0:T(8,128)(2,1)S(1)}, bf16[2,256,512]{2,1,0:T(8,128)(2,1)S(1)}, u32[]{:S(2)}, u32[]{:S(2)}) collective-permute-start(bf16[2,256,512]{2,1,0:T(8,128)(2,1)S(1)} %bitcast.97), channel_id=1, source_target_pairs={{0,1},{1,0},{2,3},{3,2},{4,5},{5,4},{6,7},{7,6},{8,9},{9,8},{10,11... | collective-permute-start | bytes 1572872 | tf_op jit(solution)/shard_map/ppermute | solution.py:27
  55.3 16.8 %collective-permute-start.6 = (bf16[128,2048]{1,0:T(8,128)(2,1)S(1)}, bf16[128,2048]{1,0:T(8,128)(2,1)}, u32[]{:S(2)}, u32[]{:S(2)}) collective-permute-start(bf16[128,2048]{1,0:T(8,128)(2,1)S(1)} %shard_map.100), channel_id=1, source_target_pairs={{0,12},{4,8},{8,4},{12,0},{1,13},{5,9},{9,5},{13,1},{2,14},{6,10},... | collective-permute-start | bytes 1572872 | tf_op jit(solution)/shard_map/ppermute | solution.py:27
  56.7 25.8 %collective-permute-start.7 = (bf16[128,2048]{1,0:T(8,128)(2,1)S(1)}, bf16[128,2048]{1,0:T(8,128)(2,1)}, u32[]{:S(2)}, u32[]{:S(2)}) collective-permute-start(bf16[128,2048]{1,0:T(8,128)(2,1)S(1)} %shard_map.100), channel_id=1, source_target_pairs={{0,4},{4,0},{8,12},{12,8},{1,5},{5,1},{9,13},{13,9},{2,6},{6,2},{1... | collective-permute-start | bytes 1572872 | tf_op jit(solution)/shard_map/ppermute | solution.py:27
  82.4 16.6 %collective-permute-start.8 = (bf16[128,2048]{1,0:T(8,128)(2,1)S(1)}, bf16[128,2048]{1,0:T(8,128)(2,1)S(1)}, u32[]{:S(2)}, u32[]{:S(2)}) collective-permute-start(bf16[128,2048]{1,0:T(8,128)(2,1)S(1)} %shard_map.101), channel_id=1, source_target_pairs={{0,12},{4,8},{8,4},{12,0},{1,13},{5,9},{9,5},{13,1},{2,14},{6,10},... | collective-permute-start | bytes 1572872 | tf_op jit(solution)/shard_map/ppermute | solution.py:27
  83.8 24.8 %collective-permute-start.9 = (bf16[128,2048]{1,0:T(8,128)(2,1)S(1)}, bf16[128,2048]{1,0:T(8,128)(2,1)S(1)}, u32[]{:S(2)}, u32[]{:S(2)}) collective-permute-start(bf16[128,2048]{1,0:T(8,128)(2,1)S(1)} %shard_map.101), channel_id=1, source_target_pairs={{0,4},{4,0},{8,12},{12,8},{1,5},{5,1},{9,13},{13,9},{2,6},{6,2},{1... | collective-permute-start | bytes 1572872 | tf_op jit(solution)/shard_map/ppermute | solution.py:27
  108.8 6.9 %collective-permute-start.11 = (bf16[2,32,2048]{2,1,0:T(8,128)(2,1)S(1)}, bf16[2,32,2048]{2,1,0:T(8,128)(2,1)S(1)}, u32[]{:S(2)}, u32[]{:S(2)}) collective-permute-start(bf16[2,32,2048]{2,1,0:T(8,128)(2,1)S(1)} %get-tuple-element.84), channel_id=1, source_target_pairs={{0,1},{1,0},{2,3},{3,2},{4,5},{5,4},{6,7},{7,6},{8,9},{9,8},{10,11... | collective-permute-start | bytes 786440 | tf_op jit(solution)/shard_map/ppermute | solution.py:27
  108.9 9.2 %collective-permute-start.12 = (bf16[2,32,2048]{2,1,0:T(8,128)(2,1)S(1)}, bf16[2,32,2048]{2,1,0:T(8,128)(2,1)S(1)}, u32[]{:S(2)}, u32[]{:S(2)}) collective-permute-start(bf16[2,32,2048]{2,1,0:T(8,128)(2,1)S(1)} %get-tuple-element.86), channel_id=1, source_target_pairs={{0,2},{1,3},{2,0},{3,1},{4,6},{5,7},{6,4},{7,5},{8,10},{9,11},{10,... | collective-permute-start | bytes 786440 | tf_op jit(solution)/shard_map/ppermute | solution.py:27
  110.5 12.3 %collective-permute-start.13 = (bf16[2,32,2048]{2,1,0:T(8,128)(2,1)S(1)}, bf16[2,32,2048]{2,1,0:T(8,128)(2,1)S(1)}, u32[]{:S(2)}, u32[]{:S(2)}) collective-permute-start(bf16[2,32,2048]{2,1,0:T(8,128)(2,1)S(1)} %get-tuple-element.85), channel_id=1, source_target_pairs={{0,3},{1,2},{2,1},{3,0},{4,7},{5,6},{6,5},{7,4},{8,11},{9,10},{10,... | collective-permute-start | bytes 786440 | tf_op jit(solution)/shard_map/ppermute | solution.py:27
  110.8 14.2 %collective-permute-start.10 = (bf16[128,2048]{1,0:T(8,128)(2,1)S(1)}, bf16[128,2048]{1,0:T(8,128)(2,1)S(1)}, u32[]{:S(2)}, u32[]{:S(2)}) collective-permute-start(bf16[128,2048]{1,0:T(8,128)(2,1)S(1)} %broadcast_select_fusion.1), channel_id=1, source_target_pairs={{0,8},{12,4},{4,0},{8,12},{1,9},{13,5},{5,1},{9,13},{2,10},{14,6},... | collective-permute-start | bytes 1572872 | tf_op jit(solution)/shard_map/ppermute | solution.py:34
  125.2 9.2 %collective-permute-start.16 = (bf16[2,32,2048]{2,1,0:T(8,128)(2,1)S(1)}, bf16[2,32,2048]{2,1,0:T(8,128)(2,1)S(1)}, u32[]{:S(2)}, u32[]{:S(2)}) collective-permute-start(bf16[2,32,2048]{2,1,0:T(8,128)(2,1)S(1)} %get-tuple-element.83), channel_id=1, source_target_pairs={{0,2},{1,3},{2,0},{3,1},{4,6},{5,7},{6,4},{7,5},{8,10},{9,11},{10,... | collective-permute-start | bytes 786440 | tf_op jit(solution)/shard_map/ppermute | solution.py:27
  126.8 12.3 %collective-permute-start.17 = (bf16[2,32,2048]{2,1,0:T(8,128)(2,1)S(1)}, bf16[2,32,2048]{2,1,0:T(8,128)(2,1)S(1)}, u32[]{:S(2)}, u32[]{:S(2)}) collective-permute-start(bf16[2,32,2048]{2,1,0:T(8,128)(2,1)S(1)} %get-tuple-element.82), channel_id=1, source_target_pairs={{0,3},{1,2},{2,1},{3,0},{4,7},{5,6},{6,5},{7,4},{8,11},{9,10},{10,... | collective-permute-start | bytes 786440 | tf_op jit(solution)/shard_map/ppermute | solution.py:27
  127.1 15.2 %collective-permute-start.14 = (bf16[128,2048]{1,0:T(8,128)(2,1)S(1)}, bf16[128,2048]{1,0:T(8,128)(2,1)S(1)}, u32[]{:S(2)}, u32[]{:S(2)}) collective-permute-start(bf16[128,2048]{1,0:T(8,128)(2,1)S(1)} %broadcast_select_fusion), channel_id=1, source_target_pairs={{0,8},{12,4},{4,0},{8,12},{1,9},{13,5},{5,1},{9,13},{2,10},{14,6},... | collective-permute-start | bytes 1572872 | tf_op jit(solution)/shard_map/ppermute | solution.py:34
  143.8 7.0 %collective-permute-start.20 = (bf16[2,32,2048]{2,1,0:T(8,128)(2,1)S(1)}, bf16[2,32,2048]{2,1,0:T(8,128)(2,1)S(1)}, u32[]{:S(2)}, u32[]{:S(2)}) collective-permute-start(bf16[2,32,2048]{2,1,0:T(8,128)(2,1)S(1)} %get-tuple-element.78), channel_id=1, source_target_pairs={{0,1},{1,0},{2,3},{3,2},{4,5},{5,4},{6,7},{7,6},{8,9},{9,8},{10,11... | collective-permute-start | bytes 786440 | tf_op jit(solution)/shard_map/ppermute | solution.py:27
  143.9 9.2 %collective-permute-start.21 = (bf16[2,32,2048]{2,1,0:T(8,128)(2,1)S(1)}, bf16[2,32,2048]{2,1,0:T(8,128)(2,1)S(1)}, u32[]{:S(2)}, u32[]{:S(2)}) collective-permute-start(bf16[2,32,2048]{2,1,0:T(8,128)(2,1)S(1)} %get-tuple-element.80), channel_id=1, source_target_pairs={{0,2},{1,3},{2,0},{3,1},{4,6},{5,7},{6,4},{7,5},{8,10},{9,11},{10,... | collective-permute-start | bytes 786440 | tf_op jit(solution)/shard_map/ppermute | solution.py:27
  145.4 12.3 %collective-permute-start.22 = (bf16[2,32,2048]{2,1,0:T(8,128)(2,1)S(1)}, bf16[2,32,2048]{2,1,0:T(8,128)(2,1)S(1)}, u32[]{:S(2)}, u32[]{:S(2)}) collective-permute-start(bf16[2,32,2048]{2,1,0:T(8,128)(2,1)S(1)} %get-tuple-element.79), channel_id=1, source_target_pairs={{0,3},{1,2},{2,1},{3,0},{4,7},{5,6},{6,5},{7,4},{8,11},{9,10},{10,... | collective-permute-start | bytes 786440 | tf_op jit(solution)/shard_map/ppermute | solution.py:27
  145.8 12.2 %collective-permute-start.19 = (bf16[64,2048]{1,0:T(8,128)(2,1)S(1)}, bf16[64,2048]{1,0:T(8,128)(2,1)S(1)}, u32[]{:S(2)}, u32[]{:S(2)}) collective-permute-start(bf16[64,2048]{1,0:T(8,128)(2,1)S(1)} %pad_maximum_fusion.3), channel_id=1, source_target_pairs={{0,4},{4,0},{8,12},{12,8},{1,5},{5,1},{9,13},{13,9},{2,6},{6,2},{1... | collective-permute-start | bytes 786440 | tf_op jit(solution)/shard_map/ppermute | solution.py:27
  148.3 14.6 %collective-permute-start.18 = (bf16[64,2048]{1,0:T(8,128)(2,1)S(1)}, bf16[64,2048]{1,0:T(8,128)(2,1)S(1)}, u32[]{:S(2)}, u32[]{:S(2)}) collective-permute-start(bf16[64,2048]{1,0:T(8,128)(2,1)S(1)} %pad_maximum_fusion.2), channel_id=1, source_target_pairs={{0,12},{4,8},{8,4},{12,0},{1,13},{5,9},{9,5},{13,1},{2,14},{6,10},... | collective-permute-start | bytes 786440 | tf_op jit(solution)/shard_map/ppermute | solution.py:27
  163.0 9.2 %collective-permute-start.24 = (bf16[2,32,2048]{2,1,0:T(8,128)(2,1)S(1)}, bf16[2,32,2048]{2,1,0:T(8,128)(2,1)S(1)}, u32[]{:S(2)}, u32[]{:S(2)}) collective-permute-start(bf16[2,32,2048]{2,1,0:T(8,128)(2,1)S(1)} %get-tuple-element.77), channel_id=1, source_target_pairs={{0,2},{1,3},{2,0},{3,1},{4,6},{5,7},{6,4},{7,5},{8,10},{9,11},{10,... | collective-permute-start | bytes 786440 | tf_op jit(solution)/shard_map/ppermute | solution.py:27
  164.5 12.3 %collective-permute-start.25 = (bf16[2,32,2048]{2,1,0:T(8,128)(2,1)S(1)}, bf16[2,32,2048]{2,1,0:T(8,128)(2,1)S(1)}, u32[]{:S(2)}, u32[]{:S(2)}) collective-permute-start(bf16[2,32,2048]{2,1,0:T(8,128)(2,1)S(1)} %get-tuple-element.76), channel_id=1, source_target_pairs={{0,3},{1,2},{2,1},{3,0},{4,7},{5,6},{6,5},{7,4},{8,11},{9,10},{10,... | collective-permute-start | bytes 786440 | tf_op jit(solution)/shard_map/ppermute | solution.py:27
  164.8 13.9 %collective-permute-start.26 = (bf16[64,2048]{1,0:T(8,128)(2,1)S(1)}, bf16[64,2048]{1,0:T(8,128)(2,1)S(1)}, u32[]{:S(2)}, u32[]{:S(2)}) collective-permute-start(bf16[64,2048]{1,0:T(8,128)(2,1)S(1)} %pad_maximum_fusion.4), channel_id=1, source_target_pairs={{0,8},{4,12},{8,0},{12,4},{1,9},{5,13},{9,1},{13,5},{2,10},{6,14},... | collective-permute-start | bytes 786440 | tf_op jit(solution)/shard_map/ppermute | solution.py:27
  (17 other events, 288.7 us)

commit v7 on v6

--- a/solution.py
+++ b/solution.py
@@ -10,6 +10,7 @@
 
 BLK = 128
 CHUNKS = 2
+LIGHT = pl.CostEstimate(flops=1, bytes_accessed=1, transcendentals=0)
 
 
 def rms_scale(values, gain):
@@ -34,26 +35,50 @@
     return lax.ppermute(passed, "pool", [(0, 2), (3, 1), (1, 0), (2, 3)])
 
 
-def exchange_sum(pieces, axis):
-    index = lax.axis_index(axis)
-    total = lax.dynamic_index_in_dim(pieces, index, 0, keepdims=False).astype(jnp.float32)
-    for flip in range(1, lax.axis_size(axis)):
-        away = lax.dynamic_index_in_dim(pieces, index ^ flip, 0, keepdims=False)
-        total = total + swap(away.astype(jnp.bfloat16), axis, flip).astype(jnp.float32)
-    return total
+def project_kernel(block_count, share_count, share, *refs):
+    blocks, weight, outs = refs[:block_count], refs[block_count], refs[block_count + 1 :]
+    part_rows = blocks[0].shape[0] // share_count
+    picked = []
+    for flip in range(share_count):
+        start = pl.multiple_of((share[0] ^ flip) * part_rows, part_rows)
+        picked += [block[pl.ds(start, part_rows), :] for block in blocks]
+    product = jnp.dot(
+        jnp.concatenate(picked, axis=0), weight[...], preferred_element_type=jnp.float32
+    )
+    rows = block_count * part_rows
+    for flip in range(share_count):
+        outs[flip][...] = product[flip * rows : (flip + 1) * rows].astype(outs[flip].dtype)
 
 
 def project_out(blocks, out_weight):
-    rows = jnp.concatenate(blocks, axis=0)
-    partial = jnp.dot(rows, out_weight, preferred_element_type=jnp.float32)
-    return partial.astype(jnp.bfloat16)
-
-
-def sum_shares(partial, count):
     axes = ("heads", "sub")
-    pieces = partial.reshape(count, lax.axis_size(axes), -1, partial.shape[1])
-    total = exchange_sum(jnp.moveaxis(pieces, 1, 0), axes).astype(jnp.bfloat16)
-    return [total[i] for i in range(count)]
+    share_count = lax.axis_size(axes)
+    share = lax.axis_index(axes).astype(jnp.int32).reshape(1)
+    depth, columns = out_weight.shape
+    rows = sum(block.shape[0] for block in blocks) // share_count
+    tile = min(columns, 512)
+    whole = pl.BlockSpec(memory_space=pltpu.VMEM)
+    return pl.pallas_call(
+        functools.partial(project_kernel, len(blocks), share_count),
+        grid=(columns // tile,),
+        in_specs=[pl.BlockSpec(memory_space=pltpu.SMEM)]
+        + [whole for _ in blocks]
+        + [pl.BlockSpec((depth, tile), lambda n: (0, n))],
+        out_specs=[pl.BlockSpec((rows, tile), lambda n: (0, n))] * share_count,
+        out_shape=[
+            jax.ShapeDtypeStruct((rows, columns), jnp.bfloat16 if flip else jnp.float32)
+            for flip in range(share_count)
+        ],
+        compiler_params=pltpu.CompilerParams(vmem_limit_bytes=32 * 1024 * 1024),
+        cost_estimate=LIGHT,
+    )(share, *blocks, out_weight)
+
+
+def sum_shares(pieces):
+    total = pieces[0]
+    for flip in range(1, len(pieces)):
+        total = total + swap(pieces[flip], ("heads", "sub"), flip).astype(jnp.float32)
+    return total.astype(jnp.bfloat16)
 
 
 def find_blocks(place_holder, place_block, serving_request, items):
@@ -155,13 +180,7 @@
             pltpu.VMEM((slots, 2 * head_width), jnp.bfloat16),
         ],
         compiler_params=pltpu.CompilerParams(vmem_limit_bytes=32 * 1024 * 1024),
-        cost_estimate=pl.CostEstimate(
-            flops=requests
-            * slots
-            * (4 * text * width + 2 * rank_width * heads_here * pair_width),
-            bytes_accessed=requests * (4 * text * width + 2 * slots * rank_width),
-            transcendentals=requests * text * slots * (width // head_width),
-        ),
+        cost_estimate=LIGHT,
     )(scalars, queries, *parts, kv_flat, q_gain, k_gain)
 
 
@@ -195,9 +214,9 @@
         jnp.dot(selector, image_count), pool_index * requests_here, requests_here
     )
     scalars = jnp.concatenate([share.reshape(1), count_here])
-    pieces = fetch_pieces(latent_store, wanted)
-    pieces, kv_flat, scalars = tie((pieces, kv_flat, scalars))
-    chosen = jnp.concatenate(pieces, axis=0).at[where].get(mode="promise_in_bounds")
+    pieces = jnp.concatenate(fetch_pieces(latent_store, wanted), axis=0)
+    chosen = pieces.at[where].get(mode="promise_in_bounds")
+    chosen, kv_flat, scalars = tie((chosen, kv_flat, scalars))
     chosen = chosen.reshape(requests_here, -1, rank_width)
     over_heads = [chosen] + [swap(chosen, "heads", flip) for flip in range(1, heads_size)]
     parts = []
@@ -216,8 +235,8 @@
         outputs = []
         for chunk in range(CHUNKS):
             rows = lax.all_gather(attended(chunk), "pool", axis=0)
-            blocks = [rows[i] for i in range(pool_size)]
-            mine = jnp.stack(sum_shares(project_out(blocks, out_weight), pool_size))
+            mine = sum_shares(project_out([rows[i] for i in range(pool_size)], out_weight))
+            mine = mine.reshape(pool_size, -1, columns)
             back = lax.all_to_all(mine, "pool", split_axis=0, concat_axis=0, tiled=True)
             outputs.append(jnp.moveaxis(back, 0, 1).reshape(-1, pool_size * columns))
         return jnp.concatenate(outputs, axis=0)
@@ -225,37 +244,37 @@
     first = attended(0)
     across0, beside0 = swap(first, "pool", 3), swap(first, "pool", 1)
     last = attended(1)
-    first, last, across0, beside0 = tie((first, last, across0, beside0))
     across1, beside1 = swap(last, "pool", 3), swap(last, "pool", 1)
-    partial = project_out([first, last, beside0, across0], out_weight)
-    first, last, across0, across1, beside1, partial = tie(
-        (first, last, across0, across1, beside1, partial)
-    )
-    half = partial.shape[0] // 2
-    own, partial = partial[:half], partial[half:]
+    own = project_out([first, last], out_weight)
+    across0, beside0, own = tie((across0, beside0, own))
     second0 = second_hop(first, across0)
-    out_beside0, out_across0 = sum_shares(partial, 2)
-    partial = project_out([beside1, across1], out_weight)
-    second0, out_beside0, out_across0, partial, own, last, across1 = tie(
-        (second0, out_beside0, out_across0, partial, own, last, across1)
-    )
+    own = sum_shares(own)
+    pieces = project_out([beside0, across0], out_weight)
+    across1, beside1, own, pieces = tie((across1, beside1, own, pieces))
     second1 = second_hop(last, across1)
-    out_beside1, out_across1 = sum_shares(partial, 2)
-    partial = project_out([second0], out_weight)
-    second1, out_beside1, out_across1, partial, out_beside0, out_across0, own = tie(
-        (second1, out_beside1, out_across1, partial, out_beside0, out_across0, own)
-    )
-    back_across = swap(jnp.concatenate([out_across0, out_across1]), "pool", 3)
-    back_beside = swap(jnp.concatenate([out_beside0, out_beside1]), "pool", 1)
-    partial = jnp.concatenate([partial, project_out([second1], out_weight)])
-    out_second = jnp.concatenate(sum_shares(partial, 2))
-    back_across, back_beside, out_second, own = tie((back_across, back_beside, out_second, own))
-    back_second = swap(out_second, "pool", 2)
-    own = jnp.concatenate(sum_shares(own, 2))
+    near0 = sum_shares(pieces)
+    pieces = project_out([beside1, across1], out_weight)
+    second0, near0, pieces = tie((second0, near0, pieces))
+    half = near0.shape[0] // 2
+    back0 = swap(near0[:half], "pool", 1), swap(near0[half:], "pool", 3)
+    near1 = sum_shares(pieces)
+    pieces = project_out([second0], out_weight)
+    second1, near1, pieces, back0 = tie((second1, near1, pieces, back0))
+    back1 = swap(near1[:half], "pool", 1), swap(near1[half:], "pool", 3)
+    back_second0 = swap(sum_shares(pieces), "pool", 2)
+    far1 = sum_shares(project_out([second1], out_weight))
+    back1, back_second0, far1 = tie((back1, back_second0, far1))
+    back_second1 = swap(far1, "pool", 2)
+    backs = [
+        [own[:half], back0[0], back_second0, back0[1]],
+        [own[half:], back1[0], back_second1, back1[1]],
+    ]
     output = jnp.zeros((part_rows, pool_size * columns), jnp.bfloat16)
-    backs = [own, back_beside, back_second, back_across]
-    for flip in (0, 1, 3, 2):
-        output = lax.dynamic_update_slice(output, backs[flip], (0, (pool_index ^ flip) * columns))
+    for chunk in range(CHUNKS):
+        for flip in (0, 1, 3, 2):
+            output = lax.dynamic_update_slice(
+                output, backs[chunk][flip], (chunk * half, (pool_index ^ flip) * columns)
+            )
     return output
 
 

time: 180 us -> 172 us (0.956)
  Pallas kernels: 12.4 us -> 29.8 us
  waiting for transfers between devices: 102 us -> 87 us
  matrix products: 15.1 us -> 1.94 us
  local copies, waits for them, and re-layouts: 10.8 us -> 13.7 us
    pallas_call x0 -> x5, Pallas kernels: none -> 17.4 us  [project_out(): pl.pallas_call(functools.partial(project_kernel, len(blocks), share_count...]
    dot_general x4 -> x0, matrix products: 13.2 us -> none  [project_out(): partial = jnp.dot(rows, out_weight, preferred_element_type=jnp.float32)]
    ppermute x25 -> x31, waiting for transfers between devices: 96.8 us -> 87 us  [swap(): lax.ppermute(values, axis, [(i, i ^ flip) for i in range(lax.axis_size(ax...]
    ppermute x2, waiting for transfers between devices: 5.18 us -> 0.01 us  [second_hop(): return lax.ppermute(passed, 'pool', [(0, 2), (3, 1), (1, 0), (2, 3)])]
    unnamed x28, local copies, waits for them, and re-layouts: 2.79 us -> 6.17 us
    ppermute x25 -> x31, starting transfers between devices: 29.4 us -> 32.5 us  [swap(): lax.ppermute(values, axis, [(i, i ^ flip) for i in range(lax.axis_size(ax...]
    ppermute x2, starting transfers between devices: 5.96 us -> 3.02 us  [second_hop(): return lax.ppermute(passed, 'pool', [(0, 2), (3, 1), (1, 0), (2, 3)])]
  transfers between devices with their start and end apart: 27 -> 33, of which waited for: 20 -> 20; matrix products, arithmetic and copies ran while one was open for 8% -> 1% of each run, Pallas kernels for 3% -> 12%
where the time goes in v7:
time: 172 us; the launch traced here: 171 us
  waiting for transfers between devices  87 us (51%)
  starting transfers between devices  35.5 us (21%)
  Pallas kernels  29.8 us (17%)
  local copies, waits for them, and re-layouts  13.7 us (8%)
  other arithmetic  3.13 us (2%)
  matrix products  1.94 us (1%)
    ppermute x31, waiting for transfers between devices, swap(): lax.ppermute(values, axis, [(i, i ^ flip) for i in range(lax.axis_size(ax...  87 us
    ppermute x31, starting transfers between devices, swap(): lax.ppermute(values, axis, [(i, i ^ flip) for i in range(lax.axis_size(ax...  32.5 us
    pallas_call x5, Pallas kernels, project_out(): pl.pallas_call(functools.partial(project_kernel, len(blocks), share_count...  17.4 us
    pallas_call x2, Pallas kernels, attend(): pl.pallas_call(functools.partial(attend_kernel, len(parts)), grid=(reques...  12.4 us
    unnamed x28, local copies, waits for them, and re-layouts  6.17 us
  transfers between devices with their start and end apart: 33, of which 20 were waited for; matrix products, arithmetic and copies ran while one was open for 1% of the time, Pallas kernels for 12%

profile of v7, /device:TPU:0, one launch (start us, length us, event | category | flops | bytes accessed | tf_op | source)
XLA Modules:
  0.0 171.4 jit_solution(2393179532821311489)
XLA Ops:
  3.7 2.8 %gather_fusion.1 = bf16[32,32,512]{2,1,0:T(8,128)(2,1)S(1)} fusion(bf16[128,32,512]{2,1,0:T(8,128)(2,1)} %bitcast.36, s32[1024]{0:T(1024)S(1)} %pad_clamp_fusion.1), kind=kCustom, calls=%fused_computation.1 | custom fusion | bytes 2097280 | tf_op jit(solution)/shard_map/gather | solution.py:109
  7.3 3.0 %collective-permute-start = (bf16[8,32,512]{2,1,0:T(8,128)(2,1)}, bf16[8,32,512]{2,1,0:T(8,128)(2,1)S(1)}, u32[]{:S(2)}, u32[]{:S(2)}) collective-permute-start(bf16[8,32,512]{2,1,0:T(8,128)(2,1)} %get-tuple-element.115), channel_id=1, source_target_pairs={{0,4},{4,0},{8,12},{12,8},{1,5},{5,1},{9,13},{13,9},{2,6},{6,2},{1... | collective-permute-start | bytes 786440 | tf_op jit(solution)/shard_map/ppermute | solution.py:28
  10.3 2.6 %collective-permute-start.1 = (bf16[8,32,512]{2,1,0:T(8,128)(2,1)S(1)}, bf16[8,32,512]{2,1,0:T(8,128)(2,1)S(1)}, u32[]{:S(2)}, u32[]{:S(2)}) collective-permute-start(bf16[8,32,512]{2,1,0:T(8,128)(2,1)S(1)} %get-tuple-element.114), channel_id=1, source_target_pairs={{0,8},{4,12},{8,0},{12,4},{1,9},{5,13},{9,1},{13,5},{2,10},{6,14},... | collective-permute-start | bytes 786440 | tf_op jit(solution)/shard_map/ppermute | solution.py:28
  13.7 8.1 %collective-permute-done = bf16[8,32,512]{2,1,0:T(8,128)(2,1)S(1)} collective-permute-done((bf16[8,32,512]{2,1,0:T(8,128)(2,1)}, bf16[8,32,512]{2,1,0:T(8,128)(2,1)S(1)}, u32[]{:S(2)}, u32[]{:S(2)}) %collective-permute-start) | collective-permute-done | bytes 262176 | tf_op jit(solution)/shard_map/ppermute | solution.py:28
  21.8 9.9 %collective-permute-done.1 = bf16[8,32,512]{2,1,0:T(8,128)(2,1)S(1)} collective-permute-done((bf16[8,32,512]{2,1,0:T(8,128)(2,1)S(1)}, bf16[8,32,512]{2,1,0:T(8,128)(2,1)S(1)}, u32[]{:S(2)}, u32[]{:S(2)}) %collective-permute-start.1) | collective-permute-done | bytes 262176 | tf_op jit(solution)/shard_map/ppermute | solution.py:28
  37.1 10.0 %collective-permute-done.4.refs_2_ = bf16[2,256,512]{2,1,0:T(8,128)(2,1)S(1)} collective-permute-done((bf16[2,256,512]{2,1,0:T(8,128)(2,1)S(1)}, bf16[2,256,512]{2,1,0:T(8,128)(2,1)S(1)}, u32[]{:S(2)}, u32[]{:S(2)}) %collective-permute-start.4) | collective-permute-done | bytes 524320 | tf_op jit(solution)/shard_map/ppermute | solution.py:28
  49.1 6.2 %shard_map.101.refs_0_ = bf16[128,2048]{1,0:T(8,128)(2,1)S(1)} custom-call(s32[3]{0:T(128)S(1)} %pad_add_fusion.scalars, bf16[2,2,2,32,2048]{4,3,2,1,0:T(8,128)(2,1)S(1)} %bitcast.30, bf16[2,256,512]{2,1,0:T(8,128)(2,1)S(1)} %bitcast.28, bf16[2,256,512]{2,1,0:T(8,128)(2,1)S(1)} %collective-permute-done.3.refs_1_, ...), custom_call_target="tpu_custom_call" | custom-call | flops 1 | bytes 1 | tf_op jit(solution)/shard_map/pallas_call | solution.py:164
  56.7 6.1 %collective-permute-start.9 = (bf16[128,2048]{1,0:T(8,128)(2,1)S(1)}, bf16[128,2048]{1,0:T(8,128)(2,1)}, u32[]{:S(2)}, u32[]{:S(2)}) collective-permute-start(bf16[128,2048]{1,0:T(8,128)(2,1)S(1)} %shard_map.101.refs_0_), channel_id=1, source_target_pairs={{0,4},{4,0},{8,12},{12,8},{1,5},{5,1},{9,13},{13,9},{2,6},{6,2},{1... | collective-permute-start | bytes 1572872 | tf_op jit(solution)/shard_map/ppermute | solution.py:28
  64.9 6.2 %shard_map.100.refs_1_ = bf16[128,2048]{1,0:T(8,128)(2,1)S(1)} custom-call(s32[3]{0:T(128)S(1)} %pad_add_fusion.scalars, bf16[2,2,2,32,2048]{4,3,2,1,0:T(8,128)(2,1)S(1)} %bitcast.31, bf16[2,256,512]{2,1,0:T(8,128)(2,1)S(1)} %bitcast.29, bf16[2,256,512]{2,1,0:T(8,128)(2,1)S(1)} %copy-done.5, bf16[2,256,512]{2,1,0:T(8,128)(2,1)S(1)} %collective-permute-done.4.refs_2_, ...), custom_call_target="tpu_custom_call" | custom-call | flops 1 | bytes 1 | tf_op jit(solution)/shard_map/pallas_call | solution.py:164
  72.5 3.4 %copy-done.1 = bf16[2048,2048]{1,0:T(8,128)(2,1)S(1)} copy-done((bf16[2048,2048]{1,0:T(8,128)(2,1)S(1)}, bf16[2048,2048]{1,0:T(8,128)(2,1)}, u32[]{:S(2)}) %copy-start.1) | copy-done | bytes 8388632
  75.8 3.7 %shard_map.102 = (f32[64,2048]{1,0:T(8,128)S(1)}, bf16[64,2048]{1,0:T(8,128)(2,1)S(1)}, bf16[64,2048]{1,0:T(8,128)(2,1)S(1)}, bf16[64,2048]{1,0:T(8,128)(2,1)S(1)}) custom-call(s32[1]{0:T(128)} %bitcast.6.share, bf16[128,2048]{1,0:T(8,128)(2,1)S(1)} %shard_map.101.refs_0_, bf16[128,2048]{1,0:T(8,128)(2,1)S(1)} %shard_map.100.refs_1_, ...), custom_call_target="tpu_custom_call" | custom-call | flops 1 | bytes 1 | tf_op jit(solution)/shard_map/pallas_call | solution.py:61
  79.5 3.8 %collective-permute-done.9.refs_0_ = bf16[128,2048]{1,0:T(8,128)(2,1)} collective-permute-done((bf16[128,2048]{1,0:T(8,128)(2,1)S(1)}, bf16[128,2048]{1,0:T(8,128)(2,1)}, u32[]{:S(2)}, u32[]{:S(2)}) %collective-permute-start.9) | collective-permute-done | bytes 524320 | tf_op jit(solution)/shard_map/ppermute | solution.py:28
  85.3 4.7 %shard_map.103 = (f32[64,2048]{1,0:T(8,128)S(1)}, bf16[64,2048]{1,0:T(8,128)(2,1)S(1)}, bf16[64,2048]{1,0:T(8,128)(2,1)S(1)}, bf16[64,2048]{1,0:T(8,128)(2,1)S(1)}) custom-call(s32[1]{0:T(128)} %bitcast.6.share, bf16[128,2048]{1,0:T(8,128)(2,1)} %collective-permute-done.9.refs_0_, bf16[128,2048]{1,0:T(8,128)(2,1)} %collective-permute-done.8.refs_1_, ...), custom_call_target="tpu_custom_call" | custom-call | flops 1 | bytes 1 | tf_op jit(solution)/shard_map/pallas_call | solution.py:61
  92.5 4.8 %collective-permute-done.12 = bf16[64,2048]{1,0:T(8,128)(2,1)S(1)} collective-permute-done((bf16[64,2048]{1,0:T(8,128)(2,1)S(1)}, bf16[64,2048]{1,0:T(8,128)(2,1)S(1)}, u32[]{:S(2)}, u32[]{:S(2)}) %collective-permute-start.12) | collective-permute-done | bytes 262176 | tf_op jit(solution)/shard_map/ppermute | solution.py:28
  97.4 7.5 %collective-permute-done.7.refs_0_ = bf16[128,2048]{1,0:T(8,128)(2,1)S(1)} collective-permute-done((bf16[128,2048]{1,0:T(8,128)(2,1)S(1)}, bf16[128,2048]{1,0:T(8,128)(2,1)S(1)}, u32[]{:S(2)}, u32[]{:S(2)}) %collective-permute-start.7) | collective-permute-done | bytes 524320 | tf_op jit(solution)/shard_map/ppermute | solution.py:28
  108.3 3.7 %shard_map.104 = (f32[64,2048]{1,0:T(8,128)S(1)}, bf16[64,2048]{1,0:T(8,128)(2,1)S(1)}, bf16[64,2048]{1,0:T(8,128)(2,1)S(1)}, bf16[64,2048]{1,0:T(8,128)(2,1)S(1)}) custom-call(s32[1]{0:T(128)} %bitcast.6.share, bf16[128,2048]{1,0:T(8,128)(2,1)S(1)} %collective-permute-done.7.refs_0_, bf16[128,2048]{1,0:T(8,128)(2,1)S(1)} %collective-permute-done.6.refs_1_, ...), custom_call_target="tpu_custom_call" | custom-call | flops 1 | bytes 1 | tf_op jit(solution)/shard_map/pallas_call | solution.py:61
  114.0 4.8 %collective-permute-done.17 = bf16[64,2048]{1,0:T(8,128)(2,1)S(1)} collective-permute-done((bf16[64,2048]{1,0:T(8,128)(2,1)S(1)}, bf16[64,2048]{1,0:T(8,128)(2,1)S(1)}, u32[]{:S(2)}, u32[]{:S(2)}) %collective-permute-start.17) | collective-permute-done | bytes 262176 | tf_op jit(solution)/shard_map/ppermute | solution.py:28
  121.1 2.7 %shard_map.105 = (f32[32,2048]{1,0:T(8,128)S(1)}, bf16[32,2048]{1,0:T(8,128)(2,1)S(1)}, bf16[32,2048]{1,0:T(8,128)(2,1)S(1)}, bf16[32,2048]{1,0:T(8,128)(2,1)S(1)}) custom-call(s32[1]{0:T(128)} %bitcast.6.share, bf16[128,2048]{1,0:T(8,128)(2,1)S(1)} %collective-permute-done.14.refs_0_, bf16[2048,2048]{1,0:T(8,128)(2,1)S(1)} %copy-done.2), custom_call_target="tpu_custom_call" | custom-call | flops 1 | bytes 1 | tf_op jit(solution)/shard_map/pallas_call | solution.py:61
  128.7 3.9 %collective-permute-done.20 = bf16[64,2048]{1,0:T(8,128)(2,1)S(1)} collective-permute-done((bf16[64,2048]{1,0:T(8,128)(2,1)S(1)}, bf16[64,2048]{1,0:T(8,128)(2,1)S(1)}, u32[]{:S(2)}, u32[]{:S(2)}) %collective-permute-start.20) | collective-permute-done | bytes 262176 | tf_op jit(solution)/shard_map/ppermute | solution.py:28
  133.6 2.7 %shard_map.106 = (f32[32,2048]{1,0:T(8,128)S(1)}, bf16[32,2048]{1,0:T(8,128)(2,1)S(1)}, bf16[32,2048]{1,0:T(8,128)(2,1)S(1)}, bf16[32,2048]{1,0:T(8,128)(2,1)S(1)}) custom-call(s32[1]{0:T(128)} %bitcast.6.share, bf16[128,2048]{1,0:T(8,128)(2,1)S(1)} %collective-permute-done.13.refs_0_, bf16[2048,2048]{1,0:T(8,128)(2,1)S(1)} %copy-done.2), custom_call_target="tpu_custom_call" | custom-call | flops 1 | bytes 1 | tf_op jit(solution)/shard_map/pallas_call | solution.py:61
  140.4 5.1 %collective-permute-done.26 = bf16[32,2048]{1,0:T(8,128)(2,1)S(1)} collective-permute-done((bf16[32,2048]{1,0:T(8,128)(2,1)S(1)}, bf16[32,2048]{1,0:T(8,128)(2,1)S(1)}, u32[]{:S(2)}, u32[]{:S(2)}) %collective-permute-start.26) | collective-permute-done | bytes 131104 | tf_op jit(solution)/shard_map/ppermute | solution.py:28
  150.6 5.0 %collective-permute-done.24 = bf16[32,2048]{1,0:T(8,128)(2,1)S(1)} collective-permute-done((bf16[32,2048]{1,0:T(8,128)(2,1)S(1)}, bf16[32,2048]{1,0:T(8,128)(2,1)S(1)}, u32[]{:S(2)}, u32[]{:S(2)}) %collective-permute-start.24) | collective-permute-done | bytes 131104 | tf_op jit(solution)/shard_map/ppermute | solution.py:28
  155.5 7.0 %collective-permute-done.28 = bf16[32,2048]{1,0:T(8,128)(2,1)S(1)} collective-permute-done((bf16[32,2048]{1,0:T(8,128)(2,1)S(1)}, bf16[32,2048]{1,0:T(8,128)(2,1)S(1)}, u32[]{:S(2)}, u32[]{:S(2)}) %collective-permute-start.28) | collective-permute-done | bytes 131104 | tf_op jit(solution)/shard_map/ppermute | solution.py:28
  162.7 8.1 %collective-permute-done.32 = bf16[32,2048]{1,0:T(8,128)(2,1)S(1)} collective-permute-done((bf16[32,2048]{1,0:T(8,128)(2,1)S(1)}, bf16[32,2048]{1,0:T(8,128)(2,1)S(1)}, u32[]{:S(2)}, u32[]{:S(2)}) %collective-permute-start.32) | collective-permute-done | bytes 131104 | tf_op jit(solution)/shard_map/ppermute | solution.py:28
  (121 shorter events, 45.4 us)
Async XLA Ops:
  7.3 14.5 %collective-permute-start = (bf16[8,32,512]{2,1,0:T(8,128)(2,1)}, bf16[8,32,512]{2,1,0:T(8,128)(2,1)S(1)}, u32[]{:S(2)}, u32[]{:S(2)}) collective-permute-start(bf16[8,32,512]{2,1,0:T(8,128)(2,1)} %get-tuple-element.115), channel_id=1, source_target_pairs={{0,4},{4,0},{8,12},{12,8},{1,5},{5,1},{9,13},{13,9},{2,6},{6,2},{1... | collective-permute-start | bytes 786440 | tf_op jit(solution)/shard_map/ppermute | solution.py:28
  10.3 21.4 %collective-permute-start.1 = (bf16[8,32,512]{2,1,0:T(8,128)(2,1)S(1)}, bf16[8,32,512]{2,1,0:T(8,128)(2,1)S(1)}, u32[]{:S(2)}, u32[]{:S(2)}) collective-permute-start(bf16[8,32,512]{2,1,0:T(8,128)(2,1)S(1)} %get-tuple-element.114), channel_id=1, source_target_pairs={{0,8},{4,12},{8,0},{12,4},{1,9},{5,13},{9,1},{13,5},{2,10},{6,14},... | collective-permute-start | bytes 786440 | tf_op jit(solution)/shard_map/ppermute | solution.py:28
  12.9 18.8 %collective-permute-start.2 = (bf16[8,32,512]{2,1,0:T(8,128)(2,1)S(1)}, bf16[8,32,512]{2,1,0:T(8,128)(2,1)}, u32[]{:S(2)}, u32[]{:S(2)}) collective-permute-start(bf16[8,32,512]{2,1,0:T(8,128)(2,1)S(1)} %get-tuple-element.116), channel_id=1, source_target_pairs={{0,12},{4,8},{8,4},{12,0},{1,13},{5,9},{9,5},{13,1},{2,14},{6,10},... | collective-permute-start | bytes 786440 | tf_op jit(solution)/shard_map/ppermute | solution.py:28
  35.6 11.6 %collective-permute-start.4 = (bf16[2,256,512]{2,1,0:T(8,128)(2,1)S(1)}, bf16[2,256,512]{2,1,0:T(8,128)(2,1)S(1)}, u32[]{:S(2)}, u32[]{:S(2)}) collective-permute-start(bf16[2,256,512]{2,1,0:T(8,128)(2,1)S(1)} %bitcast.26), channel_id=1, source_target_pairs={{0,2},{2,0},{1,3},{3,1},{4,6},{6,4},{5,7},{7,5},{8,10},{10,8},{9,1... | collective-permute-start | bytes 1572872 | tf_op jit(solution)/shard_map/ppermute | solution.py:28
  37.1 10.0 %collective-permute-start.3 = (bf16[2,256,512]{2,1,0:T(8,128)(2,1)S(1)}, bf16[2,256,512]{2,1,0:T(8,128)(2,1)S(1)}, u32[]{:S(2)}, u32[]{:S(2)}) collective-permute-start(bf16[2,256,512]{2,1,0:T(8,128)(2,1)S(1)} %bitcast.27), channel_id=1, source_target_pairs={{0,1},{1,0},{2,3},{3,2},{4,5},{5,4},{6,7},{7,6},{8,9},{9,8},{10,11... | collective-permute-start | bytes 1572872 | tf_op jit(solution)/shard_map/ppermute | solution.py:28
  55.3 24.3 %collective-permute-start.8 = (bf16[128,2048]{1,0:T(8,128)(2,1)S(1)}, bf16[128,2048]{1,0:T(8,128)(2,1)}, u32[]{:S(2)}, u32[]{:S(2)}) collective-permute-start(bf16[128,2048]{1,0:T(8,128)(2,1)S(1)} %shard_map.101.refs_0_), channel_id=1, source_target_pairs={{0,12},{4,8},{8,4},{12,0},{1,13},{5,9},{9,5},{13,1},{2,14},{6,10},... | collective-permute-start | bytes 1572872 | tf_op jit(solution)/shard_map/ppermute | solution.py:28
  56.7 26.7 %collective-permute-start.9 = (bf16[128,2048]{1,0:T(8,128)(2,1)S(1)}, bf16[128,2048]{1,0:T(8,128)(2,1)}, u32[]{:S(2)}, u32[]{:S(2)}) collective-permute-start(bf16[128,2048]{1,0:T(8,128)(2,1)S(1)} %shard_map.101.refs_0_), channel_id=1, source_target_pairs={{0,4},{4,0},{8,12},{12,8},{1,5},{5,1},{9,13},{13,9},{2,6},{6,2},{1... | collective-permute-start | bytes 1572872 | tf_op jit(solution)/shard_map/ppermute | solution.py:28
  71.0 26.4 %collective-permute-start.6 = (bf16[128,2048]{1,0:T(8,128)(2,1)S(1)}, bf16[128,2048]{1,0:T(8,128)(2,1)S(1)}, u32[]{:S(2)}, u32[]{:S(2)}) collective-permute-start(bf16[128,2048]{1,0:T(8,128)(2,1)S(1)} %shard_map.100.refs_1_), channel_id=1, source_target_pairs={{0,12},{4,8},{8,4},{12,0},{1,13},{5,9},{9,5},{13,1},{2,14},{6,10},... | collective-permute-start | bytes 1572872 | tf_op jit(solution)/shard_map/ppermute | solution.py:28
  72.5 32.4 %collective-permute-start.7 = (bf16[128,2048]{1,0:T(8,128)(2,1)S(1)}, bf16[128,2048]{1,0:T(8,128)(2,1)S(1)}, u32[]{:S(2)}, u32[]{:S(2)}) collective-permute-start(bf16[128,2048]{1,0:T(8,128)(2,1)S(1)} %shard_map.100.refs_1_), channel_id=1, source_target_pairs={{0,4},{4,0},{8,12},{12,8},{1,5},{5,1},{9,13},{13,9},{2,6},{6,2},{1... | collective-permute-start | bytes 1572872 | tf_op jit(solution)/shard_map/ppermute | solution.py:28
  83.3 9.1 %collective-permute-start.11 = (bf16[64,2048]{1,0:T(8,128)(2,1)S(1)}, bf16[64,2048]{1,0:T(8,128)(2,1)S(1)}, u32[]{:S(2)}, u32[]{:S(2)}) collective-permute-start(bf16[64,2048]{1,0:T(8,128)(2,1)S(1)} %get-tuple-element.68), channel_id=1, source_target_pairs={{0,2},{1,3},{2,0},{3,1},{4,6},{5,7},{6,4},{7,5},{8,10},{9,11},{10,... | collective-permute-start | bytes 786440 | tf_op jit(solution)/shard_map/ppermute | solution.py:28
  84.8 12.5 %collective-permute-start.12 = (bf16[64,2048]{1,0:T(8,128)(2,1)S(1)}, bf16[64,2048]{1,0:T(8,128)(2,1)S(1)}, u32[]{:S(2)}, u32[]{:S(2)}) collective-permute-start(bf16[64,2048]{1,0:T(8,128)(2,1)S(1)} %get-tuple-element.69), channel_id=1, source_target_pairs={{0,3},{1,2},{2,1},{3,0},{4,7},{5,6},{6,5},{7,4},{8,11},{9,10},{10,... | collective-permute-start | bytes 786440 | tf_op jit(solution)/shard_map/ppermute | solution.py:28
  90.0 28.9 %collective-permute-start.14 = (bf16[128,2048]{1,0:T(8,128)(2,1)S(1)}, bf16[128,2048]{1,0:T(8,128)(2,1)S(1)}, u32[]{:S(2)}, u32[]{:S(2)}) collective-permute-start(bf16[128,2048]{1,0:T(8,128)(2,1)S(1)} %broadcast_select_fusion), channel_id=1, source_target_pairs={{0,8},{12,4},{4,0},{8,12},{1,9},{13,5},{5,1},{9,13},{2,10},{14,6},... | collective-permute-start | bytes 1572872 | tf_op jit(solution)/shard_map/ppermute | solution.py:35
  104.9 9.1 %collective-permute-start.16 = (bf16[64,2048]{1,0:T(8,128)(2,1)S(1)}, bf16[64,2048]{1,0:T(8,128)(2,1)S(1)}, u32[]{:S(2)}, u32[]{:S(2)}) collective-permute-start(bf16[64,2048]{1,0:T(8,128)(2,1)S(1)} %get-tuple-element.80), channel_id=1, source_target_pairs={{0,2},{1,3},{2,0},{3,1},{4,6},{5,7},{6,4},{7,5},{8,10},{9,11},{10,... | collective-permute-start | bytes 786440 | tf_op jit(solution)/shard_map/ppermute | solution.py:28
  106.4 12.4 %collective-permute-start.17 = (bf16[64,2048]{1,0:T(8,128)(2,1)S(1)}, bf16[64,2048]{1,0:T(8,128)(2,1)S(1)}, u32[]{:S(2)}, u32[]{:S(2)}) collective-permute-start(bf16[64,2048]{1,0:T(8,128)(2,1)S(1)} %get-tuple-element.81), channel_id=1, source_target_pairs={{0,3},{1,2},{2,1},{3,0},{4,7},{5,6},{6,5},{7,4},{8,11},{9,10},{10,... | collective-permute-start | bytes 786440 | tf_op jit(solution)/shard_map/ppermute | solution.py:28
  106.8 26.8 %collective-permute-start.13 = (bf16[128,2048]{1,0:T(8,128)(2,1)S(1)}, bf16[128,2048]{1,0:T(8,128)(2,1)S(1)}, u32[]{:S(2)}, u32[]{:S(2)}) collective-permute-start(bf16[128,2048]{1,0:T(8,128)(2,1)S(1)} %broadcast_select_fusion.1), channel_id=1, source_target_pairs={{0,8},{12,4},{4,0},{8,12},{1,9},{13,5},{5,1},{9,13},{2,10},{14,6},... | collective-permute-start | bytes 1572872 | tf_op jit(solution)/shard_map/ppermute | solution.py:35
  119.5 9.2 %collective-permute-start.19 = (bf16[64,2048]{1,0:T(8,128)(2,1)S(1)}, bf16[64,2048]{1,0:T(8,128)(2,1)S(1)}, u32[]{:S(2)}, u32[]{:S(2)}) collective-permute-start(bf16[64,2048]{1,0:T(8,128)(2,1)S(1)} %get-tuple-element.89), channel_id=1, source_target_pairs={{0,2},{1,3},{2,0},{3,1},{4,6},{5,7},{6,4},{7,5},{8,10},{9,11},{10,... | collective-permute-start | bytes 786440 | tf_op jit(solution)/shard_map/ppermute | solution.py:28
  121.0 11.5 %collective-permute-start.20 = (bf16[64,2048]{1,0:T(8,128)(2,1)S(1)}, bf16[64,2048]{1,0:T(8,128)(2,1)S(1)}, u32[]{:S(2)}, u32[]{:S(2)}) collective-permute-start(bf16[64,2048]{1,0:T(8,128)(2,1)S(1)} %get-tuple-element.90), channel_id=1, source_target_pairs={{0,3},{1,2},{2,1},{3,0},{4,7},{5,6},{6,5},{7,4},{8,11},{9,10},{10,... | collective-permute-start | bytes 786440 | tf_op jit(solution)/shard_map/ppermute | solution.py:28
  123.7 9.0 %collective-permute-start.21 = (bf16[32,2048]{1,0:T(8,128)(2,1)S(1)}, bf16[32,2048]{1,0:T(8,128)(2,1)S(1)}, u32[]{:S(2)}, u32[]{:S(2)}) collective-permute-start(bf16[32,2048]{1,0:T(8,128)(2,1)S(1)} %get-tuple-element.120), channel_id=1, source_target_pairs={{0,4},{4,0},{8,12},{12,8},{1,5},{5,1},{9,13},{13,9},{2,6},{6,2},{1... | collective-permute-start | bytes 393224 | tf_op jit(solution)/shard_map/ppermute | solution.py:28
  125.0 8.6 %collective-permute-start.22 = (bf16[32,2048]{1,0:T(8,128)(2,1)S(1)}, bf16[32,2048]{1,0:T(8,128)(2,1)S(1)}, u32[]{:S(2)}, u32[]{:S(2)}) collective-permute-start(bf16[32,2048]{1,0:T(8,128)(2,1)S(1)} %get-tuple-element.119), channel_id=1, source_target_pairs={{0,12},{4,8},{8,4},{12,0},{1,13},{5,9},{9,5},{13,1},{2,14},{6,10},... | collective-permute-start | bytes 393224 | tf_op jit(solution)/shard_map/ppermute | solution.py:28
  136.2 13.3 %collective-permute-start.29 = (bf16[32,2048]{1,0:T(8,128)(2,1)S(1)}, bf16[32,2048]{1,0:T(8,128)(2,1)S(1)}, u32[]{:S(2)}, u32[]{:S(2)}) collective-permute-start(bf16[32,2048]{1,0:T(8,128)(2,1)S(1)} %get-tuple-element.106), channel_id=1, source_target_pairs={{0,1},{1,0},{2,3},{3,2},{4,5},{5,4},{6,7},{7,6},{8,9},{9,8},{10,11... | collective-permute-start | bytes 393224 | tf_op jit(solution)/shard_map/ppermute | solution.py:28
  136.5 13.5 %collective-permute-start.30 = (bf16[32,2048]{1,0:T(8,128)(2,1)S(1)}, bf16[32,2048]{1,0:T(8,128)(2,1)S(1)}, u32[]{:S(2)}, u32[]{:S(2)}) collective-permute-start(bf16[32,2048]{1,0:T(8,128)(2,1)S(1)} %get-tuple-element.107), channel_id=1, source_target_pairs={{0,2},{1,3},{2,0},{3,1},{4,6},{5,7},{6,4},{7,5},{8,10},{9,11},{10,... | collective-permute-start | bytes 393224 | tf_op jit(solution)/shard_map/ppermute | solution.py:28
  138.6 8.9 %collective-permute-start.27 = (bf16[32,2048]{1,0:T(8,128)(2,1)S(1)}, bf16[32,2048]{1,0:T(8,128)(2,1)S(1)}, u32[]{:S(2)}, u32[]{:S(2)}) collective-permute-start(bf16[32,2048]{1,0:T(8,128)(2,1)S(1)} %get-tuple-element.103), channel_id=1, source_target_pairs={{0,3},{1,2},{2,1},{3,0},{4,7},{5,6},{6,5},{7,4},{8,11},{9,10},{10,... | collective-permute-start | bytes 393224 | tf_op jit(solution)/shard_map/ppermute | solution.py:28
  139.9 10.2 %collective-permute-start.31 = (bf16[32,2048]{1,0:T(8,128)(2,1)S(1)}, bf16[32,2048]{1,0:T(8,128)(2,1)S(1)}, u32[]{:S(2)}, u32[]{:S(2)}) collective-permute-start(bf16[32,2048]{1,0:T(8,128)(2,1)S(1)} %get-tuple-element.108), channel_id=1, source_target_pairs={{0,3},{1,2},{2,1},{3,0},{4,7},{5,6},{6,5},{7,4},{8,11},{9,10},{10,... | collective-permute-start | bytes 393224 | tf_op jit(solution)/shard_map/ppermute | solution.py:28
  149.5 13.0 %collective-permute-start.28 = (bf16[32,2048]{1,0:T(8,128)(2,1)S(1)}, bf16[32,2048]{1,0:T(8,128)(2,1)S(1)}, u32[]{:S(2)}, u32[]{:S(2)}) collective-permute-start(bf16[32,2048]{1,0:T(8,128)(2,1)S(1)} %add_convert_fusion.4), channel_id=1, source_target_pairs={{0,8},{4,12},{8,0},{12,4},{1,9},{5,13},{9,1},{13,5},{2,10},{6,14},... | collective-permute-start | bytes 393224 | tf_op jit(solution)/shard_map/ppermute | solution.py:28
  (23 other events, 258.7 us)

commit v8 on v7

--- a/solution.py
+++ b/solution.py
@@ -78,6 +78,20 @@
     total = pieces[0]
     for flip in range(1, len(pieces)):
         total = total + swap(pieces[flip], ("heads", "sub"), flip).astype(jnp.float32)
+    return total.astype(jnp.bfloat16)
+
+
+def sum_in_turn(pieces):
+    sub_size = lax.axis_size("sub")
+    by_sub = []
+    for first in range(0, len(pieces), sub_size):
+        total = pieces[first].astype(jnp.float32)
+        for flip in range(1, sub_size):
+            total = total + swap(pieces[first + flip], "sub", flip).astype(jnp.float32)
+        by_sub.append(total)
+    total = by_sub[0]
+    for flip in range(1, len(by_sub)):
+        total = total + swap(by_sub[flip].astype(jnp.bfloat16), "heads", flip).astype(jnp.float32)
     return total.astype(jnp.bfloat16)
 
 
@@ -248,22 +262,20 @@
     own = project_out([first, last], out_weight)
     across0, beside0, own = tie((across0, beside0, own))
     second0 = second_hop(first, across0)
-    own = sum_shares(own)
-    pieces = project_out([beside0, across0], out_weight)
-    across1, beside1, own, pieces = tie((across1, beside1, own, pieces))
+    own = sum_in_turn(own)
+    near0 = sum_shares(project_out([beside0, across0], out_weight))
+    across1, beside1, own, near0 = tie((across1, beside1, own, near0))
     second1 = second_hop(last, across1)
-    near0 = sum_shares(pieces)
-    pieces = project_out([beside1, across1], out_weight)
-    second0, near0, pieces = tie((second0, near0, pieces))
     half = near0.shape[0] // 2
     back0 = swap(near0[:half], "pool", 1), swap(near0[half:], "pool", 3)
-    near1 = sum_shares(pieces)
-    pieces = project_out([second0], out_weight)
-    second1, near1, pieces, back0 = tie((second1, near1, pieces, back0))
+    near1 = sum_shares(project_out([beside1, across1], out_weight))
+    second0, near1, back0 = tie((second0, near1, back0))
     back1 = swap(near1[:half], "pool", 1), swap(near1[half:], "pool", 3)
-    back_second0 = swap(sum_shares(pieces), "pool", 2)
+    far0 = sum_shares(project_out([second0], out_weight))
+    second1, far0, back1 = tie((second1, far0, back1))
+    back_second0 = swap(far0, "pool", 2)
     far1 = sum_shares(project_out([second1], out_weight))
-    back1, back_second0, far1 = tie((back1, back_second0, far1))
+    back_second0, far1 = tie((back_second0, far1))
     back_second1 = swap(far1, "pool", 2)
     backs = [
         [own[:half], back0[0], back_second0, back0[1]],

time: 172 us -> 167 us (0.971)
  starting transfers between devices: 35.5 us -> 32.1 us
  waiting for transfers between devices: 87 us -> 85.1 us
    ppermute x2, starting transfers between devices: 3.02 us -> 1 us  [second_hop(): return lax.ppermute(passed, 'pool', [(0, 2), (3, 1), (1, 0), (2, 3)])]
    ppermute x31, waiting for transfers between devices: 87 us -> 85.1 us  [swap(): lax.ppermute(values, axis, [(i, i ^ flip) for i in range(lax.axis_size(ax...]
  transfers between devices with their start and end apart: 33 -> 33, of which waited for: 20 -> 19; matrix products, arithmetic and copies ran while one was open for 1% -> 1% of each run, Pallas kernels for 12% -> 13%
where the time goes in v8:
time: 167 us; the launch traced here: 166 us
  waiting for transfers between devices  85.1 us (51%)
  starting transfers between devices  32.1 us (19%)
  Pallas kernels  29.7 us (18%)
  local copies, waits for them, and re-layouts  13.7 us (8%)
  other arithmetic  3.16 us (2%)
  matrix products  1.94 us (1%)
    ppermute x31, waiting for transfers between devices, swap(): lax.ppermute(values, axis, [(i, i ^ flip) for i in range(lax.axis_size(ax...  85.1 us
    ppermute x31, starting transfers between devices, swap(): lax.ppermute(values, axis, [(i, i ^ flip) for i in range(lax.axis_size(ax...  31.1 us
    pallas_call x5, Pallas kernels, project_out(): pl.pallas_call(functools.partial(project_kernel, len(blocks), share_count...  17.4 us
    pallas_call x2, Pallas kernels, attend(): pl.pallas_call(functools.partial(attend_kernel, len(parts)), grid=(reques...  12.4 us
    unnamed x28, local copies, waits for them, and re-layouts  6.17 us
  transfers between devices with their start and end apart: 33, of which 19 were waited for; matrix products, arithmetic and copies ran while one was open for 1% of the time, Pallas kernels for 13%

profile of v8, /device:TPU:0, one launch (start us, length us, event | category | flops | bytes accessed | tf_op | source)
XLA Modules:
  0.0 166.2 jit_solution(15758265051137017444)
XLA Ops:
  3.7 2.8 %gather_fusion.1 = bf16[32,32,512]{2,1,0:T(8,128)(2,1)S(1)} fusion(bf16[128,32,512]{2,1,0:T(8,128)(2,1)} %bitcast.36, s32[1024]{0:T(1024)S(1)} %pad_clamp_fusion.1), kind=kCustom, calls=%fused_computation.1 | custom fusion | bytes 2097280 | tf_op jit(solution)/shard_map/gather | solution.py:123
  7.3 3.0 %collective-permute-start = (bf16[8,32,512]{2,1,0:T(8,128)(2,1)}, bf16[8,32,512]{2,1,0:T(8,128)(2,1)S(1)}, u32[]{:S(2)}, u32[]{:S(2)}) collective-permute-start(bf16[8,32,512]{2,1,0:T(8,128)(2,1)} %get-tuple-element.93), channel_id=1, source_target_pairs={{0,4},{4,0},{8,12},{12,8},{1,5},{5,1},{9,13},{13,9},{2,6},{6,2},{1... | collective-permute-start | bytes 786440 | tf_op jit(solution)/shard_map/ppermute | solution.py:28
  13.7 8.1 %collective-permute-done = bf16[8,32,512]{2,1,0:T(8,128)(2,1)S(1)} collective-permute-done((bf16[8,32,512]{2,1,0:T(8,128)(2,1)}, bf16[8,32,512]{2,1,0:T(8,128)(2,1)S(1)}, u32[]{:S(2)}, u32[]{:S(2)}) %collective-permute-start) | collective-permute-done | bytes 262176 | tf_op jit(solution)/shard_map/ppermute | solution.py:28
  21.8 9.9 %collective-permute-done.1 = bf16[8,32,512]{2,1,0:T(8,128)(2,1)S(1)} collective-permute-done((bf16[8,32,512]{2,1,0:T(8,128)(2,1)S(1)}, bf16[8,32,512]{2,1,0:T(8,128)(2,1)S(1)}, u32[]{:S(2)}, u32[]{:S(2)}) %collective-permute-start.1) | collective-permute-done | bytes 262176 | tf_op jit(solution)/shard_map/ppermute | solution.py:28
  37.1 10.0 %collective-permute-done.4.refs_2_ = bf16[2,256,512]{2,1,0:T(8,128)(2,1)S(1)} collective-permute-done((bf16[2,256,512]{2,1,0:T(8,128)(2,1)S(1)}, bf16[2,256,512]{2,1,0:T(8,128)(2,1)S(1)}, u32[]{:S(2)}, u32[]{:S(2)}) %collective-permute-start.4) | collective-permute-done | bytes 524320 | tf_op jit(solution)/shard_map/ppermute | solution.py:28
  49.1 6.2 %shard_map.101.refs_0_ = bf16[128,2048]{1,0:T(8,128)(2,1)S(1)} custom-call(s32[3]{0:T(128)S(1)} %pad_add_fusion.scalars, bf16[2,2,2,32,2048]{4,3,2,1,0:T(8,128)(2,1)S(1)} %bitcast.30, bf16[2,256,512]{2,1,0:T(8,128)(2,1)S(1)} %bitcast.28, bf16[2,256,512]{2,1,0:T(8,128)(2,1)S(1)} %collective-permute-done.3.refs_1_, ...), custom_call_target="tpu_custom_call" | custom-call | flops 1 | bytes 1 | tf_op jit(solution)/shard_map/pallas_call | solution.py:178
  56.7 6.1 %collective-permute-start.9 = (bf16[128,2048]{1,0:T(8,128)(2,1)S(1)}, bf16[128,2048]{1,0:T(8,128)(2,1)}, u32[]{:S(2)}, u32[]{:S(2)}) collective-permute-start(bf16[128,2048]{1,0:T(8,128)(2,1)S(1)} %shard_map.101.refs_0_), channel_id=1, source_target_pairs={{0,4},{4,0},{8,12},{12,8},{1,5},{5,1},{9,13},{13,9},{2,6},{6,2},{1... | collective-permute-start | bytes 1572872 | tf_op jit(solution)/shard_map/ppermute | solution.py:28
  64.9 6.2 %shard_map.100.refs_1_ = bf16[128,2048]{1,0:T(8,128)(2,1)S(1)} custom-call(s32[3]{0:T(128)S(1)} %pad_add_fusion.scalars, bf16[2,2,2,32,2048]{4,3,2,1,0:T(8,128)(2,1)S(1)} %bitcast.31, bf16[2,256,512]{2,1,0:T(8,128)(2,1)S(1)} %bitcast.29, bf16[2,256,512]{2,1,0:T(8,128)(2,1)S(1)} %copy-done.5, bf16[2,256,512]{2,1,0:T(8,128)(2,1)S(1)} %collective-permute-done.4.refs_2_, ...), custom_call_target="tpu_custom_call" | custom-call | flops 1 | bytes 1 | tf_op jit(solution)/shard_map/pallas_call | solution.py:178
  72.5 3.4 %copy-done.1 = bf16[2048,2048]{1,0:T(8,128)(2,1)S(1)} copy-done((bf16[2048,2048]{1,0:T(8,128)(2,1)S(1)}, bf16[2048,2048]{1,0:T(8,128)(2,1)}, u32[]{:S(2)}) %copy-start.1) | copy-done | bytes 8388632
  75.8 3.7 %shard_map.102 = (f32[64,2048]{1,0:T(8,128)S(1)}, bf16[64,2048]{1,0:T(8,128)(2,1)S(1)}, bf16[64,2048]{1,0:T(8,128)(2,1)S(1)}, bf16[64,2048]{1,0:T(8,128)(2,1)S(1)}) custom-call(s32[1]{0:T(128)} %bitcast.6.share, bf16[128,2048]{1,0:T(8,128)(2,1)S(1)} %shard_map.101.refs_0_, bf16[128,2048]{1,0:T(8,128)(2,1)S(1)} %shard_map.100.refs_1_, ...), custom_call_target="tpu_custom_call" | custom-call | flops 1 | bytes 1 | tf_op jit(solution)/shard_map/pallas_call | solution.py:61
  79.5 3.8 %collective-permute-done.9.refs_0_ = bf16[128,2048]{1,0:T(8,128)(2,1)} collective-permute-done((bf16[128,2048]{1,0:T(8,128)(2,1)S(1)}, bf16[128,2048]{1,0:T(8,128)(2,1)}, u32[]{:S(2)}, u32[]{:S(2)}) %collective-permute-start.9) | collective-permute-done | bytes 524320 | tf_op jit(solution)/shard_map/ppermute | solution.py:28
  83.3 4.7 %shard_map.103 = (f32[64,2048]{1,0:T(8,128)S(1)}, bf16[64,2048]{1,0:T(8,128)(2,1)S(1)}, bf16[64,2048]{1,0:T(8,128)(2,1)S(1)}, bf16[64,2048]{1,0:T(8,128)(2,1)S(1)}) custom-call(s32[1]{0:T(128)} %bitcast.6.share, bf16[128,2048]{1,0:T(8,128)(2,1)} %collective-permute-done.9.refs_0_, bf16[128,2048]{1,0:T(8,128)(2,1)} %collective-permute-done.8.refs_1_, ...), custom_call_target="tpu_custom_call" | custom-call | flops 1 | bytes 1 | tf_op jit(solution)/shard_map/pallas_call | solution.py:61
  92.0 5.3 %collective-permute-done.14 = bf16[64,2048]{1,0:T(8,128)(2,1)S(1)} collective-permute-done((bf16[64,2048]{1,0:T(8,128)(2,1)S(1)}, bf16[64,2048]{1,0:T(8,128)(2,1)S(1)}, u32[]{:S(2)}, u32[]{:S(2)}) %collective-permute-start.14) | collective-permute-done | bytes 262176 | tf_op jit(solution)/shard_map/ppermute | solution.py:28
  97.8 4.2 %collective-permute-done.15 = bf16[64,2048]{1,0:T(8,128)(2,1)S(1)} collective-permute-done((bf16[64,2048]{1,0:T(8,128)(2,1)S(1)}, bf16[64,2048]{1,0:T(8,128)(2,1)S(1)}, u32[]{:S(2)}, u32[]{:S(2)}) %collective-permute-start.15) | collective-permute-done | bytes 262176 | tf_op jit(solution)/shard_map/ppermute | solution.py:28
  103.7 7.2 %collective-permute-done.12 = bf16[64,2048]{1,0:T(8,128)(2,1)S(1)} collective-permute-done((bf16[64,2048]{1,0:T(8,128)(2,1)S(1)}, bf16[64,2048]{1,0:T(8,128)(2,1)S(1)}, u32[]{:S(2)}, u32[]{:S(2)}) %collective-permute-start.12) | collective-permute-done | bytes 262176 | tf_op jit(solution)/shard_map/ppermute | solution.py:28
  111.0 3.7 %shard_map.104 = (f32[64,2048]{1,0:T(8,128)S(1)}, bf16[64,2048]{1,0:T(8,128)(2,1)S(1)}, bf16[64,2048]{1,0:T(8,128)(2,1)S(1)}, bf16[64,2048]{1,0:T(8,128)(2,1)S(1)}) custom-call(s32[1]{0:T(128)} %bitcast.6.share, bf16[128,2048]{1,0:T(8,128)(2,1)S(1)} %collective-permute-done.7.refs_0_, bf16[128,2048]{1,0:T(8,128)(2,1)S(1)} %collective-permute-done.6.refs_1_, ...), custom_call_target="tpu_custom_call" | custom-call | flops 1 | bytes 1 | tf_op jit(solution)/shard_map/pallas_call | solution.py:61
  118.8 5.1 %collective-permute-done.18 = bf16[64,2048]{1,0:T(8,128)(2,1)S(1)} collective-permute-done((bf16[64,2048]{1,0:T(8,128)(2,1)S(1)}, bf16[64,2048]{1,0:T(8,128)(2,1)S(1)}, u32[]{:S(2)}, u32[]{:S(2)}) %collective-permute-start.18) | collective-permute-done | bytes 262176 | tf_op jit(solution)/shard_map/ppermute | solution.py:28
  124.4 4.2 %collective-permute-done.19 = bf16[64,2048]{1,0:T(8,128)(2,1)S(1)} collective-permute-done((bf16[64,2048]{1,0:T(8,128)(2,1)S(1)}, bf16[64,2048]{1,0:T(8,128)(2,1)S(1)}, u32[]{:S(2)}, u32[]{:S(2)}) %collective-permute-start.19) | collective-permute-done | bytes 262176 | tf_op jit(solution)/shard_map/ppermute | solution.py:28
  128.8 2.7 %shard_map.105 = (f32[32,2048]{1,0:T(8,128)S(1)}, bf16[32,2048]{1,0:T(8,128)(2,1)S(1)}, bf16[32,2048]{1,0:T(8,128)(2,1)S(1)}, bf16[32,2048]{1,0:T(8,128)(2,1)S(1)}) custom-call(s32[1]{0:T(128)} %bitcast.6.share, bf16[128,2048]{1,0:T(8,128)(2,1)S(1)} %collective-permute-done.16.refs_0_, bf16[2048,2048]{1,0:T(8,128)(2,1)S(1)} %copy-done.2), custom_call_target="tpu_custom_call" | custom-call | flops 1 | bytes 1 | tf_op jit(solution)/shard_map/pallas_call | solution.py:61
  135.8 2.7 %collective-permute-done.24 = bf16[32,2048]{1,0:T(8,128)(2,1)S(1)} collective-permute-done((bf16[32,2048]{1,0:T(8,128)(2,1)S(1)}, bf16[32,2048]{1,0:T(8,128)(2,1)S(1)}, u32[]{:S(2)}, u32[]{:S(2)}) %collective-permute-start.24) | collective-permute-done | bytes 131104 | tf_op jit(solution)/shard_map/ppermute | solution.py:28
  139.8 3.8 %collective-permute-done.27 = bf16[32,2048]{1,0:T(8,128)(2,1)S(1)} collective-permute-done((bf16[32,2048]{1,0:T(8,128)(2,1)S(1)}, bf16[32,2048]{1,0:T(8,128)(2,1)S(1)}, u32[]{:S(2)}, u32[]{:S(2)}) %collective-permute-start.27) | collective-permute-done | bytes 131104 | tf_op jit(solution)/shard_map/ppermute | solution.py:28
  148.9 3.7 %collective-permute-done.30 = bf16[32,2048]{1,0:T(8,128)(2,1)S(1)} collective-permute-done((bf16[32,2048]{1,0:T(8,128)(2,1)S(1)}, bf16[32,2048]{1,0:T(8,128)(2,1)S(1)}, u32[]{:S(2)}, u32[]{:S(2)}) %collective-permute-start.30) | collective-permute-done | bytes 131104 | tf_op jit(solution)/shard_map/ppermute | solution.py:28
  154.6 3.1 %collective-permute-done.28 = bf16[32,2048]{1,0:T(8,128)(2,1)S(1)} collective-permute-done((bf16[32,2048]{1,0:T(8,128)(2,1)S(1)}, bf16[32,2048]{1,0:T(8,128)(2,1)S(1)}, u32[]{:S(2)}, u32[]{:S(2)}) %collective-permute-start.28) | collective-permute-done | bytes 131104 | tf_op jit(solution)/shard_map/ppermute | solution.py:28
  157.9 7.7 %collective-permute-done.32 = bf16[32,2048]{1,0:T(8,128)(2,1)S(1)} collective-permute-done((bf16[32,2048]{1,0:T(8,128)(2,1)S(1)}, bf16[32,2048]{1,0:T(8,128)(2,1)S(1)}, u32[]{:S(2)}, u32[]{:S(2)}) %collective-permute-start.32) | collective-permute-done | bytes 131104 | tf_op jit(solution)/shard_map/ppermute | solution.py:28
  (122 shorter events, 44.7 us)
Async XLA Ops:
  7.3 14.5 %collective-permute-start = (bf16[8,32,512]{2,1,0:T(8,128)(2,1)}, bf16[8,32,512]{2,1,0:T(8,128)(2,1)S(1)}, u32[]{:S(2)}, u32[]{:S(2)}) collective-permute-start(bf16[8,32,512]{2,1,0:T(8,128)(2,1)} %get-tuple-element.93), channel_id=1, source_target_pairs={{0,4},{4,0},{8,12},{12,8},{1,5},{5,1},{9,13},{13,9},{2,6},{6,2},{1... | collective-permute-start | bytes 786440 | tf_op jit(solution)/shard_map/ppermute | solution.py:28
  10.3 21.4 %collective-permute-start.1 = (bf16[8,32,512]{2,1,0:T(8,128)(2,1)S(1)}, bf16[8,32,512]{2,1,0:T(8,128)(2,1)S(1)}, u32[]{:S(2)}, u32[]{:S(2)}) collective-permute-start(bf16[8,32,512]{2,1,0:T(8,128)(2,1)S(1)} %get-tuple-element.92), channel_id=1, source_target_pairs={{0,8},{4,12},{8,0},{12,4},{1,9},{5,13},{9,1},{13,5},{2,10},{6,14},... | collective-permute-start | bytes 786440 | tf_op jit(solution)/shard_map/ppermute | solution.py:28
  12.9 18.8 %collective-permute-start.2 = (bf16[8,32,512]{2,1,0:T(8,128)(2,1)S(1)}, bf16[8,32,512]{2,1,0:T(8,128)(2,1)}, u32[]{:S(2)}, u32[]{:S(2)}) collective-permute-start(bf16[8,32,512]{2,1,0:T(8,128)(2,1)S(1)} %get-tuple-element.94), channel_id=1, source_target_pairs={{0,12},{4,8},{8,4},{12,0},{1,13},{5,9},{9,5},{13,1},{2,14},{6,10},... | collective-permute-start | bytes 786440 | tf_op jit(solution)/shard_map/ppermute | solution.py:28
  35.6 11.6 %collective-permute-start.4 = (bf16[2,256,512]{2,1,0:T(8,128)(2,1)S(1)}, bf16[2,256,512]{2,1,0:T(8,128)(2,1)S(1)}, u32[]{:S(2)}, u32[]{:S(2)}) collective-permute-start(bf16[2,256,512]{2,1,0:T(8,128)(2,1)S(1)} %bitcast.26), channel_id=1, source_target_pairs={{0,2},{2,0},{1,3},{3,1},{4,6},{6,4},{5,7},{7,5},{8,10},{10,8},{9,1... | collective-permute-start | bytes 1572872 | tf_op jit(solution)/shard_map/ppermute | solution.py:28
  37.1 10.0 %collective-permute-start.3 = (bf16[2,256,512]{2,1,0:T(8,128)(2,1)S(1)}, bf16[2,256,512]{2,1,0:T(8,128)(2,1)S(1)}, u32[]{:S(2)}, u32[]{:S(2)}) collective-permute-start(bf16[2,256,512]{2,1,0:T(8,128)(2,1)S(1)} %bitcast.27), channel_id=1, source_target_pairs={{0,1},{1,0},{2,3},{3,2},{4,5},{5,4},{6,7},{7,6},{8,9},{9,8},{10,11... | collective-permute-start | bytes 1572872 | tf_op jit(solution)/shard_map/ppermute | solution.py:28
  55.3 24.3 %collective-permute-start.8 = (bf16[128,2048]{1,0:T(8,128)(2,1)S(1)}, bf16[128,2048]{1,0:T(8,128)(2,1)}, u32[]{:S(2)}, u32[]{:S(2)}) collective-permute-start(bf16[128,2048]{1,0:T(8,128)(2,1)S(1)} %shard_map.101.refs_0_), channel_id=1, source_target_pairs={{0,12},{4,8},{8,4},{12,0},{1,13},{5,9},{9,5},{13,1},{2,14},{6,10},... | collective-permute-start | bytes 1572872 | tf_op jit(solution)/shard_map/ppermute | solution.py:28
  56.7 26.7 %collective-permute-start.9 = (bf16[128,2048]{1,0:T(8,128)(2,1)S(1)}, bf16[128,2048]{1,0:T(8,128)(2,1)}, u32[]{:S(2)}, u32[]{:S(2)}) collective-permute-start(bf16[128,2048]{1,0:T(8,128)(2,1)S(1)} %shard_map.101.refs_0_), channel_id=1, source_target_pairs={{0,4},{4,0},{8,12},{12,8},{1,5},{5,1},{9,13},{13,9},{2,6},{6,2},{1... | collective-permute-start | bytes 1572872 | tf_op jit(solution)/shard_map/ppermute | solution.py:28
  71.0 39.9 %collective-permute-start.6 = (bf16[128,2048]{1,0:T(8,128)(2,1)S(1)}, bf16[128,2048]{1,0:T(8,128)(2,1)S(1)}, u32[]{:S(2)}, u32[]{:S(2)}) collective-permute-start(bf16[128,2048]{1,0:T(8,128)(2,1)S(1)} %shard_map.100.refs_1_), channel_id=1, source_target_pairs={{0,12},{4,8},{8,4},{12,0},{1,13},{5,9},{9,5},{13,1},{2,14},{6,10},... | collective-permute-start | bytes 1572872 | tf_op jit(solution)/shard_map/ppermute | solution.py:28
  72.5 38.5 %collective-permute-start.7 = (bf16[128,2048]{1,0:T(8,128)(2,1)S(1)}, bf16[128,2048]{1,0:T(8,128)(2,1)S(1)}, u32[]{:S(2)}, u32[]{:S(2)}) collective-permute-start(bf16[128,2048]{1,0:T(8,128)(2,1)S(1)} %shard_map.100.refs_1_), channel_id=1, source_target_pairs={{0,4},{4,0},{8,12},{12,8},{1,5},{5,1},{9,13},{13,9},{2,6},{6,2},{1... | collective-permute-start | bytes 1572872 | tf_op jit(solution)/shard_map/ppermute | solution.py:28
  88.1 9.2 %collective-permute-start.14 = (bf16[64,2048]{1,0:T(8,128)(2,1)S(1)}, bf16[64,2048]{1,0:T(8,128)(2,1)S(1)}, u32[]{:S(2)}, u32[]{:S(2)}) collective-permute-start(bf16[64,2048]{1,0:T(8,128)(2,1)S(1)} %get-tuple-element.63), channel_id=1, source_target_pairs={{0,2},{1,3},{2,0},{3,1},{4,6},{5,7},{6,4},{7,5},{8,10},{9,11},{10,... | collective-permute-start | bytes 786440 | tf_op jit(solution)/shard_map/ppermute | solution.py:28
  91.2 10.8 %collective-permute-start.15 = (bf16[64,2048]{1,0:T(8,128)(2,1)S(1)}, bf16[64,2048]{1,0:T(8,128)(2,1)S(1)}, u32[]{:S(2)}, u32[]{:S(2)}) collective-permute-start(bf16[64,2048]{1,0:T(8,128)(2,1)S(1)} %get-tuple-element.64), channel_id=1, source_target_pairs={{0,3},{1,2},{2,1},{3,0},{4,7},{5,6},{6,5},{7,4},{8,11},{9,10},{10,... | collective-permute-start | bytes 786440 | tf_op jit(solution)/shard_map/ppermute | solution.py:28
  91.6 12.0 %collective-permute-start.10 = (bf16[64,2048]{1,0:T(8,128)(2,1)S(1)}, bf16[64,2048]{1,0:T(8,128)(2,1)S(1)}, u32[]{:S(2)}, u32[]{:S(2)}) collective-permute-start(bf16[64,2048]{1,0:T(8,128)(2,1)S(1)} %get-tuple-element.56), channel_id=1, source_target_pairs={{0,1},{1,0},{2,3},{3,2},{4,5},{5,4},{6,7},{7,6},{8,9},{9,8},{10,11... | collective-permute-start | bytes 786440 | tf_op jit(solution)/shard_map/ppermute | solution.py:28
  97.3 31.4 %collective-permute-start.16 = (bf16[128,2048]{1,0:T(8,128)(2,1)S(1)}, bf16[128,2048]{1,0:T(8,128)(2,1)S(1)}, u32[]{:S(2)}, u32[]{:S(2)}) collective-permute-start(bf16[128,2048]{1,0:T(8,128)(2,1)S(1)} %broadcast_select_fusion.1), channel_id=1, source_target_pairs={{0,8},{12,4},{4,0},{8,12},{1,9},{13,5},{5,1},{9,13},{2,10},{14,6},... | collective-permute-start | bytes 1572872 | tf_op jit(solution)/shard_map/ppermute | solution.py:35
  102.0 8.8 %collective-permute-start.12 = (bf16[64,2048]{1,0:T(8,128)(2,1)S(1)}, bf16[64,2048]{1,0:T(8,128)(2,1)S(1)}, u32[]{:S(2)}, u32[]{:S(2)}) collective-permute-start(bf16[64,2048]{1,0:T(8,128)(2,1)S(1)} %add_convert_fusion.3), channel_id=1, source_target_pairs={{0,2},{2,0},{1,3},{3,1},{4,6},{6,4},{5,7},{7,5},{8,10},{10,8},{9,1... | collective-permute-start | bytes 786440 | tf_op jit(solution)/shard_map/ppermute | solution.py:28
  114.8 9.2 %collective-permute-start.18 = (bf16[64,2048]{1,0:T(8,128)(2,1)S(1)}, bf16[64,2048]{1,0:T(8,128)(2,1)S(1)}, u32[]{:S(2)}, u32[]{:S(2)}) collective-permute-start(bf16[64,2048]{1,0:T(8,128)(2,1)S(1)} %get-tuple-element.70), channel_id=1, source_target_pairs={{0,2},{1,3},{2,0},{3,1},{4,6},{5,7},{6,4},{7,5},{8,10},{9,11},{10,... | collective-permute-start | bytes 786440 | tf_op jit(solution)/shard_map/ppermute | solution.py:28
  116.3 12.3 %collective-permute-start.19 = (bf16[64,2048]{1,0:T(8,128)(2,1)S(1)}, bf16[64,2048]{1,0:T(8,128)(2,1)S(1)}, u32[]{:S(2)}, u32[]{:S(2)}) collective-permute-start(bf16[64,2048]{1,0:T(8,128)(2,1)S(1)} %get-tuple-element.71), channel_id=1, source_target_pairs={{0,3},{1,2},{2,1},{3,0},{4,7},{5,6},{6,5},{7,4},{8,11},{9,10},{10,... | collective-permute-start | bytes 786440 | tf_op jit(solution)/shard_map/ppermute | solution.py:28
  116.6 12.1 %collective-permute-start.20 = (bf16[32,2048]{1,0:T(8,128)(2,1)S(1)}, bf16[32,2048]{1,0:T(8,128)(2,1)S(1)}, u32[]{:S(2)}, u32[]{:S(2)}) collective-permute-start(bf16[32,2048]{1,0:T(8,128)(2,1)S(1)} %get-tuple-element.98), channel_id=1, source_target_pairs={{0,4},{4,0},{8,12},{12,8},{1,5},{5,1},{9,13},{13,9},{2,6},{6,2},{1... | collective-permute-start | bytes 393224 | tf_op jit(solution)/shard_map/ppermute | solution.py:28
  117.4 11.4 %collective-permute-start.21 = (bf16[32,2048]{1,0:T(8,128)(2,1)S(1)}, bf16[32,2048]{1,0:T(8,128)(2,1)S(1)}, u32[]{:S(2)}, u32[]{:S(2)}) collective-permute-start(bf16[32,2048]{1,0:T(8,128)(2,1)S(1)} %get-tuple-element.97), channel_id=1, source_target_pairs={{0,12},{4,8},{8,4},{12,0},{1,13},{5,9},{9,5},{13,1},{2,14},{6,10},... | collective-permute-start | bytes 393224 | tf_op jit(solution)/shard_map/ppermute | solution.py:28
  123.9 19.7 %collective-permute-start.22 = (bf16[128,2048]{1,0:T(8,128)(2,1)S(1)}, bf16[128,2048]{1,0:T(8,128)(2,1)S(1)}, u32[]{:S(2)}, u32[]{:S(2)}) collective-permute-start(bf16[128,2048]{1,0:T(8,128)(2,1)S(1)} %broadcast_select_fusion), channel_id=1, source_target_pairs={{0,8},{12,4},{4,0},{8,12},{1,9},{13,5},{5,1},{9,13},{2,10},{14,6},... | collective-permute-start | bytes 1572872 | tf_op jit(solution)/shard_map/ppermute | solution.py:35
  134.3 9.3 %collective-permute-start.27 = (bf16[32,2048]{1,0:T(8,128)(2,1)S(1)}, bf16[32,2048]{1,0:T(8,128)(2,1)S(1)}, u32[]{:S(2)}, u32[]{:S(2)}) collective-permute-start(bf16[32,2048]{1,0:T(8,128)(2,1)S(1)} %get-tuple-element.95), channel_id=1, source_target_pairs={{0,12},{4,8},{8,4},{12,0},{1,13},{5,9},{9,5},{13,1},{2,14},{6,10},... | collective-permute-start | bytes 393224 | tf_op jit(solution)/shard_map/ppermute | solution.py:28
  146.3 6.4 %collective-permute-start.30 = (bf16[32,2048]{1,0:T(8,128)(2,1)S(1)}, bf16[32,2048]{1,0:T(8,128)(2,1)S(1)}, u32[]{:S(2)}, u32[]{:S(2)}) collective-permute-start(bf16[32,2048]{1,0:T(8,128)(2,1)S(1)} %get-tuple-element.85), channel_id=1, source_target_pairs={{0,2},{1,3},{2,0},{3,1},{4,6},{5,7},{6,4},{7,5},{8,10},{9,11},{10,... | collective-permute-start | bytes 393224 | tf_op jit(solution)/shard_map/ppermute | solution.py:28
  147.9 6.7 %collective-permute-start.31 = (bf16[32,2048]{1,0:T(8,128)(2,1)S(1)}, bf16[32,2048]{1,0:T(8,128)(2,1)S(1)}, u32[]{:S(2)}, u32[]{:S(2)}) collective-permute-start(bf16[32,2048]{1,0:T(8,128)(2,1)S(1)} %get-tuple-element.86), channel_id=1, source_target_pairs={{0,3},{1,2},{2,1},{3,0},{4,7},{5,6},{6,5},{7,4},{8,11},{9,10},{10,... | collective-permute-start | bytes 393224 | tf_op jit(solution)/shard_map/ppermute | solution.py:28
  148.2 9.5 %collective-permute-start.28 = (bf16[32,2048]{1,0:T(8,128)(2,1)S(1)}, bf16[32,2048]{1,0:T(8,128)(2,1)S(1)}, u32[]{:S(2)}, u32[]{:S(2)}) collective-permute-start(bf16[32,2048]{1,0:T(8,128)(2,1)S(1)} %add_convert_fusion.5), channel_id=1, source_target_pairs={{0,8},{4,12},{8,0},{12,4},{1,9},{5,13},{9,1},{13,5},{2,10},{6,14},... | collective-permute-start | bytes 393224 | tf_op jit(solution)/shard_map/ppermute | solution.py:28
  157.7 7.8 %collective-permute-start.32 = (bf16[32,2048]{1,0:T(8,128)(2,1)S(1)}, bf16[32,2048]{1,0:T(8,128)(2,1)S(1)}, u32[]{:S(2)}, u32[]{:S(2)}) collective-permute-start(bf16[32,2048]{1,0:T(8,128)(2,1)S(1)} %add_convert_fusion.4), channel_id=1, source_target_pairs={{0,8},{4,12},{8,0},{12,4},{1,9},{5,13},{9,1},{13,5},{2,10},{6,14},... | collective-permute-start | bytes 393224 | tf_op jit(solution)/shard_map/ppermute | solution.py:28
  (23 other events, 237.4 us)

commit v9 on v8

--- a/solution.py
+++ b/solution.py
@@ -35,17 +35,21 @@
     return lax.ppermute(passed, "pool", [(0, 2), (3, 1), (1, 0), (2, 3)])
 
 
-def project_kernel(block_count, share_count, share, *refs):
-    blocks, weight, outs = refs[:block_count], refs[block_count], refs[block_count + 1 :]
-    part_rows = blocks[0].shape[0] // share_count
+def project_kernel(widths, share_count, share, *refs):
+    count = sum(widths)
+    parts, weight, outs = list(refs[:count]), refs[count], refs[count + 1 :]
+    part_rows = parts[0].shape[0] // share_count
+    blocks = [[parts.pop(0) for _ in range(width)] for width in widths]
     picked = []
     for flip in range(share_count):
         start = pl.multiple_of((share[0] ^ flip) * part_rows, part_rows)
-        picked += [block[pl.ds(start, part_rows), :] for block in blocks]
+        for block in blocks:
+            pieces = [part[pl.ds(start, part_rows), :] for part in block]
+            picked.append(jnp.concatenate(pieces, axis=1) if len(pieces) > 1 else pieces[0])
     product = jnp.dot(
         jnp.concatenate(picked, axis=0), weight[...], preferred_element_type=jnp.float32
     )
-    rows = block_count * part_rows
+    rows = len(blocks) * part_rows
     for flip in range(share_count):
         outs[flip][...] = product[flip * rows : (flip + 1) * rows].astype(outs[flip].dtype)
 
@@ -55,14 +59,15 @@
     share_count = lax.axis_size(axes)
     share = lax.axis_index(axes).astype(jnp.int32).reshape(1)
     depth, columns = out_weight.shape
-    rows = sum(block.shape[0] for block in blocks) // share_count
+    parts = [part for block in blocks for part in block]
+    rows = len(blocks) * parts[0].shape[0] // share_count
     tile = min(columns, 512)
     whole = pl.BlockSpec(memory_space=pltpu.VMEM)
     return pl.pallas_call(
-        functools.partial(project_kernel, len(blocks), share_count),
+        functools.partial(project_kernel, [len(block) for block in blocks], share_count),
         grid=(columns // tile,),
         in_specs=[pl.BlockSpec(memory_space=pltpu.SMEM)]
-        + [whole for _ in blocks]
+        + [whole for _ in parts]
         + [pl.BlockSpec((depth, tile), lambda n: (0, n))],
         out_specs=[pl.BlockSpec((rows, tile), lambda n: (0, n))] * share_count,
         out_shape=[
@@ -71,7 +76,7 @@
         ],
         compiler_params=pltpu.CompilerParams(vmem_limit_bytes=32 * 1024 * 1024),
         cost_estimate=LIGHT,
-    )(share, *blocks, out_weight)
+    )(share, *parts, out_weight)
 
 
 def sum_shares(pieces):
@@ -249,7 +254,7 @@
         outputs = []
         for chunk in range(CHUNKS):
             rows = lax.all_gather(attended(chunk), "pool", axis=0)
-            mine = sum_shares(project_out([rows[i] for i in range(pool_size)], out_weight))
+            mine = sum_shares(project_out([[rows[i]] for i in range(pool_size)], out_weight))
             mine = mine.reshape(pool_size, -1, columns)
             back = lax.all_to_all(mine, "pool", split_axis=0, concat_axis=0, tiled=True)
             outputs.append(jnp.moveaxis(back, 0, 1).reshape(-1, pool_size * columns))
@@ -259,34 +264,34 @@
     across0, beside0 = swap(first, "pool", 3), swap(first, "pool", 1)
     last = attended(1)
     across1, beside1 = swap(last, "pool", 3), swap(last, "pool", 1)
-    own = project_out([first, last], out_weight)
+    own = project_out([[first], [last]], out_weight)
     across0, beside0, own = tie((across0, beside0, own))
     second0 = second_hop(first, across0)
-    own = sum_in_turn(own)
-    near0 = sum_shares(project_out([beside0, across0], out_weight))
-    across1, beside1, own, near0 = tie((across1, beside1, own, near0))
-    second1 = second_hop(last, across1)
+    near0 = sum_shares(project_out([[beside0], [across0]], out_weight))
+    across1, beside1, near0 = tie((across1, beside1, near0))
+    width = last.shape[1] // 2
+    second1 = [
+        second_hop(last[:, i : i + width], across1[:, i : i + width]) for i in (0, width)
+    ]
     half = near0.shape[0] // 2
     back0 = swap(near0[:half], "pool", 1), swap(near0[half:], "pool", 3)
-    near1 = sum_shares(project_out([beside1, across1], out_weight))
-    second0, near1, back0 = tie((second0, near1, back0))
+    near1 = sum_shares(project_out([[beside1], [across1]], out_weight))
+    second0, second1[0], near1, back0 = tie((second0, second1[0], near1, back0))
     back1 = swap(near1[:half], "pool", 1), swap(near1[half:], "pool", 3)
-    far0 = sum_shares(project_out([second0], out_weight))
+    far0 = sum_shares(project_out([[second0]], out_weight))
     second1, far0, back1 = tie((second1, far0, back1))
     back_second0 = swap(far0, "pool", 2)
     far1 = sum_shares(project_out([second1], out_weight))
     back_second0, far1 = tie((back_second0, far1))
     back_second1 = swap(far1, "pool", 2)
-    backs = [
-        [own[:half], back0[0], back_second0, back0[1]],
-        [own[half:], back1[0], back_second1, back1[1]],
-    ]
+    own = sum_in_turn(own)
+    backs = [(0, 1, back0[0]), (0, 3, back0[1]), (1, 1, back1[0]), (1, 3, back1[1])]
+    backs += [(0, 2, back_second0), (0, 0, own), (1, 2, back_second1)]
     output = jnp.zeros((part_rows, pool_size * columns), jnp.bfloat16)
-    for chunk in range(CHUNKS):
-        for flip in (0, 1, 3, 2):
-            output = lax.dynamic_update_slice(
-                output, backs[chunk][flip], (chunk * half, (pool_index ^ flip) * columns)
-            )
+    for chunk, flip, block in backs:
+        output = lax.dynamic_update_slice(
+            output, block, (chunk * half, (pool_index ^ flip) * columns)
+        )
     return output
 
 

time: 167 us -> 173 us (1.036)
  waiting for transfers between devices: 85.1 us -> 92.5 us
    ppermute x31, waiting for transfers between devices: 85.1 us -> 92.5 us  [swap(): lax.ppermute(values, axis, [(i, i ^ flip) for i in range(lax.axis_size(ax...]
    ppermute x31, starting transfers between devices: 31.1 us -> 28.8 us  [swap(): lax.ppermute(values, axis, [(i, i ^ flip) for i in range(lax.axis_size(ax...]
  transfers between devices with their start and end apart: 33 -> 34, of which waited for: 19 -> 19; matrix products, arithmetic and copies ran while one was open for 1% -> 1% of each run, Pallas kernels for 13% -> 14%
where the time goes in v9:
time: 173 us
  waiting for transfers between devices  92.5 us (53%)
  starting transfers between devices  31.5 us (18%)
  Pallas kernels  29.7 us (17%)
  local copies, waits for them, and re-layouts  13.7 us (8%)
  other arithmetic  3.17 us (2%)
  matrix products  1.94 us (1%)
    ppermute x31, waiting for transfers between devices, swap(): lax.ppermute(values, axis, [(i, i ^ flip) for i in range(lax.axis_size(ax...  92.5 us
    ppermute x31, starting transfers between devices, swap(): lax.ppermute(values, axis, [(i, i ^ flip) for i in range(lax.axis_size(ax...  28.8 us
    pallas_call x5, Pallas kernels, project_out(): pl.pallas_call(functools.partial(project_kernel, [len(block) for block in...  17.4 us
    pallas_call x2, Pallas kernels, attend(): pl.pallas_call(functools.partial(attend_kernel, len(parts)), grid=(reques...  12.4 us
    unnamed x28, local copies, waits for them, and re-layouts  6.17 us
  transfers between devices with their start and end apart: 34, of which 19 were waited for; matrix products, arithmetic and copies ran while one was open for 1% of the time, Pallas kernels for 14%

profile of v9, /device:TPU:0, one launch (start us, length us, event | category | flops | bytes accessed | tf_op | source)
XLA Modules:
  0.0 173.0 jit_solution(15777533867210481932)
XLA Ops:
  3.7 2.8 %gather_fusion.1 = bf16[32,32,512]{2,1,0:T(8,128)(2,1)S(1)} fusion(bf16[128,32,512]{2,1,0:T(8,128)(2,1)} %bitcast.36, s32[1024]{0:T(1024)S(1)} %pad_clamp_fusion.1), kind=kCustom, calls=%fused_computation.1 | custom fusion | bytes 2097280 | tf_op jit(solution)/shard_map/gather | solution.py:128
  7.3 3.0 %collective-permute-start = (bf16[8,32,512]{2,1,0:T(8,128)(2,1)}, bf16[8,32,512]{2,1,0:T(8,128)(2,1)S(1)}, u32[]{:S(2)}, u32[]{:S(2)}) collective-permute-start(bf16[8,32,512]{2,1,0:T(8,128)(2,1)} %get-tuple-element.97), channel_id=1, source_target_pairs={{0,4},{4,0},{8,12},{12,8},{1,5},{5,1},{9,13},{13,9},{2,6},{6,2},{1... | collective-permute-start | bytes 786440 | tf_op jit(solution)/shard_map/ppermute | solution.py:28
  13.7 8.1 %collective-permute-done = bf16[8,32,512]{2,1,0:T(8,128)(2,1)S(1)} collective-permute-done((bf16[8,32,512]{2,1,0:T(8,128)(2,1)}, bf16[8,32,512]{2,1,0:T(8,128)(2,1)S(1)}, u32[]{:S(2)}, u32[]{:S(2)}) %collective-permute-start) | collective-permute-done | bytes 262176 | tf_op jit(solution)/shard_map/ppermute | solution.py:28
  21.8 9.9 %collective-permute-done.1 = bf16[8,32,512]{2,1,0:T(8,128)(2,1)S(1)} collective-permute-done((bf16[8,32,512]{2,1,0:T(8,128)(2,1)S(1)}, bf16[8,32,512]{2,1,0:T(8,128)(2,1)S(1)}, u32[]{:S(2)}, u32[]{:S(2)}) %collective-permute-start.1) | collective-permute-done | bytes 262176 | tf_op jit(solution)/shard_map/ppermute | solution.py:28
  37.1 10.0 %collective-permute-done.4.refs_2_ = bf16[2,256,512]{2,1,0:T(8,128)(2,1)S(1)} collective-permute-done((bf16[2,256,512]{2,1,0:T(8,128)(2,1)S(1)}, bf16[2,256,512]{2,1,0:T(8,128)(2,1)S(1)}, u32[]{:S(2)}, u32[]{:S(2)}) %collective-permute-start.4) | collective-permute-done | bytes 524320 | tf_op jit(solution)/shard_map/ppermute | solution.py:28
  49.1 6.2 %shard_map.100.refs_0_ = bf16[128,2048]{1,0:T(8,128)(2,1)S(1)} custom-call(s32[3]{0:T(128)S(1)} %pad_add_fusion.scalars, bf16[2,2,2,32,2048]{4,3,2,1,0:T(8,128)(2,1)S(1)} %bitcast.30, bf16[2,256,512]{2,1,0:T(8,128)(2,1)S(1)} %bitcast.28, bf16[2,256,512]{2,1,0:T(8,128)(2,1)S(1)} %collective-permute-done.3.refs_1_, ...), custom_call_target="tpu_custom_call" | custom-call | flops 1 | bytes 1 | tf_op jit(solution)/shard_map/pallas_call | solution.py:183
  56.7 6.1 %collective-permute-start.7 = (bf16[128,2048]{1,0:T(8,128)(2,1)S(1)}, bf16[128,2048]{1,0:T(8,128)(2,1)}, u32[]{:S(2)}, u32[]{:S(2)}) collective-permute-start(bf16[128,2048]{1,0:T(8,128)(2,1)S(1)} %shard_map.100.refs_0_), channel_id=1, source_target_pairs={{0,4},{4,0},{8,12},{12,8},{1,5},{5,1},{9,13},{13,9},{2,6},{6,2},{1... | collective-permute-start | bytes 1572872 | tf_op jit(solution)/shard_map/ppermute | solution.py:28
  64.9 6.2 %shard_map.101.refs_1_ = bf16[128,2048]{1,0:T(8,128)(2,1)S(1)} custom-call(s32[3]{0:T(128)S(1)} %pad_add_fusion.scalars, bf16[2,2,2,32,2048]{4,3,2,1,0:T(8,128)(2,1)S(1)} %bitcast.31, bf16[2,256,512]{2,1,0:T(8,128)(2,1)S(1)} %bitcast.29, bf16[2,256,512]{2,1,0:T(8,128)(2,1)S(1)} %copy-done.5, bf16[2,256,512]{2,1,0:T(8,128)(2,1)S(1)} %collective-permute-done.4.refs_2_, ...), custom_call_target="tpu_custom_call" | custom-call | flops 1 | bytes 1 | tf_op jit(solution)/shard_map/pallas_call | solution.py:183
  72.5 3.4 %copy-done.1 = bf16[2048,2048]{1,0:T(8,128)(2,1)S(1)} copy-done((bf16[2048,2048]{1,0:T(8,128)(2,1)S(1)}, bf16[2048,2048]{1,0:T(8,128)(2,1)}, u32[]{:S(2)}) %copy-start.1) | copy-done | bytes 8388632
  75.9 3.7 %shard_map.102 = (f32[64,2048]{1,0:T(8,128)S(1)}, bf16[64,2048]{1,0:T(8,128)(2,1)S(1)}, bf16[64,2048]{1,0:T(8,128)(2,1)S(1)}, bf16[64,2048]{1,0:T(8,128)(2,1)S(1)}) custom-call(s32[1]{0:T(128)} %bitcast.6.share, bf16[128,2048]{1,0:T(8,128)(2,1)S(1)} %shard_map.100.refs_0_, bf16[128,2048]{1,0:T(8,128)(2,1)S(1)} %shard_map.101.refs_1_, ...), custom_call_target="tpu_custom_call" | custom-call | flops 1 | bytes 1 | tf_op jit(solution)/shard_map/pallas_call | solution.py:66
  79.6 2.9 %collective-permute-done.7.refs_0_ = bf16[128,2048]{1,0:T(8,128)(2,1)} collective-permute-done((bf16[128,2048]{1,0:T(8,128)(2,1)S(1)}, bf16[128,2048]{1,0:T(8,128)(2,1)}, u32[]{:S(2)}, u32[]{:S(2)}) %collective-permute-start.7) | collective-permute-done | bytes 524320 | tf_op jit(solution)/shard_map/ppermute | solution.py:28
  82.5 4.7 %shard_map.103 = (f32[64,2048]{1,0:T(8,128)S(1)}, bf16[64,2048]{1,0:T(8,128)(2,1)S(1)}, bf16[64,2048]{1,0:T(8,128)(2,1)S(1)}, bf16[64,2048]{1,0:T(8,128)(2,1)S(1)}) custom-call(s32[1]{0:T(128)} %bitcast.6.share, bf16[128,2048]{1,0:T(8,128)(2,1)} %collective-permute-done.7.refs_0_, bf16[128,2048]{1,0:T(8,128)(2,1)} %collective-permute-done.6.refs_1_, ...), custom_call_target="tpu_custom_call" | custom-call | flops 1 | bytes 1 | tf_op jit(solution)/shard_map/pallas_call | solution.py:66
  91.7 4.8 %collective-permute-done.12 = bf16[64,2048]{1,0:T(8,128)(2,1)S(1)} collective-permute-done((bf16[64,2048]{1,0:T(8,128)(2,1)S(1)}, bf16[64,2048]{1,0:T(8,128)(2,1)S(1)}, u32[]{:S(2)}, u32[]{:S(2)}) %collective-permute-start.12) | collective-permute-done | bytes 262176 | tf_op jit(solution)/shard_map/ppermute | solution.py:28
  96.5 4.7 %collective-permute-done.13 = bf16[64,2048]{1,0:T(8,128)(2,1)S(1)} collective-permute-done((bf16[64,2048]{1,0:T(8,128)(2,1)S(1)}, bf16[64,2048]{1,0:T(8,128)(2,1)S(1)}, u32[]{:S(2)}, u32[]{:S(2)}) %collective-permute-start.13) | collective-permute-done | bytes 262176 | tf_op jit(solution)/shard_map/ppermute | solution.py:28
  101.9 3.8 %collective-permute-done.9.refs_1_ = bf16[128,2048]{1,0:T(8,128)(2,1)S(1)} collective-permute-done((bf16[128,2048]{1,0:T(8,128)(2,1)S(1)}, bf16[128,2048]{1,0:T(8,128)(2,1)S(1)}, u32[]{:S(2)}, u32[]{:S(2)}) %collective-permute-start.9) | collective-permute-done | bytes 524320 | tf_op jit(solution)/shard_map/ppermute | solution.py:28
  105.7 3.7 %shard_map.104 = (f32[64,2048]{1,0:T(8,128)S(1)}, bf16[64,2048]{1,0:T(8,128)(2,1)S(1)}, bf16[64,2048]{1,0:T(8,128)(2,1)S(1)}, bf16[64,2048]{1,0:T(8,128)(2,1)S(1)}) custom-call(s32[1]{0:T(128)} %bitcast.6.share, bf16[128,2048]{1,0:T(8,128)(2,1)S(1)} %collective-permute-done.10.refs_0_, bf16[128,2048]{1,0:T(8,128)(2,1)S(1)} %collective-permute-done.9.refs_1_, ...), custom_call_target="tpu_custom_call" | custom-call | flops 1 | bytes 1 | tf_op jit(solution)/shard_map/pallas_call | solution.py:66
  111.6 7.1 %collective-permute-done.16 = bf16[64,2048]{1,0:T(8,128)(2,1)S(1)} collective-permute-done((bf16[64,2048]{1,0:T(8,128)(2,1)S(1)}, bf16[64,2048]{1,0:T(8,128)(2,1)S(1)}, u32[]{:S(2)}, u32[]{:S(2)}) %collective-permute-start.16) | collective-permute-done | bytes 262176 | tf_op jit(solution)/shard_map/ppermute | solution.py:28
  118.6 4.7 %collective-permute-done.17 = bf16[64,2048]{1,0:T(8,128)(2,1)S(1)} collective-permute-done((bf16[64,2048]{1,0:T(8,128)(2,1)S(1)}, bf16[64,2048]{1,0:T(8,128)(2,1)S(1)}, u32[]{:S(2)}, u32[]{:S(2)}) %collective-permute-start.17) | collective-permute-done | bytes 262176 | tf_op jit(solution)/shard_map/ppermute | solution.py:28
  125.1 6.4 %collective-permute-done.19 = bf16[32,2048]{1,0:T(8,128)(2,1)S(1)} collective-permute-done((bf16[32,2048]{1,0:T(8,128)(2,1)S(1)}, bf16[32,2048]{1,0:T(8,128)(2,1)S(1)}, u32[]{:S(2)}, u32[]{:S(2)}) %collective-permute-start.19) | collective-permute-done | bytes 131104 | tf_op jit(solution)/shard_map/ppermute | solution.py:28
  131.5 2.7 %shard_map.105 = (f32[32,2048]{1,0:T(8,128)S(1)}, bf16[32,2048]{1,0:T(8,128)(2,1)S(1)}, bf16[32,2048]{1,0:T(8,128)(2,1)S(1)}, bf16[32,2048]{1,0:T(8,128)(2,1)S(1)}) custom-call(s32[1]{0:T(128)} %bitcast.6.share, bf16[128,2048]{1,0:T(8,128)(2,1)S(1)} %collective-permute-done.8.refs_0_, bf16[2048,2048]{1,0:T(8,128)(2,1)S(1)} %copy-done.2), custom_call_target="tpu_custom_call" | custom-call | flops 1 | bytes 1 | tf_op jit(solution)/shard_map/pallas_call | solution.py:66
  137.8 2.8 %collective-permute-done.22 = bf16[32,2048]{1,0:T(8,128)(2,1)S(1)} collective-permute-done((bf16[32,2048]{1,0:T(8,128)(2,1)S(1)}, bf16[32,2048]{1,0:T(8,128)(2,1)S(1)}, u32[]{:S(2)}, u32[]{:S(2)}) %collective-permute-start.22) | collective-permute-done | bytes 131104 | tf_op jit(solution)/shard_map/ppermute | solution.py:28
  145.5 4.9 %collective-permute-done.25 = bf16[32,2048]{1,0:T(8,128)(2,1)S(1)} collective-permute-done((bf16[32,2048]{1,0:T(8,128)(2,1)S(1)}, bf16[32,2048]{1,0:T(8,128)(2,1)S(1)}, u32[]{:S(2)}, u32[]{:S(2)}) %collective-permute-start.25) | collective-permute-done | bytes 131104 | tf_op jit(solution)/shard_map/ppermute | solution.py:28
  155.1 4.4 %collective-permute-done.28 = bf16[32,2048]{1,0:T(8,128)(2,1)S(1)} collective-permute-done((bf16[32,2048]{1,0:T(8,128)(2,1)S(1)}, bf16[32,2048]{1,0:T(8,128)(2,1)S(1)}, u32[]{:S(2)}, u32[]{:S(2)}) %collective-permute-start.28) | collective-permute-done | bytes 131104 | tf_op jit(solution)/shard_map/ppermute | solution.py:28
  163.4 8.9 %collective-permute-done.33 = bf16[32,2048]{1,0:T(8,128)(2,1)S(1)} collective-permute-done((bf16[32,2048]{1,0:T(8,128)(2,1)S(1)}, bf16[32,2048]{1,0:T(8,128)(2,1)S(1)}, u32[]{:S(2)}, u32[]{:S(2)}) %collective-permute-start.33) | collective-permute-done | bytes 131104 | tf_op jit(solution)/shard_map/ppermute | solution.py:28
  (122 shorter events, 46.9 us)
Async XLA Ops:
  7.3 14.5 %collective-permute-start = (bf16[8,32,512]{2,1,0:T(8,128)(2,1)}, bf16[8,32,512]{2,1,0:T(8,128)(2,1)S(1)}, u32[]{:S(2)}, u32[]{:S(2)}) collective-permute-start(bf16[8,32,512]{2,1,0:T(8,128)(2,1)} %get-tuple-element.97), channel_id=1, source_target_pairs={{0,4},{4,0},{8,12},{12,8},{1,5},{5,1},{9,13},{13,9},{2,6},{6,2},{1... | collective-permute-start | bytes 786440 | tf_op jit(solution)/shard_map/ppermute | solution.py:28
  10.3 21.4 %collective-permute-start.1 = (bf16[8,32,512]{2,1,0:T(8,128)(2,1)S(1)}, bf16[8,32,512]{2,1,0:T(8,128)(2,1)S(1)}, u32[]{:S(2)}, u32[]{:S(2)}) collective-permute-start(bf16[8,32,512]{2,1,0:T(8,128)(2,1)S(1)} %get-tuple-element.96), channel_id=1, source_target_pairs={{0,8},{4,12},{8,0},{12,4},{1,9},{5,13},{9,1},{13,5},{2,10},{6,14},... | collective-permute-start | bytes 786440 | tf_op jit(solution)/shard_map/ppermute | solution.py:28
  12.9 18.8 %collective-permute-start.2 = (bf16[8,32,512]{2,1,0:T(8,128)(2,1)S(1)}, bf16[8,32,512]{2,1,0:T(8,128)(2,1)}, u32[]{:S(2)}, u32[]{:S(2)}) collective-permute-start(bf16[8,32,512]{2,1,0:T(8,128)(2,1)S(1)} %get-tuple-element.98), channel_id=1, source_target_pairs={{0,12},{4,8},{8,4},{12,0},{1,13},{5,9},{9,5},{13,1},{2,14},{6,10},... | collective-permute-start | bytes 786440 | tf_op jit(solution)/shard_map/ppermute | solution.py:28
  35.6 11.6 %collective-permute-start.4 = (bf16[2,256,512]{2,1,0:T(8,128)(2,1)S(1)}, bf16[2,256,512]{2,1,0:T(8,128)(2,1)S(1)}, u32[]{:S(2)}, u32[]{:S(2)}) collective-permute-start(bf16[2,256,512]{2,1,0:T(8,128)(2,1)S(1)} %bitcast.26), channel_id=1, source_target_pairs={{0,2},{2,0},{1,3},{3,1},{4,6},{6,4},{5,7},{7,5},{8,10},{10,8},{9,1... | collective-permute-start | bytes 1572872 | tf_op jit(solution)/shard_map/ppermute | solution.py:28
  37.1 10.0 %collective-permute-start.3 = (bf16[2,256,512]{2,1,0:T(8,128)(2,1)S(1)}, bf16[2,256,512]{2,1,0:T(8,128)(2,1)S(1)}, u32[]{:S(2)}, u32[]{:S(2)}) collective-permute-start(bf16[2,256,512]{2,1,0:T(8,128)(2,1)S(1)} %bitcast.27), channel_id=1, source_target_pairs={{0,1},{1,0},{2,3},{3,2},{4,5},{5,4},{6,7},{7,6},{8,9},{9,8},{10,11... | collective-permute-start | bytes 1572872 | tf_op jit(solution)/shard_map/ppermute | solution.py:28
  55.3 24.3 %collective-permute-start.6 = (bf16[128,2048]{1,0:T(8,128)(2,1)S(1)}, bf16[128,2048]{1,0:T(8,128)(2,1)}, u32[]{:S(2)}, u32[]{:S(2)}) collective-permute-start(bf16[128,2048]{1,0:T(8,128)(2,1)S(1)} %shard_map.100.refs_0_), channel_id=1, source_target_pairs={{0,12},{4,8},{8,4},{12,0},{1,13},{5,9},{9,5},{13,1},{2,14},{6,10},... | collective-permute-start | bytes 1572872 | tf_op jit(solution)/shard_map/ppermute | solution.py:28
  56.7 25.8 %collective-permute-start.7 = (bf16[128,2048]{1,0:T(8,128)(2,1)S(1)}, bf16[128,2048]{1,0:T(8,128)(2,1)}, u32[]{:S(2)}, u32[]{:S(2)}) collective-permute-start(bf16[128,2048]{1,0:T(8,128)(2,1)S(1)} %shard_map.100.refs_0_), channel_id=1, source_target_pairs={{0,4},{4,0},{8,12},{12,8},{1,5},{5,1},{9,13},{13,9},{2,6},{6,2},{1... | collective-permute-start | bytes 1572872 | tf_op jit(solution)/shard_map/ppermute | solution.py:28
  71.0 30.9 %collective-permute-start.10 = (bf16[128,2048]{1,0:T(8,128)(2,1)S(1)}, bf16[128,2048]{1,0:T(8,128)(2,1)S(1)}, u32[]{:S(2)}, u32[]{:S(2)}) collective-permute-start(bf16[128,2048]{1,0:T(8,128)(2,1)S(1)} %shard_map.101.refs_1_), channel_id=1, source_target_pairs={{0,4},{4,0},{8,12},{12,8},{1,5},{5,1},{9,13},{13,9},{2,6},{6,2},{1... | collective-permute-start | bytes 1572872 | tf_op jit(solution)/shard_map/ppermute | solution.py:28
  71.1 34.6 %collective-permute-start.9 = (bf16[128,2048]{1,0:T(8,128)(2,1)S(1)}, bf16[128,2048]{1,0:T(8,128)(2,1)S(1)}, u32[]{:S(2)}, u32[]{:S(2)}) collective-permute-start(bf16[128,2048]{1,0:T(8,128)(2,1)S(1)} %shard_map.101.refs_1_), channel_id=1, source_target_pairs={{0,12},{4,8},{8,4},{12,0},{1,13},{5,9},{9,5},{13,1},{2,14},{6,10},... | collective-permute-start | bytes 1572872 | tf_op jit(solution)/shard_map/ppermute | solution.py:28
  87.3 9.2 %collective-permute-start.12 = (bf16[64,2048]{1,0:T(8,128)(2,1)S(1)}, bf16[64,2048]{1,0:T(8,128)(2,1)S(1)}, u32[]{:S(2)}, u32[]{:S(2)}) collective-permute-start(bf16[64,2048]{1,0:T(8,128)(2,1)S(1)} %get-tuple-element.60), channel_id=1, source_target_pairs={{0,2},{1,3},{2,0},{3,1},{4,6},{5,7},{6,4},{7,5},{8,10},{9,11},{10,... | collective-permute-start | bytes 786440 | tf_op jit(solution)/shard_map/ppermute | solution.py:28
  88.9 12.3 %collective-permute-start.13 = (bf16[64,2048]{1,0:T(8,128)(2,1)S(1)}, bf16[64,2048]{1,0:T(8,128)(2,1)S(1)}, u32[]{:S(2)}, u32[]{:S(2)}) collective-permute-start(bf16[64,2048]{1,0:T(8,128)(2,1)S(1)} %get-tuple-element.61), channel_id=1, source_target_pairs={{0,3},{1,2},{2,1},{3,0},{4,7},{5,6},{6,5},{7,4},{8,11},{9,10},{10,... | collective-permute-start | bytes 786440 | tf_op jit(solution)/shard_map/ppermute | solution.py:28
  89.3 42.2 %collective-permute-start.8 = (bf16[128,2048]{1,0:T(8,128)(2,1)S(1)}, bf16[128,2048]{1,0:T(8,128)(2,1)S(1)}, u32[]{:S(2)}, u32[]{:S(2)}) collective-permute-start(bf16[128,2048]{1,0:T(8,128)(2,1)S(1)} %broadcast_select_fusion), channel_id=1, source_target_pairs={{0,8},{12,4},{4,0},{8,12},{1,9},{13,5},{5,1},{9,13},{2,10},{14,6},... | collective-permute-start | bytes 1572872 | tf_op jit(solution)/shard_map/ppermute | solution.py:35
  96.5 14.5 %collective-permute-start.31 = (bf16[64,2048]{1,0:T(8,128)(2,1)S(1)}, bf16[64,2048]{1,0:T(8,128)(2,1)S(1)}, u32[]{:S(2)}, u32[]{:S(2)}) collective-permute-start(bf16[64,2048]{1,0:T(8,128)(2,1)S(1)} %get-tuple-element.91), channel_id=1, source_target_pairs={{0,1},{1,0},{2,3},{3,2},{4,5},{5,4},{6,7},{7,6},{8,9},{9,8},{10,11... | collective-permute-start | bytes 786440 | tf_op jit(solution)/shard_map/ppermute | solution.py:28
  101.2 62.1 %collective-permute-start.30 = (bf16[64,2048]{1,0:T(8,128)(2,1)S(1)}, bf16[64,2048]{1,0:T(8,128)(2,1)S(1)}, u32[]{:S(2)}, u32[]{:S(2)}) collective-permute-start(bf16[64,2048]{1,0:T(8,128)(2,1)S(1)} %get-tuple-element.89), channel_id=1, source_target_pairs={{0,1},{1,0},{2,3},{3,2},{4,5},{5,4},{6,7},{7,6},{8,9},{9,8},{10,11... | collective-permute-start | bytes 786440 | tf_op jit(solution)/shard_map/ppermute | solution.py:28
  109.5 9.2 %collective-permute-start.16 = (bf16[64,2048]{1,0:T(8,128)(2,1)S(1)}, bf16[64,2048]{1,0:T(8,128)(2,1)S(1)}, u32[]{:S(2)}, u32[]{:S(2)}) collective-permute-start(bf16[64,2048]{1,0:T(8,128)(2,1)S(1)} %get-tuple-element.66), channel_id=1, source_target_pairs={{0,2},{1,3},{2,0},{3,1},{4,6},{5,7},{6,4},{7,5},{8,10},{9,11},{10,... | collective-permute-start | bytes 786440 | tf_op jit(solution)/shard_map/ppermute | solution.py:28
  111.0 12.3 %collective-permute-start.17 = (bf16[64,2048]{1,0:T(8,128)(2,1)S(1)}, bf16[64,2048]{1,0:T(8,128)(2,1)S(1)}, u32[]{:S(2)}, u32[]{:S(2)}) collective-permute-start(bf16[64,2048]{1,0:T(8,128)(2,1)S(1)} %get-tuple-element.67), channel_id=1, source_target_pairs={{0,3},{1,2},{2,1},{3,0},{4,7},{5,6},{6,5},{7,4},{8,11},{9,10},{10,... | collective-permute-start | bytes 786440 | tf_op jit(solution)/shard_map/ppermute | solution.py:28
  111.5 20.0 %collective-permute-start.14 = (bf16[128,1024]{1,0:T(8,128)(2,1)S(1)}, bf16[128,1024]{1,0:T(8,128)(2,1)S(1)}, u32[]{:S(2)}, u32[]{:S(2)}) collective-permute-start(bf16[128,1024]{1,0:T(8,128)(2,1)S(1)} %get-tuple-element.94), channel_id=1, source_target_pairs={{0,8},{12,4},{4,0},{8,12},{1,9},{13,5},{5,1},{9,13},{2,10},{14,6},... | collective-permute-start | bytes 786440 | tf_op jit(solution)/shard_map/ppermute | solution.py:35
  123.3 8.1 %collective-permute-start.19 = (bf16[32,2048]{1,0:T(8,128)(2,1)S(1)}, bf16[32,2048]{1,0:T(8,128)(2,1)S(1)}, u32[]{:S(2)}, u32[]{:S(2)}) collective-permute-start(bf16[32,2048]{1,0:T(8,128)(2,1)S(1)} %get-tuple-element.101), channel_id=1, source_target_pairs={{0,12},{4,8},{8,4},{12,0},{1,13},{5,9},{9,5},{13,1},{2,14},{6,10},... | collective-permute-start | bytes 393224 | tf_op jit(solution)/shard_map/ppermute | solution.py:28
  124.8 19.1 %collective-permute-start.20 = (bf16[128,1024]{1,0:T(8,128)(2,1)S(1)}, bf16[128,1024]{1,0:T(8,128)(2,1)S(1)}, u32[]{:S(2)}, u32[]{:S(2)}) collective-permute-start(bf16[128,1024]{1,0:T(8,128)(2,1)S(1)} %get-tuple-element.93), channel_id=1, source_target_pairs={{0,8},{12,4},{4,0},{8,12},{1,9},{13,5},{5,1},{9,13},{2,10},{14,6},... | collective-permute-start | bytes 786440 | tf_op jit(solution)/shard_map/ppermute | solution.py:35
  135.8 6.7 %collective-permute-start.23 = (bf16[32,2048]{1,0:T(8,128)(2,1)S(1)}, bf16[32,2048]{1,0:T(8,128)(2,1)S(1)}, u32[]{:S(2)}, u32[]{:S(2)}) collective-permute-start(bf16[32,2048]{1,0:T(8,128)(2,1)S(1)} %get-tuple-element.76), channel_id=1, source_target_pairs={{0,3},{1,2},{2,1},{3,0},{4,7},{5,6},{6,5},{7,4},{8,11},{9,10},{10,... | collective-permute-start | bytes 393224 | tf_op jit(solution)/shard_map/ppermute | solution.py:28
  136.2 27.1 %collective-permute-start.32 = (bf16[64,2048]{1,0:T(8,128)(2,1)S(1)}, bf16[64,2048]{1,0:T(8,128)(2,1)S(1)}, u32[]{:S(2)}, u32[]{:S(2)}) collective-permute-start(bf16[64,2048]{1,0:T(8,128)(2,1)S(1)} %add_convert_fusion.1), channel_id=1, source_target_pairs={{0,2},{2,0},{1,3},{3,1},{4,6},{6,4},{5,7},{7,5},{8,10},{10,8},{9,1... | collective-permute-start | bytes 786440 | tf_op jit(solution)/shard_map/ppermute | solution.py:28
  142.5 7.9 %collective-permute-start.25 = (bf16[32,2048]{1,0:T(8,128)(2,1)S(1)}, bf16[32,2048]{1,0:T(8,128)(2,1)S(1)}, u32[]{:S(2)}, u32[]{:S(2)}) collective-permute-start(bf16[32,2048]{1,0:T(8,128)(2,1)S(1)} %get-tuple-element.99), channel_id=1, source_target_pairs={{0,12},{4,8},{8,4},{12,0},{1,13},{5,9},{9,5},{13,1},{2,14},{6,10},... | collective-permute-start | bytes 393224 | tf_op jit(solution)/shard_map/ppermute | solution.py:28
  155.1 8.2 %collective-permute-start.26 = (bf16[32,2048]{1,0:T(8,128)(2,1)S(1)}, bf16[32,2048]{1,0:T(8,128)(2,1)S(1)}, u32[]{:S(2)}, u32[]{:S(2)}) collective-permute-start(bf16[32,2048]{1,0:T(8,128)(2,1)S(1)} %add_convert_fusion.5), channel_id=1, source_target_pairs={{0,8},{4,12},{8,0},{12,4},{1,9},{5,13},{9,1},{13,5},{2,10},{6,14},... | collective-permute-start | bytes 393224 | tf_op jit(solution)/shard_map/ppermute | solution.py:28
  163.3 9.0 %collective-permute-start.33 = (bf16[32,2048]{1,0:T(8,128)(2,1)S(1)}, bf16[32,2048]{1,0:T(8,128)(2,1)S(1)}, u32[]{:S(2)}, u32[]{:S(2)}) collective-permute-start(bf16[32,2048]{1,0:T(8,128)(2,1)S(1)} %add_convert_fusion.4), channel_id=1, source_target_pairs={{0,8},{4,12},{8,0},{12,4},{1,9},{5,13},{9,1},{13,5},{2,10},{6,14},... | collective-permute-start | bytes 393224 | tf_op jit(solution)/shard_map/ppermute | solution.py:28
  (24 other events, 244.8 us)

commit v10 on v8

--- a/solution.py
+++ b/solution.py
@@ -9,7 +9,6 @@
 from jax.sharding import PartitionSpec as P
 
 BLK = 128
-CHUNKS = 2
 LIGHT = pl.CostEstimate(flops=1, bytes_accessed=1, transcendentals=0)
 
 
@@ -37,15 +36,16 @@
 
 def project_kernel(block_count, share_count, share, *refs):
     blocks, weight, outs = refs[:block_count], refs[block_count], refs[block_count + 1 :]
-    part_rows = blocks[0].shape[0] // share_count
     picked = []
     for flip in range(share_count):
-        start = pl.multiple_of((share[0] ^ flip) * part_rows, part_rows)
-        picked += [block[pl.ds(start, part_rows), :] for block in blocks]
+        for block in blocks:
+            part_rows = block.shape[0] // share_count
+            start = pl.multiple_of((share[0] ^ flip) * part_rows, part_rows)
+            picked.append(block[pl.ds(start, part_rows), :])
     product = jnp.dot(
         jnp.concatenate(picked, axis=0), weight[...], preferred_element_type=jnp.float32
     )
-    rows = block_count * part_rows
+    rows = product.shape[0] // share_count
     for flip in range(share_count):
         outs[flip][...] = product[flip * rows : (flip + 1) * rows].astype(outs[flip].dtype)
 
@@ -74,11 +74,13 @@
     )(share, *blocks, out_weight)
 
 
-def sum_shares(pieces):
-    total = pieces[0]
-    for flip in range(1, len(pieces)):
-        total = total + swap(pieces[flip], ("heads", "sub"), flip).astype(jnp.float32)
-    return total.astype(jnp.bfloat16)
+def send_shares(pieces):
+    axes = ("heads", "sub")
+    return [pieces[0]] + [swap(pieces[flip], axes, flip) for flip in range(1, len(pieces))]
+
+
+def add_shares(pieces):
+    return sum(piece.astype(jnp.float32) for piece in pieces).astype(jnp.bfloat16)
 
 
 def sum_in_turn(pieces):
@@ -150,7 +152,7 @@
     for first in range(0, per_group, together):
         normed = []
         for head in range(first, first + together):
-            query = queries[0, :, 0, :, head * head_width : (head + 1) * head_width]
+            query = queries[0, :, :, head * head_width : (head + 1) * head_width]
             query = query.reshape(text, head_width).astype(jnp.float32)
             normed.append(rms_scale(query, q_gain[...]).astype(jnp.bfloat16))
         scores = lax.dot_general(
@@ -168,12 +170,12 @@
             out[:, columns] = result[i * text : (i + 1) * text]
 
 
-def attend(chunk, queries, parts, kv_flat, q_gain, k_gain, scalars):
-    requests, request_shares, _, part_rows, width = queries.shape
+def attend(chunk, rows, queries, parts, kv_flat, q_gain, k_gain, scalars):
+    requests, request_shares, _, width = queries.shape
     heads_here, rank_width, pair_width = kv_flat.shape
     head_width = q_gain.shape[1]
     slots = len(parts) * parts[0].shape[1]
-    text = request_shares * part_rows
+    text = request_shares * rows
     whole = pl.BlockSpec(memory_space=pltpu.VMEM)
     return pl.pallas_call(
         functools.partial(attend_kernel, len(parts)),
@@ -181,8 +183,8 @@
         in_specs=[
             pl.BlockSpec(memory_space=pltpu.SMEM),
             pl.BlockSpec(
-                (1, request_shares, 1, part_rows, width // heads_here),
-                lambda r, g: (r, 0, chunk, 0, g),
+                (1, request_shares, rows, width // heads_here),
+                lambda r, g: (r, 0, chunk, g),
             ),
         ]
         + [whole for _ in parts]
@@ -237,19 +239,21 @@
     for part in over_heads:
         parts += [part] + [swap(part, "sub", flip) for flip in range(1, sub_size)]
     part_rows = requests_here * text_rows // share_count
-    shaped = queries.reshape(
-        requests_here, share_count // requests_here, CHUNKS, part_rows // CHUNKS, -1
-    )
+    shaped = queries.reshape(requests_here, share_count // requests_here, part_rows, -1)
+    few = part_rows // 2
+    chunk_rows = part_rows - few, few
 
     def attended(chunk):
-        return attend(chunk, shaped, parts, kv_flat, *gains, scalars)
+        rows = chunk_rows[chunk]
+        start = sum(chunk_rows[:chunk]) // rows
+        return attend(start, rows, shaped, parts, kv_flat, *gains, scalars)
 
     columns = out_weight.shape[1]
     if pool_size != 4:
         outputs = []
-        for chunk in range(CHUNKS):
+        for chunk in range(len(chunk_rows)):
             rows = lax.all_gather(attended(chunk), "pool", axis=0)
-            mine = sum_shares(project_out([rows[i] for i in range(pool_size)], out_weight))
+            mine = add_shares(send_shares(project_out([rows[i] for i in range(pool_size)], out_weight)))
             mine = mine.reshape(pool_size, -1, columns)
             back = lax.all_to_all(mine, "pool", split_axis=0, concat_axis=0, tiled=True)
             outputs.append(jnp.moveaxis(back, 0, 1).reshape(-1, pool_size * columns))
@@ -262,31 +266,28 @@
     own = project_out([first, last], out_weight)
     across0, beside0, own = tie((across0, beside0, own))
     second0 = second_hop(first, across0)
+    near0 = send_shares(project_out([beside0, across0], out_weight))
+    across1, beside1, near0 = tie((across1, beside1, near0))
+    second1 = second_hop(last, across1)
+    many, few = chunk_rows
+    near0 = add_shares(near0)
+    back0 = swap(near0[:many], "pool", 1), swap(near0[many:], "pool", 3)
+    near1 = send_shares(project_out([beside1, across1], out_weight))
+    second0, near1, back0 = tie((second0, near1, back0))
+    far0 = send_shares(project_out([second0], out_weight))
+    near1 = add_shares(near1)
+    back1 = swap(near1[:few], "pool", 1), swap(near1[few:], "pool", 3)
+    second1, far0, back1 = tie((second1, far0, back1))
+    back_second0 = swap(add_shares(far0), "pool", 2)
+    far1 = send_shares(project_out([second1], out_weight))
+    back_second0, far1 = tie((back_second0, far1))
+    back_second1 = swap(add_shares(far1), "pool", 2)
     own = sum_in_turn(own)
-    near0 = sum_shares(project_out([beside0, across0], out_weight))
-    across1, beside1, own, near0 = tie((across1, beside1, own, near0))
-    second1 = second_hop(last, across1)
-    half = near0.shape[0] // 2
-    back0 = swap(near0[:half], "pool", 1), swap(near0[half:], "pool", 3)
-    near1 = sum_shares(project_out([beside1, across1], out_weight))
-    second0, near1, back0 = tie((second0, near1, back0))
-    back1 = swap(near1[:half], "pool", 1), swap(near1[half:], "pool", 3)
-    far0 = sum_shares(project_out([second0], out_weight))
-    second1, far0, back1 = tie((second1, far0, back1))
-    back_second0 = swap(far0, "pool", 2)
-    far1 = sum_shares(project_out([second1], out_weight))
-    back_second0, far1 = tie((back_second0, far1))
-    back_second1 = swap(far1, "pool", 2)
-    backs = [
-        [own[:half], back0[0], back_second0, back0[1]],
-        [own[half:], back1[0], back_second1, back1[1]],
-    ]
+    backs = [(0, 1, back0[0]), (0, 3, back0[1]), (many, 1, back1[0]), (many, 3, back1[1])]
+    backs += [(0, 2, back_second0), (0, 0, own), (many, 2, back_second1)]
     output = jnp.zeros((part_rows, pool_size * columns), jnp.bfloat16)
-    for chunk in range(CHUNKS):
-        for flip in (0, 1, 3, 2):
-            output = lax.dynamic_update_slice(
-                output, backs[chunk][flip], (chunk * half, (pool_index ^ flip) * columns)
-            )
+    for row, flip, block in backs:
+        output = lax.dynamic_update_slice(output, block, (row, (pool_index ^ flip) * columns))
     return output
 
 

time: 167 us -> 165 us (0.988)
  waiting for transfers between devices: 85.1 us -> 80.8 us
  starting transfers between devices: 32.1 us -> 35.3 us
    ppermute x31, waiting for transfers between devices: 85.1 us -> 80.8 us  [swap(): lax.ppermute(values, axis, [(i, i ^ flip) for i in range(lax.axis_size(ax...]
    ppermute x31, starting transfers between devices: 31.1 us -> 34.5 us  [swap(): lax.ppermute(values, axis, [(i, i ^ flip) for i in range(lax.axis_size(ax...]
    unnamed x28 -> x24, local copies, waits for them, and re-layouts: 6.17 us -> 7.46 us
  transfers between devices with their start and end apart: 33 -> 33, of which waited for: 19 -> 18; matrix products, arithmetic and copies ran while one was open for 1% -> 1% of each run, Pallas kernels for 13% -> 14%
where the time goes in v10:
time: 165 us
  waiting for transfers between devices  80.8 us (49%)
  starting transfers between devices  35.3 us (21%)
  Pallas kernels  29.9 us (18%)
  local copies, waits for them, and re-layouts  13.9 us (8%)
  other arithmetic  2.35 us (1%)
  matrix products  1.94 us (1%)
    ppermute x31, waiting for transfers between devices, swap(): lax.ppermute(values, axis, [(i, i ^ flip) for i in range(lax.axis_size(ax...  80.8 us
    ppermute x31, starting transfers between devices, swap(): lax.ppermute(values, axis, [(i, i ^ flip) for i in range(lax.axis_size(ax...  34.5 us
    pallas_call x5, Pallas kernels, project_out(): pl.pallas_call(functools.partial(project_kernel, len(blocks), share_count...  17.5 us
    pallas_call x2, Pallas kernels, attend(): pl.pallas_call(functools.partial(attend_kernel, len(parts)), grid=(reques...  12.4 us
    unnamed x24, local copies, waits for them, and re-layouts  7.46 us
  transfers between devices with their start and end apart: 33, of which 18 were waited for; matrix products, arithmetic and copies ran while one was open for 1% of the time, Pallas kernels for 14%

profile of v10, /device:TPU:0, one launch (start us, length us, event | category | flops | bytes accessed | tf_op | source)
XLA Modules:
  0.0 164.7 jit_solution(3164842480504910346)
XLA Ops:
  3.7 2.8 %gather_fusion.1 = bf16[32,32,512]{2,1,0:T(8,128)(2,1)S(1)} fusion(bf16[128,32,512]{2,1,0:T(8,128)(2,1)} %bitcast.38, s32[1024]{0:T(1024)S(1)} %pad_clamp_fusion.1), kind=kCustom, calls=%fused_computation.1 | custom fusion | bytes 2097280 | tf_op jit(solution)/shard_map/gather | solution.py:125
  7.4 3.0 %collective-permute-start = (bf16[8,32,512]{2,1,0:T(8,128)(2,1)}, bf16[8,32,512]{2,1,0:T(8,128)(2,1)}, u32[]{:S(2)}, u32[]{:S(2)}) collective-permute-start(bf16[8,32,512]{2,1,0:T(8,128)(2,1)} %get-tuple-element.115), channel_id=1, source_target_pairs={{0,4},{4,0},{8,12},{12,8},{1,5},{5,1},{9,13},{13,9},{2,6},{6,2},{1... | collective-permute-start | bytes 786440 | tf_op jit(solution)/shard_map/ppermute | solution.py:27
  13.8 8.1 %collective-permute-done = bf16[8,32,512]{2,1,0:T(8,128)(2,1)} collective-permute-done((bf16[8,32,512]{2,1,0:T(8,128)(2,1)}, bf16[8,32,512]{2,1,0:T(8,128)(2,1)}, u32[]{:S(2)}, u32[]{:S(2)}) %collective-permute-start) | collective-permute-done | bytes 262176 | tf_op jit(solution)/shard_map/ppermute | solution.py:27
  21.9 10.2 %collective-permute-done.1 = bf16[8,32,512]{2,1,0:T(8,128)(2,1)} collective-permute-done((bf16[8,32,512]{2,1,0:T(8,128)(2,1)}, bf16[8,32,512]{2,1,0:T(8,128)(2,1)}, u32[]{:S(2)}, u32[]{:S(2)}) %collective-permute-start.1) | collective-permute-done | bytes 262176 | tf_op jit(solution)/shard_map/ppermute | solution.py:27
  35.5 9.7 %collective-permute-done.4.refs_2_ = bf16[2,256,512]{2,1,0:T(8,128)(2,1)S(1)} collective-permute-done((bf16[2,256,512]{2,1,0:T(8,128)(2,1)S(1)}, bf16[2,256,512]{2,1,0:T(8,128)(2,1)S(1)}, u32[]{:S(2)}, u32[]{:S(2)}) %collective-permute-start.4) | collective-permute-done | bytes 524320 | tf_op jit(solution)/shard_map/ppermute | solution.py:27
  47.1 6.2 %shard_map.100.refs_0_ = bf16[128,2048]{1,0:T(8,128)(2,1)S(1)} custom-call(s32[3]{0:T(128)S(1)} %pad_add_fusion.scalars, bf16[2,2,64,2048]{3,2,1,0:T(8,128)(2,1)S(1)} %bitcast.32, bf16[2,256,512]{2,1,0:T(8,128)(2,1)S(1)} %bitcast.30, bf16[2,256,512]{2,1,0:T(8,128)(2,1)S(1)} %collective-permute-done.3.refs_1_, ...), custom_call_target="tpu_custom_call" | custom-call | flops 1 | bytes 1 | tf_op jit(solution)/shard_map/pallas_call | solution.py:180
  54.8 6.3 %collective-permute-start.7 = (bf16[128,2048]{1,0:T(8,128)(2,1)S(1)}, bf16[128,2048]{1,0:T(8,128)(2,1)}, u32[]{:S(2)}, u32[]{:S(2)}) collective-permute-start(bf16[128,2048]{1,0:T(8,128)(2,1)S(1)} %shard_map.100.refs_0_), channel_id=1, source_target_pairs={{0,4},{4,0},{8,12},{12,8},{1,5},{5,1},{9,13},{13,9},{2,6},{6,2},{1... | collective-permute-start | bytes 1572872 | tf_op jit(solution)/shard_map/ppermute | solution.py:27
  61.1 6.2 %shard_map.101.refs_1_ = bf16[128,2048]{1,0:T(8,128)(2,1)S(1)} custom-call(s32[3]{0:T(128)S(1)} %pad_add_fusion.scalars, bf16[2,2,64,2048]{3,2,1,0:T(8,128)(2,1)S(1)} %bitcast.33, bf16[2,256,512]{2,1,0:T(8,128)(2,1)S(1)} %bitcast.31, bf16[2,256,512]{2,1,0:T(8,128)(2,1)S(1)} %collective-permute-done.3.refs_1_, ...), custom_call_target="tpu_custom_call" | custom-call | flops 1 | bytes 1 | tf_op jit(solution)/shard_map/pallas_call | solution.py:180
  68.7 3.4 %copy-done.1 = bf16[2048,2048]{1,0:T(8,128)(2,1)S(1)} copy-done((bf16[2048,2048]{1,0:T(8,128)(2,1)S(1)}, bf16[2048,2048]{1,0:T(8,128)(2,1)}, u32[]{:S(2)}) %copy-start.1) | copy-done | bytes 8388632
  72.1 3.7 %shard_map.102 = (f32[64,2048]{1,0:T(8,128)S(1)}, bf16[64,2048]{1,0:T(8,128)(2,1)S(1)}, bf16[64,2048]{1,0:T(8,128)(2,1)S(1)}, bf16[64,2048]{1,0:T(8,128)(2,1)S(1)}) custom-call(s32[1]{0:T(128)} %bitcast.6.share, bf16[128,2048]{1,0:T(8,128)(2,1)S(1)} %shard_map.100.refs_0_, bf16[128,2048]{1,0:T(8,128)(2,1)S(1)} %shard_map.101.refs_1_, ...), custom_call_target="tpu_custom_call" | custom-call | flops 1 | bytes 1 | tf_op jit(solution)/shard_map/pallas_call | solution.py:61
  75.8 4.8 %collective-permute-done.7.refs_0_ = bf16[128,2048]{1,0:T(8,128)(2,1)} collective-permute-done((bf16[128,2048]{1,0:T(8,128)(2,1)S(1)}, bf16[128,2048]{1,0:T(8,128)(2,1)}, u32[]{:S(2)}, u32[]{:S(2)}) %collective-permute-start.7) | collective-permute-done | bytes 524320 | tf_op jit(solution)/shard_map/ppermute | solution.py:27
  80.6 3.4 %copy-done.2 = bf16[2048,2048]{1,0:T(8,128)(2,1)S(1)} copy-done((bf16[2048,2048]{1,0:T(8,128)(2,1)S(1)}, bf16[2048,2048]{1,0:T(8,128)(2,1)}, u32[]{:S(2)}) %copy-start.2) | copy-done | bytes 8388632
  84.0 4.8 %shard_map.103 = (f32[64,2048]{1,0:T(8,128)S(1)}, bf16[64,2048]{1,0:T(8,128)(2,1)S(1)}, bf16[64,2048]{1,0:T(8,128)(2,1)S(1)}, bf16[64,2048]{1,0:T(8,128)(2,1)S(1)}) custom-call(s32[1]{0:T(128)} %bitcast.6.share, bf16[128,2048]{1,0:T(8,128)(2,1)} %collective-permute-done.7.refs_0_, bf16[128,2048]{1,0:T(8,128)(2,1)} %collective-permute-done.6.refs_1_, ...), custom_call_target="tpu_custom_call" | custom-call | flops 1 | bytes 1 | tf_op jit(solution)/shard_map/pallas_call | solution.py:61
  93.2 10.5 %collective-permute-done.9.refs_1_ = bf16[128,2048]{1,0:T(8,128)(2,1)S(1)} collective-permute-done((bf16[128,2048]{1,0:T(8,128)(2,1)S(1)}, bf16[128,2048]{1,0:T(8,128)(2,1)S(1)}, u32[]{:S(2)}, u32[]{:S(2)}) %collective-permute-start.9) | collective-permute-done | bytes 524320 | tf_op jit(solution)/shard_map/ppermute | solution.py:27
  105.8 3.7 %shard_map.104 = (f32[64,2048]{1,0:T(8,128)S(1)}, bf16[64,2048]{1,0:T(8,128)(2,1)S(1)}, bf16[64,2048]{1,0:T(8,128)(2,1)S(1)}, bf16[64,2048]{1,0:T(8,128)(2,1)S(1)}) custom-call(s32[1]{0:T(128)} %bitcast.6.share, bf16[128,2048]{1,0:T(8,128)(2,1)S(1)} %collective-permute-done.10.refs_0_, bf16[128,2048]{1,0:T(8,128)(2,1)S(1)} %collective-permute-done.9.refs_1_, ...), custom_call_target="tpu_custom_call" | custom-call | flops 1 | bytes 1 | tf_op jit(solution)/shard_map/pallas_call | solution.py:61
  111.2 6.5 %collective-permute-done.17 = bf16[32,2048]{1,0:T(8,128)(2,1)S(1)} collective-permute-done((bf16[32,2048]{1,0:T(8,128)(2,1)S(1)}, bf16[32,2048]{1,0:T(8,128)(2,1)S(1)}, u32[]{:S(2)}, u32[]{:S(2)}) %collective-permute-start.17) | collective-permute-done | bytes 131104 | tf_op jit(solution)/shard_map/ppermute | solution.py:27
  119.9 6.3 %collective-permute-done.16 = bf16[64,2048]{1,0:T(8,128)(2,1)S(1)} collective-permute-done((bf16[64,2048]{1,0:T(8,128)(2,1)S(1)}, bf16[64,2048]{1,0:T(8,128)(2,1)S(1)}, u32[]{:S(2)}, u32[]{:S(2)}) %collective-permute-start.16) | collective-permute-done | bytes 262176 | tf_op jit(solution)/shard_map/ppermute | solution.py:27
  128.7 2.7 %shard_map.105 = (f32[32,2048]{1,0:T(8,128)S(1)}, bf16[32,2048]{1,0:T(8,128)(2,1)S(1)}, bf16[32,2048]{1,0:T(8,128)(2,1)S(1)}, bf16[32,2048]{1,0:T(8,128)(2,1)S(1)}) custom-call(s32[1]{0:T(128)} %bitcast.6.share, bf16[128,2048]{1,0:T(8,128)(2,1)S(1)} %collective-permute-done.8.refs_0_, bf16[2048,2048]{1,0:T(8,128)(2,1)S(1)} %bitcast.25), custom_call_target="tpu_custom_call" | custom-call | flops 1 | bytes 1 | tf_op jit(solution)/shard_map/pallas_call | solution.py:61
  132.3 4.3 %collective-permute-done.23 = bf16[32,2048]{1,0:T(8,128)(2,1)S(1)} collective-permute-done((bf16[32,2048]{1,0:T(8,128)(2,1)S(1)}, bf16[32,2048]{1,0:T(8,128)(2,1)S(1)}, u32[]{:S(2)}, u32[]{:S(2)}) %collective-permute-start.23) | collective-permute-done | bytes 131104 | tf_op jit(solution)/shard_map/ppermute | solution.py:27
  143.2 2.7 %shard_map.106 = (f32[32,2048]{1,0:T(8,128)S(1)}, bf16[32,2048]{1,0:T(8,128)(2,1)S(1)}, bf16[32,2048]{1,0:T(8,128)(2,1)S(1)}, bf16[32,2048]{1,0:T(8,128)(2,1)S(1)}) custom-call(s32[1]{0:T(128)} %bitcast.6.share, bf16[128,2048]{1,0:T(8,128)(2,1)S(1)} %collective-permute-done.19.refs_0_, bf16[2048,2048]{1,0:T(8,128)(2,1)S(1)} %bitcast.25), custom_call_target="tpu_custom_call" | custom-call | flops 1 | bytes 1 | tf_op jit(solution)/shard_map/pallas_call | solution.py:61
  147.9 2.6 %collective-permute-done.25 = bf16[32,2048]{1,0:T(8,128)(2,1)S(1)} collective-permute-done((bf16[32,2048]{1,0:T(8,128)(2,1)S(1)}, bf16[32,2048]{1,0:T(8,128)(2,1)S(1)}, u32[]{:S(2)}, u32[]{:S(2)}) %collective-permute-start.25) | collective-permute-done | bytes 131104 | tf_op jit(solution)/shard_map/ppermute | solution.py:27
  154.3 2.8 %collective-permute-start.32 = (bf16[32,2048]{1,0:T(8,128)(2,1)S(1)}, bf16[32,2048]{1,0:T(8,128)(2,1)S(1)}, u32[]{:S(2)}, u32[]{:S(2)}) collective-permute-start(bf16[32,2048]{1,0:T(8,128)(2,1)S(1)} %add_convert_fusion.4), channel_id=1, source_target_pairs={{0,8},{4,12},{8,0},{12,4},{1,9},{5,13},{9,1},{13,5},{2,10},{6,14},... | collective-permute-start | bytes 393224 | tf_op jit(solution)/shard_map/ppermute | solution.py:27
  157.2 3.2 %collective-permute-done.31 = bf16[64,2048]{1,0:T(8,128)(2,1)S(1)} collective-permute-done((bf16[64,2048]{1,0:T(8,128)(2,1)S(1)}, bf16[64,2048]{1,0:T(8,128)(2,1)S(1)}, u32[]{:S(2)}, u32[]{:S(2)}) %collective-permute-start.31) | collective-permute-done | bytes 262176 | tf_op jit(solution)/shard_map/ppermute | solution.py:27
  160.4 3.6 %collective-permute-done.32 = bf16[32,2048]{1,0:T(8,128)(2,1)S(1)} collective-permute-done((bf16[32,2048]{1,0:T(8,128)(2,1)S(1)}, bf16[32,2048]{1,0:T(8,128)(2,1)S(1)}, u32[]{:S(2)}, u32[]{:S(2)}) %collective-permute-start.32) | collective-permute-done | bytes 131104 | tf_op jit(solution)/shard_map/ppermute | solution.py:27
  (117 shorter events, 42.8 us)
Async XLA Ops:
  7.4 14.5 %collective-permute-start = (bf16[8,32,512]{2,1,0:T(8,128)(2,1)}, bf16[8,32,512]{2,1,0:T(8,128)(2,1)}, u32[]{:S(2)}, u32[]{:S(2)}) collective-permute-start(bf16[8,32,512]{2,1,0:T(8,128)(2,1)} %get-tuple-element.115), channel_id=1, source_target_pairs={{0,4},{4,0},{8,12},{12,8},{1,5},{5,1},{9,13},{13,9},{2,6},{6,2},{1... | collective-permute-start | bytes 786440 | tf_op jit(solution)/shard_map/ppermute | solution.py:27
  10.4 21.7 %collective-permute-start.1 = (bf16[8,32,512]{2,1,0:T(8,128)(2,1)}, bf16[8,32,512]{2,1,0:T(8,128)(2,1)}, u32[]{:S(2)}, u32[]{:S(2)}) collective-permute-start(bf16[8,32,512]{2,1,0:T(8,128)(2,1)} %get-tuple-element.114), channel_id=1, source_target_pairs={{0,8},{4,12},{8,0},{12,4},{1,9},{5,13},{9,1},{13,5},{2,10},{6,14},... | collective-permute-start | bytes 786440 | tf_op jit(solution)/shard_map/ppermute | solution.py:27
  13.0 19.1 %collective-permute-start.2 = (bf16[8,32,512]{2,1,0:T(8,128)(2,1)}, bf16[8,32,512]{2,1,0:T(8,128)(2,1)}, u32[]{:S(2)}, u32[]{:S(2)}) collective-permute-start(bf16[8,32,512]{2,1,0:T(8,128)(2,1)} %get-tuple-element.116), channel_id=1, source_target_pairs={{0,12},{4,8},{8,4},{12,0},{1,13},{5,9},{9,5},{13,1},{2,14},{6,10},... | collective-permute-start | bytes 786440 | tf_op jit(solution)/shard_map/ppermute | solution.py:27
  34.0 11.3 %collective-permute-start.4 = (bf16[2,256,512]{2,1,0:T(8,128)(2,1)S(1)}, bf16[2,256,512]{2,1,0:T(8,128)(2,1)S(1)}, u32[]{:S(2)}, u32[]{:S(2)}) collective-permute-start(bf16[2,256,512]{2,1,0:T(8,128)(2,1)S(1)} %bitcast.28), channel_id=1, source_target_pairs={{0,2},{2,0},{1,3},{3,1},{4,6},{6,4},{5,7},{7,5},{8,10},{10,8},{9,1... | collective-permute-start | bytes 1572872 | tf_op jit(solution)/shard_map/ppermute | solution.py:27
  35.5 9.7 %collective-permute-start.3 = (bf16[2,256,512]{2,1,0:T(8,128)(2,1)S(1)}, bf16[2,256,512]{2,1,0:T(8,128)(2,1)S(1)}, u32[]{:S(2)}, u32[]{:S(2)}) collective-permute-start(bf16[2,256,512]{2,1,0:T(8,128)(2,1)S(1)} %bitcast.29), channel_id=1, source_target_pairs={{0,1},{1,0},{2,3},{3,2},{4,5},{5,4},{6,7},{7,6},{8,9},{9,8},{10,11... | collective-permute-start | bytes 1572872 | tf_op jit(solution)/shard_map/ppermute | solution.py:27
  53.3 22.5 %collective-permute-start.6 = (bf16[128,2048]{1,0:T(8,128)(2,1)S(1)}, bf16[128,2048]{1,0:T(8,128)(2,1)}, u32[]{:S(2)}, u32[]{:S(2)}) collective-permute-start(bf16[128,2048]{1,0:T(8,128)(2,1)S(1)} %shard_map.100.refs_0_), channel_id=1, source_target_pairs={{0,12},{4,8},{8,4},{12,0},{1,13},{5,9},{9,5},{13,1},{2,14},{6,10},... | collective-permute-start | bytes 1572872 | tf_op jit(solution)/shard_map/ppermute | solution.py:27
  54.8 25.9 %collective-permute-start.7 = (bf16[128,2048]{1,0:T(8,128)(2,1)S(1)}, bf16[128,2048]{1,0:T(8,128)(2,1)}, u32[]{:S(2)}, u32[]{:S(2)}) collective-permute-start(bf16[128,2048]{1,0:T(8,128)(2,1)S(1)} %shard_map.100.refs_0_), channel_id=1, source_target_pairs={{0,4},{4,0},{8,12},{12,8},{1,5},{5,1},{9,13},{13,9},{2,6},{6,2},{1... | collective-permute-start | bytes 1572872 | tf_op jit(solution)/shard_map/ppermute | solution.py:27
  67.2 25.2 %collective-permute-start.10 = (bf16[128,2048]{1,0:T(8,128)(2,1)S(1)}, bf16[128,2048]{1,0:T(8,128)(2,1)S(1)}, u32[]{:S(2)}, u32[]{:S(2)}) collective-permute-start(bf16[128,2048]{1,0:T(8,128)(2,1)S(1)} %shard_map.101.refs_1_), channel_id=1, source_target_pairs={{0,4},{4,0},{8,12},{12,8},{1,5},{5,1},{9,13},{13,9},{2,6},{6,2},{1... | collective-permute-start | bytes 1572872 | tf_op jit(solution)/shard_map/ppermute | solution.py:27
  67.3 36.4 %collective-permute-start.9 = (bf16[128,2048]{1,0:T(8,128)(2,1)S(1)}, bf16[128,2048]{1,0:T(8,128)(2,1)S(1)}, u32[]{:S(2)}, u32[]{:S(2)}) collective-permute-start(bf16[128,2048]{1,0:T(8,128)(2,1)S(1)} %shard_map.101.refs_1_), channel_id=1, source_target_pairs={{0,12},{4,8},{8,4},{12,0},{1,13},{5,9},{9,5},{13,1},{2,14},{6,10},... | collective-permute-start | bytes 1572872 | tf_op jit(solution)/shard_map/ppermute | solution.py:27
  88.8 14.9 %collective-permute-start.11 = (bf16[64,2048]{1,0:T(8,128)(2,1)S(1)}, bf16[64,2048]{1,0:T(8,128)(2,1)S(1)}, u32[]{:S(2)}, u32[]{:S(2)}) collective-permute-start(bf16[64,2048]{1,0:T(8,128)(2,1)S(1)} %get-tuple-element.69), channel_id=1, source_target_pairs={{0,1},{1,0},{2,3},{3,2},{4,5},{5,4},{6,7},{7,6},{8,9},{9,8},{10,11... | collective-permute-start | bytes 786440 | tf_op jit(solution)/shard_map/ppermute | solution.py:27
  88.9 14.9 %collective-permute-start.12 = (bf16[64,2048]{1,0:T(8,128)(2,1)S(1)}, bf16[64,2048]{1,0:T(8,128)(2,1)S(1)}, u32[]{:S(2)}, u32[]{:S(2)}) collective-permute-start(bf16[64,2048]{1,0:T(8,128)(2,1)S(1)} %get-tuple-element.70), channel_id=1, source_target_pairs={{0,2},{1,3},{2,0},{3,1},{4,6},{5,7},{6,4},{7,5},{8,10},{9,11},{10,... | collective-permute-start | bytes 786440 | tf_op jit(solution)/shard_map/ppermute | solution.py:27
  90.4 13.4 %collective-permute-start.13 = (bf16[64,2048]{1,0:T(8,128)(2,1)S(1)}, bf16[64,2048]{1,0:T(8,128)(2,1)S(1)}, u32[]{:S(2)}, u32[]{:S(2)}) collective-permute-start(bf16[64,2048]{1,0:T(8,128)(2,1)S(1)} %get-tuple-element.71), channel_id=1, source_target_pairs={{0,3},{1,2},{2,1},{3,0},{4,7},{5,6},{6,5},{7,4},{8,11},{9,10},{10,... | collective-permute-start | bytes 786440 | tf_op jit(solution)/shard_map/ppermute | solution.py:27
  92.4 33.8 %collective-permute-start.8 = (bf16[128,2048]{1,0:T(8,128)(2,1)S(1)}, bf16[128,2048]{1,0:T(8,128)(2,1)S(1)}, u32[]{:S(2)}, u32[]{:S(2)}) collective-permute-start(bf16[128,2048]{1,0:T(8,128)(2,1)S(1)} %broadcast_select_fusion.1), channel_id=1, source_target_pairs={{0,8},{12,4},{4,0},{8,12},{1,9},{13,5},{5,1},{9,13},{2,10},{14,6},... | collective-permute-start | bytes 1572872 | tf_op jit(solution)/shard_map/ppermute | solution.py:34
  103.9 13.7 %collective-permute-start.17 = (bf16[32,2048]{1,0:T(8,128)(2,1)S(1)}, bf16[32,2048]{1,0:T(8,128)(2,1)S(1)}, u32[]{:S(2)}, u32[]{:S(2)}) collective-permute-start(bf16[32,2048]{1,0:T(8,128)(2,1)S(1)} %get-tuple-element.120), channel_id=1, source_target_pairs={{0,4},{4,0},{8,12},{12,8},{1,5},{5,1},{9,13},{13,9},{2,6},{6,2},{1... | collective-permute-start | bytes 393224 | tf_op jit(solution)/shard_map/ppermute | solution.py:27
  104.0 15.8 %collective-permute-start.18 = (bf16[32,2048]{1,0:T(8,128)(2,1)S(1)}, bf16[32,2048]{1,0:T(8,128)(2,1)S(1)}, u32[]{:S(2)}, u32[]{:S(2)}) collective-permute-start(bf16[32,2048]{1,0:T(8,128)(2,1)S(1)} %get-tuple-element.119), channel_id=1, source_target_pairs={{0,12},{4,8},{8,4},{12,0},{1,13},{5,9},{9,5},{13,1},{2,14},{6,10},... | collective-permute-start | bytes 393224 | tf_op jit(solution)/shard_map/ppermute | solution.py:27
  109.5 10.3 %collective-permute-start.14 = (bf16[64,2048]{1,0:T(8,128)(2,1)S(1)}, bf16[64,2048]{1,0:T(8,128)(2,1)S(1)}, u32[]{:S(2)}, u32[]{:S(2)}) collective-permute-start(bf16[64,2048]{1,0:T(8,128)(2,1)S(1)} %get-tuple-element.75), channel_id=1, source_target_pairs={{0,1},{1,0},{2,3},{3,2},{4,5},{5,4},{6,7},{7,6},{8,9},{9,8},{10,11... | collective-permute-start | bytes 786440 | tf_op jit(solution)/shard_map/ppermute | solution.py:27
  109.6 10.2 %collective-permute-start.15 = (bf16[64,2048]{1,0:T(8,128)(2,1)S(1)}, bf16[64,2048]{1,0:T(8,128)(2,1)S(1)}, u32[]{:S(2)}, u32[]{:S(2)}) collective-permute-start(bf16[64,2048]{1,0:T(8,128)(2,1)S(1)} %get-tuple-element.76), channel_id=1, source_target_pairs={{0,2},{1,3},{2,0},{3,1},{4,6},{5,7},{6,4},{7,5},{8,10},{9,11},{10,... | collective-permute-start | bytes 786440 | tf_op jit(solution)/shard_map/ppermute | solution.py:27
  119.8 21.1 %collective-permute-start.19 = (bf16[128,2048]{1,0:T(8,128)(2,1)S(1)}, bf16[128,2048]{1,0:T(8,128)(2,1)S(1)}, u32[]{:S(2)}, u32[]{:S(2)}) collective-permute-start(bf16[128,2048]{1,0:T(8,128)(2,1)S(1)} %broadcast_select_fusion), channel_id=1, source_target_pairs={{0,8},{12,4},{4,0},{8,12},{1,9},{13,5},{5,1},{9,13},{2,10},{14,6},... | collective-permute-start | bytes 1572872 | tf_op jit(solution)/shard_map/ppermute | solution.py:34
  126.3 10.2 %collective-permute-start.23 = (bf16[32,2048]{1,0:T(8,128)(2,1)S(1)}, bf16[32,2048]{1,0:T(8,128)(2,1)S(1)}, u32[]{:S(2)}, u32[]{:S(2)}) collective-permute-start(bf16[32,2048]{1,0:T(8,128)(2,1)S(1)} %get-tuple-element.118), channel_id=1, source_target_pairs={{0,4},{4,0},{8,12},{12,8},{1,5},{5,1},{9,13},{13,9},{2,6},{6,2},{1... | collective-permute-start | bytes 393224 | tf_op jit(solution)/shard_map/ppermute | solution.py:27
  126.4 12.6 %collective-permute-start.24 = (bf16[32,2048]{1,0:T(8,128)(2,1)S(1)}, bf16[32,2048]{1,0:T(8,128)(2,1)S(1)}, u32[]{:S(2)}, u32[]{:S(2)}) collective-permute-start(bf16[32,2048]{1,0:T(8,128)(2,1)S(1)} %get-tuple-element.117), channel_id=1, source_target_pairs={{0,12},{4,8},{8,4},{12,0},{1,13},{5,9},{9,5},{13,1},{2,14},{6,10},... | collective-permute-start | bytes 393224 | tf_op jit(solution)/shard_map/ppermute | solution.py:27
  139.0 18.2 %collective-permute-start.29 = (bf16[64,2048]{1,0:T(8,128)(2,1)S(1)}, bf16[64,2048]{1,0:T(8,128)(2,1)S(1)}, u32[]{:S(2)}, u32[]{:S(2)}) collective-permute-start(bf16[64,2048]{1,0:T(8,128)(2,1)S(1)} %get-tuple-element.106), channel_id=1, source_target_pairs={{0,1},{1,0},{2,3},{3,2},{4,5},{5,4},{6,7},{7,6},{8,9},{9,8},{10,11... | collective-permute-start | bytes 786440 | tf_op jit(solution)/shard_map/ppermute | solution.py:27
  141.0 9.5 %collective-permute-start.25 = (bf16[32,2048]{1,0:T(8,128)(2,1)S(1)}, bf16[32,2048]{1,0:T(8,128)(2,1)S(1)}, u32[]{:S(2)}, u32[]{:S(2)}) collective-permute-start(bf16[32,2048]{1,0:T(8,128)(2,1)S(1)} %add_convert_fusion.5), channel_id=1, source_target_pairs={{0,8},{4,12},{8,0},{12,4},{1,9},{5,13},{9,1},{13,5},{2,10},{6,14},... | collective-permute-start | bytes 393224 | tf_op jit(solution)/shard_map/ppermute | solution.py:27
  150.5 9.8 %collective-permute-start.31 = (bf16[64,2048]{1,0:T(8,128)(2,1)S(1)}, bf16[64,2048]{1,0:T(8,128)(2,1)S(1)}, u32[]{:S(2)}, u32[]{:S(2)}) collective-permute-start(bf16[64,2048]{1,0:T(8,128)(2,1)S(1)} %add_convert_fusion.1), channel_id=1, source_target_pairs={{0,2},{2,0},{1,3},{3,1},{4,6},{6,4},{5,7},{7,5},{8,10},{10,8},{9,1... | collective-permute-start | bytes 786440 | tf_op jit(solution)/shard_map/ppermute | solution.py:27
  154.3 9.7 %collective-permute-start.32 = (bf16[32,2048]{1,0:T(8,128)(2,1)S(1)}, bf16[32,2048]{1,0:T(8,128)(2,1)S(1)}, u32[]{:S(2)}, u32[]{:S(2)}) collective-permute-start(bf16[32,2048]{1,0:T(8,128)(2,1)S(1)} %add_convert_fusion.4), channel_id=1, source_target_pairs={{0,8},{4,12},{8,0},{12,4},{1,9},{5,13},{9,1},{13,5},{2,10},{6,14},... | collective-permute-start | bytes 393224 | tf_op jit(solution)/shard_map/ppermute | solution.py:27
  (21 other events, 284.4 us)

commit v11 on v10

--- a/solution.py
+++ b/solution.py
@@ -34,67 +34,81 @@
     return lax.ppermute(passed, "pool", [(0, 2), (3, 1), (1, 0), (2, 3)])
 
 
-def project_kernel(block_count, share_count, share, *refs):
+def project_kernel(block_count, flips, share, *refs):
     blocks, weight, outs = refs[:block_count], refs[block_count], refs[block_count + 1 :]
     picked = []
-    for flip in range(share_count):
+    for flip in flips:
         for block in blocks:
-            part_rows = block.shape[0] // share_count
+            part_rows = block.shape[0] // len(flips)
             start = pl.multiple_of((share[0] ^ flip) * part_rows, part_rows)
             picked.append(block[pl.ds(start, part_rows), :])
     product = jnp.dot(
         jnp.concatenate(picked, axis=0), weight[...], preferred_element_type=jnp.float32
     )
-    rows = product.shape[0] // share_count
-    for flip in range(share_count):
-        outs[flip][...] = product[flip * rows : (flip + 1) * rows].astype(outs[flip].dtype)
-
-
-def project_out(blocks, out_weight):
+    rows = product.shape[0] // len(outs)
+    for i, out in enumerate(outs):
+        out[...] = product[i * rows : (i + 1) * rows].astype(out.dtype)
+
+
+def project_out(blocks, out_weight, direct=False):
     axes = ("heads", "sub")
     share_count = lax.axis_size(axes)
     share = lax.axis_index(axes).astype(jnp.int32).reshape(1)
     depth, columns = out_weight.shape
-    rows = sum(block.shape[0] for block in blocks) // share_count
+    flips = [*range(0, share_count, 2), *range(1, share_count, 2)]
+    count = share_count if direct else 2
+    rows = sum(block.shape[0] for block in blocks) // count
     tile = min(columns, 512)
     whole = pl.BlockSpec(memory_space=pltpu.VMEM)
     return pl.pallas_call(
-        functools.partial(project_kernel, len(blocks), share_count),
+        functools.partial(
+            project_kernel, len(blocks), list(range(share_count)) if direct else flips
+        ),
         grid=(columns // tile,),
         in_specs=[pl.BlockSpec(memory_space=pltpu.SMEM)]
         + [whole for _ in blocks]
         + [pl.BlockSpec((depth, tile), lambda n: (0, n))],
-        out_specs=[pl.BlockSpec((rows, tile), lambda n: (0, n))] * share_count,
+        out_specs=[pl.BlockSpec((rows, tile), lambda n: (0, n))] * count,
         out_shape=[
-            jax.ShapeDtypeStruct((rows, columns), jnp.bfloat16 if flip else jnp.float32)
-            for flip in range(share_count)
+            jax.ShapeDtypeStruct((rows, columns), jnp.bfloat16 if i else jnp.float32)
+            for i in range(count)
         ],
         compiler_params=pltpu.CompilerParams(vmem_limit_bytes=32 * 1024 * 1024),
         cost_estimate=LIGHT,
     )(share, *blocks, out_weight)
 
 
-def send_shares(pieces):
+def send_direct(pieces):
     axes = ("heads", "sub")
     return [pieces[0]] + [swap(pieces[flip], axes, flip) for flip in range(1, len(pieces))]
 
 
+def add_direct(pieces):
+    return sum(piece.astype(jnp.float32) for piece in pieces).astype(jnp.bfloat16)
+
+
+def send_sub(pieces):
+    keep, away = pieces
+    return keep, swap(away, "sub", 1)
+
+
+def send_heads(pieces):
+    keep, got = pieces
+    heads_size = lax.axis_size("heads")
+    rows = keep.shape[0] // heads_size
+    received = []
+    for flip in range(1, heads_size):
+        part = slice(flip * rows, (flip + 1) * rows)
+        both = keep[part] + got[part].astype(jnp.float32)
+        received.append(swap(both.astype(jnp.bfloat16), "heads", flip))
+    return keep, got, received
+
+
 def add_shares(pieces):
-    return sum(piece.astype(jnp.float32) for piece in pieces).astype(jnp.bfloat16)
-
-
-def sum_in_turn(pieces):
-    sub_size = lax.axis_size("sub")
-    by_sub = []
-    for first in range(0, len(pieces), sub_size):
-        total = pieces[first].astype(jnp.float32)
-        for flip in range(1, sub_size):
-            total = total + swap(pieces[first + flip], "sub", flip).astype(jnp.float32)
-        by_sub.append(total)
-    total = by_sub[0]
-    for flip in range(1, len(by_sub)):
-        total = total + swap(by_sub[flip].astype(jnp.bfloat16), "heads", flip).astype(jnp.float32)
-    return total.astype(jnp.bfloat16)
+    keep, got, received = pieces
+    rows = keep.shape[0] // (len(received) + 1)
+    total = keep[:rows] + got[:rows].astype(jnp.float32)
+    return sum((part.astype(jnp.float32) for part in received), total).astype(jnp.bfloat16)
 
 
 def find_blocks(place_holder, place_block, serving_request, items):
@@ -253,7 +267,11 @@
         outputs = []
         for chunk in range(len(chunk_rows)):
             rows = lax.all_gather(attended(chunk), "pool", axis=0)
-            mine = add_shares(send_shares(project_out([rows[i] for i in range(pool_size)], out_weight)))
+            mine = add_direct(
+                send_direct(
+                    project_out([rows[i] for i in range(pool_size)], out_weight, direct=True)
+                )
+            )
             mine = mine.reshape(pool_size, -1, columns)
             back = lax.all_to_all(mine, "pool", split_axis=0, concat_axis=0, tiled=True)
             outputs.append(jnp.moveaxis(back, 0, 1).reshape(-1, pool_size * columns))
@@ -266,23 +284,24 @@
     own = project_out([first, last], out_weight)
     across0, beside0, own = tie((across0, beside0, own))
     second0 = second_hop(first, across0)
-    near0 = send_shares(project_out([beside0, across0], out_weight))
+    near0 = send_direct(project_out([beside0, across0], out_weight, direct=True))
     across1, beside1, near0 = tie((across1, beside1, near0))
     second1 = second_hop(last, across1)
     many, few = chunk_rows
-    near0 = add_shares(near0)
+    near0 = add_direct(near0)
     back0 = swap(near0[:many], "pool", 1), swap(near0[many:], "pool", 3)
-    near1 = send_shares(project_out([beside1, across1], out_weight))
-    second0, near1, back0 = tie((second0, near1, back0))
-    far0 = send_shares(project_out([second0], out_weight))
+    near1 = send_sub(project_out([beside1, across1], out_weight))
+    second0, near1 = tie((second0, near1))
+    near1 = send_heads(near1)
+    far0 = send_heads(send_sub(project_out([second0], out_weight)))
+    second1, near1, back0, far0, own = tie((second1, near1, back0, far0, own))
+    back_second0 = swap(add_shares(far0), "pool", 2)
     near1 = add_shares(near1)
     back1 = swap(near1[:few], "pool", 1), swap(near1[few:], "pool", 3)
-    second1, far0, back1 = tie((second1, far0, back1))
-    back_second0 = swap(add_shares(far0), "pool", 2)
-    far1 = send_shares(project_out([second1], out_weight))
-    back_second0, far1 = tie((back_second0, far1))
+    far1 = send_heads(send_sub(project_out([second1], out_weight)))
+    back_second0, back1, far1 = tie((back_second0, back1, far1))
     back_second1 = swap(add_shares(far1), "pool", 2)
-    own = sum_in_turn(own)
+    own = add_shares(send_heads(send_sub(own)))
     backs = [(0, 1, back0[0]), (0, 3, back0[1]), (many, 1, back1[0]), (many, 3, back1[1])]
     backs += [(0, 2, back_second0), (0, 0, own), (many, 2, back_second1)]
     output = jnp.zeros((part_rows, pool_size * columns), jnp.bfloat16)

time: 165 us -> 168 us (1.018)
  waiting for transfers between devices: 80.8 us -> 64.7 us
  local copies, waits for them, and re-layouts: 13.9 us -> 22.7 us
  starting transfers between devices: 35.3 us -> 43.6 us
  other arithmetic: 2.35 us -> 4.08 us
    ppermute x31 -> x27, waiting for transfers between devices: 80.8 us -> 53.4 us  [swap(): lax.ppermute(values, axis, [(i, i ^ flip) for i in range(lax.axis_size(ax...]
    ppermute x2, starting transfers between devices: 0.81 us -> 12.2 us  [second_hop(): return lax.ppermute(passed, 'pool', [(0, 2), (3, 1), (1, 0), (2, 3)])]
    ppermute x2, waiting for transfers between devices: 0.01 us -> 11.3 us  [second_hop(): return lax.ppermute(passed, 'pool', [(0, 2), (3, 1), (1, 0), (2, 3)])]
    unnamed x24 -> x42, local copies, waits for them, and re-layouts: 7.46 us -> 12.6 us
    ppermute x31 -> x27, starting transfers between devices: 34.5 us -> 31.4 us  [swap(): lax.ppermute(values, axis, [(i, i ^ flip) for i in range(lax.axis_size(ax...]
    dynamic_update_slice x6, local copies, waits for them, and re-layouts: 0.73 us -> 2.54 us  [per_device(): lax.dynamic_update_slice(output, block, (row, (pool_index ^ flip) * colum...]
  transfers between devices with their start and end apart: 33 -> 29, of which waited for: 18 -> 13; matrix products, arithmetic and copies ran while one was open for 1% -> 3% of each run, Pallas kernels for 14% -> 13%
where the time goes in v11:
time: 168 us; the launch traced here: 167 us
  waiting for transfers between devices  64.7 us (39%)
  starting transfers between devices  43.6 us (26%)
  Pallas kernels  29.8 us (18%)
  local copies, waits for them, and re-layouts  22.7 us (14%)
  other arithmetic  4.08 us (2%)
  matrix products  1.94 us (1%)
    ppermute x27, waiting for transfers between devices, swap(): lax.ppermute(values, axis, [(i, i ^ flip) for i in range(lax.axis_size(ax...  53.4 us
    ppermute x27, starting transfers between devices, swap(): lax.ppermute(values, axis, [(i, i ^ flip) for i in range(lax.axis_size(ax...  31.4 us
    pallas_call x5, Pallas kernels, project_out(): pl.pallas_call(functools.partial(project_kernel, len(blocks), list(range(...  17.5 us
    unnamed x42, local copies, waits for them, and re-layouts  12.6 us
    pallas_call x2, Pallas kernels, attend(): pl.pallas_call(functools.partial(attend_kernel, len(parts)), grid=(reques...  12.4 us
    ppermute x2, starting transfers between devices, second_hop(): return lax.ppermute(passed, 'pool', [(0, 2), (3, 1), (1, 0), (2, 3)])  12.2 us
    ppermute x2, waiting for transfers between devices, second_hop(): return lax.ppermute(passed, 'pool', [(0, 2), (3, 1), (1, 0), (2, 3)])  11.3 us
  transfers between devices with their start and end apart: 29, of which 13 were waited for; matrix products, arithmetic and copies ran while one was open for 3% of the time, Pallas kernels for 13%

profile of v11, /device:TPU:0, one launch (start us, length us, event | category | flops | bytes accessed | tf_op | source)
XLA Modules:
  0.0 167.3 jit_solution(2415270426496020838)
XLA Ops:
  3.7 2.8 %gather_fusion.1 = bf16[32,32,512]{2,1,0:T(8,128)(2,1)S(1)} fusion(bf16[128,32,512]{2,1,0:T(8,128)(2,1)} %bitcast.38, s32[1024]{0:T(1024)S(1)} %pad_clamp_fusion.1), kind=kCustom, calls=%fused_computation.1 | custom fusion | bytes 2097280 | tf_op jit(solution)/shard_map/gather | solution.py:139
  7.4 3.0 %collective-permute-start = (bf16[8,32,512]{2,1,0:T(8,128)(2,1)}, bf16[8,32,512]{2,1,0:T(8,128)(2,1)S(1)}, u32[]{:S(2)}, u32[]{:S(2)}) collective-permute-start(bf16[8,32,512]{2,1,0:T(8,128)(2,1)} %get-tuple-element.97), channel_id=1, source_target_pairs={{0,4},{4,0},{8,12},{12,8},{1,5},{5,1},{9,13},{13,9},{2,6},{6,2},{1... | collective-permute-start | bytes 786440 | tf_op jit(solution)/shard_map/ppermute | solution.py:27
  13.8 8.0 %collective-permute-done = bf16[8,32,512]{2,1,0:T(8,128)(2,1)S(1)} collective-permute-done((bf16[8,32,512]{2,1,0:T(8,128)(2,1)}, bf16[8,32,512]{2,1,0:T(8,128)(2,1)S(1)}, u32[]{:S(2)}, u32[]{:S(2)}) %collective-permute-start) | collective-permute-done | bytes 262176 | tf_op jit(solution)/shard_map/ppermute | solution.py:27
  21.8 10.3 %collective-permute-done.1 = bf16[8,32,512]{2,1,0:T(8,128)(2,1)} collective-permute-done((bf16[8,32,512]{2,1,0:T(8,128)(2,1)}, bf16[8,32,512]{2,1,0:T(8,128)(2,1)}, u32[]{:S(2)}, u32[]{:S(2)}) %collective-permute-start.1) | collective-permute-done | bytes 262176 | tf_op jit(solution)/shard_map/ppermute | solution.py:27
  37.6 9.7 %collective-permute-done.4.refs_2_ = bf16[2,256,512]{2,1,0:T(8,128)(2,1)S(1)} collective-permute-done((bf16[2,256,512]{2,1,0:T(8,128)(2,1)S(1)}, bf16[2,256,512]{2,1,0:T(8,128)(2,1)S(1)}, u32[]{:S(2)}, u32[]{:S(2)}) %collective-permute-start.4) | collective-permute-done | bytes 524320 | tf_op jit(solution)/shard_map/ppermute | solution.py:27
  49.2 6.2 %shard_map.101.refs_0_ = bf16[128,2048]{1,0:T(8,128)(2,1)S(1)} custom-call(s32[3]{0:T(128)S(1)} %pad_add_fusion.scalars, bf16[2,2,64,2048]{3,2,1,0:T(8,128)(2,1)S(1)} %bitcast.32, bf16[2,256,512]{2,1,0:T(8,128)(2,1)S(1)} %bitcast.30, bf16[2,256,512]{2,1,0:T(8,128)(2,1)S(1)} %collective-permute-done.3.refs_1_, ...), custom_call_target="tpu_custom_call" | custom-call | flops 1 | bytes 1 | tf_op jit(solution)/shard_map/pallas_call | solution.py:194
  56.8 6.3 %collective-permute-start.9 = (bf16[128,2048]{1,0:T(8,128)(2,1)S(1)}, bf16[128,2048]{1,0:T(8,128)(2,1)}, u32[]{:S(2)}, u32[]{:S(2)}) collective-permute-start(bf16[128,2048]{1,0:T(8,128)(2,1)S(1)} %shard_map.101.refs_0_), channel_id=1, source_target_pairs={{0,4},{4,0},{8,12},{12,8},{1,5},{5,1},{9,13},{13,9},{2,6},{6,2},{1... | collective-permute-start | bytes 1572872 | tf_op jit(solution)/shard_map/ppermute | solution.py:27
  63.1 6.2 %shard_map.100.refs_1_ = bf16[128,2048]{1,0:T(8,128)(2,1)S(1)} custom-call(s32[3]{0:T(128)S(1)} %pad_add_fusion.scalars, bf16[2,2,64,2048]{3,2,1,0:T(8,128)(2,1)S(1)} %bitcast.33, bf16[2,256,512]{2,1,0:T(8,128)(2,1)S(1)} %bitcast.31, bf16[2,256,512]{2,1,0:T(8,128)(2,1)S(1)} %collective-permute-done.3.refs_1_, ...), custom_call_target="tpu_custom_call" | custom-call | flops 1 | bytes 1 | tf_op jit(solution)/shard_map/pallas_call | solution.py:194
  70.7 3.4 %copy-done.1 = bf16[2048,2048]{1,0:T(8,128)(2,1)S(1)} copy-done((bf16[2048,2048]{1,0:T(8,128)(2,1)S(1)}, bf16[2048,2048]{1,0:T(8,128)(2,1)}, u32[]{:S(2)}) %copy-start.1) | copy-done | bytes 8388632
  74.1 3.7 %shard_map.102 = (f32[128,2048]{1,0:T(8,128)S(1)}, bf16[128,2048]{1,0:T(8,128)(2,1)S(1)}) custom-call(s32[1]{0:T(128)} %bitcast.6.share, bf16[128,2048]{1,0:T(8,128)(2,1)S(1)} %shard_map.101.refs_0_, bf16[128,2048]{1,0:T(8,128)(2,1)S(1)} %shard_map.100.refs_1_, bf16[2048,2048]{1,0:T(8,128)(2,1)S(1)} %copy-done.1), custom_call_target="tpu_custom_call" | custom-call | flops 1 | bytes 1 | tf_op jit(solution)/shard_map/pallas_call | solution.py:63
  78.6 5.0 %collective-permute-done.9.refs_0_ = bf16[128,2048]{1,0:T(8,128)(2,1)} collective-permute-done((bf16[128,2048]{1,0:T(8,128)(2,1)S(1)}, bf16[128,2048]{1,0:T(8,128)(2,1)}, u32[]{:S(2)}, u32[]{:S(2)}) %collective-permute-start.9) | collective-permute-done | bytes 524320 | tf_op jit(solution)/shard_map/ppermute | solution.py:27
  83.5 3.4 %copy-done.2 = bf16[2048,2048]{1,0:T(8,128)(2,1)S(1)} copy-done((bf16[2048,2048]{1,0:T(8,128)(2,1)S(1)}, bf16[2048,2048]{1,0:T(8,128)(2,1)}, u32[]{:S(2)}) %copy-start.2) | copy-done | bytes 8388632
  86.9 4.8 %shard_map.103 = (f32[64,2048]{1,0:T(8,128)S(1)}, bf16[64,2048]{1,0:T(8,128)(2,1)S(1)}, bf16[64,2048]{1,0:T(8,128)(2,1)S(1)}, bf16[64,2048]{1,0:T(8,128)(2,1)S(1)}) custom-call(s32[1]{0:T(128)} %bitcast.6.share, bf16[128,2048]{1,0:T(8,128)(2,1)} %collective-permute-done.9.refs_0_, bf16[128,2048]{1,0:T(8,128)(2,1)} %collective-permute-done.8.refs_1_, ...), custom_call_target="tpu_custom_call" | custom-call | flops 1 | bytes 1 | tf_op jit(solution)/shard_map/pallas_call | solution.py:63
  94.6 10.8 %collective-permute-start.14 = (bf16[128,2048]{1,0:T(8,128)(2,1)S(1)}, bf16[128,2048]{1,0:T(8,128)(2,1)S(1)}, u32[]{:S(2)}, u32[]{:S(2)}) collective-permute-start(bf16[128,2048]{1,0:T(8,128)(2,1)S(1)} %broadcast_select_fusion), channel_id=1, source_target_pairs={{0,8},{12,4},{4,0},{8,12},{1,9},{13,5},{5,1},{9,13},{2,10},{14,6},... | collective-permute-start | bytes 1572872 | tf_op jit(solution)/shard_map/ppermute | solution.py:34
  105.7 3.7 %shard_map.104 = (f32[128,2048]{1,0:T(8,128)S(1)}, bf16[128,2048]{1,0:T(8,128)(2,1)S(1)}) custom-call(s32[1]{0:T(128)} %bitcast.6.share, bf16[128,2048]{1,0:T(8,128)(2,1)S(1)} %collective-permute-done.7.refs_0_, bf16[128,2048]{1,0:T(8,128)(2,1)S(1)} %collective-permute-done.6.refs_1_, bf16[2048,2048]{1,0:T(8,128)(2,1)S(1)} %bitcast.25), custom_call_target="tpu_custom_call" | custom-call | flops 1 | bytes 1 | tf_op jit(solution)/shard_map/pallas_call | solution.py:63
  114.9 3.3 %collective-permute-done.14.refs_0_ = bf16[128,2048]{1,0:T(8,128)(2,1)S(1)} collective-permute-done((bf16[128,2048]{1,0:T(8,128)(2,1)S(1)}, bf16[128,2048]{1,0:T(8,128)(2,1)S(1)}, u32[]{:S(2)}, u32[]{:S(2)}) %collective-permute-start.14) | collective-permute-done | bytes 524320 | tf_op jit(solution)/shard_map/ppermute | solution.py:34
  118.2 2.7 %shard_map.105 = (f32[64,2048]{1,0:T(8,128)S(1)}, bf16[64,2048]{1,0:T(8,128)(2,1)S(1)}) custom-call(s32[1]{0:T(128)} %bitcast.6.share, bf16[128,2048]{1,0:T(8,128)(2,1)S(1)} %collective-permute-done.14.refs_0_, bf16[2048,2048]{1,0:T(8,128)(2,1)S(1)} %bitcast.25), custom_call_target="tpu_custom_call" | custom-call | flops 1 | bytes 1 | tf_op jit(solution)/shard_map/pallas_call | solution.py:63
  126.4 8.0 %collective-permute-done.13.refs_0_ = bf16[128,2048]{1,0:T(8,128)(2,1)S(1)} collective-permute-done((bf16[128,2048]{1,0:T(8,128)(2,1)}, bf16[128,2048]{1,0:T(8,128)(2,1)S(1)}, u32[]{:S(2)}, u32[]{:S(2)}) %collective-permute-start.13) | collective-permute-done | bytes 524320 | tf_op jit(solution)/shard_map/ppermute | solution.py:34
  134.5 3.4 %copy-done.3 = bf16[2048,2048]{1,0:T(8,128)(2,1)S(1)} copy-done((bf16[2048,2048]{1,0:T(8,128)(2,1)S(1)}, bf16[2048,2048]{1,0:T(8,128)(2,1)}, u32[]{:S(2)}) %copy-start.3) | copy-done | bytes 8388632
  137.9 2.7 %shard_map.106 = (f32[64,2048]{1,0:T(8,128)S(1)}, bf16[64,2048]{1,0:T(8,128)(2,1)S(1)}) custom-call(s32[1]{0:T(128)} %bitcast.6.share, bf16[128,2048]{1,0:T(8,128)(2,1)S(1)} %collective-permute-done.13.refs_0_, bf16[2048,2048]{1,0:T(8,128)(2,1)S(1)} %copy-done.3), custom_call_target="tpu_custom_call" | custom-call | flops 1 | bytes 1 | tf_op jit(solution)/shard_map/pallas_call | solution.py:63
  140.8 2.8 %collective-permute-start.22 = (bf16[32,2048]{1,0:T(8,128)(2,1)S(1)}, bf16[32,2048]{1,0:T(8,128)(2,1)S(1)}, u32[]{:S(2)}, u32[]{:S(2)}) collective-permute-start(bf16[32,2048]{1,0:T(8,128)(2,1)S(1)} %get-tuple-element.100), channel_id=1, source_target_pairs={{0,4},{4,0},{8,12},{12,8},{1,5},{5,1},{9,13},{13,9},{2,6},{6,2},{1... | collective-permute-start | bytes 393224 | tf_op jit(solution)/shard_map/ppermute | solution.py:27
  148.8 3.3 %collective-permute-done.23 = bf16[32,2048]{1,0:T(8,128)(2,1)S(1)} collective-permute-done((bf16[32,2048]{1,0:T(8,128)(2,1)S(1)}, bf16[32,2048]{1,0:T(8,128)(2,1)S(1)}, u32[]{:S(2)}, u32[]{:S(2)}) %collective-permute-start.23) | collective-permute-done | bytes 131104 | tf_op jit(solution)/shard_map/ppermute | solution.py:27
  152.1 5.3 %collective-permute-done.21 = bf16[32,2048]{1,0:T(8,128)(2,1)S(1)} collective-permute-done((bf16[32,2048]{1,0:T(8,128)(2,1)S(1)}, bf16[32,2048]{1,0:T(8,128)(2,1)S(1)}, u32[]{:S(2)}, u32[]{:S(2)}) %collective-permute-start.21) | collective-permute-done | bytes 131104 | tf_op jit(solution)/shard_map/ppermute | solution.py:27
  159.2 6.4 %collective-permute-done.27 = bf16[64,2048]{1,0:T(8,128)(2,1)S(1)} collective-permute-done((bf16[64,2048]{1,0:T(8,128)(2,1)S(1)}, bf16[64,2048]{1,0:T(8,128)(2,1)S(1)}, u32[]{:S(2)}, u32[]{:S(2)}) %collective-permute-start.27) | collective-permute-done | bytes 262176 | tf_op jit(solution)/shard_map/ppermute | solution.py:27
  (130 shorter events, 41.9 us)
Async XLA Ops:
  7.4 14.4 %collective-permute-start = (bf16[8,32,512]{2,1,0:T(8,128)(2,1)}, bf16[8,32,512]{2,1,0:T(8,128)(2,1)S(1)}, u32[]{:S(2)}, u32[]{:S(2)}) collective-permute-start(bf16[8,32,512]{2,1,0:T(8,128)(2,1)} %get-tuple-element.97), channel_id=1, source_target_pairs={{0,4},{4,0},{8,12},{12,8},{1,5},{5,1},{9,13},{13,9},{2,6},{6,2},{1... | collective-permute-start | bytes 786440 | tf_op jit(solution)/shard_map/ppermute | solution.py:27
  10.4 21.7 %collective-permute-start.1 = (bf16[8,32,512]{2,1,0:T(8,128)(2,1)}, bf16[8,32,512]{2,1,0:T(8,128)(2,1)}, u32[]{:S(2)}, u32[]{:S(2)}) collective-permute-start(bf16[8,32,512]{2,1,0:T(8,128)(2,1)} %get-tuple-element.96), channel_id=1, source_target_pairs={{0,8},{4,12},{8,0},{12,4},{1,9},{5,13},{9,1},{13,5},{2,10},{6,14},... | collective-permute-start | bytes 786440 | tf_op jit(solution)/shard_map/ppermute | solution.py:27
  13.0 19.1 %collective-permute-start.2 = (bf16[8,32,512]{2,1,0:T(8,128)(2,1)S(1)}, bf16[8,32,512]{2,1,0:T(8,128)(2,1)}, u32[]{:S(2)}, u32[]{:S(2)}) collective-permute-start(bf16[8,32,512]{2,1,0:T(8,128)(2,1)S(1)} %get-tuple-element.98), channel_id=1, source_target_pairs={{0,12},{4,8},{8,4},{12,0},{1,13},{5,9},{9,5},{13,1},{2,14},{6,10},... | collective-permute-start | bytes 786440 | tf_op jit(solution)/shard_map/ppermute | solution.py:27
  36.0 11.3 %collective-permute-start.4 = (bf16[2,256,512]{2,1,0:T(8,128)(2,1)S(1)}, bf16[2,256,512]{2,1,0:T(8,128)(2,1)S(1)}, u32[]{:S(2)}, u32[]{:S(2)}) collective-permute-start(bf16[2,256,512]{2,1,0:T(8,128)(2,1)S(1)} %bitcast.28), channel_id=1, source_target_pairs={{0,2},{2,0},{1,3},{3,1},{4,6},{6,4},{5,7},{7,5},{8,10},{10,8},{9,1... | collective-permute-start | bytes 1572872 | tf_op jit(solution)/shard_map/ppermute | solution.py:27
  37.6 9.7 %collective-permute-start.3 = (bf16[2,256,512]{2,1,0:T(8,128)(2,1)S(1)}, bf16[2,256,512]{2,1,0:T(8,128)(2,1)S(1)}, u32[]{:S(2)}, u32[]{:S(2)}) collective-permute-start(bf16[2,256,512]{2,1,0:T(8,128)(2,1)S(1)} %bitcast.29), channel_id=1, source_target_pairs={{0,1},{1,0},{2,3},{3,2},{4,5},{5,4},{6,7},{7,6},{8,9},{9,8},{10,11... | collective-permute-start | bytes 1572872 | tf_op jit(solution)/shard_map/ppermute | solution.py:27
  55.4 23.2 %collective-permute-start.8 = (bf16[128,2048]{1,0:T(8,128)(2,1)S(1)}, bf16[128,2048]{1,0:T(8,128)(2,1)}, u32[]{:S(2)}, u32[]{:S(2)}) collective-permute-start(bf16[128,2048]{1,0:T(8,128)(2,1)S(1)} %shard_map.101.refs_0_), channel_id=1, source_target_pairs={{0,12},{4,8},{8,4},{12,0},{1,13},{5,9},{9,5},{13,1},{2,14},{6,10},... | collective-permute-start | bytes 1572872 | tf_op jit(solution)/shard_map/ppermute | solution.py:27
  56.8 26.7 %collective-permute-start.9 = (bf16[128,2048]{1,0:T(8,128)(2,1)S(1)}, bf16[128,2048]{1,0:T(8,128)(2,1)}, u32[]{:S(2)}, u32[]{:S(2)}) collective-permute-start(bf16[128,2048]{1,0:T(8,128)(2,1)S(1)} %shard_map.101.refs_0_), channel_id=1, source_target_pairs={{0,4},{4,0},{8,12},{12,8},{1,5},{5,1},{9,13},{13,9},{2,6},{6,2},{1... | collective-permute-start | bytes 1572872 | tf_op jit(solution)/shard_map/ppermute | solution.py:27
  69.3 25.3 %collective-permute-start.6 = (bf16[128,2048]{1,0:T(8,128)(2,1)S(1)}, bf16[128,2048]{1,0:T(8,128)(2,1)S(1)}, u32[]{:S(2)}, u32[]{:S(2)}) collective-permute-start(bf16[128,2048]{1,0:T(8,128)(2,1)S(1)} %shard_map.100.refs_1_), channel_id=1, source_target_pairs={{0,12},{4,8},{8,4},{12,0},{1,13},{5,9},{9,5},{13,1},{2,14},{6,10},... | collective-permute-start | bytes 1572872 | tf_op jit(solution)/shard_map/ppermute | solution.py:27
  70.7 34.7 %collective-permute-start.7 = (bf16[128,2048]{1,0:T(8,128)(2,1)S(1)}, bf16[128,2048]{1,0:T(8,128)(2,1)S(1)}, u32[]{:S(2)}, u32[]{:S(2)}) collective-permute-start(bf16[128,2048]{1,0:T(8,128)(2,1)S(1)} %shard_map.100.refs_1_), channel_id=1, source_target_pairs={{0,4},{4,0},{8,12},{12,8},{1,5},{5,1},{9,13},{13,9},{2,6},{6,2},{1... | collective-permute-start | bytes 1572872 | tf_op jit(solution)/shard_map/ppermute | solution.py:27
  91.7 13.7 %collective-permute-start.10 = (bf16[64,2048]{1,0:T(8,128)(2,1)S(1)}, bf16[64,2048]{1,0:T(8,128)(2,1)S(1)}, u32[]{:S(2)}, u32[]{:S(2)}) collective-permute-start(bf16[64,2048]{1,0:T(8,128)(2,1)S(1)} %get-tuple-element.58), channel_id=1, source_target_pairs={{0,1},{1,0},{2,3},{3,2},{4,5},{5,4},{6,7},{7,6},{8,9},{9,8},{10,11... | collective-permute-start | bytes 786440 | tf_op jit(solution)/shard_map/ppermute | solution.py:27
  91.8 13.6 %collective-permute-start.11 = (bf16[64,2048]{1,0:T(8,128)(2,1)S(1)}, bf16[64,2048]{1,0:T(8,128)(2,1)S(1)}, u32[]{:S(2)}, u32[]{:S(2)}) collective-permute-start(bf16[64,2048]{1,0:T(8,128)(2,1)S(1)} %get-tuple-element.59), channel_id=1, source_target_pairs={{0,2},{1,3},{2,0},{3,1},{4,6},{5,7},{6,4},{7,5},{8,10},{9,11},{10,... | collective-permute-start | bytes 786440 | tf_op jit(solution)/shard_map/ppermute | solution.py:27
  93.4 12.3 %collective-permute-start.12 = (bf16[64,2048]{1,0:T(8,128)(2,1)S(1)}, bf16[64,2048]{1,0:T(8,128)(2,1)S(1)}, u32[]{:S(2)}, u32[]{:S(2)}) collective-permute-start(bf16[64,2048]{1,0:T(8,128)(2,1)S(1)} %get-tuple-element.60), channel_id=1, source_target_pairs={{0,3},{1,2},{2,1},{3,0},{4,7},{5,6},{6,5},{7,4},{8,11},{9,10},{10,... | collective-permute-start | bytes 786440 | tf_op jit(solution)/shard_map/ppermute | solution.py:27
  94.6 23.6 %collective-permute-start.14 = (bf16[128,2048]{1,0:T(8,128)(2,1)S(1)}, bf16[128,2048]{1,0:T(8,128)(2,1)S(1)}, u32[]{:S(2)}, u32[]{:S(2)}) collective-permute-start(bf16[128,2048]{1,0:T(8,128)(2,1)S(1)} %broadcast_select_fusion), channel_id=1, source_target_pairs={{0,8},{12,4},{4,0},{8,12},{1,9},{13,5},{5,1},{9,13},{2,10},{14,6},... | collective-permute-start | bytes 1572872 | tf_op jit(solution)/shard_map/ppermute | solution.py:34
  109.4 8.8 %collective-permute-start.15 = (bf16[128,2048]{1,0:T(8,128)(2,1)S(1)}, bf16[128,2048]{1,0:T(8,128)(2,1)S(1)}, u32[]{:S(2)}, u32[]{:S(2)}) collective-permute-start(bf16[128,2048]{1,0:T(8,128)(2,1)S(1)} %get-tuple-element.64), channel_id=1, source_target_pairs={{0,1},{1,0},{2,3},{3,2},{4,5},{5,4},{6,7},{7,6},{8,9},{9,8},{10,11... | collective-permute-start | bytes 1572872 | tf_op jit(solution)/shard_map/ppermute | solution.py:27
  110.6 13.5 %collective-permute-start.17 = (bf16[32,2048]{1,0:T(8,128)(2,1)}, bf16[32,2048]{1,0:T(8,128)(2,1)}, u32[]{:S(2)}, u32[]{:S(2)}) collective-permute-start(bf16[32,2048]{1,0:T(8,128)(2,1)} %get-tuple-element.102), channel_id=1, source_target_pairs={{0,4},{4,0},{8,12},{12,8},{1,5},{5,1},{9,13},{13,9},{2,6},{6,2},{1... | collective-permute-start | bytes 393224 | tf_op jit(solution)/shard_map/ppermute | solution.py:27
  111.1 15.3 %collective-permute-start.18 = (bf16[32,2048]{1,0:T(8,128)(2,1)}, bf16[32,2048]{1,0:T(8,128)(2,1)}, u32[]{:S(2)}, u32[]{:S(2)}) collective-permute-start(bf16[32,2048]{1,0:T(8,128)(2,1)} %get-tuple-element.101), channel_id=1, source_target_pairs={{0,12},{4,8},{8,4},{12,0},{1,13},{5,9},{9,5},{13,1},{2,14},{6,10},... | collective-permute-start | bytes 393224 | tf_op jit(solution)/shard_map/ppermute | solution.py:27
  113.5 21.0 %collective-permute-start.13 = (bf16[128,2048]{1,0:T(8,128)(2,1)}, bf16[128,2048]{1,0:T(8,128)(2,1)S(1)}, u32[]{:S(2)}, u32[]{:S(2)}) collective-permute-start(bf16[128,2048]{1,0:T(8,128)(2,1)} %broadcast_select_fusion.1), channel_id=1, source_target_pairs={{0,8},{12,4},{4,0},{8,12},{1,9},{13,5},{5,1},{9,13},{2,10},{14,6},... | collective-permute-start | bytes 1572872 | tf_op jit(solution)/shard_map/ppermute | solution.py:34
  121.1 13.4 %collective-permute-start.16 = (bf16[64,2048]{1,0:T(8,128)(2,1)S(1)}, bf16[64,2048]{1,0:T(8,128)(2,1)S(1)}, u32[]{:S(2)}, u32[]{:S(2)}) collective-permute-start(bf16[64,2048]{1,0:T(8,128)(2,1)S(1)} %add_convert_fusion.4), channel_id=1, source_target_pairs={{0,2},{2,0},{1,3},{3,1},{4,6},{6,4},{5,7},{7,5},{8,10},{10,8},{9,1... | collective-permute-start | bytes 786440 | tf_op jit(solution)/shard_map/ppermute | solution.py:27
  122.6 11.8 %collective-permute-start.20 = (bf16[32,2048]{1,0:T(8,128)(2,1)S(1)}, bf16[32,2048]{1,0:T(8,128)(2,1)S(1)}, u32[]{:S(2)}, u32[]{:S(2)}) collective-permute-start(bf16[32,2048]{1,0:T(8,128)(2,1)S(1)} %add_convert_fusion.8), channel_id=1, source_target_pairs={{0,2},{2,0},{1,3},{3,1},{4,6},{6,4},{5,7},{7,5},{8,10},{10,8},{9,1... | collective-permute-start | bytes 393224 | tf_op jit(solution)/shard_map/ppermute | solution.py:27
  143.6 8.5 %collective-permute-start.23 = (bf16[32,2048]{1,0:T(8,128)(2,1)S(1)}, bf16[32,2048]{1,0:T(8,128)(2,1)S(1)}, u32[]{:S(2)}, u32[]{:S(2)}) collective-permute-start(bf16[32,2048]{1,0:T(8,128)(2,1)S(1)} %get-tuple-element.99), channel_id=1, source_target_pairs={{0,12},{4,8},{8,4},{12,0},{1,13},{5,9},{9,5},{13,1},{2,14},{6,10},... | collective-permute-start | bytes 393224 | tf_op jit(solution)/shard_map/ppermute | solution.py:27
  145.0 12.4 %collective-permute-start.21 = (bf16[32,2048]{1,0:T(8,128)(2,1)S(1)}, bf16[32,2048]{1,0:T(8,128)(2,1)S(1)}, u32[]{:S(2)}, u32[]{:S(2)}) collective-permute-start(bf16[32,2048]{1,0:T(8,128)(2,1)S(1)} %add_convert_fusion.7), channel_id=1, source_target_pairs={{0,8},{4,12},{8,0},{12,4},{1,9},{5,13},{9,1},{13,5},{2,10},{6,14},... | collective-permute-start | bytes 393224 | tf_op jit(solution)/shard_map/ppermute | solution.py:27
  145.2 12.3 %collective-permute-start.26 = (bf16[128,2048]{1,0:T(8,128)(2,1)S(1)}, bf16[128,2048]{1,0:T(8,128)(2,1)S(1)}, u32[]{:S(2)}, u32[]{:S(2)}) collective-permute-start(bf16[128,2048]{1,0:T(8,128)(2,1)S(1)} %copy-done.10), channel_id=1, source_target_pairs={{0,1},{1,0},{2,3},{3,2},{4,5},{5,4},{6,7},{7,6},{8,9},{9,8},{10,11... | collective-permute-start | bytes 1572872 | tf_op jit(solution)/shard_map/ppermute | solution.py:27
  146.3 11.1 %collective-permute-start.25 = (bf16[32,2048]{1,0:T(8,128)(2,1)S(1)}, bf16[32,2048]{1,0:T(8,128)(2,1)S(1)}, u32[]{:S(2)}, u32[]{:S(2)}) collective-permute-start(bf16[32,2048]{1,0:T(8,128)(2,1)S(1)} %add_convert_fusion.6), channel_id=1, source_target_pairs={{0,2},{2,0},{1,3},{3,1},{4,6},{6,4},{5,7},{7,5},{8,10},{10,8},{9,1... | collective-permute-start | bytes 393224 | tf_op jit(solution)/shard_map/ppermute | solution.py:27
  157.4 8.2 %collective-permute-start.28 = (bf16[32,2048]{1,0:T(8,128)(2,1)S(1)}, bf16[32,2048]{1,0:T(8,128)(2,1)S(1)}, u32[]{:S(2)}, u32[]{:S(2)}) collective-permute-start(bf16[32,2048]{1,0:T(8,128)(2,1)S(1)} %add_convert_fusion.5), channel_id=1, source_target_pairs={{0,8},{4,12},{8,0},{12,4},{1,9},{5,13},{9,1},{13,5},{2,10},{6,14},... | collective-permute-start | bytes 393224 | tf_op jit(solution)/shard_map/ppermute | solution.py:27
  (26 other events, 301.8 us)

commit v12 on v11

--- a/solution.py
+++ b/solution.py
@@ -73,7 +73,7 @@
             jax.ShapeDtypeStruct((rows, columns), jnp.bfloat16 if i else jnp.float32)
             for i in range(count)
         ],
-        compiler_params=pltpu.CompilerParams(vmem_limit_bytes=32 * 1024 * 1024),
+        compiler_params=pltpu.CompilerParams(vmem_limit_bytes=16 * 1024 * 1024),
         cost_estimate=LIGHT,
     )(share, *blocks, out_weight)
 
@@ -209,7 +209,7 @@
             pltpu.VMEM((slots, head_width), jnp.bfloat16),
             pltpu.VMEM((slots, 2 * head_width), jnp.bfloat16),
         ],
-        compiler_params=pltpu.CompilerParams(vmem_limit_bytes=32 * 1024 * 1024),
+        compiler_params=pltpu.CompilerParams(vmem_limit_bytes=16 * 1024 * 1024),
         cost_estimate=LIGHT,
     )(scalars, queries, *parts, kv_flat, q_gain, k_gain)
 
@@ -285,25 +285,27 @@
     across0, beside0, own = tie((across0, beside0, own))
     second0 = second_hop(first, across0)
     near0 = send_direct(project_out([beside0, across0], out_weight, direct=True))
-    across1, beside1, near0 = tie((across1, beside1, near0))
+    across1, beside1, near0, own = tie((across1, beside1, near0, own))
     second1 = second_hop(last, across1)
-    many, few = chunk_rows
-    near0 = add_direct(near0)
-    back0 = swap(near0[:many], "pool", 1), swap(near0[many:], "pool", 3)
     near1 = send_sub(project_out([beside1, across1], out_weight))
     second0, near1 = tie((second0, near1))
     near1 = send_heads(near1)
     far0 = send_heads(send_sub(project_out([second0], out_weight)))
-    second1, near1, back0, far0, own = tie((second1, near1, back0, far0, own))
+    near0 = add_direct(near0)
+    own = send_heads(send_sub(own))
+    second1, near0, near1, far0, own = tie((second1, near0, near1, far0, own))
+    many, few = chunk_rows
+    near1 = add_shares(near1)
+    back_beside = swap(jnp.concatenate([near0[:many], near1[:few]]), "pool", 1)
+    back_across = swap(jnp.concatenate([near0[many:], near1[few:]]), "pool", 3)
     back_second0 = swap(add_shares(far0), "pool", 2)
-    near1 = add_shares(near1)
-    back1 = swap(near1[:few], "pool", 1), swap(near1[few:], "pool", 3)
-    far1 = send_heads(send_sub(project_out([second1], out_weight)))
-    back_second0, back1, far1 = tie((back_second0, back1, far1))
-    back_second1 = swap(add_shares(far1), "pool", 2)
-    own = add_shares(send_heads(send_sub(own)))
-    backs = [(0, 1, back0[0]), (0, 3, back0[1]), (many, 1, back1[0]), (many, 3, back1[1])]
-    backs += [(0, 2, back_second0), (0, 0, own), (many, 2, back_second1)]
+    far1 = send_direct(project_out([second1], out_weight, direct=True))
+    back_beside, back_across, back_second0, far1 = tie(
+        (back_beside, back_across, back_second0, far1)
+    )
+    back_second1 = swap(add_direct(far1), "pool", 2)
+    backs = [(0, 0, add_shares(own)), (0, 1, back_beside), (0, 3, back_across)]
+    backs += [(0, 2, back_second0), (many, 2, back_second1)]
     output = jnp.zeros((part_rows, pool_size * columns), jnp.bfloat16)
     for row, flip, block in backs:
         output = lax.dynamic_update_slice(output, block, (row, (pool_index ^ flip) * columns))

time: 168 us -> 164 us (0.976)
  waiting for transfers between devices: 64.7 us -> 80.5 us
  starting transfers between devices: 43.6 us -> 32 us
  local copies, waits for them, and re-layouts: 22.7 us -> 15.3 us
    ppermute x27 -> x26, waiting for transfers between devices: 53.4 us -> 73.9 us  [swap(): lax.ppermute(values, axis, [(i, i ^ flip) for i in range(lax.axis_size(ax...]
    ppermute x2, starting transfers between devices: 12.2 us -> 2.08 us  [second_hop(): return lax.ppermute(passed, 'pool', [(0, 2), (3, 1), (1, 0), (2, 3)])]
    ppermute x2, waiting for transfers between devices: 11.3 us -> 6.55 us  [second_hop(): return lax.ppermute(passed, 'pool', [(0, 2), (3, 1), (1, 0), (2, 3)])]
    unnamed x42 -> x30, local copies, waits for them, and re-layouts: 12.6 us -> 8.88 us
    dynamic_update_slice x6 -> x4, local copies, waits for them, and re-layouts: 2.54 us -> 0.73 us  [per_device(): lax.dynamic_update_slice(output, block, (row, (pool_index ^ flip) * colum...]
    ppermute x27 -> x26, starting transfers between devices: 31.4 us -> 29.9 us  [swap(): lax.ppermute(values, axis, [(i, i ^ flip) for i in range(lax.axis_size(ax...]
  transfers between devices with their start and end apart: 29 -> 28, of which waited for: 13 -> 14; matrix products, arithmetic and copies ran while one was open for 3% -> 2% of each run, Pallas kernels for 13% -> 15%
where the time goes in v12:
time: 164 us
  waiting for transfers between devices  80.5 us (49%)
  starting transfers between devices  32 us (20%)
  Pallas kernels  30 us (18%)
  local copies, waits for them, and re-layouts  15.3 us (9%)
  other arithmetic  3.6 us (2%)
  matrix products  1.94 us (1%)
    ppermute x26, waiting for transfers between devices, swap(): lax.ppermute(values, axis, [(i, i ^ flip) for i in range(lax.axis_size(ax...  73.9 us
    ppermute x26, starting transfers between devices, swap(): lax.ppermute(values, axis, [(i, i ^ flip) for i in range(lax.axis_size(ax...  29.9 us
    pallas_call x5, Pallas kernels, project_out(): pl.pallas_call(functools.partial(project_kernel, len(blocks), list(range(...  17.6 us
    pallas_call x2, Pallas kernels, attend(): pl.pallas_call(functools.partial(attend_kernel, len(parts)), grid=(reques...  12.4 us
    unnamed x30, local copies, waits for them, and re-layouts  8.88 us
    ppermute x2, waiting for transfers between devices, second_hop(): return lax.ppermute(passed, 'pool', [(0, 2), (3, 1), (1, 0), (2, 3)])  6.55 us
  transfers between devices with their start and end apart: 28, of which 14 were waited for; matrix products, arithmetic and copies ran while one was open for 2% of the time, Pallas kernels for 15%

profile of v12, /device:TPU:0, one launch (start us, length us, event | category | flops | bytes accessed | tf_op | source)
XLA Modules:
  0.0 163.7 jit_solution(16116254936167691175)
XLA Ops:
  3.7 2.8 %gather_fusion.1 = bf16[32,32,512]{2,1,0:T(8,128)(2,1)S(1)} fusion(bf16[128,32,512]{2,1,0:T(8,128)(2,1)} %bitcast.36, s32[1024]{0:T(1024)S(1)} %pad_clamp_fusion.1), kind=kCustom, calls=%fused_computation.1 | custom fusion | bytes 2097280 | tf_op jit(solution)/shard_map/gather | solution.py:139
  7.4 3.0 %collective-permute-start = (bf16[8,32,512]{2,1,0:T(8,128)(2,1)}, bf16[8,32,512]{2,1,0:T(8,128)(2,1)}, u32[]{:S(2)}, u32[]{:S(2)}) collective-permute-start(bf16[8,32,512]{2,1,0:T(8,128)(2,1)} %get-tuple-element.107), channel_id=1, source_target_pairs={{0,4},{4,0},{8,12},{12,8},{1,5},{5,1},{9,13},{13,9},{2,6},{6,2},{1... | collective-permute-start | bytes 786440 | tf_op jit(solution)/shard_map/ppermute | solution.py:27
  10.4 2.6 %collective-permute-start.1 = (bf16[8,32,512]{2,1,0:T(8,128)(2,1)}, bf16[8,32,512]{2,1,0:T(8,128)(2,1)S(1)}, u32[]{:S(2)}, u32[]{:S(2)}) collective-permute-start(bf16[8,32,512]{2,1,0:T(8,128)(2,1)} %get-tuple-element.106), channel_id=1, source_target_pairs={{0,8},{4,12},{8,0},{12,4},{1,9},{5,13},{9,1},{13,5},{2,10},{6,14},... | collective-permute-start | bytes 786440 | tf_op jit(solution)/shard_map/ppermute | solution.py:27
  13.8 8.1 %collective-permute-done = bf16[8,32,512]{2,1,0:T(8,128)(2,1)} collective-permute-done((bf16[8,32,512]{2,1,0:T(8,128)(2,1)}, bf16[8,32,512]{2,1,0:T(8,128)(2,1)}, u32[]{:S(2)}, u32[]{:S(2)}) %collective-permute-start) | collective-permute-done | bytes 262176 | tf_op jit(solution)/shard_map/ppermute | solution.py:27
  21.9 10.1 %collective-permute-done.1 = bf16[8,32,512]{2,1,0:T(8,128)(2,1)S(1)} collective-permute-done((bf16[8,32,512]{2,1,0:T(8,128)(2,1)}, bf16[8,32,512]{2,1,0:T(8,128)(2,1)S(1)}, u32[]{:S(2)}, u32[]{:S(2)}) %collective-permute-start.1) | collective-permute-done | bytes 262176 | tf_op jit(solution)/shard_map/ppermute | solution.py:27
  36.8 9.0 %collective-permute-done.4.refs_2_ = bf16[2,256,512]{2,1,0:T(8,128)(2,1)S(1)} collective-permute-done((bf16[2,256,512]{2,1,0:T(8,128)(2,1)S(1)}, bf16[2,256,512]{2,1,0:T(8,128)(2,1)S(1)}, u32[]{:S(2)}, u32[]{:S(2)}) %collective-permute-start.4) | collective-permute-done | bytes 524320 | tf_op jit(solution)/shard_map/ppermute | solution.py:27
  47.7 6.2 %shard_map.101.refs_0_ = bf16[128,2048]{1,0:T(8,128)(2,1)S(1)} custom-call(s32[3]{0:T(128)S(1)} %pad_add_fusion.scalars, bf16[2,2,64,2048]{3,2,1,0:T(8,128)(2,1)S(1)} %bitcast.30, bf16[2,256,512]{2,1,0:T(8,128)(2,1)S(1)} %bitcast.28, bf16[2,256,512]{2,1,0:T(8,128)(2,1)S(1)} %collective-permute-done.3.refs_1_, ...), custom_call_target="tpu_custom_call" | custom-call | flops 1 | bytes 1 | tf_op jit(solution)/shard_map/pallas_call | solution.py:194
  55.3 6.3 %collective-permute-start.9 = (bf16[128,2048]{1,0:T(8,128)(2,1)S(1)}, bf16[128,2048]{1,0:T(8,128)(2,1)S(1)}, u32[]{:S(2)}, u32[]{:S(2)}) collective-permute-start(bf16[128,2048]{1,0:T(8,128)(2,1)S(1)} %shard_map.101.refs_0_), channel_id=1, source_target_pairs={{0,4},{4,0},{8,12},{12,8},{1,5},{5,1},{9,13},{13,9},{2,6},{6,2},{1... | collective-permute-start | bytes 1572872 | tf_op jit(solution)/shard_map/ppermute | solution.py:27
  61.6 6.2 %shard_map.100.refs_1_ = bf16[128,2048]{1,0:T(8,128)(2,1)S(1)} custom-call(s32[3]{0:T(128)S(1)} %pad_add_fusion.scalars, bf16[2,2,64,2048]{3,2,1,0:T(8,128)(2,1)S(1)} %bitcast.31, bf16[2,256,512]{2,1,0:T(8,128)(2,1)S(1)} %bitcast.29, bf16[2,256,512]{2,1,0:T(8,128)(2,1)S(1)} %collective-permute-done.3.refs_1_, ...), custom_call_target="tpu_custom_call" | custom-call | flops 1 | bytes 1 | tf_op jit(solution)/shard_map/pallas_call | solution.py:194
  69.2 3.4 %copy-done.1 = bf16[2048,2048]{1,0:T(8,128)(2,1)S(1)} copy-done((bf16[2048,2048]{1,0:T(8,128)(2,1)S(1)}, bf16[2048,2048]{1,0:T(8,128)(2,1)}, u32[]{:S(2)}) %copy-start.1) | copy-done | bytes 8388632
  72.6 3.6 %shard_map.102 = (f32[128,2048]{1,0:T(8,128)S(1)}, bf16[128,2048]{1,0:T(8,128)(2,1)S(1)}) custom-call(s32[1]{0:T(128)} %bitcast.6.share, bf16[128,2048]{1,0:T(8,128)(2,1)S(1)} %shard_map.101.refs_0_, bf16[128,2048]{1,0:T(8,128)(2,1)S(1)} %shard_map.100.refs_1_, bf16[2048,2048]{1,0:T(8,128)(2,1)S(1)} %copy-done.1), custom_call_target="tpu_custom_call" | custom-call | flops 1 | bytes 1 | tf_op jit(solution)/shard_map/pallas_call | solution.py:63
  76.3 5.6 %collective-permute-done.9.refs_0_ = bf16[128,2048]{1,0:T(8,128)(2,1)S(1)} collective-permute-done((bf16[128,2048]{1,0:T(8,128)(2,1)S(1)}, bf16[128,2048]{1,0:T(8,128)(2,1)S(1)}, u32[]{:S(2)}, u32[]{:S(2)}) %collective-permute-start.9) | collective-permute-done | bytes 524320 | tf_op jit(solution)/shard_map/ppermute | solution.py:27
  81.9 4.3 %shard_map.103 = (f32[64,2048]{1,0:T(8,128)S(1)}, bf16[64,2048]{1,0:T(8,128)(2,1)}, bf16[64,2048]{1,0:T(8,128)(2,1)}, bf16[64,2048]{1,0:T(8,128)(2,1)S(1)}) custom-call(s32[1]{0:T(128)} %bitcast.6.share, bf16[128,2048]{1,0:T(8,128)(2,1)S(1)} %collective-permute-done.9.refs_0_, bf16[128,2048]{1,0:T(8,128)(2,1)S(1)} %collective-permute-done.8.refs_1_, ...), custom_call_target="tpu_custom_call" | custom-call | flops 1 | bytes 1 | tf_op jit(solution)/shard_map/pallas_call | solution.py:63
  88.1 5.0 %collective-permute-done.6.refs_1_ = bf16[128,2048]{1,0:T(8,128)(2,1)S(1)} collective-permute-done((bf16[128,2048]{1,0:T(8,128)(2,1)S(1)}, bf16[128,2048]{1,0:T(8,128)(2,1)S(1)}, u32[]{:S(2)}, u32[]{:S(2)}) %collective-permute-start.6) | collective-permute-done | bytes 524320 | tf_op jit(solution)/shard_map/ppermute | solution.py:27
  93.1 10.4 %collective-permute-done.7.refs_0_ = bf16[128,2048]{1,0:T(8,128)(2,1)} collective-permute-done((bf16[128,2048]{1,0:T(8,128)(2,1)S(1)}, bf16[128,2048]{1,0:T(8,128)(2,1)}, u32[]{:S(2)}, u32[]{:S(2)}) %collective-permute-start.7) | collective-permute-done | bytes 524320 | tf_op jit(solution)/shard_map/ppermute | solution.py:27
  105.5 3.4 %copy-done.3 = bf16[2048,2048]{1,0:T(8,128)(2,1)S(1)} copy-done((bf16[2048,2048]{1,0:T(8,128)(2,1)S(1)}, bf16[2048,2048]{1,0:T(8,128)(2,1)}, u32[]{:S(2)}) %copy-start.3) | copy-done | bytes 8388632
  108.8 4.5 %shard_map.104 = (f32[128,2048]{1,0:T(8,128)S(1)}, bf16[128,2048]{1,0:T(8,128)(2,1)S(1)}) custom-call(s32[1]{0:T(128)} %bitcast.6.share, bf16[128,2048]{1,0:T(8,128)(2,1)} %collective-permute-done.7.refs_0_, bf16[128,2048]{1,0:T(8,128)(2,1)S(1)} %collective-permute-done.6.refs_1_, bf16[2048,2048]{1,0:T(8,128)(2,1)S(1)} %copy-done.3), custom_call_target="tpu_custom_call" | custom-call | flops 1 | bytes 1 | tf_op jit(solution)/shard_map/pallas_call | solution.py:63
  115.7 2.8 %collective-permute-done.14.refs_0_ = bf16[128,2048]{1,0:T(8,128)(2,1)S(1)} collective-permute-done((bf16[128,2048]{1,0:T(8,128)(2,1)S(1)}, bf16[128,2048]{1,0:T(8,128)(2,1)S(1)}, u32[]{:S(2)}, u32[]{:S(2)}) %collective-permute-start.14) | collective-permute-done | bytes 524320 | tf_op jit(solution)/shard_map/ppermute | solution.py:34
  118.5 2.6 %shard_map.105 = (f32[64,2048]{1,0:T(8,128)S(1)}, bf16[64,2048]{1,0:T(8,128)(2,1)S(1)}) custom-call(s32[1]{0:T(128)} %bitcast.6.share, bf16[128,2048]{1,0:T(8,128)(2,1)S(1)} %collective-permute-done.14.refs_0_, bf16[2048,2048]{1,0:T(8,128)(2,1)S(1)} %copy-done.3), custom_call_target="tpu_custom_call" | custom-call | flops 1 | bytes 1 | tf_op jit(solution)/shard_map/pallas_call | solution.py:63
  125.6 3.7 %collective-permute-done.13.refs_0_ = bf16[128,2048]{1,0:T(8,128)(2,1)S(1)} collective-permute-done((bf16[128,2048]{1,0:T(8,128)(2,1)S(1)}, bf16[128,2048]{1,0:T(8,128)(2,1)S(1)}, u32[]{:S(2)}, u32[]{:S(2)}) %collective-permute-start.13) | collective-permute-done | bytes 524320 | tf_op jit(solution)/shard_map/ppermute | solution.py:34
  132.9 2.6 %collective-permute-start.23 = (bf16[32,2048]{1,0:T(8,128)(2,1)S(1)}, bf16[32,2048]{1,0:T(8,128)(2,1)S(1)}, u32[]{:S(2)}, u32[]{:S(2)}) collective-permute-start(bf16[32,2048]{1,0:T(8,128)(2,1)S(1)} %add_convert_fusion.6), channel_id=1, source_target_pairs={{0,8},{4,12},{8,0},{12,4},{1,9},{5,13},{9,1},{13,5},{2,10},{6,14},... | collective-permute-start | bytes 393224 | tf_op jit(solution)/shard_map/ppermute | solution.py:27
  142.3 6.4 %collective-permute-done.23 = bf16[32,2048]{1,0:T(8,128)(2,1)S(1)} collective-permute-done((bf16[32,2048]{1,0:T(8,128)(2,1)S(1)}, bf16[32,2048]{1,0:T(8,128)(2,1)S(1)}, u32[]{:S(2)}, u32[]{:S(2)}) %collective-permute-start.23) | collective-permute-done | bytes 131104 | tf_op jit(solution)/shard_map/ppermute | solution.py:27
  149.0 5.5 %collective-permute-done.26 = bf16[32,2048]{1,0:T(8,128)(2,1)S(1)} collective-permute-done((bf16[32,2048]{1,0:T(8,128)(2,1)S(1)}, bf16[32,2048]{1,0:T(8,128)(2,1)S(1)}, u32[]{:S(2)}, u32[]{:S(2)}) %collective-permute-start.26) | collective-permute-done | bytes 131104 | tf_op jit(solution)/shard_map/ppermute | solution.py:27
  154.8 8.3 %collective-permute-done.27 = bf16[32,2048]{1,0:T(8,128)(2,1)S(1)} collective-permute-done((bf16[32,2048]{1,0:T(8,128)(2,1)S(1)}, bf16[32,2048]{1,0:T(8,128)(2,1)S(1)}, u32[]{:S(2)}, u32[]{:S(2)}) %collective-permute-start.27) | collective-permute-done | bytes 131104 | tf_op jit(solution)/shard_map/ppermute | solution.py:27
  (114 shorter events, 36.7 us)
Async XLA Ops:
  7.4 14.5 %collective-permute-start = (bf16[8,32,512]{2,1,0:T(8,128)(2,1)}, bf16[8,32,512]{2,1,0:T(8,128)(2,1)}, u32[]{:S(2)}, u32[]{:S(2)}) collective-permute-start(bf16[8,32,512]{2,1,0:T(8,128)(2,1)} %get-tuple-element.107), channel_id=1, source_target_pairs={{0,4},{4,0},{8,12},{12,8},{1,5},{5,1},{9,13},{13,9},{2,6},{6,2},{1... | collective-permute-start | bytes 786440 | tf_op jit(solution)/shard_map/ppermute | solution.py:27
  10.4 21.6 %collective-permute-start.1 = (bf16[8,32,512]{2,1,0:T(8,128)(2,1)}, bf16[8,32,512]{2,1,0:T(8,128)(2,1)S(1)}, u32[]{:S(2)}, u32[]{:S(2)}) collective-permute-start(bf16[8,32,512]{2,1,0:T(8,128)(2,1)} %get-tuple-element.106), channel_id=1, source_target_pairs={{0,8},{4,12},{8,0},{12,4},{1,9},{5,13},{9,1},{13,5},{2,10},{6,14},... | collective-permute-start | bytes 786440 | tf_op jit(solution)/shard_map/ppermute | solution.py:27
  13.0 19.0 %collective-permute-start.2 = (bf16[8,32,512]{2,1,0:T(8,128)(2,1)}, bf16[8,32,512]{2,1,0:T(8,128)(2,1)S(1)}, u32[]{:S(2)}, u32[]{:S(2)}) collective-permute-start(bf16[8,32,512]{2,1,0:T(8,128)(2,1)} %get-tuple-element.108), channel_id=1, source_target_pairs={{0,12},{4,8},{8,4},{12,0},{1,13},{5,9},{9,5},{13,1},{2,14},{6,10},... | collective-permute-start | bytes 786440 | tf_op jit(solution)/shard_map/ppermute | solution.py:27
  35.3 10.6 %collective-permute-start.4 = (bf16[2,256,512]{2,1,0:T(8,128)(2,1)S(1)}, bf16[2,256,512]{2,1,0:T(8,128)(2,1)S(1)}, u32[]{:S(2)}, u32[]{:S(2)}) collective-permute-start(bf16[2,256,512]{2,1,0:T(8,128)(2,1)S(1)} %bitcast.26), channel_id=1, source_target_pairs={{0,2},{2,0},{1,3},{3,1},{4,6},{6,4},{5,7},{7,5},{8,10},{10,8},{9,1... | collective-permute-start | bytes 1572872 | tf_op jit(solution)/shard_map/ppermute | solution.py:27
  36.8 9.0 %collective-permute-start.3 = (bf16[2,256,512]{2,1,0:T(8,128)(2,1)S(1)}, bf16[2,256,512]{2,1,0:T(8,128)(2,1)S(1)}, u32[]{:S(2)}, u32[]{:S(2)}) collective-permute-start(bf16[2,256,512]{2,1,0:T(8,128)(2,1)S(1)} %bitcast.27), channel_id=1, source_target_pairs={{0,1},{1,0},{2,3},{3,2},{4,5},{5,4},{6,7},{7,6},{8,9},{9,8},{10,11... | collective-permute-start | bytes 1572872 | tf_op jit(solution)/shard_map/ppermute | solution.py:27
  53.9 22.4 %collective-permute-start.8 = (bf16[128,2048]{1,0:T(8,128)(2,1)S(1)}, bf16[128,2048]{1,0:T(8,128)(2,1)S(1)}, u32[]{:S(2)}, u32[]{:S(2)}) collective-permute-start(bf16[128,2048]{1,0:T(8,128)(2,1)S(1)} %shard_map.101.refs_0_), channel_id=1, source_target_pairs={{0,12},{4,8},{8,4},{12,0},{1,13},{5,9},{9,5},{13,1},{2,14},{6,10},... | collective-permute-start | bytes 1572872 | tf_op jit(solution)/shard_map/ppermute | solution.py:27
  55.3 26.6 %collective-permute-start.9 = (bf16[128,2048]{1,0:T(8,128)(2,1)S(1)}, bf16[128,2048]{1,0:T(8,128)(2,1)S(1)}, u32[]{:S(2)}, u32[]{:S(2)}) collective-permute-start(bf16[128,2048]{1,0:T(8,128)(2,1)S(1)} %shard_map.101.refs_0_), channel_id=1, source_target_pairs={{0,4},{4,0},{8,12},{12,8},{1,5},{5,1},{9,13},{13,9},{2,6},{6,2},{1... | collective-permute-start | bytes 1572872 | tf_op jit(solution)/shard_map/ppermute | solution.py:27
  67.8 25.3 %collective-permute-start.6 = (bf16[128,2048]{1,0:T(8,128)(2,1)S(1)}, bf16[128,2048]{1,0:T(8,128)(2,1)S(1)}, u32[]{:S(2)}, u32[]{:S(2)}) collective-permute-start(bf16[128,2048]{1,0:T(8,128)(2,1)S(1)} %shard_map.100.refs_1_), channel_id=1, source_target_pairs={{0,12},{4,8},{8,4},{12,0},{1,13},{5,9},{9,5},{13,1},{2,14},{6,10},... | collective-permute-start | bytes 1572872 | tf_op jit(solution)/shard_map/ppermute | solution.py:27
  69.2 34.3 %collective-permute-start.7 = (bf16[128,2048]{1,0:T(8,128)(2,1)S(1)}, bf16[128,2048]{1,0:T(8,128)(2,1)}, u32[]{:S(2)}, u32[]{:S(2)}) collective-permute-start(bf16[128,2048]{1,0:T(8,128)(2,1)S(1)} %shard_map.100.refs_1_), channel_id=1, source_target_pairs={{0,4},{4,0},{8,12},{12,8},{1,5},{5,1},{9,13},{13,9},{2,6},{6,2},{1... | collective-permute-start | bytes 1572872 | tf_op jit(solution)/shard_map/ppermute | solution.py:27
  86.2 17.3 %collective-permute-start.10 = (bf16[64,2048]{1,0:T(8,128)(2,1)}, bf16[64,2048]{1,0:T(8,128)(2,1)}, u32[]{:S(2)}, u32[]{:S(2)}) collective-permute-start(bf16[64,2048]{1,0:T(8,128)(2,1)} %get-tuple-element.63), channel_id=1, source_target_pairs={{0,1},{1,0},{2,3},{3,2},{4,5},{5,4},{6,7},{7,6},{8,9},{9,8},{10,11... | collective-permute-start | bytes 786440 | tf_op jit(solution)/shard_map/ppermute | solution.py:27
  86.3 17.3 %collective-permute-start.11 = (bf16[64,2048]{1,0:T(8,128)(2,1)}, bf16[64,2048]{1,0:T(8,128)(2,1)}, u32[]{:S(2)}, u32[]{:S(2)}) collective-permute-start(bf16[64,2048]{1,0:T(8,128)(2,1)} %get-tuple-element.64), channel_id=1, source_target_pairs={{0,2},{1,3},{2,0},{3,1},{4,6},{5,7},{6,4},{7,5},{8,10},{9,11},{10,... | collective-permute-start | bytes 786440 | tf_op jit(solution)/shard_map/ppermute | solution.py:27
  87.8 15.8 %collective-permute-start.12 = (bf16[64,2048]{1,0:T(8,128)(2,1)S(1)}, bf16[64,2048]{1,0:T(8,128)(2,1)}, u32[]{:S(2)}, u32[]{:S(2)}) collective-permute-start(bf16[64,2048]{1,0:T(8,128)(2,1)S(1)} %get-tuple-element.65), channel_id=1, source_target_pairs={{0,3},{1,2},{2,1},{3,0},{4,7},{5,6},{6,5},{7,4},{8,11},{9,10},{10,... | collective-permute-start | bytes 786440 | tf_op jit(solution)/shard_map/ppermute | solution.py:27
  103.6 10.5 %collective-permute-start.19 = (bf16[128,2048]{1,0:T(8,128)(2,1)}, bf16[128,2048]{1,0:T(8,128)(2,1)S(1)}, u32[]{:S(2)}, u32[]{:S(2)}) collective-permute-start(bf16[128,2048]{1,0:T(8,128)(2,1)} %copy-done.8), channel_id=1, source_target_pairs={{0,1},{1,0},{2,3},{3,2},{4,5},{5,4},{6,7},{7,6},{8,9},{9,8},{10,11... | collective-permute-start | bytes 1572872 | tf_op jit(solution)/shard_map/ppermute | solution.py:27
  103.7 14.8 %collective-permute-start.14 = (bf16[128,2048]{1,0:T(8,128)(2,1)S(1)}, bf16[128,2048]{1,0:T(8,128)(2,1)S(1)}, u32[]{:S(2)}, u32[]{:S(2)}) collective-permute-start(bf16[128,2048]{1,0:T(8,128)(2,1)S(1)} %broadcast_select_fusion), channel_id=1, source_target_pairs={{0,8},{12,4},{4,0},{8,12},{1,9},{13,5},{5,1},{9,13},{2,10},{14,6},... | collective-permute-start | bytes 1572872 | tf_op jit(solution)/shard_map/ppermute | solution.py:34
  113.7 15.6 %collective-permute-start.13 = (bf16[128,2048]{1,0:T(8,128)(2,1)S(1)}, bf16[128,2048]{1,0:T(8,128)(2,1)S(1)}, u32[]{:S(2)}, u32[]{:S(2)}) collective-permute-start(bf16[128,2048]{1,0:T(8,128)(2,1)S(1)} %broadcast_select_fusion.1), channel_id=1, source_target_pairs={{0,8},{12,4},{4,0},{8,12},{1,9},{13,5},{5,1},{9,13},{2,10},{14,6},... | collective-permute-start | bytes 1572872 | tf_op jit(solution)/shard_map/ppermute | solution.py:34
  114.1 15.2 %collective-permute-start.20 = (bf16[64,2048]{1,0:T(8,128)(2,1)S(1)}, bf16[64,2048]{1,0:T(8,128)(2,1)S(1)}, u32[]{:S(2)}, u32[]{:S(2)}) collective-permute-start(bf16[64,2048]{1,0:T(8,128)(2,1)S(1)} %add_convert_fusion.2), channel_id=1, source_target_pairs={{0,2},{2,0},{1,3},{3,1},{4,6},{6,4},{5,7},{7,5},{8,10},{10,8},{9,1... | collective-permute-start | bytes 786440 | tf_op jit(solution)/shard_map/ppermute | solution.py:27
  121.3 9.2 %collective-permute-start.16 = (bf16[64,2048]{1,0:T(8,128)(2,1)S(1)}, bf16[64,2048]{1,0:T(8,128)(2,1)S(1)}, u32[]{:S(2)}, u32[]{:S(2)}) collective-permute-start(bf16[64,2048]{1,0:T(8,128)(2,1)S(1)} %add_convert_fusion.3), channel_id=1, source_target_pairs={{0,2},{2,0},{1,3},{3,1},{4,6},{6,4},{5,7},{7,5},{8,10},{10,8},{9,1... | collective-permute-start | bytes 786440 | tf_op jit(solution)/shard_map/ppermute | solution.py:27
  122.9 10.0 %collective-permute-start.18 = (bf16[32,2048]{1,0:T(8,128)(2,1)S(1)}, bf16[32,2048]{1,0:T(8,128)(2,1)S(1)}, u32[]{:S(2)}, u32[]{:S(2)}) collective-permute-start(bf16[32,2048]{1,0:T(8,128)(2,1)S(1)} %add_convert_fusion.7), channel_id=1, source_target_pairs={{0,2},{2,0},{1,3},{3,1},{4,6},{6,4},{5,7},{7,5},{8,10},{10,8},{9,1... | collective-permute-start | bytes 393224 | tf_op jit(solution)/shard_map/ppermute | solution.py:27
  132.9 15.8 %collective-permute-start.23 = (bf16[32,2048]{1,0:T(8,128)(2,1)S(1)}, bf16[32,2048]{1,0:T(8,128)(2,1)S(1)}, u32[]{:S(2)}, u32[]{:S(2)}) collective-permute-start(bf16[32,2048]{1,0:T(8,128)(2,1)S(1)} %add_convert_fusion.6), channel_id=1, source_target_pairs={{0,8},{4,12},{8,0},{12,4},{1,9},{5,13},{9,1},{13,5},{2,10},{6,14},... | collective-permute-start | bytes 393224 | tf_op jit(solution)/shard_map/ppermute | solution.py:27
  135.8 18.7 %collective-permute-start.22 = (bf16[64,2048]{1,0:T(8,128)(2,1)S(1)}, bf16[64,2048]{1,0:T(8,128)(2,1)S(1)}, u32[]{:S(2)}, u32[]{:S(2)}) collective-permute-start(bf16[64,2048]{1,0:T(8,128)(2,1)S(1)} %pad_maximum_fusion.2), channel_id=1, source_target_pairs={{0,12},{4,8},{8,4},{12,0},{1,13},{5,9},{9,5},{13,1},{2,14},{6,10},... | collective-permute-start | bytes 786440 | tf_op jit(solution)/shard_map/ppermute | solution.py:27
  138.0 16.5 %collective-permute-start.21 = (bf16[64,2048]{1,0:T(8,128)(2,1)S(1)}, bf16[64,2048]{1,0:T(8,128)(2,1)S(1)}, u32[]{:S(2)}, u32[]{:S(2)}) collective-permute-start(bf16[64,2048]{1,0:T(8,128)(2,1)S(1)} %pad_maximum_fusion.1), channel_id=1, source_target_pairs={{0,4},{4,0},{8,12},{12,8},{1,5},{5,1},{9,13},{13,9},{2,6},{6,2},{1... | collective-permute-start | bytes 786440 | tf_op jit(solution)/shard_map/ppermute | solution.py:27
  140.7 8.2 %collective-permute-start.24 = (bf16[32,2048]{1,0:T(8,128)(2,1)S(1)}, bf16[32,2048]{1,0:T(8,128)(2,1)S(1)}, u32[]{:S(2)}, u32[]{:S(2)}) collective-permute-start(bf16[32,2048]{1,0:T(8,128)(2,1)S(1)} %get-tuple-element.95), channel_id=1, source_target_pairs={{0,1},{1,0},{2,3},{3,2},{4,5},{5,4},{6,7},{7,6},{8,9},{9,8},{10,11... | collective-permute-start | bytes 393224 | tf_op jit(solution)/shard_map/ppermute | solution.py:27
  140.8 8.2 %collective-permute-start.25 = (bf16[32,2048]{1,0:T(8,128)(2,1)S(1)}, bf16[32,2048]{1,0:T(8,128)(2,1)S(1)}, u32[]{:S(2)}, u32[]{:S(2)}) collective-permute-start(bf16[32,2048]{1,0:T(8,128)(2,1)S(1)} %get-tuple-element.96), channel_id=1, source_target_pairs={{0,2},{1,3},{2,0},{3,1},{4,6},{5,7},{6,4},{7,5},{8,10},{9,11},{10,... | collective-permute-start | bytes 393224 | tf_op jit(solution)/shard_map/ppermute | solution.py:27
  154.6 8.4 %collective-permute-start.27 = (bf16[32,2048]{1,0:T(8,128)(2,1)S(1)}, bf16[32,2048]{1,0:T(8,128)(2,1)S(1)}, u32[]{:S(2)}, u32[]{:S(2)}) collective-permute-start(bf16[32,2048]{1,0:T(8,128)(2,1)S(1)} %add_convert_fusion.5), channel_id=1, source_target_pairs={{0,8},{4,12},{8,0},{12,4},{1,9},{5,13},{9,1},{13,5},{2,10},{6,14},... | collective-permute-start | bytes 393224 | tf_op jit(solution)/shard_map/ppermute | solution.py:27
  (19 other events, 223.8 us)

commit v13 on v12

--- a/solution.py
+++ b/solution.py
@@ -14,13 +14,6 @@
 
 def rms_scale(values, gain):
     return values * lax.rsqrt(jnp.mean(values * values, axis=-1, keepdims=True) + 1e-05) * gain
-
-
-def pair_rank(holders):
-    count = holders.shape[1]
-    same = holders[:, :, None] == holders[:, None, :]
-    earlier = jnp.arange(count)[None, :] < jnp.arange(count)[:, None]
-    return jnp.sum((same & earlier[None]).astype(jnp.int32), axis=2)
 
 
 def swap(values, axis, flip):
@@ -111,35 +104,95 @@
     return sum((part.astype(jnp.float32) for part in received), total).astype(jnp.bfloat16)
 
 
-def find_blocks(place_holder, place_block, serving_request, items):
+def fetch_kernel(
+    place, holder, block, serving, counts, store, where, scalars, *refs, pool_size, share_count
+):
+    pieces, (table, rank_of, sems) = refs[:pool_size], refs[pool_size:]
+    pool_index, share = place[0], place[1]
+    capacity = pieces[0].shape[0]
+    blocks_each = holder.shape[1]
+    requests_here = scalars.shape[0] - 1
+    spare = pool_size * capacity
+    copies = []
+    for flip in range(pool_size):
+        for slot in range(capacity):
+            table[flip * capacity + slot] = 0
+        rank = 0
+        for i in range(requests_here):
+            request = serving[(pool_index ^ flip) * requests_here + i]
+            for j in range(blocks_each):
+                held = holder[request, j] == pool_index
+                table[jnp.where(held, flip * capacity + rank, spare)] = block[request, j]
+                rank = rank + held.astype(jnp.int32)
+        for slot in range(capacity):
+            index = flip * capacity + slot
+            source = store.at[table[index] * share_count + share]
+            copies.append(pltpu.make_async_copy(source, pieces[flip].at[slot], sems.at[index]))
+            copies[-1].start()
+    for i in range(pool_size):
+        rank_of[i] = 0
+    scalars[0] = share
+    for i in range(requests_here):
+        request = serving[pool_index * requests_here + i]
+        scalars[1 + i] = counts[request]
+        for j in range(blocks_each):
+            held_by = holder[request, j]
+            where[0, i * blocks_each + j] = held_by ^ pool_index
+            where[1, i * blocks_each + j] = rank_of[held_by]
+            rank_of[held_by] = rank_of[held_by] + 1
+    for copy in copies:
+        copy.wait()
+
+
+def fetch(latent_store, place_holder, place_block, serving_request, image_count, items):
     pool_size = lax.axis_size("pool")
-    pool_index = lax.axis_index("pool")
+    share_count = lax.axis_size(("heads", "sub"))
+    place = jnp.stack([lax.axis_index("pool"), lax.axis_index(("heads", "sub"))])
     capacity = 2 * ((items + pool_size - 1) // pool_size)
-    total_requests = serving_request.shape[0]
-    request_ids = jnp.arange(total_requests, dtype=jnp.int32)
-    selector = (serving_request[:, None] == request_ids[None, :]).astype(jnp.int32)
-    holders = jnp.dot(selector, place_holder).reshape(pool_size, items)
-    blocks = jnp.dot(selector, place_block).reshape(pool_size, items)
-    ranks = pair_rank(holders)
-    slot_ids = jnp.arange(capacity, dtype=jnp.int32)
-    matched = (holders[:, None, :] == pool_index) & (ranks[:, None, :] == slot_ids[None, :, None])
-    send_block = jnp.sum(jnp.where(matched, blocks[:, None, :], 0), axis=2)
-    partners = jnp.arange(pool_size, dtype=jnp.int32) ^ pool_index
-    wanted = send_block.at[partners].get(mode="promise_in_bounds")
-    my_holders = lax.dynamic_index_in_dim(holders, pool_index, 0, keepdims=False)
-    my_ranks = lax.dynamic_index_in_dim(ranks, pool_index, 0, keepdims=False)
-    return selector, wanted, (my_holders ^ pool_index) * capacity + my_ranks
-
-
-def fetch_pieces(latent_store, wanted):
-    share_count = lax.axis_size(("heads", "sub"))
-    share = lax.axis_index(("heads", "sub"))
     rows = BLK // share_count
     store = latent_store.reshape(-1, rows, latent_store.shape[1])
-    outgoing = store.at[wanted.reshape(-1) * share_count + share].get(mode="promise_in_bounds")
-    outgoing = outgoing.reshape(*wanted.shape, rows, -1)
-    arriving = {flip: swap(outgoing[flip], "pool", flip) for flip in (*range(2, len(wanted)), 1)}
-    return [outgoing[0]] + [arriving[flip] for flip in range(1, len(wanted))]
+    piece = jax.ShapeDtypeStruct((capacity, rows, store.shape[2]), store.dtype)
+    requests_here = items // place_holder.shape[1]
+    smem = pl.BlockSpec(memory_space=pltpu.SMEM)
+    where, scalars, *pieces = pl.pallas_call(
+        functools.partial(fetch_kernel, pool_size=pool_size, share_count=share_count),
+        in_specs=[smem] * 5 + [pl.BlockSpec(memory_space=pltpu.HBM)],
+        out_specs=[smem, smem] + [pl.BlockSpec(memory_space=pltpu.VMEM)] * pool_size,
+        out_shape=[
+            jax.ShapeDtypeStruct((2, items), jnp.int32),
+            jax.ShapeDtypeStruct((1 + requests_here,), jnp.int32),
+        ]
+        + [piece] * pool_size,
+        scratch_shapes=[
+            pltpu.SMEM((pool_size * capacity + 1,), jnp.int32),
+            pltpu.SMEM((pool_size,), jnp.int32),
+            pltpu.SemaphoreType.DMA((pool_size * capacity,)),
+        ],
+        cost_estimate=LIGHT,
+    )(place.astype(jnp.int32), place_holder, place_block, serving_request, image_count, store)
+    return where, scalars, pieces
+
+
+def choose_kernel(where, *refs):
+    pieces, out = refs[:-1], refs[-1]
+    for i in range(out.shape[0]):
+        flip, slot = where[0, i], where[1, i]
+        for other, piece in enumerate(pieces):
+
+            @pl.when(flip == other)
+            def _(piece=piece):
+                out[i] = piece[slot]
+
+
+def choose(where, pieces):
+    whole = pl.BlockSpec(memory_space=pltpu.VMEM)
+    return pl.pallas_call(
+        choose_kernel,
+        in_specs=[pl.BlockSpec(memory_space=pltpu.SMEM)] + [whole] * len(pieces),
+        out_specs=whole,
+        out_shape=jax.ShapeDtypeStruct((where.shape[1], *pieces[0].shape[1:]), pieces[0].dtype),
+        cost_estimate=LIGHT,
+    )(where, *pieces)
 
 
 def attend_kernel(share_count, scalars, queries, *refs):
@@ -237,15 +290,13 @@
     items = requests_here * blocks_each
     rank_width = latent_store.shape[1]
     tie = lax.optimization_barrier
-    selector, wanted, where = find_blocks(place_holder, place_block, serving_request, items)
+    where, scalars, pieces = fetch(
+        latent_store, place_holder, place_block, serving_request, image_count, items
+    )
     kv_flat = jnp.moveaxis(kv_up.reshape(rank_width, kv_up.shape[1], -1), 1, 0)
     gains = q_gain.reshape(1, -1), k_gain.reshape(1, -1)
-    count_here = lax.dynamic_slice_in_dim(
-        jnp.dot(selector, image_count), pool_index * requests_here, requests_here
-    )
-    scalars = jnp.concatenate([share.reshape(1), count_here])
-    pieces = jnp.concatenate(fetch_pieces(latent_store, wanted), axis=0)
-    chosen = pieces.at[where].get(mode="promise_in_bounds")
+    arriving = [swap(pieces[flip], "pool", flip) for flip in range(1, pool_size)]
+    chosen = choose(where, pieces[:1] + arriving)
     chosen, kv_flat, scalars = tie((chosen, kv_flat, scalars))
     chosen = chosen.reshape(requests_here, -1, rank_width)
     over_heads = [chosen] + [swap(chosen, "heads", flip) for flip in range(1, heads_size)]

time: 164 us -> 164 us (level)
  Pallas kernels: 30 us -> 35.7 us
  local copies, waits for them, and re-layouts: 15.3 us -> 11.3 us
  waiting for transfers between devices: 80.5 us -> 83.5 us
  matrix products: 1.94 us -> 0 us
  starting transfers between devices: 32 us -> 30.1 us
    pallas_call x0 -> x2, Pallas kernels: none -> 5.76 us  [the longest x1 3.38 us: fetch(): pl.pallas_call(functools.partial(fetch_kernel, pool_size=pool_size, share...]
    gather x3 -> x0, local copies, waits for them, and re-layouts: 3.95 us -> none  [the longest x1 2.8 us: fetch_pieces(): store.at[wanted.reshape(-1) * share_count + share]]
    ppermute x26, waiting for transfers between devices: 73.9 us -> 76.1 us  [swap(): lax.ppermute(values, axis, [(i, i ^ flip) for i in range(lax.axis_size(ax...]
    reshape x2, local copies, waits for them, and re-layouts: 0.41 us -> 2.38 us  [per_device(): kv_flat = jnp.moveaxis(kv_up.reshape(rank_width, kv_up.shape[1], -1), 1, 0)]
    dot_general x3 -> x0, matrix products: 1.94 us -> none  [the longest x1 0.9 us: find_blocks(): blocks = jnp.dot(selector, place_block).reshape(pool_size, items)]
    ppermute x26, starting transfers between devices: 29.9 us -> 28.1 us  [swap(): lax.ppermute(values, axis, [(i, i ^ flip) for i in range(lax.axis_size(ax...]
  transfers between devices with their start and end apart: 28 -> 28, of which waited for: 14 -> 15; matrix products, arithmetic and copies ran while one was open for 2% -> 3% of each run, Pallas kernels for 15% -> 15%
where the time goes in v13:
time: 164 us; the launch traced here: 163 us
  waiting for transfers between devices  83.5 us (51%)
  Pallas kernels  35.7 us (22%)
  starting transfers between devices  30.1 us (18%)
  local copies, waits for them, and re-layouts  11.3 us (7%)
  other arithmetic  2.45 us (1%)
    ppermute x26, waiting for transfers between devices, swap(): lax.ppermute(values, axis, [(i, i ^ flip) for i in range(lax.axis_size(ax...  76.1 us
    ppermute x26, starting transfers between devices, swap(): lax.ppermute(values, axis, [(i, i ^ flip) for i in range(lax.axis_size(ax...  28.1 us
    pallas_call x5, Pallas kernels, project_out(): pl.pallas_call(functools.partial(project_kernel, len(blocks), list(range(...  17.6 us
    pallas_call x2, Pallas kernels, attend(): pl.pallas_call(functools.partial(attend_kernel, len(parts)), grid=(reques...  12.3 us
    unnamed x30, local copies, waits for them, and re-layouts  8.05 us
    ppermute x2, waiting for transfers between devices, second_hop(): return lax.ppermute(passed, 'pool', [(0, 2), (3, 1), (1, 0), (2, 3)])  7.36 us
    pallas_call x1, Pallas kernels, fetch(): pl.pallas_call(functools.partial(fetch_kernel, pool_size=pool_size, share...  3.38 us
  transfers between devices with their start and end apart: 28, of which 15 were waited for; matrix products, arithmetic and copies ran while one was open for 3% of the time, Pallas kernels for 15%

profile of v13, /device:TPU:0, one launch (start us, length us, event | category | flops | bytes accessed | tf_op | source)
XLA Modules:
  0.0 163.3 jit_solution(4826430151005997670)
XLA Ops:
  0.7 3.4 %shard_map.100 = (s32[2,16]{1,0:T(2,128)}, s32[3]{0:T(128)}, bf16[8,32,512]{2,1,0:T(8,128)(2,1)}, bf16[8,32,512]{2,1,0:T(8,128)(2,1)}, bf16[8,32,512]{2,1,0:T(8,128)(2,1)}, /*index=5*/bf16[8,32,512]{2,1,0:T(8,128)(2,1)}) custom-call(s32[2]{0:T(128)} %pad_add_fusion.place, s32[8,8]{1,0:T(8,128)} %holder.1, s32[8,8]{1,0:T(8,128)} %block.1, s32[8]{0:T(128)} %serving.1, ...), custom_call_target="tpu_custom_call" | custom-call | flops 1 | bytes 1 | tf_op jit(solution)/shard_map/pallas_call | solution.py:157
  4.0 3.5 %collective-permute-start = (bf16[8,32,512]{2,1,0:T(8,128)(2,1)}, bf16[8,32,512]{2,1,0:T(8,128)(2,1)S(1)}, u32[]{:S(2)}, u32[]{:S(2)}) collective-permute-start(bf16[8,32,512]{2,1,0:T(8,128)(2,1)} %get-tuple-element.63), channel_id=1, source_target_pairs={{0,4},{4,0},{8,12},{12,8},{1,5},{5,1},{9,13},{13,9},{2,6},{6,2},{1... | collective-permute-start | bytes 786440 | tf_op jit(solution)/shard_map/ppermute | solution.py:20
  7.5 2.5 %collective-permute-start.1 = (bf16[8,32,512]{2,1,0:T(8,128)(2,1)}, bf16[8,32,512]{2,1,0:T(8,128)(2,1)S(1)}, u32[]{:S(2)}, u32[]{:S(2)}) collective-permute-start(bf16[8,32,512]{2,1,0:T(8,128)(2,1)} %get-tuple-element.64), channel_id=1, source_target_pairs={{0,8},{4,12},{8,0},{12,4},{1,9},{5,13},{9,1},{13,5},{2,10},{6,14},... | collective-permute-start | bytes 786440 | tf_op jit(solution)/shard_map/ppermute | solution.py:20
  12.5 6.4 %collective-permute-done.refs_1_ = bf16[8,32,512]{2,1,0:T(8,128)(2,1)S(1)} collective-permute-done((bf16[8,32,512]{2,1,0:T(8,128)(2,1)}, bf16[8,32,512]{2,1,0:T(8,128)(2,1)S(1)}, u32[]{:S(2)}, u32[]{:S(2)}) %collective-permute-start) | collective-permute-done | bytes 262176 | tf_op jit(solution)/shard_map/ppermute | solution.py:20
  18.9 10.2 %collective-permute-done.1.refs_2_ = bf16[8,32,512]{2,1,0:T(8,128)(2,1)S(1)} collective-permute-done((bf16[8,32,512]{2,1,0:T(8,128)(2,1)}, bf16[8,32,512]{2,1,0:T(8,128)(2,1)S(1)}, u32[]{:S(2)}, u32[]{:S(2)}) %collective-permute-start.1) | collective-permute-done | bytes 262176 | tf_op jit(solution)/shard_map/ppermute | solution.py:20
  34.5 9.0 %collective-permute-done.4.refs_2_ = bf16[2,256,512]{2,1,0:T(8,128)(2,1)S(1)} collective-permute-done((bf16[2,256,512]{2,1,0:T(8,128)(2,1)}, bf16[2,256,512]{2,1,0:T(8,128)(2,1)S(1)}, u32[]{:S(2)}, u32[]{:S(2)}) %collective-permute-start.4) | collective-permute-done | bytes 524320 | tf_op jit(solution)/shard_map/ppermute | solution.py:20
  48.5 6.1 %shard_map.103.refs_0_ = bf16[128,2048]{1,0:T(8,128)(2,1)S(1)} custom-call(s32[3]{0:T(128)S(1)} %copy-done.9, bf16[2,2,64,2048]{3,2,1,0:T(8,128)(2,1)S(1)} %bitcast.16, bf16[2,256,512]{2,1,0:T(8,128)(2,1)S(1)} %bitcast.14, bf16[2,256,512]{2,1,0:T(8,128)(2,1)S(1)} %collective-permute-done.3.refs_1_, bf16[2,256,512]{2,1,0:T(8,128)(2,1)S(1)} %collective-permute-done.4.refs_2_, ...), custom_call_target="tpu_custom_call" | custom-call | flops 1 | bytes 1 | tf_op jit(solution)/shard_map/pallas_call | solution.py:247
  56.1 6.3 %collective-permute-start.9 = (bf16[128,2048]{1,0:T(8,128)(2,1)S(1)}, bf16[128,2048]{1,0:T(8,128)(2,1)S(1)}, u32[]{:S(2)}, u32[]{:S(2)}) collective-permute-start(bf16[128,2048]{1,0:T(8,128)(2,1)S(1)} %shard_map.103.refs_0_), channel_id=1, source_target_pairs={{0,4},{4,0},{8,12},{12,8},{1,5},{5,1},{9,13},{13,9},{2,6},{6,2},{1... | collective-permute-start | bytes 1572872 | tf_op jit(solution)/shard_map/ppermute | solution.py:20
  62.4 6.2 %shard_map.102.refs_1_ = bf16[128,2048]{1,0:T(8,128)(2,1)S(1)} custom-call(s32[3]{0:T(128)S(1)} %copy-done.9, bf16[2,2,64,2048]{3,2,1,0:T(8,128)(2,1)S(1)} %bitcast.17, bf16[2,256,512]{2,1,0:T(8,128)(2,1)S(1)} %bitcast.15, bf16[2,256,512]{2,1,0:T(8,128)(2,1)S(1)} %collective-permute-done.3.refs_1_, bf16[2,256,512]{2,1,0:T(8,128)(2,1)S(1)} %collective-permute-done.4.refs_2_, ...), custom_call_target="tpu_custom_call" | custom-call | flops 1 | bytes 1 | tf_op jit(solution)/shard_map/pallas_call | solution.py:247
  70.0 3.6 %shard_map.104 = (f32[128,2048]{1,0:T(8,128)S(1)}, bf16[128,2048]{1,0:T(8,128)(2,1)S(1)}) custom-call(s32[1]{0:T(128)} %bitcast.1.share, bf16[128,2048]{1,0:T(8,128)(2,1)S(1)} %shard_map.103.refs_0_, bf16[128,2048]{1,0:T(8,128)(2,1)S(1)} %shard_map.102.refs_1_, bf16[2048,2048]{1,0:T(8,128)(2,1)S(1)} %copy-done), custom_call_target="tpu_custom_call" | custom-call | flops 1 | bytes 1 | tf_op jit(solution)/shard_map/pallas_call | solution.py:56
  73.6 9.0 %collective-permute-done.9.refs_0_ = bf16[128,2048]{1,0:T(8,128)(2,1)S(1)} collective-permute-done((bf16[128,2048]{1,0:T(8,128)(2,1)S(1)}, bf16[128,2048]{1,0:T(8,128)(2,1)S(1)}, u32[]{:S(2)}, u32[]{:S(2)}) %collective-permute-start.9) | collective-permute-done | bytes 524320 | tf_op jit(solution)/shard_map/ppermute | solution.py:20
  82.6 4.3 %shard_map.105 = (f32[64,2048]{1,0:T(8,128)S(1)}, bf16[64,2048]{1,0:T(8,128)(2,1)}, bf16[64,2048]{1,0:T(8,128)(2,1)}, bf16[64,2048]{1,0:T(8,128)(2,1)S(1)}) custom-call(s32[1]{0:T(128)} %bitcast.1.share, bf16[128,2048]{1,0:T(8,128)(2,1)S(1)} %collective-permute-done.9.refs_0_, bf16[128,2048]{1,0:T(8,128)(2,1)S(1)} %collective-permute-done.8.refs_1_, ...), custom_call_target="tpu_custom_call" | custom-call | flops 1 | bytes 1 | tf_op jit(solution)/shard_map/pallas_call | solution.py:56
  89.6 4.3 %collective-permute-done.6.refs_1_ = bf16[128,2048]{1,0:T(8,128)(2,1)S(1)} collective-permute-done((bf16[128,2048]{1,0:T(8,128)(2,1)S(1)}, bf16[128,2048]{1,0:T(8,128)(2,1)S(1)}, u32[]{:S(2)}, u32[]{:S(2)}) %collective-permute-start.6) | collective-permute-done | bytes 524320 | tf_op jit(solution)/shard_map/ppermute | solution.py:20
  93.9 10.5 %collective-permute-done.7.refs_0_ = bf16[128,2048]{1,0:T(8,128)(2,1)} collective-permute-done((bf16[128,2048]{1,0:T(8,128)(2,1)S(1)}, bf16[128,2048]{1,0:T(8,128)(2,1)}, u32[]{:S(2)}, u32[]{:S(2)}) %collective-permute-start.7) | collective-permute-done | bytes 524320 | tf_op jit(solution)/shard_map/ppermute | solution.py:20
  105.2 3.4 %copy-done.1 = bf16[2048,2048]{1,0:T(8,128)(2,1)S(1)} copy-done((bf16[2048,2048]{1,0:T(8,128)(2,1)S(1)}, bf16[2048,2048]{1,0:T(8,128)(2,1)}, u32[]{:S(2)}) %copy-start.1) | copy-done | bytes 8388632
  108.6 4.5 %shard_map.106 = (f32[128,2048]{1,0:T(8,128)S(1)}, bf16[128,2048]{1,0:T(8,128)(2,1)S(1)}) custom-call(s32[1]{0:T(128)} %bitcast.1.share, bf16[128,2048]{1,0:T(8,128)(2,1)} %collective-permute-done.7.refs_0_, bf16[128,2048]{1,0:T(8,128)(2,1)S(1)} %collective-permute-done.6.refs_1_, bf16[2048,2048]{1,0:T(8,128)(2,1)S(1)} %copy-done.1), custom_call_target="tpu_custom_call" | custom-call | flops 1 | bytes 1 | tf_op jit(solution)/shard_map/pallas_call | solution.py:56
  116.2 3.0 %collective-permute-done.14.refs_0_ = bf16[128,2048]{1,0:T(8,128)(2,1)S(1)} collective-permute-done((bf16[128,2048]{1,0:T(8,128)(2,1)S(1)}, bf16[128,2048]{1,0:T(8,128)(2,1)S(1)}, u32[]{:S(2)}, u32[]{:S(2)}) %collective-permute-start.14) | collective-permute-done | bytes 524320 | tf_op jit(solution)/shard_map/ppermute | solution.py:27
  119.3 2.7 %shard_map.107 = (f32[64,2048]{1,0:T(8,128)S(1)}, bf16[64,2048]{1,0:T(8,128)(2,1)S(1)}) custom-call(s32[1]{0:T(128)} %bitcast.1.share, bf16[128,2048]{1,0:T(8,128)(2,1)S(1)} %collective-permute-done.14.refs_0_, bf16[2048,2048]{1,0:T(8,128)(2,1)S(1)} %copy-done.1), custom_call_target="tpu_custom_call" | custom-call | flops 1 | bytes 1 | tf_op jit(solution)/shard_map/pallas_call | solution.py:56
  125.8 4.3 %collective-permute-done.13.refs_0_ = bf16[128,2048]{1,0:T(8,128)(2,1)S(1)} collective-permute-done((bf16[128,2048]{1,0:T(8,128)(2,1)S(1)}, bf16[128,2048]{1,0:T(8,128)(2,1)S(1)}, u32[]{:S(2)}, u32[]{:S(2)}) %collective-permute-start.13) | collective-permute-done | bytes 524320 | tf_op jit(solution)/shard_map/ppermute | solution.py:27
  131.2 2.4 %collective-permute-done.18 = bf16[32,2048]{1,0:T(8,128)(2,1)S(1)} collective-permute-done((bf16[32,2048]{1,0:T(8,128)(2,1)S(1)}, bf16[32,2048]{1,0:T(8,128)(2,1)S(1)}, u32[]{:S(2)}, u32[]{:S(2)}) %collective-permute-start.18) | collective-permute-done | bytes 131104 | tf_op jit(solution)/shard_map/ppermute | solution.py:20
  137.8 2.6 %shard_map.108 = (f32[32,2048]{1,0:T(8,128)S(1)}, bf16[32,2048]{1,0:T(8,128)(2,1)S(1)}, bf16[32,2048]{1,0:T(8,128)(2,1)S(1)}, bf16[32,2048]{1,0:T(8,128)(2,1)S(1)}) custom-call(s32[1]{0:T(128)} %bitcast.1.share, bf16[128,2048]{1,0:T(8,128)(2,1)S(1)} %collective-permute-done.13.refs_0_, bf16[2048,2048]{1,0:T(8,128)(2,1)S(1)} %copy-done.1), custom_call_target="tpu_custom_call" | custom-call | flops 1 | bytes 1 | tf_op jit(solution)/shard_map/pallas_call | solution.py:56
  141.4 7.7 %collective-permute-done.23 = bf16[32,2048]{1,0:T(8,128)(2,1)S(1)} collective-permute-done((bf16[32,2048]{1,0:T(8,128)(2,1)S(1)}, bf16[32,2048]{1,0:T(8,128)(2,1)S(1)}, u32[]{:S(2)}, u32[]{:S(2)}) %collective-permute-start.23) | collective-permute-done | bytes 131104 | tf_op jit(solution)/shard_map/ppermute | solution.py:20
  149.4 5.0 %collective-permute-done.26 = bf16[32,2048]{1,0:T(8,128)(2,1)S(1)} collective-permute-done((bf16[32,2048]{1,0:T(8,128)(2,1)S(1)}, bf16[32,2048]{1,0:T(8,128)(2,1)S(1)}, u32[]{:S(2)}, u32[]{:S(2)}) %collective-permute-start.26) | collective-permute-done | bytes 131104 | tf_op jit(solution)/shard_map/ppermute | solution.py:20
  154.6 8.0 %collective-permute-done.27 = bf16[32,2048]{1,0:T(8,128)(2,1)S(1)} collective-permute-done((bf16[32,2048]{1,0:T(8,128)(2,1)S(1)}, bf16[32,2048]{1,0:T(8,128)(2,1)S(1)}, u32[]{:S(2)}, u32[]{:S(2)}) %collective-permute-start.27) | collective-permute-done | bytes 131104 | tf_op jit(solution)/shard_map/ppermute | solution.py:20
  (93 shorter events, 34.1 us)
Async XLA Ops:
  4.0 14.8 %collective-permute-start = (bf16[8,32,512]{2,1,0:T(8,128)(2,1)}, bf16[8,32,512]{2,1,0:T(8,128)(2,1)S(1)}, u32[]{:S(2)}, u32[]{:S(2)}) collective-permute-start(bf16[8,32,512]{2,1,0:T(8,128)(2,1)} %get-tuple-element.63), channel_id=1, source_target_pairs={{0,4},{4,0},{8,12},{12,8},{1,5},{5,1},{9,13},{13,9},{2,6},{6,2},{1... | collective-permute-start | bytes 786440 | tf_op jit(solution)/shard_map/ppermute | solution.py:20
  7.5 21.6 %collective-permute-start.1 = (bf16[8,32,512]{2,1,0:T(8,128)(2,1)}, bf16[8,32,512]{2,1,0:T(8,128)(2,1)S(1)}, u32[]{:S(2)}, u32[]{:S(2)}) collective-permute-start(bf16[8,32,512]{2,1,0:T(8,128)(2,1)} %get-tuple-element.64), channel_id=1, source_target_pairs={{0,8},{4,12},{8,0},{12,4},{1,9},{5,13},{9,1},{13,5},{2,10},{6,14},... | collective-permute-start | bytes 786440 | tf_op jit(solution)/shard_map/ppermute | solution.py:20
  10.1 19.0 %collective-permute-start.2 = (bf16[8,32,512]{2,1,0:T(8,128)(2,1)}, bf16[8,32,512]{2,1,0:T(8,128)(2,1)S(1)}, u32[]{:S(2)}, u32[]{:S(2)}) collective-permute-start(bf16[8,32,512]{2,1,0:T(8,128)(2,1)} %get-tuple-element.65), channel_id=1, source_target_pairs={{0,12},{4,8},{8,4},{12,0},{1,13},{5,9},{9,5},{13,1},{2,14},{6,10},... | collective-permute-start | bytes 786440 | tf_op jit(solution)/shard_map/ppermute | solution.py:20
  32.3 11.3 %collective-permute-start.4 = (bf16[2,256,512]{2,1,0:T(8,128)(2,1)}, bf16[2,256,512]{2,1,0:T(8,128)(2,1)S(1)}, u32[]{:S(2)}, u32[]{:S(2)}) collective-permute-start(bf16[2,256,512]{2,1,0:T(8,128)(2,1)} %bitcast.12), channel_id=1, source_target_pairs={{0,2},{2,0},{1,3},{3,1},{4,6},{6,4},{5,7},{7,5},{8,10},{10,8},{9,1... | collective-permute-start | bytes 1572872 | tf_op jit(solution)/shard_map/ppermute | solution.py:20
  34.5 9.1 %collective-permute-start.3 = (bf16[2,256,512]{2,1,0:T(8,128)(2,1)}, bf16[2,256,512]{2,1,0:T(8,128)(2,1)S(1)}, u32[]{:S(2)}, u32[]{:S(2)}) collective-permute-start(bf16[2,256,512]{2,1,0:T(8,128)(2,1)} %bitcast.13), channel_id=1, source_target_pairs={{0,1},{1,0},{2,3},{3,2},{4,5},{5,4},{6,7},{7,6},{8,9},{9,8},{10,11... | collective-permute-start | bytes 1572872 | tf_op jit(solution)/shard_map/ppermute | solution.py:20
  54.7 19.0 %collective-permute-start.8 = (bf16[128,2048]{1,0:T(8,128)(2,1)S(1)}, bf16[128,2048]{1,0:T(8,128)(2,1)S(1)}, u32[]{:S(2)}, u32[]{:S(2)}) collective-permute-start(bf16[128,2048]{1,0:T(8,128)(2,1)S(1)} %shard_map.103.refs_0_), channel_id=1, source_target_pairs={{0,12},{4,8},{8,4},{12,0},{1,13},{5,9},{9,5},{13,1},{2,14},{6,10},... | collective-permute-start | bytes 1572872 | tf_op jit(solution)/shard_map/ppermute | solution.py:20
  56.1 26.5 %collective-permute-start.9 = (bf16[128,2048]{1,0:T(8,128)(2,1)S(1)}, bf16[128,2048]{1,0:T(8,128)(2,1)S(1)}, u32[]{:S(2)}, u32[]{:S(2)}) collective-permute-start(bf16[128,2048]{1,0:T(8,128)(2,1)S(1)} %shard_map.103.refs_0_), channel_id=1, source_target_pairs={{0,4},{4,0},{8,12},{12,8},{1,5},{5,1},{9,13},{13,9},{2,6},{6,2},{1... | collective-permute-start | bytes 1572872 | tf_op jit(solution)/shard_map/ppermute | solution.py:20
  68.6 25.3 %collective-permute-start.6 = (bf16[128,2048]{1,0:T(8,128)(2,1)S(1)}, bf16[128,2048]{1,0:T(8,128)(2,1)S(1)}, u32[]{:S(2)}, u32[]{:S(2)}) collective-permute-start(bf16[128,2048]{1,0:T(8,128)(2,1)S(1)} %shard_map.102.refs_1_), channel_id=1, source_target_pairs={{0,12},{4,8},{8,4},{12,0},{1,13},{5,9},{9,5},{13,1},{2,14},{6,10},... | collective-permute-start | bytes 1572872 | tf_op jit(solution)/shard_map/ppermute | solution.py:20
  70.0 34.3 %collective-permute-start.7 = (bf16[128,2048]{1,0:T(8,128)(2,1)S(1)}, bf16[128,2048]{1,0:T(8,128)(2,1)}, u32[]{:S(2)}, u32[]{:S(2)}) collective-permute-start(bf16[128,2048]{1,0:T(8,128)(2,1)S(1)} %shard_map.102.refs_1_), channel_id=1, source_target_pairs={{0,4},{4,0},{8,12},{12,8},{1,5},{5,1},{9,13},{13,9},{2,6},{6,2},{1... | collective-permute-start | bytes 1572872 | tf_op jit(solution)/shard_map/ppermute | solution.py:20
  87.7 16.6 %collective-permute-start.10 = (bf16[64,2048]{1,0:T(8,128)(2,1)}, bf16[64,2048]{1,0:T(8,128)(2,1)}, u32[]{:S(2)}, u32[]{:S(2)}) collective-permute-start(bf16[64,2048]{1,0:T(8,128)(2,1)} %get-tuple-element.75), channel_id=1, source_target_pairs={{0,1},{1,0},{2,3},{3,2},{4,5},{5,4},{6,7},{7,6},{8,9},{9,8},{10,11... | collective-permute-start | bytes 786440 | tf_op jit(solution)/shard_map/ppermute | solution.py:20
  87.7 16.6 %collective-permute-start.11 = (bf16[64,2048]{1,0:T(8,128)(2,1)}, bf16[64,2048]{1,0:T(8,128)(2,1)}, u32[]{:S(2)}, u32[]{:S(2)}) collective-permute-start(bf16[64,2048]{1,0:T(8,128)(2,1)} %get-tuple-element.76), channel_id=1, source_target_pairs={{0,2},{1,3},{2,0},{3,1},{4,6},{5,7},{6,4},{7,5},{8,10},{9,11},{10,... | collective-permute-start | bytes 786440 | tf_op jit(solution)/shard_map/ppermute | solution.py:20
  88.7 15.6 %collective-permute-start.12 = (bf16[64,2048]{1,0:T(8,128)(2,1)S(1)}, bf16[64,2048]{1,0:T(8,128)(2,1)}, u32[]{:S(2)}, u32[]{:S(2)}) collective-permute-start(bf16[64,2048]{1,0:T(8,128)(2,1)S(1)} %get-tuple-element.77), channel_id=1, source_target_pairs={{0,3},{1,2},{2,1},{3,0},{4,7},{5,6},{6,5},{7,4},{8,11},{9,10},{10,... | collective-permute-start | bytes 786440 | tf_op jit(solution)/shard_map/ppermute | solution.py:20
  104.3 10.4 %collective-permute-start.19 = (bf16[128,2048]{1,0:T(8,128)(2,1)}, bf16[128,2048]{1,0:T(8,128)(2,1)S(1)}, u32[]{:S(2)}, u32[]{:S(2)}) collective-permute-start(bf16[128,2048]{1,0:T(8,128)(2,1)} %copy-done.10), channel_id=1, source_target_pairs={{0,1},{1,0},{2,3},{3,2},{4,5},{5,4},{6,7},{7,6},{8,9},{9,8},{10,11... | collective-permute-start | bytes 1572872 | tf_op jit(solution)/shard_map/ppermute | solution.py:20
  104.5 14.8 %collective-permute-start.14 = (bf16[128,2048]{1,0:T(8,128)(2,1)S(1)}, bf16[128,2048]{1,0:T(8,128)(2,1)S(1)}, u32[]{:S(2)}, u32[]{:S(2)}) collective-permute-start(bf16[128,2048]{1,0:T(8,128)(2,1)S(1)} %broadcast_select_fusion), channel_id=1, source_target_pairs={{0,8},{12,4},{4,0},{8,12},{1,9},{13,5},{5,1},{9,13},{2,10},{14,6},... | collective-permute-start | bytes 1572872 | tf_op jit(solution)/shard_map/ppermute | solution.py:27
  113.4 16.7 %collective-permute-start.13 = (bf16[128,2048]{1,0:T(8,128)(2,1)S(1)}, bf16[128,2048]{1,0:T(8,128)(2,1)S(1)}, u32[]{:S(2)}, u32[]{:S(2)}) collective-permute-start(bf16[128,2048]{1,0:T(8,128)(2,1)S(1)} %broadcast_select_fusion.1), channel_id=1, source_target_pairs={{0,8},{12,4},{4,0},{8,12},{1,9},{13,5},{5,1},{9,13},{2,10},{14,6},... | collective-permute-start | bytes 1572872 | tf_op jit(solution)/shard_map/ppermute | solution.py:27
  114.8 15.3 %collective-permute-start.20 = (bf16[64,2048]{1,0:T(8,128)(2,1)S(1)}, bf16[64,2048]{1,0:T(8,128)(2,1)S(1)}, u32[]{:S(2)}, u32[]{:S(2)}) collective-permute-start(bf16[64,2048]{1,0:T(8,128)(2,1)S(1)} %add_convert_fusion.2), channel_id=1, source_target_pairs={{0,2},{2,0},{1,3},{3,1},{4,6},{6,4},{5,7},{7,5},{8,10},{10,8},{9,1... | collective-permute-start | bytes 786440 | tf_op jit(solution)/shard_map/ppermute | solution.py:20
  122.1 9.2 %collective-permute-start.16 = (bf16[64,2048]{1,0:T(8,128)(2,1)S(1)}, bf16[64,2048]{1,0:T(8,128)(2,1)S(1)}, u32[]{:S(2)}, u32[]{:S(2)}) collective-permute-start(bf16[64,2048]{1,0:T(8,128)(2,1)S(1)} %add_convert_fusion.3), channel_id=1, source_target_pairs={{0,2},{2,0},{1,3},{3,1},{4,6},{6,4},{5,7},{7,5},{8,10},{10,8},{9,1... | collective-permute-start | bytes 786440 | tf_op jit(solution)/shard_map/ppermute | solution.py:20
  123.6 10.1 %collective-permute-start.18 = (bf16[32,2048]{1,0:T(8,128)(2,1)S(1)}, bf16[32,2048]{1,0:T(8,128)(2,1)S(1)}, u32[]{:S(2)}, u32[]{:S(2)}) collective-permute-start(bf16[32,2048]{1,0:T(8,128)(2,1)S(1)} %add_convert_fusion.7), channel_id=1, source_target_pairs={{0,2},{2,0},{1,3},{3,1},{4,6},{6,4},{5,7},{7,5},{8,10},{10,8},{9,1... | collective-permute-start | bytes 393224 | tf_op jit(solution)/shard_map/ppermute | solution.py:20
  133.7 15.5 %collective-permute-start.23 = (bf16[32,2048]{1,0:T(8,128)(2,1)S(1)}, bf16[32,2048]{1,0:T(8,128)(2,1)S(1)}, u32[]{:S(2)}, u32[]{:S(2)}) collective-permute-start(bf16[32,2048]{1,0:T(8,128)(2,1)S(1)} %add_convert_fusion.6), channel_id=1, source_target_pairs={{0,8},{4,12},{8,0},{12,4},{1,9},{5,13},{9,1},{13,5},{2,10},{6,14},... | collective-permute-start | bytes 393224 | tf_op jit(solution)/shard_map/ppermute | solution.py:20
  135.5 18.9 %collective-permute-start.22 = (bf16[64,2048]{1,0:T(8,128)(2,1)S(1)}, bf16[64,2048]{1,0:T(8,128)(2,1)S(1)}, u32[]{:S(2)}, u32[]{:S(2)}) collective-permute-start(bf16[64,2048]{1,0:T(8,128)(2,1)S(1)} %pad_maximum_fusion.1), channel_id=1, source_target_pairs={{0,12},{4,8},{8,4},{12,0},{1,13},{5,9},{9,5},{13,1},{2,14},{6,10},... | collective-permute-start | bytes 786440 | tf_op jit(solution)/shard_map/ppermute | solution.py:20
  137.7 16.6 %collective-permute-start.21 = (bf16[64,2048]{1,0:T(8,128)(2,1)S(1)}, bf16[64,2048]{1,0:T(8,128)(2,1)S(1)}, u32[]{:S(2)}, u32[]{:S(2)}) collective-permute-start(bf16[64,2048]{1,0:T(8,128)(2,1)S(1)} %pad_maximum_fusion), channel_id=1, source_target_pairs={{0,4},{4,0},{8,12},{12,8},{1,5},{5,1},{9,13},{13,9},{2,6},{6,2},{1... | collective-permute-start | bytes 786440 | tf_op jit(solution)/shard_map/ppermute | solution.py:20
  140.4 9.0 %collective-permute-start.24 = (bf16[32,2048]{1,0:T(8,128)(2,1)S(1)}, bf16[32,2048]{1,0:T(8,128)(2,1)S(1)}, u32[]{:S(2)}, u32[]{:S(2)}) collective-permute-start(bf16[32,2048]{1,0:T(8,128)(2,1)S(1)} %get-tuple-element.107), channel_id=1, source_target_pairs={{0,1},{1,0},{2,3},{3,2},{4,5},{5,4},{6,7},{7,6},{8,9},{9,8},{10,11... | collective-permute-start | bytes 393224 | tf_op jit(solution)/shard_map/ppermute | solution.py:20
  140.5 8.9 %collective-permute-start.25 = (bf16[32,2048]{1,0:T(8,128)(2,1)S(1)}, bf16[32,2048]{1,0:T(8,128)(2,1)S(1)}, u32[]{:S(2)}, u32[]{:S(2)}) collective-permute-start(bf16[32,2048]{1,0:T(8,128)(2,1)S(1)} %get-tuple-element.108), channel_id=1, source_target_pairs={{0,2},{1,3},{2,0},{3,1},{4,6},{5,7},{6,4},{7,5},{8,10},{9,11},{10,... | collective-permute-start | bytes 393224 | tf_op jit(solution)/shard_map/ppermute | solution.py:20
  154.4 8.2 %collective-permute-start.27 = (bf16[32,2048]{1,0:T(8,128)(2,1)S(1)}, bf16[32,2048]{1,0:T(8,128)(2,1)S(1)}, u32[]{:S(2)}, u32[]{:S(2)}) collective-permute-start(bf16[32,2048]{1,0:T(8,128)(2,1)S(1)} %add_convert_fusion.5), channel_id=1, source_target_pairs={{0,8},{4,12},{8,0},{12,4},{1,9},{5,13},{9,1},{13,5},{2,10},{6,14},... | collective-permute-start | bytes 393224 | tf_op jit(solution)/shard_map/ppermute | solution.py:20
  (19 other events, 208.0 us)

commit v14 on v13

--- a/solution.py
+++ b/solution.py
@@ -105,13 +105,13 @@
 
 
 def fetch_kernel(
-    place, holder, block, serving, counts, store, where, scalars, *refs, pool_size, share_count
+    place, holder, block, serving, store, where, *refs, pool_size, share_count
 ):
     pieces, (table, rank_of, sems) = refs[:pool_size], refs[pool_size:]
     pool_index, share = place[0], place[1]
     capacity = pieces[0].shape[0]
     blocks_each = holder.shape[1]
-    requests_here = scalars.shape[0] - 1
+    requests_here = where.shape[1] // blocks_each
     spare = pool_size * capacity
     copies = []
     for flip in range(pool_size):
@@ -131,10 +131,8 @@
             copies[-1].start()
     for i in range(pool_size):
         rank_of[i] = 0
-    scalars[0] = share
     for i in range(requests_here):
         request = serving[pool_index * requests_here + i]
-        scalars[1 + i] = counts[request]
         for j in range(blocks_each):
             held_by = holder[request, j]
             where[0, i * blocks_each + j] = held_by ^ pool_index
@@ -144,33 +142,27 @@
         copy.wait()
 
 
-def fetch(latent_store, place_holder, place_block, serving_request, image_count, items):
+def fetch(place, latent_store, place_holder, place_block, serving_request, items):
     pool_size = lax.axis_size("pool")
     share_count = lax.axis_size(("heads", "sub"))
-    place = jnp.stack([lax.axis_index("pool"), lax.axis_index(("heads", "sub"))])
     capacity = 2 * ((items + pool_size - 1) // pool_size)
     rows = BLK // share_count
     store = latent_store.reshape(-1, rows, latent_store.shape[1])
     piece = jax.ShapeDtypeStruct((capacity, rows, store.shape[2]), store.dtype)
-    requests_here = items // place_holder.shape[1]
     smem = pl.BlockSpec(memory_space=pltpu.SMEM)
-    where, scalars, *pieces = pl.pallas_call(
+    where, *pieces = pl.pallas_call(
         functools.partial(fetch_kernel, pool_size=pool_size, share_count=share_count),
-        in_specs=[smem] * 5 + [pl.BlockSpec(memory_space=pltpu.HBM)],
-        out_specs=[smem, smem] + [pl.BlockSpec(memory_space=pltpu.VMEM)] * pool_size,
-        out_shape=[
-            jax.ShapeDtypeStruct((2, items), jnp.int32),
-            jax.ShapeDtypeStruct((1 + requests_here,), jnp.int32),
-        ]
-        + [piece] * pool_size,
+        in_specs=[smem] * 4 + [pl.BlockSpec(memory_space=pltpu.HBM)],
+        out_specs=[smem] + [pl.BlockSpec(memory_space=pltpu.VMEM)] * pool_size,
+        out_shape=[jax.ShapeDtypeStruct((2, items), jnp.int32)] + [piece] * pool_size,
         scratch_shapes=[
             pltpu.SMEM((pool_size * capacity + 1,), jnp.int32),
             pltpu.SMEM((pool_size,), jnp.int32),
             pltpu.SemaphoreType.DMA((pool_size * capacity,)),
         ],
         cost_estimate=LIGHT,
-    )(place.astype(jnp.int32), place_holder, place_block, serving_request, image_count, store)
-    return where, scalars, pieces
+    )(place, place_holder, place_block, serving_request, store)
+    return where, pieces
 
 
 def choose_kernel(where, *refs):
@@ -191,23 +183,25 @@
         in_specs=[pl.BlockSpec(memory_space=pltpu.SMEM)] + [whole] * len(pieces),
         out_specs=whole,
         out_shape=jax.ShapeDtypeStruct((where.shape[1], *pieces[0].shape[1:]), pieces[0].dtype),
+        compiler_params=pltpu.CompilerParams(vmem_limit_bytes=8 * 1024 * 1024),
         cost_estimate=LIGHT,
     )(where, *pieces)
 
 
 def attend_kernel(share_count, scalars, queries, *refs):
-    parts, (kv_up, q_gain, k_gain, out, keys, values) = refs[:share_count], refs[share_count:]
+    parts, (kv_up, gains, out, keys, values) = refs[:share_count], refs[share_count:]
     request = pl.program_id(0)
-    head_width = q_gain.shape[1]
+    q_gain, k_gain = gains[0:1, :], gains[1:2, :]
+    head_width = gains.shape[1]
     text, width = out.shape
     per_group = width // head_width
     part_slots = parts[0].shape[1]
     share_rows = BLK // share_count
-    count, share = scalars[1 + request], scalars[0]
+    share, count = scalars[0], scalars[1 + request]
     for flip in range(share_count):
         rows = pl.ds(flip * part_slots, part_slots)
         projected = jnp.dot(parts[flip][request], kv_up[...], preferred_element_type=jnp.float32)
-        key = rms_scale(projected[:, :head_width], k_gain[...])
+        key = rms_scale(projected[:, :head_width], k_gain)
         keys[rows, :] = key.astype(jnp.bfloat16)
         slot = lax.broadcasted_iota(jnp.int32, (part_slots, head_width), 0)
         position = (slot // share_rows) * BLK + (share ^ flip) * share_rows + slot % share_rows
@@ -221,7 +215,7 @@
         for head in range(first, first + together):
             query = queries[0, :, :, head * head_width : (head + 1) * head_width]
             query = query.reshape(text, head_width).astype(jnp.float32)
-            normed.append(rms_scale(query, q_gain[...]).astype(jnp.bfloat16))
+            normed.append(rms_scale(query, q_gain).astype(jnp.bfloat16))
         scores = lax.dot_general(
             jnp.concatenate(normed, axis=0),
             keys[...],
@@ -237,10 +231,10 @@
             out[:, columns] = result[i * text : (i + 1) * text]
 
 
-def attend(chunk, rows, queries, parts, kv_flat, q_gain, k_gain, scalars):
+def attend(chunk, rows, queries, parts, kv_flat, gains, scalars):
     requests, request_shares, _, width = queries.shape
     heads_here, rank_width, pair_width = kv_flat.shape
-    head_width = q_gain.shape[1]
+    head_width = gains.shape[1]
     slots = len(parts) * parts[0].shape[1]
     text = request_shares * rows
     whole = pl.BlockSpec(memory_space=pltpu.VMEM)
@@ -255,7 +249,7 @@
             ),
         ]
         + [whole for _ in parts]
-        + [pl.BlockSpec((None, rank_width, pair_width), lambda r, g: (g, 0, 0)), whole, whole],
+        + [pl.BlockSpec((None, rank_width, pair_width), lambda r, g: (g, 0, 0)), whole],
         out_specs=pl.BlockSpec((text, width // heads_here), lambda r, g: (r, g)),
         out_shape=jax.ShapeDtypeStruct((requests * text, width), jnp.bfloat16),
         scratch_shapes=[
@@ -264,7 +258,7 @@
         ],
         compiler_params=pltpu.CompilerParams(vmem_limit_bytes=16 * 1024 * 1024),
         cost_estimate=LIGHT,
-    )(scalars, queries, *parts, kv_flat, q_gain, k_gain)
+    )(scalars, queries, *parts, kv_flat, gains)
 
 
 def per_device(
@@ -290,14 +284,21 @@
     items = requests_here * blocks_each
     rank_width = latent_store.shape[1]
     tie = lax.optimization_barrier
-    where, scalars, pieces = fetch(
-        latent_store, place_holder, place_block, serving_request, image_count, items
-    )
+    place = jnp.stack([pool_index, share]).astype(jnp.int32)
+    where, pieces = fetch(place, latent_store, place_holder, place_block, serving_request, items)
     kv_flat = jnp.moveaxis(kv_up.reshape(rank_width, kv_up.shape[1], -1), 1, 0)
-    gains = q_gain.reshape(1, -1), k_gain.reshape(1, -1)
+    gains = jnp.stack([q_gain, k_gain])
+    request_ids = jnp.arange(serving_request.shape[0], dtype=jnp.int32)
+    served_here = lax.dynamic_slice_in_dim(
+        serving_request, pool_index * requests_here, requests_here
+    )
+    count_here = jnp.sum(
+        jnp.where(served_here[:, None] == request_ids[None, :], image_count[None, :], 0), axis=1
+    )
+    scalars = jnp.concatenate([share.reshape(1), count_here])
     arriving = [swap(pieces[flip], "pool", flip) for flip in range(1, pool_size)]
     chosen = choose(where, pieces[:1] + arriving)
-    chosen, kv_flat, scalars = tie((chosen, kv_flat, scalars))
+    chosen, kv_flat, gains, scalars = tie((chosen, kv_flat, gains, scalars))
     chosen = chosen.reshape(requests_here, -1, rank_width)
     over_heads = [chosen] + [swap(chosen, "heads", flip) for flip in range(1, heads_size)]
     parts = []
@@ -311,7 +312,7 @@
     def attended(chunk):
         rows = chunk_rows[chunk]
         start = sum(chunk_rows[:chunk]) // rows
-        return attend(start, rows, shaped, parts, kv_flat, *gains, scalars)
+        return attend(start, rows, shaped, parts, kv_flat, gains, scalars)
 
     columns = out_weight.shape[1]
     if pool_size != 4:

time: 164 us -> 160 us (0.976)
  waiting for transfers between devices: 83.5 us -> 78.4 us
  other arithmetic: 2.45 us -> 5.26 us
    ppermute x26, waiting for transfers between devices: 76.1 us -> 72 us  [swap(): lax.ppermute(values, axis, [(i, i ^ flip) for i in range(lax.axis_size(ax...]
    unnamed x30 -> x16, local copies, waits for them, and re-layouts: 8.05 us -> 5.99 us
  transfers between devices with their start and end apart: 28 -> 28, of which waited for: 15 -> 15; matrix products, arithmetic and copies ran while one was open for 3% -> 5% of each run, Pallas kernels for 15% -> 15%
where the time goes in v14:
time: 160 us; the launch traced here: 159 us
  waiting for transfers between devices  78.4 us (49%)
  Pallas kernels  34.6 us (22%)
  starting transfers between devices  30.7 us (19%)
  local copies, waits for them, and re-layouts  9.93 us (6%)
  other arithmetic  5.26 us (3%)
    ppermute x26, waiting for transfers between devices, swap(): lax.ppermute(values, axis, [(i, i ^ flip) for i in range(lax.axis_size(ax...  72 us
    ppermute x26, starting transfers between devices, swap(): lax.ppermute(values, axis, [(i, i ^ flip) for i in range(lax.axis_size(ax...  27.6 us
    pallas_call x5, Pallas kernels, project_out(): pl.pallas_call(functools.partial(project_kernel, len(blocks), list(range(...  17.7 us
    pallas_call x2, Pallas kernels, attend(): pl.pallas_call(functools.partial(attend_kernel, len(parts)), grid=(reques...  12.3 us
    ppermute x2, waiting for transfers between devices, second_hop(): return lax.ppermute(passed, 'pool', [(0, 2), (3, 1), (1, 0), (2, 3)])  6.31 us
    unnamed x16, local copies, waits for them, and re-layouts  5.99 us
    pallas_call x1, Pallas kernels, fetch(): pl.pallas_call(functools.partial(fetch_kernel, pool_size=pool_size, share...  3.75 us
  transfers between devices with their start and end apart: 28, of which 15 were waited for; matrix products, arithmetic and copies ran while one was open for 5% of the time, Pallas kernels for 15%

profile of v14, /device:TPU:0, one launch (start us, length us, event | category | flops | bytes accessed | tf_op | source)
XLA Modules:
  0.0 159.2 jit_solution(3273003134222858755)
XLA Ops:
  0.6 3.8 %shard_map.100 = (s32[2,16]{1,0:T(2,128)}, bf16[8,32,512]{2,1,0:T(8,128)(2,1)}, bf16[8,32,512]{2,1,0:T(8,128)(2,1)}, bf16[8,32,512]{2,1,0:T(8,128)(2,1)}, bf16[8,32,512]{2,1,0:T(8,128)(2,1)}) custom-call(s32[2]{0:T(128)} %pad_add_fusion.place, s32[8,8]{1,0:T(8,128)} %holder.1, s32[8,8]{1,0:T(8,128)} %block.1, s32[8]{0:T(128)} %serving.1, ...), custom_call_target="tpu_custom_call" | custom-call | flops 1 | bytes 1 | tf_op jit(solution)/shard_map/pallas_call | solution.py:153
  4.4 3.1 %collective-permute-start = (bf16[8,32,512]{2,1,0:T(8,128)(2,1)}, bf16[8,32,512]{2,1,0:T(8,128)(2,1)S(1)}, u32[]{:S(2)}, u32[]{:S(2)}) collective-permute-start(bf16[8,32,512]{2,1,0:T(8,128)(2,1)} %get-tuple-element.63), channel_id=1, source_target_pairs={{0,4},{4,0},{8,12},{12,8},{1,5},{5,1},{9,13},{13,9},{2,6},{6,2},{1... | collective-permute-start | bytes 786440 | tf_op jit(solution)/shard_map/ppermute | solution.py:20
  7.5 2.6 %collective-permute-start.1 = (bf16[8,32,512]{2,1,0:T(8,128)(2,1)}, bf16[8,32,512]{2,1,0:T(8,128)(2,1)S(1)}, u32[]{:S(2)}, u32[]{:S(2)}) collective-permute-start(bf16[8,32,512]{2,1,0:T(8,128)(2,1)} %get-tuple-element.64), channel_id=1, source_target_pairs={{0,8},{4,12},{8,0},{12,4},{1,9},{5,13},{9,1},{13,5},{2,10},{6,14},... | collective-permute-start | bytes 786440 | tf_op jit(solution)/shard_map/ppermute | solution.py:20
  15.0 3.8 %collective-permute-done.refs_1_ = bf16[8,32,512]{2,1,0:T(8,128)(2,1)S(1)} collective-permute-done((bf16[8,32,512]{2,1,0:T(8,128)(2,1)}, bf16[8,32,512]{2,1,0:T(8,128)(2,1)S(1)}, u32[]{:S(2)}, u32[]{:S(2)}) %collective-permute-start) | collective-permute-done | bytes 262176 | tf_op jit(solution)/shard_map/ppermute | solution.py:20
  18.8 10.3 %collective-permute-done.1.refs_2_ = bf16[8,32,512]{2,1,0:T(8,128)(2,1)S(1)} collective-permute-done((bf16[8,32,512]{2,1,0:T(8,128)(2,1)}, bf16[8,32,512]{2,1,0:T(8,128)(2,1)S(1)}, u32[]{:S(2)}, u32[]{:S(2)}) %collective-permute-start.1) | collective-permute-done | bytes 262176 | tf_op jit(solution)/shard_map/ppermute | solution.py:20
  33.9 9.2 %collective-permute-done.4.refs_2_ = bf16[2,256,512]{2,1,0:T(8,128)(2,1)S(1)} collective-permute-done((bf16[2,256,512]{2,1,0:T(8,128)(2,1)S(1)}, bf16[2,256,512]{2,1,0:T(8,128)(2,1)S(1)}, u32[]{:S(2)}, u32[]{:S(2)}) %collective-permute-start.4) | collective-permute-done | bytes 524320 | tf_op jit(solution)/shard_map/ppermute | solution.py:20
  45.0 6.1 %shard_map.103.refs_0_ = bf16[128,2048]{1,0:T(8,128)(2,1)S(1)} custom-call(s32[3]{0:T(128)S(1)} %pad_add_fusion.1.scalars, bf16[2,2,64,2048]{3,2,1,0:T(8,128)(2,1)S(1)} %bitcast.16, bf16[2,256,512]{2,1,0:T(8,128)(2,1)S(1)} %bitcast.14, bf16[2,256,512]{2,1,0:T(8,128)(2,1)S(1)} %collective-permute-done.3.refs_1_, ...), custom_call_target="tpu_custom_call" | custom-call | flops 1 | bytes 1 | tf_op jit(solution)/shard_map/pallas_call | solution.py:241
  51.1 2.6 %collective-permute-start.8 = (bf16[128,2048]{1,0:T(8,128)(2,1)S(1)}, bf16[128,2048]{1,0:T(8,128)(2,1)S(1)}, u32[]{:S(2)}, u32[]{:S(2)}) collective-permute-start(bf16[128,2048]{1,0:T(8,128)(2,1)S(1)} %shard_map.103.refs_0_), channel_id=1, source_target_pairs={{0,12},{4,8},{8,4},{12,0},{1,13},{5,9},{9,5},{13,1},{2,14},{6,10},... | collective-permute-start | bytes 1572872 | tf_op jit(solution)/shard_map/ppermute | solution.py:20
  53.6 5.3 %collective-permute-start.9 = (bf16[128,2048]{1,0:T(8,128)(2,1)S(1)}, bf16[128,2048]{1,0:T(8,128)(2,1)S(1)}, u32[]{:S(2)}, u32[]{:S(2)}) collective-permute-start(bf16[128,2048]{1,0:T(8,128)(2,1)S(1)} %shard_map.103.refs_0_), channel_id=1, source_target_pairs={{0,4},{4,0},{8,12},{12,8},{1,5},{5,1},{9,13},{13,9},{2,6},{6,2},{1... | collective-permute-start | bytes 1572872 | tf_op jit(solution)/shard_map/ppermute | solution.py:20
  58.9 6.1 %shard_map.102.refs_1_ = bf16[128,2048]{1,0:T(8,128)(2,1)S(1)} custom-call(s32[3]{0:T(128)S(1)} %pad_add_fusion.1.scalars, bf16[2,2,64,2048]{3,2,1,0:T(8,128)(2,1)S(1)} %bitcast.17, bf16[2,256,512]{2,1,0:T(8,128)(2,1)S(1)} %bitcast.15, bf16[2,256,512]{2,1,0:T(8,128)(2,1)S(1)} %collective-permute-done.3.refs_1_, ...), custom_call_target="tpu_custom_call" | custom-call | flops 1 | bytes 1 | tf_op jit(solution)/shard_map/pallas_call | solution.py:241
  66.2 4.2 %shard_map.104 = (f32[128,2048]{1,0:T(8,128)S(1)}, bf16[128,2048]{1,0:T(8,128)(2,1)}) custom-call(s32[1]{0:T(128)} %bitcast.1.share, bf16[128,2048]{1,0:T(8,128)(2,1)S(1)} %shard_map.103.refs_0_, bf16[128,2048]{1,0:T(8,128)(2,1)S(1)} %shard_map.102.refs_1_, bf16[2048,2048]{1,0:T(8,128)(2,1)S(1)} %copy-done), custom_call_target="tpu_custom_call" | custom-call | flops 1 | bytes 1 | tf_op jit(solution)/shard_map/pallas_call | solution.py:56
  71.4 7.7 %collective-permute-done.9.refs_0_ = bf16[128,2048]{1,0:T(8,128)(2,1)S(1)} collective-permute-done((bf16[128,2048]{1,0:T(8,128)(2,1)S(1)}, bf16[128,2048]{1,0:T(8,128)(2,1)S(1)}, u32[]{:S(2)}, u32[]{:S(2)}) %collective-permute-start.9) | collective-permute-done | bytes 524320 | tf_op jit(solution)/shard_map/ppermute | solution.py:20
  79.1 3.6 %shard_map.105 = (f32[64,2048]{1,0:T(8,128)S(1)}, bf16[64,2048]{1,0:T(8,128)(2,1)S(1)}, bf16[64,2048]{1,0:T(8,128)(2,1)S(1)}, bf16[64,2048]{1,0:T(8,128)(2,1)S(1)}) custom-call(s32[1]{0:T(128)} %bitcast.1.share, bf16[128,2048]{1,0:T(8,128)(2,1)S(1)} %collective-permute-done.9.refs_0_, bf16[128,2048]{1,0:T(8,128)(2,1)S(1)} %collective-permute-done.8.refs_1_, ...), custom_call_target="tpu_custom_call" | custom-call | flops 1 | bytes 1 | tf_op jit(solution)/shard_map/pallas_call | solution.py:56
  84.7 5.6 %collective-permute-done.6.refs_1_ = bf16[128,2048]{1,0:T(8,128)(2,1)S(1)} collective-permute-done((bf16[128,2048]{1,0:T(8,128)(2,1)S(1)}, bf16[128,2048]{1,0:T(8,128)(2,1)S(1)}, u32[]{:S(2)}, u32[]{:S(2)}) %collective-permute-start.6) | collective-permute-done | bytes 524320 | tf_op jit(solution)/shard_map/ppermute | solution.py:20
  90.3 10.5 %collective-permute-done.7.refs_0_ = bf16[128,2048]{1,0:T(8,128)(2,1)} collective-permute-done((bf16[128,2048]{1,0:T(8,128)(2,1)S(1)}, bf16[128,2048]{1,0:T(8,128)(2,1)}, u32[]{:S(2)}, u32[]{:S(2)}) %collective-permute-start.7) | collective-permute-done | bytes 524320 | tf_op jit(solution)/shard_map/ppermute | solution.py:20
  102.5 3.4 %copy-done.1 = bf16[2048,2048]{1,0:T(8,128)(2,1)S(1)} copy-done((bf16[2048,2048]{1,0:T(8,128)(2,1)S(1)}, bf16[2048,2048]{1,0:T(8,128)(2,1)}, u32[]{:S(2)}) %copy-start.1) | copy-done | bytes 8388632
  105.9 4.5 %shard_map.106 = (f32[128,2048]{1,0:T(8,128)S(1)}, bf16[128,2048]{1,0:T(8,128)(2,1)S(1)}) custom-call(s32[1]{0:T(128)} %bitcast.1.share, bf16[128,2048]{1,0:T(8,128)(2,1)} %collective-permute-done.7.refs_0_, bf16[128,2048]{1,0:T(8,128)(2,1)S(1)} %collective-permute-done.6.refs_1_, bf16[2048,2048]{1,0:T(8,128)(2,1)S(1)} %copy-done.1), custom_call_target="tpu_custom_call" | custom-call | flops 1 | bytes 1 | tf_op jit(solution)/shard_map/pallas_call | solution.py:56
  115.7 2.7 %shard_map.107 = (f32[64,2048]{1,0:T(8,128)S(1)}, bf16[64,2048]{1,0:T(8,128)(2,1)S(1)}) custom-call(s32[1]{0:T(128)} %bitcast.1.share, bf16[128,2048]{1,0:T(8,128)(2,1)S(1)} %collective-permute-done.14.refs_0_, bf16[2048,2048]{1,0:T(8,128)(2,1)S(1)} %copy-done.1), custom_call_target="tpu_custom_call" | custom-call | flops 1 | bytes 1 | tf_op jit(solution)/shard_map/pallas_call | solution.py:56
  122.1 4.4 %collective-permute-done.13.refs_0_ = bf16[128,2048]{1,0:T(8,128)(2,1)S(1)} collective-permute-done((bf16[128,2048]{1,0:T(8,128)(2,1)S(1)}, bf16[128,2048]{1,0:T(8,128)(2,1)S(1)}, u32[]{:S(2)}, u32[]{:S(2)}) %collective-permute-start.13) | collective-permute-done | bytes 524320 | tf_op jit(solution)/shard_map/ppermute | solution.py:27
  127.7 2.5 %collective-permute-done.18 = bf16[32,2048]{1,0:T(8,128)(2,1)S(1)} collective-permute-done((bf16[32,2048]{1,0:T(8,128)(2,1)S(1)}, bf16[32,2048]{1,0:T(8,128)(2,1)S(1)}, u32[]{:S(2)}, u32[]{:S(2)}) %collective-permute-start.18) | collective-permute-done | bytes 131104 | tf_op jit(solution)/shard_map/ppermute | solution.py:20
  134.6 2.7 %shard_map.108 = (f32[32,2048]{1,0:T(8,128)S(1)}, bf16[32,2048]{1,0:T(8,128)(2,1)S(1)}, bf16[32,2048]{1,0:T(8,128)(2,1)S(1)}, bf16[32,2048]{1,0:T(8,128)(2,1)S(1)}) custom-call(s32[1]{0:T(128)} %bitcast.1.share, bf16[128,2048]{1,0:T(8,128)(2,1)S(1)} %collective-permute-done.13.refs_0_, bf16[2048,2048]{1,0:T(8,128)(2,1)S(1)} %copy-done.1), custom_call_target="tpu_custom_call" | custom-call | flops 1 | bytes 1 | tf_op jit(solution)/shard_map/pallas_call | solution.py:56
  138.0 7.9 %collective-permute-done.23 = bf16[32,2048]{1,0:T(8,128)(2,1)S(1)} collective-permute-done((bf16[32,2048]{1,0:T(8,128)(2,1)S(1)}, bf16[32,2048]{1,0:T(8,128)(2,1)S(1)}, u32[]{:S(2)}, u32[]{:S(2)}) %collective-permute-start.23) | collective-permute-done | bytes 131104 | tf_op jit(solution)/shard_map/ppermute | solution.py:20
  146.1 4.7 %collective-permute-done.26 = bf16[32,2048]{1,0:T(8,128)(2,1)S(1)} collective-permute-done((bf16[32,2048]{1,0:T(8,128)(2,1)S(1)}, bf16[32,2048]{1,0:T(8,128)(2,1)S(1)}, u32[]{:S(2)}, u32[]{:S(2)}) %collective-permute-start.26) | collective-permute-done | bytes 131104 | tf_op jit(solution)/shard_map/ppermute | solution.py:20
  152.2 6.4 %collective-permute-done.27 = bf16[32,2048]{1,0:T(8,128)(2,1)S(1)} collective-permute-done((bf16[32,2048]{1,0:T(8,128)(2,1)S(1)}, bf16[32,2048]{1,0:T(8,128)(2,1)S(1)}, u32[]{:S(2)}, u32[]{:S(2)}) %collective-permute-start.27) | collective-permute-done | bytes 131104 | tf_op jit(solution)/shard_map/ppermute | solution.py:20
  (83 shorter events, 35.6 us)
Async XLA Ops:
  4.4 14.4 %collective-permute-start = (bf16[8,32,512]{2,1,0:T(8,128)(2,1)}, bf16[8,32,512]{2,1,0:T(8,128)(2,1)S(1)}, u32[]{:S(2)}, u32[]{:S(2)}) collective-permute-start(bf16[8,32,512]{2,1,0:T(8,128)(2,1)} %get-tuple-element.63), channel_id=1, source_target_pairs={{0,4},{4,0},{8,12},{12,8},{1,5},{5,1},{9,13},{13,9},{2,6},{6,2},{1... | collective-permute-start | bytes 786440 | tf_op jit(solution)/shard_map/ppermute | solution.py:20
  7.5 21.6 %collective-permute-start.1 = (bf16[8,32,512]{2,1,0:T(8,128)(2,1)}, bf16[8,32,512]{2,1,0:T(8,128)(2,1)S(1)}, u32[]{:S(2)}, u32[]{:S(2)}) collective-permute-start(bf16[8,32,512]{2,1,0:T(8,128)(2,1)} %get-tuple-element.64), channel_id=1, source_target_pairs={{0,8},{4,12},{8,0},{12,4},{1,9},{5,13},{9,1},{13,5},{2,10},{6,14},... | collective-permute-start | bytes 786440 | tf_op jit(solution)/shard_map/ppermute | solution.py:20
  10.1 19.0 %collective-permute-start.2 = (bf16[8,32,512]{2,1,0:T(8,128)(2,1)}, bf16[8,32,512]{2,1,0:T(8,128)(2,1)S(1)}, u32[]{:S(2)}, u32[]{:S(2)}) collective-permute-start(bf16[8,32,512]{2,1,0:T(8,128)(2,1)} %get-tuple-element.65), channel_id=1, source_target_pairs={{0,12},{4,8},{8,4},{12,0},{1,13},{5,9},{9,5},{13,1},{2,14},{6,10},... | collective-permute-start | bytes 786440 | tf_op jit(solution)/shard_map/ppermute | solution.py:20
  31.6 11.4 %collective-permute-start.4 = (bf16[2,256,512]{2,1,0:T(8,128)(2,1)S(1)}, bf16[2,256,512]{2,1,0:T(8,128)(2,1)S(1)}, u32[]{:S(2)}, u32[]{:S(2)}) collective-permute-start(bf16[2,256,512]{2,1,0:T(8,128)(2,1)S(1)} %bitcast.12), channel_id=1, source_target_pairs={{0,2},{2,0},{1,3},{3,1},{4,6},{6,4},{5,7},{7,5},{8,10},{10,8},{9,1... | collective-permute-start | bytes 1572872 | tf_op jit(solution)/shard_map/ppermute | solution.py:20
  33.9 9.2 %collective-permute-start.3 = (bf16[2,256,512]{2,1,0:T(8,128)(2,1)S(1)}, bf16[2,256,512]{2,1,0:T(8,128)(2,1)S(1)}, u32[]{:S(2)}, u32[]{:S(2)}) collective-permute-start(bf16[2,256,512]{2,1,0:T(8,128)(2,1)S(1)} %bitcast.13), channel_id=1, source_target_pairs={{0,1},{1,0},{2,3},{3,2},{4,5},{5,4},{6,7},{7,6},{8,9},{9,8},{10,11... | collective-permute-start | bytes 1572872 | tf_op jit(solution)/shard_map/ppermute | solution.py:20
  51.1 20.4 %collective-permute-start.8 = (bf16[128,2048]{1,0:T(8,128)(2,1)S(1)}, bf16[128,2048]{1,0:T(8,128)(2,1)S(1)}, u32[]{:S(2)}, u32[]{:S(2)}) collective-permute-start(bf16[128,2048]{1,0:T(8,128)(2,1)S(1)} %shard_map.103.refs_0_), channel_id=1, source_target_pairs={{0,12},{4,8},{8,4},{12,0},{1,13},{5,9},{9,5},{13,1},{2,14},{6,10},... | collective-permute-start | bytes 1572872 | tf_op jit(solution)/shard_map/ppermute | solution.py:20
  53.6 25.5 %collective-permute-start.9 = (bf16[128,2048]{1,0:T(8,128)(2,1)S(1)}, bf16[128,2048]{1,0:T(8,128)(2,1)S(1)}, u32[]{:S(2)}, u32[]{:S(2)}) collective-permute-start(bf16[128,2048]{1,0:T(8,128)(2,1)S(1)} %shard_map.103.refs_0_), channel_id=1, source_target_pairs={{0,4},{4,0},{8,12},{12,8},{1,5},{5,1},{9,13},{13,9},{2,6},{6,2},{1... | collective-permute-start | bytes 1572872 | tf_op jit(solution)/shard_map/ppermute | solution.py:20
  65.1 25.2 %collective-permute-start.6 = (bf16[128,2048]{1,0:T(8,128)(2,1)S(1)}, bf16[128,2048]{1,0:T(8,128)(2,1)S(1)}, u32[]{:S(2)}, u32[]{:S(2)}) collective-permute-start(bf16[128,2048]{1,0:T(8,128)(2,1)S(1)} %shard_map.102.refs_1_), channel_id=1, source_target_pairs={{0,12},{4,8},{8,4},{12,0},{1,13},{5,9},{9,5},{13,1},{2,14},{6,10},... | collective-permute-start | bytes 1572872 | tf_op jit(solution)/shard_map/ppermute | solution.py:20
  66.2 34.5 %collective-permute-start.7 = (bf16[128,2048]{1,0:T(8,128)(2,1)S(1)}, bf16[128,2048]{1,0:T(8,128)(2,1)}, u32[]{:S(2)}, u32[]{:S(2)}) collective-permute-start(bf16[128,2048]{1,0:T(8,128)(2,1)S(1)} %shard_map.102.refs_1_), channel_id=1, source_target_pairs={{0,4},{4,0},{8,12},{12,8},{1,5},{5,1},{9,13},{13,9},{2,6},{6,2},{1... | collective-permute-start | bytes 1572872 | tf_op jit(solution)/shard_map/ppermute | solution.py:20
  82.7 18.0 %collective-permute-start.10 = (bf16[64,2048]{1,0:T(8,128)(2,1)S(1)}, bf16[64,2048]{1,0:T(8,128)(2,1)}, u32[]{:S(2)}, u32[]{:S(2)}) collective-permute-start(bf16[64,2048]{1,0:T(8,128)(2,1)S(1)} %get-tuple-element.75), channel_id=1, source_target_pairs={{0,1},{1,0},{2,3},{3,2},{4,5},{5,4},{6,7},{7,6},{8,9},{9,8},{10,11... | collective-permute-start | bytes 786440 | tf_op jit(solution)/shard_map/ppermute | solution.py:20
  82.8 17.9 %collective-permute-start.11 = (bf16[64,2048]{1,0:T(8,128)(2,1)S(1)}, bf16[64,2048]{1,0:T(8,128)(2,1)}, u32[]{:S(2)}, u32[]{:S(2)}) collective-permute-start(bf16[64,2048]{1,0:T(8,128)(2,1)S(1)} %get-tuple-element.76), channel_id=1, source_target_pairs={{0,2},{1,3},{2,0},{3,1},{4,6},{5,7},{6,4},{7,5},{8,10},{9,11},{10,... | collective-permute-start | bytes 786440 | tf_op jit(solution)/shard_map/ppermute | solution.py:20
  83.8 17.0 %collective-permute-start.12 = (bf16[64,2048]{1,0:T(8,128)(2,1)S(1)}, bf16[64,2048]{1,0:T(8,128)(2,1)}, u32[]{:S(2)}, u32[]{:S(2)}) collective-permute-start(bf16[64,2048]{1,0:T(8,128)(2,1)S(1)} %get-tuple-element.77), channel_id=1, source_target_pairs={{0,3},{1,2},{2,1},{3,0},{4,7},{5,6},{6,5},{7,4},{8,11},{9,10},{10,... | collective-permute-start | bytes 786440 | tf_op jit(solution)/shard_map/ppermute | solution.py:20
  100.8 11.5 %collective-permute-start.19 = (bf16[128,2048]{1,0:T(8,128)(2,1)}, bf16[128,2048]{1,0:T(8,128)(2,1)S(1)}, u32[]{:S(2)}, u32[]{:S(2)}) collective-permute-start(bf16[128,2048]{1,0:T(8,128)(2,1)} %get-tuple-element.94), channel_id=1, source_target_pairs={{0,1},{1,0},{2,3},{3,2},{4,5},{5,4},{6,7},{7,6},{8,9},{9,8},{10,11... | collective-permute-start | bytes 1572872 | tf_op jit(solution)/shard_map/ppermute | solution.py:20
  100.9 14.8 %collective-permute-start.14 = (bf16[128,2048]{1,0:T(8,128)(2,1)S(1)}, bf16[128,2048]{1,0:T(8,128)(2,1)S(1)}, u32[]{:S(2)}, u32[]{:S(2)}) collective-permute-start(bf16[128,2048]{1,0:T(8,128)(2,1)S(1)} %broadcast_select_fusion), channel_id=1, source_target_pairs={{0,8},{12,4},{4,0},{8,12},{1,9},{13,5},{5,1},{9,13},{2,10},{14,6},... | collective-permute-start | bytes 1572872 | tf_op jit(solution)/shard_map/ppermute | solution.py:27
  110.7 15.9 %collective-permute-start.13 = (bf16[128,2048]{1,0:T(8,128)(2,1)S(1)}, bf16[128,2048]{1,0:T(8,128)(2,1)S(1)}, u32[]{:S(2)}, u32[]{:S(2)}) collective-permute-start(bf16[128,2048]{1,0:T(8,128)(2,1)S(1)} %broadcast_select_fusion.1), channel_id=1, source_target_pairs={{0,8},{12,4},{4,0},{8,12},{1,9},{13,5},{5,1},{9,13},{2,10},{14,6},... | collective-permute-start | bytes 1572872 | tf_op jit(solution)/shard_map/ppermute | solution.py:27
  113.4 13.1 %collective-permute-start.20 = (bf16[64,2048]{1,0:T(8,128)(2,1)S(1)}, bf16[64,2048]{1,0:T(8,128)(2,1)S(1)}, u32[]{:S(2)}, u32[]{:S(2)}) collective-permute-start(bf16[64,2048]{1,0:T(8,128)(2,1)S(1)} %add_convert_fusion.2), channel_id=1, source_target_pairs={{0,2},{2,0},{1,3},{3,1},{4,6},{6,4},{5,7},{7,5},{8,10},{10,8},{9,1... | collective-permute-start | bytes 786440 | tf_op jit(solution)/shard_map/ppermute | solution.py:20
  118.5 9.2 %collective-permute-start.16 = (bf16[64,2048]{1,0:T(8,128)(2,1)S(1)}, bf16[64,2048]{1,0:T(8,128)(2,1)S(1)}, u32[]{:S(2)}, u32[]{:S(2)}) collective-permute-start(bf16[64,2048]{1,0:T(8,128)(2,1)S(1)} %add_convert_fusion.3), channel_id=1, source_target_pairs={{0,2},{2,0},{1,3},{3,1},{4,6},{6,4},{5,7},{7,5},{8,10},{10,8},{9,1... | collective-permute-start | bytes 786440 | tf_op jit(solution)/shard_map/ppermute | solution.py:20
  120.0 10.1 %collective-permute-start.18 = (bf16[32,2048]{1,0:T(8,128)(2,1)S(1)}, bf16[32,2048]{1,0:T(8,128)(2,1)S(1)}, u32[]{:S(2)}, u32[]{:S(2)}) collective-permute-start(bf16[32,2048]{1,0:T(8,128)(2,1)S(1)} %add_convert_fusion.7), channel_id=1, source_target_pairs={{0,2},{2,0},{1,3},{3,1},{4,6},{6,4},{5,7},{7,5},{8,10},{10,8},{9,1... | collective-permute-start | bytes 393224 | tf_op jit(solution)/shard_map/ppermute | solution.py:20
  130.2 15.7 %collective-permute-start.23 = (bf16[32,2048]{1,0:T(8,128)(2,1)S(1)}, bf16[32,2048]{1,0:T(8,128)(2,1)S(1)}, u32[]{:S(2)}, u32[]{:S(2)}) collective-permute-start(bf16[32,2048]{1,0:T(8,128)(2,1)S(1)} %add_convert_fusion.6), channel_id=1, source_target_pairs={{0,8},{4,12},{8,0},{12,4},{1,9},{5,13},{9,1},{13,5},{2,10},{6,14},... | collective-permute-start | bytes 393224 | tf_op jit(solution)/shard_map/ppermute | solution.py:20
  132.8 18.0 %collective-permute-start.22 = (bf16[64,2048]{1,0:T(8,128)(2,1)S(1)}, bf16[64,2048]{1,0:T(8,128)(2,1)S(1)}, u32[]{:S(2)}, u32[]{:S(2)}) collective-permute-start(bf16[64,2048]{1,0:T(8,128)(2,1)S(1)} %pad_maximum_fusion.1), channel_id=1, source_target_pairs={{0,12},{4,8},{8,4},{12,0},{1,13},{5,9},{9,5},{13,1},{2,14},{6,10},... | collective-permute-start | bytes 786440 | tf_op jit(solution)/shard_map/ppermute | solution.py:20
  134.5 16.3 %collective-permute-start.21 = (bf16[64,2048]{1,0:T(8,128)(2,1)S(1)}, bf16[64,2048]{1,0:T(8,128)(2,1)S(1)}, u32[]{:S(2)}, u32[]{:S(2)}) collective-permute-start(bf16[64,2048]{1,0:T(8,128)(2,1)S(1)} %pad_maximum_fusion), channel_id=1, source_target_pairs={{0,4},{4,0},{8,12},{12,8},{1,5},{5,1},{9,13},{13,9},{2,6},{6,2},{1... | collective-permute-start | bytes 786440 | tf_op jit(solution)/shard_map/ppermute | solution.py:20
  137.3 8.8 %collective-permute-start.24 = (bf16[32,2048]{1,0:T(8,128)(2,1)S(1)}, bf16[32,2048]{1,0:T(8,128)(2,1)S(1)}, u32[]{:S(2)}, u32[]{:S(2)}) collective-permute-start(bf16[32,2048]{1,0:T(8,128)(2,1)S(1)} %get-tuple-element.107), channel_id=1, source_target_pairs={{0,1},{1,0},{2,3},{3,2},{4,5},{5,4},{6,7},{7,6},{8,9},{9,8},{10,11... | collective-permute-start | bytes 393224 | tf_op jit(solution)/shard_map/ppermute | solution.py:20
  137.4 8.7 %collective-permute-start.25 = (bf16[32,2048]{1,0:T(8,128)(2,1)S(1)}, bf16[32,2048]{1,0:T(8,128)(2,1)S(1)}, u32[]{:S(2)}, u32[]{:S(2)}) collective-permute-start(bf16[32,2048]{1,0:T(8,128)(2,1)S(1)} %get-tuple-element.108), channel_id=1, source_target_pairs={{0,2},{1,3},{2,0},{3,1},{4,6},{5,7},{6,4},{7,5},{8,10},{9,11},{10,... | collective-permute-start | bytes 393224 | tf_op jit(solution)/shard_map/ppermute | solution.py:20
  150.9 7.7 %collective-permute-start.27 = (bf16[32,2048]{1,0:T(8,128)(2,1)S(1)}, bf16[32,2048]{1,0:T(8,128)(2,1)S(1)}, u32[]{:S(2)}, u32[]{:S(2)}) collective-permute-start(bf16[32,2048]{1,0:T(8,128)(2,1)S(1)} %add_convert_fusion.5), channel_id=1, source_target_pairs={{0,8},{4,12},{8,0},{12,4},{1,9},{5,13},{9,1},{13,5},{2,10},{6,14},... | collective-permute-start | bytes 393224 | tf_op jit(solution)/shard_map/ppermute | solution.py:20
  (12 other events, 150.9 us)

commit v15 on v14

--- a/solution.py
+++ b/solution.py
@@ -339,25 +339,24 @@
     near0 = send_direct(project_out([beside0, across0], out_weight, direct=True))
     across1, beside1, near0, own = tie((across1, beside1, near0, own))
     second1 = second_hop(last, across1)
+    many, few = chunk_rows
+    near0 = add_direct(near0)
+    back0 = swap(near0[:many], "pool", 1), swap(near0[many:], "pool", 3)
     near1 = send_sub(project_out([beside1, across1], out_weight))
     second0, near1 = tie((second0, near1))
     near1 = send_heads(near1)
     far0 = send_heads(send_sub(project_out([second0], out_weight)))
-    near0 = add_direct(near0)
-    own = send_heads(send_sub(own))
-    second1, near0, near1, far0, own = tie((second1, near0, near1, far0, own))
-    many, few = chunk_rows
+    far1 = project_out([second1], out_weight)
+    back0, near1, far0, far1, own = tie((back0, near1, far0, far1, own))
     near1 = add_shares(near1)
-    back_beside = swap(jnp.concatenate([near0[:many], near1[:few]]), "pool", 1)
-    back_across = swap(jnp.concatenate([near0[many:], near1[few:]]), "pool", 3)
+    back1 = swap(near1[:few], "pool", 1), swap(near1[few:], "pool", 3)
     back_second0 = swap(add_shares(far0), "pool", 2)
-    far1 = send_direct(project_out([second1], out_weight, direct=True))
-    back_beside, back_across, back_second0, far1 = tie(
-        (back_beside, back_across, back_second0, far1)
-    )
-    back_second1 = swap(add_direct(far1), "pool", 2)
-    backs = [(0, 0, add_shares(own)), (0, 1, back_beside), (0, 3, back_across)]
-    backs += [(0, 2, back_second0), (many, 2, back_second1)]
+    far1 = send_heads(send_sub(far1))
+    back1, back_second0, far1 = tie((back1, back_second0, far1))
+    back_second1 = swap(add_shares(far1), "pool", 2)
+    own = add_shares(send_heads(send_sub(own)))
+    backs = [(0, 1, back0[0]), (0, 3, back0[1]), (many, 1, back1[0]), (many, 3, back1[1])]
+    backs += [(0, 2, back_second0), (0, 0, own), (many, 2, back_second1)]
     output = jnp.zeros((part_rows, pool_size * columns), jnp.bfloat16)
     for row, flip, block in backs:
         output = lax.dynamic_update_slice(output, block, (row, (pool_index ^ flip) * columns))

time: 160 us -> 159 us (level)
  waiting for transfers between devices: 78.4 us -> 52.2 us
  starting transfers between devices: 30.7 us -> 45.4 us
  local copies, waits for them, and re-layouts: 9.93 us -> 22.7 us
  Pallas kernels: 34.6 us -> 33 us
    ppermute x26 -> x27, waiting for transfers between devices: 72 us -> 45.4 us  [swap(): lax.ppermute(values, axis, [(i, i ^ flip) for i in range(lax.axis_size(ax...]
    unnamed x16 -> x38, local copies, waits for them, and re-layouts: 5.99 us -> 16.2 us
    ppermute x2, starting transfers between devices: 3.18 us -> 11.8 us  [second_hop(): return lax.ppermute(passed, 'pool', [(0, 2), (3, 1), (1, 0), (2, 3)])]
    ppermute x26 -> x27, starting transfers between devices: 27.6 us -> 33.6 us  [swap(): lax.ppermute(values, axis, [(i, i ^ flip) for i in range(lax.axis_size(ax...]
    dynamic_update_slice x4 -> x6, local copies, waits for them, and re-layouts: 0.73 us -> 2.54 us  [per_device(): lax.dynamic_update_slice(output, block, (row, (pool_index ^ flip) * colum...]
    pallas_call x5, Pallas kernels: 17.7 us -> 15.9 us  [project_out(): pl.pallas_call(functools.partial(project_kernel, len(blocks), list(range(...]
  transfers between devices with their start and end apart: 28 -> 29, of which waited for: 15 -> 14; matrix products, arithmetic and copies ran while one was open for 5% -> 6% of each run, Pallas kernels for 15% -> 14%
where the time goes in v15:
time: 159 us
  waiting for transfers between devices  52.2 us (33%)
  starting transfers between devices  45.4 us (29%)
  Pallas kernels  33 us (21%)
  local copies, waits for them, and re-layouts  22.7 us (14%)
  other arithmetic  5.16 us (3%)
    ppermute x27, waiting for transfers between devices, swap(): lax.ppermute(values, axis, [(i, i ^ flip) for i in range(lax.axis_size(ax...  45.4 us
    ppermute x27, starting transfers between devices, swap(): lax.ppermute(values, axis, [(i, i ^ flip) for i in range(lax.axis_size(ax...  33.6 us
    unnamed x38, local copies, waits for them, and re-layouts  16.2 us
    pallas_call x5, Pallas kernels, project_out(): pl.pallas_call(functools.partial(project_kernel, len(blocks), list(range(...  15.9 us
    pallas_call x2, Pallas kernels, attend(): pl.pallas_call(functools.partial(attend_kernel, len(parts)), grid=(reques...  12.4 us
    ppermute x2, starting transfers between devices, second_hop(): return lax.ppermute(passed, 'pool', [(0, 2), (3, 1), (1, 0), (2, 3)])  11.8 us
    ppermute x2, waiting for transfers between devices, second_hop(): return lax.ppermute(passed, 'pool', [(0, 2), (3, 1), (1, 0), (2, 3)])  6.79 us
    pallas_call x1, Pallas kernels, fetch(): pl.pallas_call(functools.partial(fetch_kernel, pool_size=pool_size, share...  3.7 us
  transfers between devices with their start and end apart: 29, of which 14 were waited for; matrix products, arithmetic and copies ran while one was open for 6% of the time, Pallas kernels for 14%

profile of v15, /device:TPU:0, one launch (start us, length us, event | category | flops | bytes accessed | tf_op | source)
XLA Modules:
  0.0 158.8 jit_solution(15703009553914306871)
XLA Ops:
  0.7 3.7 %shard_map.100 = (s32[2,16]{1,0:T(2,128)}, bf16[8,32,512]{2,1,0:T(8,128)(2,1)}, bf16[8,32,512]{2,1,0:T(8,128)(2,1)}, bf16[8,32,512]{2,1,0:T(8,128)(2,1)}, bf16[8,32,512]{2,1,0:T(8,128)(2,1)}) custom-call(s32[2]{0:T(128)} %pad_add_fusion.place, s32[8,8]{1,0:T(8,128)} %holder.1, s32[8,8]{1,0:T(8,128)} %block.1, s32[8]{0:T(128)} %serving.1, ...), custom_call_target="tpu_custom_call" | custom-call | flops 1 | bytes 1 | tf_op jit(solution)/shard_map/pallas_call | solution.py:153
  4.4 2.7 %collective-permute-start = (bf16[8,32,512]{2,1,0:T(8,128)(2,1)}, bf16[8,32,512]{2,1,0:T(8,128)(2,1)S(1)}, u32[]{:S(2)}, u32[]{:S(2)}) collective-permute-start(bf16[8,32,512]{2,1,0:T(8,128)(2,1)} %get-tuple-element.61), channel_id=1, source_target_pairs={{0,4},{4,0},{8,12},{12,8},{1,5},{5,1},{9,13},{13,9},{2,6},{6,2},{1... | collective-permute-start | bytes 786440 | tf_op jit(solution)/shard_map/ppermute | solution.py:20
  7.1 3.0 %collective-permute-start.1 = (bf16[8,32,512]{2,1,0:T(8,128)(2,1)}, bf16[8,32,512]{2,1,0:T(8,128)(2,1)S(1)}, u32[]{:S(2)}, u32[]{:S(2)}) collective-permute-start(bf16[8,32,512]{2,1,0:T(8,128)(2,1)} %get-tuple-element.62), channel_id=1, source_target_pairs={{0,8},{4,12},{8,0},{12,4},{1,9},{5,13},{9,1},{13,5},{2,10},{6,14},... | collective-permute-start | bytes 786440 | tf_op jit(solution)/shard_map/ppermute | solution.py:20
  14.8 3.8 %collective-permute-done.refs_1_ = bf16[8,32,512]{2,1,0:T(8,128)(2,1)S(1)} collective-permute-done((bf16[8,32,512]{2,1,0:T(8,128)(2,1)}, bf16[8,32,512]{2,1,0:T(8,128)(2,1)S(1)}, u32[]{:S(2)}, u32[]{:S(2)}) %collective-permute-start) | collective-permute-done | bytes 262176 | tf_op jit(solution)/shard_map/ppermute | solution.py:20
  18.6 10.1 %collective-permute-done.1.refs_2_ = bf16[8,32,512]{2,1,0:T(8,128)(2,1)S(1)} collective-permute-done((bf16[8,32,512]{2,1,0:T(8,128)(2,1)}, bf16[8,32,512]{2,1,0:T(8,128)(2,1)S(1)}, u32[]{:S(2)}, u32[]{:S(2)}) %collective-permute-start.1) | collective-permute-done | bytes 262176 | tf_op jit(solution)/shard_map/ppermute | solution.py:20
  33.7 9.2 %collective-permute-done.4.refs_2_ = bf16[2,256,512]{2,1,0:T(8,128)(2,1)S(1)} collective-permute-done((bf16[2,256,512]{2,1,0:T(8,128)(2,1)S(1)}, bf16[2,256,512]{2,1,0:T(8,128)(2,1)S(1)}, u32[]{:S(2)}, u32[]{:S(2)}) %collective-permute-start.4) | collective-permute-done | bytes 524320 | tf_op jit(solution)/shard_map/ppermute | solution.py:20
  44.8 6.2 %shard_map.103.refs_0_ = bf16[128,2048]{1,0:T(8,128)(2,1)S(1)} custom-call(s32[3]{0:T(128)S(1)} %pad_add_fusion.1.scalars, bf16[2,2,64,2048]{3,2,1,0:T(8,128)(2,1)S(1)} %bitcast.18, bf16[2,256,512]{2,1,0:T(8,128)(2,1)S(1)} %bitcast.16, bf16[2,256,512]{2,1,0:T(8,128)(2,1)S(1)} %collective-permute-done.3.refs_1_, ...), custom_call_target="tpu_custom_call" | custom-call | flops 1 | bytes 1 | tf_op jit(solution)/shard_map/pallas_call | solution.py:241
  53.5 5.3 %collective-permute-start.9 = (bf16[128,2048]{1,0:T(8,128)(2,1)S(1)}, bf16[128,2048]{1,0:T(8,128)(2,1)S(1)}, u32[]{:S(2)}, u32[]{:S(2)}) collective-permute-start(bf16[128,2048]{1,0:T(8,128)(2,1)S(1)} %shard_map.103.refs_0_), channel_id=1, source_target_pairs={{0,4},{4,0},{8,12},{12,8},{1,5},{5,1},{9,13},{13,9},{2,6},{6,2},{1... | collective-permute-start | bytes 1572872 | tf_op jit(solution)/shard_map/ppermute | solution.py:20
  58.7 6.2 %shard_map.102.refs_1_ = bf16[128,2048]{1,0:T(8,128)(2,1)S(1)} custom-call(s32[3]{0:T(128)S(1)} %pad_add_fusion.1.scalars, bf16[2,2,64,2048]{3,2,1,0:T(8,128)(2,1)S(1)} %bitcast.19, bf16[2,256,512]{2,1,0:T(8,128)(2,1)S(1)} %bitcast.17, bf16[2,256,512]{2,1,0:T(8,128)(2,1)S(1)} %collective-permute-done.3.refs_1_, ...), custom_call_target="tpu_custom_call" | custom-call | flops 1 | bytes 1 | tf_op jit(solution)/shard_map/pallas_call | solution.py:241
  66.7 3.4 %copy-done = bf16[2048,2048]{1,0:T(8,128)(2,1)S(1)} copy-done((bf16[2048,2048]{1,0:T(8,128)(2,1)S(1)}, bf16[2048,2048]{1,0:T(8,128)(2,1)}, u32[]{:S(2)}) %copy-start) | copy-done | bytes 8388632
  70.1 3.6 %shard_map.104 = (f32[128,2048]{1,0:T(8,128)S(1)}, bf16[128,2048]{1,0:T(8,128)(2,1)S(1)}) custom-call(s32[1]{0:T(128)} %bitcast.1.share, bf16[128,2048]{1,0:T(8,128)(2,1)S(1)} %shard_map.103.refs_0_, bf16[128,2048]{1,0:T(8,128)(2,1)S(1)} %shard_map.102.refs_1_, bf16[2048,2048]{1,0:T(8,128)(2,1)S(1)} %copy-done), custom_call_target="tpu_custom_call" | custom-call | flops 1 | bytes 1 | tf_op jit(solution)/shard_map/pallas_call | solution.py:56
  75.4 3.5 %collective-permute-done.9.refs_0_ = bf16[128,2048]{1,0:T(8,128)(2,1)S(1)} collective-permute-done((bf16[128,2048]{1,0:T(8,128)(2,1)S(1)}, bf16[128,2048]{1,0:T(8,128)(2,1)S(1)}, u32[]{:S(2)}, u32[]{:S(2)}) %collective-permute-start.9) | collective-permute-done | bytes 524320 | tf_op jit(solution)/shard_map/ppermute | solution.py:20
  79.0 3.4 %copy-done.1 = bf16[2048,2048]{1,0:T(8,128)(2,1)S(1)} copy-done((bf16[2048,2048]{1,0:T(8,128)(2,1)S(1)}, bf16[2048,2048]{1,0:T(8,128)(2,1)}, u32[]{:S(2)}) %copy-start.1) | copy-done | bytes 8388632
  82.4 3.6 %shard_map.105 = (f32[64,2048]{1,0:T(8,128)S(1)}, bf16[64,2048]{1,0:T(8,128)(2,1)S(1)}, bf16[64,2048]{1,0:T(8,128)(2,1)S(1)}, bf16[64,2048]{1,0:T(8,128)(2,1)S(1)}) custom-call(s32[1]{0:T(128)} %bitcast.1.share, bf16[128,2048]{1,0:T(8,128)(2,1)S(1)} %collective-permute-done.9.refs_0_, bf16[128,2048]{1,0:T(8,128)(2,1)S(1)} %collective-permute-done.8.refs_1_, ...), custom_call_target="tpu_custom_call" | custom-call | flops 1 | bytes 1 | tf_op jit(solution)/shard_map/pallas_call | solution.py:56
  90.2 11.8 %collective-permute-start.15 = (bf16[128,2048]{1,0:T(8,128)(2,1)S(1)}, bf16[128,2048]{1,0:T(8,128)(2,1)S(1)}, u32[]{:S(2)}, u32[]{:S(2)}) collective-permute-start(bf16[128,2048]{1,0:T(8,128)(2,1)S(1)} %broadcast_select_fusion.1), channel_id=1, source_target_pairs={{0,8},{12,4},{4,0},{8,12},{1,9},{13,5},{5,1},{9,13},{2,10},{14,6},... | collective-permute-start | bytes 1572872 | tf_op jit(solution)/shard_map/ppermute | solution.py:27
  104.1 3.6 %shard_map.106 = (f32[128,2048]{1,0:T(8,128)S(1)}, bf16[128,2048]{1,0:T(8,128)(2,1)S(1)}) custom-call(s32[1]{0:T(128)} %bitcast.1.share, bf16[128,2048]{1,0:T(8,128)(2,1)S(1)} %copy-done.7, bf16[128,2048]{1,0:T(8,128)(2,1)S(1)} %collective-permute-done.6.refs_1_, bf16[2048,2048]{1,0:T(8,128)(2,1)S(1)} %bitcast.11), custom_call_target="tpu_custom_call" | custom-call | flops 1 | bytes 1 | tf_op jit(solution)/shard_map/pallas_call | solution.py:56
  114.4 2.5 %shard_map.107 = (f32[64,2048]{1,0:T(8,128)S(1)}, bf16[64,2048]{1,0:T(8,128)(2,1)S(1)}) custom-call(s32[1]{0:T(128)} %bitcast.1.share, bf16[128,2048]{1,0:T(8,128)(2,1)S(1)} %collective-permute-done.15.refs_0_, bf16[2048,2048]{1,0:T(8,128)(2,1)S(1)} %bitcast.11), custom_call_target="tpu_custom_call" | custom-call | flops 1 | bytes 1 | tf_op jit(solution)/shard_map/pallas_call | solution.py:56
  121.2 4.5 %collective-permute-done.20.refs_0_ = bf16[128,2048]{1,0:T(8,128)(2,1)S(1)} collective-permute-done((bf16[128,2048]{1,0:T(8,128)(2,1)}, bf16[128,2048]{1,0:T(8,128)(2,1)S(1)}, u32[]{:S(2)}, u32[]{:S(2)}) %collective-permute-start.20) | collective-permute-done | bytes 524320 | tf_op jit(solution)/shard_map/ppermute | solution.py:27
  125.7 3.4 %copy-done.2 = bf16[2048,2048]{1,0:T(8,128)(2,1)S(1)} copy-done((bf16[2048,2048]{1,0:T(8,128)(2,1)S(1)}, bf16[2048,2048]{1,0:T(8,128)(2,1)}, u32[]{:S(2)}) %copy-start.2) | copy-done | bytes 8388632
  129.1 2.5 %shard_map.108 = (f32[64,2048]{1,0:T(8,128)S(1)}, bf16[64,2048]{1,0:T(8,128)(2,1)S(1)}) custom-call(s32[1]{0:T(128)} %bitcast.1.share, bf16[128,2048]{1,0:T(8,128)(2,1)S(1)} %collective-permute-done.20.refs_0_, bf16[2048,2048]{1,0:T(8,128)(2,1)S(1)} %copy-done.2), custom_call_target="tpu_custom_call" | custom-call | flops 1 | bytes 1 | tf_op jit(solution)/shard_map/pallas_call | solution.py:56
  132.4 2.8 %collective-permute-start.23 = (bf16[32,2048]{1,0:T(8,128)(2,1)S(1)}, bf16[32,2048]{1,0:T(8,128)(2,1)S(1)}, u32[]{:S(2)}, u32[]{:S(2)}) collective-permute-start(bf16[32,2048]{1,0:T(8,128)(2,1)S(1)} %add_convert_fusion.7), channel_id=1, source_target_pairs={{0,8},{4,12},{8,0},{12,4},{1,9},{5,13},{9,1},{13,5},{2,10},{6,14},... | collective-permute-start | bytes 393224 | tf_op jit(solution)/shard_map/ppermute | solution.py:20
  142.5 3.7 %collective-permute-done.22 = bf16[32,2048]{1,0:T(8,128)(2,1)S(1)} collective-permute-done((bf16[32,2048]{1,0:T(8,128)(2,1)S(1)}, bf16[32,2048]{1,0:T(8,128)(2,1)S(1)}, u32[]{:S(2)}, u32[]{:S(2)}) %collective-permute-start.22) | collective-permute-done | bytes 131104 | tf_op jit(solution)/shard_map/ppermute | solution.py:20
  146.3 3.0 %collective-permute-start.28 = (bf16[32,2048]{1,0:T(8,128)(2,1)S(1)}, bf16[32,2048]{1,0:T(8,128)(2,1)S(1)}, u32[]{:S(2)}, u32[]{:S(2)}) collective-permute-start(bf16[32,2048]{1,0:T(8,128)(2,1)S(1)} %add_convert_fusion.5), channel_id=1, source_target_pairs={{0,8},{4,12},{8,0},{12,4},{1,9},{5,13},{9,1},{13,5},{2,10},{6,14},... | collective-permute-start | bytes 393224 | tf_op jit(solution)/shard_map/ppermute | solution.py:20
  149.8 7.3 %collective-permute-done.27 = bf16[64,2048]{1,0:T(8,128)(2,1)S(1)} collective-permute-done((bf16[64,2048]{1,0:T(8,128)(2,1)S(1)}, bf16[64,2048]{1,0:T(8,128)(2,1)S(1)}, u32[]{:S(2)}, u32[]{:S(2)}) %collective-permute-start.27) | collective-permute-done | bytes 262176 | tf_op jit(solution)/shard_map/ppermute | solution.py:20
  (109 shorter events, 45.5 us)
Async XLA Ops:
  4.4 14.3 %collective-permute-start = (bf16[8,32,512]{2,1,0:T(8,128)(2,1)}, bf16[8,32,512]{2,1,0:T(8,128)(2,1)S(1)}, u32[]{:S(2)}, u32[]{:S(2)}) collective-permute-start(bf16[8,32,512]{2,1,0:T(8,128)(2,1)} %get-tuple-element.61), channel_id=1, source_target_pairs={{0,4},{4,0},{8,12},{12,8},{1,5},{5,1},{9,13},{13,9},{2,6},{6,2},{1... | collective-permute-start | bytes 786440 | tf_op jit(solution)/shard_map/ppermute | solution.py:20
  7.1 21.6 %collective-permute-start.1 = (bf16[8,32,512]{2,1,0:T(8,128)(2,1)}, bf16[8,32,512]{2,1,0:T(8,128)(2,1)S(1)}, u32[]{:S(2)}, u32[]{:S(2)}) collective-permute-start(bf16[8,32,512]{2,1,0:T(8,128)(2,1)} %get-tuple-element.62), channel_id=1, source_target_pairs={{0,8},{4,12},{8,0},{12,4},{1,9},{5,13},{9,1},{13,5},{2,10},{6,14},... | collective-permute-start | bytes 786440 | tf_op jit(solution)/shard_map/ppermute | solution.py:20
  10.1 18.6 %collective-permute-start.2 = (bf16[8,32,512]{2,1,0:T(8,128)(2,1)}, bf16[8,32,512]{2,1,0:T(8,128)(2,1)S(1)}, u32[]{:S(2)}, u32[]{:S(2)}) collective-permute-start(bf16[8,32,512]{2,1,0:T(8,128)(2,1)} %get-tuple-element.63), channel_id=1, source_target_pairs={{0,12},{4,8},{8,4},{12,0},{1,13},{5,9},{9,5},{13,1},{2,14},{6,10},... | collective-permute-start | bytes 786440 | tf_op jit(solution)/shard_map/ppermute | solution.py:20
  31.3 11.6 %collective-permute-start.4 = (bf16[2,256,512]{2,1,0:T(8,128)(2,1)S(1)}, bf16[2,256,512]{2,1,0:T(8,128)(2,1)S(1)}, u32[]{:S(2)}, u32[]{:S(2)}) collective-permute-start(bf16[2,256,512]{2,1,0:T(8,128)(2,1)S(1)} %bitcast.14), channel_id=1, source_target_pairs={{0,2},{2,0},{1,3},{3,1},{4,6},{6,4},{5,7},{7,5},{8,10},{10,8},{9,1... | collective-permute-start | bytes 1572872 | tf_op jit(solution)/shard_map/ppermute | solution.py:20
  33.7 9.2 %collective-permute-start.3 = (bf16[2,256,512]{2,1,0:T(8,128)(2,1)S(1)}, bf16[2,256,512]{2,1,0:T(8,128)(2,1)S(1)}, u32[]{:S(2)}, u32[]{:S(2)}) collective-permute-start(bf16[2,256,512]{2,1,0:T(8,128)(2,1)S(1)} %bitcast.15), channel_id=1, source_target_pairs={{0,1},{1,0},{2,3},{3,2},{4,5},{5,4},{6,7},{7,6},{8,9},{9,8},{10,11... | collective-permute-start | bytes 1572872 | tf_op jit(solution)/shard_map/ppermute | solution.py:20
  51.0 24.4 %collective-permute-start.8 = (bf16[128,2048]{1,0:T(8,128)(2,1)S(1)}, bf16[128,2048]{1,0:T(8,128)(2,1)S(1)}, u32[]{:S(2)}, u32[]{:S(2)}) collective-permute-start(bf16[128,2048]{1,0:T(8,128)(2,1)S(1)} %shard_map.103.refs_0_), channel_id=1, source_target_pairs={{0,12},{4,8},{8,4},{12,0},{1,13},{5,9},{9,5},{13,1},{2,14},{6,10},... | collective-permute-start | bytes 1572872 | tf_op jit(solution)/shard_map/ppermute | solution.py:20
  53.5 25.5 %collective-permute-start.9 = (bf16[128,2048]{1,0:T(8,128)(2,1)S(1)}, bf16[128,2048]{1,0:T(8,128)(2,1)S(1)}, u32[]{:S(2)}, u32[]{:S(2)}) collective-permute-start(bf16[128,2048]{1,0:T(8,128)(2,1)S(1)} %shard_map.103.refs_0_), channel_id=1, source_target_pairs={{0,4},{4,0},{8,12},{12,8},{1,5},{5,1},{9,13},{13,9},{2,6},{6,2},{1... | collective-permute-start | bytes 1572872 | tf_op jit(solution)/shard_map/ppermute | solution.py:20
  65.0 25.3 %collective-permute-start.6 = (bf16[128,2048]{1,0:T(8,128)(2,1)S(1)}, bf16[128,2048]{1,0:T(8,128)(2,1)S(1)}, u32[]{:S(2)}, u32[]{:S(2)}) collective-permute-start(bf16[128,2048]{1,0:T(8,128)(2,1)S(1)} %shard_map.102.refs_1_), channel_id=1, source_target_pairs={{0,12},{4,8},{8,4},{12,0},{1,13},{5,9},{9,5},{13,1},{2,14},{6,10},... | collective-permute-start | bytes 1572872 | tf_op jit(solution)/shard_map/ppermute | solution.py:20
  66.7 35.3 %collective-permute-start.7 = (bf16[128,2048]{1,0:T(8,128)(2,1)S(1)}, bf16[128,2048]{1,0:T(8,128)(2,1)S(1)}, u32[]{:S(2)}, u32[]{:S(2)}) collective-permute-start(bf16[128,2048]{1,0:T(8,128)(2,1)S(1)} %shard_map.102.refs_1_), channel_id=1, source_target_pairs={{0,4},{4,0},{8,12},{12,8},{1,5},{5,1},{9,13},{13,9},{2,6},{6,2},{1... | collective-permute-start | bytes 1572872 | tf_op jit(solution)/shard_map/ppermute | solution.py:20
  86.0 16.1 %collective-permute-start.10 = (bf16[64,2048]{1,0:T(8,128)(2,1)S(1)}, bf16[64,2048]{1,0:T(8,128)(2,1)S(1)}, u32[]{:S(2)}, u32[]{:S(2)}) collective-permute-start(bf16[64,2048]{1,0:T(8,128)(2,1)S(1)} %get-tuple-element.73), channel_id=1, source_target_pairs={{0,1},{1,0},{2,3},{3,2},{4,5},{5,4},{6,7},{7,6},{8,9},{9,8},{10,11... | collective-permute-start | bytes 786440 | tf_op jit(solution)/shard_map/ppermute | solution.py:20
  86.1 16.0 %collective-permute-start.11 = (bf16[64,2048]{1,0:T(8,128)(2,1)S(1)}, bf16[64,2048]{1,0:T(8,128)(2,1)S(1)}, u32[]{:S(2)}, u32[]{:S(2)}) collective-permute-start(bf16[64,2048]{1,0:T(8,128)(2,1)S(1)} %get-tuple-element.74), channel_id=1, source_target_pairs={{0,2},{1,3},{2,0},{3,1},{4,6},{5,7},{6,4},{7,5},{8,10},{9,11},{10,... | collective-permute-start | bytes 786440 | tf_op jit(solution)/shard_map/ppermute | solution.py:20
  87.0 15.0 %collective-permute-start.12 = (bf16[64,2048]{1,0:T(8,128)(2,1)S(1)}, bf16[64,2048]{1,0:T(8,128)(2,1)S(1)}, u32[]{:S(2)}, u32[]{:S(2)}) collective-permute-start(bf16[64,2048]{1,0:T(8,128)(2,1)S(1)} %get-tuple-element.75), channel_id=1, source_target_pairs={{0,3},{1,2},{2,1},{3,0},{4,7},{5,6},{6,5},{7,4},{8,11},{9,10},{10,... | collective-permute-start | bytes 786440 | tf_op jit(solution)/shard_map/ppermute | solution.py:20
  90.2 24.2 %collective-permute-start.15 = (bf16[128,2048]{1,0:T(8,128)(2,1)S(1)}, bf16[128,2048]{1,0:T(8,128)(2,1)S(1)}, u32[]{:S(2)}, u32[]{:S(2)}) collective-permute-start(bf16[128,2048]{1,0:T(8,128)(2,1)S(1)} %broadcast_select_fusion.1), channel_id=1, source_target_pairs={{0,8},{12,4},{4,0},{8,12},{1,9},{13,5},{5,1},{9,13},{2,10},{14,6},... | collective-permute-start | bytes 1572872 | tf_op jit(solution)/shard_map/ppermute | solution.py:27
  103.0 22.7 %collective-permute-start.20 = (bf16[128,2048]{1,0:T(8,128)(2,1)}, bf16[128,2048]{1,0:T(8,128)(2,1)S(1)}, u32[]{:S(2)}, u32[]{:S(2)}) collective-permute-start(bf16[128,2048]{1,0:T(8,128)(2,1)} %broadcast_select_fusion), channel_id=1, source_target_pairs={{0,8},{12,4},{4,0},{8,12},{1,9},{13,5},{5,1},{9,13},{2,10},{14,6},... | collective-permute-start | bytes 1572872 | tf_op jit(solution)/shard_map/ppermute | solution.py:27
  108.6 23.0 %collective-permute-start.13 = (bf16[32,2048]{1,0:T(8,128)(2,1)}, bf16[32,2048]{1,0:T(8,128)(2,1)}, u32[]{:S(2)}, u32[]{:S(2)}) collective-permute-start(bf16[32,2048]{1,0:T(8,128)(2,1)} %get-tuple-element.116), channel_id=1, source_target_pairs={{0,4},{4,0},{8,12},{12,8},{1,5},{5,1},{9,13},{13,9},{2,6},{6,2},{1... | collective-permute-start | bytes 393224 | tf_op jit(solution)/shard_map/ppermute | solution.py:20
  110.6 21.7 %collective-permute-start.14 = (bf16[32,2048]{1,0:T(8,128)(2,1)}, bf16[32,2048]{1,0:T(8,128)(2,1)}, u32[]{:S(2)}, u32[]{:S(2)}) collective-permute-start(bf16[32,2048]{1,0:T(8,128)(2,1)} %get-tuple-element.115), channel_id=1, source_target_pairs={{0,12},{4,8},{8,4},{12,0},{1,13},{5,9},{9,5},{13,1},{2,14},{6,10},... | collective-permute-start | bytes 393224 | tf_op jit(solution)/shard_map/ppermute | solution.py:20
  117.8 14.5 %collective-permute-start.17 = (bf16[64,2048]{1,0:T(8,128)(2,1)}, bf16[64,2048]{1,0:T(8,128)(2,1)S(1)}, u32[]{:S(2)}, u32[]{:S(2)}) collective-permute-start(bf16[64,2048]{1,0:T(8,128)(2,1)} %add_convert_fusion.3), channel_id=1, source_target_pairs={{0,2},{2,0},{1,3},{3,1},{4,6},{6,4},{5,7},{7,5},{8,10},{10,8},{9,1... | collective-permute-start | bytes 786440 | tf_op jit(solution)/shard_map/ppermute | solution.py:20
  119.9 12.4 %collective-permute-start.19 = (bf16[32,2048]{1,0:T(8,128)(2,1)}, bf16[32,2048]{1,0:T(8,128)(2,1)S(1)}, u32[]{:S(2)}, u32[]{:S(2)}) collective-permute-start(bf16[32,2048]{1,0:T(8,128)(2,1)} %add_convert_fusion.8), channel_id=1, source_target_pairs={{0,2},{2,0},{1,3},{3,1},{4,6},{6,4},{5,7},{7,5},{8,10},{10,8},{9,1... | collective-permute-start | bytes 393224 | tf_op jit(solution)/shard_map/ppermute | solution.py:20
  132.4 10.1 %collective-permute-start.23 = (bf16[32,2048]{1,0:T(8,128)(2,1)S(1)}, bf16[32,2048]{1,0:T(8,128)(2,1)S(1)}, u32[]{:S(2)}, u32[]{:S(2)}) collective-permute-start(bf16[32,2048]{1,0:T(8,128)(2,1)S(1)} %add_convert_fusion.7), channel_id=1, source_target_pairs={{0,8},{4,12},{8,0},{12,4},{1,9},{5,13},{9,1},{13,5},{2,10},{6,14},... | collective-permute-start | bytes 393224 | tf_op jit(solution)/shard_map/ppermute | solution.py:20
  135.6 10.7 %collective-permute-start.22 = (bf16[32,2048]{1,0:T(8,128)(2,1)S(1)}, bf16[32,2048]{1,0:T(8,128)(2,1)S(1)}, u32[]{:S(2)}, u32[]{:S(2)}) collective-permute-start(bf16[32,2048]{1,0:T(8,128)(2,1)S(1)} %get-tuple-element.113), channel_id=1, source_target_pairs={{0,12},{4,8},{8,4},{12,0},{1,13},{5,9},{9,5},{13,1},{2,14},{6,10},... | collective-permute-start | bytes 393224 | tf_op jit(solution)/shard_map/ppermute | solution.py:20
  137.1 12.2 %collective-permute-start.26 = (bf16[128,2048]{1,0:T(8,128)(2,1)S(1)}, bf16[128,2048]{1,0:T(8,128)(2,1)S(1)}, u32[]{:S(2)}, u32[]{:S(2)}) collective-permute-start(bf16[128,2048]{1,0:T(8,128)(2,1)S(1)} %copy-done.11), channel_id=1, source_target_pairs={{0,1},{1,0},{2,3},{3,2},{4,5},{5,4},{6,7},{7,6},{8,9},{9,8},{10,11... | collective-permute-start | bytes 1572872 | tf_op jit(solution)/shard_map/ppermute | solution.py:20
  138.1 8.2 %collective-permute-start.25 = (bf16[32,2048]{1,0:T(8,128)(2,1)S(1)}, bf16[32,2048]{1,0:T(8,128)(2,1)S(1)}, u32[]{:S(2)}, u32[]{:S(2)}) collective-permute-start(bf16[32,2048]{1,0:T(8,128)(2,1)S(1)} %add_convert_fusion.6), channel_id=1, source_target_pairs={{0,2},{2,0},{1,3},{3,1},{4,6},{6,4},{5,7},{7,5},{8,10},{10,8},{9,1... | collective-permute-start | bytes 393224 | tf_op jit(solution)/shard_map/ppermute | solution.py:20
  146.3 10.9 %collective-permute-start.28 = (bf16[32,2048]{1,0:T(8,128)(2,1)S(1)}, bf16[32,2048]{1,0:T(8,128)(2,1)S(1)}, u32[]{:S(2)}, u32[]{:S(2)}) collective-permute-start(bf16[32,2048]{1,0:T(8,128)(2,1)S(1)} %add_convert_fusion.5), channel_id=1, source_target_pairs={{0,8},{4,12},{8,0},{12,4},{1,9},{5,13},{9,1},{13,5},{2,10},{6,14},... | collective-permute-start | bytes 393224 | tf_op jit(solution)/shard_map/ppermute | solution.py:20
  149.4 7.7 %collective-permute-start.27 = (bf16[64,2048]{1,0:T(8,128)(2,1)S(1)}, bf16[64,2048]{1,0:T(8,128)(2,1)S(1)}, u32[]{:S(2)}, u32[]{:S(2)}) collective-permute-start(bf16[64,2048]{1,0:T(8,128)(2,1)S(1)} %add_convert_fusion.1), channel_id=1, source_target_pairs={{0,2},{2,0},{1,3},{3,1},{4,6},{6,4},{5,7},{7,5},{8,10},{10,8},{9,1... | collective-permute-start | bytes 786440 | tf_op jit(solution)/shard_map/ppermute | solution.py:20
  (24 other events, 192.6 us)

commit v16 on v15

--- a/solution.py
+++ b/solution.py
@@ -165,11 +165,11 @@
     return where, pieces
 
 
-def choose_kernel(where, *refs):
+def choose_kernel(order, where, *refs):
     pieces, out = refs[:-1], refs[-1]
     for i in range(out.shape[0]):
         flip, slot = where[0, i], where[1, i]
-        for other, piece in enumerate(pieces):
+        for other, piece in zip(order, pieces):
 
             @pl.when(flip == other)
             def _(piece=piece):
@@ -177,15 +177,16 @@
 
 
 def choose(where, pieces):
+    order = [0, *range(2, len(pieces)), 1]
     whole = pl.BlockSpec(memory_space=pltpu.VMEM)
     return pl.pallas_call(
-        choose_kernel,
+        functools.partial(choose_kernel, order),
         in_specs=[pl.BlockSpec(memory_space=pltpu.SMEM)] + [whole] * len(pieces),
         out_specs=whole,
         out_shape=jax.ShapeDtypeStruct((where.shape[1], *pieces[0].shape[1:]), pieces[0].dtype),
         compiler_params=pltpu.CompilerParams(vmem_limit_bytes=8 * 1024 * 1024),
         cost_estimate=LIGHT,
-    )(where, *pieces)
+    )(where, *[pieces[flip] for flip in order])
 
 
 def attend_kernel(share_count, scalars, queries, *refs):
@@ -296,8 +297,13 @@
         jnp.where(served_here[:, None] == request_ids[None, :], image_count[None, :], 0), axis=1
     )
     scalars = jnp.concatenate([share.reshape(1), count_here])
-    arriving = [swap(pieces[flip], "pool", flip) for flip in range(1, pool_size)]
-    chosen = choose(where, pieces[:1] + arriving)
+    for flip in [*range(2, pool_size), 1]:
+        pieces[flip] = swap(pieces[flip], "pool", flip)
+    capacity = pieces[0].shape[0]
+    pieces[0] = jnp.roll(pieces[0], 1, axis=0)
+    local = jnp.where(where[0] == 0, 1, 0)
+    where = jnp.stack([where[0], (where[1] + local) % capacity])
+    chosen = choose(where, pieces)
     chosen, kv_flat, gains, scalars = tie((chosen, kv_flat, gains, scalars))
     chosen = chosen.reshape(requests_here, -1, rank_width)
     over_heads = [chosen] + [swap(chosen, "heads", flip) for flip in range(1, heads_size)]
@@ -352,9 +358,10 @@
     back1 = swap(near1[:few], "pool", 1), swap(near1[few:], "pool", 3)
     back_second0 = swap(add_shares(far0), "pool", 2)
     far1 = send_heads(send_sub(far1))
-    back1, back_second0, far1 = tie((back1, back_second0, far1))
+    own = send_heads(send_sub(own))
+    back1, back_second0, far1, own = tie((back1, back_second0, far1, own))
     back_second1 = swap(add_shares(far1), "pool", 2)
-    own = add_shares(send_heads(send_sub(own)))
+    own = add_shares(own)
     backs = [(0, 1, back0[0]), (0, 3, back0[1]), (many, 1, back1[0]), (many, 3, back1[1])]
     backs += [(0, 2, back_second0), (0, 0, own), (many, 2, back_second1)]
     output = jnp.zeros((part_rows, pool_size * columns), jnp.bfloat16)

time: 159 us -> 157 us (0.987)
  waiting for transfers between devices: 52.2 us -> 48.4 us
    ppermute x27, waiting for transfers between devices: 45.4 us -> 41.1 us  [swap(): lax.ppermute(values, axis, [(i, i ^ flip) for i in range(lax.axis_size(ax...]
    unnamed x38, local copies, waits for them, and re-layouts: 16.2 us -> 13.7 us
    slice x0 -> x2, local copies, waits for them, and re-layouts: none -> 1.72 us  [per_device(): pieces[0] = jnp.roll(pieces[0], 1, axis=0)]
  transfers between devices with their start and end apart: 29 -> 29, of which waited for: 14 -> 12; matrix products, arithmetic and copies ran while one was open for 6% -> 8% of each run, Pallas kernels for 14% -> 14%
where the time goes in v16:
time: 157 us; the launch traced here: 156 us
  waiting for transfers between devices  48.4 us (31%)
  starting transfers between devices  46.8 us (30%)
  Pallas kernels  33 us (21%)
  local copies, waits for them, and re-layouts  21.9 us (14%)
  other arithmetic  5.95 us (4%)
    ppermute x27, waiting for transfers between devices, swap(): lax.ppermute(values, axis, [(i, i ^ flip) for i in range(lax.axis_size(ax...  41.1 us
    ppermute x27, starting transfers between devices, swap(): lax.ppermute(values, axis, [(i, i ^ flip) for i in range(lax.axis_size(ax...  33.7 us
    pallas_call x5, Pallas kernels, project_out(): pl.pallas_call(functools.partial(project_kernel, len(blocks), list(range(...  15.9 us
    unnamed x38, local copies, waits for them, and re-layouts  13.7 us
    ppermute x2, starting transfers between devices, second_hop(): return lax.ppermute(passed, 'pool', [(0, 2), (3, 1), (1, 0), (2, 3)])  13.1 us
    pallas_call x2, Pallas kernels, attend(): pl.pallas_call(functools.partial(attend_kernel, len(parts)), grid=(reques...  12.4 us
    ppermute x2, waiting for transfers between devices, second_hop(): return lax.ppermute(passed, 'pool', [(0, 2), (3, 1), (1, 0), (2, 3)])  7.21 us
    pallas_call x1, Pallas kernels, fetch(): pl.pallas_call(functools.partial(fetch_kernel, pool_size=pool_size, share...  3.75 us
  transfers between devices with their start and end apart: 29, of which 12 were waited for; matrix products, arithmetic and copies ran while one was open for 8% of the time, Pallas kernels for 14%

profile of v16, /device:TPU:0, one launch (start us, length us, event | category | flops | bytes accessed | tf_op | source)
XLA Modules:
  0.0 156.4 jit_solution(11647333045492637288)
XLA Ops:
  0.7 3.7 %shard_map.100 = (s32[2,16]{1,0:T(2,128)}, bf16[8,32,512]{2,1,0:T(8,128)(2,1)}, bf16[8,32,512]{2,1,0:T(8,128)(2,1)}, bf16[8,32,512]{2,1,0:T(8,128)(2,1)}, bf16[8,32,512]{2,1,0:T(8,128)(2,1)}) custom-call(s32[2]{0:T(128)} %pad_add_fusion.1.place, s32[8,8]{1,0:T(8,128)} %holder.1, s32[8,8]{1,0:T(8,128)} %block.1, s32[8]{0:T(128)} %serving.1, ...), custom_call_target="tpu_custom_call" | custom-call | flops 1 | bytes 1 | tf_op jit(solution)/shard_map/pallas_call | solution.py:153
  4.4 4.1 %collective-permute-start = (bf16[8,32,512]{2,1,0:T(8,128)(2,1)}, bf16[8,32,512]{2,1,0:T(8,128)(2,1)S(1)}, u32[]{:S(2)}, u32[]{:S(2)}) collective-permute-start(bf16[8,32,512]{2,1,0:T(8,128)(2,1)} %get-tuple-element.64), channel_id=1, source_target_pairs={{0,8},{4,12},{8,0},{12,4},{1,9},{5,13},{9,1},{13,5},{2,10},{6,14},... | collective-permute-start | bytes 786440 | tf_op jit(solution)/shard_map/ppermute | solution.py:20
  17.1 10.1 %collective-permute-done.refs_1_ = bf16[8,32,512]{2,1,0:T(8,128)(2,1)S(1)} collective-permute-done((bf16[8,32,512]{2,1,0:T(8,128)(2,1)}, bf16[8,32,512]{2,1,0:T(8,128)(2,1)S(1)}, u32[]{:S(2)}, u32[]{:S(2)}) %collective-permute-start) | collective-permute-done | bytes 262176 | tf_op jit(solution)/shard_map/ppermute | solution.py:20
  30.3 10.2 %collective-permute-done.4.refs_2_ = bf16[2,256,512]{2,1,0:T(8,128)(2,1)S(1)} collective-permute-done((bf16[2,256,512]{2,1,0:T(8,128)(2,1)S(1)}, bf16[2,256,512]{2,1,0:T(8,128)(2,1)S(1)}, u32[]{:S(2)}, u32[]{:S(2)}) %collective-permute-start.4) | collective-permute-done | bytes 524320 | tf_op jit(solution)/shard_map/ppermute | solution.py:20
  42.4 6.2 %shard_map.103.refs_0_ = bf16[128,2048]{1,0:T(8,128)(2,1)S(1)} custom-call(s32[3]{0:T(128)S(1)} %pad_add_fusion.2.scalars, bf16[2,2,64,2048]{3,2,1,0:T(8,128)(2,1)S(1)} %bitcast.18, bf16[2,256,512]{2,1,0:T(8,128)(2,1)S(1)} %bitcast.16, bf16[2,256,512]{2,1,0:T(8,128)(2,1)S(1)} %collective-permute-done.3.refs_1_, ...), custom_call_target="tpu_custom_call" | custom-call | flops 1 | bytes 1 | tf_op jit(solution)/shard_map/pallas_call | solution.py:242
  48.6 3.7 %collective-permute-start.8 = (bf16[128,2048]{1,0:T(8,128)(2,1)S(1)}, bf16[128,2048]{1,0:T(8,128)(2,1)S(1)}, u32[]{:S(2)}, u32[]{:S(2)}) collective-permute-start(bf16[128,2048]{1,0:T(8,128)(2,1)S(1)} %shard_map.103.refs_0_), channel_id=1, source_target_pairs={{0,12},{4,8},{8,4},{12,0},{1,13},{5,9},{9,5},{13,1},{2,14},{6,10},... | collective-permute-start | bytes 1572872 | tf_op jit(solution)/shard_map/ppermute | solution.py:20
  52.3 5.3 %collective-permute-start.9 = (bf16[128,2048]{1,0:T(8,128)(2,1)S(1)}, bf16[128,2048]{1,0:T(8,128)(2,1)S(1)}, u32[]{:S(2)}, u32[]{:S(2)}) collective-permute-start(bf16[128,2048]{1,0:T(8,128)(2,1)S(1)} %shard_map.103.refs_0_), channel_id=1, source_target_pairs={{0,4},{4,0},{8,12},{12,8},{1,5},{5,1},{9,13},{13,9},{2,6},{6,2},{1... | collective-permute-start | bytes 1572872 | tf_op jit(solution)/shard_map/ppermute | solution.py:20
  57.6 6.2 %shard_map.102.refs_1_ = bf16[128,2048]{1,0:T(8,128)(2,1)S(1)} custom-call(s32[3]{0:T(128)S(1)} %pad_add_fusion.2.scalars, bf16[2,2,64,2048]{3,2,1,0:T(8,128)(2,1)S(1)} %bitcast.19, bf16[2,256,512]{2,1,0:T(8,128)(2,1)S(1)} %bitcast.17, bf16[2,256,512]{2,1,0:T(8,128)(2,1)S(1)} %collective-permute-done.3.refs_1_, ...), custom_call_target="tpu_custom_call" | custom-call | flops 1 | bytes 1 | tf_op jit(solution)/shard_map/pallas_call | solution.py:242
  64.9 3.4 %copy-done = bf16[2048,2048]{1,0:T(8,128)(2,1)S(1)} copy-done((bf16[2048,2048]{1,0:T(8,128)(2,1)S(1)}, bf16[2048,2048]{1,0:T(8,128)(2,1)}, u32[]{:S(2)}) %copy-start) | copy-done | bytes 8388632
  68.3 3.6 %shard_map.104 = (f32[128,2048]{1,0:T(8,128)S(1)}, bf16[128,2048]{1,0:T(8,128)(2,1)S(1)}) custom-call(s32[1]{0:T(128)} %bitcast.1.share, bf16[128,2048]{1,0:T(8,128)(2,1)S(1)} %shard_map.103.refs_0_, bf16[128,2048]{1,0:T(8,128)(2,1)S(1)} %shard_map.102.refs_1_, bf16[2048,2048]{1,0:T(8,128)(2,1)S(1)} %copy-done), custom_call_target="tpu_custom_call" | custom-call | flops 1 | bytes 1 | tf_op jit(solution)/shard_map/pallas_call | solution.py:56
  73.7 3.0 %collective-permute-done.9.refs_0_ = bf16[128,2048]{1,0:T(8,128)(2,1)S(1)} collective-permute-done((bf16[128,2048]{1,0:T(8,128)(2,1)S(1)}, bf16[128,2048]{1,0:T(8,128)(2,1)S(1)}, u32[]{:S(2)}, u32[]{:S(2)}) %collective-permute-start.9) | collective-permute-done | bytes 524320 | tf_op jit(solution)/shard_map/ppermute | solution.py:20
  76.6 3.4 %copy-done.1 = bf16[2048,2048]{1,0:T(8,128)(2,1)S(1)} copy-done((bf16[2048,2048]{1,0:T(8,128)(2,1)S(1)}, bf16[2048,2048]{1,0:T(8,128)(2,1)}, u32[]{:S(2)}) %copy-start.1) | copy-done | bytes 8388632
  80.0 3.6 %shard_map.105 = (f32[64,2048]{1,0:T(8,128)S(1)}, bf16[64,2048]{1,0:T(8,128)(2,1)S(1)}, bf16[64,2048]{1,0:T(8,128)(2,1)S(1)}, bf16[64,2048]{1,0:T(8,128)(2,1)S(1)}) custom-call(s32[1]{0:T(128)} %bitcast.1.share, bf16[128,2048]{1,0:T(8,128)(2,1)S(1)} %collective-permute-done.9.refs_0_, bf16[128,2048]{1,0:T(8,128)(2,1)S(1)} %collective-permute-done.8.refs_1_, ...), custom_call_target="tpu_custom_call" | custom-call | flops 1 | bytes 1 | tf_op jit(solution)/shard_map/pallas_call | solution.py:56
  87.8 13.1 %collective-permute-start.15 = (bf16[128,2048]{1,0:T(8,128)(2,1)S(1)}, bf16[128,2048]{1,0:T(8,128)(2,1)S(1)}, u32[]{:S(2)}, u32[]{:S(2)}) collective-permute-start(bf16[128,2048]{1,0:T(8,128)(2,1)S(1)} %broadcast_select_fusion.1), channel_id=1, source_target_pairs={{0,8},{12,4},{4,0},{8,12},{1,9},{13,5},{5,1},{9,13},{2,10},{14,6},... | collective-permute-start | bytes 1572872 | tf_op jit(solution)/shard_map/ppermute | solution.py:27
  102.9 3.6 %shard_map.106 = (f32[128,2048]{1,0:T(8,128)S(1)}, bf16[128,2048]{1,0:T(8,128)(2,1)S(1)}) custom-call(s32[1]{0:T(128)} %bitcast.1.share, bf16[128,2048]{1,0:T(8,128)(2,1)S(1)} %copy-done.7, bf16[128,2048]{1,0:T(8,128)(2,1)S(1)} %collective-permute-done.6.refs_1_, bf16[2048,2048]{1,0:T(8,128)(2,1)S(1)} %bitcast.11), custom_call_target="tpu_custom_call" | custom-call | flops 1 | bytes 1 | tf_op jit(solution)/shard_map/pallas_call | solution.py:56
  110.4 2.9 %collective-permute-done.15.refs_0_ = bf16[128,2048]{1,0:T(8,128)(2,1)S(1)} collective-permute-done((bf16[128,2048]{1,0:T(8,128)(2,1)S(1)}, bf16[128,2048]{1,0:T(8,128)(2,1)S(1)}, u32[]{:S(2)}, u32[]{:S(2)}) %collective-permute-start.15) | collective-permute-done | bytes 524320 | tf_op jit(solution)/shard_map/ppermute | solution.py:27
  113.3 2.5 %shard_map.107 = (f32[64,2048]{1,0:T(8,128)S(1)}, bf16[64,2048]{1,0:T(8,128)(2,1)S(1)}) custom-call(s32[1]{0:T(128)} %bitcast.1.share, bf16[128,2048]{1,0:T(8,128)(2,1)S(1)} %collective-permute-done.15.refs_0_, bf16[2048,2048]{1,0:T(8,128)(2,1)S(1)} %bitcast.11), custom_call_target="tpu_custom_call" | custom-call | flops 1 | bytes 1 | tf_op jit(solution)/shard_map/pallas_call | solution.py:56
  120.2 4.3 %collective-permute-done.20.refs_0_ = bf16[128,2048]{1,0:T(8,128)(2,1)S(1)} collective-permute-done((bf16[128,2048]{1,0:T(8,128)(2,1)}, bf16[128,2048]{1,0:T(8,128)(2,1)S(1)}, u32[]{:S(2)}, u32[]{:S(2)}) %collective-permute-start.20) | collective-permute-done | bytes 524320 | tf_op jit(solution)/shard_map/ppermute | solution.py:27
  124.6 3.4 %copy-done.2 = bf16[2048,2048]{1,0:T(8,128)(2,1)S(1)} copy-done((bf16[2048,2048]{1,0:T(8,128)(2,1)S(1)}, bf16[2048,2048]{1,0:T(8,128)(2,1)}, u32[]{:S(2)}) %copy-start.2) | copy-done | bytes 8388632
  128.0 2.5 %shard_map.108 = (f32[64,2048]{1,0:T(8,128)S(1)}, bf16[64,2048]{1,0:T(8,128)(2,1)S(1)}) custom-call(s32[1]{0:T(128)} %bitcast.1.share, bf16[128,2048]{1,0:T(8,128)(2,1)S(1)} %collective-permute-done.20.refs_0_, bf16[2048,2048]{1,0:T(8,128)(2,1)S(1)} %copy-done.2), custom_call_target="tpu_custom_call" | custom-call | flops 1 | bytes 1 | tf_op jit(solution)/shard_map/pallas_call | solution.py:56
  131.2 3.3 %collective-permute-start.23 = (bf16[32,2048]{1,0:T(8,128)(2,1)S(1)}, bf16[32,2048]{1,0:T(8,128)(2,1)S(1)}, u32[]{:S(2)}, u32[]{:S(2)}) collective-permute-start(bf16[32,2048]{1,0:T(8,128)(2,1)S(1)} %add_convert_fusion.7), channel_id=1, source_target_pairs={{0,8},{4,12},{8,0},{12,4},{1,9},{5,13},{9,1},{13,5},{2,10},{6,14},... | collective-permute-start | bytes 393224 | tf_op jit(solution)/shard_map/ppermute | solution.py:20
  142.3 3.0 %collective-permute-done.21 = bf16[32,2048]{1,0:T(8,128)(2,1)S(1)} collective-permute-done((bf16[32,2048]{1,0:T(8,128)(2,1)S(1)}, bf16[32,2048]{1,0:T(8,128)(2,1)S(1)}, u32[]{:S(2)}, u32[]{:S(2)}) %collective-permute-start.21) | collective-permute-done | bytes 131104 | tf_op jit(solution)/shard_map/ppermute | solution.py:20
  145.3 2.6 %collective-permute-done.25 = bf16[32,2048]{1,0:T(8,128)(2,1)S(1)} collective-permute-done((bf16[32,2048]{1,0:T(8,128)(2,1)S(1)}, bf16[32,2048]{1,0:T(8,128)(2,1)S(1)}, u32[]{:S(2)}, u32[]{:S(2)}) %collective-permute-start.25) | collective-permute-done | bytes 131104 | tf_op jit(solution)/shard_map/ppermute | solution.py:20
  149.9 5.8 %collective-permute-done.28 = bf16[32,2048]{1,0:T(8,128)(2,1)S(1)} collective-permute-done((bf16[32,2048]{1,0:T(8,128)(2,1)S(1)}, bf16[32,2048]{1,0:T(8,128)(2,1)S(1)}, u32[]{:S(2)}, u32[]{:S(2)}) %collective-permute-start.28) | collective-permute-done | bytes 131104 | tf_op jit(solution)/shard_map/ppermute | solution.py:20
  (114 shorter events, 42.3 us)
Async XLA Ops:
  4.4 22.8 %collective-permute-start = (bf16[8,32,512]{2,1,0:T(8,128)(2,1)}, bf16[8,32,512]{2,1,0:T(8,128)(2,1)S(1)}, u32[]{:S(2)}, u32[]{:S(2)}) collective-permute-start(bf16[8,32,512]{2,1,0:T(8,128)(2,1)} %get-tuple-element.64), channel_id=1, source_target_pairs={{0,8},{4,12},{8,0},{12,4},{1,9},{5,13},{9,1},{13,5},{2,10},{6,14},... | collective-permute-start | bytes 786440 | tf_op jit(solution)/shard_map/ppermute | solution.py:20
  8.5 18.6 %collective-permute-start.1 = (bf16[8,32,512]{2,1,0:T(8,128)(2,1)}, bf16[8,32,512]{2,1,0:T(8,128)(2,1)S(1)}, u32[]{:S(2)}, u32[]{:S(2)}) collective-permute-start(bf16[8,32,512]{2,1,0:T(8,128)(2,1)} %get-tuple-element.65), channel_id=1, source_target_pairs={{0,12},{4,8},{8,4},{12,0},{1,13},{5,9},{9,5},{13,1},{2,14},{6,10},... | collective-permute-start | bytes 786440 | tf_op jit(solution)/shard_map/ppermute | solution.py:20
  9.9 17.8 %collective-permute-start.2 = (bf16[8,32,512]{2,1,0:T(8,128)(2,1)}, bf16[8,32,512]{2,1,0:T(8,128)(2,1)S(1)}, u32[]{:S(2)}, u32[]{:S(2)}) collective-permute-start(bf16[8,32,512]{2,1,0:T(8,128)(2,1)} %get-tuple-element.66), channel_id=1, source_target_pairs={{0,4},{4,0},{8,12},{12,8},{1,5},{5,1},{9,13},{13,9},{2,6},{6,2},{1... | collective-permute-start | bytes 786440 | tf_op jit(solution)/shard_map/ppermute | solution.py:20
  28.6 11.9 %collective-permute-start.4 = (bf16[2,256,512]{2,1,0:T(8,128)(2,1)S(1)}, bf16[2,256,512]{2,1,0:T(8,128)(2,1)S(1)}, u32[]{:S(2)}, u32[]{:S(2)}) collective-permute-start(bf16[2,256,512]{2,1,0:T(8,128)(2,1)S(1)} %bitcast.14), channel_id=1, source_target_pairs={{0,2},{2,0},{1,3},{3,1},{4,6},{6,4},{5,7},{7,5},{8,10},{10,8},{9,1... | collective-permute-start | bytes 1572872 | tf_op jit(solution)/shard_map/ppermute | solution.py:20
  30.3 10.2 %collective-permute-start.3 = (bf16[2,256,512]{2,1,0:T(8,128)(2,1)S(1)}, bf16[2,256,512]{2,1,0:T(8,128)(2,1)S(1)}, u32[]{:S(2)}, u32[]{:S(2)}) collective-permute-start(bf16[2,256,512]{2,1,0:T(8,128)(2,1)S(1)} %bitcast.15), channel_id=1, source_target_pairs={{0,1},{1,0},{2,3},{3,2},{4,5},{5,4},{6,7},{7,6},{8,9},{9,8},{10,11... | collective-permute-start | bytes 1572872 | tf_op jit(solution)/shard_map/ppermute | solution.py:20
  48.6 25.1 %collective-permute-start.8 = (bf16[128,2048]{1,0:T(8,128)(2,1)S(1)}, bf16[128,2048]{1,0:T(8,128)(2,1)S(1)}, u32[]{:S(2)}, u32[]{:S(2)}) collective-permute-start(bf16[128,2048]{1,0:T(8,128)(2,1)S(1)} %shard_map.103.refs_0_), channel_id=1, source_target_pairs={{0,12},{4,8},{8,4},{12,0},{1,13},{5,9},{9,5},{13,1},{2,14},{6,10},... | collective-permute-start | bytes 1572872 | tf_op jit(solution)/shard_map/ppermute | solution.py:20
  52.3 24.3 %collective-permute-start.9 = (bf16[128,2048]{1,0:T(8,128)(2,1)S(1)}, bf16[128,2048]{1,0:T(8,128)(2,1)S(1)}, u32[]{:S(2)}, u32[]{:S(2)}) collective-permute-start(bf16[128,2048]{1,0:T(8,128)(2,1)S(1)} %shard_map.103.refs_0_), channel_id=1, source_target_pairs={{0,4},{4,0},{8,12},{12,8},{1,5},{5,1},{9,13},{13,9},{2,6},{6,2},{1... | collective-permute-start | bytes 1572872 | tf_op jit(solution)/shard_map/ppermute | solution.py:20
  63.8 23.9 %collective-permute-start.6 = (bf16[128,2048]{1,0:T(8,128)(2,1)S(1)}, bf16[128,2048]{1,0:T(8,128)(2,1)S(1)}, u32[]{:S(2)}, u32[]{:S(2)}) collective-permute-start(bf16[128,2048]{1,0:T(8,128)(2,1)S(1)} %shard_map.102.refs_1_), channel_id=1, source_target_pairs={{0,12},{4,8},{8,4},{12,0},{1,13},{5,9},{9,5},{13,1},{2,14},{6,10},... | collective-permute-start | bytes 1572872 | tf_op jit(solution)/shard_map/ppermute | solution.py:20
  64.9 36.0 %collective-permute-start.7 = (bf16[128,2048]{1,0:T(8,128)(2,1)S(1)}, bf16[128,2048]{1,0:T(8,128)(2,1)S(1)}, u32[]{:S(2)}, u32[]{:S(2)}) collective-permute-start(bf16[128,2048]{1,0:T(8,128)(2,1)S(1)} %shard_map.102.refs_1_), channel_id=1, source_target_pairs={{0,4},{4,0},{8,12},{12,8},{1,5},{5,1},{9,13},{13,9},{2,6},{6,2},{1... | collective-permute-start | bytes 1572872 | tf_op jit(solution)/shard_map/ppermute | solution.py:20
  83.6 17.3 %collective-permute-start.10 = (bf16[64,2048]{1,0:T(8,128)(2,1)S(1)}, bf16[64,2048]{1,0:T(8,128)(2,1)S(1)}, u32[]{:S(2)}, u32[]{:S(2)}) collective-permute-start(bf16[64,2048]{1,0:T(8,128)(2,1)S(1)} %get-tuple-element.76), channel_id=1, source_target_pairs={{0,1},{1,0},{2,3},{3,2},{4,5},{5,4},{6,7},{7,6},{8,9},{9,8},{10,11... | collective-permute-start | bytes 786440 | tf_op jit(solution)/shard_map/ppermute | solution.py:20
  83.7 17.2 %collective-permute-start.11 = (bf16[64,2048]{1,0:T(8,128)(2,1)S(1)}, bf16[64,2048]{1,0:T(8,128)(2,1)S(1)}, u32[]{:S(2)}, u32[]{:S(2)}) collective-permute-start(bf16[64,2048]{1,0:T(8,128)(2,1)S(1)} %get-tuple-element.77), channel_id=1, source_target_pairs={{0,2},{1,3},{2,0},{3,1},{4,6},{5,7},{6,4},{7,5},{8,10},{9,11},{10,... | collective-permute-start | bytes 786440 | tf_op jit(solution)/shard_map/ppermute | solution.py:20
  85.0 15.9 %collective-permute-start.12 = (bf16[64,2048]{1,0:T(8,128)(2,1)S(1)}, bf16[64,2048]{1,0:T(8,128)(2,1)S(1)}, u32[]{:S(2)}, u32[]{:S(2)}) collective-permute-start(bf16[64,2048]{1,0:T(8,128)(2,1)S(1)} %get-tuple-element.78), channel_id=1, source_target_pairs={{0,3},{1,2},{2,1},{3,0},{4,7},{5,6},{6,5},{7,4},{8,11},{9,10},{10,... | collective-permute-start | bytes 786440 | tf_op jit(solution)/shard_map/ppermute | solution.py:20
  87.8 25.5 %collective-permute-start.15 = (bf16[128,2048]{1,0:T(8,128)(2,1)S(1)}, bf16[128,2048]{1,0:T(8,128)(2,1)S(1)}, u32[]{:S(2)}, u32[]{:S(2)}) collective-permute-start(bf16[128,2048]{1,0:T(8,128)(2,1)S(1)} %broadcast_select_fusion.1), channel_id=1, source_target_pairs={{0,8},{12,4},{4,0},{8,12},{1,9},{13,5},{5,1},{9,13},{2,10},{14,6},... | collective-permute-start | bytes 1572872 | tf_op jit(solution)/shard_map/ppermute | solution.py:27
  101.9 22.7 %collective-permute-start.20 = (bf16[128,2048]{1,0:T(8,128)(2,1)}, bf16[128,2048]{1,0:T(8,128)(2,1)S(1)}, u32[]{:S(2)}, u32[]{:S(2)}) collective-permute-start(bf16[128,2048]{1,0:T(8,128)(2,1)} %broadcast_select_fusion), channel_id=1, source_target_pairs={{0,8},{12,4},{4,0},{8,12},{1,9},{13,5},{5,1},{9,13},{2,10},{14,6},... | collective-permute-start | bytes 1572872 | tf_op jit(solution)/shard_map/ppermute | solution.py:27
  107.5 23.1 %collective-permute-start.13 = (bf16[32,2048]{1,0:T(8,128)(2,1)}, bf16[32,2048]{1,0:T(8,128)(2,1)}, u32[]{:S(2)}, u32[]{:S(2)}) collective-permute-start(bf16[32,2048]{1,0:T(8,128)(2,1)} %get-tuple-element.122), channel_id=1, source_target_pairs={{0,4},{4,0},{8,12},{12,8},{1,5},{5,1},{9,13},{13,9},{2,6},{6,2},{1... | collective-permute-start | bytes 393224 | tf_op jit(solution)/shard_map/ppermute | solution.py:20
  109.5 21.1 %collective-permute-start.14 = (bf16[32,2048]{1,0:T(8,128)(2,1)}, bf16[32,2048]{1,0:T(8,128)(2,1)}, u32[]{:S(2)}, u32[]{:S(2)}) collective-permute-start(bf16[32,2048]{1,0:T(8,128)(2,1)} %get-tuple-element.121), channel_id=1, source_target_pairs={{0,12},{4,8},{8,4},{12,0},{1,13},{5,9},{9,5},{13,1},{2,14},{6,10},... | collective-permute-start | bytes 393224 | tf_op jit(solution)/shard_map/ppermute | solution.py:20
  116.7 13.9 %collective-permute-start.17 = (bf16[64,2048]{1,0:T(8,128)(2,1)}, bf16[64,2048]{1,0:T(8,128)(2,1)S(1)}, u32[]{:S(2)}, u32[]{:S(2)}) collective-permute-start(bf16[64,2048]{1,0:T(8,128)(2,1)} %add_convert_fusion.3), channel_id=1, source_target_pairs={{0,2},{2,0},{1,3},{3,1},{4,6},{6,4},{5,7},{7,5},{8,10},{10,8},{9,1... | collective-permute-start | bytes 786440 | tf_op jit(solution)/shard_map/ppermute | solution.py:20
  119.5 11.1 %collective-permute-start.19 = (bf16[32,2048]{1,0:T(8,128)(2,1)}, bf16[32,2048]{1,0:T(8,128)(2,1)S(1)}, u32[]{:S(2)}, u32[]{:S(2)}) collective-permute-start(bf16[32,2048]{1,0:T(8,128)(2,1)} %add_convert_fusion.8), channel_id=1, source_target_pairs={{0,2},{2,0},{1,3},{3,1},{4,6},{6,4},{5,7},{7,5},{8,10},{10,8},{9,1... | collective-permute-start | bytes 393224 | tf_op jit(solution)/shard_map/ppermute | solution.py:20
  130.7 8.1 %collective-permute-start.24 = (bf16[64,2048]{1,0:T(8,128)(2,1)S(1)}, bf16[64,2048]{1,0:T(8,128)(2,1)S(1)}, u32[]{:S(2)}, u32[]{:S(2)}) collective-permute-start(bf16[64,2048]{1,0:T(8,128)(2,1)S(1)} %get-tuple-element.107), channel_id=1, source_target_pairs={{0,1},{1,0},{2,3},{3,2},{4,5},{5,4},{6,7},{7,6},{8,9},{9,8},{10,11... | collective-permute-start | bytes 786440 | tf_op jit(solution)/shard_map/ppermute | solution.py:20
  131.2 11.1 %collective-permute-start.23 = (bf16[32,2048]{1,0:T(8,128)(2,1)S(1)}, bf16[32,2048]{1,0:T(8,128)(2,1)S(1)}, u32[]{:S(2)}, u32[]{:S(2)}) collective-permute-start(bf16[32,2048]{1,0:T(8,128)(2,1)S(1)} %add_convert_fusion.7), channel_id=1, source_target_pairs={{0,8},{4,12},{8,0},{12,4},{1,9},{5,13},{9,1},{13,5},{2,10},{6,14},... | collective-permute-start | bytes 393224 | tf_op jit(solution)/shard_map/ppermute | solution.py:20
  134.7 10.6 %collective-permute-start.21 = (bf16[32,2048]{1,0:T(8,128)(2,1)S(1)}, bf16[32,2048]{1,0:T(8,128)(2,1)S(1)}, u32[]{:S(2)}, u32[]{:S(2)}) collective-permute-start(bf16[32,2048]{1,0:T(8,128)(2,1)S(1)} %get-tuple-element.120), channel_id=1, source_target_pairs={{0,4},{4,0},{8,12},{12,8},{1,5},{5,1},{9,13},{13,9},{2,6},{6,2},{1... | collective-permute-start | bytes 393224 | tf_op jit(solution)/shard_map/ppermute | solution.py:20
  135.0 10.3 %collective-permute-start.22 = (bf16[32,2048]{1,0:T(8,128)(2,1)S(1)}, bf16[32,2048]{1,0:T(8,128)(2,1)S(1)}, u32[]{:S(2)}, u32[]{:S(2)}) collective-permute-start(bf16[32,2048]{1,0:T(8,128)(2,1)S(1)} %get-tuple-element.119), channel_id=1, source_target_pairs={{0,12},{4,8},{8,4},{12,0},{1,13},{5,9},{9,5},{13,1},{2,14},{6,10},... | collective-permute-start | bytes 393224 | tf_op jit(solution)/shard_map/ppermute | solution.py:20
  137.3 10.6 %collective-permute-start.27 = (bf16[64,2048]{1,0:T(8,128)(2,1)S(1)}, bf16[64,2048]{1,0:T(8,128)(2,1)S(1)}, u32[]{:S(2)}, u32[]{:S(2)}) collective-permute-start(bf16[64,2048]{1,0:T(8,128)(2,1)S(1)} %add_convert_fusion.1), channel_id=1, source_target_pairs={{0,2},{2,0},{1,3},{3,1},{4,6},{6,4},{5,7},{7,5},{8,10},{10,8},{9,1... | collective-permute-start | bytes 786440 | tf_op jit(solution)/shard_map/ppermute | solution.py:20
  138.8 9.1 %collective-permute-start.25 = (bf16[32,2048]{1,0:T(8,128)(2,1)S(1)}, bf16[32,2048]{1,0:T(8,128)(2,1)S(1)}, u32[]{:S(2)}, u32[]{:S(2)}) collective-permute-start(bf16[32,2048]{1,0:T(8,128)(2,1)S(1)} %add_convert_fusion.6), channel_id=1, source_target_pairs={{0,2},{2,0},{1,3},{3,1},{4,6},{6,4},{5,7},{7,5},{8,10},{10,8},{9,1... | collective-permute-start | bytes 393224 | tf_op jit(solution)/shard_map/ppermute | solution.py:20
  (24 other events, 190.0 us)

commit v17 on v16

--- a/solution.py
+++ b/solution.py
@@ -66,7 +66,7 @@
             jax.ShapeDtypeStruct((rows, columns), jnp.bfloat16 if i else jnp.float32)
             for i in range(count)
         ],
-        compiler_params=pltpu.CompilerParams(vmem_limit_bytes=16 * 1024 * 1024),
+        compiler_params=pltpu.CompilerParams(vmem_limit_bytes=10 * 1024 * 1024),
         cost_estimate=LIGHT,
     )(share, *blocks, out_weight)
 
@@ -199,14 +199,14 @@
     part_slots = parts[0].shape[1]
     share_rows = BLK // share_count
     share, count = scalars[0], scalars[1 + request]
+    slot = lax.broadcasted_iota(jnp.int32, (part_slots, head_width), 0)
+    position = (slot // share_rows) * BLK + slot % share_rows
     for flip in range(share_count):
         rows = pl.ds(flip * part_slots, part_slots)
         projected = jnp.dot(parts[flip][request], kv_up[...], preferred_element_type=jnp.float32)
         key = rms_scale(projected[:, :head_width], k_gain)
         keys[rows, :] = key.astype(jnp.bfloat16)
-        slot = lax.broadcasted_iota(jnp.int32, (part_slots, head_width), 0)
-        position = (slot // share_rows) * BLK + (share ^ flip) * share_rows + slot % share_rows
-        live = jnp.where(position < count, 1.0, 0.0)
+        live = jnp.where(position < count - (share ^ flip) * share_rows, 1.0, 0.0)
         values[rows, :head_width] = (projected[:, head_width:] * live).astype(jnp.bfloat16)
         values[rows, head_width:] = live.astype(jnp.bfloat16)
     scale = math.log2(math.e) / math.sqrt(head_width)
@@ -257,7 +257,7 @@
             pltpu.VMEM((slots, head_width), jnp.bfloat16),
             pltpu.VMEM((slots, 2 * head_width), jnp.bfloat16),
         ],
-        compiler_params=pltpu.CompilerParams(vmem_limit_bytes=16 * 1024 * 1024),
+        compiler_params=pltpu.CompilerParams(vmem_limit_bytes=12 * 1024 * 1024),
         cost_estimate=LIGHT,
     )(scalars, queries, *parts, kv_flat, gains)
 

time: 157 us -> 157 us (level)
  no operation moved by 1% of the time
where the time goes in v17:
time: 157 us
  starting transfers between devices  48.3 us (31%)
  waiting for transfers between devices  48 us (31%)
  Pallas kernels  32.5 us (21%)
  local copies, waits for them, and re-layouts  21.9 us (14%)
  other arithmetic  5.95 us (4%)
    ppermute x27, waiting for transfers between devices, swap(): lax.ppermute(values, axis, [(i, i ^ flip) for i in range(lax.axis_size(ax...  40.9 us
    ppermute x27, starting transfers between devices, swap(): lax.ppermute(values, axis, [(i, i ^ flip) for i in range(lax.axis_size(ax...  35 us
    pallas_call x5, Pallas kernels, project_out(): pl.pallas_call(functools.partial(project_kernel, len(blocks), list(range(...  15.9 us
    unnamed x38, local copies, waits for them, and re-layouts  13.7 us
    ppermute x2, starting transfers between devices, second_hop(): return lax.ppermute(passed, 'pool', [(0, 2), (3, 1), (1, 0), (2, 3)])  13.3 us
    pallas_call x2, Pallas kernels, attend(): pl.pallas_call(functools.partial(attend_kernel, len(parts)), grid=(reques...  12.3 us
    ppermute x2, waiting for transfers between devices, second_hop(): return lax.ppermute(passed, 'pool', [(0, 2), (3, 1), (1, 0), (2, 3)])  7.08 us
    pallas_call x1, Pallas kernels, fetch(): pl.pallas_call(functools.partial(fetch_kernel, pool_size=pool_size, share...  3.37 us
  transfers between devices with their start and end apart: 29, of which 12 were waited for; matrix products, arithmetic and copies ran while one was open for 8% of the time, Pallas kernels for 14%

profile of v17, /device:TPU:0, one launch (start us, length us, event | category | flops | bytes accessed | tf_op | source)
XLA Modules:
  0.0 156.9 jit_solution(9449855106941137678)
XLA Ops:
  0.7 3.4 %shard_map.100 = (s32[2,16]{1,0:T(2,128)}, bf16[8,32,512]{2,1,0:T(8,128)(2,1)}, bf16[8,32,512]{2,1,0:T(8,128)(2,1)}, bf16[8,32,512]{2,1,0:T(8,128)(2,1)}, bf16[8,32,512]{2,1,0:T(8,128)(2,1)}) custom-call(s32[2]{0:T(128)} %pad_add_fusion.1.place, s32[8,8]{1,0:T(8,128)} %holder.1, s32[8,8]{1,0:T(8,128)} %block.1, s32[8]{0:T(128)} %serving.1, ...), custom_call_target="tpu_custom_call" | custom-call | flops 1 | bytes 1 | tf_op jit(solution)/shard_map/pallas_call | solution.py:153
  4.0 4.5 %collective-permute-start = (bf16[8,32,512]{2,1,0:T(8,128)(2,1)}, bf16[8,32,512]{2,1,0:T(8,128)(2,1)S(1)}, u32[]{:S(2)}, u32[]{:S(2)}) collective-permute-start(bf16[8,32,512]{2,1,0:T(8,128)(2,1)} %get-tuple-element.64), channel_id=1, source_target_pairs={{0,8},{4,12},{8,0},{12,4},{1,9},{5,13},{9,1},{13,5},{2,10},{6,14},... | collective-permute-start | bytes 786440 | tf_op jit(solution)/shard_map/ppermute | solution.py:20
  17.3 9.8 %collective-permute-done.refs_1_ = bf16[8,32,512]{2,1,0:T(8,128)(2,1)S(1)} collective-permute-done((bf16[8,32,512]{2,1,0:T(8,128)(2,1)}, bf16[8,32,512]{2,1,0:T(8,128)(2,1)S(1)}, u32[]{:S(2)}, u32[]{:S(2)}) %collective-permute-start) | collective-permute-done | bytes 262176 | tf_op jit(solution)/shard_map/ppermute | solution.py:20
  30.2 10.3 %collective-permute-done.4.refs_2_ = bf16[2,256,512]{2,1,0:T(8,128)(2,1)S(1)} collective-permute-done((bf16[2,256,512]{2,1,0:T(8,128)(2,1)S(1)}, bf16[2,256,512]{2,1,0:T(8,128)(2,1)S(1)}, u32[]{:S(2)}, u32[]{:S(2)}) %collective-permute-start.4) | collective-permute-done | bytes 524320 | tf_op jit(solution)/shard_map/ppermute | solution.py:20
  42.3 6.1 %shard_map.103.refs_0_ = bf16[128,2048]{1,0:T(8,128)(2,1)S(1)} custom-call(s32[3]{0:T(128)S(1)} %pad_add_fusion.2.scalars, bf16[2,2,64,2048]{3,2,1,0:T(8,128)(2,1)S(1)} %bitcast.18, bf16[2,256,512]{2,1,0:T(8,128)(2,1)S(1)} %bitcast.16, bf16[2,256,512]{2,1,0:T(8,128)(2,1)S(1)} %collective-permute-done.3.refs_1_, ...), custom_call_target="tpu_custom_call" | custom-call | flops 1 | bytes 1 | tf_op jit(solution)/shard_map/pallas_call | solution.py:242
  48.5 4.4 %collective-permute-start.8 = (bf16[128,2048]{1,0:T(8,128)(2,1)S(1)}, bf16[128,2048]{1,0:T(8,128)(2,1)S(1)}, u32[]{:S(2)}, u32[]{:S(2)}) collective-permute-start(bf16[128,2048]{1,0:T(8,128)(2,1)S(1)} %shard_map.103.refs_0_), channel_id=1, source_target_pairs={{0,12},{4,8},{8,4},{12,0},{1,13},{5,9},{9,5},{13,1},{2,14},{6,10},... | collective-permute-start | bytes 1572872 | tf_op jit(solution)/shard_map/ppermute | solution.py:20
  52.9 5.3 %collective-permute-start.9 = (bf16[128,2048]{1,0:T(8,128)(2,1)S(1)}, bf16[128,2048]{1,0:T(8,128)(2,1)S(1)}, u32[]{:S(2)}, u32[]{:S(2)}) collective-permute-start(bf16[128,2048]{1,0:T(8,128)(2,1)S(1)} %shard_map.103.refs_0_), channel_id=1, source_target_pairs={{0,4},{4,0},{8,12},{12,8},{1,5},{5,1},{9,13},{13,9},{2,6},{6,2},{1... | collective-permute-start | bytes 1572872 | tf_op jit(solution)/shard_map/ppermute | solution.py:20
  58.1 6.2 %shard_map.102.refs_1_ = bf16[128,2048]{1,0:T(8,128)(2,1)S(1)} custom-call(s32[3]{0:T(128)S(1)} %pad_add_fusion.2.scalars, bf16[2,2,64,2048]{3,2,1,0:T(8,128)(2,1)S(1)} %bitcast.19, bf16[2,256,512]{2,1,0:T(8,128)(2,1)S(1)} %bitcast.17, bf16[2,256,512]{2,1,0:T(8,128)(2,1)S(1)} %collective-permute-done.3.refs_1_, ...), custom_call_target="tpu_custom_call" | custom-call | flops 1 | bytes 1 | tf_op jit(solution)/shard_map/pallas_call | solution.py:242
  65.3 3.4 %copy-done = bf16[2048,2048]{1,0:T(8,128)(2,1)S(1)} copy-done((bf16[2048,2048]{1,0:T(8,128)(2,1)S(1)}, bf16[2048,2048]{1,0:T(8,128)(2,1)}, u32[]{:S(2)}) %copy-start) | copy-done | bytes 8388632
  68.7 3.6 %shard_map.104 = (f32[128,2048]{1,0:T(8,128)S(1)}, bf16[128,2048]{1,0:T(8,128)(2,1)S(1)}) custom-call(s32[1]{0:T(128)} %bitcast.1.share, bf16[128,2048]{1,0:T(8,128)(2,1)S(1)} %shard_map.103.refs_0_, bf16[128,2048]{1,0:T(8,128)(2,1)S(1)} %shard_map.102.refs_1_, bf16[2048,2048]{1,0:T(8,128)(2,1)S(1)} %copy-done), custom_call_target="tpu_custom_call" | custom-call | flops 1 | bytes 1 | tf_op jit(solution)/shard_map/pallas_call | solution.py:56
  74.1 2.9 %collective-permute-done.9.refs_0_ = bf16[128,2048]{1,0:T(8,128)(2,1)S(1)} collective-permute-done((bf16[128,2048]{1,0:T(8,128)(2,1)S(1)}, bf16[128,2048]{1,0:T(8,128)(2,1)S(1)}, u32[]{:S(2)}, u32[]{:S(2)}) %collective-permute-start.9) | collective-permute-done | bytes 524320 | tf_op jit(solution)/shard_map/ppermute | solution.py:20
  77.0 3.4 %copy-done.1 = bf16[2048,2048]{1,0:T(8,128)(2,1)S(1)} copy-done((bf16[2048,2048]{1,0:T(8,128)(2,1)S(1)}, bf16[2048,2048]{1,0:T(8,128)(2,1)}, u32[]{:S(2)}) %copy-start.1) | copy-done | bytes 8388632
  80.3 3.6 %shard_map.105 = (f32[64,2048]{1,0:T(8,128)S(1)}, bf16[64,2048]{1,0:T(8,128)(2,1)S(1)}, bf16[64,2048]{1,0:T(8,128)(2,1)S(1)}, bf16[64,2048]{1,0:T(8,128)(2,1)S(1)}) custom-call(s32[1]{0:T(128)} %bitcast.1.share, bf16[128,2048]{1,0:T(8,128)(2,1)S(1)} %collective-permute-done.9.refs_0_, bf16[128,2048]{1,0:T(8,128)(2,1)S(1)} %collective-permute-done.8.refs_1_, ...), custom_call_target="tpu_custom_call" | custom-call | flops 1 | bytes 1 | tf_op jit(solution)/shard_map/pallas_call | solution.py:56
  88.1 13.3 %collective-permute-start.15 = (bf16[128,2048]{1,0:T(8,128)(2,1)S(1)}, bf16[128,2048]{1,0:T(8,128)(2,1)S(1)}, u32[]{:S(2)}, u32[]{:S(2)}) collective-permute-start(bf16[128,2048]{1,0:T(8,128)(2,1)S(1)} %broadcast_select_fusion.1), channel_id=1, source_target_pairs={{0,8},{12,4},{4,0},{8,12},{1,9},{13,5},{5,1},{9,13},{2,10},{14,6},... | collective-permute-start | bytes 1572872 | tf_op jit(solution)/shard_map/ppermute | solution.py:27
  103.5 3.6 %shard_map.106 = (f32[128,2048]{1,0:T(8,128)S(1)}, bf16[128,2048]{1,0:T(8,128)(2,1)S(1)}) custom-call(s32[1]{0:T(128)} %bitcast.1.share, bf16[128,2048]{1,0:T(8,128)(2,1)S(1)} %copy-done.7, bf16[128,2048]{1,0:T(8,128)(2,1)S(1)} %collective-permute-done.6.refs_1_, bf16[2048,2048]{1,0:T(8,128)(2,1)S(1)} %bitcast.11), custom_call_target="tpu_custom_call" | custom-call | flops 1 | bytes 1 | tf_op jit(solution)/shard_map/pallas_call | solution.py:56
  110.9 2.9 %collective-permute-done.15.refs_0_ = bf16[128,2048]{1,0:T(8,128)(2,1)S(1)} collective-permute-done((bf16[128,2048]{1,0:T(8,128)(2,1)S(1)}, bf16[128,2048]{1,0:T(8,128)(2,1)S(1)}, u32[]{:S(2)}, u32[]{:S(2)}) %collective-permute-start.15) | collective-permute-done | bytes 524320 | tf_op jit(solution)/shard_map/ppermute | solution.py:27
  113.8 2.5 %shard_map.107 = (f32[64,2048]{1,0:T(8,128)S(1)}, bf16[64,2048]{1,0:T(8,128)(2,1)S(1)}) custom-call(s32[1]{0:T(128)} %bitcast.1.share, bf16[128,2048]{1,0:T(8,128)(2,1)S(1)} %collective-permute-done.15.refs_0_, bf16[2048,2048]{1,0:T(8,128)(2,1)S(1)} %bitcast.11), custom_call_target="tpu_custom_call" | custom-call | flops 1 | bytes 1 | tf_op jit(solution)/shard_map/pallas_call | solution.py:56
  120.9 4.2 %collective-permute-done.20.refs_0_ = bf16[128,2048]{1,0:T(8,128)(2,1)S(1)} collective-permute-done((bf16[128,2048]{1,0:T(8,128)(2,1)}, bf16[128,2048]{1,0:T(8,128)(2,1)S(1)}, u32[]{:S(2)}, u32[]{:S(2)}) %collective-permute-start.20) | collective-permute-done | bytes 524320 | tf_op jit(solution)/shard_map/ppermute | solution.py:27
  125.1 3.4 %copy-done.2 = bf16[2048,2048]{1,0:T(8,128)(2,1)S(1)} copy-done((bf16[2048,2048]{1,0:T(8,128)(2,1)S(1)}, bf16[2048,2048]{1,0:T(8,128)(2,1)}, u32[]{:S(2)}) %copy-start.2) | copy-done | bytes 8388632
  128.5 2.6 %shard_map.108 = (f32[64,2048]{1,0:T(8,128)S(1)}, bf16[64,2048]{1,0:T(8,128)(2,1)S(1)}) custom-call(s32[1]{0:T(128)} %bitcast.1.share, bf16[128,2048]{1,0:T(8,128)(2,1)S(1)} %collective-permute-done.20.refs_0_, bf16[2048,2048]{1,0:T(8,128)(2,1)S(1)} %copy-done.2), custom_call_target="tpu_custom_call" | custom-call | flops 1 | bytes 1 | tf_op jit(solution)/shard_map/pallas_call | solution.py:56
  131.7 3.3 %collective-permute-start.23 = (bf16[32,2048]{1,0:T(8,128)(2,1)S(1)}, bf16[32,2048]{1,0:T(8,128)(2,1)S(1)}, u32[]{:S(2)}, u32[]{:S(2)}) collective-permute-start(bf16[32,2048]{1,0:T(8,128)(2,1)S(1)} %add_convert_fusion.7), channel_id=1, source_target_pairs={{0,8},{4,12},{8,0},{12,4},{1,9},{5,13},{9,1},{13,5},{2,10},{6,14},... | collective-permute-start | bytes 393224 | tf_op jit(solution)/shard_map/ppermute | solution.py:20
  142.8 3.0 %collective-permute-done.21 = bf16[32,2048]{1,0:T(8,128)(2,1)S(1)} collective-permute-done((bf16[32,2048]{1,0:T(8,128)(2,1)S(1)}, bf16[32,2048]{1,0:T(8,128)(2,1)S(1)}, u32[]{:S(2)}, u32[]{:S(2)}) %collective-permute-start.21) | collective-permute-done | bytes 131104 | tf_op jit(solution)/shard_map/ppermute | solution.py:20
  145.9 2.6 %collective-permute-done.25 = bf16[32,2048]{1,0:T(8,128)(2,1)S(1)} collective-permute-done((bf16[32,2048]{1,0:T(8,128)(2,1)S(1)}, bf16[32,2048]{1,0:T(8,128)(2,1)S(1)}, u32[]{:S(2)}, u32[]{:S(2)}) %collective-permute-start.25) | collective-permute-done | bytes 131104 | tf_op jit(solution)/shard_map/ppermute | solution.py:20
  150.5 5.8 %collective-permute-done.28 = bf16[32,2048]{1,0:T(8,128)(2,1)S(1)} collective-permute-done((bf16[32,2048]{1,0:T(8,128)(2,1)S(1)}, bf16[32,2048]{1,0:T(8,128)(2,1)S(1)}, u32[]{:S(2)}, u32[]{:S(2)}) %collective-permute-start.28) | collective-permute-done | bytes 131104 | tf_op jit(solution)/shard_map/ppermute | solution.py:20
  (114 shorter events, 42.6 us)
Async XLA Ops:
  4.0 23.1 %collective-permute-start = (bf16[8,32,512]{2,1,0:T(8,128)(2,1)}, bf16[8,32,512]{2,1,0:T(8,128)(2,1)S(1)}, u32[]{:S(2)}, u32[]{:S(2)}) collective-permute-start(bf16[8,32,512]{2,1,0:T(8,128)(2,1)} %get-tuple-element.64), channel_id=1, source_target_pairs={{0,8},{4,12},{8,0},{12,4},{1,9},{5,13},{9,1},{13,5},{2,10},{6,14},... | collective-permute-start | bytes 786440 | tf_op jit(solution)/shard_map/ppermute | solution.py:20
  8.5 18.6 %collective-permute-start.1 = (bf16[8,32,512]{2,1,0:T(8,128)(2,1)}, bf16[8,32,512]{2,1,0:T(8,128)(2,1)S(1)}, u32[]{:S(2)}, u32[]{:S(2)}) collective-permute-start(bf16[8,32,512]{2,1,0:T(8,128)(2,1)} %get-tuple-element.65), channel_id=1, source_target_pairs={{0,12},{4,8},{8,4},{12,0},{1,13},{5,9},{9,5},{13,1},{2,14},{6,10},... | collective-permute-start | bytes 786440 | tf_op jit(solution)/shard_map/ppermute | solution.py:20
  9.9 17.7 %collective-permute-start.2 = (bf16[8,32,512]{2,1,0:T(8,128)(2,1)}, bf16[8,32,512]{2,1,0:T(8,128)(2,1)S(1)}, u32[]{:S(2)}, u32[]{:S(2)}) collective-permute-start(bf16[8,32,512]{2,1,0:T(8,128)(2,1)} %get-tuple-element.66), channel_id=1, source_target_pairs={{0,4},{4,0},{8,12},{12,8},{1,5},{5,1},{9,13},{13,9},{2,6},{6,2},{1... | collective-permute-start | bytes 786440 | tf_op jit(solution)/shard_map/ppermute | solution.py:20
  28.6 11.9 %collective-permute-start.4 = (bf16[2,256,512]{2,1,0:T(8,128)(2,1)S(1)}, bf16[2,256,512]{2,1,0:T(8,128)(2,1)S(1)}, u32[]{:S(2)}, u32[]{:S(2)}) collective-permute-start(bf16[2,256,512]{2,1,0:T(8,128)(2,1)S(1)} %bitcast.14), channel_id=1, source_target_pairs={{0,2},{2,0},{1,3},{3,1},{4,6},{6,4},{5,7},{7,5},{8,10},{10,8},{9,1... | collective-permute-start | bytes 1572872 | tf_op jit(solution)/shard_map/ppermute | solution.py:20
  30.2 10.3 %collective-permute-start.3 = (bf16[2,256,512]{2,1,0:T(8,128)(2,1)S(1)}, bf16[2,256,512]{2,1,0:T(8,128)(2,1)S(1)}, u32[]{:S(2)}, u32[]{:S(2)}) collective-permute-start(bf16[2,256,512]{2,1,0:T(8,128)(2,1)S(1)} %bitcast.15), channel_id=1, source_target_pairs={{0,1},{1,0},{2,3},{3,2},{4,5},{5,4},{6,7},{7,6},{8,9},{9,8},{10,11... | collective-permute-start | bytes 1572872 | tf_op jit(solution)/shard_map/ppermute | solution.py:20
  48.5 25.6 %collective-permute-start.8 = (bf16[128,2048]{1,0:T(8,128)(2,1)S(1)}, bf16[128,2048]{1,0:T(8,128)(2,1)S(1)}, u32[]{:S(2)}, u32[]{:S(2)}) collective-permute-start(bf16[128,2048]{1,0:T(8,128)(2,1)S(1)} %shard_map.103.refs_0_), channel_id=1, source_target_pairs={{0,12},{4,8},{8,4},{12,0},{1,13},{5,9},{9,5},{13,1},{2,14},{6,10},... | collective-permute-start | bytes 1572872 | tf_op jit(solution)/shard_map/ppermute | solution.py:20
  52.9 24.1 %collective-permute-start.9 = (bf16[128,2048]{1,0:T(8,128)(2,1)S(1)}, bf16[128,2048]{1,0:T(8,128)(2,1)S(1)}, u32[]{:S(2)}, u32[]{:S(2)}) collective-permute-start(bf16[128,2048]{1,0:T(8,128)(2,1)S(1)} %shard_map.103.refs_0_), channel_id=1, source_target_pairs={{0,4},{4,0},{8,12},{12,8},{1,5},{5,1},{9,13},{13,9},{2,6},{6,2},{1... | collective-permute-start | bytes 1572872 | tf_op jit(solution)/shard_map/ppermute | solution.py:20
  64.3 23.8 %collective-permute-start.6 = (bf16[128,2048]{1,0:T(8,128)(2,1)S(1)}, bf16[128,2048]{1,0:T(8,128)(2,1)S(1)}, u32[]{:S(2)}, u32[]{:S(2)}) collective-permute-start(bf16[128,2048]{1,0:T(8,128)(2,1)S(1)} %shard_map.102.refs_1_), channel_id=1, source_target_pairs={{0,12},{4,8},{8,4},{12,0},{1,13},{5,9},{9,5},{13,1},{2,14},{6,10},... | collective-permute-start | bytes 1572872 | tf_op jit(solution)/shard_map/ppermute | solution.py:20
  65.3 36.1 %collective-permute-start.7 = (bf16[128,2048]{1,0:T(8,128)(2,1)S(1)}, bf16[128,2048]{1,0:T(8,128)(2,1)S(1)}, u32[]{:S(2)}, u32[]{:S(2)}) collective-permute-start(bf16[128,2048]{1,0:T(8,128)(2,1)S(1)} %shard_map.102.refs_1_), channel_id=1, source_target_pairs={{0,4},{4,0},{8,12},{12,8},{1,5},{5,1},{9,13},{13,9},{2,6},{6,2},{1... | collective-permute-start | bytes 1572872 | tf_op jit(solution)/shard_map/ppermute | solution.py:20
  84.0 17.5 %collective-permute-start.10 = (bf16[64,2048]{1,0:T(8,128)(2,1)S(1)}, bf16[64,2048]{1,0:T(8,128)(2,1)S(1)}, u32[]{:S(2)}, u32[]{:S(2)}) collective-permute-start(bf16[64,2048]{1,0:T(8,128)(2,1)S(1)} %get-tuple-element.76), channel_id=1, source_target_pairs={{0,1},{1,0},{2,3},{3,2},{4,5},{5,4},{6,7},{7,6},{8,9},{9,8},{10,11... | collective-permute-start | bytes 786440 | tf_op jit(solution)/shard_map/ppermute | solution.py:20
  84.0 17.4 %collective-permute-start.11 = (bf16[64,2048]{1,0:T(8,128)(2,1)S(1)}, bf16[64,2048]{1,0:T(8,128)(2,1)S(1)}, u32[]{:S(2)}, u32[]{:S(2)}) collective-permute-start(bf16[64,2048]{1,0:T(8,128)(2,1)S(1)} %get-tuple-element.77), channel_id=1, source_target_pairs={{0,2},{1,3},{2,0},{3,1},{4,6},{5,7},{6,4},{7,5},{8,10},{9,11},{10,... | collective-permute-start | bytes 786440 | tf_op jit(solution)/shard_map/ppermute | solution.py:20
  85.6 15.8 %collective-permute-start.12 = (bf16[64,2048]{1,0:T(8,128)(2,1)S(1)}, bf16[64,2048]{1,0:T(8,128)(2,1)S(1)}, u32[]{:S(2)}, u32[]{:S(2)}) collective-permute-start(bf16[64,2048]{1,0:T(8,128)(2,1)S(1)} %get-tuple-element.78), channel_id=1, source_target_pairs={{0,3},{1,2},{2,1},{3,0},{4,7},{5,6},{6,5},{7,4},{8,11},{9,10},{10,... | collective-permute-start | bytes 786440 | tf_op jit(solution)/shard_map/ppermute | solution.py:20
  88.1 25.6 %collective-permute-start.15 = (bf16[128,2048]{1,0:T(8,128)(2,1)S(1)}, bf16[128,2048]{1,0:T(8,128)(2,1)S(1)}, u32[]{:S(2)}, u32[]{:S(2)}) collective-permute-start(bf16[128,2048]{1,0:T(8,128)(2,1)S(1)} %broadcast_select_fusion.1), channel_id=1, source_target_pairs={{0,8},{12,4},{4,0},{8,12},{1,9},{13,5},{5,1},{9,13},{2,10},{14,6},... | collective-permute-start | bytes 1572872 | tf_op jit(solution)/shard_map/ppermute | solution.py:27
  102.4 22.7 %collective-permute-start.20 = (bf16[128,2048]{1,0:T(8,128)(2,1)}, bf16[128,2048]{1,0:T(8,128)(2,1)S(1)}, u32[]{:S(2)}, u32[]{:S(2)}) collective-permute-start(bf16[128,2048]{1,0:T(8,128)(2,1)} %broadcast_select_fusion), channel_id=1, source_target_pairs={{0,8},{12,4},{4,0},{8,12},{1,9},{13,5},{5,1},{9,13},{2,10},{14,6},... | collective-permute-start | bytes 1572872 | tf_op jit(solution)/shard_map/ppermute | solution.py:27
  108.0 23.1 %collective-permute-start.13 = (bf16[32,2048]{1,0:T(8,128)(2,1)}, bf16[32,2048]{1,0:T(8,128)(2,1)}, u32[]{:S(2)}, u32[]{:S(2)}) collective-permute-start(bf16[32,2048]{1,0:T(8,128)(2,1)} %get-tuple-element.122), channel_id=1, source_target_pairs={{0,4},{4,0},{8,12},{12,8},{1,5},{5,1},{9,13},{13,9},{2,6},{6,2},{1... | collective-permute-start | bytes 393224 | tf_op jit(solution)/shard_map/ppermute | solution.py:20
  110.0 21.1 %collective-permute-start.14 = (bf16[32,2048]{1,0:T(8,128)(2,1)}, bf16[32,2048]{1,0:T(8,128)(2,1)}, u32[]{:S(2)}, u32[]{:S(2)}) collective-permute-start(bf16[32,2048]{1,0:T(8,128)(2,1)} %get-tuple-element.121), channel_id=1, source_target_pairs={{0,12},{4,8},{8,4},{12,0},{1,13},{5,9},{9,5},{13,1},{2,14},{6,10},... | collective-permute-start | bytes 393224 | tf_op jit(solution)/shard_map/ppermute | solution.py:20
  117.2 13.9 %collective-permute-start.17 = (bf16[64,2048]{1,0:T(8,128)(2,1)}, bf16[64,2048]{1,0:T(8,128)(2,1)S(1)}, u32[]{:S(2)}, u32[]{:S(2)}) collective-permute-start(bf16[64,2048]{1,0:T(8,128)(2,1)} %add_convert_fusion.3), channel_id=1, source_target_pairs={{0,2},{2,0},{1,3},{3,1},{4,6},{6,4},{5,7},{7,5},{8,10},{10,8},{9,1... | collective-permute-start | bytes 786440 | tf_op jit(solution)/shard_map/ppermute | solution.py:20
  120.1 11.0 %collective-permute-start.19 = (bf16[32,2048]{1,0:T(8,128)(2,1)}, bf16[32,2048]{1,0:T(8,128)(2,1)S(1)}, u32[]{:S(2)}, u32[]{:S(2)}) collective-permute-start(bf16[32,2048]{1,0:T(8,128)(2,1)} %add_convert_fusion.8), channel_id=1, source_target_pairs={{0,2},{2,0},{1,3},{3,1},{4,6},{6,4},{5,7},{7,5},{8,10},{10,8},{9,1... | collective-permute-start | bytes 393224 | tf_op jit(solution)/shard_map/ppermute | solution.py:20
  131.2 8.3 %collective-permute-start.24 = (bf16[64,2048]{1,0:T(8,128)(2,1)S(1)}, bf16[64,2048]{1,0:T(8,128)(2,1)S(1)}, u32[]{:S(2)}, u32[]{:S(2)}) collective-permute-start(bf16[64,2048]{1,0:T(8,128)(2,1)S(1)} %get-tuple-element.107), channel_id=1, source_target_pairs={{0,1},{1,0},{2,3},{3,2},{4,5},{5,4},{6,7},{7,6},{8,9},{9,8},{10,11... | collective-permute-start | bytes 786440 | tf_op jit(solution)/shard_map/ppermute | solution.py:20
  131.7 11.1 %collective-permute-start.23 = (bf16[32,2048]{1,0:T(8,128)(2,1)S(1)}, bf16[32,2048]{1,0:T(8,128)(2,1)S(1)}, u32[]{:S(2)}, u32[]{:S(2)}) collective-permute-start(bf16[32,2048]{1,0:T(8,128)(2,1)S(1)} %add_convert_fusion.7), channel_id=1, source_target_pairs={{0,8},{4,12},{8,0},{12,4},{1,9},{5,13},{9,1},{13,5},{2,10},{6,14},... | collective-permute-start | bytes 393224 | tf_op jit(solution)/shard_map/ppermute | solution.py:20
  135.2 10.6 %collective-permute-start.21 = (bf16[32,2048]{1,0:T(8,128)(2,1)S(1)}, bf16[32,2048]{1,0:T(8,128)(2,1)S(1)}, u32[]{:S(2)}, u32[]{:S(2)}) collective-permute-start(bf16[32,2048]{1,0:T(8,128)(2,1)S(1)} %get-tuple-element.120), channel_id=1, source_target_pairs={{0,4},{4,0},{8,12},{12,8},{1,5},{5,1},{9,13},{13,9},{2,6},{6,2},{1... | collective-permute-start | bytes 393224 | tf_op jit(solution)/shard_map/ppermute | solution.py:20
  135.6 10.3 %collective-permute-start.22 = (bf16[32,2048]{1,0:T(8,128)(2,1)S(1)}, bf16[32,2048]{1,0:T(8,128)(2,1)S(1)}, u32[]{:S(2)}, u32[]{:S(2)}) collective-permute-start(bf16[32,2048]{1,0:T(8,128)(2,1)S(1)} %get-tuple-element.119), channel_id=1, source_target_pairs={{0,12},{4,8},{8,4},{12,0},{1,13},{5,9},{9,5},{13,1},{2,14},{6,10},... | collective-permute-start | bytes 393224 | tf_op jit(solution)/shard_map/ppermute | solution.py:20
  137.8 10.6 %collective-permute-start.27 = (bf16[64,2048]{1,0:T(8,128)(2,1)S(1)}, bf16[64,2048]{1,0:T(8,128)(2,1)S(1)}, u32[]{:S(2)}, u32[]{:S(2)}) collective-permute-start(bf16[64,2048]{1,0:T(8,128)(2,1)S(1)} %add_convert_fusion.1), channel_id=1, source_target_pairs={{0,2},{2,0},{1,3},{3,1},{4,6},{6,4},{5,7},{7,5},{8,10},{10,8},{9,1... | collective-permute-start | bytes 786440 | tf_op jit(solution)/shard_map/ppermute | solution.py:20
  139.5 9.0 %collective-permute-start.25 = (bf16[32,2048]{1,0:T(8,128)(2,1)S(1)}, bf16[32,2048]{1,0:T(8,128)(2,1)S(1)}, u32[]{:S(2)}, u32[]{:S(2)}) collective-permute-start(bf16[32,2048]{1,0:T(8,128)(2,1)S(1)} %add_convert_fusion.6), channel_id=1, source_target_pairs={{0,2},{2,0},{1,3},{3,1},{4,6},{6,4},{5,7},{7,5},{8,10},{10,8},{9,1... | collective-permute-start | bytes 393224 | tf_op jit(solution)/shard_map/ppermute | solution.py:20
  (24 other events, 190.6 us)

commit v18 on v17

--- a/solution.py
+++ b/solution.py
@@ -189,75 +189,78 @@
     )(where, *[pieces[flip] for flip in order])
 
 
-def attend_kernel(share_count, scalars, queries, *refs):
+def attend_kernel(start, rows, share_count, scalars, queries, *refs):
     parts, (kv_up, gains, out, keys, values) = refs[:share_count], refs[share_count:]
-    request = pl.program_id(0)
     q_gain, k_gain = gains[0:1, :], gains[1:2, :]
+    requests, request_shares, _, width = queries.shape
+    heads_here = kv_up.shape[0]
     head_width = gains.shape[1]
-    text, width = out.shape
-    per_group = width // head_width
+    text = request_shares * rows
+    per_group = width // heads_here // head_width
     part_slots = parts[0].shape[1]
     share_rows = BLK // share_count
-    share, count = scalars[0], scalars[1 + request]
+    share = scalars[0]
     slot = lax.broadcasted_iota(jnp.int32, (part_slots, head_width), 0)
     position = (slot // share_rows) * BLK + slot % share_rows
-    for flip in range(share_count):
-        rows = pl.ds(flip * part_slots, part_slots)
-        projected = jnp.dot(parts[flip][request], kv_up[...], preferred_element_type=jnp.float32)
-        key = rms_scale(projected[:, :head_width], k_gain)
-        keys[rows, :] = key.astype(jnp.bfloat16)
-        live = jnp.where(position < count - (share ^ flip) * share_rows, 1.0, 0.0)
-        values[rows, :head_width] = (projected[:, head_width:] * live).astype(jnp.bfloat16)
-        values[rows, head_width:] = live.astype(jnp.bfloat16)
     scale = math.log2(math.e) / math.sqrt(head_width)
     together = min(per_group, max(1, 256 // text))
-    for first in range(0, per_group, together):
-        normed = []
-        for head in range(first, first + together):
-            query = queries[0, :, :, head * head_width : (head + 1) * head_width]
-            query = query.reshape(text, head_width).astype(jnp.float32)
-            normed.append(rms_scale(query, q_gain).astype(jnp.bfloat16))
-        scores = lax.dot_general(
-            jnp.concatenate(normed, axis=0),
-            keys[...],
-            (((1,), (1,)), ((), ())),
-            preferred_element_type=jnp.float32,
-        )
-        expo = jnp.exp2(scores * scale).astype(jnp.bfloat16)
-        total = jnp.dot(expo, values[...], preferred_element_type=jnp.float32)
-        result = (total[:, :head_width] / total[:, head_width:]).astype(jnp.bfloat16)
-        for i in range(together):
-            head = first + i
-            columns = slice(head * head_width, (head + 1) * head_width)
-            out[:, columns] = result[i * text : (i + 1) * text]
-
-
-def attend(chunk, rows, queries, parts, kv_flat, gains, scalars):
+    for request in range(requests):
+        count = scalars[1 + request]
+        for flip in range(share_count):
+            run = pl.ds(flip * part_slots, part_slots)
+            live = jnp.where(position < count - (share ^ flip) * share_rows, 1.0, 0.0)
+            for group in range(heads_here):
+                pair = request * heads_here + group
+                projected = jnp.dot(
+                    parts[flip][request], kv_up[group], preferred_element_type=jnp.float32
+                )
+                key = rms_scale(projected[:, :head_width], k_gain)
+                keys[pair, run, :] = key.astype(jnp.bfloat16)
+                value = projected[:, head_width:] * live
+                values[pair, run, :head_width] = value.astype(jnp.bfloat16)
+                values[pair, run, head_width:] = live.astype(jnp.bfloat16)
+        for group in range(heads_here):
+            pair = request * heads_here + group
+            for first in range(group * per_group, (group + 1) * per_group, together):
+                normed = []
+                for head in range(first, first + together):
+                    columns = slice(head * head_width, (head + 1) * head_width)
+                    query = queries[request, :, start : start + rows, columns]
+                    query = query.reshape(text, head_width).astype(jnp.float32)
+                    normed.append(rms_scale(query, q_gain).astype(jnp.bfloat16))
+                scores = lax.dot_general(
+                    jnp.concatenate(normed, axis=0),
+                    keys[pair],
+                    (((1,), (1,)), ((), ())),
+                    preferred_element_type=jnp.float32,
+                )
+                expo = jnp.exp2(scores * scale).astype(jnp.bfloat16)
+                total = jnp.dot(expo, values[pair], preferred_element_type=jnp.float32)
+                result = (total[:, :head_width] / total[:, head_width:]).astype(jnp.bfloat16)
+                for i in range(together):
+                    head = first + i
+                    columns = slice(head * head_width, (head + 1) * head_width)
+                    out[request * text : (request + 1) * text, columns] = result[
+                        i * text : (i + 1) * text
+                    ]
+
+
+def attend(start, rows, queries, parts, kv_flat, gains, scalars):
     requests, request_shares, _, width = queries.shape
-    heads_here, rank_width, pair_width = kv_flat.shape
+    heads_here = kv_flat.shape[0]
     head_width = gains.shape[1]
     slots = len(parts) * parts[0].shape[1]
-    text = request_shares * rows
     whole = pl.BlockSpec(memory_space=pltpu.VMEM)
     return pl.pallas_call(
-        functools.partial(attend_kernel, len(parts)),
-        grid=(requests, heads_here),
-        in_specs=[
-            pl.BlockSpec(memory_space=pltpu.SMEM),
-            pl.BlockSpec(
-                (1, request_shares, rows, width // heads_here),
-                lambda r, g: (r, 0, chunk, g),
-            ),
-        ]
-        + [whole for _ in parts]
-        + [pl.BlockSpec((None, rank_width, pair_width), lambda r, g: (g, 0, 0)), whole],
-        out_specs=pl.BlockSpec((text, width // heads_here), lambda r, g: (r, g)),
-        out_shape=jax.ShapeDtypeStruct((requests * text, width), jnp.bfloat16),
+        functools.partial(attend_kernel, start, rows, len(parts)),
+        in_specs=[pl.BlockSpec(memory_space=pltpu.SMEM)] + [whole] * (len(parts) + 3),
+        out_specs=whole,
+        out_shape=jax.ShapeDtypeStruct((requests * request_shares * rows, width), jnp.bfloat16),
         scratch_shapes=[
-            pltpu.VMEM((slots, head_width), jnp.bfloat16),
-            pltpu.VMEM((slots, 2 * head_width), jnp.bfloat16),
+            pltpu.VMEM((requests * heads_here, slots, head_width), jnp.bfloat16),
+            pltpu.VMEM((requests * heads_here, slots, 2 * head_width), jnp.bfloat16),
         ],
-        compiler_params=pltpu.CompilerParams(vmem_limit_bytes=12 * 1024 * 1024),
+        compiler_params=pltpu.CompilerParams(vmem_limit_bytes=20 * 1024 * 1024),
         cost_estimate=LIGHT,
     )(scalars, queries, *parts, kv_flat, gains)
 
@@ -317,7 +320,7 @@
 
     def attended(chunk):
         rows = chunk_rows[chunk]
-        start = sum(chunk_rows[:chunk]) // rows
+        start = sum(chunk_rows[:chunk])
         return attend(start, rows, shaped, parts, kv_flat, gains, scalars)
 
     columns = out_weight.shape[1]

time: 157 us -> 156 us (level)
  Pallas kernels: 32.5 us -> 29.6 us
  waiting for transfers between devices: 48 us -> 49.8 us
    pallas_call x2, Pallas kernels: 12.3 us -> 8.82 us  [attend(): pl.pallas_call(functools.partial(attend_kernel, start, rows, len(parts)),...]
    ppermute x27, waiting for transfers between devices: 40.9 us -> 42.6 us  [swap(): lax.ppermute(values, axis, [(i, i ^ flip) for i in range(lax.axis_size(ax...]
  transfers between devices with their start and end apart: 29 -> 29, of which waited for: 12 -> 12; matrix products, arithmetic and copies ran while one was open for 8% -> 8% of each run, Pallas kernels for 14% -> 13%
where the time goes in v18:
time: 156 us; the launch traced here: 155 us
  waiting for transfers between devices  49.8 us (32%)
  starting transfers between devices  47.2 us (30%)
  Pallas kernels  29.6 us (19%)
  local copies, waits for them, and re-layouts  21.9 us (14%)
  other arithmetic  5.95 us (4%)
    ppermute x27, waiting for transfers between devices, swap(): lax.ppermute(values, axis, [(i, i ^ flip) for i in range(lax.axis_size(ax...  42.6 us
    ppermute x27, starting transfers between devices, swap(): lax.ppermute(values, axis, [(i, i ^ flip) for i in range(lax.axis_size(ax...  33.9 us
    pallas_call x5, Pallas kernels, project_out(): pl.pallas_call(functools.partial(project_kernel, len(blocks), list(range(...  15.9 us
    unnamed x38, local copies, waits for them, and re-layouts  13.7 us
    ppermute x2, starting transfers between devices, second_hop(): return lax.ppermute(passed, 'pool', [(0, 2), (3, 1), (1, 0), (2, 3)])  13.3 us
    pallas_call x2, Pallas kernels, attend(): pl.pallas_call(functools.partial(attend_kernel, start, rows, len(parts)),...  8.82 us
    ppermute x2, waiting for transfers between devices, second_hop(): return lax.ppermute(passed, 'pool', [(0, 2), (3, 1), (1, 0), (2, 3)])  7.22 us
    pallas_call x1, Pallas kernels, fetch(): pl.pallas_call(functools.partial(fetch_kernel, pool_size=pool_size, share...  3.74 us
  transfers between devices with their start and end apart: 29, of which 12 were waited for; matrix products, arithmetic and copies ran while one was open for 8% of the time, Pallas kernels for 13%

profile of v18, /device:TPU:0, one launch (start us, length us, event | category | flops | bytes accessed | tf_op | source)
XLA Modules:
  0.0 154.9 jit_solution(12251593544462167703)
XLA Ops:
  0.7 3.7 %shard_map.100 = (s32[2,16]{1,0:T(2,128)}, bf16[8,32,512]{2,1,0:T(8,128)(2,1)}, bf16[8,32,512]{2,1,0:T(8,128)(2,1)}, bf16[8,32,512]{2,1,0:T(8,128)(2,1)}, bf16[8,32,512]{2,1,0:T(8,128)(2,1)}) custom-call(s32[2]{0:T(128)} %pad_add_fusion.1.place, s32[8,8]{1,0:T(8,128)} %holder.1, s32[8,8]{1,0:T(8,128)} %block.1, s32[8]{0:T(128)} %serving.1, ...), custom_call_target="tpu_custom_call" | custom-call | flops 1 | bytes 1 | tf_op jit(solution)/shard_map/pallas_call | solution.py:153
  4.4 4.1 %collective-permute-start = (bf16[8,32,512]{2,1,0:T(8,128)(2,1)}, bf16[8,32,512]{2,1,0:T(8,128)(2,1)S(1)}, u32[]{:S(2)}, u32[]{:S(2)}) collective-permute-start(bf16[8,32,512]{2,1,0:T(8,128)(2,1)} %get-tuple-element.64), channel_id=1, source_target_pairs={{0,8},{4,12},{8,0},{12,4},{1,9},{5,13},{9,1},{13,5},{2,10},{6,14},... | collective-permute-start | bytes 786440 | tf_op jit(solution)/shard_map/ppermute | solution.py:20
  17.2 9.9 %collective-permute-done.refs_1_ = bf16[8,32,512]{2,1,0:T(8,128)(2,1)S(1)} collective-permute-done((bf16[8,32,512]{2,1,0:T(8,128)(2,1)}, bf16[8,32,512]{2,1,0:T(8,128)(2,1)S(1)}, u32[]{:S(2)}, u32[]{:S(2)}) %collective-permute-start) | collective-permute-done | bytes 262176 | tf_op jit(solution)/shard_map/ppermute | solution.py:20
  30.4 10.2 %collective-permute-done.4.refs_2_ = bf16[2,256,512]{2,1,0:T(8,128)(2,1)S(1)} collective-permute-done((bf16[2,256,512]{2,1,0:T(8,128)(2,1)S(1)}, bf16[2,256,512]{2,1,0:T(8,128)(2,1)S(1)}, u32[]{:S(2)}, u32[]{:S(2)}) %collective-permute-start.4) | collective-permute-done | bytes 524320 | tf_op jit(solution)/shard_map/ppermute | solution.py:20
  42.5 4.4 %shard_map.103.refs_0_ = bf16[128,2048]{1,0:T(8,128)(2,1)S(1)} custom-call(s32[3]{0:T(128)S(1)} %pad_add_fusion.2.scalars, bf16[2,2,64,2048]{3,2,1,0:T(8,128)(2,1)S(1)} %bitcast.18, bf16[2,256,512]{2,1,0:T(8,128)(2,1)S(1)} %bitcast.16, bf16[2,256,512]{2,1,0:T(8,128)(2,1)S(1)} %collective-permute-done.3.refs_1_, ...), custom_call_target="tpu_custom_call" | custom-call | flops 1 | bytes 1 | tf_op jit(solution)/shard_map/pallas_call | solution.py:254
  46.9 3.9 %collective-permute-start.8 = (bf16[128,2048]{1,0:T(8,128)(2,1)S(1)}, bf16[128,2048]{1,0:T(8,128)(2,1)S(1)}, u32[]{:S(2)}, u32[]{:S(2)}) collective-permute-start(bf16[128,2048]{1,0:T(8,128)(2,1)S(1)} %shard_map.103.refs_0_), channel_id=1, source_target_pairs={{0,12},{4,8},{8,4},{12,0},{1,13},{5,9},{9,5},{13,1},{2,14},{6,10},... | collective-permute-start | bytes 1572872 | tf_op jit(solution)/shard_map/ppermute | solution.py:20
  50.8 5.3 %collective-permute-start.9 = (bf16[128,2048]{1,0:T(8,128)(2,1)S(1)}, bf16[128,2048]{1,0:T(8,128)(2,1)S(1)}, u32[]{:S(2)}, u32[]{:S(2)}) collective-permute-start(bf16[128,2048]{1,0:T(8,128)(2,1)S(1)} %shard_map.103.refs_0_), channel_id=1, source_target_pairs={{0,4},{4,0},{8,12},{12,8},{1,5},{5,1},{9,13},{13,9},{2,6},{6,2},{1... | collective-permute-start | bytes 1572872 | tf_op jit(solution)/shard_map/ppermute | solution.py:20
  56.1 4.4 %shard_map.102.refs_1_ = bf16[128,2048]{1,0:T(8,128)(2,1)S(1)} custom-call(s32[3]{0:T(128)S(1)} %pad_add_fusion.2.scalars, bf16[2,2,64,2048]{3,2,1,0:T(8,128)(2,1)S(1)} %bitcast.19, bf16[2,256,512]{2,1,0:T(8,128)(2,1)S(1)} %bitcast.17, bf16[2,256,512]{2,1,0:T(8,128)(2,1)S(1)} %collective-permute-done.3.refs_1_, ...), custom_call_target="tpu_custom_call" | custom-call | flops 1 | bytes 1 | tf_op jit(solution)/shard_map/pallas_call | solution.py:254
  61.5 3.4 %copy-done = bf16[2048,2048]{1,0:T(8,128)(2,1)S(1)} copy-done((bf16[2048,2048]{1,0:T(8,128)(2,1)S(1)}, bf16[2048,2048]{1,0:T(8,128)(2,1)}, u32[]{:S(2)}) %copy-start) | copy-done | bytes 8388632
  64.9 3.6 %shard_map.104 = (f32[128,2048]{1,0:T(8,128)S(1)}, bf16[128,2048]{1,0:T(8,128)(2,1)S(1)}) custom-call(s32[1]{0:T(128)} %bitcast.1.share, bf16[128,2048]{1,0:T(8,128)(2,1)S(1)} %shard_map.103.refs_0_, bf16[128,2048]{1,0:T(8,128)(2,1)S(1)} %shard_map.102.refs_1_, bf16[2048,2048]{1,0:T(8,128)(2,1)S(1)} %copy-done), custom_call_target="tpu_custom_call" | custom-call | flops 1 | bytes 1 | tf_op jit(solution)/shard_map/pallas_call | solution.py:56
  70.3 4.6 %collective-permute-done.9.refs_0_ = bf16[128,2048]{1,0:T(8,128)(2,1)S(1)} collective-permute-done((bf16[128,2048]{1,0:T(8,128)(2,1)S(1)}, bf16[128,2048]{1,0:T(8,128)(2,1)S(1)}, u32[]{:S(2)}, u32[]{:S(2)}) %collective-permute-start.9) | collective-permute-done | bytes 524320 | tf_op jit(solution)/shard_map/ppermute | solution.py:20
  74.9 3.4 %copy-done.1 = bf16[2048,2048]{1,0:T(8,128)(2,1)S(1)} copy-done((bf16[2048,2048]{1,0:T(8,128)(2,1)S(1)}, bf16[2048,2048]{1,0:T(8,128)(2,1)}, u32[]{:S(2)}) %copy-start.1) | copy-done | bytes 8388632
  78.3 3.6 %shard_map.105 = (f32[64,2048]{1,0:T(8,128)S(1)}, bf16[64,2048]{1,0:T(8,128)(2,1)S(1)}, bf16[64,2048]{1,0:T(8,128)(2,1)S(1)}, bf16[64,2048]{1,0:T(8,128)(2,1)S(1)}) custom-call(s32[1]{0:T(128)} %bitcast.1.share, bf16[128,2048]{1,0:T(8,128)(2,1)S(1)} %collective-permute-done.9.refs_0_, bf16[128,2048]{1,0:T(8,128)(2,1)S(1)} %collective-permute-done.8.refs_1_, ...), custom_call_target="tpu_custom_call" | custom-call | flops 1 | bytes 1 | tf_op jit(solution)/shard_map/pallas_call | solution.py:56
  86.1 13.3 %collective-permute-start.15 = (bf16[128,2048]{1,0:T(8,128)(2,1)S(1)}, bf16[128,2048]{1,0:T(8,128)(2,1)S(1)}, u32[]{:S(2)}, u32[]{:S(2)}) collective-permute-start(bf16[128,2048]{1,0:T(8,128)(2,1)S(1)} %broadcast_select_fusion.1), channel_id=1, source_target_pairs={{0,8},{12,4},{4,0},{8,12},{1,9},{13,5},{5,1},{9,13},{2,10},{14,6},... | collective-permute-start | bytes 1572872 | tf_op jit(solution)/shard_map/ppermute | solution.py:27
  101.4 3.6 %shard_map.106 = (f32[128,2048]{1,0:T(8,128)S(1)}, bf16[128,2048]{1,0:T(8,128)(2,1)S(1)}) custom-call(s32[1]{0:T(128)} %bitcast.1.share, bf16[128,2048]{1,0:T(8,128)(2,1)S(1)} %copy-done.7, bf16[128,2048]{1,0:T(8,128)(2,1)S(1)} %collective-permute-done.6.refs_1_, bf16[2048,2048]{1,0:T(8,128)(2,1)S(1)} %bitcast.11), custom_call_target="tpu_custom_call" | custom-call | flops 1 | bytes 1 | tf_op jit(solution)/shard_map/pallas_call | solution.py:56
  108.8 2.9 %collective-permute-done.15.refs_0_ = bf16[128,2048]{1,0:T(8,128)(2,1)S(1)} collective-permute-done((bf16[128,2048]{1,0:T(8,128)(2,1)S(1)}, bf16[128,2048]{1,0:T(8,128)(2,1)S(1)}, u32[]{:S(2)}, u32[]{:S(2)}) %collective-permute-start.15) | collective-permute-done | bytes 524320 | tf_op jit(solution)/shard_map/ppermute | solution.py:27
  111.7 2.5 %shard_map.107 = (f32[64,2048]{1,0:T(8,128)S(1)}, bf16[64,2048]{1,0:T(8,128)(2,1)S(1)}) custom-call(s32[1]{0:T(128)} %bitcast.1.share, bf16[128,2048]{1,0:T(8,128)(2,1)S(1)} %collective-permute-done.15.refs_0_, bf16[2048,2048]{1,0:T(8,128)(2,1)S(1)} %bitcast.11), custom_call_target="tpu_custom_call" | custom-call | flops 1 | bytes 1 | tf_op jit(solution)/shard_map/pallas_call | solution.py:56
  118.7 4.4 %collective-permute-done.20.refs_0_ = bf16[128,2048]{1,0:T(8,128)(2,1)S(1)} collective-permute-done((bf16[128,2048]{1,0:T(8,128)(2,1)}, bf16[128,2048]{1,0:T(8,128)(2,1)S(1)}, u32[]{:S(2)}, u32[]{:S(2)}) %collective-permute-start.20) | collective-permute-done | bytes 524320 | tf_op jit(solution)/shard_map/ppermute | solution.py:27
  123.0 3.4 %copy-done.2 = bf16[2048,2048]{1,0:T(8,128)(2,1)S(1)} copy-done((bf16[2048,2048]{1,0:T(8,128)(2,1)S(1)}, bf16[2048,2048]{1,0:T(8,128)(2,1)}, u32[]{:S(2)}) %copy-start.2) | copy-done | bytes 8388632
  126.4 2.6 %shard_map.108 = (f32[64,2048]{1,0:T(8,128)S(1)}, bf16[64,2048]{1,0:T(8,128)(2,1)S(1)}) custom-call(s32[1]{0:T(128)} %bitcast.1.share, bf16[128,2048]{1,0:T(8,128)(2,1)S(1)} %collective-permute-done.20.refs_0_, bf16[2048,2048]{1,0:T(8,128)(2,1)S(1)} %copy-done.2), custom_call_target="tpu_custom_call" | custom-call | flops 1 | bytes 1 | tf_op jit(solution)/shard_map/pallas_call | solution.py:56
  129.7 3.3 %collective-permute-start.23 = (bf16[32,2048]{1,0:T(8,128)(2,1)S(1)}, bf16[32,2048]{1,0:T(8,128)(2,1)S(1)}, u32[]{:S(2)}, u32[]{:S(2)}) collective-permute-start(bf16[32,2048]{1,0:T(8,128)(2,1)S(1)} %add_convert_fusion.7), channel_id=1, source_target_pairs={{0,8},{4,12},{8,0},{12,4},{1,9},{5,13},{9,1},{13,5},{2,10},{6,14},... | collective-permute-start | bytes 393224 | tf_op jit(solution)/shard_map/ppermute | solution.py:20
  140.8 3.0 %collective-permute-done.21 = bf16[32,2048]{1,0:T(8,128)(2,1)S(1)} collective-permute-done((bf16[32,2048]{1,0:T(8,128)(2,1)S(1)}, bf16[32,2048]{1,0:T(8,128)(2,1)S(1)}, u32[]{:S(2)}, u32[]{:S(2)}) %collective-permute-start.21) | collective-permute-done | bytes 131104 | tf_op jit(solution)/shard_map/ppermute | solution.py:20
  143.8 2.6 %collective-permute-done.25 = bf16[32,2048]{1,0:T(8,128)(2,1)S(1)} collective-permute-done((bf16[32,2048]{1,0:T(8,128)(2,1)S(1)}, bf16[32,2048]{1,0:T(8,128)(2,1)S(1)}, u32[]{:S(2)}, u32[]{:S(2)}) %collective-permute-start.25) | collective-permute-done | bytes 131104 | tf_op jit(solution)/shard_map/ppermute | solution.py:20
  148.4 5.8 %collective-permute-done.28 = bf16[32,2048]{1,0:T(8,128)(2,1)S(1)} collective-permute-done((bf16[32,2048]{1,0:T(8,128)(2,1)S(1)}, bf16[32,2048]{1,0:T(8,128)(2,1)S(1)}, u32[]{:S(2)}, u32[]{:S(2)}) %collective-permute-start.28) | collective-permute-done | bytes 131104 | tf_op jit(solution)/shard_map/ppermute | solution.py:20
  (114 shorter events, 42.7 us)
Async XLA Ops:
  4.4 22.7 %collective-permute-start = (bf16[8,32,512]{2,1,0:T(8,128)(2,1)}, bf16[8,32,512]{2,1,0:T(8,128)(2,1)S(1)}, u32[]{:S(2)}, u32[]{:S(2)}) collective-permute-start(bf16[8,32,512]{2,1,0:T(8,128)(2,1)} %get-tuple-element.64), channel_id=1, source_target_pairs={{0,8},{4,12},{8,0},{12,4},{1,9},{5,13},{9,1},{13,5},{2,10},{6,14},... | collective-permute-start | bytes 786440 | tf_op jit(solution)/shard_map/ppermute | solution.py:20
  8.5 18.6 %collective-permute-start.1 = (bf16[8,32,512]{2,1,0:T(8,128)(2,1)}, bf16[8,32,512]{2,1,0:T(8,128)(2,1)S(1)}, u32[]{:S(2)}, u32[]{:S(2)}) collective-permute-start(bf16[8,32,512]{2,1,0:T(8,128)(2,1)} %get-tuple-element.65), channel_id=1, source_target_pairs={{0,12},{4,8},{8,4},{12,0},{1,13},{5,9},{9,5},{13,1},{2,14},{6,10},... | collective-permute-start | bytes 786440 | tf_op jit(solution)/shard_map/ppermute | solution.py:20
  9.9 17.7 %collective-permute-start.2 = (bf16[8,32,512]{2,1,0:T(8,128)(2,1)}, bf16[8,32,512]{2,1,0:T(8,128)(2,1)S(1)}, u32[]{:S(2)}, u32[]{:S(2)}) collective-permute-start(bf16[8,32,512]{2,1,0:T(8,128)(2,1)} %get-tuple-element.66), channel_id=1, source_target_pairs={{0,4},{4,0},{8,12},{12,8},{1,5},{5,1},{9,13},{13,9},{2,6},{6,2},{1... | collective-permute-start | bytes 786440 | tf_op jit(solution)/shard_map/ppermute | solution.py:20
  28.7 11.9 %collective-permute-start.4 = (bf16[2,256,512]{2,1,0:T(8,128)(2,1)S(1)}, bf16[2,256,512]{2,1,0:T(8,128)(2,1)S(1)}, u32[]{:S(2)}, u32[]{:S(2)}) collective-permute-start(bf16[2,256,512]{2,1,0:T(8,128)(2,1)S(1)} %bitcast.14), channel_id=1, source_target_pairs={{0,2},{2,0},{1,3},{3,1},{4,6},{6,4},{5,7},{7,5},{8,10},{10,8},{9,1... | collective-permute-start | bytes 1572872 | tf_op jit(solution)/shard_map/ppermute | solution.py:20
  30.4 10.2 %collective-permute-start.3 = (bf16[2,256,512]{2,1,0:T(8,128)(2,1)S(1)}, bf16[2,256,512]{2,1,0:T(8,128)(2,1)S(1)}, u32[]{:S(2)}, u32[]{:S(2)}) collective-permute-start(bf16[2,256,512]{2,1,0:T(8,128)(2,1)S(1)} %bitcast.15), channel_id=1, source_target_pairs={{0,1},{1,0},{2,3},{3,2},{4,5},{5,4},{6,7},{7,6},{8,9},{9,8},{10,11... | collective-permute-start | bytes 1572872 | tf_op jit(solution)/shard_map/ppermute | solution.py:20
  46.9 23.4 %collective-permute-start.8 = (bf16[128,2048]{1,0:T(8,128)(2,1)S(1)}, bf16[128,2048]{1,0:T(8,128)(2,1)S(1)}, u32[]{:S(2)}, u32[]{:S(2)}) collective-permute-start(bf16[128,2048]{1,0:T(8,128)(2,1)S(1)} %shard_map.103.refs_0_), channel_id=1, source_target_pairs={{0,12},{4,8},{8,4},{12,0},{1,13},{5,9},{9,5},{13,1},{2,14},{6,10},... | collective-permute-start | bytes 1572872 | tf_op jit(solution)/shard_map/ppermute | solution.py:20
  50.8 24.1 %collective-permute-start.9 = (bf16[128,2048]{1,0:T(8,128)(2,1)S(1)}, bf16[128,2048]{1,0:T(8,128)(2,1)S(1)}, u32[]{:S(2)}, u32[]{:S(2)}) collective-permute-start(bf16[128,2048]{1,0:T(8,128)(2,1)S(1)} %shard_map.103.refs_0_), channel_id=1, source_target_pairs={{0,4},{4,0},{8,12},{12,8},{1,5},{5,1},{9,13},{13,9},{2,6},{6,2},{1... | collective-permute-start | bytes 1572872 | tf_op jit(solution)/shard_map/ppermute | solution.py:20
  60.5 25.6 %collective-permute-start.6 = (bf16[128,2048]{1,0:T(8,128)(2,1)S(1)}, bf16[128,2048]{1,0:T(8,128)(2,1)S(1)}, u32[]{:S(2)}, u32[]{:S(2)}) collective-permute-start(bf16[128,2048]{1,0:T(8,128)(2,1)S(1)} %shard_map.102.refs_1_), channel_id=1, source_target_pairs={{0,12},{4,8},{8,4},{12,0},{1,13},{5,9},{9,5},{13,1},{2,14},{6,10},... | collective-permute-start | bytes 1572872 | tf_op jit(solution)/shard_map/ppermute | solution.py:20
  61.5 37.8 %collective-permute-start.7 = (bf16[128,2048]{1,0:T(8,128)(2,1)S(1)}, bf16[128,2048]{1,0:T(8,128)(2,1)S(1)}, u32[]{:S(2)}, u32[]{:S(2)}) collective-permute-start(bf16[128,2048]{1,0:T(8,128)(2,1)S(1)} %shard_map.102.refs_1_), channel_id=1, source_target_pairs={{0,4},{4,0},{8,12},{12,8},{1,5},{5,1},{9,13},{13,9},{2,6},{6,2},{1... | collective-permute-start | bytes 1572872 | tf_op jit(solution)/shard_map/ppermute | solution.py:20
  81.9 17.5 %collective-permute-start.10 = (bf16[64,2048]{1,0:T(8,128)(2,1)S(1)}, bf16[64,2048]{1,0:T(8,128)(2,1)S(1)}, u32[]{:S(2)}, u32[]{:S(2)}) collective-permute-start(bf16[64,2048]{1,0:T(8,128)(2,1)S(1)} %get-tuple-element.76), channel_id=1, source_target_pairs={{0,1},{1,0},{2,3},{3,2},{4,5},{5,4},{6,7},{7,6},{8,9},{9,8},{10,11... | collective-permute-start | bytes 786440 | tf_op jit(solution)/shard_map/ppermute | solution.py:20
  82.0 17.4 %collective-permute-start.11 = (bf16[64,2048]{1,0:T(8,128)(2,1)S(1)}, bf16[64,2048]{1,0:T(8,128)(2,1)S(1)}, u32[]{:S(2)}, u32[]{:S(2)}) collective-permute-start(bf16[64,2048]{1,0:T(8,128)(2,1)S(1)} %get-tuple-element.77), channel_id=1, source_target_pairs={{0,2},{1,3},{2,0},{3,1},{4,6},{5,7},{6,4},{7,5},{8,10},{9,11},{10,... | collective-permute-start | bytes 786440 | tf_op jit(solution)/shard_map/ppermute | solution.py:20
  83.4 16.0 %collective-permute-start.12 = (bf16[64,2048]{1,0:T(8,128)(2,1)S(1)}, bf16[64,2048]{1,0:T(8,128)(2,1)S(1)}, u32[]{:S(2)}, u32[]{:S(2)}) collective-permute-start(bf16[64,2048]{1,0:T(8,128)(2,1)S(1)} %get-tuple-element.78), channel_id=1, source_target_pairs={{0,3},{1,2},{2,1},{3,0},{4,7},{5,6},{6,5},{7,4},{8,11},{9,10},{10,... | collective-permute-start | bytes 786440 | tf_op jit(solution)/shard_map/ppermute | solution.py:20
  86.1 25.6 %collective-permute-start.15 = (bf16[128,2048]{1,0:T(8,128)(2,1)S(1)}, bf16[128,2048]{1,0:T(8,128)(2,1)S(1)}, u32[]{:S(2)}, u32[]{:S(2)}) collective-permute-start(bf16[128,2048]{1,0:T(8,128)(2,1)S(1)} %broadcast_select_fusion.1), channel_id=1, source_target_pairs={{0,8},{12,4},{4,0},{8,12},{1,9},{13,5},{5,1},{9,13},{2,10},{14,6},... | collective-permute-start | bytes 1572872 | tf_op jit(solution)/shard_map/ppermute | solution.py:27
  100.3 22.7 %collective-permute-start.20 = (bf16[128,2048]{1,0:T(8,128)(2,1)}, bf16[128,2048]{1,0:T(8,128)(2,1)S(1)}, u32[]{:S(2)}, u32[]{:S(2)}) collective-permute-start(bf16[128,2048]{1,0:T(8,128)(2,1)} %broadcast_select_fusion), channel_id=1, source_target_pairs={{0,8},{12,4},{4,0},{8,12},{1,9},{13,5},{5,1},{9,13},{2,10},{14,6},... | collective-permute-start | bytes 1572872 | tf_op jit(solution)/shard_map/ppermute | solution.py:27
  105.9 23.1 %collective-permute-start.13 = (bf16[32,2048]{1,0:T(8,128)(2,1)}, bf16[32,2048]{1,0:T(8,128)(2,1)}, u32[]{:S(2)}, u32[]{:S(2)}) collective-permute-start(bf16[32,2048]{1,0:T(8,128)(2,1)} %get-tuple-element.122), channel_id=1, source_target_pairs={{0,4},{4,0},{8,12},{12,8},{1,5},{5,1},{9,13},{13,9},{2,6},{6,2},{1... | collective-permute-start | bytes 393224 | tf_op jit(solution)/shard_map/ppermute | solution.py:20
  107.9 21.1 %collective-permute-start.14 = (bf16[32,2048]{1,0:T(8,128)(2,1)}, bf16[32,2048]{1,0:T(8,128)(2,1)}, u32[]{:S(2)}, u32[]{:S(2)}) collective-permute-start(bf16[32,2048]{1,0:T(8,128)(2,1)} %get-tuple-element.121), channel_id=1, source_target_pairs={{0,12},{4,8},{8,4},{12,0},{1,13},{5,9},{9,5},{13,1},{2,14},{6,10},... | collective-permute-start | bytes 393224 | tf_op jit(solution)/shard_map/ppermute | solution.py:20
  115.1 13.9 %collective-permute-start.17 = (bf16[64,2048]{1,0:T(8,128)(2,1)}, bf16[64,2048]{1,0:T(8,128)(2,1)S(1)}, u32[]{:S(2)}, u32[]{:S(2)}) collective-permute-start(bf16[64,2048]{1,0:T(8,128)(2,1)} %add_convert_fusion.3), channel_id=1, source_target_pairs={{0,2},{2,0},{1,3},{3,1},{4,6},{6,4},{5,7},{7,5},{8,10},{10,8},{9,1... | collective-permute-start | bytes 786440 | tf_op jit(solution)/shard_map/ppermute | solution.py:20
  117.9 11.1 %collective-permute-start.19 = (bf16[32,2048]{1,0:T(8,128)(2,1)}, bf16[32,2048]{1,0:T(8,128)(2,1)S(1)}, u32[]{:S(2)}, u32[]{:S(2)}) collective-permute-start(bf16[32,2048]{1,0:T(8,128)(2,1)} %add_convert_fusion.8), channel_id=1, source_target_pairs={{0,2},{2,0},{1,3},{3,1},{4,6},{6,4},{5,7},{7,5},{8,10},{10,8},{9,1... | collective-permute-start | bytes 393224 | tf_op jit(solution)/shard_map/ppermute | solution.py:20
  129.1 8.1 %collective-permute-start.24 = (bf16[64,2048]{1,0:T(8,128)(2,1)S(1)}, bf16[64,2048]{1,0:T(8,128)(2,1)S(1)}, u32[]{:S(2)}, u32[]{:S(2)}) collective-permute-start(bf16[64,2048]{1,0:T(8,128)(2,1)S(1)} %get-tuple-element.107), channel_id=1, source_target_pairs={{0,1},{1,0},{2,3},{3,2},{4,5},{5,4},{6,7},{7,6},{8,9},{9,8},{10,11... | collective-permute-start | bytes 786440 | tf_op jit(solution)/shard_map/ppermute | solution.py:20
  129.7 11.1 %collective-permute-start.23 = (bf16[32,2048]{1,0:T(8,128)(2,1)S(1)}, bf16[32,2048]{1,0:T(8,128)(2,1)S(1)}, u32[]{:S(2)}, u32[]{:S(2)}) collective-permute-start(bf16[32,2048]{1,0:T(8,128)(2,1)S(1)} %add_convert_fusion.7), channel_id=1, source_target_pairs={{0,8},{4,12},{8,0},{12,4},{1,9},{5,13},{9,1},{13,5},{2,10},{6,14},... | collective-permute-start | bytes 393224 | tf_op jit(solution)/shard_map/ppermute | solution.py:20
  133.1 10.6 %collective-permute-start.21 = (bf16[32,2048]{1,0:T(8,128)(2,1)S(1)}, bf16[32,2048]{1,0:T(8,128)(2,1)S(1)}, u32[]{:S(2)}, u32[]{:S(2)}) collective-permute-start(bf16[32,2048]{1,0:T(8,128)(2,1)S(1)} %get-tuple-element.120), channel_id=1, source_target_pairs={{0,4},{4,0},{8,12},{12,8},{1,5},{5,1},{9,13},{13,9},{2,6},{6,2},{1... | collective-permute-start | bytes 393224 | tf_op jit(solution)/shard_map/ppermute | solution.py:20
  133.5 10.3 %collective-permute-start.22 = (bf16[32,2048]{1,0:T(8,128)(2,1)S(1)}, bf16[32,2048]{1,0:T(8,128)(2,1)S(1)}, u32[]{:S(2)}, u32[]{:S(2)}) collective-permute-start(bf16[32,2048]{1,0:T(8,128)(2,1)S(1)} %get-tuple-element.119), channel_id=1, source_target_pairs={{0,12},{4,8},{8,4},{12,0},{1,13},{5,9},{9,5},{13,1},{2,14},{6,10},... | collective-permute-start | bytes 393224 | tf_op jit(solution)/shard_map/ppermute | solution.py:20
  135.8 10.6 %collective-permute-start.27 = (bf16[64,2048]{1,0:T(8,128)(2,1)S(1)}, bf16[64,2048]{1,0:T(8,128)(2,1)S(1)}, u32[]{:S(2)}, u32[]{:S(2)}) collective-permute-start(bf16[64,2048]{1,0:T(8,128)(2,1)S(1)} %add_convert_fusion.1), channel_id=1, source_target_pairs={{0,2},{2,0},{1,3},{3,1},{4,6},{6,4},{5,7},{7,5},{8,10},{10,8},{9,1... | collective-permute-start | bytes 786440 | tf_op jit(solution)/shard_map/ppermute | solution.py:20
  137.3 9.1 %collective-permute-start.25 = (bf16[32,2048]{1,0:T(8,128)(2,1)S(1)}, bf16[32,2048]{1,0:T(8,128)(2,1)S(1)}, u32[]{:S(2)}, u32[]{:S(2)}) collective-permute-start(bf16[32,2048]{1,0:T(8,128)(2,1)S(1)} %add_convert_fusion.6), channel_id=1, source_target_pairs={{0,2},{2,0},{1,3},{3,1},{4,6},{6,4},{5,7},{7,5},{8,10},{10,8},{9,1... | collective-permute-start | bytes 393224 | tf_op jit(solution)/shard_map/ppermute | solution.py:20
  (24 other events, 192.0 us)

commit v19 on v18

--- a/solution.py
+++ b/solution.py
@@ -85,23 +85,24 @@
     return keep, swap(away, "sub", 1)
 
 
-def send_heads(pieces):
+def send_heads(pieces, start=0, stop=None):
     keep, got = pieces
     heads_size = lax.axis_size("heads")
     rows = keep.shape[0] // heads_size
+    stop = rows if stop is None else stop
     received = []
     for flip in range(1, heads_size):
-        part = slice(flip * rows, (flip + 1) * rows)
+        part = slice(flip * rows + start, flip * rows + stop)
         both = keep[part] + got[part].astype(jnp.float32)
         received.append(swap(both.astype(jnp.bfloat16), "heads", flip))
     return keep, got, received
 
 
-def add_shares(pieces):
+def add_shares(pieces, start=0):
     keep, got, received = pieces
-    rows = keep.shape[0] // (len(received) + 1)
-    total = keep[:rows] + got[:rows].astype(jnp.float32)
-    return sum((part.astype(jnp.float32) for part in received), total).astype(jnp.bfloat16)
+    part = slice(start, start + received[0].shape[0])
+    total = keep[part] + got[part].astype(jnp.float32)
+    return sum((piece.astype(jnp.float32) for piece in received), total).astype(jnp.bfloat16)
 
 
 def fetch_kernel(
@@ -361,12 +362,13 @@
     back1 = swap(near1[:few], "pool", 1), swap(near1[few:], "pool", 3)
     back_second0 = swap(add_shares(far0), "pool", 2)
     far1 = send_heads(send_sub(far1))
-    own = send_heads(send_sub(own))
-    back1, back_second0, far1, own = tie((back1, back_second0, far1, own))
+    own = send_sub(own)
+    own0, own1 = send_heads(own, 0, many), send_heads(own, many, many + few)
+    back1, back_second0, far1, own0 = tie((back1, back_second0, far1, own0))
     back_second1 = swap(add_shares(far1), "pool", 2)
-    own = add_shares(own)
+    own0, own1 = add_shares(own0), add_shares(own1, many)
     backs = [(0, 1, back0[0]), (0, 3, back0[1]), (many, 1, back1[0]), (many, 3, back1[1])]
-    backs += [(0, 2, back_second0), (0, 0, own), (many, 2, back_second1)]
+    backs += [(0, 2, back_second0), (0, 0, own0), (many, 0, own1), (many, 2, back_second1)]
     output = jnp.zeros((part_rows, pool_size * columns), jnp.bfloat16)
     for row, flip, block in backs:
         output = lax.dynamic_update_slice(output, block, (row, (pool_index ^ flip) * columns))

time: 156 us -> 154 us (0.987)
  waiting for transfers between devices: 49.8 us -> 45.5 us
  starting transfers between devices: 47.2 us -> 50.3 us
    ppermute x27 -> x28, waiting for transfers between devices: 42.6 us -> 38.5 us  [swap(): lax.ppermute(values, axis, [(i, i ^ flip) for i in range(lax.axis_size(ax...]
    ppermute x27 -> x28, starting transfers between devices: 33.9 us -> 37 us  [swap(): lax.ppermute(values, axis, [(i, i ^ flip) for i in range(lax.axis_size(ax...]
  transfers between devices with their start and end apart: 29 -> 30, of which waited for: 12 -> 12; matrix products, arithmetic and copies ran while one was open for 8% -> 8% of each run, Pallas kernels for 13% -> 13%
where the time goes in v19:
time: 154 us
  starting transfers between devices  50.3 us (33%)
  waiting for transfers between devices  45.5 us (30%)
  Pallas kernels  29.6 us (19%)
  local copies, waits for them, and re-layouts  21.9 us (14%)
  other arithmetic  5.96 us (4%)
    ppermute x28, waiting for transfers between devices, swap(): lax.ppermute(values, axis, [(i, i ^ flip) for i in range(lax.axis_size(ax...  38.5 us
    ppermute x28, starting transfers between devices, swap(): lax.ppermute(values, axis, [(i, i ^ flip) for i in range(lax.axis_size(ax...  37 us
    pallas_call x5, Pallas kernels, project_out(): pl.pallas_call(functools.partial(project_kernel, len(blocks), list(range(...  15.9 us
    unnamed x38, local copies, waits for them, and re-layouts  13.7 us
    ppermute x2, starting transfers between devices, second_hop(): return lax.ppermute(passed, 'pool', [(0, 2), (3, 1), (1, 0), (2, 3)])  13.3 us
    pallas_call x2, Pallas kernels, attend(): pl.pallas_call(functools.partial(attend_kernel, start, rows, len(parts)),...  8.82 us
    ppermute x2, waiting for transfers between devices, second_hop(): return lax.ppermute(passed, 'pool', [(0, 2), (3, 1), (1, 0), (2, 3)])  7.06 us
    pallas_call x1, Pallas kernels, fetch(): pl.pallas_call(functools.partial(fetch_kernel, pool_size=pool_size, share...  3.75 us
  transfers between devices with their start and end apart: 30, of which 12 were waited for; matrix products, arithmetic and copies ran while one was open for 8% of the time, Pallas kernels for 13%

profile of v19, /device:TPU:0, one launch (start us, length us, event | category | flops | bytes accessed | tf_op | source)
XLA Modules:
  0.0 153.7 jit_solution(9163479646700495454)
XLA Ops:
  0.6 3.7 %shard_map.100 = (s32[2,16]{1,0:T(2,128)}, bf16[8,32,512]{2,1,0:T(8,128)(2,1)}, bf16[8,32,512]{2,1,0:T(8,128)(2,1)}, bf16[8,32,512]{2,1,0:T(8,128)(2,1)}, bf16[8,32,512]{2,1,0:T(8,128)(2,1)}) custom-call(s32[2]{0:T(128)} %pad_add_fusion.1.place, s32[8,8]{1,0:T(8,128)} %holder.1, s32[8,8]{1,0:T(8,128)} %block.1, s32[8]{0:T(128)} %serving.1, ...), custom_call_target="tpu_custom_call" | custom-call | flops 1 | bytes 1 | tf_op jit(solution)/shard_map/pallas_call | solution.py:154
  4.4 3.7 %collective-permute-start = (bf16[8,32,512]{2,1,0:T(8,128)(2,1)}, bf16[8,32,512]{2,1,0:T(8,128)(2,1)S(1)}, u32[]{:S(2)}, u32[]{:S(2)}) collective-permute-start(bf16[8,32,512]{2,1,0:T(8,128)(2,1)} %get-tuple-element.64), channel_id=1, source_target_pairs={{0,8},{4,12},{8,0},{12,4},{1,9},{5,13},{9,1},{13,5},{2,10},{6,14},... | collective-permute-start | bytes 786440 | tf_op jit(solution)/shard_map/ppermute | solution.py:20
  14.2 2.3 %reshape.24 = bf16[512,2,256]{2,1,0:T(2,128)(2,1)S(1)} reshape(bf16[512,2,2,128]{3,2,1,0:T(2,128)(2,1)} %param.12) | data formatting | bytes 1048576 | tf_op jit(solution)/shard_map/reshape | solution.py:294
  17.3 9.4 %collective-permute-done.refs_1_ = bf16[8,32,512]{2,1,0:T(8,128)(2,1)S(1)} collective-permute-done((bf16[8,32,512]{2,1,0:T(8,128)(2,1)}, bf16[8,32,512]{2,1,0:T(8,128)(2,1)S(1)}, u32[]{:S(2)}, u32[]{:S(2)}) %collective-permute-start) | collective-permute-done | bytes 262176 | tf_op jit(solution)/shard_map/ppermute | solution.py:20
  30.4 9.8 %collective-permute-done.4.refs_2_ = bf16[2,256,512]{2,1,0:T(8,128)(2,1)S(1)} collective-permute-done((bf16[2,256,512]{2,1,0:T(8,128)(2,1)S(1)}, bf16[2,256,512]{2,1,0:T(8,128)(2,1)S(1)}, u32[]{:S(2)}, u32[]{:S(2)}) %collective-permute-start.4) | collective-permute-done | bytes 524320 | tf_op jit(solution)/shard_map/ppermute | solution.py:20
  42.1 4.4 %shard_map.103.refs_0_ = bf16[128,2048]{1,0:T(8,128)(2,1)S(1)} custom-call(s32[3]{0:T(128)S(1)} %pad_add_fusion.2.scalars, bf16[2,2,64,2048]{3,2,1,0:T(8,128)(2,1)S(1)} %bitcast.18, bf16[2,256,512]{2,1,0:T(8,128)(2,1)S(1)} %bitcast.16, bf16[2,256,512]{2,1,0:T(8,128)(2,1)S(1)} %collective-permute-done.3.refs_1_, ...), custom_call_target="tpu_custom_call" | custom-call | flops 1 | bytes 1 | tf_op jit(solution)/shard_map/pallas_call | solution.py:255
  46.5 4.3 %collective-permute-start.8 = (bf16[128,2048]{1,0:T(8,128)(2,1)S(1)}, bf16[128,2048]{1,0:T(8,128)(2,1)S(1)}, u32[]{:S(2)}, u32[]{:S(2)}) collective-permute-start(bf16[128,2048]{1,0:T(8,128)(2,1)S(1)} %shard_map.103.refs_0_), channel_id=1, source_target_pairs={{0,12},{4,8},{8,4},{12,0},{1,13},{5,9},{9,5},{13,1},{2,14},{6,10},... | collective-permute-start | bytes 1572872 | tf_op jit(solution)/shard_map/ppermute | solution.py:20
  50.9 5.3 %collective-permute-start.9 = (bf16[128,2048]{1,0:T(8,128)(2,1)S(1)}, bf16[128,2048]{1,0:T(8,128)(2,1)S(1)}, u32[]{:S(2)}, u32[]{:S(2)}) collective-permute-start(bf16[128,2048]{1,0:T(8,128)(2,1)S(1)} %shard_map.103.refs_0_), channel_id=1, source_target_pairs={{0,4},{4,0},{8,12},{12,8},{1,5},{5,1},{9,13},{13,9},{2,6},{6,2},{1... | collective-permute-start | bytes 1572872 | tf_op jit(solution)/shard_map/ppermute | solution.py:20
  56.2 4.4 %shard_map.102.refs_1_ = bf16[128,2048]{1,0:T(8,128)(2,1)S(1)} custom-call(s32[3]{0:T(128)S(1)} %pad_add_fusion.2.scalars, bf16[2,2,64,2048]{3,2,1,0:T(8,128)(2,1)S(1)} %bitcast.19, bf16[2,256,512]{2,1,0:T(8,128)(2,1)S(1)} %bitcast.17, bf16[2,256,512]{2,1,0:T(8,128)(2,1)S(1)} %collective-permute-done.3.refs_1_, ...), custom_call_target="tpu_custom_call" | custom-call | flops 1 | bytes 1 | tf_op jit(solution)/shard_map/pallas_call | solution.py:255
  61.6 3.4 %copy-done = bf16[2048,2048]{1,0:T(8,128)(2,1)S(1)} copy-done((bf16[2048,2048]{1,0:T(8,128)(2,1)S(1)}, bf16[2048,2048]{1,0:T(8,128)(2,1)}, u32[]{:S(2)}) %copy-start) | copy-done | bytes 8388632
  65.0 3.6 %shard_map.104 = (f32[128,2048]{1,0:T(8,128)S(1)}, bf16[128,2048]{1,0:T(8,128)(2,1)S(1)}) custom-call(s32[1]{0:T(128)} %bitcast.1.share, bf16[128,2048]{1,0:T(8,128)(2,1)S(1)} %shard_map.103.refs_0_, bf16[128,2048]{1,0:T(8,128)(2,1)S(1)} %shard_map.102.refs_1_, bf16[2048,2048]{1,0:T(8,128)(2,1)S(1)} %copy-done), custom_call_target="tpu_custom_call" | custom-call | flops 1 | bytes 1 | tf_op jit(solution)/shard_map/pallas_call | solution.py:56
  70.4 4.6 %collective-permute-done.9.refs_0_ = bf16[128,2048]{1,0:T(8,128)(2,1)S(1)} collective-permute-done((bf16[128,2048]{1,0:T(8,128)(2,1)S(1)}, bf16[128,2048]{1,0:T(8,128)(2,1)S(1)}, u32[]{:S(2)}, u32[]{:S(2)}) %collective-permute-start.9) | collective-permute-done | bytes 524320 | tf_op jit(solution)/shard_map/ppermute | solution.py:20
  75.0 3.4 %copy-done.1 = bf16[2048,2048]{1,0:T(8,128)(2,1)S(1)} copy-done((bf16[2048,2048]{1,0:T(8,128)(2,1)S(1)}, bf16[2048,2048]{1,0:T(8,128)(2,1)}, u32[]{:S(2)}) %copy-start.1) | copy-done | bytes 8388632
  78.4 3.6 %shard_map.105 = (f32[64,2048]{1,0:T(8,128)S(1)}, bf16[64,2048]{1,0:T(8,128)(2,1)S(1)}, bf16[64,2048]{1,0:T(8,128)(2,1)S(1)}, bf16[64,2048]{1,0:T(8,128)(2,1)S(1)}) custom-call(s32[1]{0:T(128)} %bitcast.1.share, bf16[128,2048]{1,0:T(8,128)(2,1)S(1)} %collective-permute-done.9.refs_0_, bf16[128,2048]{1,0:T(8,128)(2,1)S(1)} %collective-permute-done.8.refs_1_, ...), custom_call_target="tpu_custom_call" | custom-call | flops 1 | bytes 1 | tf_op jit(solution)/shard_map/pallas_call | solution.py:56
  86.1 13.3 %collective-permute-start.15 = (bf16[128,2048]{1,0:T(8,128)(2,1)S(1)}, bf16[128,2048]{1,0:T(8,128)(2,1)S(1)}, u32[]{:S(2)}, u32[]{:S(2)}) collective-permute-start(bf16[128,2048]{1,0:T(8,128)(2,1)S(1)} %broadcast_select_fusion.1), channel_id=1, source_target_pairs={{0,8},{12,4},{4,0},{8,12},{1,9},{13,5},{5,1},{9,13},{2,10},{14,6},... | collective-permute-start | bytes 1572872 | tf_op jit(solution)/shard_map/ppermute | solution.py:27
  101.5 3.6 %shard_map.106 = (f32[128,2048]{1,0:T(8,128)S(1)}, bf16[128,2048]{1,0:T(8,128)(2,1)S(1)}) custom-call(s32[1]{0:T(128)} %bitcast.1.share, bf16[128,2048]{1,0:T(8,128)(2,1)S(1)} %copy-done.7, bf16[128,2048]{1,0:T(8,128)(2,1)S(1)} %collective-permute-done.6.refs_1_, bf16[2048,2048]{1,0:T(8,128)(2,1)S(1)} %bitcast.11), custom_call_target="tpu_custom_call" | custom-call | flops 1 | bytes 1 | tf_op jit(solution)/shard_map/pallas_call | solution.py:56
  109.0 2.8 %collective-permute-done.15.refs_0_ = bf16[128,2048]{1,0:T(8,128)(2,1)S(1)} collective-permute-done((bf16[128,2048]{1,0:T(8,128)(2,1)S(1)}, bf16[128,2048]{1,0:T(8,128)(2,1)S(1)}, u32[]{:S(2)}, u32[]{:S(2)}) %collective-permute-start.15) | collective-permute-done | bytes 524320 | tf_op jit(solution)/shard_map/ppermute | solution.py:27
  111.8 2.5 %shard_map.107 = (f32[64,2048]{1,0:T(8,128)S(1)}, bf16[64,2048]{1,0:T(8,128)(2,1)S(1)}) custom-call(s32[1]{0:T(128)} %bitcast.1.share, bf16[128,2048]{1,0:T(8,128)(2,1)S(1)} %collective-permute-done.15.refs_0_, bf16[2048,2048]{1,0:T(8,128)(2,1)S(1)} %bitcast.11), custom_call_target="tpu_custom_call" | custom-call | flops 1 | bytes 1 | tf_op jit(solution)/shard_map/pallas_call | solution.py:56
  118.9 4.3 %collective-permute-done.20.refs_0_ = bf16[128,2048]{1,0:T(8,128)(2,1)S(1)} collective-permute-done((bf16[128,2048]{1,0:T(8,128)(2,1)}, bf16[128,2048]{1,0:T(8,128)(2,1)S(1)}, u32[]{:S(2)}, u32[]{:S(2)}) %collective-permute-start.20) | collective-permute-done | bytes 524320 | tf_op jit(solution)/shard_map/ppermute | solution.py:27
  123.1 3.4 %copy-done.2 = bf16[2048,2048]{1,0:T(8,128)(2,1)S(1)} copy-done((bf16[2048,2048]{1,0:T(8,128)(2,1)S(1)}, bf16[2048,2048]{1,0:T(8,128)(2,1)}, u32[]{:S(2)}) %copy-start.2) | copy-done | bytes 8388632
  126.5 2.6 %shard_map.108 = (f32[64,2048]{1,0:T(8,128)S(1)}, bf16[64,2048]{1,0:T(8,128)(2,1)S(1)}) custom-call(s32[1]{0:T(128)} %bitcast.1.share, bf16[128,2048]{1,0:T(8,128)(2,1)S(1)} %collective-permute-done.20.refs_0_, bf16[2048,2048]{1,0:T(8,128)(2,1)S(1)} %copy-done.2), custom_call_target="tpu_custom_call" | custom-call | flops 1 | bytes 1 | tf_op jit(solution)/shard_map/pallas_call | solution.py:56
  129.8 3.3 %collective-permute-start.23 = (bf16[32,2048]{1,0:T(8,128)(2,1)S(1)}, bf16[32,2048]{1,0:T(8,128)(2,1)S(1)}, u32[]{:S(2)}, u32[]{:S(2)}) collective-permute-start(bf16[32,2048]{1,0:T(8,128)(2,1)S(1)} %add_convert_fusion.9), channel_id=1, source_target_pairs={{0,8},{4,12},{8,0},{12,4},{1,9},{5,13},{9,1},{13,5},{2,10},{6,14},... | collective-permute-start | bytes 393224 | tf_op jit(solution)/shard_map/ppermute | solution.py:20
  144.6 2.3 %collective-permute-start.29 = (bf16[32,2048]{1,0:T(8,128)(2,1)S(1)}, bf16[32,2048]{1,0:T(8,128)(2,1)S(1)}, u32[]{:S(2)}, u32[]{:S(2)}) collective-permute-start(bf16[32,2048]{1,0:T(8,128)(2,1)S(1)} %add_convert_fusion.3), channel_id=1, source_target_pairs={{0,8},{4,12},{8,0},{12,4},{1,9},{5,13},{9,1},{13,5},{2,10},{6,14},... | collective-permute-start | bytes 393224 | tf_op jit(solution)/shard_map/ppermute | solution.py:20
  147.1 5.9 %collective-permute-done.29 = bf16[32,2048]{1,0:T(8,128)(2,1)S(1)} collective-permute-done((bf16[32,2048]{1,0:T(8,128)(2,1)S(1)}, bf16[32,2048]{1,0:T(8,128)(2,1)S(1)}, u32[]{:S(2)}, u32[]{:S(2)}) %collective-permute-start.29) | collective-permute-done | bytes 131104 | tf_op jit(solution)/shard_map/ppermute | solution.py:20
  (117 shorter events, 43.4 us)
Async XLA Ops:
  4.4 22.4 %collective-permute-start = (bf16[8,32,512]{2,1,0:T(8,128)(2,1)}, bf16[8,32,512]{2,1,0:T(8,128)(2,1)S(1)}, u32[]{:S(2)}, u32[]{:S(2)}) collective-permute-start(bf16[8,32,512]{2,1,0:T(8,128)(2,1)} %get-tuple-element.64), channel_id=1, source_target_pairs={{0,8},{4,12},{8,0},{12,4},{1,9},{5,13},{9,1},{13,5},{2,10},{6,14},... | collective-permute-start | bytes 786440 | tf_op jit(solution)/shard_map/ppermute | solution.py:20
  8.1 18.6 %collective-permute-start.1 = (bf16[8,32,512]{2,1,0:T(8,128)(2,1)}, bf16[8,32,512]{2,1,0:T(8,128)(2,1)S(1)}, u32[]{:S(2)}, u32[]{:S(2)}) collective-permute-start(bf16[8,32,512]{2,1,0:T(8,128)(2,1)} %get-tuple-element.65), channel_id=1, source_target_pairs={{0,12},{4,8},{8,4},{12,0},{1,13},{5,9},{9,5},{13,1},{2,14},{6,10},... | collective-permute-start | bytes 786440 | tf_op jit(solution)/shard_map/ppermute | solution.py:20
  9.8 17.4 %collective-permute-start.2 = (bf16[8,32,512]{2,1,0:T(8,128)(2,1)}, bf16[8,32,512]{2,1,0:T(8,128)(2,1)S(1)}, u32[]{:S(2)}, u32[]{:S(2)}) collective-permute-start(bf16[8,32,512]{2,1,0:T(8,128)(2,1)} %get-tuple-element.66), channel_id=1, source_target_pairs={{0,4},{4,0},{8,12},{12,8},{1,5},{5,1},{9,13},{13,9},{2,6},{6,2},{1... | collective-permute-start | bytes 786440 | tf_op jit(solution)/shard_map/ppermute | solution.py:20
  28.4 11.8 %collective-permute-start.4 = (bf16[2,256,512]{2,1,0:T(8,128)(2,1)S(1)}, bf16[2,256,512]{2,1,0:T(8,128)(2,1)S(1)}, u32[]{:S(2)}, u32[]{:S(2)}) collective-permute-start(bf16[2,256,512]{2,1,0:T(8,128)(2,1)S(1)} %bitcast.14), channel_id=1, source_target_pairs={{0,2},{2,0},{1,3},{3,1},{4,6},{6,4},{5,7},{7,5},{8,10},{10,8},{9,1... | collective-permute-start | bytes 1572872 | tf_op jit(solution)/shard_map/ppermute | solution.py:20
  30.4 9.8 %collective-permute-start.3 = (bf16[2,256,512]{2,1,0:T(8,128)(2,1)S(1)}, bf16[2,256,512]{2,1,0:T(8,128)(2,1)S(1)}, u32[]{:S(2)}, u32[]{:S(2)}) collective-permute-start(bf16[2,256,512]{2,1,0:T(8,128)(2,1)S(1)} %bitcast.15), channel_id=1, source_target_pairs={{0,1},{1,0},{2,3},{3,2},{4,5},{5,4},{6,7},{7,6},{8,9},{9,8},{10,11... | collective-permute-start | bytes 1572872 | tf_op jit(solution)/shard_map/ppermute | solution.py:20
  46.5 23.8 %collective-permute-start.8 = (bf16[128,2048]{1,0:T(8,128)(2,1)S(1)}, bf16[128,2048]{1,0:T(8,128)(2,1)S(1)}, u32[]{:S(2)}, u32[]{:S(2)}) collective-permute-start(bf16[128,2048]{1,0:T(8,128)(2,1)S(1)} %shard_map.103.refs_0_), channel_id=1, source_target_pairs={{0,12},{4,8},{8,4},{12,0},{1,13},{5,9},{9,5},{13,1},{2,14},{6,10},... | collective-permute-start | bytes 1572872 | tf_op jit(solution)/shard_map/ppermute | solution.py:20
  50.9 24.1 %collective-permute-start.9 = (bf16[128,2048]{1,0:T(8,128)(2,1)S(1)}, bf16[128,2048]{1,0:T(8,128)(2,1)S(1)}, u32[]{:S(2)}, u32[]{:S(2)}) collective-permute-start(bf16[128,2048]{1,0:T(8,128)(2,1)S(1)} %shard_map.103.refs_0_), channel_id=1, source_target_pairs={{0,4},{4,0},{8,12},{12,8},{1,5},{5,1},{9,13},{13,9},{2,6},{6,2},{1... | collective-permute-start | bytes 1572872 | tf_op jit(solution)/shard_map/ppermute | solution.py:20
  60.6 25.6 %collective-permute-start.6 = (bf16[128,2048]{1,0:T(8,128)(2,1)S(1)}, bf16[128,2048]{1,0:T(8,128)(2,1)S(1)}, u32[]{:S(2)}, u32[]{:S(2)}) collective-permute-start(bf16[128,2048]{1,0:T(8,128)(2,1)S(1)} %shard_map.102.refs_1_), channel_id=1, source_target_pairs={{0,12},{4,8},{8,4},{12,0},{1,13},{5,9},{9,5},{13,1},{2,14},{6,10},... | collective-permute-start | bytes 1572872 | tf_op jit(solution)/shard_map/ppermute | solution.py:20
  61.6 37.8 %collective-permute-start.7 = (bf16[128,2048]{1,0:T(8,128)(2,1)S(1)}, bf16[128,2048]{1,0:T(8,128)(2,1)S(1)}, u32[]{:S(2)}, u32[]{:S(2)}) collective-permute-start(bf16[128,2048]{1,0:T(8,128)(2,1)S(1)} %shard_map.102.refs_1_), channel_id=1, source_target_pairs={{0,4},{4,0},{8,12},{12,8},{1,5},{5,1},{9,13},{13,9},{2,6},{6,2},{1... | collective-permute-start | bytes 1572872 | tf_op jit(solution)/shard_map/ppermute | solution.py:20
  82.0 17.5 %collective-permute-start.10 = (bf16[64,2048]{1,0:T(8,128)(2,1)S(1)}, bf16[64,2048]{1,0:T(8,128)(2,1)S(1)}, u32[]{:S(2)}, u32[]{:S(2)}) collective-permute-start(bf16[64,2048]{1,0:T(8,128)(2,1)S(1)} %get-tuple-element.76), channel_id=1, source_target_pairs={{0,1},{1,0},{2,3},{3,2},{4,5},{5,4},{6,7},{7,6},{8,9},{9,8},{10,11... | collective-permute-start | bytes 786440 | tf_op jit(solution)/shard_map/ppermute | solution.py:20
  82.1 17.4 %collective-permute-start.11 = (bf16[64,2048]{1,0:T(8,128)(2,1)S(1)}, bf16[64,2048]{1,0:T(8,128)(2,1)S(1)}, u32[]{:S(2)}, u32[]{:S(2)}) collective-permute-start(bf16[64,2048]{1,0:T(8,128)(2,1)S(1)} %get-tuple-element.77), channel_id=1, source_target_pairs={{0,2},{1,3},{2,0},{3,1},{4,6},{5,7},{6,4},{7,5},{8,10},{9,11},{10,... | collective-permute-start | bytes 786440 | tf_op jit(solution)/shard_map/ppermute | solution.py:20
  83.6 15.9 %collective-permute-start.12 = (bf16[64,2048]{1,0:T(8,128)(2,1)S(1)}, bf16[64,2048]{1,0:T(8,128)(2,1)S(1)}, u32[]{:S(2)}, u32[]{:S(2)}) collective-permute-start(bf16[64,2048]{1,0:T(8,128)(2,1)S(1)} %get-tuple-element.78), channel_id=1, source_target_pairs={{0,3},{1,2},{2,1},{3,0},{4,7},{5,6},{6,5},{7,4},{8,11},{9,10},{10,... | collective-permute-start | bytes 786440 | tf_op jit(solution)/shard_map/ppermute | solution.py:20
  86.1 25.6 %collective-permute-start.15 = (bf16[128,2048]{1,0:T(8,128)(2,1)S(1)}, bf16[128,2048]{1,0:T(8,128)(2,1)S(1)}, u32[]{:S(2)}, u32[]{:S(2)}) collective-permute-start(bf16[128,2048]{1,0:T(8,128)(2,1)S(1)} %broadcast_select_fusion.1), channel_id=1, source_target_pairs={{0,8},{12,4},{4,0},{8,12},{1,9},{13,5},{5,1},{9,13},{2,10},{14,6},... | collective-permute-start | bytes 1572872 | tf_op jit(solution)/shard_map/ppermute | solution.py:27
  100.5 22.7 %collective-permute-start.20 = (bf16[128,2048]{1,0:T(8,128)(2,1)}, bf16[128,2048]{1,0:T(8,128)(2,1)S(1)}, u32[]{:S(2)}, u32[]{:S(2)}) collective-permute-start(bf16[128,2048]{1,0:T(8,128)(2,1)} %broadcast_select_fusion), channel_id=1, source_target_pairs={{0,8},{12,4},{4,0},{8,12},{1,9},{13,5},{5,1},{9,13},{2,10},{14,6},... | collective-permute-start | bytes 1572872 | tf_op jit(solution)/shard_map/ppermute | solution.py:27
  106.1 23.0 %collective-permute-start.13 = (bf16[32,2048]{1,0:T(8,128)(2,1)}, bf16[32,2048]{1,0:T(8,128)(2,1)}, u32[]{:S(2)}, u32[]{:S(2)}) collective-permute-start(bf16[32,2048]{1,0:T(8,128)(2,1)} %get-tuple-element.124), channel_id=1, source_target_pairs={{0,4},{4,0},{8,12},{12,8},{1,5},{5,1},{9,13},{13,9},{2,6},{6,2},{1... | collective-permute-start | bytes 393224 | tf_op jit(solution)/shard_map/ppermute | solution.py:20
  108.1 21.0 %collective-permute-start.14 = (bf16[32,2048]{1,0:T(8,128)(2,1)}, bf16[32,2048]{1,0:T(8,128)(2,1)}, u32[]{:S(2)}, u32[]{:S(2)}) collective-permute-start(bf16[32,2048]{1,0:T(8,128)(2,1)} %get-tuple-element.123), channel_id=1, source_target_pairs={{0,12},{4,8},{8,4},{12,0},{1,13},{5,9},{9,5},{13,1},{2,14},{6,10},... | collective-permute-start | bytes 393224 | tf_op jit(solution)/shard_map/ppermute | solution.py:20
  115.2 13.9 %collective-permute-start.17 = (bf16[64,2048]{1,0:T(8,128)(2,1)}, bf16[64,2048]{1,0:T(8,128)(2,1)S(1)}, u32[]{:S(2)}, u32[]{:S(2)}) collective-permute-start(bf16[64,2048]{1,0:T(8,128)(2,1)} %add_convert_fusion.1), channel_id=1, source_target_pairs={{0,2},{2,0},{1,3},{3,1},{4,6},{6,4},{5,7},{7,5},{8,10},{10,8},{9,1... | collective-permute-start | bytes 786440 | tf_op jit(solution)/shard_map/ppermute | solution.py:20
  118.1 11.0 %collective-permute-start.19 = (bf16[32,2048]{1,0:T(8,128)(2,1)}, bf16[32,2048]{1,0:T(8,128)(2,1)S(1)}, u32[]{:S(2)}, u32[]{:S(2)}) collective-permute-start(bf16[32,2048]{1,0:T(8,128)(2,1)} %add_convert_fusion.10), channel_id=1, source_target_pairs={{0,2},{2,0},{1,3},{3,1},{4,6},{6,4},{5,7},{7,5},{8,10},{10,8},{9,1... | collective-permute-start | bytes 393224 | tf_op jit(solution)/shard_map/ppermute | solution.py:20
  129.1 8.3 %collective-permute-start.26 = (bf16[128,2048]{1,0:T(8,128)(2,1)S(1)}, bf16[128,2048]{1,0:T(8,128)(2,1)S(1)}, u32[]{:S(2)}, u32[]{:S(2)}) collective-permute-start(bf16[128,2048]{1,0:T(8,128)(2,1)S(1)} %copy-done.11), channel_id=1, source_target_pairs={{0,1},{1,0},{2,3},{3,2},{4,5},{5,4},{6,7},{7,6},{8,9},{9,8},{10,11... | collective-permute-start | bytes 1572872 | tf_op jit(solution)/shard_map/ppermute | solution.py:20
  129.8 11.1 %collective-permute-start.23 = (bf16[32,2048]{1,0:T(8,128)(2,1)S(1)}, bf16[32,2048]{1,0:T(8,128)(2,1)S(1)}, u32[]{:S(2)}, u32[]{:S(2)}) collective-permute-start(bf16[32,2048]{1,0:T(8,128)(2,1)S(1)} %add_convert_fusion.9), channel_id=1, source_target_pairs={{0,8},{4,12},{8,0},{12,4},{1,9},{5,13},{9,1},{13,5},{2,10},{6,14},... | collective-permute-start | bytes 393224 | tf_op jit(solution)/shard_map/ppermute | solution.py:20
  133.2 10.6 %collective-permute-start.21 = (bf16[32,2048]{1,0:T(8,128)(2,1)S(1)}, bf16[32,2048]{1,0:T(8,128)(2,1)S(1)}, u32[]{:S(2)}, u32[]{:S(2)}) collective-permute-start(bf16[32,2048]{1,0:T(8,128)(2,1)S(1)} %get-tuple-element.122), channel_id=1, source_target_pairs={{0,4},{4,0},{8,12},{12,8},{1,5},{5,1},{9,13},{13,9},{2,6},{6,2},{1... | collective-permute-start | bytes 393224 | tf_op jit(solution)/shard_map/ppermute | solution.py:20
  133.6 10.3 %collective-permute-start.22 = (bf16[32,2048]{1,0:T(8,128)(2,1)S(1)}, bf16[32,2048]{1,0:T(8,128)(2,1)S(1)}, u32[]{:S(2)}, u32[]{:S(2)}) collective-permute-start(bf16[32,2048]{1,0:T(8,128)(2,1)S(1)} %get-tuple-element.121), channel_id=1, source_target_pairs={{0,12},{4,8},{8,4},{12,0},{1,13},{5,9},{9,5},{13,1},{2,14},{6,10},... | collective-permute-start | bytes 393224 | tf_op jit(solution)/shard_map/ppermute | solution.py:20
  135.8 8.0 %collective-permute-start.25 = (bf16[32,2048]{1,0:T(8,128)(2,1)S(1)}, bf16[32,2048]{1,0:T(8,128)(2,1)S(1)}, u32[]{:S(2)}, u32[]{:S(2)}) collective-permute-start(bf16[32,2048]{1,0:T(8,128)(2,1)S(1)} %add_convert_fusion.8), channel_id=1, source_target_pairs={{0,2},{2,0},{1,3},{3,1},{4,6},{6,4},{5,7},{7,5},{8,10},{10,8},{9,1... | collective-permute-start | bytes 393224 | tf_op jit(solution)/shard_map/ppermute | solution.py:20
  144.6 8.4 %collective-permute-start.29 = (bf16[32,2048]{1,0:T(8,128)(2,1)S(1)}, bf16[32,2048]{1,0:T(8,128)(2,1)S(1)}, u32[]{:S(2)}, u32[]{:S(2)}) collective-permute-start(bf16[32,2048]{1,0:T(8,128)(2,1)S(1)} %add_convert_fusion.3), channel_id=1, source_target_pairs={{0,8},{4,12},{8,0},{12,4},{1,9},{5,13},{9,1},{13,5},{2,10},{6,14},... | collective-permute-start | bytes 393224 | tf_op jit(solution)/shard_map/ppermute | solution.py:20
  (25 other events, 199.1 us)

commit v20 on v19

--- a/solution.py
+++ b/solution.py
@@ -43,7 +43,7 @@
         out[...] = product[i * rows : (i + 1) * rows].astype(out.dtype)
 
 
-def project_out(blocks, out_weight, direct=False):
+def project_out(blocks, out_weight, direct=False, vmem=10):
     axes = ("heads", "sub")
     share_count = lax.axis_size(axes)
     share = lax.axis_index(axes).astype(jnp.int32).reshape(1)
@@ -66,7 +66,7 @@
             jax.ShapeDtypeStruct((rows, columns), jnp.bfloat16 if i else jnp.float32)
             for i in range(count)
         ],
-        compiler_params=pltpu.CompilerParams(vmem_limit_bytes=10 * 1024 * 1024),
+        compiler_params=pltpu.CompilerParams(vmem_limit_bytes=vmem * 1024 * 1024),
         cost_estimate=LIGHT,
     )(share, *blocks, out_weight)
 
@@ -356,7 +356,7 @@
     second0, near1 = tie((second0, near1))
     near1 = send_heads(near1)
     far0 = send_heads(send_sub(project_out([second0], out_weight)))
-    far1 = project_out([second1], out_weight)
+    far1 = project_out([second1], out_weight, vmem=54)
     back0, near1, far0, far1, own = tie((back0, near1, far0, far1, own))
     near1 = add_shares(near1)
     back1 = swap(near1[:few], "pool", 1), swap(near1[few:], "pool", 3)

time: 154 us -> 155 us (level)
  local copies, waits for them, and re-layouts: 21.9 us -> 17.4 us
  Pallas kernels: 29.6 us -> 33.9 us
  other arithmetic: 5.96 us -> 7.64 us
    unnamed x38 -> x28, local copies, waits for them, and re-layouts: 13.7 us -> 9.26 us
    pallas_call x5, Pallas kernels: 15.9 us -> 20.2 us  [project_out(): pl.pallas_call(functools.partial(project_kernel, len(blocks), list(range(...]
  transfers between devices with their start and end apart: 30 -> 30, of which waited for: 12 -> 12; matrix products, arithmetic and copies ran while one was open for 8% -> 9% of each run, Pallas kernels for 13% -> 16%
where the time goes in v20:
time: 155 us
  starting transfers between devices  49.1 us (32%)
  waiting for transfers between devices  46.3 us (30%)
  Pallas kernels  33.9 us (22%)
  local copies, waits for them, and re-layouts  17.4 us (11%)
  other arithmetic  7.64 us (5%)
    ppermute x28, waiting for transfers between devices, swap(): lax.ppermute(values, axis, [(i, i ^ flip) for i in range(lax.axis_size(ax...  38.4 us
    ppermute x28, starting transfers between devices, swap(): lax.ppermute(values, axis, [(i, i ^ flip) for i in range(lax.axis_size(ax...  35.5 us
    pallas_call x5, Pallas kernels, project_out(): pl.pallas_call(functools.partial(project_kernel, len(blocks), list(range(...  20.2 us
    ppermute x2, starting transfers between devices, second_hop(): return lax.ppermute(passed, 'pool', [(0, 2), (3, 1), (1, 0), (2, 3)])  13.6 us
    unnamed x28, local copies, waits for them, and re-layouts  9.26 us
    pallas_call x2, Pallas kernels, attend(): pl.pallas_call(functools.partial(attend_kernel, start, rows, len(parts)),...  8.82 us
    ppermute x2, waiting for transfers between devices, second_hop(): return lax.ppermute(passed, 'pool', [(0, 2), (3, 1), (1, 0), (2, 3)])  7.87 us
    pallas_call x1, Pallas kernels, fetch(): pl.pallas_call(functools.partial(fetch_kernel, pool_size=pool_size, share...  3.75 us
  transfers between devices with their start and end apart: 30, of which 12 were waited for; matrix products, arithmetic and copies ran while one was open for 9% of the time, Pallas kernels for 16%

profile of v20, /device:TPU:0, one launch (start us, length us, event | category | flops | bytes accessed | tf_op | source)
XLA Modules:
  0.0 154.7 jit_solution(6034834012104180828)
XLA Ops:
  0.6 3.7 %shard_map.100 = (s32[2,16]{1,0:T(2,128)}, bf16[8,32,512]{2,1,0:T(8,128)(2,1)}, bf16[8,32,512]{2,1,0:T(8,128)(2,1)}, bf16[8,32,512]{2,1,0:T(8,128)(2,1)}, bf16[8,32,512]{2,1,0:T(8,128)(2,1)}) custom-call(s32[2]{0:T(128)} %pad_add_fusion.1.place, s32[8,8]{1,0:T(8,128)} %holder.1, s32[8,8]{1,0:T(8,128)} %block.1, s32[8]{0:T(128)} %serving.1, ...), custom_call_target="tpu_custom_call" | custom-call | flops 1 | bytes 1 | tf_op jit(solution)/shard_map/pallas_call | solution.py:154
  4.3 4.1 %collective-permute-start = (bf16[8,32,512]{2,1,0:T(8,128)(2,1)}, bf16[8,32,512]{2,1,0:T(8,128)(2,1)S(1)}, u32[]{:S(2)}, u32[]{:S(2)}) collective-permute-start(bf16[8,32,512]{2,1,0:T(8,128)(2,1)} %get-tuple-element.64), channel_id=1, source_target_pairs={{0,8},{4,12},{8,0},{12,4},{1,9},{5,13},{9,1},{13,5},{2,10},{6,14},... | collective-permute-start | bytes 786440 | tf_op jit(solution)/shard_map/ppermute | solution.py:20
  13.9 2.3 %reshape.24 = bf16[512,2,256]{2,1,0:T(2,128)(2,1)S(1)} reshape(bf16[512,2,2,128]{3,2,1,0:T(2,128)(2,1)} %param.12) | data formatting | bytes 1048576 | tf_op jit(solution)/shard_map/reshape | solution.py:294
  17.0 10.0 %collective-permute-done.refs_1_ = bf16[8,32,512]{2,1,0:T(8,128)(2,1)S(1)} collective-permute-done((bf16[8,32,512]{2,1,0:T(8,128)(2,1)}, bf16[8,32,512]{2,1,0:T(8,128)(2,1)S(1)}, u32[]{:S(2)}, u32[]{:S(2)}) %collective-permute-start) | collective-permute-done | bytes 262176 | tf_op jit(solution)/shard_map/ppermute | solution.py:20
  30.3 10.2 %collective-permute-done.4.refs_2_ = bf16[2,256,512]{2,1,0:T(8,128)(2,1)S(1)} collective-permute-done((bf16[2,256,512]{2,1,0:T(8,128)(2,1)S(1)}, bf16[2,256,512]{2,1,0:T(8,128)(2,1)S(1)}, u32[]{:S(2)}, u32[]{:S(2)}) %collective-permute-start.4) | collective-permute-done | bytes 524320 | tf_op jit(solution)/shard_map/ppermute | solution.py:20
  40.5 1.9 %collective-permute-done.5.refs_3_ = bf16[2,256,512]{2,1,0:T(8,128)(2,1)S(1)} collective-permute-done((bf16[2,256,512]{2,1,0:T(8,128)(2,1)S(1)}, bf16[2,256,512]{2,1,0:T(8,128)(2,1)S(1)}, u32[]{:S(2)}, u32[]{:S(2)}) %collective-permute-start.5) | collective-permute-done | bytes 524320 | tf_op jit(solution)/shard_map/ppermute | solution.py:20
  42.5 4.4 %shard_map.103.refs_0_ = bf16[128,2048]{1,0:T(8,128)(2,1)S(1)} custom-call(s32[3]{0:T(128)S(1)} %pad_add_fusion.2.scalars, bf16[2,2,64,2048]{3,2,1,0:T(8,128)(2,1)S(1)} %bitcast.18, bf16[2,256,512]{2,1,0:T(8,128)(2,1)S(1)} %bitcast.16, bf16[2,256,512]{2,1,0:T(8,128)(2,1)S(1)} %collective-permute-done.3.refs_1_, ...), custom_call_target="tpu_custom_call" | custom-call | flops 1 | bytes 1 | tf_op jit(solution)/shard_map/pallas_call | solution.py:255
  46.9 3.8 %collective-permute-start.8 = (bf16[128,2048]{1,0:T(8,128)(2,1)S(1)}, bf16[128,2048]{1,0:T(8,128)(2,1)S(1)}, u32[]{:S(2)}, u32[]{:S(2)}) collective-permute-start(bf16[128,2048]{1,0:T(8,128)(2,1)S(1)} %shard_map.103.refs_0_), channel_id=1, source_target_pairs={{0,12},{4,8},{8,4},{12,0},{1,13},{5,9},{9,5},{13,1},{2,14},{6,10},... | collective-permute-start | bytes 1572872 | tf_op jit(solution)/shard_map/ppermute | solution.py:20
  50.7 5.3 %collective-permute-start.9 = (bf16[128,2048]{1,0:T(8,128)(2,1)S(1)}, bf16[128,2048]{1,0:T(8,128)(2,1)}, u32[]{:S(2)}, u32[]{:S(2)}) collective-permute-start(bf16[128,2048]{1,0:T(8,128)(2,1)S(1)} %shard_map.103.refs_0_), channel_id=1, source_target_pairs={{0,4},{4,0},{8,12},{12,8},{1,5},{5,1},{9,13},{13,9},{2,6},{6,2},{1... | collective-permute-start | bytes 1572872 | tf_op jit(solution)/shard_map/ppermute | solution.py:20
  56.0 4.4 %shard_map.102.refs_1_ = bf16[128,2048]{1,0:T(8,128)(2,1)S(1)} custom-call(s32[3]{0:T(128)S(1)} %pad_add_fusion.2.scalars, bf16[2,2,64,2048]{3,2,1,0:T(8,128)(2,1)S(1)} %bitcast.19, bf16[2,256,512]{2,1,0:T(8,128)(2,1)S(1)} %bitcast.17, bf16[2,256,512]{2,1,0:T(8,128)(2,1)S(1)} %collective-permute-done.3.refs_1_, ...), custom_call_target="tpu_custom_call" | custom-call | flops 1 | bytes 1 | tf_op jit(solution)/shard_map/pallas_call | solution.py:255
  61.4 3.4 %copy-done = bf16[2048,2048]{1,0:T(8,128)(2,1)S(1)} copy-done((bf16[2048,2048]{1,0:T(8,128)(2,1)S(1)}, bf16[2048,2048]{1,0:T(8,128)(2,1)}, u32[]{:S(2)}) %copy-start) | copy-done | bytes 8388632
  64.8 3.6 %shard_map.104 = (f32[128,2048]{1,0:T(8,128)S(1)}, bf16[128,2048]{1,0:T(8,128)(2,1)S(1)}) custom-call(s32[1]{0:T(128)} %bitcast.1.share, bf16[128,2048]{1,0:T(8,128)(2,1)S(1)} %shard_map.103.refs_0_, bf16[128,2048]{1,0:T(8,128)(2,1)S(1)} %shard_map.102.refs_1_, bf16[2048,2048]{1,0:T(8,128)(2,1)S(1)} %copy-done), custom_call_target="tpu_custom_call" | custom-call | flops 1 | bytes 1 | tf_op jit(solution)/shard_map/pallas_call | solution.py:56
  70.2 4.8 %collective-permute-done.9.refs_0_ = bf16[128,2048]{1,0:T(8,128)(2,1)} collective-permute-done((bf16[128,2048]{1,0:T(8,128)(2,1)S(1)}, bf16[128,2048]{1,0:T(8,128)(2,1)}, u32[]{:S(2)}, u32[]{:S(2)}) %collective-permute-start.9) | collective-permute-done | bytes 524320 | tf_op jit(solution)/shard_map/ppermute | solution.py:20
  75.0 3.4 %copy-done.1 = bf16[2048,2048]{1,0:T(8,128)(2,1)S(1)} copy-done((bf16[2048,2048]{1,0:T(8,128)(2,1)S(1)}, bf16[2048,2048]{1,0:T(8,128)(2,1)}, u32[]{:S(2)}) %copy-start.1) | copy-done | bytes 8388632
  78.4 4.6 %shard_map.105 = (f32[64,2048]{1,0:T(8,128)S(1)}, bf16[64,2048]{1,0:T(8,128)(2,1)S(1)}, bf16[64,2048]{1,0:T(8,128)(2,1)S(1)}, bf16[64,2048]{1,0:T(8,128)(2,1)S(1)}) custom-call(s32[1]{0:T(128)} %bitcast.1.share, bf16[128,2048]{1,0:T(8,128)(2,1)} %collective-permute-done.9.refs_0_, bf16[128,2048]{1,0:T(8,128)(2,1)S(1)} %collective-permute-done.8.refs_1_, ...), custom_call_target="tpu_custom_call" | custom-call | flops 1 | bytes 1 | tf_op jit(solution)/shard_map/pallas_call | solution.py:56
  86.0 13.2 %collective-permute-start.15 = (bf16[128,2048]{1,0:T(8,128)(2,1)S(1)}, bf16[128,2048]{1,0:T(8,128)(2,1)S(1)}, u32[]{:S(2)}, u32[]{:S(2)}) collective-permute-start(bf16[128,2048]{1,0:T(8,128)(2,1)S(1)} %broadcast_select_fusion.1), channel_id=1, source_target_pairs={{0,8},{12,4},{4,0},{8,12},{1,9},{13,5},{5,1},{9,13},{2,10},{14,6},... | collective-permute-start | bytes 1572872 | tf_op jit(solution)/shard_map/ppermute | solution.py:27
  100.5 3.6 %shard_map.106 = (f32[128,2048]{1,0:T(8,128)S(1)}, bf16[128,2048]{1,0:T(8,128)(2,1)S(1)}) custom-call(s32[1]{0:T(128)} %bitcast.1.share, bf16[128,2048]{1,0:T(8,128)(2,1)S(1)} %collective-permute-done.7.refs_0_, bf16[128,2048]{1,0:T(8,128)(2,1)S(1)} %collective-permute-done.6.refs_1_, bf16[2048,2048]{1,0:T(8,128)(2,1)S(1)} %bitcast.11), custom_call_target="tpu_custom_call" | custom-call | flops 1 | bytes 1 | tf_op jit(solution)/shard_map/pallas_call | solution.py:56
  108.1 3.5 %collective-permute-done.15.refs_0_ = bf16[128,2048]{1,0:T(8,128)(2,1)S(1)} collective-permute-done((bf16[128,2048]{1,0:T(8,128)(2,1)S(1)}, bf16[128,2048]{1,0:T(8,128)(2,1)S(1)}, u32[]{:S(2)}, u32[]{:S(2)}) %collective-permute-start.15) | collective-permute-done | bytes 524320 | tf_op jit(solution)/shard_map/ppermute | solution.py:27
  111.6 2.5 %shard_map.107 = (f32[64,2048]{1,0:T(8,128)S(1)}, bf16[64,2048]{1,0:T(8,128)(2,1)S(1)}) custom-call(s32[1]{0:T(128)} %bitcast.1.share, bf16[128,2048]{1,0:T(8,128)(2,1)S(1)} %collective-permute-done.15.refs_0_, bf16[2048,2048]{1,0:T(8,128)(2,1)S(1)} %bitcast.11), custom_call_target="tpu_custom_call" | custom-call | flops 1 | bytes 1 | tf_op jit(solution)/shard_map/pallas_call | solution.py:56
  118.6 4.3 %collective-permute-done.20.refs_0_ = bf16[128,2048]{1,0:T(8,128)(2,1)} collective-permute-done((bf16[128,2048]{1,0:T(8,128)(2,1)}, bf16[128,2048]{1,0:T(8,128)(2,1)}, u32[]{:S(2)}, u32[]{:S(2)}) %collective-permute-start.20) | collective-permute-done | bytes 524320 | tf_op jit(solution)/shard_map/ppermute | solution.py:27
  122.9 5.8 %shard_map.108 = (f32[64,2048]{1,0:T(8,128)}, bf16[64,2048]{1,0:T(8,128)(2,1)}) custom-call(s32[1]{0:T(128)} %bitcast.1.share, bf16[128,2048]{1,0:T(8,128)(2,1)} %collective-permute-done.20.refs_0_, bf16[2048,2048]{1,0:T(8,128)(2,1)} %refs_1_.3), custom_call_target="tpu_custom_call" | custom-call | flops 1 | bytes 1 | tf_op jit(solution)/shard_map/pallas_call | solution.py:56
  129.4 3.4 %collective-permute-start.23 = (bf16[32,2048]{1,0:T(8,128)(2,1)S(1)}, bf16[32,2048]{1,0:T(8,128)(2,1)S(1)}, u32[]{:S(2)}, u32[]{:S(2)}) collective-permute-start(bf16[32,2048]{1,0:T(8,128)(2,1)S(1)} %add_convert_fusion.9), channel_id=1, source_target_pairs={{0,8},{4,12},{8,0},{12,4},{1,9},{5,13},{9,1},{13,5},{2,10},{6,14},... | collective-permute-start | bytes 393224 | tf_op jit(solution)/shard_map/ppermute | solution.py:20
  143.6 2.1 %collective-permute-done.27 = bf16[32,2048]{1,0:T(8,128)(2,1)S(1)} collective-permute-done((bf16[32,2048]{1,0:T(8,128)(2,1)S(1)}, bf16[32,2048]{1,0:T(8,128)(2,1)S(1)}, u32[]{:S(2)}, u32[]{:S(2)}) %collective-permute-start.27) | collective-permute-done | bytes 131104 | tf_op jit(solution)/shard_map/ppermute | solution.py:20
  148.7 5.3 %collective-permute-done.29 = bf16[32,2048]{1,0:T(8,128)(2,1)S(1)} collective-permute-done((bf16[32,2048]{1,0:T(8,128)(2,1)S(1)}, bf16[32,2048]{1,0:T(8,128)(2,1)S(1)}, u32[]{:S(2)}, u32[]{:S(2)}) %collective-permute-start.29) | collective-permute-done | bytes 131104 | tf_op jit(solution)/shard_map/ppermute | solution.py:20
  (107 shorter events, 40.5 us)
Async XLA Ops:
  4.3 22.7 %collective-permute-start = (bf16[8,32,512]{2,1,0:T(8,128)(2,1)}, bf16[8,32,512]{2,1,0:T(8,128)(2,1)S(1)}, u32[]{:S(2)}, u32[]{:S(2)}) collective-permute-start(bf16[8,32,512]{2,1,0:T(8,128)(2,1)} %get-tuple-element.64), channel_id=1, source_target_pairs={{0,8},{4,12},{8,0},{12,4},{1,9},{5,13},{9,1},{13,5},{2,10},{6,14},... | collective-permute-start | bytes 786440 | tf_op jit(solution)/shard_map/ppermute | solution.py:20
  8.4 18.6 %collective-permute-start.1 = (bf16[8,32,512]{2,1,0:T(8,128)(2,1)}, bf16[8,32,512]{2,1,0:T(8,128)(2,1)S(1)}, u32[]{:S(2)}, u32[]{:S(2)}) collective-permute-start(bf16[8,32,512]{2,1,0:T(8,128)(2,1)} %get-tuple-element.65), channel_id=1, source_target_pairs={{0,12},{4,8},{8,4},{12,0},{1,13},{5,9},{9,5},{13,1},{2,14},{6,10},... | collective-permute-start | bytes 786440 | tf_op jit(solution)/shard_map/ppermute | solution.py:20
  9.8 17.7 %collective-permute-start.2 = (bf16[8,32,512]{2,1,0:T(8,128)(2,1)}, bf16[8,32,512]{2,1,0:T(8,128)(2,1)S(1)}, u32[]{:S(2)}, u32[]{:S(2)}) collective-permute-start(bf16[8,32,512]{2,1,0:T(8,128)(2,1)} %get-tuple-element.66), channel_id=1, source_target_pairs={{0,4},{4,0},{8,12},{12,8},{1,5},{5,1},{9,13},{13,9},{2,6},{6,2},{1... | collective-permute-start | bytes 786440 | tf_op jit(solution)/shard_map/ppermute | solution.py:20
  28.7 11.9 %collective-permute-start.4 = (bf16[2,256,512]{2,1,0:T(8,128)(2,1)S(1)}, bf16[2,256,512]{2,1,0:T(8,128)(2,1)S(1)}, u32[]{:S(2)}, u32[]{:S(2)}) collective-permute-start(bf16[2,256,512]{2,1,0:T(8,128)(2,1)S(1)} %bitcast.14), channel_id=1, source_target_pairs={{0,2},{2,0},{1,3},{3,1},{4,6},{6,4},{5,7},{7,5},{8,10},{10,8},{9,1... | collective-permute-start | bytes 1572872 | tf_op jit(solution)/shard_map/ppermute | solution.py:20
  30.3 10.2 %collective-permute-start.3 = (bf16[2,256,512]{2,1,0:T(8,128)(2,1)S(1)}, bf16[2,256,512]{2,1,0:T(8,128)(2,1)S(1)}, u32[]{:S(2)}, u32[]{:S(2)}) collective-permute-start(bf16[2,256,512]{2,1,0:T(8,128)(2,1)S(1)} %bitcast.15), channel_id=1, source_target_pairs={{0,1},{1,0},{2,3},{3,2},{4,5},{5,4},{6,7},{7,6},{8,9},{9,8},{10,11... | collective-permute-start | bytes 1572872 | tf_op jit(solution)/shard_map/ppermute | solution.py:20
  46.9 23.3 %collective-permute-start.8 = (bf16[128,2048]{1,0:T(8,128)(2,1)S(1)}, bf16[128,2048]{1,0:T(8,128)(2,1)S(1)}, u32[]{:S(2)}, u32[]{:S(2)}) collective-permute-start(bf16[128,2048]{1,0:T(8,128)(2,1)S(1)} %shard_map.103.refs_0_), channel_id=1, source_target_pairs={{0,12},{4,8},{8,4},{12,0},{1,13},{5,9},{9,5},{13,1},{2,14},{6,10},... | collective-permute-start | bytes 1572872 | tf_op jit(solution)/shard_map/ppermute | solution.py:20
  50.7 24.3 %collective-permute-start.9 = (bf16[128,2048]{1,0:T(8,128)(2,1)S(1)}, bf16[128,2048]{1,0:T(8,128)(2,1)}, u32[]{:S(2)}, u32[]{:S(2)}) collective-permute-start(bf16[128,2048]{1,0:T(8,128)(2,1)S(1)} %shard_map.103.refs_0_), channel_id=1, source_target_pairs={{0,4},{4,0},{8,12},{12,8},{1,5},{5,1},{9,13},{13,9},{2,6},{6,2},{1... | collective-permute-start | bytes 1572872 | tf_op jit(solution)/shard_map/ppermute | solution.py:20
  60.4 25.7 %collective-permute-start.6 = (bf16[128,2048]{1,0:T(8,128)(2,1)S(1)}, bf16[128,2048]{1,0:T(8,128)(2,1)S(1)}, u32[]{:S(2)}, u32[]{:S(2)}) collective-permute-start(bf16[128,2048]{1,0:T(8,128)(2,1)S(1)} %shard_map.102.refs_1_), channel_id=1, source_target_pairs={{0,12},{4,8},{8,4},{12,0},{1,13},{5,9},{9,5},{13,1},{2,14},{6,10},... | collective-permute-start | bytes 1572872 | tf_op jit(solution)/shard_map/ppermute | solution.py:20
  61.4 37.8 %collective-permute-start.7 = (bf16[128,2048]{1,0:T(8,128)(2,1)S(1)}, bf16[128,2048]{1,0:T(8,128)(2,1)S(1)}, u32[]{:S(2)}, u32[]{:S(2)}) collective-permute-start(bf16[128,2048]{1,0:T(8,128)(2,1)S(1)} %shard_map.102.refs_1_), channel_id=1, source_target_pairs={{0,4},{4,0},{8,12},{12,8},{1,5},{5,1},{9,13},{13,9},{2,6},{6,2},{1... | collective-permute-start | bytes 1572872 | tf_op jit(solution)/shard_map/ppermute | solution.py:20
  83.0 16.2 %collective-permute-start.10 = (bf16[64,2048]{1,0:T(8,128)(2,1)S(1)}, bf16[64,2048]{1,0:T(8,128)(2,1)S(1)}, u32[]{:S(2)}, u32[]{:S(2)}) collective-permute-start(bf16[64,2048]{1,0:T(8,128)(2,1)S(1)} %get-tuple-element.76), channel_id=1, source_target_pairs={{0,1},{1,0},{2,3},{3,2},{4,5},{5,4},{6,7},{7,6},{8,9},{9,8},{10,11... | collective-permute-start | bytes 786440 | tf_op jit(solution)/shard_map/ppermute | solution.py:20
  83.1 16.2 %collective-permute-start.11 = (bf16[64,2048]{1,0:T(8,128)(2,1)S(1)}, bf16[64,2048]{1,0:T(8,128)(2,1)S(1)}, u32[]{:S(2)}, u32[]{:S(2)}) collective-permute-start(bf16[64,2048]{1,0:T(8,128)(2,1)S(1)} %get-tuple-element.77), channel_id=1, source_target_pairs={{0,2},{1,3},{2,0},{3,1},{4,6},{5,7},{6,4},{7,5},{8,10},{9,11},{10,... | collective-permute-start | bytes 786440 | tf_op jit(solution)/shard_map/ppermute | solution.py:20
  84.5 14.8 %collective-permute-start.12 = (bf16[64,2048]{1,0:T(8,128)(2,1)S(1)}, bf16[64,2048]{1,0:T(8,128)(2,1)S(1)}, u32[]{:S(2)}, u32[]{:S(2)}) collective-permute-start(bf16[64,2048]{1,0:T(8,128)(2,1)S(1)} %get-tuple-element.78), channel_id=1, source_target_pairs={{0,3},{1,2},{2,1},{3,0},{4,7},{5,6},{6,5},{7,4},{8,11},{9,10},{10,... | collective-permute-start | bytes 786440 | tf_op jit(solution)/shard_map/ppermute | solution.py:20
  86.0 25.5 %collective-permute-start.15 = (bf16[128,2048]{1,0:T(8,128)(2,1)S(1)}, bf16[128,2048]{1,0:T(8,128)(2,1)S(1)}, u32[]{:S(2)}, u32[]{:S(2)}) collective-permute-start(bf16[128,2048]{1,0:T(8,128)(2,1)S(1)} %broadcast_select_fusion.1), channel_id=1, source_target_pairs={{0,8},{12,4},{4,0},{8,12},{1,9},{13,5},{5,1},{9,13},{2,10},{14,6},... | collective-permute-start | bytes 1572872 | tf_op jit(solution)/shard_map/ppermute | solution.py:27
  100.1 22.8 %collective-permute-start.20 = (bf16[128,2048]{1,0:T(8,128)(2,1)}, bf16[128,2048]{1,0:T(8,128)(2,1)}, u32[]{:S(2)}, u32[]{:S(2)}) collective-permute-start(bf16[128,2048]{1,0:T(8,128)(2,1)} %broadcast_select_fusion), channel_id=1, source_target_pairs={{0,8},{12,4},{4,0},{8,12},{1,9},{13,5},{5,1},{9,13},{2,10},{14,6},... | collective-permute-start | bytes 1572872 | tf_op jit(solution)/shard_map/ppermute | solution.py:27
  105.1 23.7 %collective-permute-start.13 = (bf16[32,2048]{1,0:T(8,128)(2,1)}, bf16[32,2048]{1,0:T(8,128)(2,1)}, u32[]{:S(2)}, u32[]{:S(2)}) collective-permute-start(bf16[32,2048]{1,0:T(8,128)(2,1)} %get-tuple-element.124), channel_id=1, source_target_pairs={{0,4},{4,0},{8,12},{12,8},{1,5},{5,1},{9,13},{13,9},{2,6},{6,2},{1... | collective-permute-start | bytes 393224 | tf_op jit(solution)/shard_map/ppermute | solution.py:20
  106.7 22.0 %collective-permute-start.14 = (bf16[32,2048]{1,0:T(8,128)(2,1)}, bf16[32,2048]{1,0:T(8,128)(2,1)}, u32[]{:S(2)}, u32[]{:S(2)}) collective-permute-start(bf16[32,2048]{1,0:T(8,128)(2,1)} %get-tuple-element.123), channel_id=1, source_target_pairs={{0,12},{4,8},{8,4},{12,0},{1,13},{5,9},{9,5},{13,1},{2,14},{6,10},... | collective-permute-start | bytes 393224 | tf_op jit(solution)/shard_map/ppermute | solution.py:20
  115.0 13.8 %collective-permute-start.17 = (bf16[64,2048]{1,0:T(8,128)(2,1)}, bf16[64,2048]{1,0:T(8,128)(2,1)S(1)}, u32[]{:S(2)}, u32[]{:S(2)}) collective-permute-start(bf16[64,2048]{1,0:T(8,128)(2,1)} %add_convert_fusion.1), channel_id=1, source_target_pairs={{0,2},{2,0},{1,3},{3,1},{4,6},{6,4},{5,7},{7,5},{8,10},{10,8},{9,1... | collective-permute-start | bytes 786440 | tf_op jit(solution)/shard_map/ppermute | solution.py:20
  117.8 10.9 %collective-permute-start.19 = (bf16[32,2048]{1,0:T(8,128)(2,1)}, bf16[32,2048]{1,0:T(8,128)(2,1)S(1)}, u32[]{:S(2)}, u32[]{:S(2)}) collective-permute-start(bf16[32,2048]{1,0:T(8,128)(2,1)} %add_convert_fusion.10), channel_id=1, source_target_pairs={{0,2},{2,0},{1,3},{3,1},{4,6},{6,4},{5,7},{7,5},{8,10},{10,8},{9,1... | collective-permute-start | bytes 393224 | tf_op jit(solution)/shard_map/ppermute | solution.py:20
  128.8 9.2 %collective-permute-start.26 = (bf16[128,2048]{1,0:T(8,128)(2,1)S(1)}, bf16[128,2048]{1,0:T(8,128)(2,1)S(1)}, u32[]{:S(2)}, u32[]{:S(2)}) collective-permute-start(bf16[128,2048]{1,0:T(8,128)(2,1)S(1)} %copy-done.6), channel_id=1, source_target_pairs={{0,1},{1,0},{2,3},{3,2},{4,5},{5,4},{6,7},{7,6},{8,9},{9,8},{10,11... | collective-permute-start | bytes 1572872 | tf_op jit(solution)/shard_map/ppermute | solution.py:20
  129.4 11.2 %collective-permute-start.23 = (bf16[32,2048]{1,0:T(8,128)(2,1)S(1)}, bf16[32,2048]{1,0:T(8,128)(2,1)S(1)}, u32[]{:S(2)}, u32[]{:S(2)}) collective-permute-start(bf16[32,2048]{1,0:T(8,128)(2,1)S(1)} %add_convert_fusion.9), channel_id=1, source_target_pairs={{0,8},{4,12},{8,0},{12,4},{1,9},{5,13},{9,1},{13,5},{2,10},{6,14},... | collective-permute-start | bytes 393224 | tf_op jit(solution)/shard_map/ppermute | solution.py:20
  133.0 10.6 %collective-permute-start.21 = (bf16[32,2048]{1,0:T(8,128)(2,1)S(1)}, bf16[32,2048]{1,0:T(8,128)(2,1)S(1)}, u32[]{:S(2)}, u32[]{:S(2)}) collective-permute-start(bf16[32,2048]{1,0:T(8,128)(2,1)S(1)} %get-tuple-element.122), channel_id=1, source_target_pairs={{0,4},{4,0},{8,12},{12,8},{1,5},{5,1},{9,13},{13,9},{2,6},{6,2},{1... | collective-permute-start | bytes 393224 | tf_op jit(solution)/shard_map/ppermute | solution.py:20
  133.4 10.2 %collective-permute-start.22 = (bf16[32,2048]{1,0:T(8,128)(2,1)S(1)}, bf16[32,2048]{1,0:T(8,128)(2,1)S(1)}, u32[]{:S(2)}, u32[]{:S(2)}) collective-permute-start(bf16[32,2048]{1,0:T(8,128)(2,1)S(1)} %get-tuple-element.121), channel_id=1, source_target_pairs={{0,12},{4,8},{8,4},{12,0},{1,13},{5,9},{9,5},{13,1},{2,14},{6,10},... | collective-permute-start | bytes 393224 | tf_op jit(solution)/shard_map/ppermute | solution.py:20
  138.1 7.6 %collective-permute-start.27 = (bf16[32,2048]{1,0:T(8,128)(2,1)S(1)}, bf16[32,2048]{1,0:T(8,128)(2,1)S(1)}, u32[]{:S(2)}, u32[]{:S(2)}) collective-permute-start(bf16[32,2048]{1,0:T(8,128)(2,1)S(1)} %get-tuple-element.120), channel_id=1, source_target_pairs={{0,2},{2,0},{1,3},{3,1},{4,6},{6,4},{5,7},{7,5},{8,10},{10,8},{9,1... | collective-permute-start | bytes 393224 | tf_op jit(solution)/shard_map/ppermute | solution.py:20
  140.6 8.0 %collective-permute-start.28 = (bf16[32,2048]{1,0:T(8,128)(2,1)S(1)}, bf16[32,2048]{1,0:T(8,128)(2,1)S(1)}, u32[]{:S(2)}, u32[]{:S(2)}) collective-permute-start(bf16[32,2048]{1,0:T(8,128)(2,1)S(1)} %get-tuple-element.119), channel_id=1, source_target_pairs={{0,2},{2,0},{1,3},{3,1},{4,6},{6,4},{5,7},{7,5},{8,10},{10,8},{9,1... | collective-permute-start | bytes 393224 | tf_op jit(solution)/shard_map/ppermute | solution.py:20
  (20 other events, 218.5 us)

commit v21 on v19

--- a/solution.py
+++ b/solution.py
@@ -28,19 +28,24 @@
 
 
 def project_kernel(block_count, flips, share, *refs):
-    blocks, weight, outs = refs[:block_count], refs[block_count], refs[block_count + 1 :]
-    picked = []
+    blocks, weight = refs[:block_count], refs[block_count]
+    outs, rows = refs[block_count + 1 : -1], refs[-1]
+    done = 0
     for flip in flips:
         for block in blocks:
             part_rows = block.shape[0] // len(flips)
             start = pl.multiple_of((share[0] ^ flip) * part_rows, part_rows)
-            picked.append(block[pl.ds(start, part_rows), :])
-    product = jnp.dot(
-        jnp.concatenate(picked, axis=0), weight[...], preferred_element_type=jnp.float32
-    )
-    rows = product.shape[0] // len(outs)
-    for i, out in enumerate(outs):
-        out[...] = product[i * rows : (i + 1) * rows].astype(out.dtype)
+            rows[done : done + part_rows, :] = block[pl.ds(start, part_rows), :]
+            done += part_rows
+    columns = weight.shape[1]
+    tile = min(columns, 512)
+    each = rows.shape[0] // len(outs)
+    for n in range(0, columns, tile):
+        product = jnp.dot(
+            rows[...], weight[:, n : n + tile], preferred_element_type=jnp.float32
+        )
+        for i, out in enumerate(outs):
+            out[:, n : n + tile] = product[i * each : (i + 1) * each].astype(out.dtype)
 
 
 def project_out(blocks, out_weight, direct=False):
@@ -51,22 +56,19 @@
     flips = [*range(0, share_count, 2), *range(1, share_count, 2)]
     count = share_count if direct else 2
     rows = sum(block.shape[0] for block in blocks) // count
-    tile = min(columns, 512)
     whole = pl.BlockSpec(memory_space=pltpu.VMEM)
     return pl.pallas_call(
         functools.partial(
             project_kernel, len(blocks), list(range(share_count)) if direct else flips
         ),
-        grid=(columns // tile,),
-        in_specs=[pl.BlockSpec(memory_space=pltpu.SMEM)]
-        + [whole for _ in blocks]
-        + [pl.BlockSpec((depth, tile), lambda n: (0, n))],
-        out_specs=[pl.BlockSpec((rows, tile), lambda n: (0, n))] * count,
+        in_specs=[pl.BlockSpec(memory_space=pltpu.SMEM)] + [whole] * (len(blocks) + 1),
+        out_specs=[whole] * count,
         out_shape=[
             jax.ShapeDtypeStruct((rows, columns), jnp.bfloat16 if i else jnp.float32)
             for i in range(count)
         ],
-        compiler_params=pltpu.CompilerParams(vmem_limit_bytes=10 * 1024 * 1024),
+        scratch_shapes=[pltpu.VMEM((rows * count, depth), jnp.bfloat16)],
+        compiler_params=pltpu.CompilerParams(vmem_limit_bytes=24 * 1024 * 1024),
         cost_estimate=LIGHT,
     )(share, *blocks, out_weight)
 

time: 154 us -> 155 us (level)
  waiting for transfers between devices: 45.5 us -> 51.9 us
  Pallas kernels: 29.6 us -> 23.6 us
    pallas_call x5, Pallas kernels: 15.9 us -> 9.82 us  [project_out(): pl.pallas_call(functools.partial(project_kernel, len(blocks), list(range(...]
    ppermute x28, waiting for transfers between devices: 38.5 us -> 42.3 us  [swap(): lax.ppermute(values, axis, [(i, i ^ flip) for i in range(lax.axis_size(ax...]
    ppermute x2, waiting for transfers between devices: 7.06 us -> 9.53 us  [second_hop(): return lax.ppermute(passed, 'pool', [(0, 2), (3, 1), (1, 0), (2, 3)])]
  transfers between devices with their start and end apart: 30 -> 30, of which waited for: 12 -> 13; matrix products, arithmetic and copies ran while one was open for 8% -> 8% of each run, Pallas kernels for 13% -> 9%
where the time goes in v21:
time: 155 us; the launch traced here: 154 us
  waiting for transfers between devices  51.9 us (33%)
  starting transfers between devices  50.3 us (32%)
  Pallas kernels  23.6 us (15%)
  local copies, waits for them, and re-layouts  21.9 us (14%)
  other arithmetic  5.96 us (4%)
    ppermute x28, waiting for transfers between devices, swap(): lax.ppermute(values, axis, [(i, i ^ flip) for i in range(lax.axis_size(ax...  42.3 us
    ppermute x28, starting transfers between devices, swap(): lax.ppermute(values, axis, [(i, i ^ flip) for i in range(lax.axis_size(ax...  37 us
    unnamed x38, local copies, waits for them, and re-layouts  13.7 us
    ppermute x2, starting transfers between devices, second_hop(): return lax.ppermute(passed, 'pool', [(0, 2), (3, 1), (1, 0), (2, 3)])  13.3 us
    pallas_call x5, Pallas kernels, project_out(): pl.pallas_call(functools.partial(project_kernel, len(blocks), list(range(...  9.82 us
    ppermute x2, waiting for transfers between devices, second_hop(): return lax.ppermute(passed, 'pool', [(0, 2), (3, 1), (1, 0), (2, 3)])  9.53 us
    pallas_call x2, Pallas kernels, attend(): pl.pallas_call(functools.partial(attend_kernel, start, rows, len(parts)),...  8.82 us
    pallas_call x1, Pallas kernels, fetch(): pl.pallas_call(functools.partial(fetch_kernel, pool_size=pool_size, share...  3.81 us
  transfers between devices with their start and end apart: 30, of which 13 were waited for; matrix products, arithmetic and copies ran while one was open for 8% of the time, Pallas kernels for 9%

profile of v21, /device:TPU:0, one launch (start us, length us, event | category | flops | bytes accessed | tf_op | source)
XLA Modules:
  0.0 154.0 jit_solution(7250601502554712654)
XLA Ops:
  0.6 3.8 %shard_map.100 = (s32[2,16]{1,0:T(2,128)}, bf16[8,32,512]{2,1,0:T(8,128)(2,1)}, bf16[8,32,512]{2,1,0:T(8,128)(2,1)}, bf16[8,32,512]{2,1,0:T(8,128)(2,1)}, bf16[8,32,512]{2,1,0:T(8,128)(2,1)}) custom-call(s32[2]{0:T(128)} %pad_add_fusion.1.place, s32[8,8]{1,0:T(8,128)} %holder.1, s32[8,8]{1,0:T(8,128)} %block.1, s32[8]{0:T(128)} %serving.1, ...), custom_call_target="tpu_custom_call" | custom-call | flops 1 | bytes 1 | tf_op jit(solution)/shard_map/pallas_call | solution.py:156
  4.4 3.7 %collective-permute-start = (bf16[8,32,512]{2,1,0:T(8,128)(2,1)}, bf16[8,32,512]{2,1,0:T(8,128)(2,1)S(1)}, u32[]{:S(2)}, u32[]{:S(2)}) collective-permute-start(bf16[8,32,512]{2,1,0:T(8,128)(2,1)} %get-tuple-element.64), channel_id=1, source_target_pairs={{0,8},{4,12},{8,0},{12,4},{1,9},{5,13},{9,1},{13,5},{2,10},{6,14},... | collective-permute-start | bytes 786440 | tf_op jit(solution)/shard_map/ppermute | solution.py:20
  14.2 2.3 %reshape.24 = bf16[512,2,256]{2,1,0:T(2,128)(2,1)S(1)} reshape(bf16[512,2,2,128]{3,2,1,0:T(2,128)(2,1)} %param.12) | data formatting | bytes 1048576 | tf_op jit(solution)/shard_map/reshape | solution.py:296
  17.3 9.4 %collective-permute-done.refs_1_ = bf16[8,32,512]{2,1,0:T(8,128)(2,1)S(1)} collective-permute-done((bf16[8,32,512]{2,1,0:T(8,128)(2,1)}, bf16[8,32,512]{2,1,0:T(8,128)(2,1)S(1)}, u32[]{:S(2)}, u32[]{:S(2)}) %collective-permute-start) | collective-permute-done | bytes 262176 | tf_op jit(solution)/shard_map/ppermute | solution.py:20
  28.4 2.1 %collective-permute-start.4 = (bf16[2,256,512]{2,1,0:T(8,128)(2,1)S(1)}, bf16[2,256,512]{2,1,0:T(8,128)(2,1)S(1)}, u32[]{:S(2)}, u32[]{:S(2)}) collective-permute-start(bf16[2,256,512]{2,1,0:T(8,128)(2,1)S(1)} %bitcast.14), channel_id=1, source_target_pairs={{0,2},{2,0},{1,3},{3,1},{4,6},{6,4},{5,7},{7,5},{8,10},{10,8},{9,1... | collective-permute-start | bytes 1572872 | tf_op jit(solution)/shard_map/ppermute | solution.py:20
  30.5 9.8 %collective-permute-done.4.refs_2_ = bf16[2,256,512]{2,1,0:T(8,128)(2,1)S(1)} collective-permute-done((bf16[2,256,512]{2,1,0:T(8,128)(2,1)S(1)}, bf16[2,256,512]{2,1,0:T(8,128)(2,1)S(1)}, u32[]{:S(2)}, u32[]{:S(2)}) %collective-permute-start.4) | collective-permute-done | bytes 524320 | tf_op jit(solution)/shard_map/ppermute | solution.py:20
  42.2 4.4 %shard_map.103.refs_0_ = bf16[128,2048]{1,0:T(8,128)(2,1)S(1)} custom-call(s32[3]{0:T(128)S(1)} %pad_add_fusion.2.scalars, bf16[2,2,64,2048]{3,2,1,0:T(8,128)(2,1)S(1)} %bitcast.18, bf16[2,256,512]{2,1,0:T(8,128)(2,1)S(1)} %bitcast.16, bf16[2,256,512]{2,1,0:T(8,128)(2,1)S(1)} %collective-permute-done.3.refs_1_, ...), custom_call_target="tpu_custom_call" | custom-call | flops 1 | bytes 1 | tf_op jit(solution)/shard_map/pallas_call | solution.py:257
  46.6 4.2 %collective-permute-start.8 = (bf16[128,2048]{1,0:T(8,128)(2,1)S(1)}, bf16[128,2048]{1,0:T(8,128)(2,1)S(1)}, u32[]{:S(2)}, u32[]{:S(2)}) collective-permute-start(bf16[128,2048]{1,0:T(8,128)(2,1)S(1)} %shard_map.103.refs_0_), channel_id=1, source_target_pairs={{0,12},{4,8},{8,4},{12,0},{1,13},{5,9},{9,5},{13,1},{2,14},{6,10},... | collective-permute-start | bytes 1572872 | tf_op jit(solution)/shard_map/ppermute | solution.py:20
  50.9 5.3 %collective-permute-start.9 = (bf16[128,2048]{1,0:T(8,128)(2,1)S(1)}, bf16[128,2048]{1,0:T(8,128)(2,1)S(1)}, u32[]{:S(2)}, u32[]{:S(2)}) collective-permute-start(bf16[128,2048]{1,0:T(8,128)(2,1)S(1)} %shard_map.103.refs_0_), channel_id=1, source_target_pairs={{0,4},{4,0},{8,12},{12,8},{1,5},{5,1},{9,13},{13,9},{2,6},{6,2},{1... | collective-permute-start | bytes 1572872 | tf_op jit(solution)/shard_map/ppermute | solution.py:20
  56.2 4.4 %shard_map.102.refs_1_ = bf16[128,2048]{1,0:T(8,128)(2,1)S(1)} custom-call(s32[3]{0:T(128)S(1)} %pad_add_fusion.2.scalars, bf16[2,2,64,2048]{3,2,1,0:T(8,128)(2,1)S(1)} %bitcast.19, bf16[2,256,512]{2,1,0:T(8,128)(2,1)S(1)} %bitcast.17, bf16[2,256,512]{2,1,0:T(8,128)(2,1)S(1)} %collective-permute-done.3.refs_1_, ...), custom_call_target="tpu_custom_call" | custom-call | flops 1 | bytes 1 | tf_op jit(solution)/shard_map/pallas_call | solution.py:257
  61.6 3.4 %copy-done = bf16[2048,2048]{1,0:T(8,128)(2,1)S(1)} copy-done((bf16[2048,2048]{1,0:T(8,128)(2,1)S(1)}, bf16[2048,2048]{1,0:T(8,128)(2,1)}, u32[]{:S(2)}) %copy-start) | copy-done | bytes 8388632
  65.0 2.4 %shard_map.104 = (f32[128,2048]{1,0:T(8,128)S(1)}, bf16[128,2048]{1,0:T(8,128)(2,1)S(1)}) custom-call(s32[1]{0:T(128)} %bitcast.1.share, bf16[128,2048]{1,0:T(8,128)(2,1)S(1)} %shard_map.103.refs_0_, bf16[128,2048]{1,0:T(8,128)(2,1)S(1)} %shard_map.102.refs_1_, bf16[2048,2048]{1,0:T(8,128)(2,1)S(1)} %copy-done), custom_call_target="tpu_custom_call" | custom-call | flops 1 | bytes 1 | tf_op jit(solution)/shard_map/pallas_call | solution.py:60
  69.2 5.8 %collective-permute-done.9.refs_0_ = bf16[128,2048]{1,0:T(8,128)(2,1)S(1)} collective-permute-done((bf16[128,2048]{1,0:T(8,128)(2,1)S(1)}, bf16[128,2048]{1,0:T(8,128)(2,1)S(1)}, u32[]{:S(2)}, u32[]{:S(2)}) %collective-permute-start.9) | collective-permute-done | bytes 524320 | tf_op jit(solution)/shard_map/ppermute | solution.py:20
  75.0 3.4 %copy-done.1 = bf16[2048,2048]{1,0:T(8,128)(2,1)S(1)} copy-done((bf16[2048,2048]{1,0:T(8,128)(2,1)S(1)}, bf16[2048,2048]{1,0:T(8,128)(2,1)}, u32[]{:S(2)}) %copy-start.1) | copy-done | bytes 8388632
  78.4 2.4 %shard_map.105 = (f32[64,2048]{1,0:T(8,128)S(1)}, bf16[64,2048]{1,0:T(8,128)(2,1)S(1)}, bf16[64,2048]{1,0:T(8,128)(2,1)S(1)}, bf16[64,2048]{1,0:T(8,128)(2,1)S(1)}) custom-call(s32[1]{0:T(128)} %bitcast.1.share, bf16[128,2048]{1,0:T(8,128)(2,1)S(1)} %collective-permute-done.9.refs_0_, bf16[128,2048]{1,0:T(8,128)(2,1)S(1)} %collective-permute-done.8.refs_1_, ...), custom_call_target="tpu_custom_call" | custom-call | flops 1 | bytes 1 | tf_op jit(solution)/shard_map/pallas_call | solution.py:60
  82.8 3.4 %collective-permute-done.6.refs_1_ = bf16[128,2048]{1,0:T(8,128)(2,1)S(1)} collective-permute-done((bf16[128,2048]{1,0:T(8,128)(2,1)S(1)}, bf16[128,2048]{1,0:T(8,128)(2,1)S(1)}, u32[]{:S(2)}, u32[]{:S(2)}) %collective-permute-start.6) | collective-permute-done | bytes 524320 | tf_op jit(solution)/shard_map/ppermute | solution.py:20
  86.1 13.3 %collective-permute-start.15 = (bf16[128,2048]{1,0:T(8,128)(2,1)S(1)}, bf16[128,2048]{1,0:T(8,128)(2,1)S(1)}, u32[]{:S(2)}, u32[]{:S(2)}) collective-permute-start(bf16[128,2048]{1,0:T(8,128)(2,1)S(1)} %broadcast_select_fusion.1), channel_id=1, source_target_pairs={{0,8},{12,4},{4,0},{8,12},{1,9},{13,5},{5,1},{9,13},{2,10},{14,6},... | collective-permute-start | bytes 1572872 | tf_op jit(solution)/shard_map/ppermute | solution.py:27
  101.5 2.4 %shard_map.106 = (f32[128,2048]{1,0:T(8,128)S(1)}, bf16[128,2048]{1,0:T(8,128)(2,1)S(1)}) custom-call(s32[1]{0:T(128)} %bitcast.1.share, bf16[128,2048]{1,0:T(8,128)(2,1)S(1)} %copy-done.7, bf16[128,2048]{1,0:T(8,128)(2,1)S(1)} %collective-permute-done.6.refs_1_, bf16[2048,2048]{1,0:T(8,128)(2,1)S(1)} %bitcast.11), custom_call_target="tpu_custom_call" | custom-call | flops 1 | bytes 1 | tf_op jit(solution)/shard_map/pallas_call | solution.py:60
  107.7 4.1 %collective-permute-done.15.refs_0_ = bf16[128,2048]{1,0:T(8,128)(2,1)S(1)} collective-permute-done((bf16[128,2048]{1,0:T(8,128)(2,1)S(1)}, bf16[128,2048]{1,0:T(8,128)(2,1)S(1)}, u32[]{:S(2)}, u32[]{:S(2)}) %collective-permute-start.15) | collective-permute-done | bytes 524320 | tf_op jit(solution)/shard_map/ppermute | solution.py:27
  117.7 5.5 %collective-permute-done.20.refs_0_ = bf16[128,2048]{1,0:T(8,128)(2,1)S(1)} collective-permute-done((bf16[128,2048]{1,0:T(8,128)(2,1)}, bf16[128,2048]{1,0:T(8,128)(2,1)S(1)}, u32[]{:S(2)}, u32[]{:S(2)}) %collective-permute-start.20) | collective-permute-done | bytes 524320 | tf_op jit(solution)/shard_map/ppermute | solution.py:27
  123.1 3.4 %copy-done.2 = bf16[2048,2048]{1,0:T(8,128)(2,1)S(1)} copy-done((bf16[2048,2048]{1,0:T(8,128)(2,1)S(1)}, bf16[2048,2048]{1,0:T(8,128)(2,1)}, u32[]{:S(2)}) %copy-start.2) | copy-done | bytes 8388632
  129.4 2.5 %collective-permute-start.23 = (bf16[32,2048]{1,0:T(8,128)(2,1)S(1)}, bf16[32,2048]{1,0:T(8,128)(2,1)S(1)}, u32[]{:S(2)}, u32[]{:S(2)}) collective-permute-start(bf16[32,2048]{1,0:T(8,128)(2,1)S(1)} %add_convert_fusion.9), channel_id=1, source_target_pairs={{0,8},{4,12},{8,0},{12,4},{1,9},{5,13},{9,1},{13,5},{2,10},{6,14},... | collective-permute-start | bytes 393224 | tf_op jit(solution)/shard_map/ppermute | solution.py:20
  144.0 2.8 %collective-permute-start.29 = (bf16[32,2048]{1,0:T(8,128)(2,1)S(1)}, bf16[32,2048]{1,0:T(8,128)(2,1)S(1)}, u32[]{:S(2)}, u32[]{:S(2)}) collective-permute-start(bf16[32,2048]{1,0:T(8,128)(2,1)S(1)} %add_convert_fusion.3), channel_id=1, source_target_pairs={{0,8},{4,12},{8,0},{12,4},{1,9},{5,13},{9,1},{13,5},{2,10},{6,14},... | collective-permute-start | bytes 393224 | tf_op jit(solution)/shard_map/ppermute | solution.py:20
  147.0 6.3 %collective-permute-done.29 = bf16[32,2048]{1,0:T(8,128)(2,1)S(1)} collective-permute-done((bf16[32,2048]{1,0:T(8,128)(2,1)S(1)}, bf16[32,2048]{1,0:T(8,128)(2,1)S(1)}, u32[]{:S(2)}, u32[]{:S(2)}) %collective-permute-start.29) | collective-permute-done | bytes 131104 | tf_op jit(solution)/shard_map/ppermute | solution.py:20
  (117 shorter events, 43.3 us)
Async XLA Ops:
  4.4 22.3 %collective-permute-start = (bf16[8,32,512]{2,1,0:T(8,128)(2,1)}, bf16[8,32,512]{2,1,0:T(8,128)(2,1)S(1)}, u32[]{:S(2)}, u32[]{:S(2)}) collective-permute-start(bf16[8,32,512]{2,1,0:T(8,128)(2,1)} %get-tuple-element.64), channel_id=1, source_target_pairs={{0,8},{4,12},{8,0},{12,4},{1,9},{5,13},{9,1},{13,5},{2,10},{6,14},... | collective-permute-start | bytes 786440 | tf_op jit(solution)/shard_map/ppermute | solution.py:20
  8.1 18.6 %collective-permute-start.1 = (bf16[8,32,512]{2,1,0:T(8,128)(2,1)}, bf16[8,32,512]{2,1,0:T(8,128)(2,1)S(1)}, u32[]{:S(2)}, u32[]{:S(2)}) collective-permute-start(bf16[8,32,512]{2,1,0:T(8,128)(2,1)} %get-tuple-element.65), channel_id=1, source_target_pairs={{0,12},{4,8},{8,4},{12,0},{1,13},{5,9},{9,5},{13,1},{2,14},{6,10},... | collective-permute-start | bytes 786440 | tf_op jit(solution)/shard_map/ppermute | solution.py:20
  9.8 17.5 %collective-permute-start.2 = (bf16[8,32,512]{2,1,0:T(8,128)(2,1)}, bf16[8,32,512]{2,1,0:T(8,128)(2,1)S(1)}, u32[]{:S(2)}, u32[]{:S(2)}) collective-permute-start(bf16[8,32,512]{2,1,0:T(8,128)(2,1)} %get-tuple-element.66), channel_id=1, source_target_pairs={{0,4},{4,0},{8,12},{12,8},{1,5},{5,1},{9,13},{13,9},{2,6},{6,2},{1... | collective-permute-start | bytes 786440 | tf_op jit(solution)/shard_map/ppermute | solution.py:20
  28.4 11.9 %collective-permute-start.4 = (bf16[2,256,512]{2,1,0:T(8,128)(2,1)S(1)}, bf16[2,256,512]{2,1,0:T(8,128)(2,1)S(1)}, u32[]{:S(2)}, u32[]{:S(2)}) collective-permute-start(bf16[2,256,512]{2,1,0:T(8,128)(2,1)S(1)} %bitcast.14), channel_id=1, source_target_pairs={{0,2},{2,0},{1,3},{3,1},{4,6},{6,4},{5,7},{7,5},{8,10},{10,8},{9,1... | collective-permute-start | bytes 1572872 | tf_op jit(solution)/shard_map/ppermute | solution.py:20
  30.5 9.8 %collective-permute-start.3 = (bf16[2,256,512]{2,1,0:T(8,128)(2,1)S(1)}, bf16[2,256,512]{2,1,0:T(8,128)(2,1)S(1)}, u32[]{:S(2)}, u32[]{:S(2)}) collective-permute-start(bf16[2,256,512]{2,1,0:T(8,128)(2,1)S(1)} %bitcast.15), channel_id=1, source_target_pairs={{0,1},{1,0},{2,3},{3,2},{4,5},{5,4},{6,7},{7,6},{8,9},{9,8},{10,11... | collective-permute-start | bytes 1572872 | tf_op jit(solution)/shard_map/ppermute | solution.py:20
  46.6 22.5 %collective-permute-start.8 = (bf16[128,2048]{1,0:T(8,128)(2,1)S(1)}, bf16[128,2048]{1,0:T(8,128)(2,1)S(1)}, u32[]{:S(2)}, u32[]{:S(2)}) collective-permute-start(bf16[128,2048]{1,0:T(8,128)(2,1)S(1)} %shard_map.103.refs_0_), channel_id=1, source_target_pairs={{0,12},{4,8},{8,4},{12,0},{1,13},{5,9},{9,5},{13,1},{2,14},{6,10},... | collective-permute-start | bytes 1572872 | tf_op jit(solution)/shard_map/ppermute | solution.py:20
  50.9 24.1 %collective-permute-start.9 = (bf16[128,2048]{1,0:T(8,128)(2,1)S(1)}, bf16[128,2048]{1,0:T(8,128)(2,1)S(1)}, u32[]{:S(2)}, u32[]{:S(2)}) collective-permute-start(bf16[128,2048]{1,0:T(8,128)(2,1)S(1)} %shard_map.103.refs_0_), channel_id=1, source_target_pairs={{0,4},{4,0},{8,12},{12,8},{1,5},{5,1},{9,13},{13,9},{2,6},{6,2},{1... | collective-permute-start | bytes 1572872 | tf_op jit(solution)/shard_map/ppermute | solution.py:20
  60.6 25.6 %collective-permute-start.6 = (bf16[128,2048]{1,0:T(8,128)(2,1)S(1)}, bf16[128,2048]{1,0:T(8,128)(2,1)S(1)}, u32[]{:S(2)}, u32[]{:S(2)}) collective-permute-start(bf16[128,2048]{1,0:T(8,128)(2,1)S(1)} %shard_map.102.refs_1_), channel_id=1, source_target_pairs={{0,12},{4,8},{8,4},{12,0},{1,13},{5,9},{9,5},{13,1},{2,14},{6,10},... | collective-permute-start | bytes 1572872 | tf_op jit(solution)/shard_map/ppermute | solution.py:20
  61.6 37.8 %collective-permute-start.7 = (bf16[128,2048]{1,0:T(8,128)(2,1)S(1)}, bf16[128,2048]{1,0:T(8,128)(2,1)S(1)}, u32[]{:S(2)}, u32[]{:S(2)}) collective-permute-start(bf16[128,2048]{1,0:T(8,128)(2,1)S(1)} %shard_map.102.refs_1_), channel_id=1, source_target_pairs={{0,4},{4,0},{8,12},{12,8},{1,5},{5,1},{9,13},{13,9},{2,6},{6,2},{1... | collective-permute-start | bytes 1572872 | tf_op jit(solution)/shard_map/ppermute | solution.py:20
  80.8 18.7 %collective-permute-start.10 = (bf16[64,2048]{1,0:T(8,128)(2,1)S(1)}, bf16[64,2048]{1,0:T(8,128)(2,1)S(1)}, u32[]{:S(2)}, u32[]{:S(2)}) collective-permute-start(bf16[64,2048]{1,0:T(8,128)(2,1)S(1)} %get-tuple-element.76), channel_id=1, source_target_pairs={{0,1},{1,0},{2,3},{3,2},{4,5},{5,4},{6,7},{7,6},{8,9},{9,8},{10,11... | collective-permute-start | bytes 786440 | tf_op jit(solution)/shard_map/ppermute | solution.py:20
  80.8 18.6 %collective-permute-start.11 = (bf16[64,2048]{1,0:T(8,128)(2,1)S(1)}, bf16[64,2048]{1,0:T(8,128)(2,1)S(1)}, u32[]{:S(2)}, u32[]{:S(2)}) collective-permute-start(bf16[64,2048]{1,0:T(8,128)(2,1)S(1)} %get-tuple-element.77), channel_id=1, source_target_pairs={{0,2},{1,3},{2,0},{3,1},{4,6},{5,7},{6,4},{7,5},{8,10},{9,11},{10,... | collective-permute-start | bytes 786440 | tf_op jit(solution)/shard_map/ppermute | solution.py:20
  82.4 17.1 %collective-permute-start.12 = (bf16[64,2048]{1,0:T(8,128)(2,1)S(1)}, bf16[64,2048]{1,0:T(8,128)(2,1)S(1)}, u32[]{:S(2)}, u32[]{:S(2)}) collective-permute-start(bf16[64,2048]{1,0:T(8,128)(2,1)S(1)} %get-tuple-element.78), channel_id=1, source_target_pairs={{0,3},{1,2},{2,1},{3,0},{4,7},{5,6},{6,5},{7,4},{8,11},{9,10},{10,... | collective-permute-start | bytes 786440 | tf_op jit(solution)/shard_map/ppermute | solution.py:20
  86.1 25.6 %collective-permute-start.15 = (bf16[128,2048]{1,0:T(8,128)(2,1)S(1)}, bf16[128,2048]{1,0:T(8,128)(2,1)S(1)}, u32[]{:S(2)}, u32[]{:S(2)}) collective-permute-start(bf16[128,2048]{1,0:T(8,128)(2,1)S(1)} %broadcast_select_fusion.1), channel_id=1, source_target_pairs={{0,8},{12,4},{4,0},{8,12},{1,9},{13,5},{5,1},{9,13},{2,10},{14,6},... | collective-permute-start | bytes 1572872 | tf_op jit(solution)/shard_map/ppermute | solution.py:27
  100.5 22.7 %collective-permute-start.20 = (bf16[128,2048]{1,0:T(8,128)(2,1)}, bf16[128,2048]{1,0:T(8,128)(2,1)S(1)}, u32[]{:S(2)}, u32[]{:S(2)}) collective-permute-start(bf16[128,2048]{1,0:T(8,128)(2,1)} %broadcast_select_fusion), channel_id=1, source_target_pairs={{0,8},{12,4},{4,0},{8,12},{1,9},{13,5},{5,1},{9,13},{2,10},{14,6},... | collective-permute-start | bytes 1572872 | tf_op jit(solution)/shard_map/ppermute | solution.py:27
  103.9 7.9 %collective-permute-start.16 = (bf16[128,2048]{1,0:T(8,128)(2,1)S(1)}, bf16[128,2048]{1,0:T(8,128)(2,1)S(1)}, u32[]{:S(2)}, u32[]{:S(2)}) collective-permute-start(bf16[128,2048]{1,0:T(8,128)(2,1)S(1)} %get-tuple-element.88), channel_id=1, source_target_pairs={{0,1},{1,0},{2,3},{3,2},{4,5},{5,4},{6,7},{7,6},{8,9},{9,8},{10,11... | collective-permute-start | bytes 1572872 | tf_op jit(solution)/shard_map/ppermute | solution.py:20
  104.8 23.0 %collective-permute-start.13 = (bf16[32,2048]{1,0:T(8,128)(2,1)}, bf16[32,2048]{1,0:T(8,128)(2,1)}, u32[]{:S(2)}, u32[]{:S(2)}) collective-permute-start(bf16[32,2048]{1,0:T(8,128)(2,1)} %get-tuple-element.124), channel_id=1, source_target_pairs={{0,4},{4,0},{8,12},{12,8},{1,5},{5,1},{9,13},{13,9},{2,6},{6,2},{1... | collective-permute-start | bytes 393224 | tf_op jit(solution)/shard_map/ppermute | solution.py:20
  106.9 21.9 %collective-permute-start.14 = (bf16[32,2048]{1,0:T(8,128)(2,1)}, bf16[32,2048]{1,0:T(8,128)(2,1)}, u32[]{:S(2)}, u32[]{:S(2)}) collective-permute-start(bf16[32,2048]{1,0:T(8,128)(2,1)} %get-tuple-element.123), channel_id=1, source_target_pairs={{0,12},{4,8},{8,4},{12,0},{1,13},{5,9},{9,5},{13,1},{2,14},{6,10},... | collective-permute-start | bytes 393224 | tf_op jit(solution)/shard_map/ppermute | solution.py:20
  114.0 14.7 %collective-permute-start.17 = (bf16[64,2048]{1,0:T(8,128)(2,1)}, bf16[64,2048]{1,0:T(8,128)(2,1)S(1)}, u32[]{:S(2)}, u32[]{:S(2)}) collective-permute-start(bf16[64,2048]{1,0:T(8,128)(2,1)} %add_convert_fusion.1), channel_id=1, source_target_pairs={{0,2},{2,0},{1,3},{3,1},{4,6},{6,4},{5,7},{7,5},{8,10},{10,8},{9,1... | collective-permute-start | bytes 786440 | tf_op jit(solution)/shard_map/ppermute | solution.py:20
  116.9 11.8 %collective-permute-start.19 = (bf16[32,2048]{1,0:T(8,128)(2,1)}, bf16[32,2048]{1,0:T(8,128)(2,1)S(1)}, u32[]{:S(2)}, u32[]{:S(2)}) collective-permute-start(bf16[32,2048]{1,0:T(8,128)(2,1)} %add_convert_fusion.10), channel_id=1, source_target_pairs={{0,2},{2,0},{1,3},{3,1},{4,6},{6,4},{5,7},{7,5},{8,10},{10,8},{9,1... | collective-permute-start | bytes 393224 | tf_op jit(solution)/shard_map/ppermute | solution.py:20
  128.7 7.9 %collective-permute-start.26 = (bf16[128,2048]{1,0:T(8,128)(2,1)S(1)}, bf16[128,2048]{1,0:T(8,128)(2,1)S(1)}, u32[]{:S(2)}, u32[]{:S(2)}) collective-permute-start(bf16[128,2048]{1,0:T(8,128)(2,1)S(1)} %copy-done.11), channel_id=1, source_target_pairs={{0,1},{1,0},{2,3},{3,2},{4,5},{5,4},{6,7},{7,6},{8,9},{9,8},{10,11... | collective-permute-start | bytes 1572872 | tf_op jit(solution)/shard_map/ppermute | solution.py:20
  129.4 10.6 %collective-permute-start.23 = (bf16[32,2048]{1,0:T(8,128)(2,1)S(1)}, bf16[32,2048]{1,0:T(8,128)(2,1)S(1)}, u32[]{:S(2)}, u32[]{:S(2)}) collective-permute-start(bf16[32,2048]{1,0:T(8,128)(2,1)S(1)} %add_convert_fusion.9), channel_id=1, source_target_pairs={{0,8},{4,12},{8,0},{12,4},{1,9},{5,13},{9,1},{13,5},{2,10},{6,14},... | collective-permute-start | bytes 393224 | tf_op jit(solution)/shard_map/ppermute | solution.py:20
  132.0 9.5 %collective-permute-start.21 = (bf16[32,2048]{1,0:T(8,128)(2,1)S(1)}, bf16[32,2048]{1,0:T(8,128)(2,1)S(1)}, u32[]{:S(2)}, u32[]{:S(2)}) collective-permute-start(bf16[32,2048]{1,0:T(8,128)(2,1)S(1)} %get-tuple-element.122), channel_id=1, source_target_pairs={{0,4},{4,0},{8,12},{12,8},{1,5},{5,1},{9,13},{13,9},{2,6},{6,2},{1... | collective-permute-start | bytes 393224 | tf_op jit(solution)/shard_map/ppermute | solution.py:20
  133.6 8.8 %collective-permute-start.22 = (bf16[32,2048]{1,0:T(8,128)(2,1)S(1)}, bf16[32,2048]{1,0:T(8,128)(2,1)S(1)}, u32[]{:S(2)}, u32[]{:S(2)}) collective-permute-start(bf16[32,2048]{1,0:T(8,128)(2,1)S(1)} %get-tuple-element.121), channel_id=1, source_target_pairs={{0,12},{4,8},{8,4},{12,0},{1,13},{5,9},{9,5},{13,1},{2,14},{6,10},... | collective-permute-start | bytes 393224 | tf_op jit(solution)/shard_map/ppermute | solution.py:20
  144.0 9.3 %collective-permute-start.29 = (bf16[32,2048]{1,0:T(8,128)(2,1)S(1)}, bf16[32,2048]{1,0:T(8,128)(2,1)S(1)}, u32[]{:S(2)}, u32[]{:S(2)}) collective-permute-start(bf16[32,2048]{1,0:T(8,128)(2,1)S(1)} %add_convert_fusion.3), channel_id=1, source_target_pairs={{0,8},{4,12},{8,0},{12,4},{1,9},{5,13},{9,1},{13,5},{2,10},{6,14},... | collective-permute-start | bytes 393224 | tf_op jit(solution)/shard_map/ppermute | solution.py:20
  (25 other events, 197.6 us)

commit v22 on v21

--- a/solution.py
+++ b/solution.py
@@ -366,7 +366,7 @@
     far1 = send_heads(send_sub(far1))
     own = send_sub(own)
     own0, own1 = send_heads(own, 0, many), send_heads(own, many, many + few)
-    back1, back_second0, far1, own0 = tie((back1, back_second0, far1, own0))
+    back1, back_second0, far1 = tie((back1, back_second0, far1))
     back_second1 = swap(add_shares(far1), "pool", 2)
     own0, own1 = add_shares(own0), add_shares(own1, many)
     backs = [(0, 1, back0[0]), (0, 3, back0[1]), (many, 1, back1[0]), (many, 3, back1[1])]

time: 155 us -> 157 us (1.013)
  waiting for transfers between devices: 51.9 us -> 53.5 us
    unnamed x38 -> x34, local copies, waits for them, and re-layouts: 13.7 us -> 14.6 us
  transfers between devices with their start and end apart: 30 -> 30, of which waited for: 13 -> 14; matrix products, arithmetic and copies ran while one was open for 8% -> 8% of each run, Pallas kernels for 9% -> 9%
where the time goes in v22:
time: 157 us; the launch traced here: 156 us
  waiting for transfers between devices  53.5 us (34%)
  starting transfers between devices  50.2 us (32%)
  Pallas kernels  23.5 us (15%)
  local copies, waits for them, and re-layouts  22.8 us (15%)
  other arithmetic  5.97 us (4%)
    ppermute x28, waiting for transfers between devices, swap(): lax.ppermute(values, axis, [(i, i ^ flip) for i in range(lax.axis_size(ax...  43.8 us
    ppermute x28, starting transfers between devices, swap(): lax.ppermute(values, axis, [(i, i ^ flip) for i in range(lax.axis_size(ax...  37 us
    unnamed x34, local copies, waits for them, and re-layouts  14.6 us
    ppermute x2, starting transfers between devices, second_hop(): return lax.ppermute(passed, 'pool', [(0, 2), (3, 1), (1, 0), (2, 3)])  13.2 us
    pallas_call x5, Pallas kernels, project_out(): pl.pallas_call(functools.partial(project_kernel, len(blocks), list(range(...  9.79 us
    ppermute x2, waiting for transfers between devices, second_hop(): return lax.ppermute(passed, 'pool', [(0, 2), (3, 1), (1, 0), (2, 3)])  9.66 us
    pallas_call x2, Pallas kernels, attend(): pl.pallas_call(functools.partial(attend_kernel, start, rows, len(parts)),...  8.82 us
    pallas_call x1, Pallas kernels, fetch(): pl.pallas_call(functools.partial(fetch_kernel, pool_size=pool_size, share...  3.81 us
  transfers between devices with their start and end apart: 30, of which 14 were waited for; matrix products, arithmetic and copies ran while one was open for 8% of the time, Pallas kernels for 9%

profile of v22, /device:TPU:0, one launch (start us, length us, event | category | flops | bytes accessed | tf_op | source)
XLA Modules:
  0.0 156.3 jit_solution(6949348111496271231)
XLA Ops:
  0.7 3.8 %shard_map.100 = (s32[2,16]{1,0:T(2,128)}, bf16[8,32,512]{2,1,0:T(8,128)(2,1)}, bf16[8,32,512]{2,1,0:T(8,128)(2,1)}, bf16[8,32,512]{2,1,0:T(8,128)(2,1)}, bf16[8,32,512]{2,1,0:T(8,128)(2,1)}) custom-call(s32[2]{0:T(128)} %pad_add_fusion.1.place, s32[8,8]{1,0:T(8,128)} %holder.1, s32[8,8]{1,0:T(8,128)} %block.1, s32[8]{0:T(128)} %serving.1, ...), custom_call_target="tpu_custom_call" | custom-call | flops 1 | bytes 1 | tf_op jit(solution)/shard_map/pallas_call | solution.py:156
  4.5 4.0 %collective-permute-start = (bf16[8,32,512]{2,1,0:T(8,128)(2,1)}, bf16[8,32,512]{2,1,0:T(8,128)(2,1)S(1)}, u32[]{:S(2)}, u32[]{:S(2)}) collective-permute-start(bf16[8,32,512]{2,1,0:T(8,128)(2,1)} %get-tuple-element.61), channel_id=1, source_target_pairs={{0,8},{4,12},{8,0},{12,4},{1,9},{5,13},{9,1},{13,5},{2,10},{6,14},... | collective-permute-start | bytes 786440 | tf_op jit(solution)/shard_map/ppermute | solution.py:20
  13.9 2.3 %reshape.24 = bf16[512,2,256]{2,1,0:T(2,128)(2,1)S(1)} reshape(bf16[512,2,2,128]{3,2,1,0:T(2,128)(2,1)} %param.12) | data formatting | bytes 1048576 | tf_op jit(solution)/shard_map/reshape | solution.py:296
  17.0 10.1 %collective-permute-done.refs_1_ = bf16[8,32,512]{2,1,0:T(8,128)(2,1)S(1)} collective-permute-done((bf16[8,32,512]{2,1,0:T(8,128)(2,1)}, bf16[8,32,512]{2,1,0:T(8,128)(2,1)S(1)}, u32[]{:S(2)}, u32[]{:S(2)}) %collective-permute-start) | collective-permute-done | bytes 262176 | tf_op jit(solution)/shard_map/ppermute | solution.py:20
  30.5 10.1 %collective-permute-done.4.refs_2_ = bf16[2,256,512]{2,1,0:T(8,128)(2,1)S(1)} collective-permute-done((bf16[2,256,512]{2,1,0:T(8,128)(2,1)S(1)}, bf16[2,256,512]{2,1,0:T(8,128)(2,1)S(1)}, u32[]{:S(2)}, u32[]{:S(2)}) %collective-permute-start.4) | collective-permute-done | bytes 524320 | tf_op jit(solution)/shard_map/ppermute | solution.py:20
  42.5 4.4 %shard_map.103.refs_0_ = bf16[128,2048]{1,0:T(8,128)(2,1)S(1)} custom-call(s32[3]{0:T(128)S(1)} %pad_add_fusion.2.scalars, bf16[2,2,64,2048]{3,2,1,0:T(8,128)(2,1)S(1)} %bitcast.18, bf16[2,256,512]{2,1,0:T(8,128)(2,1)S(1)} %bitcast.16, bf16[2,256,512]{2,1,0:T(8,128)(2,1)S(1)} %collective-permute-done.3.refs_1_, ...), custom_call_target="tpu_custom_call" | custom-call | flops 1 | bytes 1 | tf_op jit(solution)/shard_map/pallas_call | solution.py:257
  47.0 3.8 %collective-permute-start.8 = (bf16[128,2048]{1,0:T(8,128)(2,1)S(1)}, bf16[128,2048]{1,0:T(8,128)(2,1)S(1)}, u32[]{:S(2)}, u32[]{:S(2)}) collective-permute-start(bf16[128,2048]{1,0:T(8,128)(2,1)S(1)} %shard_map.103.refs_0_), channel_id=1, source_target_pairs={{0,12},{4,8},{8,4},{12,0},{1,13},{5,9},{9,5},{13,1},{2,14},{6,10},... | collective-permute-start | bytes 1572872 | tf_op jit(solution)/shard_map/ppermute | solution.py:20
  50.7 5.3 %collective-permute-start.9 = (bf16[128,2048]{1,0:T(8,128)(2,1)S(1)}, bf16[128,2048]{1,0:T(8,128)(2,1)S(1)}, u32[]{:S(2)}, u32[]{:S(2)}) collective-permute-start(bf16[128,2048]{1,0:T(8,128)(2,1)S(1)} %shard_map.103.refs_0_), channel_id=1, source_target_pairs={{0,4},{4,0},{8,12},{12,8},{1,5},{5,1},{9,13},{13,9},{2,6},{6,2},{1... | collective-permute-start | bytes 1572872 | tf_op jit(solution)/shard_map/ppermute | solution.py:20
  56.0 4.4 %shard_map.102.refs_1_ = bf16[128,2048]{1,0:T(8,128)(2,1)S(1)} custom-call(s32[3]{0:T(128)S(1)} %pad_add_fusion.2.scalars, bf16[2,2,64,2048]{3,2,1,0:T(8,128)(2,1)S(1)} %bitcast.19, bf16[2,256,512]{2,1,0:T(8,128)(2,1)S(1)} %bitcast.17, bf16[2,256,512]{2,1,0:T(8,128)(2,1)S(1)} %collective-permute-done.3.refs_1_, ...), custom_call_target="tpu_custom_call" | custom-call | flops 1 | bytes 1 | tf_op jit(solution)/shard_map/pallas_call | solution.py:257
  61.5 3.4 %copy-done = bf16[2048,2048]{1,0:T(8,128)(2,1)S(1)} copy-done((bf16[2048,2048]{1,0:T(8,128)(2,1)S(1)}, bf16[2048,2048]{1,0:T(8,128)(2,1)}, u32[]{:S(2)}) %copy-start) | copy-done | bytes 8388632
  64.9 2.4 %shard_map.104 = (f32[128,2048]{1,0:T(8,128)S(1)}, bf16[128,2048]{1,0:T(8,128)(2,1)S(1)}) custom-call(s32[1]{0:T(128)} %bitcast.1.share, bf16[128,2048]{1,0:T(8,128)(2,1)S(1)} %shard_map.103.refs_0_, bf16[128,2048]{1,0:T(8,128)(2,1)S(1)} %shard_map.102.refs_1_, bf16[2048,2048]{1,0:T(8,128)(2,1)S(1)} %copy-done), custom_call_target="tpu_custom_call" | custom-call | flops 1 | bytes 1 | tf_op jit(solution)/shard_map/pallas_call | solution.py:60
  69.0 5.9 %collective-permute-done.9.refs_0_ = bf16[128,2048]{1,0:T(8,128)(2,1)S(1)} collective-permute-done((bf16[128,2048]{1,0:T(8,128)(2,1)S(1)}, bf16[128,2048]{1,0:T(8,128)(2,1)S(1)}, u32[]{:S(2)}, u32[]{:S(2)}) %collective-permute-start.9) | collective-permute-done | bytes 524320 | tf_op jit(solution)/shard_map/ppermute | solution.py:20
  75.0 3.4 %copy-done.1 = bf16[2048,2048]{1,0:T(8,128)(2,1)S(1)} copy-done((bf16[2048,2048]{1,0:T(8,128)(2,1)S(1)}, bf16[2048,2048]{1,0:T(8,128)(2,1)}, u32[]{:S(2)}) %copy-start.1) | copy-done | bytes 8388632
  78.3 2.4 %shard_map.105 = (f32[64,2048]{1,0:T(8,128)S(1)}, bf16[64,2048]{1,0:T(8,128)(2,1)S(1)}, bf16[64,2048]{1,0:T(8,128)(2,1)S(1)}, bf16[64,2048]{1,0:T(8,128)(2,1)S(1)}) custom-call(s32[1]{0:T(128)} %bitcast.1.share, bf16[128,2048]{1,0:T(8,128)(2,1)S(1)} %collective-permute-done.9.refs_0_, bf16[128,2048]{1,0:T(8,128)(2,1)S(1)} %collective-permute-done.8.refs_1_, ...), custom_call_target="tpu_custom_call" | custom-call | flops 1 | bytes 1 | tf_op jit(solution)/shard_map/pallas_call | solution.py:60
  82.7 3.4 %collective-permute-done.6.refs_1_ = bf16[128,2048]{1,0:T(8,128)(2,1)S(1)} collective-permute-done((bf16[128,2048]{1,0:T(8,128)(2,1)S(1)}, bf16[128,2048]{1,0:T(8,128)(2,1)S(1)}, u32[]{:S(2)}, u32[]{:S(2)}) %collective-permute-start.6) | collective-permute-done | bytes 524320 | tf_op jit(solution)/shard_map/ppermute | solution.py:20
  86.1 13.2 %collective-permute-start.15 = (bf16[128,2048]{1,0:T(8,128)(2,1)S(1)}, bf16[128,2048]{1,0:T(8,128)(2,1)S(1)}, u32[]{:S(2)}, u32[]{:S(2)}) collective-permute-start(bf16[128,2048]{1,0:T(8,128)(2,1)S(1)} %broadcast_select_fusion.1), channel_id=1, source_target_pairs={{0,8},{12,4},{4,0},{8,12},{1,9},{13,5},{5,1},{9,13},{2,10},{14,6},... | collective-permute-start | bytes 1572872 | tf_op jit(solution)/shard_map/ppermute | solution.py:27
  101.3 2.4 %shard_map.106 = (f32[128,2048]{1,0:T(8,128)S(1)}, bf16[128,2048]{1,0:T(8,128)(2,1)S(1)}) custom-call(s32[1]{0:T(128)} %bitcast.1.share, bf16[128,2048]{1,0:T(8,128)(2,1)S(1)} %copy-done.7, bf16[128,2048]{1,0:T(8,128)(2,1)S(1)} %collective-permute-done.6.refs_1_, bf16[2048,2048]{1,0:T(8,128)(2,1)S(1)} %bitcast.11), custom_call_target="tpu_custom_call" | custom-call | flops 1 | bytes 1 | tf_op jit(solution)/shard_map/pallas_call | solution.py:60
  107.6 4.1 %collective-permute-done.15.refs_0_ = bf16[128,2048]{1,0:T(8,128)(2,1)S(1)} collective-permute-done((bf16[128,2048]{1,0:T(8,128)(2,1)S(1)}, bf16[128,2048]{1,0:T(8,128)(2,1)S(1)}, u32[]{:S(2)}, u32[]{:S(2)}) %collective-permute-start.15) | collective-permute-done | bytes 524320 | tf_op jit(solution)/shard_map/ppermute | solution.py:27
  117.4 5.6 %collective-permute-done.20.refs_0_ = bf16[128,2048]{1,0:T(8,128)(2,1)S(1)} collective-permute-done((bf16[128,2048]{1,0:T(8,128)(2,1)}, bf16[128,2048]{1,0:T(8,128)(2,1)S(1)}, u32[]{:S(2)}, u32[]{:S(2)}) %collective-permute-start.20) | collective-permute-done | bytes 524320 | tf_op jit(solution)/shard_map/ppermute | solution.py:27
  123.0 3.4 %copy-done.2 = bf16[2048,2048]{1,0:T(8,128)(2,1)S(1)} copy-done((bf16[2048,2048]{1,0:T(8,128)(2,1)S(1)}, bf16[2048,2048]{1,0:T(8,128)(2,1)}, u32[]{:S(2)}) %copy-start.2) | copy-done | bytes 8388632
  128.7 2.6 %collective-permute-start.23 = (bf16[32,2048]{1,0:T(8,128)(2,1)S(1)}, bf16[32,2048]{1,0:T(8,128)(2,1)S(1)}, u32[]{:S(2)}, u32[]{:S(2)}) collective-permute-start(bf16[32,2048]{1,0:T(8,128)(2,1)S(1)} %add_convert_fusion.9), channel_id=1, source_target_pairs={{0,8},{4,12},{8,0},{12,4},{1,9},{5,13},{9,1},{13,5},{2,10},{6,14},... | collective-permute-start | bytes 393224 | tf_op jit(solution)/shard_map/ppermute | solution.py:20
  139.1 2.9 %collective-permute-done.22 = bf16[32,2048]{1,0:T(8,128)(2,1)S(1)} collective-permute-done((bf16[32,2048]{1,0:T(8,128)(2,1)S(1)}, bf16[32,2048]{1,0:T(8,128)(2,1)S(1)}, u32[]{:S(2)}, u32[]{:S(2)}) %collective-permute-start.22) | collective-permute-done | bytes 131104 | tf_op jit(solution)/shard_map/ppermute | solution.py:20
  142.1 4.5 %collective-permute-start.29 = (bf16[32,2048]{1,0:T(8,128)(2,1)S(1)}, bf16[32,2048]{1,0:T(8,128)(2,1)S(1)}, u32[]{:S(2)}, u32[]{:S(2)}) collective-permute-start(bf16[32,2048]{1,0:T(8,128)(2,1)S(1)} %add_convert_fusion.3), channel_id=1, source_target_pairs={{0,8},{4,12},{8,0},{12,4},{1,9},{5,13},{9,1},{13,5},{2,10},{6,14},... | collective-permute-start | bytes 393224 | tf_op jit(solution)/shard_map/ppermute | solution.py:20
  148.8 4.3 %collective-permute-done.27 = bf16[32,2048]{1,0:T(8,128)(2,1)S(1)} collective-permute-done((bf16[32,2048]{1,0:T(8,128)(2,1)S(1)}, bf16[32,2048]{1,0:T(8,128)(2,1)S(1)}, u32[]{:S(2)}, u32[]{:S(2)}) %collective-permute-start.27) | collective-permute-done | bytes 131104 | tf_op jit(solution)/shard_map/ppermute | solution.py:20
  (113 shorter events, 44.1 us)
Async XLA Ops:
  4.5 22.7 %collective-permute-start = (bf16[8,32,512]{2,1,0:T(8,128)(2,1)}, bf16[8,32,512]{2,1,0:T(8,128)(2,1)S(1)}, u32[]{:S(2)}, u32[]{:S(2)}) collective-permute-start(bf16[8,32,512]{2,1,0:T(8,128)(2,1)} %get-tuple-element.61), channel_id=1, source_target_pairs={{0,8},{4,12},{8,0},{12,4},{1,9},{5,13},{9,1},{13,5},{2,10},{6,14},... | collective-permute-start | bytes 786440 | tf_op jit(solution)/shard_map/ppermute | solution.py:20
  8.5 18.6 %collective-permute-start.1 = (bf16[8,32,512]{2,1,0:T(8,128)(2,1)}, bf16[8,32,512]{2,1,0:T(8,128)(2,1)S(1)}, u32[]{:S(2)}, u32[]{:S(2)}) collective-permute-start(bf16[8,32,512]{2,1,0:T(8,128)(2,1)} %get-tuple-element.62), channel_id=1, source_target_pairs={{0,12},{4,8},{8,4},{12,0},{1,13},{5,9},{9,5},{13,1},{2,14},{6,10},... | collective-permute-start | bytes 786440 | tf_op jit(solution)/shard_map/ppermute | solution.py:20
  9.8 17.8 %collective-permute-start.2 = (bf16[8,32,512]{2,1,0:T(8,128)(2,1)}, bf16[8,32,512]{2,1,0:T(8,128)(2,1)S(1)}, u32[]{:S(2)}, u32[]{:S(2)}) collective-permute-start(bf16[8,32,512]{2,1,0:T(8,128)(2,1)} %get-tuple-element.63), channel_id=1, source_target_pairs={{0,4},{4,0},{8,12},{12,8},{1,5},{5,1},{9,13},{13,9},{2,6},{6,2},{1... | collective-permute-start | bytes 786440 | tf_op jit(solution)/shard_map/ppermute | solution.py:20
  28.8 11.9 %collective-permute-start.4 = (bf16[2,256,512]{2,1,0:T(8,128)(2,1)S(1)}, bf16[2,256,512]{2,1,0:T(8,128)(2,1)S(1)}, u32[]{:S(2)}, u32[]{:S(2)}) collective-permute-start(bf16[2,256,512]{2,1,0:T(8,128)(2,1)S(1)} %bitcast.14), channel_id=1, source_target_pairs={{0,2},{2,0},{1,3},{3,1},{4,6},{6,4},{5,7},{7,5},{8,10},{10,8},{9,1... | collective-permute-start | bytes 1572872 | tf_op jit(solution)/shard_map/ppermute | solution.py:20
  30.5 10.1 %collective-permute-start.3 = (bf16[2,256,512]{2,1,0:T(8,128)(2,1)S(1)}, bf16[2,256,512]{2,1,0:T(8,128)(2,1)S(1)}, u32[]{:S(2)}, u32[]{:S(2)}) collective-permute-start(bf16[2,256,512]{2,1,0:T(8,128)(2,1)S(1)} %bitcast.15), channel_id=1, source_target_pairs={{0,1},{1,0},{2,3},{3,2},{4,5},{5,4},{6,7},{7,6},{8,9},{9,8},{10,11... | collective-permute-start | bytes 1572872 | tf_op jit(solution)/shard_map/ppermute | solution.py:20
  47.0 22.1 %collective-permute-start.8 = (bf16[128,2048]{1,0:T(8,128)(2,1)S(1)}, bf16[128,2048]{1,0:T(8,128)(2,1)S(1)}, u32[]{:S(2)}, u32[]{:S(2)}) collective-permute-start(bf16[128,2048]{1,0:T(8,128)(2,1)S(1)} %shard_map.103.refs_0_), channel_id=1, source_target_pairs={{0,12},{4,8},{8,4},{12,0},{1,13},{5,9},{9,5},{13,1},{2,14},{6,10},... | collective-permute-start | bytes 1572872 | tf_op jit(solution)/shard_map/ppermute | solution.py:20
  50.7 24.2 %collective-permute-start.9 = (bf16[128,2048]{1,0:T(8,128)(2,1)S(1)}, bf16[128,2048]{1,0:T(8,128)(2,1)S(1)}, u32[]{:S(2)}, u32[]{:S(2)}) collective-permute-start(bf16[128,2048]{1,0:T(8,128)(2,1)S(1)} %shard_map.103.refs_0_), channel_id=1, source_target_pairs={{0,4},{4,0},{8,12},{12,8},{1,5},{5,1},{9,13},{13,9},{2,6},{6,2},{1... | collective-permute-start | bytes 1572872 | tf_op jit(solution)/shard_map/ppermute | solution.py:20
  60.4 25.7 %collective-permute-start.6 = (bf16[128,2048]{1,0:T(8,128)(2,1)S(1)}, bf16[128,2048]{1,0:T(8,128)(2,1)S(1)}, u32[]{:S(2)}, u32[]{:S(2)}) collective-permute-start(bf16[128,2048]{1,0:T(8,128)(2,1)S(1)} %shard_map.102.refs_1_), channel_id=1, source_target_pairs={{0,12},{4,8},{8,4},{12,0},{1,13},{5,9},{9,5},{13,1},{2,14},{6,10},... | collective-permute-start | bytes 1572872 | tf_op jit(solution)/shard_map/ppermute | solution.py:20
  61.5 37.8 %collective-permute-start.7 = (bf16[128,2048]{1,0:T(8,128)(2,1)S(1)}, bf16[128,2048]{1,0:T(8,128)(2,1)S(1)}, u32[]{:S(2)}, u32[]{:S(2)}) collective-permute-start(bf16[128,2048]{1,0:T(8,128)(2,1)S(1)} %shard_map.102.refs_1_), channel_id=1, source_target_pairs={{0,4},{4,0},{8,12},{12,8},{1,5},{5,1},{9,13},{13,9},{2,6},{6,2},{1... | collective-permute-start | bytes 1572872 | tf_op jit(solution)/shard_map/ppermute | solution.py:20
  80.7 18.6 %collective-permute-start.10 = (bf16[64,2048]{1,0:T(8,128)(2,1)S(1)}, bf16[64,2048]{1,0:T(8,128)(2,1)S(1)}, u32[]{:S(2)}, u32[]{:S(2)}) collective-permute-start(bf16[64,2048]{1,0:T(8,128)(2,1)S(1)} %get-tuple-element.73), channel_id=1, source_target_pairs={{0,1},{1,0},{2,3},{3,2},{4,5},{5,4},{6,7},{7,6},{8,9},{9,8},{10,11... | collective-permute-start | bytes 786440 | tf_op jit(solution)/shard_map/ppermute | solution.py:20
  80.8 18.5 %collective-permute-start.11 = (bf16[64,2048]{1,0:T(8,128)(2,1)S(1)}, bf16[64,2048]{1,0:T(8,128)(2,1)S(1)}, u32[]{:S(2)}, u32[]{:S(2)}) collective-permute-start(bf16[64,2048]{1,0:T(8,128)(2,1)S(1)} %get-tuple-element.74), channel_id=1, source_target_pairs={{0,2},{1,3},{2,0},{3,1},{4,6},{5,7},{6,4},{7,5},{8,10},{9,11},{10,... | collective-permute-start | bytes 786440 | tf_op jit(solution)/shard_map/ppermute | solution.py:20
  82.3 17.0 %collective-permute-start.12 = (bf16[64,2048]{1,0:T(8,128)(2,1)S(1)}, bf16[64,2048]{1,0:T(8,128)(2,1)S(1)}, u32[]{:S(2)}, u32[]{:S(2)}) collective-permute-start(bf16[64,2048]{1,0:T(8,128)(2,1)S(1)} %get-tuple-element.75), channel_id=1, source_target_pairs={{0,3},{1,2},{2,1},{3,0},{4,7},{5,6},{6,5},{7,4},{8,11},{9,10},{10,... | collective-permute-start | bytes 786440 | tf_op jit(solution)/shard_map/ppermute | solution.py:20
  86.1 25.5 %collective-permute-start.15 = (bf16[128,2048]{1,0:T(8,128)(2,1)S(1)}, bf16[128,2048]{1,0:T(8,128)(2,1)S(1)}, u32[]{:S(2)}, u32[]{:S(2)}) collective-permute-start(bf16[128,2048]{1,0:T(8,128)(2,1)S(1)} %broadcast_select_fusion.1), channel_id=1, source_target_pairs={{0,8},{12,4},{4,0},{8,12},{1,9},{13,5},{5,1},{9,13},{2,10},{14,6},... | collective-permute-start | bytes 1572872 | tf_op jit(solution)/shard_map/ppermute | solution.py:27
  100.3 22.7 %collective-permute-start.20 = (bf16[128,2048]{1,0:T(8,128)(2,1)}, bf16[128,2048]{1,0:T(8,128)(2,1)S(1)}, u32[]{:S(2)}, u32[]{:S(2)}) collective-permute-start(bf16[128,2048]{1,0:T(8,128)(2,1)} %broadcast_select_fusion), channel_id=1, source_target_pairs={{0,8},{12,4},{4,0},{8,12},{1,9},{13,5},{5,1},{9,13},{2,10},{14,6},... | collective-permute-start | bytes 1572872 | tf_op jit(solution)/shard_map/ppermute | solution.py:27
  103.7 7.9 %collective-permute-start.16 = (bf16[128,2048]{1,0:T(8,128)(2,1)S(1)}, bf16[128,2048]{1,0:T(8,128)(2,1)S(1)}, u32[]{:S(2)}, u32[]{:S(2)}) collective-permute-start(bf16[128,2048]{1,0:T(8,128)(2,1)S(1)} %get-tuple-element.85), channel_id=1, source_target_pairs={{0,1},{1,0},{2,3},{3,2},{4,5},{5,4},{6,7},{7,6},{8,9},{9,8},{10,11... | collective-permute-start | bytes 1572872 | tf_op jit(solution)/shard_map/ppermute | solution.py:20
  104.7 23.1 %collective-permute-start.13 = (bf16[32,2048]{1,0:T(8,128)(2,1)}, bf16[32,2048]{1,0:T(8,128)(2,1)}, u32[]{:S(2)}, u32[]{:S(2)}) collective-permute-start(bf16[32,2048]{1,0:T(8,128)(2,1)} %get-tuple-element.118), channel_id=1, source_target_pairs={{0,4},{4,0},{8,12},{12,8},{1,5},{5,1},{9,13},{13,9},{2,6},{6,2},{1... | collective-permute-start | bytes 393224 | tf_op jit(solution)/shard_map/ppermute | solution.py:20
  106.7 21.9 %collective-permute-start.14 = (bf16[32,2048]{1,0:T(8,128)(2,1)}, bf16[32,2048]{1,0:T(8,128)(2,1)}, u32[]{:S(2)}, u32[]{:S(2)}) collective-permute-start(bf16[32,2048]{1,0:T(8,128)(2,1)} %get-tuple-element.117), channel_id=1, source_target_pairs={{0,12},{4,8},{8,4},{12,0},{1,13},{5,9},{9,5},{13,1},{2,14},{6,10},... | collective-permute-start | bytes 393224 | tf_op jit(solution)/shard_map/ppermute | solution.py:20
  113.8 14.7 %collective-permute-start.17 = (bf16[64,2048]{1,0:T(8,128)(2,1)}, bf16[64,2048]{1,0:T(8,128)(2,1)S(1)}, u32[]{:S(2)}, u32[]{:S(2)}) collective-permute-start(bf16[64,2048]{1,0:T(8,128)(2,1)} %add_convert_fusion.1), channel_id=1, source_target_pairs={{0,2},{2,0},{1,3},{3,1},{4,6},{6,4},{5,7},{7,5},{8,10},{10,8},{9,1... | collective-permute-start | bytes 786440 | tf_op jit(solution)/shard_map/ppermute | solution.py:20
  116.7 11.9 %collective-permute-start.19 = (bf16[32,2048]{1,0:T(8,128)(2,1)}, bf16[32,2048]{1,0:T(8,128)(2,1)S(1)}, u32[]{:S(2)}, u32[]{:S(2)}) collective-permute-start(bf16[32,2048]{1,0:T(8,128)(2,1)} %add_convert_fusion.10), channel_id=1, source_target_pairs={{0,2},{2,0},{1,3},{3,1},{4,6},{6,4},{5,7},{7,5},{8,10},{10,8},{9,1... | collective-permute-start | bytes 393224 | tf_op jit(solution)/shard_map/ppermute | solution.py:20
  128.7 10.1 %collective-permute-start.23 = (bf16[32,2048]{1,0:T(8,128)(2,1)S(1)}, bf16[32,2048]{1,0:T(8,128)(2,1)S(1)}, u32[]{:S(2)}, u32[]{:S(2)}) collective-permute-start(bf16[32,2048]{1,0:T(8,128)(2,1)S(1)} %add_convert_fusion.9), channel_id=1, source_target_pairs={{0,8},{4,12},{8,0},{12,4},{1,9},{5,13},{9,1},{13,5},{2,10},{6,14},... | collective-permute-start | bytes 393224 | tf_op jit(solution)/shard_map/ppermute | solution.py:20
  131.4 7.7 %collective-permute-start.21 = (bf16[32,2048]{1,0:T(8,128)(2,1)S(1)}, bf16[32,2048]{1,0:T(8,128)(2,1)S(1)}, u32[]{:S(2)}, u32[]{:S(2)}) collective-permute-start(bf16[32,2048]{1,0:T(8,128)(2,1)S(1)} %get-tuple-element.116), channel_id=1, source_target_pairs={{0,4},{4,0},{8,12},{12,8},{1,5},{5,1},{9,13},{13,9},{2,6},{6,2},{1... | collective-permute-start | bytes 393224 | tf_op jit(solution)/shard_map/ppermute | solution.py:20
  132.9 9.2 %collective-permute-start.22 = (bf16[32,2048]{1,0:T(8,128)(2,1)S(1)}, bf16[32,2048]{1,0:T(8,128)(2,1)S(1)}, u32[]{:S(2)}, u32[]{:S(2)}) collective-permute-start(bf16[32,2048]{1,0:T(8,128)(2,1)S(1)} %get-tuple-element.115), channel_id=1, source_target_pairs={{0,12},{4,8},{8,4},{12,0},{1,13},{5,9},{9,5},{13,1},{2,14},{6,10},... | collective-permute-start | bytes 393224 | tf_op jit(solution)/shard_map/ppermute | solution.py:20
  133.3 13.3 %collective-permute-start.26 = (bf16[128,2048]{1,0:T(8,128)(2,1)S(1)}, bf16[128,2048]{1,0:T(8,128)(2,1)S(1)}, u32[]{:S(2)}, u32[]{:S(2)}) collective-permute-start(bf16[128,2048]{1,0:T(8,128)(2,1)S(1)} %copy-done.9), channel_id=1, source_target_pairs={{0,1},{1,0},{2,3},{3,2},{4,5},{5,4},{6,7},{7,6},{8,9},{9,8},{10,11... | collective-permute-start | bytes 1572872 | tf_op jit(solution)/shard_map/ppermute | solution.py:20
  142.1 12.6 %collective-permute-start.29 = (bf16[32,2048]{1,0:T(8,128)(2,1)S(1)}, bf16[32,2048]{1,0:T(8,128)(2,1)S(1)}, u32[]{:S(2)}, u32[]{:S(2)}) collective-permute-start(bf16[32,2048]{1,0:T(8,128)(2,1)S(1)} %add_convert_fusion.3), channel_id=1, source_target_pairs={{0,8},{4,12},{8,0},{12,4},{1,9},{5,13},{9,1},{13,5},{2,10},{6,14},... | collective-permute-start | bytes 393224 | tf_op jit(solution)/shard_map/ppermute | solution.py:20
  (23 other events, 197.3 us)
